TPU v7x, 32 devices: a whole 2x2x4 slice. The times are simulated.
32 devices in a mesh: groups: 2 (over y), gx: 4 (over z), gy: 2 (over x), gz: 2 (over core).
Axes of the slice: x: 2, y: 2, z: 4, core: 2. Of those that a mesh axis runs over, the one named last changes fastest.
Arguments:
- tokens: bfloat16 [64, 16384], P(('groups', 'gx', 'gy', 'gz')), parts along dimension 0, may hold values from -6 to 6
- norm_gain: float32 [16384], replicated, may hold values from 0.25 to 1.75
- query_weight: bfloat16 [16384, 8192], P('gx', ('gy', 'gz')), may hold values from -0.046875 to 0.046875
- key_weight: bfloat16 [16384, 1024], P('gx', ('gy', 'gz')), may hold values from -0.046875 to 0.046875
- value_weight: bfloat16 [16384, 1024], P('gx', ('gy', 'gz')), may hold values from -0.046875 to 0.046875
- out_weight: bfloat16 [8192, 16384], P(('gy', 'gz'), 'gx'), may hold values from -0.0625 to 0.0625
- cache_keys: bfloat16 [64, 256, 1024], P(('groups', 'gx', 'gy', 'gz')), parts along dimension 0, may hold values from -200 to 200
- cache_values: bfloat16 [64, 256, 1024], P(('groups', 'gx', 'gy', 'gz')), parts along dimension 0, may hold values from -18 to 18
- lengths: int32 [64], P(('groups', 'gx', 'gy', 'gz')), parts along dimension 0, may hold values from 1 to 256, as said below
Outputs:
- attention_out: bfloat16 [64, 16384], P(('groups', 'gx', 'gy', 'gz')), parts along dimension 0
There are 2 independent parts, one for each index of `groups`. A program takes and returns all parts, laid end to end along the dimension named above; an argument that names none is the same for every part. Nothing has to cross between parts.
Inputs may be any that keep to these rules, and one draw needn't show every extreme that they name: `lengths`: each row's cache holds from 1 to 256 filled slots; some row holds exactly 256.
All inputs are finite; a program needn't handle non-finite values.
Results may differ from a plain program's by a relative error of at most 0.006.
The roundings to bfloat16 on the way count: a program that leaves them out, or rounds other values in their place, can miss the bound.
Values may be sent and summed in bfloat16 or wider, within the bound.
No kernel may reach another device: no remote copies, remote signals or barrier semaphores. Data moves between devices by JAX's collectives and lax.ppermute only.
A program may use at most 128 MiB of HBM per device.

v0:
```python
import jax
import jax.numpy as jnp
from jax import lax
from jax.sharding import PartitionSpec as P

HD = 128


def rotate(vector, position):
    half_dim = vector.shape[-1] // 2
    frequency = 500000.0 ** (-jnp.arange(half_dim, dtype=jnp.float32) / half_dim)
    angles = position.astype(jnp.float32)[:, None, None] * frequency
    cosine_part = jnp.cos(angles)
    sine_part = jnp.sin(angles)
    front_half = vector[..., :half_dim]
    back_half = vector[..., half_dim:]
    return jnp.concatenate(
        [
            front_half * cosine_part - back_half * sine_part,
            front_half * sine_part + back_half * cosine_part,
        ],
        -1,
    )


def shards(
    tokens,
    norm_gain,
    query_weight,
    key_weight,
    value_weight,
    out_weight,
    cache_keys,
    cache_values,
    lengths,
):
    row_count = tokens.shape[0]
    wide_count = lax.axis_size("gx")
    head_groups = lax.axis_size(("gy", "gz"))
    float_tokens = tokens.astype(jnp.float32)
    mean_square = jnp.mean(float_tokens * float_tokens, -1, keepdims=True)
    normed = (float_tokens * lax.rsqrt(mean_square + 1e-05) * norm_gain).astype(jnp.bfloat16)
    gathered = lax.all_gather(normed, ("gy", "gz"), axis=0, tiled=True)
    width_rows = lax.all_to_all(gathered, "gx", split_axis=1, concat_axis=0, tiled=True)
    query_cols = query_weight.shape[1]
    kv_cols = key_weight.shape[1]
    own_rows = lax.psum_scatter(
        jnp.concatenate(
            [
                jnp.dot(width_rows, query_weight, preferred_element_type=jnp.float32),
                jnp.dot(width_rows, key_weight, preferred_element_type=jnp.float32),
                jnp.dot(width_rows, value_weight, preferred_element_type=jnp.float32),
            ],
            1,
        ),
        "gx",
        scatter_dimension=0,
        tiled=True,
    ).astype(jnp.bfloat16)
    query_all, key_all, value_all = (
        lax.all_to_all(
            own_rows[:, :query_cols], ("gy", "gz"), split_axis=0, concat_axis=1, tiled=True
        ),
        lax.all_to_all(
            own_rows[:, query_cols : query_cols + kv_cols],
            ("gy", "gz"),
            split_axis=0,
            concat_axis=1,
            tiled=True,
        ),
        lax.all_to_all(
            own_rows[:, query_cols + kv_cols :],
            ("gy", "gz"),
            split_axis=0,
            concat_axis=1,
            tiled=True,
        ),
    )
    n_heads = query_all.shape[1] // HD
    kv_heads = key_all.shape[1] // HD
    group_size = n_heads // kv_heads
    slots = cache_keys.shape[1]
    query_rot = rotate(
        query_all.astype(jnp.float32).reshape(row_count, n_heads, HD), lengths
    ).astype(jnp.bfloat16)
    key_rot = rotate(key_all.astype(jnp.float32).reshape(row_count, kv_heads, HD), lengths).astype(
        jnp.bfloat16
    )
    query_group = query_rot.reshape(row_count, kv_heads, group_size, HD)
    key_cache = cache_keys.reshape(row_count, slots, kv_heads, HD)
    value_cache = cache_values.reshape(row_count, slots, kv_heads, HD)
    scale = 1.0 / HD**0.5
    scores = (
        jnp.einsum("rkgd,rskd->rkgs", query_group, key_cache, preferred_element_type=jnp.float32)
        * scale
    )
    valid_mask = (jnp.arange(slots, dtype=jnp.int32)[None, :] < lengths[:, None])[:, None, None, :]
    scores = jnp.where(valid_mask, scores, -1e30)
    fresh_score = (
        jnp.einsum("rkgd,rkd->rkg", query_group, key_rot, preferred_element_type=jnp.float32)
        * scale
    )
    top_score = jnp.maximum(jnp.max(scores, -1), fresh_score)
    weights = jnp.exp(scores - top_score[..., None])
    own_weight = jnp.exp(fresh_score - top_score)
    denominator = jnp.sum(weights, -1) + own_weight
    probability = (weights / denominator[..., None]).astype(jnp.bfloat16)
    own_prob = (own_weight / denominator).astype(jnp.bfloat16)
    mixed_heads = jnp.einsum(
        "rkgs,rskd->rkgd", probability, value_cache, preferred_element_type=jnp.float32
    )
    mixed_heads = mixed_heads + own_prob.astype(jnp.float32)[..., None] * value_all.reshape(
        row_count, kv_heads, 1, HD
    ).astype(jnp.float32)
    attended = mixed_heads.reshape(row_count, n_heads * HD).astype(jnp.bfloat16)
    head_rows = lax.all_to_all(attended, ("gy", "gz"), split_axis=1, concat_axis=0, tiled=True)
    out_partial = jnp.dot(
        lax.all_gather(head_rows, "gx", axis=0, tiled=True),
        out_weight,
        preferred_element_type=jnp.float32,
    )
    slab_width = out_partial.shape[1]
    out_partial = (
        out_partial.reshape(wide_count, head_groups, row_count, slab_width)
        .transpose(1, 0, 2, 3)
        .reshape(-1, slab_width)
    )
    out_summed = lax.psum_scatter(
        out_partial, ("gy", "gz"), scatter_dimension=0, tiled=True
    ).astype(jnp.bfloat16)
    return lax.all_to_all(out_summed, "gx", split_axis=0, concat_axis=1, tiled=True)


def solution(mesh):
    placed = (
        P(("groups", "gx", "gy", "gz"), None),
        P(),
        P("gx", ("gy", "gz")),
        P("gx", ("gy", "gz")),
        P("gx", ("gy", "gz")),
        P(("gy", "gz"), "gx"),
        P(("groups", "gx", "gy", "gz"), None, None),
        P(("groups", "gx", "gy", "gz"), None, None),
        P(("groups", "gx", "gy", "gz")),
    )
    return jax.shard_map(
        shards,
        mesh=mesh,
        in_specs=placed,
        out_specs=P(("groups", "gx", "gy", "gz"), None),
        check_vma=False,
    )
```

profile of v0, /device:TPU:0, one launch (start us, length us, event | category | flops | bytes accessed | tf_op | source)
XLA Modules:
  0.0 156.8 jit_solution(1022116726087296646)
XLA Ops:
  6.5 0.0 copy-start
  6.5 0.0 copy-start.2
  6.5 0.0 reduce-scatter.3.cloned.1.call-start
  6.5 1.2 fusion.12
  7.8 1.0 fusion.18
  8.8 0.0 copy-start.1
  8.8 7.3 %all-gather = bf16[4,2,16384]{2,1,0:T(2,128)(2,1)S(1)} all-gather(bf16[1,2,16384]{2,1,0:T(2,128)(2,1)S(1)} %fusion.18), channel_id=1, replica_groups=mesh['groups'=2,'gx'=4,'gy'=2,'gz'=2] {'gy','gz'}, dimensions={0}, use_global_device_ids=true | all-gather | bytes 327680 | tf_op jit(solution)/shard_map/all_gather | solution.py:43
  16.1 0.9 all_to_all.70
  17.0 1.1 copy.27
  18.1 14.1 %all_to_all.93 = bf16[8,4,4096]{2,0,1:T(8,128)(2,1)S(1)} all-to-all(bf16[8,4,4096]{2,0,1:T(8,128)(2,1)S(1)} %copy.27), channel_id=1, replica_groups=mesh['groups'=2,'gx'=4,'gy'=2,'gz'=2] {'gx'}, dimensions={1} | all-to-all | bytes 524288 | tf_op jit(solution)/shard_map/all_to_all | solution.py:44
  32.2 0.0 copy-done
  32.2 0.5 fusion.8
  32.7 2.1 %fusion.6 = f32[32,256]{1,0:T(8,128)S(1)} fusion(bf16[4096,256]{1,0:T(8,128)(2,1)} %param.13, bf16[8,4,4096]{2,0,1:T(8,128)(2,1)S(1)} %all_to_all.93), kind=kOutput, calls=%fused_computation.10 | convolution fusion | flops 67108864 | bytes 2392064 | tf_op jit(solution)/shard_map/dot_general | solution.py:52
  34.7 8.8 %fusion.10 = f32[32,2048]{1,0:T(8,128)S(1)} fusion(bf16[4096,2048]{1,0:T(8,128)(2,1)} %param.11, bf16[8,4,4096]{2,0,1:T(8,128)(2,1)S(1)} %all_to_all.93), kind=kOutput, calls=%fused_computation.14 | convolution fusion | flops 536870912 | bytes 17301504 | tf_op jit(solution)/shard_map/dot_general | solution.py:50
  43.5 0.8 pad_maximum_fusion
  44.3 0.0 reduce-scatter.3.cloned.1.call-update
  44.3 0.0 copy-done.2
  44.3 0.1 multiply_cosine_fusion
  44.4 19.2 %reduce-scatter.3.cloned.1.call-done = f32[8,2560]{1,0:T(8,128)} async-done(((f32[32,2560]{1,0:T(8,128)}), f32[8,2560]{1,0:T(8,128)}) %reduce-scatter.3.cloned.1.call-update) | async-done | bytes 81936 | tf_op jit(solution)/shard_map/reduce_scatter | solution.py:47
  63.6 0.9 convert_element_type.71
  64.5 0.6 all_to_all.76
  65.1 3.2 %all-to-all-start.2 = ((bf16[4,2,256]{2,1,0:T(2,128)(2,1)}), bf16[4,2,256]{2,1,0:T(2,128)(2,1)S(1)}, u32[]{:S(2)}, u32[]{:S(2)}) async-start(bf16[4,2,256]{2,1,0:T(2,128)(2,1)} %all_to_all.76), calls=%async_computation.3 | async-start | bytes 8192 | tf_op jit(solution)/shard_map/all_to_all | solution.py:64
  68.4 0.1 iota_compare_fusion
  68.4 0.6 all_to_all.74
  69.1 0.6 all_to_all.78
  69.7 2.4 %all-to-all-done.2 = bf16[4,2,256]{2,1,0:T(2,128)(2,1)S(1)} async-done(((bf16[4,2,256]{2,1,0:T(2,128)(2,1)}), bf16[4,2,256]{2,1,0:T(2,128)(2,1)S(1)}, u32[]{:S(2)}, u32[]{:S(2)}) %all-to-all-start.2) | async-done | bytes 4128 | tf_op jit(solution)/shard_map/all_to_all | solution.py:64
  72.1 3.2 %all-to-all-start.3 = ((bf16[4,2,256]{2,1,0:T(2,128)(2,1)}), bf16[4,2,256]{2,1,0:T(2,128)(2,1)S(1)}, u32[]{:S(2)}, u32[]{:S(2)}) async-start(bf16[4,2,256]{2,1,0:T(2,128)(2,1)} %all_to_all.78), calls=%async_computation.4 | async-start | bytes 8192 | tf_op jit(solution)/shard_map/all_to_all | solution.py:71
  75.4 0.1 subtract_convert_fusion.1
  75.5 3.6 %all-to-all-done.3 = bf16[4,2,256]{2,1,0:T(2,128)(2,1)S(1)} async-done(((bf16[4,2,256]{2,1,0:T(2,128)(2,1)}), bf16[4,2,256]{2,1,0:T(2,128)(2,1)S(1)}, u32[]{:S(2)}, u32[]{:S(2)}) %all-to-all-start.3) | async-done | bytes 4128 | tf_op jit(solution)/shard_map/all_to_all | solution.py:71
  79.1 3.3 %all-to-all-start.1 = ((bf16[4,2,2048]{2,1,0:T(2,128)(2,1)}), bf16[4,2,2048]{2,1,0:T(2,128)(2,1)S(1)}, u32[]{:S(2)}, u32[]{:S(2)}) async-start(bf16[4,2,2048]{2,1,0:T(2,128)(2,1)} %all_to_all.74), calls=%async_computation.2 | async-start | bytes 65536 | tf_op jit(solution)/shard_map/all_to_all | solution.py:61
  82.4 0.0 reduce-scatter.5.cloned.1.call-start
  82.4 0.1 maximum_bitcast_fusion
  82.5 3.8 %all-to-all-done.1 = bf16[4,2,2048]{2,1,0:T(2,128)(2,1)S(1)} async-done(((bf16[4,2,2048]{2,1,0:T(2,128)(2,1)}), bf16[4,2,2048]{2,1,0:T(2,128)(2,1)S(1)}, u32[]{:S(2)}, u32[]{:S(2)}) %all-to-all-start.1) | async-done | bytes 32800 | tf_op jit(solution)/shard_map/all_to_all | solution.py:61
  86.4 0.1 fusion.19
  86.5 0.2 fusion.21
  86.7 0.0 copy-done.1
  86.7 0.5 fusion.28
  87.2 0.2 fusion.15
  87.4 1.5 fusion.1
  89.0 6.3 %all_to_all.94 = bf16[2,4,2048]{2,0,1:T(2,128)(2,1)S(1)} all-to-all(bf16[2,4,2048]{2,0,1:T(2,128)(2,1)S(1)} %copy.33), channel_id=1, replica_groups=mesh['groups'=2,'gx'=4,'gy'=2,'gz'=2] {'gy','gz'}, dimensions={1} | all-to-all | bytes 65536 | tf_op jit(solution)/shard_map/all_to_all | solution.py:116
  95.4 13.6 %all_gather.7 = bf16[32,2048]{1,0:T(8,128)(2,1)S(1)} all-gather(bf16[8,2048]{1,0:T(8,128)(2,1)S(1)} %all_to_all.82), channel_id=1, replica_groups=mesh['groups'=2,'gx'=4,'gy'=2,'gz'=2] {'gx'}, dimensions={0}, use_global_device_ids=true | all-gather | bytes 163840 | tf_op jit(solution)/shard_map/all_gather | solution.py:118
  109.0 8.7 %fusion.29 = f32[32,4096]{1,0:T(8,128)S(1)} fusion(bf16[32,2048]{1,0:T(8,128)(2,1)S(1)} %all_gather.7, bf16[2048,4096]{1,0:T(8,128)(2,1)} %param.14), kind=kOutput, calls=%fused_computation.54 | convolution fusion | flops 536870912 | bytes 17432576 | tf_op jit(solution)/shard_map/dot_general | solution.py:117
  117.8 0.3 reshape.148
  118.1 1.2 reshape.149
  119.3 0.0 reduce-scatter.5.cloned.1.call-update
  119.3 18.9 %reduce-scatter.5.cloned.1.call-done = f32[8,4096]{1,0:T(8,128)} async-done(((f32[32,4096]{1,0:T(8,128)}), f32[8,4096]{1,0:T(8,128)}) %reduce-scatter.5.cloned.1.call-update) | async-done | bytes 131088 | tf_op jit(solution)/shard_map/reduce_scatter | solution.py:128
  138.2 0.9 convert_element_type.87
  139.1 0.1 all_to_all.83
  139.2 10.1 %all_to_all.95 = bf16[4,2,4096]{2,1,0:T(2,128)(2,1)S(1)} all-to-all(bf16[4,2,4096]{2,1,0:T(2,128)(2,1)S(1)} %all_to_all.83), channel_id=1, replica_groups=mesh['groups'=2,'gx'=4,'gy'=2,'gz'=2] {'gx'}, dimensions={0} | all-to-all | bytes 131072 | tf_op jit(solution)/shard_map/all_to_all | solution.py:131
  149.3 0.6 copy.54
  (20 shorter events, 0.3 us)
Async XLA Ops:
  6.5 25.7 %copy-start = (bf16[4096,256]{1,0:T(8,128)(2,1)S(1)}, bf16[4096,256]{1,0:T(8,128)(2,1)}, u32[]{:S(2)}) copy-start(bf16[4096,256]{1,0:T(8,128)(2,1)} %param.12) | copy-start | bytes 6291460
  6.5 37.8 %copy-start.2 = (s32[2]{0:T(128)S(1)}, s32[2]{0:T(128)}, u32[]{:S(2)}) copy-start(s32[2]{0:T(128)} %param.17) | copy-start | bytes 28
  6.5 57.1 %reduce-scatter.3.cloned.1.call-start = ((), (), s32[]{:S(2)}) async-start(), calls=%async_computation.8 | async-start | bytes 409600 | tf_op jit(solution)/shard_map/reduce_scatter | solution.py:47
  8.8 77.9 %copy-start.1 = (bf16[2,256,1024]{2,1,0:T(8,128)(2,1)S(1)}, bf16[2,256,1024]{2,1,0:T(8,128)(2,1)}, u32[]{:S(2)}) copy-start(bf16[2,256,1024]{2,1,0:T(8,128)(2,1)} %param.15) | copy-start | bytes 3145732
  65.1 7.0 %all-to-all-start.2 = ((bf16[4,2,256]{2,1,0:T(2,128)(2,1)}), bf16[4,2,256]{2,1,0:T(2,128)(2,1)S(1)}, u32[]{:S(2)}, u32[]{:S(2)}) async-start(bf16[4,2,256]{2,1,0:T(2,128)(2,1)} %all_to_all.76), calls=%async_computation.3 | async-start | bytes 8192 | tf_op jit(solution)/shard_map/all_to_all | solution.py:64
  72.1 7.0 %all-to-all-start.3 = ((bf16[4,2,256]{2,1,0:T(2,128)(2,1)}), bf16[4,2,256]{2,1,0:T(2,128)(2,1)S(1)}, u32[]{:S(2)}, u32[]{:S(2)}) async-start(bf16[4,2,256]{2,1,0:T(2,128)(2,1)} %all_to_all.78), calls=%async_computation.4 | async-start | bytes 8192 | tf_op jit(solution)/shard_map/all_to_all | solution.py:71
  79.1 7.2 %all-to-all-start.1 = ((bf16[4,2,2048]{2,1,0:T(2,128)(2,1)}), bf16[4,2,2048]{2,1,0:T(2,128)(2,1)S(1)}, u32[]{:S(2)}, u32[]{:S(2)}) async-start(bf16[4,2,2048]{2,1,0:T(2,128)(2,1)} %all_to_all.74), calls=%async_computation.2 | async-start | bytes 65536 | tf_op jit(solution)/shard_map/all_to_all | solution.py:61
  82.4 55.8 %reduce-scatter.5.cloned.1.call-start = ((), (), s32[]{:S(2)}) async-start(), calls=%async_computation.9 | async-start | bytes 655360 | tf_op jit(solution)/shard_map/reduce_scatter | solution.py:128
Sparse Core Ops, SparseCore 0:
  44.4 19.1 reduce-scatter.2
  119.4 18.7 reduce-scatter.4
where the time goes:
time: 158 us; the launch traced here: 157 us
  blocking collectives  51.5 us (33%)
  waiting for transfers between devices  47.9 us (30%)
  matrix products  22.3 us (14%)
  between operations  13.6 us (9%)
  starting transfers between devices  9.78 us (6%)
  local copies, waits for them, and re-layouts  6.22 us (4%)
  other arithmetic  5.51 us (3%)
    reduce_scatter x1, waiting for transfers between devices, shards(): lax.psum_scatter(jnp.concatenate([jnp.dot(width_rows, query_weight, prefe...  19.2 us
    reduce_scatter x1, waiting for transfers between devices, shards(): lax.psum_scatter(out_partial, ('gy', 'gz'), scatter_dimension=0, tiled=True)  18.9 us
    all_to_all x1, blocking collectives, shards(): lax.all_to_all(gathered, 'gx', split_axis=1, concat_axis=0, tiled=True)  14.1 us
    all_gather x1, blocking collectives, shards(): lax.all_gather(head_rows, 'gx', axis=0, tiled=True)  13.6 us
    all_to_all x1, blocking collectives, shards(): lax.all_to_all(out_summed, 'gx', split_axis=0, concat_axis=1, tiled=True)  10.1 us
    dot_general x1, matrix products, shards(): jnp.dot(width_rows, query_weight, preferred_element_type=jnp.float32)  8.77 us
    dot_general x1, matrix products, shards(): jnp.dot(lax.all_gather(head_rows, 'gx', axis=0, tiled=True), out_weight,...  8.75 us
    all_gather x1, blocking collectives, shards(): gathered = lax.all_gather(normed, ('gy', 'gz'), axis=0, tiled=True)  7.33 us
  transfers between devices with their start and end apart: 5, of which 5 were waited for; matrix products, arithmetic and copies ran while one was open for 0% of the time, Pallas kernels for 0%

commit v1 on v0

v1 whole, which is shorter than its diff:
```python
import functools

import jax
import jax.numpy as jnp
import numpy as np
from jax import lax
from jax.experimental import pallas as pl
from jax.experimental.pallas import tpu as pltpu
from jax.sharding import PartitionSpec as P

HD = 128
ROW_AXES = ("gx", "gy", "gz")
PLANE = ("gy", "gz")
MIB = 1024 * 1024
IN_VMEM = pl.BlockSpec(memory_space=pltpu.VMEM)
IN_HBM = pl.BlockSpec(memory_space=pl.ANY)
IN_SMEM = pl.BlockSpec(memory_space=pltpu.SMEM)


def norm_kernel(wide, plane, tokens_ref, gain_ref, blocks_ref):
    tokens = tokens_ref[...].astype(jnp.float32)
    mean_square = jnp.mean(tokens * tokens, -1, keepdims=True)
    normed = (tokens * lax.rsqrt(mean_square + 1e-05) * gain_ref[...]).astype(jnp.bfloat16)
    width = normed.shape[1] // wide
    for i in range(wide):
        for j in range(plane):
            blocks_ref[i * plane + j] = normed[:, i * width : (i + 1) * width]


def stream_kernel(count, chunk, rows_ref, *refs):
    weights, sums_ref = refs[:count], refs[count]
    held, sems = refs[count + 1 : 2 * count + 1], refs[2 * count + 1]
    steps = weights[0].shape[0] // chunk

    def copies(s):
        return [
            pltpu.make_async_copy(
                weights[w].at[pl.ds(s * chunk, chunk)],
                held[w].at[pl.ds(s * chunk, chunk)],
                sems.at[w, s],
            )
            for w in range(count)
        ]

    for s in range(steps):
        for copy in copies(s):
            copy.start()
    for s in range(steps):
        part = rows_ref[:, s * chunk : (s + 1) * chunk]
        at = 0
        for w, copy in enumerate(copies(s)):
            copy.wait()
            cols = weights[w].shape[1]
            term = jnp.dot(
                part, held[w][s * chunk : (s + 1) * chunk, :], preferred_element_type=jnp.float32
            )
            if s == 0:
                sums_ref[:, at : at + cols] = term
            else:
                sums_ref[:, at : at + cols] += term
            at += cols


def stream_matmul(rows, weights, chunk):
    depth = rows.shape[1]
    cols = sum(w.shape[1] for w in weights)
    count = len(weights)
    return pl.pallas_call(
        functools.partial(stream_kernel, count, chunk),
        out_shape=jax.ShapeDtypeStruct((rows.shape[0], cols), jnp.float32),
        in_specs=[IN_VMEM] + [IN_HBM] * count,
        out_specs=IN_VMEM,
        scratch_shapes=[pltpu.VMEM(w.shape, w.dtype) for w in weights]
        + [pltpu.SemaphoreType.DMA((count, depth // chunk))],
        compiler_params=pltpu.CompilerParams(vmem_limit_bytes=40 * MIB),
        cost_estimate=pl.CostEstimate(
            flops=2 * rows.shape[0] * depth * cols,
            bytes_accessed=2 * depth * cols,
            transcendentals=0,
        ),
    )(rows, *weights)


def attend_kernel(
    wide, plane, rows, query_cols, kv_cols,
    lengths_ref, partial_ref, frequency_ref, keys_hbm, values_hbm,
    blocks_ref, keys_ref, values_ref, sems,
):
    key_copy = pltpu.make_async_copy(keys_hbm, keys_ref, sems.at[0])
    value_copy = pltpu.make_async_copy(values_hbm, values_ref, sems.at[1])
    key_copy.start()
    value_copy.start()
    slots = keys_ref.shape[1]
    kv_heads = kv_cols // HD
    group = query_cols // kv_cols
    pairs = plane * rows
    scale = 1.0 / HD**0.5
    total = partial_ref[0]
    for i in range(1, wide):
        total = total + partial_ref[i]
    heads = total.astype(jnp.bfloat16).astype(jnp.float32)

    row_of = lax.broadcasted_iota(jnp.int32, (pairs, 1), 0) % rows
    position = jnp.zeros((pairs, 1), jnp.int32)
    for r in range(rows):
        position = jnp.where(row_of == r, lengths_ref[r], position)
    angles = position.astype(jnp.float32) * frequency_ref[...]
    cosine, sine = jnp.cos(angles), jnp.sin(angles)
    front = lax.broadcasted_iota(jnp.int32, (1, HD), 1) < HD // 2
    sine = jnp.where(front, -sine, sine)

    def rotate(vector):
        turned = vector * cosine + pltpu.roll(vector, HD // 2, 1) * sine
        return turned.astype(jnp.bfloat16).astype(jnp.float32)

    query, fresh, value_new = [], [], []
    for h in range(kv_heads):
        turned = jnp.stack(
            [
                rotate(heads[:, (h * group + g) * HD : (h * group + g + 1) * HD])
                for g in range(group)
            ],
            0,
        )
        turned = jnp.swapaxes(turned, 0, 1)
        at = query_cols + h * HD
        key_rot = rotate(heads[:, at : at + HD])
        fresh.append(jnp.sum(turned * key_rot[:, None, :], -1, keepdims=True) * scale)
        query.append(turned.astype(jnp.bfloat16))
        at = query_cols + kv_cols + h * HD
        value_new.append(heads[:, at : at + HD])
    key_copy.wait()
    value_copy.wait()
    slot = lax.broadcasted_iota(jnp.int32, (1, slots), 1)
    attended = []
    for h in range(kv_heads):
        mixed = []
        for p in range(pairs):
            j, r = p // rows, p % rows
            at = (j * kv_heads + h) * HD
            scores = (
                lax.dot_general(
                    query[h][p],
                    keys_ref[r, :, at : at + HD],
                    (((1,), (1,)), ((), ())),
                    preferred_element_type=jnp.float32,
                )
                * scale
            )
            scores = jnp.where(slot < lengths_ref[r], scores, -1e30)
            own = fresh[h][p]
            top = jnp.maximum(jnp.max(scores, -1, keepdims=True), own)
            weights = jnp.exp(scores - top)
            own_weight = jnp.exp(own - top)
            denominator = jnp.sum(weights, -1, keepdims=True) + own_weight
            probability = (weights / denominator).astype(jnp.bfloat16)
            own_prob = (own_weight / denominator).astype(jnp.bfloat16).astype(jnp.float32)
            mix = jnp.dot(
                probability, values_ref[r, :, at : at + HD], preferred_element_type=jnp.float32
            )
            mixed.append(mix + own_prob * value_new[h][p : p + 1])
        by_head = jnp.swapaxes(jnp.stack(mixed, 0), 0, 1)
        attended += [by_head[g] for g in range(group)]
    attended = jnp.concatenate(attended, 1)
    for j in range(plane):
        block = attended[j * rows : (j + 1) * rows].astype(jnp.bfloat16)
        for i in range(wide):
            blocks_ref[i * plane + j] = block


def sum_kernel(terms_ref, sum_ref):
    total = terms_ref[0]
    for j in range(1, terms_ref.shape[0]):
        total = total + terms_ref[j]
    sum_ref[...] = total.astype(sum_ref.dtype)


def swap_blocks(blocks, axes):
    return lax.all_to_all(blocks, axes, split_axis=0, concat_axis=0, tiled=True)


def shards(
    tokens,
    norm_gain,
    query_weight,
    key_weight,
    value_weight,
    out_weight,
    cache_keys,
    cache_values,
    lengths,
):
    rows = tokens.shape[0]
    wide = lax.axis_size("gx")
    plane = lax.axis_size(PLANE)
    owners = wide * plane
    width, query_cols = query_weight.shape
    kv_cols = key_weight.shape[1]
    depth, out_cols = out_weight.shape

    normed = pl.pallas_call(
        functools.partial(norm_kernel, wide, plane),
        out_shape=jax.ShapeDtypeStruct((owners, rows, width), jnp.bfloat16),
        in_specs=[IN_VMEM, IN_VMEM],
        out_specs=IN_VMEM,
    )(tokens, norm_gain.reshape(1, -1))
    all_rows = swap_blocks(normed, ROW_AXES).reshape(owners * rows, width)
    partial = stream_matmul(all_rows, (query_weight, key_weight, value_weight), 256)
    partial = swap_blocks(partial.reshape(owners, rows, -1), ROW_AXES)
    partial = partial.reshape(wide, plane * rows, -1)

    half_dim = HD // 2
    frequency = 500000.0 ** (-np.arange(half_dim, dtype=np.float64) / half_dim)
    frequency = np.tile(frequency.astype(np.float32), 2).reshape(1, HD)
    attended = pl.pallas_call(
        functools.partial(attend_kernel, wide, plane, rows, query_cols, kv_cols),
        out_shape=jax.ShapeDtypeStruct((owners, rows, query_cols), jnp.bfloat16),
        in_specs=[IN_SMEM, IN_VMEM, IN_VMEM, IN_HBM, IN_HBM],
        out_specs=IN_VMEM,
        scratch_shapes=[
            pltpu.VMEM(cache_keys.shape, cache_keys.dtype),
            pltpu.VMEM(cache_values.shape, cache_values.dtype),
            pltpu.SemaphoreType.DMA((2,)),
        ],
        compiler_params=pltpu.CompilerParams(vmem_limit_bytes=16 * MIB),
    )(lengths, partial, jnp.asarray(frequency), cache_keys, cache_values)
    head_rows = swap_blocks(attended, ROW_AXES)
    head_rows = head_rows.reshape(wide, plane, rows, depth).swapaxes(0, 1)
    head_rows = head_rows.reshape(owners * rows, depth)
    out_partial = stream_matmul(head_rows, (out_weight,), 256)
    out_partial = swap_blocks(out_partial.reshape(plane, wide * rows, out_cols), PLANE)
    out_own = pl.pallas_call(
        sum_kernel,
        out_shape=jax.ShapeDtypeStruct((wide * rows, out_cols), jnp.bfloat16),
        in_specs=[IN_VMEM],
        out_specs=IN_VMEM,
    )(out_partial)
    result = swap_blocks(out_own.reshape(wide, rows, out_cols), "gx")
    return result.swapaxes(0, 1).reshape(rows, wide * out_cols)


def solution(mesh):
    placed = (
        P(("groups", "gx", "gy", "gz"), None),
        P(),
        P("gx", ("gy", "gz")),
        P("gx", ("gy", "gz")),
        P("gx", ("gy", "gz")),
        P(("gy", "gz"), "gx"),
        P(("groups", "gx", "gy", "gz"), None, None),
        P(("groups", "gx", "gy", "gz"), None, None),
        P(("groups", "gx", "gy", "gz")),
    )
    return jax.shard_map(
        shards,
        mesh=mesh,
        in_specs=placed,
        out_specs=P(("groups", "gx", "gy", "gz"), None),
        check_vma=False,
    )
```

time: 158 us -> 95 us (0.60)
  waiting for transfers between devices: 47.9 us -> 0 us
  Pallas kernels: 0 us -> 26.7 us
  matrix products: 22.3 us -> 0 us
  between operations: 13.6 us -> 0.1 us
  blocking collectives: 51.5 us -> 62.3 us
  starting transfers between devices: 9.78 us -> 0 us
  other arithmetic: 5.51 us -> 0 us
    reduce_scatter x2 -> x0, waiting for transfers between devices: 38.1 us -> none  [the longest x1 19.2 us: shards(): lax.psum_scatter(jnp.concatenate([jnp.dot(width_rows, query_weight, prefe...]
    all_to_all x3 -> x5, blocking collectives: 30.5 us -> 62.3 us  [swap_blocks(): return lax.all_to_all(blocks, axes, split_axis=0, concat_axis=0, tiled=True)]
    pallas_call x0 -> x5, Pallas kernels: none -> 26.7 us  [the longest x2 16.9 us: stream_matmul(): pl.pallas_call(functools.partial(stream_kernel, count, chunk), out_shape=...]
    dot_general x7 -> x0, matrix products: 22.3 us -> none  [the longest x1 8.77 us: shards(): jnp.dot(width_rows, query_weight, preferred_element_type=jnp.float32)]
    all_gather x2 -> x0, blocking collectives: 21 us -> none  [the longest x1 13.6 us: shards(): lax.all_gather(head_rows, 'gx', axis=0, tiled=True)]
    all_to_all x3 -> x0, waiting for transfers between devices: 9.82 us -> none  [the longest x1 3.75 us: shards(): lax.all_to_all(own_rows[:, :query_cols], ('gy', 'gz'), split_axis=0, conc...]
    all_to_all x3 -> x0, starting transfers between devices: 9.73 us -> none  [the longest x1 3.26 us: shards(): lax.all_to_all(own_rows[:, :query_cols], ('gy', 'gz'), split_axis=0, conc...]
    all_to_all x7 -> x0, local copies, waits for them, and re-layouts: 3.89 us -> none  [the longest x2 1.97 us: shards(): lax.all_to_all(gathered, 'gx', split_axis=1, concat_axis=0, tiled=True)]
  transfers between devices with their start and end apart: 5 -> 0, of which waited for: 5 -> 0; matrix products, arithmetic and copies ran while one was open for 0% -> 0% of each run, Pallas kernels for 0% -> 0%
where the time goes in v1:
time: 95 us; the launch traced here: 94.4 us
  blocking collectives  62.3 us (66%)
  Pallas kernels  26.7 us (28%)
  local copies, waits for them, and re-layouts  5.37 us (6%)
    all_to_all x5, blocking collectives, swap_blocks(): return lax.all_to_all(blocks, axes, split_axis=0, concat_axis=0, tiled=True)  62.3 us
    pallas_call x2, Pallas kernels, stream_matmul(): pl.pallas_call(functools.partial(stream_kernel, count, chunk), out_shape=...  16.9 us
    pallas_call x1, Pallas kernels, shards(): pl.pallas_call(functools.partial(attend_kernel, wide, plane, rows, query_...  6.14 us
    unnamed x13, local copies, waits for them, and re-layouts  3.82 us
    pallas_call x1, Pallas kernels, shards(): pl.pallas_call(functools.partial(norm_kernel, wide, plane), out_shape=jax...  1.95 us

profile of v1, /device:TPU:0, one launch (start us, length us, event | category | flops | bytes accessed | tf_op | source)
XLA Modules:
  0.0 94.4 jit_solution(10751497434221615424)
XLA Ops:
  0.0 0.0 copy-start.5
  0.0 0.0 copy-start.4
  0.0 0.0 copy-start.2
  0.0 2.0 %shard_map.100 = bf16[16,2,4096]{2,1,0:T(2,128)(2,1)} custom-call(bf16[2,16384]{1,0:T(2,128)(2,1)} %tokens_ref.1, f32[1,16384]{1,0:T(1,128)} %bitcast.13), custom_call_target="tpu_custom_call" | custom-call | tf_op jit(solution)/shard_map/pallas_call | solution.py:201
  2.0 17.4 %all_to_all.25 = bf16[16,2,4096]{2,1,0:T(2,128)(2,1)S(1)} all-to-all(bf16[16,2,4096]{2,1,0:T(2,128)(2,1)} %shard_map.100), channel_id=1, replica_groups=mesh['groups'=2,'gx'=4,'gy'=2,'gz'=2] {'gx','gy','gz'}, dimensions={0} | all-to-all | bytes 524288 | tf_op jit(solution)/shard_map/all_to_all | solution.py:179
  19.4 0.1 reshape.28.rows_ref
  19.5 0.0 copy-start
  19.5 1.6 %copy-done = bf16[4096,256]{1,0:T(8,128)(2,1)S(1)} copy-done((bf16[4096,256]{1,0:T(8,128)(2,1)S(1)}, bf16[4096,256]{1,0:T(8,128)(2,1)}, u32[]{:S(2)}) %copy-start) | copy-done | bytes 2097176
  21.1 0.0 copy-start.1
  21.1 1.6 %copy-done.1 = bf16[4096,256]{1,0:T(8,128)(2,1)S(1)} copy-done((bf16[4096,256]{1,0:T(8,128)(2,1)S(1)}, bf16[4096,256]{1,0:T(8,128)(2,1)}, u32[]{:S(2)}) %copy-start.1) | copy-done | bytes 2097176
  22.7 0.0 copy-start.3
  22.7 10.5 %shard_map.101 = f32[32,2560]{1,0:T(8,128)S(1)} custom-call(bf16[32,4096]{1,0:T(8,128)(2,1)S(1)} %reshape.28.rows_ref, bf16[4096,2048]{1,0:T(8,128)(2,1)} %refs_0_.2, bf16[4096,256]{1,0:T(8,128)(2,1)S(1)} %copy-done, bf16[4096,256]{1,0:T(8,128)(2,1)S(1)} %copy-done.1), custom_call_target="tpu_custom_call" | custom-call | flops 671088640 | bytes 20971520 | tf_op jit(solution)/shard_map/pallas_call | solution.py:68
  33.1 0.2 reshape.29
  33.3 13.9 %all_to_all.26 = f32[16,2,2560]{2,1,0:T(2,128)S(1)} all-to-all(f32[16,2,2560]{2,1,0:T(2,128)S(1)} %reshape.29), channel_id=1, replica_groups=mesh['groups'=2,'gx'=4,'gy'=2,'gz'=2] {'gx','gy','gz'}, dimensions={0} | all-to-all | bytes 655360 | tf_op jit(solution)/shard_map/all_to_all | solution.py:179
  47.2 0.2 reshape.30.partial_ref
  47.4 0.0 copy-done.5
  47.5 0.0 copy-done.4
  47.5 0.0 copy-done.2
  47.5 0.0 copy-done.3
  47.5 6.1 %shard_map.102 = bf16[16,2,2048]{2,1,0:T(2,128)(2,1)S(1)} custom-call(s32[2]{0:T(128)S(1)} %copy-done.4, f32[4,8,2560]{2,1,0:T(8,128)S(1)} %reshape.30.partial_ref, f32[1,128]{1,0:T(1,128)S(1)} %copy-done.5, bf16[2,256,1024]{2,1,0:T(8,128)(2,1)S(1)} %copy-done.2, bf16[2,256,1024]{2,1,0:T(8,128)(2,1)S(1)} %copy-done.3), custom_call_target="tpu_custom_call" | custom-call | tf_op jit(solution)/shard_map/pallas_call | solution.py:215
  53.6 11.0 %all_to_all.27 = bf16[16,2,2048]{2,1,0:T(2,128)(2,1)S(1)} all-to-all(bf16[16,2,2048]{2,1,0:T(2,128)(2,1)S(1)} %shard_map.102), channel_id=1, replica_groups=mesh['groups'=2,'gx'=4,'gy'=2,'gz'=2] {'gx','gy','gz'}, dimensions={0} | all-to-all | bytes 262144 | tf_op jit(solution)/shard_map/all_to_all | solution.py:179
  64.6 0.1 copy.14
  64.7 0.1 reshape.32.rows_ref
  64.8 6.4 %shard_map.103 = f32[32,4096]{1,0:T(8,128)S(1)} custom-call(bf16[32,2048]{1,0:T(8,128)(2,1)S(1)} %reshape.32.rows_ref, bf16[2048,4096]{1,0:T(8,128)(2,1)} %refs_0_.3), custom_call_target="tpu_custom_call" | custom-call | flops 536870912 | bytes 16777216 | tf_op jit(solution)/shard_map/pallas_call | solution.py:68
  71.2 11.9 %all_to_all.28.terms_ref = f32[4,8,4096]{2,1,0:T(8,128)} all-to-all(f32[4,8,4096]{2,1,0:T(8,128)S(1)} %bitcast.9), channel_id=1, replica_groups=mesh['groups'=2,'gx'=4,'gy'=2,'gz'=2] {'gy','gz'}, dimensions={0} | all-to-all | bytes 1048576 | tf_op jit(solution)/shard_map/all_to_all | solution.py:179
  83.1 1.7 %shard_map.104 = bf16[8,4096]{1,0:T(8,128)(2,1)} custom-call(f32[4,8,4096]{2,1,0:T(8,128)} %all_to_all.28.terms_ref), custom_call_target="tpu_custom_call" | custom-call | tf_op jit(solution)/shard_map/pallas_call | solution.py:232
  84.8 0.9 reshape.34
  85.7 8.1 %all_to_all.29 = bf16[4,2,4096]{2,1,0:T(2,128)(2,1)S(1)} all-to-all(bf16[4,2,4096]{2,1,0:T(2,128)(2,1)S(1)} %reshape.34), channel_id=1, replica_groups=mesh['groups'=2,'gx'=4,'gy'=2,'gz'=2] {'gx'}, dimensions={0} | all-to-all | bytes 131072 | tf_op jit(solution)/shard_map/all_to_all | solution.py:179
  93.8 0.6 copy.16
Async XLA Ops:
  0.0 47.4 %copy-start.5 = (f32[1,128]{1,0:T(1,128)S(1)}, f32[1,128]{1,0:T(1,128)}, u32[]{:S(2)}) copy-start(f32[1,128]{1,0:T(1,128)} %constant.2.clone.frequency_ref) | copy-start | bytes 1540
  0.0 47.5 %copy-start.4 = (s32[2]{0:T(128)S(1)}, s32[2]{0:T(128)}, u32[]{:S(2)}) copy-start(s32[2]{0:T(128)} %lengths_ref.1) | copy-start | bytes 28
  0.0 47.5 %copy-start.2 = (bf16[2,256,1024]{2,1,0:T(8,128)(2,1)S(1)}, bf16[2,256,1024]{2,1,0:T(8,128)(2,1)}, u32[]{:S(2)}) copy-start(bf16[2,256,1024]{2,1,0:T(8,128)(2,1)} %keys_hbm.1) | copy-start | bytes 3145732
  19.5 1.6 %copy-start = (bf16[4096,256]{1,0:T(8,128)(2,1)S(1)}, bf16[4096,256]{1,0:T(8,128)(2,1)}, u32[]{:S(2)}) copy-start(bf16[4096,256]{1,0:T(8,128)(2,1)} %refs_1_.1) | copy-start | bytes 6291460
  21.1 1.6 %copy-start.1 = (bf16[4096,256]{1,0:T(8,128)(2,1)S(1)}, bf16[4096,256]{1,0:T(8,128)(2,1)}, u32[]{:S(2)}) copy-start(bf16[4096,256]{1,0:T(8,128)(2,1)} %refs_2_.1) | copy-start | bytes 6291460
  22.7 24.8 %copy-start.3 = (bf16[2,256,1024]{2,1,0:T(8,128)(2,1)S(1)}, bf16[2,256,1024]{2,1,0:T(8,128)(2,1)}, u32[]{:S(2)}) copy-start(bf16[2,256,1024]{2,1,0:T(8,128)(2,1)} %values_hbm.1) | copy-start | bytes 3145732

commit v2 on v1

v2 whole, which is shorter than its diff:
```python
import functools

import jax
import jax.numpy as jnp
import numpy as np
from jax import lax
from jax.experimental import pallas as pl
from jax.experimental.pallas import tpu as pltpu
from jax.sharding import PartitionSpec as P

HD = 128
ROW_AXES = ("gx", "gy", "gz")
CHIPS = ("gx", "gy")
PLANE = ("gy", "gz")
MIB = 1024 * 1024
IN_VMEM = pl.BlockSpec(memory_space=pltpu.VMEM)
IN_HBM = pl.BlockSpec(memory_space=pltpu.HBM)
IN_SMEM = pl.BlockSpec(memory_space=pltpu.SMEM)


def norm_kernel(wide, plane, tokens_ref, gain_ref, blocks_ref):
    tokens = tokens_ref[...].astype(jnp.float32)
    mean_square = jnp.mean(tokens * tokens, -1, keepdims=True)
    normed = (tokens * lax.rsqrt(mean_square + 1e-05) * gain_ref[...]).astype(jnp.bfloat16)
    width = normed.shape[1] // wide
    for i in range(wide):
        for j in range(plane):
            blocks_ref[i * plane + j] = normed[:, i * width : (i + 1) * width]


def project_kernel(rows_ref, query_ref, key_ref, value_ref, sums_ref):
    owners, rows, width = rows_ref.shape
    normed = rows_ref[...].reshape(owners * rows, width)
    at = 0
    for weight in (query_ref, key_ref, value_ref):
        cols = weight.shape[1]
        step = min(cols, 256)
        for c in range(0, cols, step):
            part = jnp.dot(normed, weight[:, c : c + step], preferred_element_type=jnp.float32)
            sums_ref[:, :, at : at + step] = part.reshape(owners, rows, step)
            at += step


def attend_kernel(
    wide, plane, rows, query_cols, kv_cols,
    lengths_ref, partial_ref, frequency_ref, keys_ref, values_ref, blocks_ref,
):
    slots = keys_ref.shape[1]
    kv_heads = kv_cols // HD
    all_kv = kv_heads * plane
    group = query_cols // kv_cols
    pairs = plane * rows
    scale = 1.0 / HD**0.5
    total = partial_ref[:plane]
    for i in range(1, wide):
        total = total + partial_ref[i * plane : (i + 1) * plane]
    total = total.reshape(pairs, total.shape[-1])
    heads = total.astype(jnp.bfloat16).astype(jnp.float32)

    row_of = lax.broadcasted_iota(jnp.int32, (pairs, 1), 0) % rows
    position = jnp.zeros((pairs, 1), jnp.int32)
    for r in range(rows):
        position = jnp.where(row_of == r, lengths_ref[r], position)
    angles = position.astype(jnp.float32) * frequency_ref[...]
    cosine, sine = jnp.cos(angles), jnp.sin(angles)
    front = lax.broadcasted_iota(jnp.int32, (1, HD), 1) < HD // 2
    sine = jnp.where(front, -sine, sine)

    def rotate(vector):
        return vector * cosine + pltpu.roll(vector, HD // 2, 1) * sine

    query, key_new, value_new = [], [], []
    for h in range(kv_heads):
        turned = jnp.stack(
            [
                rotate(heads[:, (h * group + g) * HD : (h * group + g + 1) * HD])
                for g in range(group)
            ],
            0,
        )
        query.append(jnp.swapaxes(turned, 0, 1))
        at = query_cols + h * HD
        key_new.append(rotate(heads[:, at : at + HD]))
        at = query_cols + kv_cols + h * HD
        value_new.append(heads[:, at : at + HD])

    def row_vector(parts, r):
        return jnp.concatenate(
            [
                parts[h][j * rows + r : j * rows + r + 1]
                for j in range(plane)
                for h in range(kv_heads)
            ],
            1,
        )

    first = lax.broadcasted_iota(jnp.int32, (16, 1), 0) == 0
    slot = lax.broadcasted_iota(jnp.int32, (slots, 1), 0)
    mixed = [[None] * pairs for h in range(kv_heads)]
    for r in range(rows):
        wide_query = []
        for kv in range(all_kv):
            j, h = kv // kv_heads, kv % kv_heads
            parts = [query[h][j * rows + r]]
            if kv:
                parts.insert(0, jnp.zeros((group, kv * HD), jnp.float32))
            if kv < all_kv - 1:
                parts.append(jnp.zeros((group, (all_kv - 1 - kv) * HD), jnp.float32))
            wide_query.append(jnp.concatenate(parts, 1))
        wide_query = jnp.concatenate(wide_query, 0).astype(jnp.bfloat16)
        contract_lanes = (((1,), (1,)), ((), ()))
        contract_rows = (((0,), (0,)), ((), ()))
        own_key = jnp.where(first, row_vector(key_new, r), 0.0).astype(jnp.bfloat16)
        own_value = jnp.where(first, row_vector(value_new, r), 0.0).astype(jnp.bfloat16)
        scores = scale * lax.dot_general(
            keys_ref[r], wide_query, contract_lanes, preferred_element_type=jnp.float32
        )
        own = scale * lax.dot_general(
            own_key, wide_query, contract_lanes, preferred_element_type=jnp.float32
        )
        scores = jnp.where(slot < lengths_ref[r], scores, -1e30)
        own = own[:1]
        top = jnp.maximum(jnp.max(scores, 0, keepdims=True), own)
        weights = jnp.exp(scores - top)
        own_weight = jnp.exp(own - top)
        denominator = jnp.sum(weights, 0, keepdims=True) + own_weight
        probability = (weights / denominator).astype(jnp.bfloat16)
        own_prob = jnp.where(first, own_weight / denominator, 0.0).astype(jnp.bfloat16)
        mix = lax.dot_general(
            probability, values_ref[r], contract_rows, preferred_element_type=jnp.float32
        )
        mix = mix + lax.dot_general(
            own_prob, own_value, contract_rows, preferred_element_type=jnp.float32
        )
        for kv in range(all_kv):
            mixed[kv % kv_heads][kv // kv_heads * rows + r] = mix[
                kv * group : (kv + 1) * group, kv * HD : (kv + 1) * HD
            ]
    attended = []
    for h in range(kv_heads):
        by_head = jnp.swapaxes(jnp.stack(mixed[h], 0), 0, 1)
        attended += [by_head[g] for g in range(group)]
    attended = jnp.concatenate(attended, 1)
    for j in range(plane):
        block = attended[j * rows : (j + 1) * rows].astype(jnp.bfloat16)
        for i in range(wide):
            blocks_ref[i * plane + j] = block


def output_kernel(core_ref, rows_ref, weight_ref, keep_ref, give_ref):
    owners, rows, depth = rows_ref.shape
    attended = rows_ref[...].reshape(owners * rows, depth)
    mine = core_ref[0] == 0
    cols = weight_ref.shape[1]
    step = min(cols, 512)
    for c in range(0, cols, step):
        part = jnp.dot(attended, weight_ref[:, c : c + step], preferred_element_type=jnp.float32)
        part = part.reshape(owners // 2, 2 * rows, step)
        even, odd = part[:, :rows], part[:, rows:]
        keep_ref[:, :, c : c + step] = jnp.where(mine, even, odd)
        give_ref[:, :, c : c + step] = jnp.where(mine, odd, even)


def add_kernel(a_ref, b_ref, sum_ref):
    sum_ref[...] = a_ref[...] + b_ref[...]


def finish_kernel(wide, terms_ref, result_ref):
    chips, _, cols = terms_ref.shape
    count = chips // wide
    for i in range(wide):
        total = terms_ref[i * count]
        for j in range(1, count):
            total = total + terms_ref[i * count + j]
        result_ref[:, i * cols : (i + 1) * cols] = total.astype(result_ref.dtype)


def swap_blocks(blocks, axes):
    return lax.all_to_all(blocks, axes, split_axis=0, concat_axis=0, tiled=True)


def shards(
    tokens,
    norm_gain,
    query_weight,
    key_weight,
    value_weight,
    out_weight,
    cache_keys,
    cache_values,
    lengths,
):
    rows = tokens.shape[0]
    wide = lax.axis_size("gx")
    plane = lax.axis_size(PLANE)
    owners = wide * plane
    width, query_cols = query_weight.shape
    kv_cols = key_weight.shape[1]
    depth, out_cols = out_weight.shape
    cols = query_cols + 2 * kv_cols

    def params(mib):
        return pltpu.CompilerParams(vmem_limit_bytes=mib * MIB)

    def cost(flops, size):
        return pl.CostEstimate(flops=flops, bytes_accessed=size, transcendentals=0)

    normed = pl.pallas_call(
        functools.partial(norm_kernel, wide, plane),
        out_shape=jax.ShapeDtypeStruct((owners, rows, width), jnp.bfloat16),
        in_specs=[IN_VMEM, IN_VMEM],
        out_specs=IN_VMEM,
        compiler_params=params(8),
        cost_estimate=cost(40 * 10**9, MIB),
    )(tokens, norm_gain.reshape(1, -1))
    all_rows = swap_blocks(normed, ROW_AXES)
    partial = pl.pallas_call(
        project_kernel,
        out_shape=jax.ShapeDtypeStruct((owners, rows, cols), jnp.float32),
        in_specs=[IN_VMEM] * 4,
        out_specs=IN_VMEM,
        compiler_params=params(8),
        cost_estimate=cost(2 * owners * rows * width * cols, 2 * width * cols),
    )(all_rows, query_weight, key_weight, value_weight)
    partial = swap_blocks(partial, ROW_AXES)

    half_dim = HD // 2
    frequency = 500000.0 ** (-np.arange(half_dim, dtype=np.float64) / half_dim)
    frequency = np.tile(frequency.astype(np.float32), 2).reshape(1, HD)
    attended = pl.pallas_call(
        functools.partial(attend_kernel, wide, plane, rows, query_cols, kv_cols),
        out_shape=jax.ShapeDtypeStruct((owners, rows, query_cols), jnp.bfloat16),
        in_specs=[IN_SMEM] + [IN_VMEM] * 4,
        out_specs=IN_VMEM,
        compiler_params=params(8),
        cost_estimate=cost(10**9, 4 * MIB),
    )(lengths, partial, jnp.asarray(frequency), cache_keys, cache_values)
    head_rows = swap_blocks(attended, ROW_AXES)
    half = jax.ShapeDtypeStruct((owners // 2, rows, out_cols), jnp.float32)
    keep, give = pl.pallas_call(
        output_kernel,
        out_shape=(half, half),
        in_specs=[IN_SMEM, IN_VMEM, IN_VMEM],
        out_specs=(IN_VMEM, IN_VMEM),
        compiler_params=params(8),
        cost_estimate=cost(2 * owners * rows * depth * out_cols, 2 * depth * out_cols),
    )(lax.axis_index("gz").reshape(1), head_rows, out_weight)
    given = lax.ppermute(give, "gz", [(0, 1), (1, 0)])
    by_core = pl.pallas_call(
        add_kernel, out_shape=half, in_specs=[IN_VMEM, IN_VMEM], out_specs=IN_VMEM
    )(keep, given)
    terms = swap_blocks(by_core, CHIPS)
    return pl.pallas_call(
        functools.partial(finish_kernel, wide),
        out_shape=jax.ShapeDtypeStruct((rows, wide * out_cols), jnp.bfloat16),
        in_specs=[IN_VMEM],
        out_specs=IN_VMEM,
    )(terms)


def solution(mesh):
    placed = (
        P(("groups", "gx", "gy", "gz"), None),
        P(),
        P("gx", ("gy", "gz")),
        P("gx", ("gy", "gz")),
        P("gx", ("gy", "gz")),
        P(("gy", "gz"), "gx"),
        P(("groups", "gx", "gy", "gz"), None, None),
        P(("groups", "gx", "gy", "gz"), None, None),
        P(("groups", "gx", "gy", "gz")),
    )
    return jax.shard_map(
        shards,
        mesh=mesh,
        in_specs=placed,
        out_specs=P(("groups", "gx", "gy", "gz"), None),
        check_vma=False,
    )
```

time: 95 us -> 80.6 us (0.85)
  blocking collectives: 62.3 us -> 44.9 us
  Pallas kernels: 26.7 us -> 13.3 us
  waiting for transfers between devices: 0 us -> 9.43 us
  local copies, waits for them, and re-layouts: 5.37 us -> 8.89 us
  starting transfers between devices: 0 us -> 3.51 us
    all_to_all x5 -> x3, blocking collectives: 62.3 us -> 44.9 us  [swap_blocks(): return lax.all_to_all(blocks, axes, split_axis=0, concat_axis=0, tiled=True)]
    pallas_call x3 -> x4, Pallas kernels: 18.6 us -> 10.1 us  [the longest x1 3.72 us: shards(): pl.pallas_call(project_kernel, out_shape=jax.ShapeDtypeStruct((owners, ro...]
    all_to_all x0 -> x1, waiting for transfers between devices: none -> 7.89 us  [swap_blocks(): return lax.all_to_all(blocks, axes, split_axis=0, concat_axis=0, tiled=True)]
    unnamed x13 -> x24, local copies, waits for them, and re-layouts: 3.82 us -> 8.89 us
    all_to_all x0 -> x1, starting transfers between devices: none -> 3.51 us  [swap_blocks(): return lax.all_to_all(blocks, axes, split_axis=0, concat_axis=0, tiled=True)]
    pallas_call x1, Pallas kernels: 6.14 us -> 2.9 us  [shards(): pl.pallas_call(functools.partial(attend_kernel, wide, plane, rows, query_...]
    pallas_call x1, Pallas kernels: 1.95 us -> 0.29 us  [shards(): pl.pallas_call(functools.partial(norm_kernel, wide, plane), out_shape=jax...]
    reshape x6 -> x0, local copies, waits for them, and re-layouts: 1.55 us -> none  [the longest x1 0.89 us: shards(): result = swap_blocks(out_own.reshape(wide, rows, out_cols), 'gx')]
  transfers between devices with their start and end apart: 0 -> 2, of which waited for: 0 -> 2; matrix products, arithmetic and copies ran while one was open for 0% -> 0% of each run, Pallas kernels for 0% -> 0%
where the time goes in v2:
time: 80.6 us; the launch traced here: 80.1 us
  blocking collectives  44.9 us (56%)
  Pallas kernels  13.3 us (17%)
  waiting for transfers between devices  9.43 us (12%)
  local copies, waits for them, and re-layouts  8.89 us (11%)
  starting transfers between devices  3.51 us (4%)
    all_to_all x3, blocking collectives, swap_blocks(): return lax.all_to_all(blocks, axes, split_axis=0, concat_axis=0, tiled=True)  44.9 us
    unnamed x24, local copies, waits for them, and re-layouts  8.89 us
    all_to_all x1, waiting for transfers between devices, swap_blocks(): return lax.all_to_all(blocks, axes, split_axis=0, concat_axis=0, tiled=True)  7.89 us
    pallas_call x1, Pallas kernels, shards(): pl.pallas_call(project_kernel, out_shape=jax.ShapeDtypeStruct((owners, ro...  3.72 us
    all_to_all x1, starting transfers between devices, swap_blocks(): return lax.all_to_all(blocks, axes, split_axis=0, concat_axis=0, tiled=True)  3.51 us
    pallas_call x1, Pallas kernels, shards(): pl.pallas_call(output_kernel, out_shape=(half, half), in_specs=[IN_SMEM,...  3.01 us
    pallas_call x1, Pallas kernels, shards(): pl.pallas_call(functools.partial(attend_kernel, wide, plane, rows, query_...  2.9 us
    pallas_call x1, Pallas kernels, shards(): pl.pallas_call(add_kernel, out_shape=half, in_specs=[IN_VMEM, IN_VMEM], o...  1.76 us
  transfers between devices with their start and end apart: 2, of which 2 were waited for; matrix products, arithmetic and copies ran while one was open for 0% of the time, Pallas kernels for 0%

profile of v2, /device:TPU:0, one launch (start us, length us, event | category | flops | bytes accessed | tf_op | source)
XLA Modules:
  0.0 80.1 jit_solution(3475571323262069306)
XLA Ops:
  0.0 0.0 copy-start.7
  0.0 0.8 %copy-done.7 = bf16[2,16384]{1,0:T(2,128)(2,1)S(1)} copy-done((bf16[2,16384]{1,0:T(2,128)(2,1)S(1)}, bf16[2,16384]{1,0:T(2,128)(2,1)}, u32[]{:S(2)}) %copy-start.7) | copy-done | bytes 65560
  0.8 0.0 copy-start.8
  0.8 0.8 %copy-done.8 = f32[16384]{0:T(1024)S(1)} copy-done((f32[16384]{0:T(1024)S(1)}, f32[16384]{0:T(1024)}, u32[]{:S(2)}) %copy-start.8) | copy-done | bytes 65560
  1.7 0.0 copy-start.1
  1.7 0.0 copy-start.2
  1.7 0.0 copy-start.3
  1.7 0.3 shard_map.100
  2.0 0.0 copy-start.5
  2.0 0.0 copy-start.6
  2.0 0.0 copy-start.9
  2.0 0.0 copy-start.10
  2.0 17.5 %all_to_all.20.rows_ref = bf16[16,2,4096]{2,1,0:T(2,128)(2,1)S(1)} all-to-all(bf16[16,2,4096]{2,1,0:T(2,128)(2,1)S(1)} %shard_map.100), channel_id=1, replica_groups=mesh['groups'=2,'gx'=4,'gy'=2,'gz'=2] {'gx','gy','gz'}, dimensions={0} | all-to-all | bytes 524288 | tf_op jit(solution)/shard_map/all_to_all | solution.py:179
  19.5 0.0 copy-done.1
  19.5 0.0 copy-done.2
  19.5 0.0 copy-done.3
  19.5 3.7 %shard_map.101 = f32[16,2,2560]{2,1,0:T(2,128)S(1)} custom-call(bf16[16,2,4096]{2,1,0:T(2,128)(2,1)S(1)} %all_to_all.20.rows_ref, bf16[4096,2048]{1,0:T(8,128)(2,1)S(1)} %copy-done.1, bf16[4096,256]{1,0:T(8,128)(2,1)S(1)} %copy-done.2, bf16[4096,256]{1,0:T(8,128)(2,1)S(1)} %copy-done.3), custom_call_target="tpu_custom_call" | custom-call | flops 671088640 | bytes 20971520 | tf_op jit(solution)/shard_map/pallas_call | solution.py:217
  23.2 13.9 %all_to_all.21.partial_ref = f32[16,2,2560]{2,1,0:T(2,128)S(1)} all-to-all(f32[16,2,2560]{2,1,0:T(2,128)S(1)} %shard_map.101), channel_id=1, replica_groups=mesh['groups'=2,'gx'=4,'gy'=2,'gz'=2] {'gx','gy','gz'}, dimensions={0} | all-to-all | bytes 655360 | tf_op jit(solution)/shard_map/all_to_all | solution.py:179
  37.1 0.0 copy-done.5
  37.1 0.0 copy-done.6
  37.1 0.0 copy-done.9
  37.1 0.0 copy-done.10
  37.1 2.9 %shard_map.102 = bf16[16,2,2048]{2,1,0:T(2,128)(2,1)} custom-call(s32[2]{0:T(128)S(1)} %copy-done.9, f32[16,2,2560]{2,1,0:T(2,128)S(1)} %all_to_all.21.partial_ref, f32[1,128]{1,0:T(1,128)S(1)} %copy-done.10, bf16[2,256,1024]{2,1,0:T(8,128)(2,1)S(1)} %copy-done.5, bf16[2,256,1024]{2,1,0:T(8,128)(2,1)S(1)} %copy-done.6), custom_call_target="tpu_custom_call" | custom-call | flops 1000000000 | bytes 4194304 | tf_op jit(solution)/shard_map/pallas_call | solution.py:230
  40.0 3.5 %all-to-all-start.2 = ((bf16[16,2,2048]{2,1,0:T(2,128)(2,1)}), bf16[16,2,2048]{2,1,0:T(2,128)(2,1)S(1)}, u32[]{:S(2)}, u32[]{:S(2)}) async-start(bf16[16,2,2048]{2,1,0:T(2,128)(2,1)} %shard_map.102), calls=%async_computation.2 | async-start | bytes 262144 | tf_op jit(solution)/shard_map/all_to_all | solution.py:179
  43.6 7.9 %all-to-all-done.2.rows_ref = bf16[16,2,2048]{2,1,0:T(2,128)(2,1)S(1)} async-done(((bf16[16,2,2048]{2,1,0:T(2,128)(2,1)}), bf16[16,2,2048]{2,1,0:T(2,128)(2,1)S(1)}, u32[]{:S(2)}, u32[]{:S(2)}) %all-to-all-start.2) | async-done | bytes 131104 | tf_op jit(solution)/shard_map/all_to_all | solution.py:179
  51.5 0.0 copy-start
  51.5 5.8 %copy-done = bf16[2048,4096]{1,0:T(8,128)(2,1)S(1)} copy-done((bf16[2048,4096]{1,0:T(8,128)(2,1)S(1)}, bf16[2048,4096]{1,0:T(8,128)(2,1)}, u32[]{:S(2)}) %copy-start) | copy-done | bytes 16777240
  57.2 3.0 %shard_map.103 = (f32[8,2,4096]{2,1,0:T(2,128)S(1)}, f32[8,2,4096]{2,1,0:T(2,128)S(1)}) custom-call(s32[1]{0:T(128)} %bitcast.core_ref, bf16[16,2,2048]{2,1,0:T(2,128)(2,1)S(1)} %all-to-all-done.2.rows_ref, bf16[2048,4096]{1,0:T(8,128)(2,1)S(1)} %copy-done), custom_call_target="tpu_custom_call" | custom-call | flops 536870912 | bytes 16777216 | tf_op jit(solution)/shard_map/pallas_call | solution.py:240
  60.2 0.0 copy-start.4
  60.3 0.7 copy-done.4
  60.9 0.0 collective-permute-start
  61.0 1.5 %collective-permute-done.b_ref = f32[8,2,4096]{2,1,0:T(2,128)S(1)} collective-permute-done((f32[8,2,4096]{2,1,0:T(2,128)S(1)}, f32[8,2,4096]{2,1,0:T(2,128)S(1)}, u32[]{:S(2)}, u32[]{:S(2)}) %collective-permute-start) | collective-permute-done | bytes 262176 | tf_op jit(solution)/shard_map/ppermute | solution.py:248
  62.5 0.0 copy-start.11
  62.5 0.7 copy-done.11
  63.2 1.8 %shard_map.104 = f32[8,2,4096]{2,1,0:T(2,128)} custom-call(f32[8,2,4096]{2,1,0:T(2,128)} %copy-done.4, f32[8,2,4096]{2,1,0:T(2,128)} %copy-done.11), custom_call_target="tpu_custom_call" | custom-call | tf_op jit(solution)/shard_map/pallas_call | solution.py:249
  65.0 13.5 %all_to_all.22.terms_ref = f32[8,2,4096]{2,1,0:T(2,128)} all-to-all(f32[8,2,4096]{2,1,0:T(2,128)} %shard_map.104), channel_id=1, replica_groups=mesh['groups'=2,'gx'=4,'gy'=2,'gz'=2] {'gx','gy'}, dimensions={0} | all-to-all | bytes 524288 | tf_op jit(solution)/shard_map/all_to_all | solution.py:179
  78.5 1.6 %shard_map.105 = bf16[2,16384]{1,0:T(2,128)(2,1)} custom-call(f32[8,2,4096]{2,1,0:T(2,128)} %all_to_all.22.terms_ref), custom_call_target="tpu_custom_call" | custom-call | tf_op jit(solution)/shard_map/pallas_call | solution.py:253
Async XLA Ops:
  0.0 0.8 %copy-start.7 = (bf16[2,16384]{1,0:T(2,128)(2,1)S(1)}, bf16[2,16384]{1,0:T(2,128)(2,1)}, u32[]{:S(2)}) copy-start(bf16[2,16384]{1,0:T(2,128)(2,1)} %tokens_ref.1) | copy-start | bytes 196612
  0.8 0.8 %copy-start.8 = (f32[16384]{0:T(1024)S(1)}, f32[16384]{0:T(1024)}, u32[]{:S(2)}) copy-start(f32[16384]{0:T(1024)} %param.11) | copy-start | bytes 196612
  1.7 17.8 %copy-start.1 = (bf16[4096,2048]{1,0:T(8,128)(2,1)S(1)}, bf16[4096,2048]{1,0:T(8,128)(2,1)}, u32[]{:S(2)}) copy-start(bf16[4096,2048]{1,0:T(8,128)(2,1)} %query_ref.1) | copy-start | bytes 50331652
  1.7 17.8 %copy-start.2 = (bf16[4096,256]{1,0:T(8,128)(2,1)S(1)}, bf16[4096,256]{1,0:T(8,128)(2,1)}, u32[]{:S(2)}) copy-start(bf16[4096,256]{1,0:T(8,128)(2,1)} %key_ref.1) | copy-start | bytes 6291460
  1.7 17.8 %copy-start.3 = (bf16[4096,256]{1,0:T(8,128)(2,1)S(1)}, bf16[4096,256]{1,0:T(8,128)(2,1)}, u32[]{:S(2)}) copy-start(bf16[4096,256]{1,0:T(8,128)(2,1)} %value_ref.1) | copy-start | bytes 6291460
  2.0 35.1 %copy-start.5 = (bf16[2,256,1024]{2,1,0:T(8,128)(2,1)S(1)}, bf16[2,256,1024]{2,1,0:T(8,128)(2,1)}, u32[]{:S(2)}) copy-start(bf16[2,256,1024]{2,1,0:T(8,128)(2,1)} %keys_ref.1) | copy-start | bytes 3145732
  2.0 35.1 %copy-start.6 = (bf16[2,256,1024]{2,1,0:T(8,128)(2,1)S(1)}, bf16[2,256,1024]{2,1,0:T(8,128)(2,1)}, u32[]{:S(2)}) copy-start(bf16[2,256,1024]{2,1,0:T(8,128)(2,1)} %values_ref.1) | copy-start | bytes 3145732
  2.0 35.1 %copy-start.9 = (s32[2]{0:T(128)S(1)}, s32[2]{0:T(128)}, u32[]{:S(2)}) copy-start(s32[2]{0:T(128)} %lengths_ref.1) | copy-start | bytes 28
  2.0 35.1 %copy-start.10 = (f32[1,128]{1,0:T(1,128)S(1)}, f32[1,128]{1,0:T(1,128)}, u32[]{:S(2)}) copy-start(f32[1,128]{1,0:T(1,128)} %constant.6.clone.frequency_ref) | copy-start | bytes 1540
  40.0 11.4 %all-to-all-start.2 = ((bf16[16,2,2048]{2,1,0:T(2,128)(2,1)}), bf16[16,2,2048]{2,1,0:T(2,128)(2,1)S(1)}, u32[]{:S(2)}, u32[]{:S(2)}) async-start(bf16[16,2,2048]{2,1,0:T(2,128)(2,1)} %shard_map.102), calls=%async_computation.2 | async-start | bytes 262144 | tf_op jit(solution)/shard_map/all_to_all | solution.py:179
  51.5 5.8 %copy-start = (bf16[2048,4096]{1,0:T(8,128)(2,1)S(1)}, bf16[2048,4096]{1,0:T(8,128)(2,1)}, u32[]{:S(2)}) copy-start(bf16[2048,4096]{1,0:T(8,128)(2,1)} %weight_ref.1) | copy-start | bytes 50331652
  60.2 0.7 copy-start.4
  60.9 1.5 %collective-permute-start = (f32[8,2,4096]{2,1,0:T(2,128)S(1)}, f32[8,2,4096]{2,1,0:T(2,128)S(1)}, u32[]{:S(2)}, u32[]{:S(2)}) collective-permute-start(f32[8,2,4096]{2,1,0:T(2,128)S(1)} %get-tuple-element.8), channel_id=1, source_target_pairs={{0,1},{1,0},{2,3},{3,2},{4,5},{5,4},{6,7},{7,6},{8,9},{9,8},{10,11... | collective-permute-start | bytes 786440 | tf_op jit(solution)/shard_map/ppermute | solution.py:248
  62.5 0.7 copy-start.11

commit v3 on v2

--- a/solution.py
+++ b/solution.py
@@ -14,7 +14,6 @@
 PLANE = ("gy", "gz")
 MIB = 1024 * 1024
 IN_VMEM = pl.BlockSpec(memory_space=pltpu.VMEM)
-IN_HBM = pl.BlockSpec(memory_space=pltpu.HBM)
 IN_SMEM = pl.BlockSpec(memory_space=pltpu.SMEM)
 
 
@@ -22,22 +21,34 @@
     tokens = tokens_ref[...].astype(jnp.float32)
     mean_square = jnp.mean(tokens * tokens, -1, keepdims=True)
     normed = (tokens * lax.rsqrt(mean_square + 1e-05) * gain_ref[...]).astype(jnp.bfloat16)
-    width = normed.shape[1] // wide
+    half = normed.shape[1] // wide // 2
     for i in range(wide):
         for j in range(plane):
-            blocks_ref[i * plane + j] = normed[:, i * width : (i + 1) * width]
-
-
-def project_kernel(rows_ref, query_ref, key_ref, value_ref, sums_ref):
-    owners, rows, width = rows_ref.shape
-    normed = rows_ref[...].reshape(owners * rows, width)
+            at = (2 * i + j % 2) * half
+            blocks_ref[i * plane + j] = normed[:, at : at + half]
+
+
+def project_kernel(own, rows_ref, query_ref, key_ref, value_ref, *refs):
+    sums_ref = refs[-1]
+    owners, rows, half = rows_ref.shape
+    core = lax.axis_index("gz")
+    at_row = pl.multiple_of((core if own else 1 - core) * half, half)
+    normed = rows_ref[...].reshape(owners * rows, half)
     at = 0
     for weight in (query_ref, key_ref, value_ref):
         cols = weight.shape[1]
         step = min(cols, 256)
         for c in range(0, cols, step):
-            part = jnp.dot(normed, weight[:, c : c + step], preferred_element_type=jnp.float32)
-            sums_ref[:, :, at : at + step] = part.reshape(owners, rows, step)
+            part = jnp.dot(
+                normed,
+                weight[pl.ds(at_row, half), c : c + step],
+                preferred_element_type=jnp.float32,
+            )
+            if own:
+                sums_ref[:, at : at + step] = part
+            else:
+                part = part + refs[0][:, at : at + step]
+                sums_ref[:, :, at : at + step] = part.reshape(owners, rows, step)
             at += step
 
 
@@ -147,10 +158,10 @@
             blocks_ref[i * plane + j] = block
 
 
-def output_kernel(core_ref, rows_ref, weight_ref, keep_ref, give_ref):
+def output_kernel(rows_ref, weight_ref, keep_ref, give_ref):
     owners, rows, depth = rows_ref.shape
     attended = rows_ref[...].reshape(owners * rows, depth)
-    mine = core_ref[0] == 0
+    mine = lax.axis_index("gz") == 0
     cols = weight_ref.shape[1]
     step = min(cols, 512)
     for c in range(0, cols, step):
@@ -177,6 +188,10 @@
 
 def swap_blocks(blocks, axes):
     return lax.all_to_all(blocks, axes, split_axis=0, concat_axis=0, tiled=True)
+
+
+def swap_cores(value):
+    return lax.ppermute(value, "gz", [(0, 1), (1, 0)])
 
 
 def shards(
@@ -205,23 +220,35 @@
     def cost(flops, size):
         return pl.CostEstimate(flops=flops, bytes_accessed=size, transcendentals=0)
 
+    half = width // 2
     normed = pl.pallas_call(
         functools.partial(norm_kernel, wide, plane),
-        out_shape=jax.ShapeDtypeStruct((owners, rows, width), jnp.bfloat16),
+        out_shape=jax.ShapeDtypeStruct((owners, rows, half), jnp.bfloat16),
         in_specs=[IN_VMEM, IN_VMEM],
         out_specs=IN_VMEM,
         compiler_params=params(8),
         cost_estimate=cost(40 * 10**9, MIB),
     )(tokens, norm_gain.reshape(1, -1))
-    all_rows = swap_blocks(normed, ROW_AXES)
+    own_half = swap_blocks(normed, ROW_AXES)
+    other_half = swap_cores(own_half)
+    weights = (query_weight, key_weight, value_weight)
+    half_cost = cost(owners * rows * width * cols, width * cols)
     partial = pl.pallas_call(
-        project_kernel,
+        functools.partial(project_kernel, True),
+        out_shape=jax.ShapeDtypeStruct((owners * rows, cols), jnp.float32),
+        in_specs=[IN_VMEM] * 4,
+        out_specs=IN_VMEM,
+        compiler_params=params(8),
+        cost_estimate=half_cost,
+    )(own_half, *weights)
+    partial = pl.pallas_call(
+        functools.partial(project_kernel, False),
         out_shape=jax.ShapeDtypeStruct((owners, rows, cols), jnp.float32),
-        in_specs=[IN_VMEM] * 4,
-        out_specs=IN_VMEM,
-        compiler_params=params(8),
-        cost_estimate=cost(2 * owners * rows * width * cols, 2 * width * cols),
-    )(all_rows, query_weight, key_weight, value_weight)
+        in_specs=[IN_VMEM] * 5,
+        out_specs=IN_VMEM,
+        compiler_params=params(8),
+        cost_estimate=half_cost,
+    )(other_half, *weights, partial)
     partial = swap_blocks(partial, ROW_AXES)
 
     half_dim = HD // 2
@@ -236,18 +263,22 @@
         cost_estimate=cost(10**9, 4 * MIB),
     )(lengths, partial, jnp.asarray(frequency), cache_keys, cache_values)
     head_rows = swap_blocks(attended, ROW_AXES)
-    half = jax.ShapeDtypeStruct((owners // 2, rows, out_cols), jnp.float32)
+    by_chip = jax.ShapeDtypeStruct((owners // 2, rows, out_cols), jnp.float32)
     keep, give = pl.pallas_call(
         output_kernel,
-        out_shape=(half, half),
-        in_specs=[IN_SMEM, IN_VMEM, IN_VMEM],
+        out_shape=(by_chip, by_chip),
+        in_specs=[IN_VMEM, IN_VMEM],
         out_specs=(IN_VMEM, IN_VMEM),
         compiler_params=params(8),
         cost_estimate=cost(2 * owners * rows * depth * out_cols, 2 * depth * out_cols),
-    )(lax.axis_index("gz").reshape(1), head_rows, out_weight)
-    given = lax.ppermute(give, "gz", [(0, 1), (1, 0)])
+    )(head_rows, out_weight)
+    given = swap_cores(give)
     by_core = pl.pallas_call(
-        add_kernel, out_shape=half, in_specs=[IN_VMEM, IN_VMEM], out_specs=IN_VMEM
+        add_kernel,
+        out_shape=by_chip,
+        in_specs=[IN_VMEM, IN_VMEM],
+        out_specs=IN_VMEM,
+        compiler_params=params(8),
     )(keep, given)
     terms = swap_blocks(by_core, CHIPS)
     return pl.pallas_call(
@@ -255,6 +286,7 @@
         out_shape=jax.ShapeDtypeStruct((rows, wide * out_cols), jnp.bfloat16),
         in_specs=[IN_VMEM],
         out_specs=IN_VMEM,
+        compiler_params=params(8),
     )(terms)
 
 

time: 80.6 us -> 66.1 us (0.82)
  waiting for transfers between devices: 9.43 us -> 1.53 us
  blocking collectives: 44.9 us -> 52.2 us
  local copies, waits for them, and re-layouts: 8.89 us -> 1.72 us
  starting transfers between devices: 3.51 us -> 0.14 us
  Pallas kernels: 13.3 us -> 10.1 us
    all_to_all x1 -> x0, waiting for transfers between devices: 7.89 us -> none  [swap_blocks(): return lax.all_to_all(blocks, axes, split_axis=0, concat_axis=0, tiled=True)]
    all_to_all x3 -> x4, blocking collectives: 44.9 us -> 52.2 us  [swap_blocks(): return lax.all_to_all(blocks, axes, split_axis=0, concat_axis=0, tiled=True)]
    unnamed x24 -> x26, local copies, waits for them, and re-layouts: 8.89 us -> 1.72 us
    all_to_all x1 -> x0, starting transfers between devices: 3.51 us -> none  [swap_blocks(): return lax.all_to_all(blocks, axes, split_axis=0, concat_axis=0, tiled=True)]
    pallas_call x3 -> x4, Pallas kernels: 8.49 us -> 6.88 us  [the longest x1 3.02 us: shards(): pl.pallas_call(output_kernel, out_shape=(by_chip, by_chip), in_specs=[IN_...]
    pallas_call x1, Pallas kernels: 1.64 us -> 0.69 us  [shards(): pl.pallas_call(functools.partial(finish_kernel, wide), out_shape=jax.Shap...]
  transfers between devices with their start and end apart: 2 -> 2, of which waited for: 2 -> 1; matrix products, arithmetic and copies ran while one was open for 0% -> 0% of each run, Pallas kernels for 0% -> 3%
where the time goes in v3:
time: 66.1 us; the launch traced here: 65.8 us
  blocking collectives  52.2 us (79%)
  Pallas kernels  10.1 us (15%)
  local copies, waits for them, and re-layouts  1.72 us (3%)
  waiting for transfers between devices  1.53 us (2%)
    all_to_all x4, blocking collectives, swap_blocks(): return lax.all_to_all(blocks, axes, split_axis=0, concat_axis=0, tiled=True)  52.2 us
    pallas_call x1, Pallas kernels, shards(): pl.pallas_call(output_kernel, out_shape=(by_chip, by_chip), in_specs=[IN_...  3.02 us
    pallas_call x1, Pallas kernels, shards(): pl.pallas_call(functools.partial(attend_kernel, wide, plane, rows, query_...  2.24 us
    pallas_call x1, Pallas kernels, shards(): pl.pallas_call(functools.partial(project_kernel, False), out_shape=jax.Sh...  1.94 us
    pallas_call x1, Pallas kernels, shards(): pl.pallas_call(functools.partial(project_kernel, True), out_shape=jax.Sha...  1.89 us
    unnamed x26, local copies, waits for them, and re-layouts  1.72 us
    ppermute x2, waiting for transfers between devices, swap_cores(): return lax.ppermute(value, 'gz', [(0, 1), (1, 0)])  1.53 us
  transfers between devices with their start and end apart: 2, of which 1 were waited for; matrix products, arithmetic and copies ran while one was open for 0% of the time, Pallas kernels for 3%

profile of v3, /device:TPU:0, one launch (start us, length us, event | category | flops | bytes accessed | tf_op | source)
XLA Modules:
  0.0 65.8 jit_solution(15940355377850857459)
XLA Ops:
  0.0 0.0 copy-start.5
  0.0 0.8 %copy-done.5 = bf16[2,16384]{1,0:T(2,128)(2,1)S(1)} copy-done((bf16[2,16384]{1,0:T(2,128)(2,1)S(1)}, bf16[2,16384]{1,0:T(2,128)(2,1)}, u32[]{:S(2)}) %copy-start.5) | copy-done | bytes 65560
  0.8 0.0 copy-start.6
  0.8 0.8 %copy-done.6 = f32[16384]{0:T(1024)S(1)} copy-done((f32[16384]{0:T(1024)S(1)}, f32[16384]{0:T(1024)}, u32[]{:S(2)}) %copy-start.6) | copy-done | bytes 65560
  1.7 0.0 copy-start
  1.7 0.0 copy-start.1
  1.7 0.0 copy-start.2
  1.7 0.3 shard_map.100
  2.0 15.4 %all_to_all.20.rows_ref = bf16[16,2,2048]{2,1,0:T(2,128)(2,1)S(1)} all-to-all(bf16[16,2,2048]{2,1,0:T(2,128)(2,1)S(1)} %shard_map.100), channel_id=1, replica_groups=mesh['groups'=2,'gx'=4,'gy'=2,'gz'=2] {'gx','gy','gz'}, dimensions={0} | all-to-all | bytes 262144 | tf_op jit(solution)/shard_map/all_to_all | solution.py:190
  17.3 0.0 copy-start.3
  17.3 0.0 copy-start.4
  17.3 0.0 copy-start.7
  17.3 0.0 copy-start.8
  17.3 0.1 collective-permute-start
  17.4 0.0 copy-done
  17.4 0.0 copy-done.1
  17.4 0.0 copy-done.2
  17.5 0.0 slice-start
  17.5 0.0 slice-start.1
  17.5 1.9 %shard_map.101.refs_0_ = f32[32,2560]{1,0:T(8,128)S(1)} custom-call(bf16[16,2,2048]{2,1,0:T(2,128)(2,1)S(1)} %all_to_all.20.rows_ref, bf16[4096,2048]{1,0:T(8,128)(2,1)S(1)} %copy-done, bf16[4096,256]{1,0:T(8,128)(2,1)S(1)} %copy-done.1, bf16[4096,256]{1,0:T(8,128)(2,1)S(1)} %copy-done.2), custom_call_target="tpu_custom_call" | custom-call | flops 335544320 | bytes 10485760 | tf_op jit(solution)/shard_map/pallas_call | solution.py:236
  19.4 0.0 slice-start.2
  19.4 0.0 slice-start.3
  19.4 0.0 collective-permute-done.rows_ref
  19.4 1.9 %shard_map.102 = f32[16,2,2560]{2,1,0:T(2,128)S(1)} custom-call(bf16[16,2,2048]{2,1,0:T(2,128)(2,1)S(1)} %collective-permute-done.rows_ref, bf16[4096,2048]{1,0:T(8,128)(2,1)S(1)} %copy-done, bf16[4096,256]{1,0:T(8,128)(2,1)S(1)} %copy-done.1, bf16[4096,256]{1,0:T(8,128)(2,1)S(1)} %copy-done.2, f32[32,2560]{1,0:T(8,128)S(1)} %shard_map.101.refs_0_), custom_call_target="tpu_custom_call" | custom-call | flops 335544320 | bytes 10485760 | tf_op jit(solution)/shard_map/pallas_call | solution.py:244
  21.4 14.0 %all_to_all.21.partial_ref = f32[16,2,2560]{2,1,0:T(2,128)S(1)} all-to-all(f32[16,2,2560]{2,1,0:T(2,128)S(1)} %shard_map.102), channel_id=1, replica_groups=mesh['groups'=2,'gx'=4,'gy'=2,'gz'=2] {'gx','gy','gz'}, dimensions={0} | all-to-all | bytes 655360 | tf_op jit(solution)/shard_map/all_to_all | solution.py:190
  35.3 0.0 copy-done.3
  35.3 0.0 copy-done.4
  35.3 0.0 copy-done.7
  35.3 0.0 copy-done.8
  35.3 2.2 %shard_map.103 = bf16[16,2,2048]{2,1,0:T(2,128)(2,1)S(1)} custom-call(s32[2]{0:T(128)S(1)} %copy-done.7, f32[16,2,2560]{2,1,0:T(2,128)S(1)} %all_to_all.21.partial_ref, f32[1,128]{1,0:T(1,128)S(1)} %copy-done.8, bf16[2,256,1024]{2,1,0:T(8,128)(2,1)S(1)} %copy-done.3, bf16[2,256,1024]{2,1,0:T(8,128)(2,1)S(1)} %copy-done.4), custom_call_target="tpu_custom_call" | custom-call | flops 1000000000 | bytes 4194304 | tf_op jit(solution)/shard_map/pallas_call | solution.py:257
  37.6 11.0 %all_to_all.22.rows_ref = bf16[16,2,2048]{2,1,0:T(2,128)(2,1)S(1)} all-to-all(bf16[16,2,2048]{2,1,0:T(2,128)(2,1)S(1)} %shard_map.103), channel_id=1, replica_groups=mesh['groups'=2,'gx'=4,'gy'=2,'gz'=2] {'gx','gy','gz'}, dimensions={0} | all-to-all | bytes 262144 | tf_op jit(solution)/shard_map/all_to_all | solution.py:190
  48.6 0.0 slice-done
  48.6 0.0 slice-done.1
  48.6 0.0 slice-done.2
  48.6 0.0 slice-done.3
  48.6 3.0 %shard_map.104 = (f32[8,2,4096]{2,1,0:T(2,128)S(1)}, f32[8,2,4096]{2,1,0:T(2,128)S(1)}) custom-call(bf16[16,2,2048]{2,1,0:T(2,128)(2,1)S(1)} %all_to_all.22.rows_ref, bf16[2048,4096]{1,0:T(8,128)(2,1)S(1)} %bitcast.2), custom_call_target="tpu_custom_call" | custom-call | flops 536870912 | bytes 16777216 | tf_op jit(solution)/shard_map/pallas_call | solution.py:267
  51.6 0.1 collective-permute-start.1
  51.7 1.5 %collective-permute-done.1.b_ref = f32[8,2,4096]{2,1,0:T(2,128)S(1)} collective-permute-done((f32[8,2,4096]{2,1,0:T(2,128)S(1)}, f32[8,2,4096]{2,1,0:T(2,128)S(1)}, u32[]{:S(2)}, u32[]{:S(2)}) %collective-permute-start.1) | collective-permute-done | bytes 262176 | tf_op jit(solution)/shard_map/ppermute | solution.py:194
  53.2 11.9 %all_to_all.23.terms_ref = f32[8,2,4096]{2,1,0:T(2,128)S(1)} all-to-all(f32[8,2,4096]{2,1,0:T(2,128)S(1)} %shard_map.105), channel_id=1, replica_groups=mesh['groups'=2,'gx'=4,'gy'=2,'gz'=2] {'gx','gy'}, dimensions={0} | all-to-all | bytes 524288 | tf_op jit(solution)/shard_map/all_to_all | solution.py:190
  65.2 0.7 %shard_map.106 = bf16[2,16384]{1,0:T(2,128)(2,1)} custom-call(f32[8,2,4096]{2,1,0:T(2,128)S(1)} %all_to_all.23.terms_ref), custom_call_target="tpu_custom_call" | custom-call | tf_op jit(solution)/shard_map/pallas_call | solution.py:284
  (2 shorter events, 0.0 us)
Async XLA Ops:
  0.0 0.8 %copy-start.5 = (bf16[2,16384]{1,0:T(2,128)(2,1)S(1)}, bf16[2,16384]{1,0:T(2,128)(2,1)}, u32[]{:S(2)}) copy-start(bf16[2,16384]{1,0:T(2,128)(2,1)} %tokens_ref.1) | copy-start | bytes 196612
  0.8 0.8 %copy-start.6 = (f32[16384]{0:T(1024)S(1)}, f32[16384]{0:T(1024)}, u32[]{:S(2)}) copy-start(f32[16384]{0:T(1024)} %param.11) | copy-start | bytes 196612
  1.7 15.7 %copy-start = (bf16[4096,2048]{1,0:T(8,128)(2,1)S(1)}, bf16[4096,2048]{1,0:T(8,128)(2,1)}, u32[]{:S(2)}) copy-start(bf16[4096,2048]{1,0:T(8,128)(2,1)} %query_ref.3) | copy-start | bytes 50331652
  1.7 15.8 %copy-start.1 = (bf16[4096,256]{1,0:T(8,128)(2,1)S(1)}, bf16[4096,256]{1,0:T(8,128)(2,1)}, u32[]{:S(2)}) copy-start(bf16[4096,256]{1,0:T(8,128)(2,1)} %key_ref.3) | copy-start | bytes 6291460
  1.7 15.8 %copy-start.2 = (bf16[4096,256]{1,0:T(8,128)(2,1)S(1)}, bf16[4096,256]{1,0:T(8,128)(2,1)}, u32[]{:S(2)}) copy-start(bf16[4096,256]{1,0:T(8,128)(2,1)} %value_ref.3) | copy-start | bytes 6291460
  17.3 18.0 %copy-start.3 = (bf16[2,256,1024]{2,1,0:T(8,128)(2,1)S(1)}, bf16[2,256,1024]{2,1,0:T(8,128)(2,1)}, u32[]{:S(2)}) copy-start(bf16[2,256,1024]{2,1,0:T(8,128)(2,1)} %keys_ref.1) | copy-start | bytes 3145732
  17.3 18.0 %copy-start.4 = (bf16[2,256,1024]{2,1,0:T(8,128)(2,1)S(1)}, bf16[2,256,1024]{2,1,0:T(8,128)(2,1)}, u32[]{:S(2)}) copy-start(bf16[2,256,1024]{2,1,0:T(8,128)(2,1)} %values_ref.1) | copy-start | bytes 3145732
  17.3 18.0 %copy-start.7 = (s32[2]{0:T(128)S(1)}, s32[2]{0:T(128)}, u32[]{:S(2)}) copy-start(s32[2]{0:T(128)} %lengths_ref.1) | copy-start | bytes 28
  17.3 18.0 %copy-start.8 = (f32[1,128]{1,0:T(1,128)S(1)}, f32[1,128]{1,0:T(1,128)}, u32[]{:S(2)}) copy-start(f32[1,128]{1,0:T(1,128)} %constant.2.clone.frequency_ref) | copy-start | bytes 1540
  17.3 2.0 %collective-permute-start = (bf16[16,2,2048]{2,1,0:T(2,128)(2,1)S(1)}, bf16[16,2,2048]{2,1,0:T(2,128)(2,1)S(1)}, u32[]{:S(2)}, u32[]{:S(2)}) collective-permute-start(bf16[16,2,2048]{2,1,0:T(2,128)(2,1)S(1)} %all_to_all.20.rows_ref), channel_id=1, source_target_pairs={{0,1},{1,0},{2,3},{3,2},{4,5},{5,4},{6,7},{7,6},{8,9},{9,8},{10,11... | collective-permute-start | bytes 393224 | tf_op jit(solution)/shard_map/ppermute | solution.py:194
  17.5 31.1 %slice-start = ((s8[16777216]{0:T(1024)(128)(4,1)}), s8[4194304]{0:T(1024)(128)(4,1)S(1)}, s32[]{:S(2)}) async-start(s8[16777216]{0:T(1024)(128)(4,1)} %bitcast.1), calls=%async_computation.4 | async-start | bytes 8388608
  17.5 31.1 %slice-start.1 = ((s8[16777216]{0:T(1024)(128)(4,1)}), s8[4194304]{0:T(1024)(128)(4,1)S(1)}, s32[]{:S(2)}) async-start(s8[16777216]{0:T(1024)(128)(4,1)} %bitcast.1), calls=%async_computation.5 | async-start | bytes 8388608
  19.4 29.2 %slice-start.2 = ((s8[16777216]{0:T(1024)(128)(4,1)}), s8[4194304]{0:T(1024)(128)(4,1)S(1)}, s32[]{:S(2)}) async-start(s8[16777216]{0:T(1024)(128)(4,1)} %bitcast.1), calls=%async_computation.6 | async-start | bytes 8388608
  19.4 29.2 %slice-start.3 = ((s8[16777216]{0:T(1024)(128)(4,1)}), s8[4194304]{0:T(1024)(128)(4,1)S(1)}, s32[]{:S(2)}) async-start(s8[16777216]{0:T(1024)(128)(4,1)} %bitcast.1), calls=%async_computation.7 | async-start | bytes 8388608
  51.6 1.6 %collective-permute-start.1 = (f32[8,2,4096]{2,1,0:T(2,128)S(1)}, f32[8,2,4096]{2,1,0:T(2,128)S(1)}, u32[]{:S(2)}, u32[]{:S(2)}) collective-permute-start(f32[8,2,4096]{2,1,0:T(2,128)S(1)} %get-tuple-element.8), channel_id=1, source_target_pairs={{0,1},{1,0},{2,3},{3,2},{4,5},{5,4},{6,7},{7,6},{8,9},{9,8},{10,11... | collective-permute-start | bytes 786440 | tf_op jit(solution)/shard_map/ppermute | solution.py:194

commit v4 on v3

--- a/solution.py
+++ b/solution.py
@@ -10,17 +10,20 @@
 
 HD = 128
 ROW_AXES = ("gx", "gy", "gz")
-CHIPS = ("gx", "gy")
 PLANE = ("gy", "gz")
 MIB = 1024 * 1024
 IN_VMEM = pl.BlockSpec(memory_space=pltpu.VMEM)
 IN_SMEM = pl.BlockSpec(memory_space=pltpu.SMEM)
 
 
-def norm_kernel(wide, plane, tokens_ref, gain_ref, blocks_ref):
+def scale_kernel(tokens_ref, scaled_ref):
     tokens = tokens_ref[...].astype(jnp.float32)
     mean_square = jnp.mean(tokens * tokens, -1, keepdims=True)
-    normed = (tokens * lax.rsqrt(mean_square + 1e-05) * gain_ref[...]).astype(jnp.bfloat16)
+    scaled_ref[...] = tokens * lax.rsqrt(mean_square + 1e-05)
+
+
+def gain_kernel(wide, plane, scaled_ref, gain_ref, blocks_ref):
+    normed = (scaled_ref[...] * gain_ref[...]).astype(jnp.bfloat16)
     half = normed.shape[1] // wide // 2
     for i in range(wide):
         for j in range(plane):
@@ -158,40 +161,67 @@
             blocks_ref[i * plane + j] = block
 
 
-def output_kernel(rows_ref, weight_ref, keep_ref, give_ref):
+def output_kernel(at, cols, rows_ref, weight_ref, keep_ref, give_ref):
     owners, rows, depth = rows_ref.shape
     attended = rows_ref[...].reshape(owners * rows, depth)
     mine = lax.axis_index("gz") == 0
-    cols = weight_ref.shape[1]
     step = min(cols, 512)
     for c in range(0, cols, step):
-        part = jnp.dot(attended, weight_ref[:, c : c + step], preferred_element_type=jnp.float32)
+        part = jnp.dot(
+            attended, weight_ref[:, at + c : at + c + step], preferred_element_type=jnp.float32
+        )
         part = part.reshape(owners // 2, 2 * rows, step)
         even, odd = part[:, :rows], part[:, rows:]
         keep_ref[:, :, c : c + step] = jnp.where(mine, even, odd)
         give_ref[:, :, c : c + step] = jnp.where(mine, odd, even)
 
 
-def add_kernel(a_ref, b_ref, sum_ref):
-    sum_ref[...] = a_ref[...] + b_ref[...]
-
-
-def finish_kernel(wide, terms_ref, result_ref):
-    chips, _, cols = terms_ref.shape
-    count = chips // wide
+def halve_kernel(a_ref, b_ref, keep_ref, give_ref):
+    half = a_ref.shape[1] // 2
+    mine = lax.axis_index("gy") // half % 2 == 0
+    low = a_ref[:, :half] + b_ref[:, :half]
+    high = a_ref[:, half:] + b_ref[:, half:]
+    keep_ref[...] = jnp.where(mine, low, high)
+    give_ref[...] = jnp.where(mine, high, low)
+
+
+def total_kernel(parts, wide, *refs):
+    sums, outs, held = refs[: 2 * parts], refs[2 * parts : -1], refs[-1]
+    cols = sums[0].shape[-1]
+    for p in range(parts):
+        total = sums[2 * p][...] + sums[2 * p + 1][...]
+        held[:, :, p * cols : (p + 1) * cols] = total.reshape(
+            wide, total.shape[-2], cols
+        ).astype(jnp.bfloat16)
+    if len(outs) == 1:
+        outs[0][...] = held[...]
+    else:
+        own = lax.axis_index("gx")
+        for k in range(wide):
+            outs[k][...] = held[own ^ k]
+
+
+def finish_kernel(*refs):
+    blocks, result_ref = refs[:-1], refs[-1]
+    own = lax.axis_index("gx")
+    cols = blocks[0].shape[-1]
+    for k, block in enumerate(blocks):
+        at = pl.multiple_of((own ^ k) * cols, cols)
+        result_ref[:, pl.ds(at, cols)] = block[...]
+
+
+def lay_kernel(blocks_ref, result_ref):
+    wide, _, cols = blocks_ref.shape
     for i in range(wide):
-        total = terms_ref[i * count]
-        for j in range(1, count):
-            total = total + terms_ref[i * count + j]
-        result_ref[:, i * cols : (i + 1) * cols] = total.astype(result_ref.dtype)
+        result_ref[:, i * cols : (i + 1) * cols] = blocks_ref[i]
 
 
 def swap_blocks(blocks, axes):
     return lax.all_to_all(blocks, axes, split_axis=0, concat_axis=0, tiled=True)
 
 
-def swap_cores(value):
-    return lax.ppermute(value, "gz", [(0, 1), (1, 0)])
+def swap_pairs(value, axis, step):
+    return lax.ppermute(value, axis, [(i, i ^ step) for i in range(lax.axis_size(axis))])
 
 
 def shards(
@@ -221,16 +251,23 @@
         return pl.CostEstimate(flops=flops, bytes_accessed=size, transcendentals=0)
 
     half = width // 2
+    scaled = pl.pallas_call(
+        scale_kernel,
+        out_shape=jax.ShapeDtypeStruct(tokens.shape, jnp.float32),
+        in_specs=[IN_VMEM],
+        out_specs=IN_VMEM,
+        compiler_params=params(8),
+        cost_estimate=cost(40 * 10**9, MIB),
+    )(tokens)
     normed = pl.pallas_call(
-        functools.partial(norm_kernel, wide, plane),
+        functools.partial(gain_kernel, wide, plane),
         out_shape=jax.ShapeDtypeStruct((owners, rows, half), jnp.bfloat16),
         in_specs=[IN_VMEM, IN_VMEM],
         out_specs=IN_VMEM,
         compiler_params=params(8),
-        cost_estimate=cost(40 * 10**9, MIB),
-    )(tokens, norm_gain.reshape(1, -1))
+    )(scaled, norm_gain.reshape(1, -1))
     own_half = swap_blocks(normed, ROW_AXES)
-    other_half = swap_cores(own_half)
+    other_half = swap_pairs(own_half, "gz", 1)
     weights = (query_weight, key_weight, value_weight)
     half_cost = cost(owners * rows * width * cols, width * cols)
     partial = pl.pallas_call(
@@ -263,31 +300,60 @@
         cost_estimate=cost(10**9, 4 * MIB),
     )(lengths, partial, jnp.asarray(frequency), cache_keys, cache_values)
     head_rows = swap_blocks(attended, ROW_AXES)
-    by_chip = jax.ShapeDtypeStruct((owners // 2, rows, out_cols), jnp.float32)
-    keep, give = pl.pallas_call(
-        output_kernel,
-        out_shape=(by_chip, by_chip),
-        in_specs=[IN_VMEM, IN_VMEM],
-        out_specs=(IN_VMEM, IN_VMEM),
-        compiler_params=params(8),
-        cost_estimate=cost(2 * owners * rows * depth * out_cols, 2 * depth * out_cols),
-    )(head_rows, out_weight)
-    given = swap_cores(give)
-    by_core = pl.pallas_call(
-        add_kernel,
-        out_shape=by_chip,
-        in_specs=[IN_VMEM, IN_VMEM],
-        out_specs=IN_VMEM,
-        compiler_params=params(8),
-    )(keep, given)
-    terms = swap_blocks(by_core, CHIPS)
+    parts, chips = 2, owners // 2
+    part_cols = out_cols // parts
+    sums = []
+    for p in range(parts):
+        shape = jax.ShapeDtypeStruct((chips, rows, part_cols), jnp.float32)
+        keep, give = pl.pallas_call(
+            functools.partial(output_kernel, p * part_cols, part_cols),
+            out_shape=(shape, shape),
+            in_specs=[IN_VMEM, IN_VMEM],
+            out_specs=(IN_VMEM, IN_VMEM),
+            compiler_params=params(8),
+            cost_estimate=cost(2 * owners * rows * depth * part_cols, 2 * depth * part_cols),
+        )(head_rows, out_weight)
+        count = chips // wide
+        keep = keep.reshape(wide, count, rows, part_cols)
+        give = swap_pairs(give, "gz", 1).reshape(keep.shape)
+        while count > 1:
+            count //= 2
+            shape = jax.ShapeDtypeStruct((wide, count, rows, part_cols), jnp.float32)
+            keep, give = pl.pallas_call(
+                halve_kernel,
+                out_shape=(shape, shape),
+                in_specs=[IN_VMEM, IN_VMEM],
+                out_specs=(IN_VMEM, IN_VMEM),
+                compiler_params=params(8),
+            )(keep, give)
+            give = swap_pairs(give, "gy", count)
+        sums += [keep, give]
+    result = jax.ShapeDtypeStruct((rows, wide * out_cols), jnp.bfloat16)
+    by_pairs = wide <= 4
+    if by_pairs:
+        shapes = [jax.ShapeDtypeStruct((rows, out_cols), jnp.bfloat16)] * wide
+    else:
+        shapes = [jax.ShapeDtypeStruct((wide, rows, out_cols), jnp.bfloat16)]
+    blocks = pl.pallas_call(
+        functools.partial(total_kernel, parts, wide),
+        out_shape=shapes,
+        in_specs=[IN_VMEM] * len(sums),
+        out_specs=[IN_VMEM] * len(shapes),
+        scratch_shapes=[pltpu.VMEM((wide, rows, out_cols), jnp.bfloat16)],
+        compiler_params=params(8),
+    )(*sums)
+    if by_pairs:
+        moved = [swap_pairs(blocks[k], "gx", k) for k in range(wide - 1, 0, -1)]
+        blocks = [blocks[0]] + moved[::-1]
+    else:
+        blocks = [swap_blocks(blocks[0], "gx")]
     return pl.pallas_call(
-        functools.partial(finish_kernel, wide),
-        out_shape=jax.ShapeDtypeStruct((rows, wide * out_cols), jnp.bfloat16),
-        in_specs=[IN_VMEM],
-        out_specs=IN_VMEM,
-        compiler_params=params(8),
-    )(terms)
+        finish_kernel if by_pairs else lay_kernel,
+        out_shape=result,
+        in_specs=[IN_VMEM] * len(blocks),
+        out_specs=IN_VMEM,
+        compiler_params=params(8),
+    )(*blocks)
 
 
 def solution(mesh):

time: 66.1 us -> 65.3 us (0.988)
  blocking collectives: 52.2 us -> 40.3 us
  starting transfers between devices: 0.14 us -> 6.43 us
  waiting for transfers between devices: 1.53 us -> 6.86 us
  local copies, waits for them, and re-layouts: 1.72 us -> 1.04 us
    all_to_all x4 -> x3, blocking collectives: 52.2 us -> 40.3 us  [swap_blocks(): return lax.all_to_all(blocks, axes, split_axis=0, concat_axis=0, tiled=True)]
    ppermute x2 -> x8, starting transfers between devices: 0.14 us -> 6.43 us  [swap_pairs(): lax.ppermute(value, axis, [(i, i ^ step) for i in range(lax.axis_size(axi...]
    ppermute x2 -> x8, waiting for transfers between devices: 1.53 us -> 6.86 us  [swap_pairs(): lax.ppermute(value, axis, [(i, i ^ step) for i in range(lax.axis_size(axi...]
    unnamed x26, local copies, waits for them, and re-layouts: 1.72 us -> 1.04 us
    pallas_call x4 -> x8, Pallas kernels: 4.02 us -> 4.2 us  [the longest x2 3.14 us: shards(): pl.pallas_call(functools.partial(output_kernel, p * part_cols, part_cols)...]
  transfers between devices with their start and end apart: 2 -> 8, of which waited for: 1 -> 5; matrix products, arithmetic and copies ran while one was open for 0% -> 0% of each run, Pallas kernels for 3% -> 5%
where the time goes in v4:
time: 65.3 us; the launch traced here: 65.1 us
  blocking collectives  40.3 us (62%)
  Pallas kernels  10.3 us (16%)
  waiting for transfers between devices  6.86 us (11%)
  starting transfers between devices  6.43 us (10%)
  local copies, waits for them, and re-layouts  1.04 us (2%)
    all_to_all x3, blocking collectives, swap_blocks(): return lax.all_to_all(blocks, axes, split_axis=0, concat_axis=0, tiled=True)  40.3 us
    ppermute x8, waiting for transfers between devices, swap_pairs(): lax.ppermute(value, axis, [(i, i ^ step) for i in range(lax.axis_size(axi...  6.86 us
    ppermute x8, starting transfers between devices, swap_pairs(): lax.ppermute(value, axis, [(i, i ^ step) for i in range(lax.axis_size(axi...  6.43 us
    pallas_call x2, Pallas kernels, shards(): pl.pallas_call(functools.partial(output_kernel, p * part_cols, part_cols)...  3.14 us
    pallas_call x1, Pallas kernels, shards(): pl.pallas_call(functools.partial(attend_kernel, wide, plane, rows, query_...  2.23 us
    pallas_call x1, Pallas kernels, shards(): pl.pallas_call(functools.partial(project_kernel, False), out_shape=jax.Sh...  1.94 us
    pallas_call x1, Pallas kernels, shards(): pl.pallas_call(functools.partial(project_kernel, True), out_shape=jax.Sha...  1.89 us
  transfers between devices with their start and end apart: 8, of which 5 were waited for; matrix products, arithmetic and copies ran while one was open for 0% of the time, Pallas kernels for 5%

profile of v4, /device:TPU:0, one launch (start us, length us, event | category | flops | bytes accessed | tf_op | source)
XLA Modules:
  0.0 65.1 jit_solution(4677406576611040310)
XLA Ops:
  0.0 0.0 copy-start.3
  0.0 0.0 copy-start.2
  0.0 0.0 copy-start.1
  0.0 0.0 copy-start
  0.0 0.0 copy-start.6
  0.0 1.0 %copy-done.6 = bf16[2,16384]{1,0:T(2,128)(2,1)S(1)} copy-done((bf16[2,16384]{1,0:T(2,128)(2,1)S(1)}, bf16[2,16384]{1,0:T(2,128)(2,1)}, u32[]{:S(2)}) %copy-start.6) | copy-done | bytes 65560
  1.0 0.2 shard_map.100.scaled_ref
  1.2 0.0 copy-done.3
  1.2 0.1 shard_map.101
  1.3 15.4 %all_to_all.15.rows_ref = bf16[16,2,2048]{2,1,0:T(2,128)(2,1)S(1)} all-to-all(bf16[16,2,2048]{2,1,0:T(2,128)(2,1)S(1)} %shard_map.101), channel_id=1, replica_groups=mesh['groups'=2,'gx'=4,'gy'=2,'gz'=2] {'gx','gy','gz'}, dimensions={0} | all-to-all | bytes 262144 | tf_op jit(solution)/shard_map/all_to_all | solution.py:220
  16.7 0.0 copy-start.4
  16.7 0.0 copy-start.5
  16.7 0.0 copy-start.7
  16.7 0.0 copy-start.8
  16.7 0.1 collective-permute-start
  16.8 0.0 copy-done.2
  16.8 0.0 copy-done.1
  16.8 0.0 copy-done
  16.8 0.0 slice-start
  16.8 0.0 slice-start.1
  16.9 1.9 %shard_map.102.refs_0_ = f32[32,2560]{1,0:T(8,128)S(1)} custom-call(bf16[16,2,2048]{2,1,0:T(2,128)(2,1)S(1)} %all_to_all.15.rows_ref, bf16[4096,2048]{1,0:T(8,128)(2,1)S(1)} %copy-done, bf16[4096,256]{1,0:T(8,128)(2,1)S(1)} %copy-done.1, bf16[4096,256]{1,0:T(8,128)(2,1)S(1)} %copy-done.2), custom_call_target="tpu_custom_call" | custom-call | flops 335544320 | bytes 10485760 | tf_op jit(solution)/shard_map/pallas_call | solution.py:273
  18.7 0.0 slice-start.2
  18.7 0.0 slice-start.3
  18.8 0.0 collective-permute-done.rows_ref
  18.8 1.9 %shard_map.103 = f32[16,2,2560]{2,1,0:T(2,128)S(1)} custom-call(bf16[16,2,2048]{2,1,0:T(2,128)(2,1)S(1)} %collective-permute-done.rows_ref, bf16[4096,2048]{1,0:T(8,128)(2,1)S(1)} %copy-done, bf16[4096,256]{1,0:T(8,128)(2,1)S(1)} %copy-done.1, bf16[4096,256]{1,0:T(8,128)(2,1)S(1)} %copy-done.2, f32[32,2560]{1,0:T(8,128)S(1)} %shard_map.102.refs_0_), custom_call_target="tpu_custom_call" | custom-call | flops 335544320 | bytes 10485760 | tf_op jit(solution)/shard_map/pallas_call | solution.py:281
  20.7 14.0 %all_to_all.16.partial_ref = f32[16,2,2560]{2,1,0:T(2,128)S(1)} all-to-all(f32[16,2,2560]{2,1,0:T(2,128)S(1)} %shard_map.103), channel_id=1, replica_groups=mesh['groups'=2,'gx'=4,'gy'=2,'gz'=2] {'gx','gy','gz'}, dimensions={0} | all-to-all | bytes 655360 | tf_op jit(solution)/shard_map/all_to_all | solution.py:220
  34.7 0.0 copy-done.4
  34.7 0.0 copy-done.5
  34.7 0.0 copy-done.7
  34.7 0.0 copy-done.8
  34.7 2.2 %shard_map.104 = bf16[16,2,2048]{2,1,0:T(2,128)(2,1)S(1)} custom-call(s32[2]{0:T(128)S(1)} %copy-done.7, f32[16,2,2560]{2,1,0:T(2,128)S(1)} %all_to_all.16.partial_ref, f32[1,128]{1,0:T(1,128)S(1)} %copy-done.8, bf16[2,256,1024]{2,1,0:T(8,128)(2,1)S(1)} %copy-done.4, bf16[2,256,1024]{2,1,0:T(8,128)(2,1)S(1)} %copy-done.5), custom_call_target="tpu_custom_call" | custom-call | flops 1000000000 | bytes 4194304 | tf_op jit(solution)/shard_map/pallas_call | solution.py:294
  36.9 11.0 %all_to_all.17.rows_ref = bf16[16,2,2048]{2,1,0:T(2,128)(2,1)S(1)} all-to-all(bf16[16,2,2048]{2,1,0:T(2,128)(2,1)S(1)} %shard_map.104), channel_id=1, replica_groups=mesh['groups'=2,'gx'=4,'gy'=2,'gz'=2] {'gx','gy','gz'}, dimensions={0} | all-to-all | bytes 262144 | tf_op jit(solution)/shard_map/all_to_all | solution.py:220
  47.9 0.0 slice-done
  47.9 0.0 slice-done.1
  47.9 0.0 slice-done.2
  47.9 0.0 slice-done.3
  48.0 1.6 %shard_map.105 = (f32[8,2,2048]{2,1,0:T(2,128)S(1)}, f32[8,2,2048]{2,1,0:T(2,128)S(1)}) custom-call(bf16[16,2,2048]{2,1,0:T(2,128)(2,1)S(1)} %all_to_all.17.rows_ref, bf16[2048,4096]{1,0:T(8,128)(2,1)S(1)} %bitcast.6), custom_call_target="tpu_custom_call" | custom-call | flops 268435456 | bytes 8388608 | tf_op jit(solution)/shard_map/pallas_call | solution.py:308
  49.5 0.1 collective-permute-start.1
  49.6 1.6 %shard_map.107 = (f32[8,2,2048]{2,1,0:T(2,128)S(1)}, f32[8,2,2048]{2,1,0:T(2,128)S(1)}) custom-call(bf16[16,2,2048]{2,1,0:T(2,128)(2,1)S(1)} %all_to_all.17.rows_ref, bf16[2048,4096]{1,0:T(8,128)(2,1)S(1)} %bitcast.6), custom_call_target="tpu_custom_call" | custom-call | flops 268435456 | bytes 8388608 | tf_op jit(solution)/shard_map/pallas_call | solution.py:308
  51.2 0.6 collective-permute-start.3
  51.8 0.0 collective-permute-done.1
  51.8 0.1 collective-permute-start.2
  51.9 0.9 %collective-permute-done.3 = f32[8,2,2048]{2,1,0:T(2,128)S(1)} collective-permute-done((f32[8,2,2048]{2,1,0:T(2,128)S(1)}, f32[8,2,2048]{2,1,0:T(2,128)S(1)}, u32[]{:S(2)}, u32[]{:S(2)}) %collective-permute-start.3) | collective-permute-done | bytes 131104 | tf_op jit(solution)/shard_map/ppermute | solution.py:224
  52.8 1.2 %collective-permute-start.4 = (f32[4,1,2,2048]{3,2,1,0:T(2,128)S(1)}, f32[4,1,2,2048]{3,2,1,0:T(2,128)S(1)}, u32[]{:S(2)}, u32[]{:S(2)}) collective-permute-start(f32[4,1,2,2048]{3,2,1,0:T(2,128)S(1)} %get-tuple-element.24), channel_id=1, source_target_pairs={{0,2},{2,0},{1,3},{3,1},{4,6},{6,4},{5,7},{7,5},{8,10},{10,8},{9,1... | collective-permute-start | bytes 196616 | tf_op jit(solution)/shard_map/ppermute | solution.py:224
  54.0 2.6 %collective-permute-done.2.refs_1_ = f32[4,1,2,2048]{3,2,1,0:T(2,128)S(1)} collective-permute-done((f32[4,1,2,2048]{3,2,1,0:T(2,128)S(1)}, f32[4,1,2,2048]{3,2,1,0:T(2,128)S(1)}, u32[]{:S(2)}, u32[]{:S(2)}) %collective-permute-start.2) | collective-permute-done | bytes 65568 | tf_op jit(solution)/shard_map/ppermute | solution.py:224
  56.5 1.0 %collective-permute-done.4.refs_3_ = f32[4,1,2,2048]{3,2,1,0:T(2,128)S(1)} collective-permute-done((f32[4,1,2,2048]{3,2,1,0:T(2,128)S(1)}, f32[4,1,2,2048]{3,2,1,0:T(2,128)S(1)}, u32[]{:S(2)}, u32[]{:S(2)}) %collective-permute-start.4) | collective-permute-done | bytes 65568 | tf_op jit(solution)/shard_map/ppermute | solution.py:224
  57.5 0.1 shard_map.109
  57.6 0.1 collective-permute-start.5
  57.7 1.3 %collective-permute-start.6 = (bf16[2,4096]{1,0:T(2,128)(2,1)S(1)}, bf16[2,4096]{1,0:T(2,128)(2,1)S(1)}, u32[]{:S(2)}, u32[]{:S(2)}) collective-permute-start(bf16[2,4096]{1,0:T(2,128)(2,1)S(1)} %get-tuple-element.27), channel_id=1, source_target_pairs={{0,8},{4,12},{8,0},{12,4},{1,9},{5,13},{9,1},{13,5},{2,10},{6,14},... | collective-permute-start | bytes 49160 | tf_op jit(solution)/shard_map/ppermute | solution.py:224
  58.9 3.1 %collective-permute-start.7 = (bf16[2,4096]{1,0:T(2,128)(2,1)S(1)}, bf16[2,4096]{1,0:T(2,128)(2,1)S(1)}, u32[]{:S(2)}, u32[]{:S(2)}) collective-permute-start(bf16[2,4096]{1,0:T(2,128)(2,1)S(1)} %get-tuple-element.28), channel_id=1, source_target_pairs={{0,12},{4,8},{8,4},{12,0},{1,13},{5,9},{9,5},{13,1},{2,14},{6,10},... | collective-permute-start | bytes 49160 | tf_op jit(solution)/shard_map/ppermute | solution.py:224
  62.0 0.0 collective-permute-done.5.refs_1_
  62.0 0.3 collective-permute-done.6.refs_2_
  62.4 2.1 %collective-permute-done.7.refs_3_ = bf16[2,4096]{1,0:T(2,128)(2,1)S(1)} collective-permute-done((bf16[2,4096]{1,0:T(2,128)(2,1)S(1)}, bf16[2,4096]{1,0:T(2,128)(2,1)S(1)}, u32[]{:S(2)}, u32[]{:S(2)}) %collective-permute-start.7) | collective-permute-done | bytes 16416 | tf_op jit(solution)/shard_map/ppermute | solution.py:224
  64.5 0.6 shard_map.110
  (3 shorter events, 0.0 us)
Async XLA Ops:
  0.0 1.2 %copy-start.3 = (f32[16384]{0:T(1024)S(1)}, f32[16384]{0:T(1024)}, u32[]{:S(2)}) copy-start(f32[16384]{0:T(1024)} %param.11) | copy-start | bytes 196612
  0.0 16.8 %copy-start.2 = (bf16[4096,256]{1,0:T(8,128)(2,1)S(1)}, bf16[4096,256]{1,0:T(8,128)(2,1)}, u32[]{:S(2)}) copy-start(bf16[4096,256]{1,0:T(8,128)(2,1)} %value_ref.3) | copy-start | bytes 6291460
  0.0 16.8 %copy-start.1 = (bf16[4096,256]{1,0:T(8,128)(2,1)S(1)}, bf16[4096,256]{1,0:T(8,128)(2,1)}, u32[]{:S(2)}) copy-start(bf16[4096,256]{1,0:T(8,128)(2,1)} %key_ref.3) | copy-start | bytes 6291460
  0.0 16.8 %copy-start = (bf16[4096,2048]{1,0:T(8,128)(2,1)S(1)}, bf16[4096,2048]{1,0:T(8,128)(2,1)}, u32[]{:S(2)}) copy-start(bf16[4096,2048]{1,0:T(8,128)(2,1)} %query_ref.3) | copy-start | bytes 50331652
  0.0 1.0 %copy-start.6 = (bf16[2,16384]{1,0:T(2,128)(2,1)S(1)}, bf16[2,16384]{1,0:T(2,128)(2,1)}, u32[]{:S(2)}) copy-start(bf16[2,16384]{1,0:T(2,128)(2,1)} %tokens_ref.1) | copy-start | bytes 196612
  16.7 18.0 %copy-start.4 = (bf16[2,256,1024]{2,1,0:T(8,128)(2,1)S(1)}, bf16[2,256,1024]{2,1,0:T(8,128)(2,1)}, u32[]{:S(2)}) copy-start(bf16[2,256,1024]{2,1,0:T(8,128)(2,1)} %keys_ref.1) | copy-start | bytes 3145732
  16.7 18.0 %copy-start.5 = (bf16[2,256,1024]{2,1,0:T(8,128)(2,1)S(1)}, bf16[2,256,1024]{2,1,0:T(8,128)(2,1)}, u32[]{:S(2)}) copy-start(bf16[2,256,1024]{2,1,0:T(8,128)(2,1)} %values_ref.1) | copy-start | bytes 3145732
  16.7 18.0 %copy-start.7 = (s32[2]{0:T(128)S(1)}, s32[2]{0:T(128)}, u32[]{:S(2)}) copy-start(s32[2]{0:T(128)} %lengths_ref.1) | copy-start | bytes 28
  16.7 18.0 %copy-start.8 = (f32[1,128]{1,0:T(1,128)S(1)}, f32[1,128]{1,0:T(1,128)}, u32[]{:S(2)}) copy-start(f32[1,128]{1,0:T(1,128)} %constant.2.clone.frequency_ref) | copy-start | bytes 1540
  16.7 2.0 %collective-permute-start = (bf16[16,2,2048]{2,1,0:T(2,128)(2,1)S(1)}, bf16[16,2,2048]{2,1,0:T(2,128)(2,1)S(1)}, u32[]{:S(2)}, u32[]{:S(2)}) collective-permute-start(bf16[16,2,2048]{2,1,0:T(2,128)(2,1)S(1)} %all_to_all.15.rows_ref), channel_id=1, source_target_pairs={{0,1},{1,0},{2,3},{3,2},{4,5},{5,4},{6,7},{7,6},{8,9},{9,8},{10,11... | collective-permute-start | bytes 393224 | tf_op jit(solution)/shard_map/ppermute | solution.py:224
  16.8 31.1 %slice-start = ((s8[16777216]{0:T(1024)(128)(4,1)}), s8[4194304]{0:T(1024)(128)(4,1)S(1)}, s32[]{:S(2)}) async-start(s8[16777216]{0:T(1024)(128)(4,1)} %bitcast.5), calls=%async_computation.3 | async-start | bytes 8388608
  16.8 31.1 %slice-start.1 = ((s8[16777216]{0:T(1024)(128)(4,1)}), s8[4194304]{0:T(1024)(128)(4,1)S(1)}, s32[]{:S(2)}) async-start(s8[16777216]{0:T(1024)(128)(4,1)} %bitcast.5), calls=%async_computation.4 | async-start | bytes 8388608
  18.7 29.2 %slice-start.2 = ((s8[16777216]{0:T(1024)(128)(4,1)}), s8[4194304]{0:T(1024)(128)(4,1)S(1)}, s32[]{:S(2)}) async-start(s8[16777216]{0:T(1024)(128)(4,1)} %bitcast.5), calls=%async_computation.5 | async-start | bytes 8388608
  18.7 29.2 %slice-start.3 = ((s8[16777216]{0:T(1024)(128)(4,1)}), s8[4194304]{0:T(1024)(128)(4,1)S(1)}, s32[]{:S(2)}) async-start(s8[16777216]{0:T(1024)(128)(4,1)} %bitcast.5), calls=%async_computation.6 | async-start | bytes 8388608
  49.5 2.2 %collective-permute-start.1 = (f32[8,2,2048]{2,1,0:T(2,128)S(1)}, f32[8,2,2048]{2,1,0:T(2,128)S(1)}, u32[]{:S(2)}, u32[]{:S(2)}) collective-permute-start(f32[8,2,2048]{2,1,0:T(2,128)S(1)} %get-tuple-element.18), channel_id=1, source_target_pairs={{0,1},{1,0},{2,3},{3,2},{4,5},{5,4},{6,7},{7,6},{8,9},{9,8},{10,11... | collective-permute-start | bytes 393224 | tf_op jit(solution)/shard_map/ppermute | solution.py:224
  51.2 1.5 %collective-permute-start.3 = (f32[8,2,2048]{2,1,0:T(2,128)S(1)}, f32[8,2,2048]{2,1,0:T(2,128)S(1)}, u32[]{:S(2)}, u32[]{:S(2)}) collective-permute-start(f32[8,2,2048]{2,1,0:T(2,128)S(1)} %get-tuple-element.22), channel_id=1, source_target_pairs={{0,1},{1,0},{2,3},{3,2},{4,5},{5,4},{6,7},{7,6},{8,9},{9,8},{10,11... | collective-permute-start | bytes 393224 | tf_op jit(solution)/shard_map/ppermute | solution.py:224
  51.8 4.7 %collective-permute-start.2 = (f32[4,1,2,2048]{3,2,1,0:T(2,128)S(1)}, f32[4,1,2,2048]{3,2,1,0:T(2,128)S(1)}, u32[]{:S(2)}, u32[]{:S(2)}) collective-permute-start(f32[4,1,2,2048]{3,2,1,0:T(2,128)S(1)} %get-tuple-element.20), channel_id=1, source_target_pairs={{0,2},{2,0},{1,3},{3,1},{4,6},{6,4},{5,7},{7,5},{8,10},{10,8},{9,1... | collective-permute-start | bytes 196616 | tf_op jit(solution)/shard_map/ppermute | solution.py:224
  52.8 4.8 %collective-permute-start.4 = (f32[4,1,2,2048]{3,2,1,0:T(2,128)S(1)}, f32[4,1,2,2048]{3,2,1,0:T(2,128)S(1)}, u32[]{:S(2)}, u32[]{:S(2)}) collective-permute-start(f32[4,1,2,2048]{3,2,1,0:T(2,128)S(1)} %get-tuple-element.24), channel_id=1, source_target_pairs={{0,2},{2,0},{1,3},{3,1},{4,6},{6,4},{5,7},{7,5},{8,10},{10,8},{9,1... | collective-permute-start | bytes 196616 | tf_op jit(solution)/shard_map/ppermute | solution.py:224
  57.6 4.5 %collective-permute-start.5 = (bf16[2,4096]{1,0:T(2,128)(2,1)S(1)}, bf16[2,4096]{1,0:T(2,128)(2,1)S(1)}, u32[]{:S(2)}, u32[]{:S(2)}) collective-permute-start(bf16[2,4096]{1,0:T(2,128)(2,1)S(1)} %get-tuple-element.26), channel_id=1, source_target_pairs={{0,4},{4,0},{8,12},{12,8},{1,5},{5,1},{9,13},{13,9},{2,6},{6,2},{1... | collective-permute-start | bytes 49160 | tf_op jit(solution)/shard_map/ppermute | solution.py:224
  57.7 4.7 %collective-permute-start.6 = (bf16[2,4096]{1,0:T(2,128)(2,1)S(1)}, bf16[2,4096]{1,0:T(2,128)(2,1)S(1)}, u32[]{:S(2)}, u32[]{:S(2)}) collective-permute-start(bf16[2,4096]{1,0:T(2,128)(2,1)S(1)} %get-tuple-element.27), channel_id=1, source_target_pairs={{0,8},{4,12},{8,0},{12,4},{1,9},{5,13},{9,1},{13,5},{2,10},{6,14},... | collective-permute-start | bytes 49160 | tf_op jit(solution)/shard_map/ppermute | solution.py:224
  58.9 5.5 %collective-permute-start.7 = (bf16[2,4096]{1,0:T(2,128)(2,1)S(1)}, bf16[2,4096]{1,0:T(2,128)(2,1)S(1)}, u32[]{:S(2)}, u32[]{:S(2)}) collective-permute-start(bf16[2,4096]{1,0:T(2,128)(2,1)S(1)} %get-tuple-element.28), channel_id=1, source_target_pairs={{0,12},{4,8},{8,4},{12,0},{1,13},{5,9},{9,5},{13,1},{2,14},{6,10},... | collective-permute-start | bytes 49160 | tf_op jit(solution)/shard_map/ppermute | solution.py:224

commit v5 on v4

--- a/solution.py
+++ b/solution.py
@@ -202,7 +202,7 @@
 
 
 def finish_kernel(*refs):
-    blocks, result_ref = refs[:-1], refs[-1]
+    blocks, result_ref = refs[-2::-1], refs[-1]
     own = lax.axis_index("gx")
     cols = blocks[0].shape[-1]
     for k, block in enumerate(blocks):
@@ -343,8 +343,7 @@
         compiler_params=params(8),
     )(*sums)
     if by_pairs:
-        moved = [swap_pairs(blocks[k], "gx", k) for k in range(wide - 1, 0, -1)]
-        blocks = [blocks[0]] + moved[::-1]
+        blocks = [swap_pairs(blocks[k], "gx", k) for k in range(wide - 1, 0, -1)] + [blocks[0]]
     else:
         blocks = [swap_blocks(blocks[0], "gx")]
     return pl.pallas_call(

time: 65.3 us -> 64.6 us (0.989)
  waiting for transfers between devices: 6.86 us -> 6.14 us
    ppermute x8, waiting for transfers between devices: 6.86 us -> 6.14 us  [swap_pairs(): lax.ppermute(value, axis, [(i, i ^ step) for i in range(lax.axis_size(axi...]
where the time goes in v5:
time: 64.6 us; the launch traced here: 64.4 us
  blocking collectives  40.3 us (62%)
  Pallas kernels  10.3 us (16%)
  starting transfers between devices  6.43 us (10%)
  waiting for transfers between devices  6.14 us (10%)
  local copies, waits for them, and re-layouts  1.04 us (2%)
    all_to_all x3, blocking collectives, swap_blocks(): return lax.all_to_all(blocks, axes, split_axis=0, concat_axis=0, tiled=True)  40.3 us
    ppermute x8, starting transfers between devices, swap_pairs(): lax.ppermute(value, axis, [(i, i ^ step) for i in range(lax.axis_size(axi...  6.43 us
    ppermute x8, waiting for transfers between devices, swap_pairs(): lax.ppermute(value, axis, [(i, i ^ step) for i in range(lax.axis_size(axi...  6.14 us
    pallas_call x2, Pallas kernels, shards(): pl.pallas_call(functools.partial(output_kernel, p * part_cols, part_cols)...  3.14 us
    pallas_call x1, Pallas kernels, shards(): pl.pallas_call(functools.partial(attend_kernel, wide, plane, rows, query_...  2.23 us
    pallas_call x1, Pallas kernels, shards(): pl.pallas_call(functools.partial(project_kernel, False), out_shape=jax.Sh...  1.94 us
    pallas_call x1, Pallas kernels, shards(): pl.pallas_call(functools.partial(project_kernel, True), out_shape=jax.Sha...  1.89 us
  transfers between devices with their start and end apart: 8, of which 5 were waited for; matrix products, arithmetic and copies ran while one was open for 0% of the time, Pallas kernels for 5%

profile of v5, /device:TPU:0, one launch (start us, length us, event | category | flops | bytes accessed | tf_op | source)
XLA Modules:
  0.0 64.4 jit_solution(16229674347385997484)
XLA Ops:
  0.0 0.0 copy-start.3
  0.0 0.0 copy-start.2
  0.0 0.0 copy-start.1
  0.0 0.0 copy-start
  0.0 0.0 copy-start.6
  0.0 1.0 %copy-done.6 = bf16[2,16384]{1,0:T(2,128)(2,1)S(1)} copy-done((bf16[2,16384]{1,0:T(2,128)(2,1)S(1)}, bf16[2,16384]{1,0:T(2,128)(2,1)}, u32[]{:S(2)}) %copy-start.6) | copy-done | bytes 65560
  1.0 0.2 shard_map.100.scaled_ref
  1.2 0.0 copy-done.3
  1.2 0.1 shard_map.101
  1.3 15.4 %all_to_all.15.rows_ref = bf16[16,2,2048]{2,1,0:T(2,128)(2,1)S(1)} all-to-all(bf16[16,2,2048]{2,1,0:T(2,128)(2,1)S(1)} %shard_map.101), channel_id=1, replica_groups=mesh['groups'=2,'gx'=4,'gy'=2,'gz'=2] {'gx','gy','gz'}, dimensions={0} | all-to-all | bytes 262144 | tf_op jit(solution)/shard_map/all_to_all | solution.py:220
  16.7 0.0 copy-start.4
  16.7 0.0 copy-start.5
  16.7 0.0 copy-start.7
  16.7 0.0 copy-start.8
  16.7 0.1 collective-permute-start
  16.8 0.0 copy-done.2
  16.8 0.0 copy-done.1
  16.8 0.0 copy-done
  16.8 0.0 slice-start
  16.8 0.0 slice-start.1
  16.9 1.9 %shard_map.102.refs_0_ = f32[32,2560]{1,0:T(8,128)S(1)} custom-call(bf16[16,2,2048]{2,1,0:T(2,128)(2,1)S(1)} %all_to_all.15.rows_ref, bf16[4096,2048]{1,0:T(8,128)(2,1)S(1)} %copy-done, bf16[4096,256]{1,0:T(8,128)(2,1)S(1)} %copy-done.1, bf16[4096,256]{1,0:T(8,128)(2,1)S(1)} %copy-done.2), custom_call_target="tpu_custom_call" | custom-call | flops 335544320 | bytes 10485760 | tf_op jit(solution)/shard_map/pallas_call | solution.py:273
  18.7 0.0 slice-start.2
  18.7 0.0 slice-start.3
  18.8 0.0 collective-permute-done.rows_ref
  18.8 1.9 %shard_map.103 = f32[16,2,2560]{2,1,0:T(2,128)S(1)} custom-call(bf16[16,2,2048]{2,1,0:T(2,128)(2,1)S(1)} %collective-permute-done.rows_ref, bf16[4096,2048]{1,0:T(8,128)(2,1)S(1)} %copy-done, bf16[4096,256]{1,0:T(8,128)(2,1)S(1)} %copy-done.1, bf16[4096,256]{1,0:T(8,128)(2,1)S(1)} %copy-done.2, f32[32,2560]{1,0:T(8,128)S(1)} %shard_map.102.refs_0_), custom_call_target="tpu_custom_call" | custom-call | flops 335544320 | bytes 10485760 | tf_op jit(solution)/shard_map/pallas_call | solution.py:281
  20.7 14.0 %all_to_all.16.partial_ref = f32[16,2,2560]{2,1,0:T(2,128)S(1)} all-to-all(f32[16,2,2560]{2,1,0:T(2,128)S(1)} %shard_map.103), channel_id=1, replica_groups=mesh['groups'=2,'gx'=4,'gy'=2,'gz'=2] {'gx','gy','gz'}, dimensions={0} | all-to-all | bytes 655360 | tf_op jit(solution)/shard_map/all_to_all | solution.py:220
  34.7 0.0 copy-done.4
  34.7 0.0 copy-done.5
  34.7 0.0 copy-done.7
  34.7 0.0 copy-done.8
  34.7 2.2 %shard_map.104 = bf16[16,2,2048]{2,1,0:T(2,128)(2,1)S(1)} custom-call(s32[2]{0:T(128)S(1)} %copy-done.7, f32[16,2,2560]{2,1,0:T(2,128)S(1)} %all_to_all.16.partial_ref, f32[1,128]{1,0:T(1,128)S(1)} %copy-done.8, bf16[2,256,1024]{2,1,0:T(8,128)(2,1)S(1)} %copy-done.4, bf16[2,256,1024]{2,1,0:T(8,128)(2,1)S(1)} %copy-done.5), custom_call_target="tpu_custom_call" | custom-call | flops 1000000000 | bytes 4194304 | tf_op jit(solution)/shard_map/pallas_call | solution.py:294
  36.9 11.0 %all_to_all.17.rows_ref = bf16[16,2,2048]{2,1,0:T(2,128)(2,1)S(1)} all-to-all(bf16[16,2,2048]{2,1,0:T(2,128)(2,1)S(1)} %shard_map.104), channel_id=1, replica_groups=mesh['groups'=2,'gx'=4,'gy'=2,'gz'=2] {'gx','gy','gz'}, dimensions={0} | all-to-all | bytes 262144 | tf_op jit(solution)/shard_map/all_to_all | solution.py:220
  47.9 0.0 slice-done
  47.9 0.0 slice-done.1
  47.9 0.0 slice-done.2
  47.9 0.0 slice-done.3
  48.0 1.6 %shard_map.105 = (f32[8,2,2048]{2,1,0:T(2,128)S(1)}, f32[8,2,2048]{2,1,0:T(2,128)S(1)}) custom-call(bf16[16,2,2048]{2,1,0:T(2,128)(2,1)S(1)} %all_to_all.17.rows_ref, bf16[2048,4096]{1,0:T(8,128)(2,1)S(1)} %bitcast.6), custom_call_target="tpu_custom_call" | custom-call | flops 268435456 | bytes 8388608 | tf_op jit(solution)/shard_map/pallas_call | solution.py:308
  49.5 0.1 collective-permute-start.1
  49.6 1.6 %shard_map.107 = (f32[8,2,2048]{2,1,0:T(2,128)S(1)}, f32[8,2,2048]{2,1,0:T(2,128)S(1)}) custom-call(bf16[16,2,2048]{2,1,0:T(2,128)(2,1)S(1)} %all_to_all.17.rows_ref, bf16[2048,4096]{1,0:T(8,128)(2,1)S(1)} %bitcast.6), custom_call_target="tpu_custom_call" | custom-call | flops 268435456 | bytes 8388608 | tf_op jit(solution)/shard_map/pallas_call | solution.py:308
  51.2 0.6 collective-permute-start.3
  51.8 0.0 collective-permute-done.1
  51.8 0.1 collective-permute-start.2
  51.9 0.9 %collective-permute-done.3 = f32[8,2,2048]{2,1,0:T(2,128)S(1)} collective-permute-done((f32[8,2,2048]{2,1,0:T(2,128)S(1)}, f32[8,2,2048]{2,1,0:T(2,128)S(1)}, u32[]{:S(2)}, u32[]{:S(2)}) %collective-permute-start.3) | collective-permute-done | bytes 131104 | tf_op jit(solution)/shard_map/ppermute | solution.py:224
  52.8 1.2 %collective-permute-start.4 = (f32[4,1,2,2048]{3,2,1,0:T(2,128)S(1)}, f32[4,1,2,2048]{3,2,1,0:T(2,128)S(1)}, u32[]{:S(2)}, u32[]{:S(2)}) collective-permute-start(f32[4,1,2,2048]{3,2,1,0:T(2,128)S(1)} %get-tuple-element.24), channel_id=1, source_target_pairs={{0,2},{2,0},{1,3},{3,1},{4,6},{6,4},{5,7},{7,5},{8,10},{10,8},{9,1... | collective-permute-start | bytes 196616 | tf_op jit(solution)/shard_map/ppermute | solution.py:224
  54.0 2.6 %collective-permute-done.2.refs_1_ = f32[4,1,2,2048]{3,2,1,0:T(2,128)S(1)} collective-permute-done((f32[4,1,2,2048]{3,2,1,0:T(2,128)S(1)}, f32[4,1,2,2048]{3,2,1,0:T(2,128)S(1)}, u32[]{:S(2)}, u32[]{:S(2)}) %collective-permute-start.2) | collective-permute-done | bytes 65568 | tf_op jit(solution)/shard_map/ppermute | solution.py:224
  56.5 1.0 %collective-permute-done.4.refs_3_ = f32[4,1,2,2048]{3,2,1,0:T(2,128)S(1)} collective-permute-done((f32[4,1,2,2048]{3,2,1,0:T(2,128)S(1)}, f32[4,1,2,2048]{3,2,1,0:T(2,128)S(1)}, u32[]{:S(2)}, u32[]{:S(2)}) %collective-permute-start.4) | collective-permute-done | bytes 65568 | tf_op jit(solution)/shard_map/ppermute | solution.py:224
  57.5 0.1 shard_map.109
  57.6 0.8 %collective-permute-start.5 = (bf16[2,4096]{1,0:T(2,128)(2,1)S(1)}, bf16[2,4096]{1,0:T(2,128)(2,1)S(1)}, u32[]{:S(2)}, u32[]{:S(2)}) collective-permute-start(bf16[2,4096]{1,0:T(2,128)(2,1)S(1)} %get-tuple-element.25), channel_id=1, source_target_pairs={{0,12},{4,8},{8,4},{12,0},{1,13},{5,9},{9,5},{13,1},{2,14},{6,10},... | collective-permute-start | bytes 49160 | tf_op jit(solution)/shard_map/ppermute | solution.py:224
  58.4 0.5 collective-permute-start.6
  58.9 3.2 %collective-permute-start.7 = (bf16[2,4096]{1,0:T(2,128)(2,1)S(1)}, bf16[2,4096]{1,0:T(2,128)(2,1)S(1)}, u32[]{:S(2)}, u32[]{:S(2)}) collective-permute-start(bf16[2,4096]{1,0:T(2,128)(2,1)S(1)} %get-tuple-element.27), channel_id=1, source_target_pairs={{0,4},{4,0},{8,12},{12,8},{1,5},{5,1},{9,13},{13,9},{2,6},{6,2},{1... | collective-permute-start | bytes 49160 | tf_op jit(solution)/shard_map/ppermute | solution.py:224
  62.0 1.1 %collective-permute-done.5.refs_0_ = bf16[2,4096]{1,0:T(2,128)(2,1)S(1)} collective-permute-done((bf16[2,4096]{1,0:T(2,128)(2,1)S(1)}, bf16[2,4096]{1,0:T(2,128)(2,1)S(1)}, u32[]{:S(2)}, u32[]{:S(2)}) %collective-permute-start.5) | collective-permute-done | bytes 16416 | tf_op jit(solution)/shard_map/ppermute | solution.py:224
  63.2 0.0 collective-permute-done.6.refs_1_
  63.2 0.6 collective-permute-done.7.refs_2_
  63.8 0.6 shard_map.110
  (3 shorter events, 0.0 us)
Async XLA Ops:
  0.0 1.2 %copy-start.3 = (f32[16384]{0:T(1024)S(1)}, f32[16384]{0:T(1024)}, u32[]{:S(2)}) copy-start(f32[16384]{0:T(1024)} %param.11) | copy-start | bytes 196612
  0.0 16.8 %copy-start.2 = (bf16[4096,256]{1,0:T(8,128)(2,1)S(1)}, bf16[4096,256]{1,0:T(8,128)(2,1)}, u32[]{:S(2)}) copy-start(bf16[4096,256]{1,0:T(8,128)(2,1)} %value_ref.3) | copy-start | bytes 6291460
  0.0 16.8 %copy-start.1 = (bf16[4096,256]{1,0:T(8,128)(2,1)S(1)}, bf16[4096,256]{1,0:T(8,128)(2,1)}, u32[]{:S(2)}) copy-start(bf16[4096,256]{1,0:T(8,128)(2,1)} %key_ref.3) | copy-start | bytes 6291460
  0.0 16.8 %copy-start = (bf16[4096,2048]{1,0:T(8,128)(2,1)S(1)}, bf16[4096,2048]{1,0:T(8,128)(2,1)}, u32[]{:S(2)}) copy-start(bf16[4096,2048]{1,0:T(8,128)(2,1)} %query_ref.3) | copy-start | bytes 50331652
  0.0 1.0 %copy-start.6 = (bf16[2,16384]{1,0:T(2,128)(2,1)S(1)}, bf16[2,16384]{1,0:T(2,128)(2,1)}, u32[]{:S(2)}) copy-start(bf16[2,16384]{1,0:T(2,128)(2,1)} %tokens_ref.1) | copy-start | bytes 196612
  16.7 18.0 %copy-start.4 = (bf16[2,256,1024]{2,1,0:T(8,128)(2,1)S(1)}, bf16[2,256,1024]{2,1,0:T(8,128)(2,1)}, u32[]{:S(2)}) copy-start(bf16[2,256,1024]{2,1,0:T(8,128)(2,1)} %keys_ref.1) | copy-start | bytes 3145732
  16.7 18.0 %copy-start.5 = (bf16[2,256,1024]{2,1,0:T(8,128)(2,1)S(1)}, bf16[2,256,1024]{2,1,0:T(8,128)(2,1)}, u32[]{:S(2)}) copy-start(bf16[2,256,1024]{2,1,0:T(8,128)(2,1)} %values_ref.1) | copy-start | bytes 3145732
  16.7 18.0 %copy-start.7 = (s32[2]{0:T(128)S(1)}, s32[2]{0:T(128)}, u32[]{:S(2)}) copy-start(s32[2]{0:T(128)} %lengths_ref.1) | copy-start | bytes 28
  16.7 18.0 %copy-start.8 = (f32[1,128]{1,0:T(1,128)S(1)}, f32[1,128]{1,0:T(1,128)}, u32[]{:S(2)}) copy-start(f32[1,128]{1,0:T(1,128)} %constant.2.clone.frequency_ref) | copy-start | bytes 1540
  16.7 2.0 %collective-permute-start = (bf16[16,2,2048]{2,1,0:T(2,128)(2,1)S(1)}, bf16[16,2,2048]{2,1,0:T(2,128)(2,1)S(1)}, u32[]{:S(2)}, u32[]{:S(2)}) collective-permute-start(bf16[16,2,2048]{2,1,0:T(2,128)(2,1)S(1)} %all_to_all.15.rows_ref), channel_id=1, source_target_pairs={{0,1},{1,0},{2,3},{3,2},{4,5},{5,4},{6,7},{7,6},{8,9},{9,8},{10,11... | collective-permute-start | bytes 393224 | tf_op jit(solution)/shard_map/ppermute | solution.py:224
  16.8 31.1 %slice-start = ((s8[16777216]{0:T(1024)(128)(4,1)}), s8[4194304]{0:T(1024)(128)(4,1)S(1)}, s32[]{:S(2)}) async-start(s8[16777216]{0:T(1024)(128)(4,1)} %bitcast.5), calls=%async_computation.3 | async-start | bytes 8388608
  16.8 31.1 %slice-start.1 = ((s8[16777216]{0:T(1024)(128)(4,1)}), s8[4194304]{0:T(1024)(128)(4,1)S(1)}, s32[]{:S(2)}) async-start(s8[16777216]{0:T(1024)(128)(4,1)} %bitcast.5), calls=%async_computation.4 | async-start | bytes 8388608
  18.7 29.2 %slice-start.2 = ((s8[16777216]{0:T(1024)(128)(4,1)}), s8[4194304]{0:T(1024)(128)(4,1)S(1)}, s32[]{:S(2)}) async-start(s8[16777216]{0:T(1024)(128)(4,1)} %bitcast.5), calls=%async_computation.5 | async-start | bytes 8388608
  18.7 29.2 %slice-start.3 = ((s8[16777216]{0:T(1024)(128)(4,1)}), s8[4194304]{0:T(1024)(128)(4,1)S(1)}, s32[]{:S(2)}) async-start(s8[16777216]{0:T(1024)(128)(4,1)} %bitcast.5), calls=%async_computation.6 | async-start | bytes 8388608
  49.5 2.2 %collective-permute-start.1 = (f32[8,2,2048]{2,1,0:T(2,128)S(1)}, f32[8,2,2048]{2,1,0:T(2,128)S(1)}, u32[]{:S(2)}, u32[]{:S(2)}) collective-permute-start(f32[8,2,2048]{2,1,0:T(2,128)S(1)} %get-tuple-element.18), channel_id=1, source_target_pairs={{0,1},{1,0},{2,3},{3,2},{4,5},{5,4},{6,7},{7,6},{8,9},{9,8},{10,11... | collective-permute-start | bytes 393224 | tf_op jit(solution)/shard_map/ppermute | solution.py:224
  51.2 1.5 %collective-permute-start.3 = (f32[8,2,2048]{2,1,0:T(2,128)S(1)}, f32[8,2,2048]{2,1,0:T(2,128)S(1)}, u32[]{:S(2)}, u32[]{:S(2)}) collective-permute-start(f32[8,2,2048]{2,1,0:T(2,128)S(1)} %get-tuple-element.22), channel_id=1, source_target_pairs={{0,1},{1,0},{2,3},{3,2},{4,5},{5,4},{6,7},{7,6},{8,9},{9,8},{10,11... | collective-permute-start | bytes 393224 | tf_op jit(solution)/shard_map/ppermute | solution.py:224
  51.8 4.7 %collective-permute-start.2 = (f32[4,1,2,2048]{3,2,1,0:T(2,128)S(1)}, f32[4,1,2,2048]{3,2,1,0:T(2,128)S(1)}, u32[]{:S(2)}, u32[]{:S(2)}) collective-permute-start(f32[4,1,2,2048]{3,2,1,0:T(2,128)S(1)} %get-tuple-element.20), channel_id=1, source_target_pairs={{0,2},{2,0},{1,3},{3,1},{4,6},{6,4},{5,7},{7,5},{8,10},{10,8},{9,1... | collective-permute-start | bytes 196616 | tf_op jit(solution)/shard_map/ppermute | solution.py:224
  52.8 4.8 %collective-permute-start.4 = (f32[4,1,2,2048]{3,2,1,0:T(2,128)S(1)}, f32[4,1,2,2048]{3,2,1,0:T(2,128)S(1)}, u32[]{:S(2)}, u32[]{:S(2)}) collective-permute-start(f32[4,1,2,2048]{3,2,1,0:T(2,128)S(1)} %get-tuple-element.24), channel_id=1, source_target_pairs={{0,2},{2,0},{1,3},{3,1},{4,6},{6,4},{5,7},{7,5},{8,10},{10,8},{9,1... | collective-permute-start | bytes 196616 | tf_op jit(solution)/shard_map/ppermute | solution.py:224
  57.6 5.6 %collective-permute-start.5 = (bf16[2,4096]{1,0:T(2,128)(2,1)S(1)}, bf16[2,4096]{1,0:T(2,128)(2,1)S(1)}, u32[]{:S(2)}, u32[]{:S(2)}) collective-permute-start(bf16[2,4096]{1,0:T(2,128)(2,1)S(1)} %get-tuple-element.25), channel_id=1, source_target_pairs={{0,12},{4,8},{8,4},{12,0},{1,13},{5,9},{9,5},{13,1},{2,14},{6,10},... | collective-permute-start | bytes 49160 | tf_op jit(solution)/shard_map/ppermute | solution.py:224
  58.4 4.8 %collective-permute-start.6 = (bf16[2,4096]{1,0:T(2,128)(2,1)S(1)}, bf16[2,4096]{1,0:T(2,128)(2,1)S(1)}, u32[]{:S(2)}, u32[]{:S(2)}) collective-permute-start(bf16[2,4096]{1,0:T(2,128)(2,1)S(1)} %get-tuple-element.26), channel_id=1, source_target_pairs={{0,8},{4,12},{8,0},{12,4},{1,9},{5,13},{9,1},{13,5},{2,10},{6,14},... | collective-permute-start | bytes 49160 | tf_op jit(solution)/shard_map/ppermute | solution.py:224
  58.9 4.9 %collective-permute-start.7 = (bf16[2,4096]{1,0:T(2,128)(2,1)S(1)}, bf16[2,4096]{1,0:T(2,128)(2,1)S(1)}, u32[]{:S(2)}, u32[]{:S(2)}) collective-permute-start(bf16[2,4096]{1,0:T(2,128)(2,1)S(1)} %get-tuple-element.27), channel_id=1, source_target_pairs={{0,4},{4,0},{8,12},{12,8},{1,5},{5,1},{9,13},{13,9},{2,6},{6,2},{1... | collective-permute-start | bytes 49160 | tf_op jit(solution)/shard_map/ppermute | solution.py:224

commit v6 on v5

v6 whole, which is shorter than its diff:
```python
import functools

import jax
import jax.numpy as jnp
import numpy as np
from jax import lax
from jax.experimental import pallas as pl
from jax.experimental.pallas import tpu as pltpu
from jax.sharding import PartitionSpec as P

HD = 128
ROW_AXES = ("gx", "gy", "gz")
PLANE = ("gy", "gz")
MIB = 1024 * 1024
IN_VMEM = pl.BlockSpec(memory_space=pltpu.VMEM)
IN_SMEM = pl.BlockSpec(memory_space=pltpu.SMEM)


def scale_kernel(tokens_ref, scaled_ref):
    tokens = tokens_ref[...].astype(jnp.float32)
    mean_square = jnp.mean(tokens * tokens, -1, keepdims=True)
    scaled_ref[...] = tokens * lax.rsqrt(mean_square + 1e-05)


def gain_kernel(wide, plane, scaled_ref, gain_ref, blocks_ref):
    normed = (scaled_ref[...] * gain_ref[...]).astype(jnp.bfloat16)
    half = normed.shape[1] // wide // 2
    for i in range(wide):
        for j in range(plane):
            at = (2 * i + j % 2) * half
            blocks_ref[i * plane + j] = normed[:, at : at + half]


def project_kernel(own, wide, plane, rows_ref, query_ref, key_ref, value_ref, _, *refs):
    owners, rows, half = rows_ref.shape
    core = lax.axis_index("gz")
    at_row = pl.multiple_of((core if own else 1 - core) * half, half)
    normed = rows_ref[...].reshape(owners * rows, half)
    sums_ref = refs[-1]
    at = 0
    for weight in (query_ref, key_ref, value_ref):
        cols = weight.shape[1]
        step = min(cols, 256)
        for c in range(0, cols, step):
            part = jnp.dot(
                normed,
                weight[pl.ds(at_row, half), c : c + step],
                preferred_element_type=jnp.float32,
            )
            if own:
                sums_ref[:, at : at + step] = part
            else:
                part = part + refs[0][:, at : at + step]
                sums_ref[:, :, at : at + step] = part.reshape(owners, rows, step)
            at += step
    if not own:
        own_wide = lax.axis_index("gx")
        own_plane = 2 * lax.axis_index("gy") + core
        for k in range(wide):
            for l in range(plane):
                refs[1 + k][l] = sums_ref[(own_wide ^ k) * plane + (own_plane ^ l)]


def share_kernel(plane, lengths_ref, keys_ref, values_ref, _, *blocks):
    rows, slots, _ = keys_ref.shape
    cols = blocks[0].shape[1]
    own_plane = 2 * lax.axis_index("gy") + lax.axis_index("gz")
    at_row = lax.broadcasted_iota(jnp.int32, (16, cols), 0)
    filled = jnp.zeros((16, cols), jnp.float32)
    for r in range(rows):
        filled = jnp.where(at_row == r, lengths_ref[r].astype(jnp.float32), filled)
    for l in range(plane):
        at = pl.multiple_of((own_plane ^ l) * cols, cols)
        for c, cache in enumerate((keys_ref, values_ref)):
            for r in range(rows):
                to = (c * rows + r) * slots
                blocks[l][to : to + slots] = cache[r, :, pl.ds(at, cols)]
        blocks[l][2 * rows * slots :] = filled.astype(jnp.bfloat16)


def attend_kernel(wide, plane, query_cols, frequency_ref, *refs):
    partials, shared, attended_ref = refs[wide - 1 :: -1], refs[wide:-1], refs[-1]
    rows, cols = partials[0].shape[1:]
    kv_cols = (cols - query_cols) // 2
    kv_heads, group = kv_cols // HD, query_cols // kv_cols
    slots = (shared[0].shape[0] - 16) // (2 * rows)
    pairs = plane * rows
    count = pairs * kv_heads
    heads = count * group
    scale = 1.0 / HD**0.5
    total = partials[0][...]
    for k in range(1, wide):
        total = total + partials[k][...]
    total = total.reshape(pairs, cols).astype(jnp.bfloat16).astype(jnp.float32)

    filled = [
        shared[p // rows][2 * rows * slots : 2 * rows * slots + 16, :HD]
        .astype(jnp.float32)[p % rows : p % rows + 1]
        for p in range(pairs)
    ]
    angles = jnp.concatenate(filled, 0) * frequency_ref[...]
    cosine, sine = jnp.cos(angles), jnp.sin(angles)
    front = lax.broadcasted_iota(jnp.int32, (1, HD), 1) < HD // 2
    sine = jnp.where(front, -sine, sine)

    def rotate(vector):
        return vector * cosine + pltpu.roll(vector, HD // 2, 1) * sine

    query, key_new, value_new = [], [], []
    for h in range(kv_heads):
        turned = [
            rotate(total[:, (h * group + g) * HD : (h * group + g + 1) * HD]) for g in range(group)
        ]
        query.append(jnp.swapaxes(jnp.stack(turned, 0), 0, 1))
        at = query_cols + h * HD
        key_new.append(rotate(total[:, at : at + HD]))
        value_new.append(total[:, at + kv_cols : at + kv_cols + HD])
    query = jnp.stack(query, 1).reshape(heads, HD)
    turned_query = query.T.astype(jnp.bfloat16)
    key_new = jnp.stack(key_new, 1).reshape(count, HD).astype(jnp.bfloat16)
    value_new = jnp.stack(value_new, 1).reshape(count, HD)

    def cached(c):
        return jnp.concatenate(
            [
                shared[p // rows][(c * rows + p % rows) * slots : (c * rows + p % rows + 1) * slots]
                for p in range(pairs)
            ],
            1,
        )

    head_pair = lax.broadcasted_iota(jnp.int32, (1, heads), 1) // group
    by_pair = jnp.concatenate(
        [jnp.where(head_pair == b, turned_query, jnp.zeros_like(turned_query)) for b in range(count)],
        0,
    )
    scores = scale * jnp.dot(cached(0), by_pair, preferred_element_type=jnp.float32)
    own = scale * jnp.dot(key_new, turned_query, preferred_element_type=jnp.float32)
    of_pair = lax.broadcasted_iota(jnp.int32, (count, 1), 0) == head_pair
    own = jnp.sum(jnp.where(of_pair, own, 0.0), 0, keepdims=True)
    length = jnp.zeros((1, heads), jnp.float32)
    for p in range(pairs):
        length = jnp.where(head_pair // kv_heads == p, filled[p][:, :1], length)
    slot = lax.broadcasted_iota(jnp.int32, (slots, 1), 0).astype(jnp.float32)
    scores = jnp.where(slot < length, scores, -1e30)
    top = jnp.maximum(jnp.max(scores, 0, keepdims=True), own)
    weights = jnp.exp(scores - top)
    own_weight = jnp.exp(own - top)
    denominator = jnp.sum(weights, 0, keepdims=True) + own_weight
    probability = (weights / denominator).astype(jnp.bfloat16)
    own_prob = (own_weight / denominator).astype(jnp.bfloat16)
    contract_rows = (((0,), (0,)), ((), ()))
    mixed = lax.dot_general(
        probability, cached(1), contract_rows, preferred_element_type=jnp.float32
    )
    own_prob = jnp.where(of_pair, own_prob.astype(jnp.float32), 0.0).astype(jnp.bfloat16)
    fresh = lax.dot_general(
        own_prob, value_new.astype(jnp.bfloat16), contract_rows, preferred_element_type=jnp.float32
    )
    mixed = [
        mixed[b * group : (b + 1) * group, b * HD : (b + 1) * HD]
        + fresh[b * group : (b + 1) * group]
        for b in range(count)
    ]
    attended = []
    for h in range(kv_heads):
        by_head = jnp.swapaxes(jnp.stack(mixed[h::kv_heads], 0), 0, 1)
        attended += [by_head[g] for g in range(group)]
    attended = jnp.concatenate(attended, 1)
    attended_ref[...] = attended.reshape(plane, rows, query_cols).astype(jnp.bfloat16)


def output_kernel(at, cols, weight_ref, *refs):
    blocks, keep_ref, give_ref = refs[:-2], refs[-2], refs[-1]
    wide = len(blocks)
    plane, rows, depth = blocks[0].shape
    attended = jnp.concatenate(
        [block[...].reshape(plane * rows, depth) for block in blocks], 0
    )
    step = min(cols, 512)
    for c in range(0, cols, step):
        part = jnp.dot(
            attended, weight_ref[:, at + c : at + c + step], preferred_element_type=jnp.float32
        )
        part = part.reshape(wide * plane // 2, 2 * rows, step)
        keep_ref[:, :, c : c + step] = part[:, :rows]
        give_ref[:, :, c : c + step] = part[:, rows:]


def halve_kernel(a_ref, b_ref, keep_ref, give_ref):
    for n in range(keep_ref.shape[0]):
        keep_ref[n] = a_ref[2 * n] + b_ref[2 * n]
        give_ref[n] = a_ref[2 * n + 1] + b_ref[2 * n + 1]


def total_kernel(parts, *refs):
    sums, blocks = refs[: 2 * parts], refs[2 * parts :]
    cols = sums[0].shape[-1]
    for p in range(parts):
        for k, block in enumerate(blocks):
            total = sums[2 * p][k] + sums[2 * p + 1][k]
            block[:, p * cols : (p + 1) * cols] = total.astype(jnp.bfloat16)


def finish_kernel(*refs):
    blocks, result_ref = refs[-2::-1], refs[-1]
    own = lax.axis_index("gx")
    cols = blocks[0].shape[-1]
    for k, block in enumerate(blocks):
        at = pl.multiple_of((own ^ k) * cols, cols)
        result_ref[:, pl.ds(at, cols)] = block[...]


def swap_blocks(blocks, axes):
    return lax.all_to_all(blocks, axes, split_axis=0, concat_axis=0, tiled=True)


def swap_pairs(value, axis, step):
    return lax.ppermute(value, axis, [(i, i ^ step) for i in range(lax.axis_size(axis))])


def swap_plane(value, step):
    return lax.ppermute(value, PLANE, [(i, i ^ step) for i in range(lax.axis_size(PLANE))])


def swap_wide(blocks):
    moved = [swap_pairs(blocks[k], "gx", k) for k in range(len(blocks) - 1, 0, -1)]
    return [blocks[0]] + moved[::-1]


def shards(
    tokens,
    norm_gain,
    query_weight,
    key_weight,
    value_weight,
    out_weight,
    cache_keys,
    cache_values,
    lengths,
):
    rows = tokens.shape[0]
    wide = lax.axis_size("gx")
    plane = lax.axis_size(PLANE)
    owners = wide * plane
    width, query_cols = query_weight.shape
    kv_cols = key_weight.shape[1]
    depth, out_cols = out_weight.shape
    cols = query_cols + 2 * kv_cols

    def params(mib):
        return pltpu.CompilerParams(vmem_limit_bytes=mib * MIB)

    def cost(flops, size):
        return pl.CostEstimate(flops=flops, bytes_accessed=size, transcendentals=0)

    half = width // 2
    scaled = pl.pallas_call(
        scale_kernel,
        out_shape=jax.ShapeDtypeStruct(tokens.shape, jnp.float32),
        in_specs=[IN_VMEM],
        out_specs=IN_VMEM,
        compiler_params=params(8),
        cost_estimate=cost(40 * 10**9, MIB),
    )(tokens)
    normed = pl.pallas_call(
        functools.partial(gain_kernel, wide, plane),
        out_shape=jax.ShapeDtypeStruct((owners, rows, half), jnp.bfloat16),
        in_specs=[IN_VMEM, IN_VMEM],
        out_specs=IN_VMEM,
        compiler_params=params(8),
    )(scaled, norm_gain.reshape(1, -1))
    shared_rows = 2 * rows * cache_keys.shape[1] + 16
    shared = pl.pallas_call(
        functools.partial(share_kernel, plane),
        out_shape=[jax.ShapeDtypeStruct((shared_rows, kv_cols), jnp.bfloat16)] * plane,
        in_specs=[IN_SMEM] + [IN_VMEM] * 3,
        out_specs=[IN_VMEM] * plane,
        compiler_params=params(8),
    )(lengths, cache_keys, cache_values, normed)
    shared = [shared[0]] + [swap_plane(shared[l], l) for l in range(1, plane)]
    own_half = swap_blocks(normed, ROW_AXES)
    other_half = swap_pairs(own_half, "gz", 1)
    weights = (query_weight, key_weight, value_weight)
    half_cost = cost(owners * rows * width * cols, width * cols)
    partial = pl.pallas_call(
        functools.partial(project_kernel, True, wide, plane),
        out_shape=jax.ShapeDtypeStruct((owners * rows, cols), jnp.float32),
        in_specs=[IN_VMEM] * 5,
        out_specs=IN_VMEM,
        compiler_params=params(8),
        cost_estimate=half_cost,
    )(own_half, *weights, shared[1])
    partial = pl.pallas_call(
        functools.partial(project_kernel, False, wide, plane),
        out_shape=[jax.ShapeDtypeStruct((plane, rows, cols), jnp.float32)] * wide,
        in_specs=[IN_VMEM] * 6,
        out_specs=[IN_VMEM] * wide,
        scratch_shapes=[pltpu.VMEM((owners, rows, cols), jnp.float32)],
        compiler_params=params(8),
        cost_estimate=half_cost,
    )(other_half, *weights, shared[1], partial)
    partial = swap_wide(partial)

    half_dim = HD // 2
    frequency = 500000.0 ** (-np.arange(half_dim, dtype=np.float64) / half_dim)
    frequency = np.tile(frequency.astype(np.float32), 2).reshape(1, HD)
    attended = pl.pallas_call(
        functools.partial(attend_kernel, wide, plane, query_cols),
        out_shape=jax.ShapeDtypeStruct((plane, rows, query_cols), jnp.bfloat16),
        in_specs=[IN_VMEM] * (1 + wide + plane),
        out_specs=IN_VMEM,
        compiler_params=params(8),
        cost_estimate=cost(10**9, 4 * MIB),
    )(jnp.asarray(frequency), *partial[::-1], *shared)
    head_rows = swap_wide([attended] * wide)
    parts = 2
    part_cols = out_cols // parts
    sums = []
    for p in range(parts):
        count = owners // 2
        shape = jax.ShapeDtypeStruct((count, rows, part_cols), jnp.float32)
        keep, give = pl.pallas_call(
            functools.partial(output_kernel, p * part_cols, part_cols),
            out_shape=(shape, shape),
            in_specs=[IN_VMEM] * (1 + wide),
            out_specs=(IN_VMEM, IN_VMEM),
            compiler_params=params(8),
            cost_estimate=cost(2 * owners * rows * depth * part_cols, 2 * depth * part_cols),
        )(out_weight, *head_rows)
        give = swap_plane(give, 1)
        step = 2
        while step < plane:
            count //= 2
            shape = jax.ShapeDtypeStruct((count, rows, part_cols), jnp.float32)
            keep, give = pl.pallas_call(
                halve_kernel,
                out_shape=(shape, shape),
                in_specs=[IN_VMEM, IN_VMEM],
                out_specs=(IN_VMEM, IN_VMEM),
                compiler_params=params(8),
            )(keep, give)
            give = swap_plane(give, step)
            step *= 2
        sums += [keep, give]
    blocks = pl.pallas_call(
        functools.partial(total_kernel, parts),
        out_shape=[jax.ShapeDtypeStruct((rows, out_cols), jnp.bfloat16)] * wide,
        in_specs=[IN_VMEM] * len(sums),
        out_specs=[IN_VMEM] * wide,
        compiler_params=params(8),
    )(*sums)
    blocks = swap_wide(blocks)
    return pl.pallas_call(
        finish_kernel,
        out_shape=jax.ShapeDtypeStruct((rows, wide * out_cols), jnp.bfloat16),
        in_specs=[IN_VMEM] * wide,
        out_specs=IN_VMEM,
        compiler_params=params(8),
    )(*blocks[::-1])


def solution(mesh):
    placed = (
        P(("groups", "gx", "gy", "gz"), None),
        P(),
        P("gx", ("gy", "gz")),
        P("gx", ("gy", "gz")),
        P("gx", ("gy", "gz")),
        P(("gy", "gz"), "gx"),
        P(("groups", "gx", "gy", "gz"), None, None),
        P(("groups", "gx", "gy", "gz"), None, None),
        P(("groups", "gx", "gy", "gz")),
    )
    return jax.shard_map(
        shards,
        mesh=mesh,
        in_specs=placed,
        out_specs=P(("groups", "gx", "gy", "gz"), None),
        check_vma=False,
    )
```

time: 64.6 us -> 72 us (1.11)
  blocking collectives: 40.3 us -> 25.4 us
  starting transfers between devices: 6.43 us -> 20 us
  waiting for transfers between devices: 6.14 us -> 15.1 us
    all_to_all x3 -> x1, blocking collectives: 40.3 us -> 25.4 us  [swap_blocks(): return lax.all_to_all(blocks, axes, split_axis=0, concat_axis=0, tiled=True)]
    ppermute x8 -> x10, starting transfers between devices: 6.43 us -> 13.6 us  [swap_pairs(): lax.ppermute(value, axis, [(i, i ^ step) for i in range(lax.axis_size(axi...]
    ppermute x0 -> x7, starting transfers between devices: none -> 6.37 us  [swap_plane(): lax.ppermute(value, PLANE, [(i, i ^ step) for i in range(lax.axis_size(PL...]
    ppermute x8 -> x10, waiting for transfers between devices: 6.14 us -> 11.7 us  [swap_pairs(): lax.ppermute(value, axis, [(i, i ^ step) for i in range(lax.axis_size(axi...]
    ppermute x0 -> x7, waiting for transfers between devices: none -> 3.37 us  [swap_plane(): lax.ppermute(value, PLANE, [(i, i ^ step) for i in range(lax.axis_size(PL...]
    pallas_call x5 -> x6, Pallas kernels: 6.77 us -> 6.5 us  [the longest x1 1.97 us: shards(): pl.pallas_call(functools.partial(project_kernel, False, wide, plane), out...]
  transfers between devices with their start and end apart: 8 -> 17, of which waited for: 5 -> 8; matrix products, arithmetic and copies ran while one was open for 0% -> 0% of each run, Pallas kernels for 5% -> 8%
where the time goes in v6:
time: 72 us; the launch traced here: 71.9 us
  blocking collectives  25.4 us (35%)
  starting transfers between devices  20 us (28%)
  waiting for transfers between devices  15.1 us (21%)
  Pallas kernels  9.94 us (14%)
  local copies, waits for them, and re-layouts  1.27 us (2%)
    all_to_all x1, blocking collectives, swap_blocks(): return lax.all_to_all(blocks, axes, split_axis=0, concat_axis=0, tiled=True)  25.4 us
    ppermute x10, starting transfers between devices, swap_pairs(): lax.ppermute(value, axis, [(i, i ^ step) for i in range(lax.axis_size(axi...  13.6 us
    ppermute x10, waiting for transfers between devices, swap_pairs(): lax.ppermute(value, axis, [(i, i ^ step) for i in range(lax.axis_size(axi...  11.7 us
    ppermute x7, starting transfers between devices, swap_plane(): lax.ppermute(value, PLANE, [(i, i ^ step) for i in range(lax.axis_size(PL...  6.37 us
    ppermute x7, waiting for transfers between devices, swap_plane(): lax.ppermute(value, PLANE, [(i, i ^ step) for i in range(lax.axis_size(PL...  3.37 us
    pallas_call x2, Pallas kernels, shards(): pl.pallas_call(functools.partial(output_kernel, p * part_cols, part_cols)...  3.1 us
    pallas_call x1, Pallas kernels, shards(): pl.pallas_call(functools.partial(project_kernel, False, wide, plane), out...  1.97 us
    pallas_call x1, Pallas kernels, shards(): pl.pallas_call(functools.partial(project_kernel, True, wide, plane), out_...  1.9 us
  transfers between devices with their start and end apart: 17, of which 8 were waited for; matrix products, arithmetic and copies ran while one was open for 0% of the time, Pallas kernels for 8%

profile of v6, /device:TPU:0, one launch (start us, length us, event | category | flops | bytes accessed | tf_op | source)
XLA Modules:
  0.0 71.9 jit_solution(5095636889482953638)
XLA Ops:
  0.0 0.0 copy-start.5
  0.0 0.0 copy-start.1
  0.0 0.0 copy-start
  0.0 0.0 copy-start.7
  0.0 1.0 %copy-done.7 = bf16[2,16384]{1,0:T(2,128)(2,1)S(1)} copy-done((bf16[2,16384]{1,0:T(2,128)(2,1)S(1)}, bf16[2,16384]{1,0:T(2,128)(2,1)}, u32[]{:S(2)}) %copy-start.7) | copy-done | bytes 65560
  1.0 0.2 shard_map.100.scaled_ref
  1.3 0.0 copy-done.5
  1.3 0.1 shard_map.101._
  1.4 0.0 copy-done.6
  1.4 0.0 copy-done.4
  1.4 0.2 copy-done.3
  1.6 0.8 %shard_map.102 = (bf16[1040,256]{1,0:T(8,128)(2,1)S(1)}, bf16[1040,256]{1,0:T(8,128)(2,1)S(1)}, bf16[1040,256]{1,0:T(8,128)(2,1)S(1)}, bf16[1040,256]{1,0:T(8,128)(2,1)S(1)}) custom-call(s32[2]{0:T(128)S(1)} %copy-done.6, bf16[2,256,1024]{2,1,0:T(8,128)(2,1)S(1)} %copy-done.3, bf16[2,256,1024]{2,1,0:T(8,128)(2,1)S(1)} %copy-done.4, ...), custom_call_target="tpu_custom_call" | custom-call | tf_op jit(solution)/shard_map/pallas_call | solution.py:274
  2.5 0.5 collective-permute-start.1
  3.0 2.6 %collective-permute-start.5 = (bf16[1040,256]{1,0:T(8,128)(2,1)S(1)}, bf16[1040,256]{1,0:T(8,128)(2,1)S(1)}, u32[]{:S(2)}, u32[]{:S(2)}) collective-permute-start(bf16[1040,256]{1,0:T(8,128)(2,1)S(1)} %get-tuple-element.31), channel_id=1, source_target_pairs={{0,2},{1,3},{2,0},{3,1},{4,6},{5,7},{6,4},{7,5},{8,10},{9,11},{10,... | collective-permute-start | bytes 1597448 | tf_op jit(solution)/shard_map/ppermute | solution.py:223
  5.5 0.1 collective-permute-start.6
  5.6 25.4 %all_to_all.5.rows_ref = bf16[16,2,2048]{2,1,0:T(2,128)(2,1)S(1)} all-to-all(bf16[16,2,2048]{2,1,0:T(2,128)(2,1)S(1)} %shard_map.101._), channel_id=1, replica_groups=mesh['groups'=2,'gx'=4,'gy'=2,'gz'=2] {'gx','gy','gz'}, dimensions={0} | all-to-all | bytes 262144 | tf_op jit(solution)/shard_map/all_to_all | solution.py:215
  31.0 0.1 collective-permute-start
  31.1 0.0 collective-permute-done.1._.refs_5_
  31.1 0.0 copy-done.2
  31.1 0.0 copy-done.1
  31.1 0.0 copy-done
  31.1 0.0 slice-start
  31.1 0.0 slice-start.1
  31.1 1.9 %shard_map.103.refs_0_ = f32[32,2560]{1,0:T(8,128)S(1)} custom-call(bf16[16,2,2048]{2,1,0:T(2,128)(2,1)S(1)} %all_to_all.5.rows_ref, bf16[4096,2048]{1,0:T(8,128)(2,1)S(1)} %copy-done, bf16[4096,256]{1,0:T(8,128)(2,1)S(1)} %copy-done.1, bf16[4096,256]{1,0:T(8,128)(2,1)S(1)} %copy-done.2, bf16[1040,256]{1,0:T(8,128)(2,1)S(1)} %collective-permute-done.1._.refs_5_), custom_call_target="tpu_custom_call" | custom-call | flops 335544320 | bytes 10485760 | tf_op jit(solution)/shard_map/pallas_call | solution.py:286
  33.0 0.0 collective-permute-done.rows_ref
  33.0 2.0 %shard_map.104 = (f32[4,2,2560]{2,1,0:T(2,128)S(1)}, f32[4,2,2560]{2,1,0:T(2,128)S(1)}, f32[4,2,2560]{2,1,0:T(2,128)S(1)}, f32[4,2,2560]{2,1,0:T(2,128)S(1)}) custom-call(bf16[16,2,2048]{2,1,0:T(2,128)(2,1)S(1)} %collective-permute-done.rows_ref, bf16[4096,2048]{1,0:T(8,128)(2,1)S(1)} %copy-done, bf16[4096,256]{1,0:T(8,128)(2,1)S(1)} %copy-done.1, ...), custom_call_target="tpu_custom_call" | custom-call | flops 335544320 | bytes 10485760 | tf_op jit(solution)/shard_map/pallas_call | solution.py:294
  35.0 3.9 %collective-permute-start.2 = (f32[4,2,2560]{2,1,0:T(2,128)S(1)}, f32[4,2,2560]{2,1,0:T(2,128)S(1)}, u32[]{:S(2)}, u32[]{:S(2)}) collective-permute-start(f32[4,2,2560]{2,1,0:T(2,128)S(1)} %get-tuple-element.26), channel_id=1, source_target_pairs={{0,12},{4,8},{8,4},{12,0},{1,13},{5,9},{9,5},{13,1},{2,14},{6,10},... | collective-permute-start | bytes 245768 | tf_op jit(solution)/shard_map/ppermute | solution.py:219
  39.0 0.0 collective-permute-start.3
  39.0 0.6 collective-permute-start.4
  39.6 0.0 collective-permute-done.5.refs_6_
  39.6 0.0 collective-permute-done.6.refs_7_
  39.6 2.7 %collective-permute-done.2.refs_0_ = f32[4,2,2560]{2,1,0:T(2,128)S(1)} collective-permute-done((f32[4,2,2560]{2,1,0:T(2,128)S(1)}, f32[4,2,2560]{2,1,0:T(2,128)S(1)}, u32[]{:S(2)}, u32[]{:S(2)}) %collective-permute-start.2) | collective-permute-done | bytes 81952 | tf_op jit(solution)/shard_map/ppermute | solution.py:219
  42.4 4.1 %collective-permute-done.3.refs_1_ = f32[4,2,2560]{2,1,0:T(2,128)S(1)} collective-permute-done((f32[4,2,2560]{2,1,0:T(2,128)S(1)}, f32[4,2,2560]{2,1,0:T(2,128)S(1)}, u32[]{:S(2)}, u32[]{:S(2)}) %collective-permute-start.3) | collective-permute-done | bytes 81952 | tf_op jit(solution)/shard_map/ppermute | solution.py:219
  46.4 0.0 collective-permute-done.4.refs_2_
  46.4 0.0 copy-done.8
  46.4 1.1 %shard_map.105.refs_0_ = bf16[4,2,2048]{2,1,0:T(2,128)(2,1)S(1)} custom-call(f32[1,128]{1,0:T(1,128)S(1)} %copy-done.8, f32[4,2,2560]{2,1,0:T(2,128)S(1)} %collective-permute-done.2.refs_0_, f32[4,2,2560]{2,1,0:T(2,128)S(1)} %collective-permute-done.3.refs_1_, f32[4,2,2560]{2,1,0:T(2,128)S(1)} %collective-permute-done.4.refs_2_, ...), custom_call_target="tpu_custom_call" | custom-call | flops 1000000000 | bytes 4194304 | tf_op jit(solution)/shard_map/pallas_call | solution.py:308
  47.5 2.5 %collective-permute-start.9 = (bf16[4,2,2048]{2,1,0:T(2,128)(2,1)S(1)}, bf16[4,2,2048]{2,1,0:T(2,128)(2,1)S(1)}, u32[]{:S(2)}, u32[]{:S(2)}) collective-permute-start(bf16[4,2,2048]{2,1,0:T(2,128)(2,1)S(1)} %shard_map.105.refs_0_), channel_id=1, source_target_pairs={{0,12},{4,8},{8,4},{12,0},{1,13},{5,9},{9,5},{13,1},{2,14},{6,10},... | collective-permute-start | bytes 98312 | tf_op jit(solution)/shard_map/ppermute | solution.py:219
  50.1 0.0 collective-permute-start.8
  50.1 1.9 %collective-permute-start.7 = (bf16[4,2,2048]{2,1,0:T(2,128)(2,1)S(1)}, bf16[4,2,2048]{2,1,0:T(2,128)(2,1)S(1)}, u32[]{:S(2)}, u32[]{:S(2)}) collective-permute-start(bf16[4,2,2048]{2,1,0:T(2,128)(2,1)S(1)} %shard_map.105.refs_0_), channel_id=1, source_target_pairs={{0,4},{4,0},{8,12},{12,8},{1,5},{5,1},{9,13},{13,9},{2,6},{6,2},{1... | collective-permute-start | bytes 98312 | tf_op jit(solution)/shard_map/ppermute | solution.py:219
  52.0 1.4 %collective-permute-done.9.refs_3_ = bf16[4,2,2048]{2,1,0:T(2,128)(2,1)S(1)} collective-permute-done((bf16[4,2,2048]{2,1,0:T(2,128)(2,1)S(1)}, bf16[4,2,2048]{2,1,0:T(2,128)(2,1)S(1)}, u32[]{:S(2)}, u32[]{:S(2)}) %collective-permute-start.9) | collective-permute-done | bytes 32800 | tf_op jit(solution)/shard_map/ppermute | solution.py:219
  53.4 1.5 %collective-permute-done.8.refs_2_ = bf16[4,2,2048]{2,1,0:T(2,128)(2,1)S(1)} collective-permute-done((bf16[4,2,2048]{2,1,0:T(2,128)(2,1)S(1)}, bf16[4,2,2048]{2,1,0:T(2,128)(2,1)S(1)}, u32[]{:S(2)}, u32[]{:S(2)}) %collective-permute-start.8) | collective-permute-done | bytes 32800 | tf_op jit(solution)/shard_map/ppermute | solution.py:219
  54.9 0.0 collective-permute-done.7.refs_1_
  54.9 0.0 slice-done
  54.9 0.0 slice-done.1
  54.9 0.0 slice-done.2
  54.9 0.0 slice-done.3
  54.9 1.5 %shard_map.106 = (f32[8,2,2048]{2,1,0:T(2,128)S(1)}, f32[8,2,2048]{2,1,0:T(2,128)S(1)}) custom-call(bf16[2048,4096]{1,0:T(8,128)(2,1)S(1)} %bitcast.2, bf16[4,2,2048]{2,1,0:T(2,128)(2,1)S(1)} %shard_map.105.refs_0_, bf16[4,2,2048]{2,1,0:T(2,128)(2,1)S(1)} %collective-permute-done.7.refs_1_, bf16[4,2,2048]{2,1,0:T(2,128)(2,1)S(1)} %collective-permute-done.8.refs_2_, ...), custom_call_target="tpu_custom_call" | custom-call | flops 268435456 | bytes 8388608 | tf_op jit(solution)/shard_map/pallas_call | solution.py:323
  56.5 0.1 collective-permute-start.10
  56.6 1.5 %shard_map.108 = (f32[8,2,2048]{2,1,0:T(2,128)S(1)}, f32[8,2,2048]{2,1,0:T(2,128)S(1)}) custom-call(bf16[2048,4096]{1,0:T(8,128)(2,1)S(1)} %bitcast.2, bf16[4,2,2048]{2,1,0:T(2,128)(2,1)S(1)} %shard_map.105.refs_0_, bf16[4,2,2048]{2,1,0:T(2,128)(2,1)S(1)} %collective-permute-done.7.refs_1_, bf16[4,2,2048]{2,1,0:T(2,128)(2,1)S(1)} %collective-permute-done.8.refs_2_, ...), custom_call_target="tpu_custom_call" | custom-call | flops 268435456 | bytes 8388608 | tf_op jit(solution)/shard_map/pallas_call | solution.py:323
  58.1 0.6 collective-permute-start.12
  58.7 0.0 collective-permute-done.10.b_ref
  58.7 1.6 %collective-permute-start.11 = (f32[4,2,2048]{2,1,0:T(2,128)S(1)}, f32[4,2,2048]{2,1,0:T(2,128)S(1)}, u32[]{:S(2)}, u32[]{:S(2)}) collective-permute-start(f32[4,2,2048]{2,1,0:T(2,128)S(1)} %get-tuple-element.36), channel_id=1, source_target_pairs={{0,2},{1,3},{2,0},{3,1},{4,6},{5,7},{6,4},{7,5},{8,10},{9,11},{10,... | collective-permute-start | bytes 196616 | tf_op jit(solution)/shard_map/ppermute | solution.py:223
  60.3 0.0 collective-permute-done.12.b_ref
  60.3 1.0 %collective-permute-start.13 = (f32[4,2,2048]{2,1,0:T(2,128)S(1)}, f32[4,2,2048]{2,1,0:T(2,128)S(1)}, u32[]{:S(2)}, u32[]{:S(2)}) collective-permute-start(f32[4,2,2048]{2,1,0:T(2,128)S(1)} %get-tuple-element.40), channel_id=1, source_target_pairs={{0,2},{1,3},{2,0},{3,1},{4,6},{5,7},{6,4},{7,5},{8,10},{9,11},{10,... | collective-permute-start | bytes 196616 | tf_op jit(solution)/shard_map/ppermute | solution.py:223
  61.3 2.1 %collective-permute-done.11.refs_1_ = f32[4,2,2048]{2,1,0:T(2,128)S(1)} collective-permute-done((f32[4,2,2048]{2,1,0:T(2,128)S(1)}, f32[4,2,2048]{2,1,0:T(2,128)S(1)}, u32[]{:S(2)}, u32[]{:S(2)}) %collective-permute-start.11) | collective-permute-done | bytes 65568 | tf_op jit(solution)/shard_map/ppermute | solution.py:223
  63.4 1.3 %collective-permute-done.13.refs_3_ = f32[4,2,2048]{2,1,0:T(2,128)S(1)} collective-permute-done((f32[4,2,2048]{2,1,0:T(2,128)S(1)}, f32[4,2,2048]{2,1,0:T(2,128)S(1)}, u32[]{:S(2)}, u32[]{:S(2)}) %collective-permute-start.13) | collective-permute-done | bytes 65568 | tf_op jit(solution)/shard_map/ppermute | solution.py:223
  64.7 0.1 shard_map.110
  64.7 1.8 %collective-permute-start.14 = (bf16[2,4096]{1,0:T(2,128)(2,1)S(1)}, bf16[2,4096]{1,0:T(2,128)(2,1)S(1)}, u32[]{:S(2)}, u32[]{:S(2)}) collective-permute-start(bf16[2,4096]{1,0:T(2,128)(2,1)S(1)} %get-tuple-element.41), channel_id=1, source_target_pairs={{0,12},{4,8},{8,4},{12,0},{1,13},{5,9},{9,5},{13,1},{2,14},{6,10},... | collective-permute-start | bytes 49160 | tf_op jit(solution)/shard_map/ppermute | solution.py:219
  66.6 0.7 collective-permute-start.15
  67.3 1.9 %collective-permute-start.16 = (bf16[2,4096]{1,0:T(2,128)(2,1)S(1)}, bf16[2,4096]{1,0:T(2,128)(2,1)S(1)}, u32[]{:S(2)}, u32[]{:S(2)}) collective-permute-start(bf16[2,4096]{1,0:T(2,128)(2,1)S(1)} %get-tuple-element.43), channel_id=1, source_target_pairs={{0,4},{4,0},{8,12},{12,8},{1,5},{5,1},{9,13},{13,9},{2,6},{6,2},{1... | collective-permute-start | bytes 49160 | tf_op jit(solution)/shard_map/ppermute | solution.py:219
  69.2 1.1 %collective-permute-done.14.refs_0_ = bf16[2,4096]{1,0:T(2,128)(2,1)S(1)} collective-permute-done((bf16[2,4096]{1,0:T(2,128)(2,1)S(1)}, bf16[2,4096]{1,0:T(2,128)(2,1)S(1)}, u32[]{:S(2)}, u32[]{:S(2)}) %collective-permute-start.14) | collective-permute-done | bytes 16416 | tf_op jit(solution)/shard_map/ppermute | solution.py:219
  70.3 0.9 %collective-permute-done.15.refs_1_ = bf16[2,4096]{1,0:T(2,128)(2,1)S(1)} collective-permute-done((bf16[2,4096]{1,0:T(2,128)(2,1)S(1)}, bf16[2,4096]{1,0:T(2,128)(2,1)S(1)}, u32[]{:S(2)}, u32[]{:S(2)}) %collective-permute-start.15) | collective-permute-done | bytes 16416 | tf_op jit(solution)/shard_map/ppermute | solution.py:219
  71.2 0.0 collective-permute-done.16.refs_2_
  71.2 0.6 shard_map.111
  (10 shorter events, 0.0 us)
Async XLA Ops:
  0.0 1.3 %copy-start.5 = (f32[16384]{0:T(1024)S(1)}, f32[16384]{0:T(1024)}, u32[]{:S(2)}) copy-start(f32[16384]{0:T(1024)} %param.11) | copy-start | bytes 196612
  0.0 1.4 %copy-start.6 = (s32[2]{0:T(128)S(1)}, s32[2]{0:T(128)}, u32[]{:S(2)}) copy-start(s32[2]{0:T(128)} %lengths_ref.1) | copy-start | bytes 28
  0.0 1.4 %copy-start.4 = (bf16[2,256,1024]{2,1,0:T(8,128)(2,1)S(1)}, bf16[2,256,1024]{2,1,0:T(8,128)(2,1)}, u32[]{:S(2)}) copy-start(bf16[2,256,1024]{2,1,0:T(8,128)(2,1)} %values_ref.1) | copy-start | bytes 3145732
  0.0 1.6 %copy-start.3 = (bf16[2,256,1024]{2,1,0:T(8,128)(2,1)S(1)}, bf16[2,256,1024]{2,1,0:T(8,128)(2,1)}, u32[]{:S(2)}) copy-start(bf16[2,256,1024]{2,1,0:T(8,128)(2,1)} %keys_ref.1) | copy-start | bytes 3145732
  0.0 31.1 %copy-start.2 = (bf16[4096,256]{1,0:T(8,128)(2,1)S(1)}, bf16[4096,256]{1,0:T(8,128)(2,1)}, u32[]{:S(2)}) copy-start(bf16[4096,256]{1,0:T(8,128)(2,1)} %value_ref.3) | copy-start | bytes 6291460
  0.0 31.1 %copy-start.1 = (bf16[4096,256]{1,0:T(8,128)(2,1)S(1)}, bf16[4096,256]{1,0:T(8,128)(2,1)}, u32[]{:S(2)}) copy-start(bf16[4096,256]{1,0:T(8,128)(2,1)} %key_ref.3) | copy-start | bytes 6291460
  0.0 31.1 %copy-start = (bf16[4096,2048]{1,0:T(8,128)(2,1)S(1)}, bf16[4096,2048]{1,0:T(8,128)(2,1)}, u32[]{:S(2)}) copy-start(bf16[4096,2048]{1,0:T(8,128)(2,1)} %query_ref.3) | copy-start | bytes 50331652
  0.0 1.0 %copy-start.7 = (bf16[2,16384]{1,0:T(2,128)(2,1)S(1)}, bf16[2,16384]{1,0:T(2,128)(2,1)}, u32[]{:S(2)}) copy-start(bf16[2,16384]{1,0:T(2,128)(2,1)} %tokens_ref.1) | copy-start | bytes 196612
  2.5 28.6 %collective-permute-start.1 = (bf16[1040,256]{1,0:T(8,128)(2,1)S(1)}, bf16[1040,256]{1,0:T(8,128)(2,1)S(1)}, u32[]{:S(2)}, u32[]{:S(2)}) collective-permute-start(bf16[1040,256]{1,0:T(8,128)(2,1)S(1)} %get-tuple-element.25), channel_id=1, source_target_pairs={{0,1},{1,0},{2,3},{3,2},{4,5},{5,4},{6,7},{7,6},{8,9},{9,8},{10,11... | collective-permute-start | bytes 1597448 | tf_op jit(solution)/shard_map/ppermute | solution.py:223
  3.0 36.6 %collective-permute-start.5 = (bf16[1040,256]{1,0:T(8,128)(2,1)S(1)}, bf16[1040,256]{1,0:T(8,128)(2,1)S(1)}, u32[]{:S(2)}, u32[]{:S(2)}) collective-permute-start(bf16[1040,256]{1,0:T(8,128)(2,1)S(1)} %get-tuple-element.31), channel_id=1, source_target_pairs={{0,2},{1,3},{2,0},{3,1},{4,6},{5,7},{6,4},{7,5},{8,10},{9,11},{10,... | collective-permute-start | bytes 1597448 | tf_op jit(solution)/shard_map/ppermute | solution.py:223
  5.5 34.1 %collective-permute-start.6 = (bf16[1040,256]{1,0:T(8,128)(2,1)S(1)}, bf16[1040,256]{1,0:T(8,128)(2,1)S(1)}, u32[]{:S(2)}, u32[]{:S(2)}) collective-permute-start(bf16[1040,256]{1,0:T(8,128)(2,1)S(1)} %get-tuple-element.32), channel_id=1, source_target_pairs={{0,3},{1,2},{2,1},{3,0},{4,7},{5,6},{6,5},{7,4},{8,11},{9,10},{10,... | collective-permute-start | bytes 1597448 | tf_op jit(solution)/shard_map/ppermute | solution.py:223
  31.0 15.5 %copy-start.8 = (f32[1,128]{1,0:T(1,128)S(1)}, f32[1,128]{1,0:T(1,128)}, u32[]{:S(2)}) copy-start(f32[1,128]{1,0:T(1,128)} %constant.2.clone.frequency_ref) | copy-start | bytes 1540
  31.0 2.1 %collective-permute-start = (bf16[16,2,2048]{2,1,0:T(2,128)(2,1)S(1)}, bf16[16,2,2048]{2,1,0:T(2,128)(2,1)S(1)}, u32[]{:S(2)}, u32[]{:S(2)}) collective-permute-start(bf16[16,2,2048]{2,1,0:T(2,128)(2,1)S(1)} %all_to_all.5.rows_ref), channel_id=1, source_target_pairs={{0,1},{1,0},{2,3},{3,2},{4,5},{5,4},{6,7},{7,6},{8,9},{9,8},{10,11... | collective-permute-start | bytes 393224 | tf_op jit(solution)/shard_map/ppermute | solution.py:219
  31.1 23.8 %slice-start = ((s8[16777216]{0:T(1024)(128)(4,1)}), s8[4194304]{0:T(1024)(128)(4,1)S(1)}, s32[]{:S(2)}) async-start(s8[16777216]{0:T(1024)(128)(4,1)} %bitcast.1), calls=%async_computation.1 | async-start | bytes 8388608
  31.1 23.8 %slice-start.1 = ((s8[16777216]{0:T(1024)(128)(4,1)}), s8[4194304]{0:T(1024)(128)(4,1)S(1)}, s32[]{:S(2)}) async-start(s8[16777216]{0:T(1024)(128)(4,1)} %bitcast.1), calls=%async_computation.2 | async-start | bytes 8388608
  33.0 21.9 %slice-start.2 = ((s8[16777216]{0:T(1024)(128)(4,1)}), s8[4194304]{0:T(1024)(128)(4,1)S(1)}, s32[]{:S(2)}) async-start(s8[16777216]{0:T(1024)(128)(4,1)} %bitcast.1), calls=%async_computation.3 | async-start | bytes 8388608
  33.0 21.9 %slice-start.3 = ((s8[16777216]{0:T(1024)(128)(4,1)}), s8[4194304]{0:T(1024)(128)(4,1)S(1)}, s32[]{:S(2)}) async-start(s8[16777216]{0:T(1024)(128)(4,1)} %bitcast.1), calls=%async_computation.4 | async-start | bytes 8388608
  35.0 7.3 %collective-permute-start.2 = (f32[4,2,2560]{2,1,0:T(2,128)S(1)}, f32[4,2,2560]{2,1,0:T(2,128)S(1)}, u32[]{:S(2)}, u32[]{:S(2)}) collective-permute-start(f32[4,2,2560]{2,1,0:T(2,128)S(1)} %get-tuple-element.26), channel_id=1, source_target_pairs={{0,12},{4,8},{8,4},{12,0},{1,13},{5,9},{9,5},{13,1},{2,14},{6,10},... | collective-permute-start | bytes 245768 | tf_op jit(solution)/shard_map/ppermute | solution.py:219
  39.0 7.5 %collective-permute-start.3 = (f32[4,2,2560]{2,1,0:T(2,128)S(1)}, f32[4,2,2560]{2,1,0:T(2,128)S(1)}, u32[]{:S(2)}, u32[]{:S(2)}) collective-permute-start(f32[4,2,2560]{2,1,0:T(2,128)S(1)} %get-tuple-element.27), channel_id=1, source_target_pairs={{0,8},{4,12},{8,0},{12,4},{1,9},{5,13},{9,1},{13,5},{2,10},{6,14},... | collective-permute-start | bytes 245768 | tf_op jit(solution)/shard_map/ppermute | solution.py:219
  39.0 7.5 %collective-permute-start.4 = (f32[4,2,2560]{2,1,0:T(2,128)S(1)}, f32[4,2,2560]{2,1,0:T(2,128)S(1)}, u32[]{:S(2)}, u32[]{:S(2)}) collective-permute-start(f32[4,2,2560]{2,1,0:T(2,128)S(1)} %get-tuple-element.28), channel_id=1, source_target_pairs={{0,4},{4,0},{8,12},{12,8},{1,5},{5,1},{9,13},{13,9},{2,6},{6,2},{1... | collective-permute-start | bytes 245768 | tf_op jit(solution)/shard_map/ppermute | solution.py:219
  47.5 5.9 %collective-permute-start.9 = (bf16[4,2,2048]{2,1,0:T(2,128)(2,1)S(1)}, bf16[4,2,2048]{2,1,0:T(2,128)(2,1)S(1)}, u32[]{:S(2)}, u32[]{:S(2)}) collective-permute-start(bf16[4,2,2048]{2,1,0:T(2,128)(2,1)S(1)} %shard_map.105.refs_0_), channel_id=1, source_target_pairs={{0,12},{4,8},{8,4},{12,0},{1,13},{5,9},{9,5},{13,1},{2,14},{6,10},... | collective-permute-start | bytes 98312 | tf_op jit(solution)/shard_map/ppermute | solution.py:219
  50.1 4.8 %collective-permute-start.8 = (bf16[4,2,2048]{2,1,0:T(2,128)(2,1)S(1)}, bf16[4,2,2048]{2,1,0:T(2,128)(2,1)S(1)}, u32[]{:S(2)}, u32[]{:S(2)}) collective-permute-start(bf16[4,2,2048]{2,1,0:T(2,128)(2,1)S(1)} %shard_map.105.refs_0_), channel_id=1, source_target_pairs={{0,8},{4,12},{8,0},{12,4},{1,9},{5,13},{9,1},{13,5},{2,10},{6,14},... | collective-permute-start | bytes 98312 | tf_op jit(solution)/shard_map/ppermute | solution.py:219
  50.1 4.8 %collective-permute-start.7 = (bf16[4,2,2048]{2,1,0:T(2,128)(2,1)S(1)}, bf16[4,2,2048]{2,1,0:T(2,128)(2,1)S(1)}, u32[]{:S(2)}, u32[]{:S(2)}) collective-permute-start(bf16[4,2,2048]{2,1,0:T(2,128)(2,1)S(1)} %shard_map.105.refs_0_), channel_id=1, source_target_pairs={{0,4},{4,0},{8,12},{12,8},{1,5},{5,1},{9,13},{13,9},{2,6},{6,2},{1... | collective-permute-start | bytes 98312 | tf_op jit(solution)/shard_map/ppermute | solution.py:219
  56.5 2.2 %collective-permute-start.10 = (f32[8,2,2048]{2,1,0:T(2,128)S(1)}, f32[8,2,2048]{2,1,0:T(2,128)S(1)}, u32[]{:S(2)}, u32[]{:S(2)}) collective-permute-start(f32[8,2,2048]{2,1,0:T(2,128)S(1)} %get-tuple-element.34), channel_id=1, source_target_pairs={{0,1},{1,0},{2,3},{3,2},{4,5},{5,4},{6,7},{7,6},{8,9},{9,8},{10,11... | collective-permute-start | bytes 393224 | tf_op jit(solution)/shard_map/ppermute | solution.py:223
  58.1 2.2 %collective-permute-start.12 = (f32[8,2,2048]{2,1,0:T(2,128)S(1)}, f32[8,2,2048]{2,1,0:T(2,128)S(1)}, u32[]{:S(2)}, u32[]{:S(2)}) collective-permute-start(f32[8,2,2048]{2,1,0:T(2,128)S(1)} %get-tuple-element.38), channel_id=1, source_target_pairs={{0,1},{1,0},{2,3},{3,2},{4,5},{5,4},{6,7},{7,6},{8,9},{9,8},{10,11... | collective-permute-start | bytes 393224 | tf_op jit(solution)/shard_map/ppermute | solution.py:223
  58.7 4.7 %collective-permute-start.11 = (f32[4,2,2048]{2,1,0:T(2,128)S(1)}, f32[4,2,2048]{2,1,0:T(2,128)S(1)}, u32[]{:S(2)}, u32[]{:S(2)}) collective-permute-start(f32[4,2,2048]{2,1,0:T(2,128)S(1)} %get-tuple-element.36), channel_id=1, source_target_pairs={{0,2},{1,3},{2,0},{3,1},{4,6},{5,7},{6,4},{7,5},{8,10},{9,11},{10,... | collective-permute-start | bytes 196616 | tf_op jit(solution)/shard_map/ppermute | solution.py:223
  60.3 4.3 %collective-permute-start.13 = (f32[4,2,2048]{2,1,0:T(2,128)S(1)}, f32[4,2,2048]{2,1,0:T(2,128)S(1)}, u32[]{:S(2)}, u32[]{:S(2)}) collective-permute-start(f32[4,2,2048]{2,1,0:T(2,128)S(1)} %get-tuple-element.40), channel_id=1, source_target_pairs={{0,2},{1,3},{2,0},{3,1},{4,6},{5,7},{6,4},{7,5},{8,10},{9,11},{10,... | collective-permute-start | bytes 196616 | tf_op jit(solution)/shard_map/ppermute | solution.py:223
  64.7 5.6 %collective-permute-start.14 = (bf16[2,4096]{1,0:T(2,128)(2,1)S(1)}, bf16[2,4096]{1,0:T(2,128)(2,1)S(1)}, u32[]{:S(2)}, u32[]{:S(2)}) collective-permute-start(bf16[2,4096]{1,0:T(2,128)(2,1)S(1)} %get-tuple-element.41), channel_id=1, source_target_pairs={{0,12},{4,8},{8,4},{12,0},{1,13},{5,9},{9,5},{13,1},{2,14},{6,10},... | collective-permute-start | bytes 49160 | tf_op jit(solution)/shard_map/ppermute | solution.py:219
  66.6 4.6 %collective-permute-start.15 = (bf16[2,4096]{1,0:T(2,128)(2,1)S(1)}, bf16[2,4096]{1,0:T(2,128)(2,1)S(1)}, u32[]{:S(2)}, u32[]{:S(2)}) collective-permute-start(bf16[2,4096]{1,0:T(2,128)(2,1)S(1)} %get-tuple-element.42), channel_id=1, source_target_pairs={{0,8},{4,12},{8,0},{12,4},{1,9},{5,13},{9,1},{13,5},{2,10},{6,14},... | collective-permute-start | bytes 49160 | tf_op jit(solution)/shard_map/ppermute | solution.py:219
  67.3 4.0 %collective-permute-start.16 = (bf16[2,4096]{1,0:T(2,128)(2,1)S(1)}, bf16[2,4096]{1,0:T(2,128)(2,1)S(1)}, u32[]{:S(2)}, u32[]{:S(2)}) collective-permute-start(bf16[2,4096]{1,0:T(2,128)(2,1)S(1)} %get-tuple-element.43), channel_id=1, source_target_pairs={{0,4},{4,0},{8,12},{12,8},{1,5},{5,1},{9,13},{13,9},{2,6},{6,2},{1... | collective-permute-start | bytes 49160 | tf_op jit(solution)/shard_map/ppermute | solution.py:219

commit v7 on v5

--- a/solution.py
+++ b/solution.py
@@ -40,7 +40,7 @@
     at = 0
     for weight in (query_ref, key_ref, value_ref):
         cols = weight.shape[1]
-        step = min(cols, 256)
+        step = min(cols, 2048)
         for c in range(0, cols, step):
             part = jnp.dot(
                 normed,
@@ -56,26 +56,28 @@
 
 
 def attend_kernel(
-    wide, plane, rows, query_cols, kv_cols,
-    lengths_ref, partial_ref, frequency_ref, keys_ref, values_ref, blocks_ref,
+    wide, plane, query_cols, lengths_ref, partial_ref, frequency_ref, keys_ref, values_ref, blocks_ref
 ):
-    slots = keys_ref.shape[1]
-    kv_heads = kv_cols // HD
-    all_kv = kv_heads * plane
-    group = query_cols // kv_cols
+    rows, slots, _ = keys_ref.shape
+    cols = partial_ref.shape[-1]
+    kv_cols = (cols - query_cols) // 2
+    kv_heads, group = kv_cols // HD, query_cols // kv_cols
     pairs = plane * rows
+    count = pairs * kv_heads
+    heads = count * group
     scale = 1.0 / HD**0.5
     total = partial_ref[:plane]
     for i in range(1, wide):
         total = total + partial_ref[i * plane : (i + 1) * plane]
-    total = total.reshape(pairs, total.shape[-1])
-    heads = total.astype(jnp.bfloat16).astype(jnp.float32)
-
-    row_of = lax.broadcasted_iota(jnp.int32, (pairs, 1), 0) % rows
-    position = jnp.zeros((pairs, 1), jnp.int32)
-    for r in range(rows):
-        position = jnp.where(row_of == r, lengths_ref[r], position)
-    angles = position.astype(jnp.float32) * frequency_ref[...]
+    total = total.reshape(pairs, cols).astype(jnp.bfloat16).astype(jnp.float32)
+
+    def by_row(index):
+        spread = jnp.zeros(index.shape, jnp.float32)
+        for r in range(rows):
+            spread = jnp.where(index == r, lengths_ref[r].astype(jnp.float32), spread)
+        return spread
+
+    angles = by_row(lax.broadcasted_iota(jnp.int32, (pairs, 1), 0) % rows) * frequency_ref[...]
     cosine, sine = jnp.cos(angles), jnp.sin(angles)
     front = lax.broadcasted_iota(jnp.int32, (1, HD), 1) < HD // 2
     sine = jnp.where(front, -sine, sine)
@@ -85,74 +87,61 @@
 
     query, key_new, value_new = [], [], []
     for h in range(kv_heads):
-        turned = jnp.stack(
-            [
-                rotate(heads[:, (h * group + g) * HD : (h * group + g + 1) * HD])
-                for g in range(group)
-            ],
-            0,
-        )
-        query.append(jnp.swapaxes(turned, 0, 1))
+        turned = [
+            rotate(total[:, (h * group + g) * HD : (h * group + g + 1) * HD]) for g in range(group)
+        ]
+        query.append(jnp.swapaxes(jnp.stack(turned, 0), 0, 1))
         at = query_cols + h * HD
-        key_new.append(rotate(heads[:, at : at + HD]))
-        at = query_cols + kv_cols + h * HD
-        value_new.append(heads[:, at : at + HD])
-
-    def row_vector(parts, r):
+        key_new.append(rotate(total[:, at : at + HD]))
+        value_new.append(total[:, at + kv_cols : at + kv_cols + HD])
+    query = jnp.stack(query, 1).reshape(heads, HD)
+    turned_query = query.T.astype(jnp.bfloat16)
+    key_new = jnp.stack(key_new, 1).reshape(count, HD).astype(jnp.bfloat16)
+    value_new = jnp.stack(value_new, 1).reshape(count, HD)
+
+    def cached(cache_ref):
         return jnp.concatenate(
             [
-                parts[h][j * rows + r : j * rows + r + 1]
-                for j in range(plane)
-                for h in range(kv_heads)
+                cache_ref[p % rows, :, p // rows * kv_cols : (p // rows + 1) * kv_cols]
+                for p in range(pairs)
             ],
             1,
         )
 
-    first = lax.broadcasted_iota(jnp.int32, (16, 1), 0) == 0
-    slot = lax.broadcasted_iota(jnp.int32, (slots, 1), 0)
-    mixed = [[None] * pairs for h in range(kv_heads)]
-    for r in range(rows):
-        wide_query = []
-        for kv in range(all_kv):
-            j, h = kv // kv_heads, kv % kv_heads
-            parts = [query[h][j * rows + r]]
-            if kv:
-                parts.insert(0, jnp.zeros((group, kv * HD), jnp.float32))
-            if kv < all_kv - 1:
-                parts.append(jnp.zeros((group, (all_kv - 1 - kv) * HD), jnp.float32))
-            wide_query.append(jnp.concatenate(parts, 1))
-        wide_query = jnp.concatenate(wide_query, 0).astype(jnp.bfloat16)
-        contract_lanes = (((1,), (1,)), ((), ()))
-        contract_rows = (((0,), (0,)), ((), ()))
-        own_key = jnp.where(first, row_vector(key_new, r), 0.0).astype(jnp.bfloat16)
-        own_value = jnp.where(first, row_vector(value_new, r), 0.0).astype(jnp.bfloat16)
-        scores = scale * lax.dot_general(
-            keys_ref[r], wide_query, contract_lanes, preferred_element_type=jnp.float32
-        )
-        own = scale * lax.dot_general(
-            own_key, wide_query, contract_lanes, preferred_element_type=jnp.float32
-        )
-        scores = jnp.where(slot < lengths_ref[r], scores, -1e30)
-        own = own[:1]
-        top = jnp.maximum(jnp.max(scores, 0, keepdims=True), own)
-        weights = jnp.exp(scores - top)
-        own_weight = jnp.exp(own - top)
-        denominator = jnp.sum(weights, 0, keepdims=True) + own_weight
-        probability = (weights / denominator).astype(jnp.bfloat16)
-        own_prob = jnp.where(first, own_weight / denominator, 0.0).astype(jnp.bfloat16)
-        mix = lax.dot_general(
-            probability, values_ref[r], contract_rows, preferred_element_type=jnp.float32
-        )
-        mix = mix + lax.dot_general(
-            own_prob, own_value, contract_rows, preferred_element_type=jnp.float32
-        )
-        for kv in range(all_kv):
-            mixed[kv % kv_heads][kv // kv_heads * rows + r] = mix[
-                kv * group : (kv + 1) * group, kv * HD : (kv + 1) * HD
-            ]
+    head_pair = lax.broadcasted_iota(jnp.int32, (1, heads), 1) // group
+    by_pair = jnp.concatenate(
+        [jnp.where(head_pair == b, turned_query, jnp.zeros_like(turned_query)) for b in range(count)],
+        0,
+    )
+    scores = scale * jnp.dot(cached(keys_ref), by_pair, preferred_element_type=jnp.float32)
+    own = scale * jnp.dot(key_new, turned_query, preferred_element_type=jnp.float32)
+    of_pair = lax.broadcasted_iota(jnp.int32, (count, 1), 0) == head_pair
+    own = jnp.sum(jnp.where(of_pair, own, 0.0), 0, keepdims=True)
+    length = by_row(head_pair // kv_heads % rows)
+    slot = lax.broadcasted_iota(jnp.int32, (slots, 1), 0).astype(jnp.float32)
+    scores = jnp.where(slot < length, scores, -1e30)
+    top = jnp.maximum(jnp.max(scores, 0, keepdims=True), own)
+    weights = jnp.exp(scores - top)
+    own_weight = jnp.exp(own - top)
+    denominator = jnp.sum(weights, 0, keepdims=True) + own_weight
+    probability = (weights / denominator).astype(jnp.bfloat16)
+    own_prob = (own_weight / denominator).astype(jnp.bfloat16)
+    contract_rows = (((0,), (0,)), ((), ()))
+    mixed = lax.dot_general(
+        probability, cached(values_ref), contract_rows, preferred_element_type=jnp.float32
+    )
+    own_prob = jnp.where(of_pair, own_prob.astype(jnp.float32), 0.0).astype(jnp.bfloat16)
+    fresh = lax.dot_general(
+        own_prob, value_new.astype(jnp.bfloat16), contract_rows, preferred_element_type=jnp.float32
+    )
+    mixed = [
+        mixed[b * group : (b + 1) * group, b * HD : (b + 1) * HD]
+        + fresh[b * group : (b + 1) * group]
+        for b in range(count)
+    ]
     attended = []
     for h in range(kv_heads):
-        by_head = jnp.swapaxes(jnp.stack(mixed[h], 0), 0, 1)
+        by_head = jnp.swapaxes(jnp.stack(mixed[h::kv_heads], 0), 0, 1)
         attended += [by_head[g] for g in range(group)]
     attended = jnp.concatenate(attended, 1)
     for j in range(plane):
@@ -165,7 +154,7 @@
     owners, rows, depth = rows_ref.shape
     attended = rows_ref[...].reshape(owners * rows, depth)
     mine = lax.axis_index("gz") == 0
-    step = min(cols, 512)
+    step = min(cols, 2048)
     for c in range(0, cols, step):
         part = jnp.dot(
             attended, weight_ref[:, at + c : at + c + step], preferred_element_type=jnp.float32
@@ -292,7 +281,7 @@
     frequency = 500000.0 ** (-np.arange(half_dim, dtype=np.float64) / half_dim)
     frequency = np.tile(frequency.astype(np.float32), 2).reshape(1, HD)
     attended = pl.pallas_call(
-        functools.partial(attend_kernel, wide, plane, rows, query_cols, kv_cols),
+        functools.partial(attend_kernel, wide, plane, query_cols),
         out_shape=jax.ShapeDtypeStruct((owners, rows, query_cols), jnp.bfloat16),
         in_specs=[IN_SMEM] + [IN_VMEM] * 4,
         out_specs=IN_VMEM,

time: 64.6 us -> 64 us (level)
  no operation moved by 1% of the time
where the time goes in v7:
time: 64 us; the launch traced here: 63.8 us
  blocking collectives  40.3 us (63%)
  Pallas kernels  9.66 us (15%)
  starting transfers between devices  6.43 us (10%)
  waiting for transfers between devices  6.14 us (10%)
  local copies, waits for them, and re-layouts  1.04 us (2%)
    all_to_all x3, blocking collectives, swap_blocks(): return lax.all_to_all(blocks, axes, split_axis=0, concat_axis=0, tiled=True)  40.3 us
    ppermute x8, starting transfers between devices, swap_pairs(): lax.ppermute(value, axis, [(i, i ^ step) for i in range(lax.axis_size(axi...  6.43 us
    ppermute x8, waiting for transfers between devices, swap_pairs(): lax.ppermute(value, axis, [(i, i ^ step) for i in range(lax.axis_size(axi...  6.14 us
    pallas_call x2, Pallas kernels, shards(): pl.pallas_call(functools.partial(output_kernel, p * part_cols, part_cols)...  3.14 us
    pallas_call x1, Pallas kernels, shards(): pl.pallas_call(functools.partial(project_kernel, False), out_shape=jax.Sh...  1.94 us
    pallas_call x1, Pallas kernels, shards(): pl.pallas_call(functools.partial(project_kernel, True), out_shape=jax.Sha...  1.89 us
    pallas_call x1, Pallas kernels, shards(): pl.pallas_call(functools.partial(attend_kernel, wide, plane, query_cols),...  1.63 us
  transfers between devices with their start and end apart: 8, of which 5 were waited for; matrix products, arithmetic and copies ran while one was open for 0% of the time, Pallas kernels for 5%

profile of v7, /device:TPU:0, one launch (start us, length us, event | category | flops | bytes accessed | tf_op | source)
XLA Modules:
  0.0 63.8 jit_solution(2415001836186089692)
XLA Ops:
  0.0 0.0 copy-start.3
  0.0 0.0 copy-start.2
  0.0 0.0 copy-start.1
  0.0 0.0 copy-start
  0.0 0.0 copy-start.6
  0.0 1.0 %copy-done.6 = bf16[2,16384]{1,0:T(2,128)(2,1)S(1)} copy-done((bf16[2,16384]{1,0:T(2,128)(2,1)S(1)}, bf16[2,16384]{1,0:T(2,128)(2,1)}, u32[]{:S(2)}) %copy-start.6) | copy-done | bytes 65560
  1.0 0.2 shard_map.100.scaled_ref
  1.2 0.0 copy-done.3
  1.2 0.1 shard_map.101
  1.3 15.4 %all_to_all.15.rows_ref = bf16[16,2,2048]{2,1,0:T(2,128)(2,1)S(1)} all-to-all(bf16[16,2,2048]{2,1,0:T(2,128)(2,1)S(1)} %shard_map.101), channel_id=1, replica_groups=mesh['groups'=2,'gx'=4,'gy'=2,'gz'=2] {'gx','gy','gz'}, dimensions={0} | all-to-all | bytes 262144 | tf_op jit(solution)/shard_map/all_to_all | solution.py:209
  16.7 0.0 copy-start.4
  16.7 0.0 copy-start.5
  16.7 0.0 copy-start.7
  16.7 0.0 copy-start.8
  16.7 0.1 collective-permute-start
  16.8 0.0 copy-done.2
  16.8 0.0 copy-done.1
  16.8 0.0 copy-done
  16.8 0.0 slice-start
  16.8 0.0 slice-start.1
  16.9 1.9 %shard_map.102.refs_0_ = f32[32,2560]{1,0:T(8,128)S(1)} custom-call(bf16[16,2,2048]{2,1,0:T(2,128)(2,1)S(1)} %all_to_all.15.rows_ref, bf16[4096,2048]{1,0:T(8,128)(2,1)S(1)} %copy-done, bf16[4096,256]{1,0:T(8,128)(2,1)S(1)} %copy-done.1, bf16[4096,256]{1,0:T(8,128)(2,1)S(1)} %copy-done.2), custom_call_target="tpu_custom_call" | custom-call | flops 335544320 | bytes 10485760 | tf_op jit(solution)/shard_map/pallas_call | solution.py:262
  18.7 0.0 slice-start.2
  18.7 0.0 slice-start.3
  18.8 0.0 collective-permute-done.rows_ref
  18.8 1.9 %shard_map.103 = f32[16,2,2560]{2,1,0:T(2,128)S(1)} custom-call(bf16[16,2,2048]{2,1,0:T(2,128)(2,1)S(1)} %collective-permute-done.rows_ref, bf16[4096,2048]{1,0:T(8,128)(2,1)S(1)} %copy-done, bf16[4096,256]{1,0:T(8,128)(2,1)S(1)} %copy-done.1, bf16[4096,256]{1,0:T(8,128)(2,1)S(1)} %copy-done.2, f32[32,2560]{1,0:T(8,128)S(1)} %shard_map.102.refs_0_), custom_call_target="tpu_custom_call" | custom-call | flops 335544320 | bytes 10485760 | tf_op jit(solution)/shard_map/pallas_call | solution.py:270
  20.7 14.0 %all_to_all.16.partial_ref = f32[16,2,2560]{2,1,0:T(2,128)S(1)} all-to-all(f32[16,2,2560]{2,1,0:T(2,128)S(1)} %shard_map.103), channel_id=1, replica_groups=mesh['groups'=2,'gx'=4,'gy'=2,'gz'=2] {'gx','gy','gz'}, dimensions={0} | all-to-all | bytes 655360 | tf_op jit(solution)/shard_map/all_to_all | solution.py:209
  34.7 0.0 copy-done.4
  34.7 0.0 copy-done.5
  34.7 0.0 copy-done.7
  34.7 0.0 copy-done.8
  34.7 1.6 %shard_map.104 = bf16[16,2,2048]{2,1,0:T(2,128)(2,1)S(1)} custom-call(s32[2]{0:T(128)S(1)} %copy-done.7, f32[16,2,2560]{2,1,0:T(2,128)S(1)} %all_to_all.16.partial_ref, f32[1,128]{1,0:T(1,128)S(1)} %copy-done.8, bf16[2,256,1024]{2,1,0:T(8,128)(2,1)S(1)} %copy-done.4, bf16[2,256,1024]{2,1,0:T(8,128)(2,1)S(1)} %copy-done.5), custom_call_target="tpu_custom_call" | custom-call | flops 1000000000 | bytes 4194304 | tf_op jit(solution)/shard_map/pallas_call | solution.py:283
  36.3 11.0 %all_to_all.17.rows_ref = bf16[16,2,2048]{2,1,0:T(2,128)(2,1)S(1)} all-to-all(bf16[16,2,2048]{2,1,0:T(2,128)(2,1)S(1)} %shard_map.104), channel_id=1, replica_groups=mesh['groups'=2,'gx'=4,'gy'=2,'gz'=2] {'gx','gy','gz'}, dimensions={0} | all-to-all | bytes 262144 | tf_op jit(solution)/shard_map/all_to_all | solution.py:209
  47.3 0.0 slice-done
  47.3 0.0 slice-done.1
  47.3 0.0 slice-done.2
  47.3 0.0 slice-done.3
  47.3 1.6 %shard_map.105 = (f32[8,2,2048]{2,1,0:T(2,128)S(1)}, f32[8,2,2048]{2,1,0:T(2,128)S(1)}) custom-call(bf16[16,2,2048]{2,1,0:T(2,128)(2,1)S(1)} %all_to_all.17.rows_ref, bf16[2048,4096]{1,0:T(8,128)(2,1)S(1)} %bitcast.6), custom_call_target="tpu_custom_call" | custom-call | flops 268435456 | bytes 8388608 | tf_op jit(solution)/shard_map/pallas_call | solution.py:297
  48.9 0.1 collective-permute-start.1
  49.0 1.6 %shard_map.107 = (f32[8,2,2048]{2,1,0:T(2,128)S(1)}, f32[8,2,2048]{2,1,0:T(2,128)S(1)}) custom-call(bf16[16,2,2048]{2,1,0:T(2,128)(2,1)S(1)} %all_to_all.17.rows_ref, bf16[2048,4096]{1,0:T(8,128)(2,1)S(1)} %bitcast.6), custom_call_target="tpu_custom_call" | custom-call | flops 268435456 | bytes 8388608 | tf_op jit(solution)/shard_map/pallas_call | solution.py:297
  50.6 0.6 collective-permute-start.3
  51.1 0.0 collective-permute-done.1
  51.2 0.1 collective-permute-start.2
  51.3 0.9 %collective-permute-done.3 = f32[8,2,2048]{2,1,0:T(2,128)S(1)} collective-permute-done((f32[8,2,2048]{2,1,0:T(2,128)S(1)}, f32[8,2,2048]{2,1,0:T(2,128)S(1)}, u32[]{:S(2)}, u32[]{:S(2)}) %collective-permute-start.3) | collective-permute-done | bytes 131104 | tf_op jit(solution)/shard_map/ppermute | solution.py:213
  52.2 1.2 %collective-permute-start.4 = (f32[4,1,2,2048]{3,2,1,0:T(2,128)S(1)}, f32[4,1,2,2048]{3,2,1,0:T(2,128)S(1)}, u32[]{:S(2)}, u32[]{:S(2)}) collective-permute-start(f32[4,1,2,2048]{3,2,1,0:T(2,128)S(1)} %get-tuple-element.24), channel_id=1, source_target_pairs={{0,2},{2,0},{1,3},{3,1},{4,6},{6,4},{5,7},{7,5},{8,10},{10,8},{9,1... | collective-permute-start | bytes 196616 | tf_op jit(solution)/shard_map/ppermute | solution.py:213
  53.4 2.6 %collective-permute-done.2.refs_1_ = f32[4,1,2,2048]{3,2,1,0:T(2,128)S(1)} collective-permute-done((f32[4,1,2,2048]{3,2,1,0:T(2,128)S(1)}, f32[4,1,2,2048]{3,2,1,0:T(2,128)S(1)}, u32[]{:S(2)}, u32[]{:S(2)}) %collective-permute-start.2) | collective-permute-done | bytes 65568 | tf_op jit(solution)/shard_map/ppermute | solution.py:213
  55.9 1.0 %collective-permute-done.4.refs_3_ = f32[4,1,2,2048]{3,2,1,0:T(2,128)S(1)} collective-permute-done((f32[4,1,2,2048]{3,2,1,0:T(2,128)S(1)}, f32[4,1,2,2048]{3,2,1,0:T(2,128)S(1)}, u32[]{:S(2)}, u32[]{:S(2)}) %collective-permute-start.4) | collective-permute-done | bytes 65568 | tf_op jit(solution)/shard_map/ppermute | solution.py:213
  56.9 0.1 shard_map.109
  57.0 0.8 %collective-permute-start.5 = (bf16[2,4096]{1,0:T(2,128)(2,1)S(1)}, bf16[2,4096]{1,0:T(2,128)(2,1)S(1)}, u32[]{:S(2)}, u32[]{:S(2)}) collective-permute-start(bf16[2,4096]{1,0:T(2,128)(2,1)S(1)} %get-tuple-element.25), channel_id=1, source_target_pairs={{0,12},{4,8},{8,4},{12,0},{1,13},{5,9},{9,5},{13,1},{2,14},{6,10},... | collective-permute-start | bytes 49160 | tf_op jit(solution)/shard_map/ppermute | solution.py:213
  57.8 0.5 collective-permute-start.6
  58.3 3.2 %collective-permute-start.7 = (bf16[2,4096]{1,0:T(2,128)(2,1)S(1)}, bf16[2,4096]{1,0:T(2,128)(2,1)S(1)}, u32[]{:S(2)}, u32[]{:S(2)}) collective-permute-start(bf16[2,4096]{1,0:T(2,128)(2,1)S(1)} %get-tuple-element.27), channel_id=1, source_target_pairs={{0,4},{4,0},{8,12},{12,8},{1,5},{5,1},{9,13},{13,9},{2,6},{6,2},{1... | collective-permute-start | bytes 49160 | tf_op jit(solution)/shard_map/ppermute | solution.py:213
  61.4 1.1 %collective-permute-done.5.refs_0_ = bf16[2,4096]{1,0:T(2,128)(2,1)S(1)} collective-permute-done((bf16[2,4096]{1,0:T(2,128)(2,1)S(1)}, bf16[2,4096]{1,0:T(2,128)(2,1)S(1)}, u32[]{:S(2)}, u32[]{:S(2)}) %collective-permute-start.5) | collective-permute-done | bytes 16416 | tf_op jit(solution)/shard_map/ppermute | solution.py:213
  62.6 0.0 collective-permute-done.6.refs_1_
  62.6 0.6 collective-permute-done.7.refs_2_
  63.1 0.6 shard_map.110
  (3 shorter events, 0.0 us)
Async XLA Ops:
  0.0 1.2 %copy-start.3 = (f32[16384]{0:T(1024)S(1)}, f32[16384]{0:T(1024)}, u32[]{:S(2)}) copy-start(f32[16384]{0:T(1024)} %param.11) | copy-start | bytes 196612
  0.0 16.8 %copy-start.2 = (bf16[4096,256]{1,0:T(8,128)(2,1)S(1)}, bf16[4096,256]{1,0:T(8,128)(2,1)}, u32[]{:S(2)}) copy-start(bf16[4096,256]{1,0:T(8,128)(2,1)} %value_ref.3) | copy-start | bytes 6291460
  0.0 16.8 %copy-start.1 = (bf16[4096,256]{1,0:T(8,128)(2,1)S(1)}, bf16[4096,256]{1,0:T(8,128)(2,1)}, u32[]{:S(2)}) copy-start(bf16[4096,256]{1,0:T(8,128)(2,1)} %key_ref.3) | copy-start | bytes 6291460
  0.0 16.8 %copy-start = (bf16[4096,2048]{1,0:T(8,128)(2,1)S(1)}, bf16[4096,2048]{1,0:T(8,128)(2,1)}, u32[]{:S(2)}) copy-start(bf16[4096,2048]{1,0:T(8,128)(2,1)} %query_ref.3) | copy-start | bytes 50331652
  0.0 1.0 %copy-start.6 = (bf16[2,16384]{1,0:T(2,128)(2,1)S(1)}, bf16[2,16384]{1,0:T(2,128)(2,1)}, u32[]{:S(2)}) copy-start(bf16[2,16384]{1,0:T(2,128)(2,1)} %tokens_ref.1) | copy-start | bytes 196612
  16.7 18.0 %copy-start.4 = (bf16[2,256,1024]{2,1,0:T(8,128)(2,1)S(1)}, bf16[2,256,1024]{2,1,0:T(8,128)(2,1)}, u32[]{:S(2)}) copy-start(bf16[2,256,1024]{2,1,0:T(8,128)(2,1)} %keys_ref.1) | copy-start | bytes 3145732
  16.7 18.0 %copy-start.5 = (bf16[2,256,1024]{2,1,0:T(8,128)(2,1)S(1)}, bf16[2,256,1024]{2,1,0:T(8,128)(2,1)}, u32[]{:S(2)}) copy-start(bf16[2,256,1024]{2,1,0:T(8,128)(2,1)} %values_ref.1) | copy-start | bytes 3145732
  16.7 18.0 %copy-start.7 = (s32[2]{0:T(128)S(1)}, s32[2]{0:T(128)}, u32[]{:S(2)}) copy-start(s32[2]{0:T(128)} %lengths_ref.1) | copy-start | bytes 28
  16.7 18.0 %copy-start.8 = (f32[1,128]{1,0:T(1,128)S(1)}, f32[1,128]{1,0:T(1,128)}, u32[]{:S(2)}) copy-start(f32[1,128]{1,0:T(1,128)} %constant.2.clone.frequency_ref) | copy-start | bytes 1540
  16.7 2.0 %collective-permute-start = (bf16[16,2,2048]{2,1,0:T(2,128)(2,1)S(1)}, bf16[16,2,2048]{2,1,0:T(2,128)(2,1)S(1)}, u32[]{:S(2)}, u32[]{:S(2)}) collective-permute-start(bf16[16,2,2048]{2,1,0:T(2,128)(2,1)S(1)} %all_to_all.15.rows_ref), channel_id=1, source_target_pairs={{0,1},{1,0},{2,3},{3,2},{4,5},{5,4},{6,7},{7,6},{8,9},{9,8},{10,11... | collective-permute-start | bytes 393224 | tf_op jit(solution)/shard_map/ppermute | solution.py:213
  16.8 30.5 %slice-start = ((s8[16777216]{0:T(1024)(128)(4,1)}), s8[4194304]{0:T(1024)(128)(4,1)S(1)}, s32[]{:S(2)}) async-start(s8[16777216]{0:T(1024)(128)(4,1)} %bitcast.5), calls=%async_computation.3 | async-start | bytes 8388608
  16.8 30.5 %slice-start.1 = ((s8[16777216]{0:T(1024)(128)(4,1)}), s8[4194304]{0:T(1024)(128)(4,1)S(1)}, s32[]{:S(2)}) async-start(s8[16777216]{0:T(1024)(128)(4,1)} %bitcast.5), calls=%async_computation.4 | async-start | bytes 8388608
  18.7 28.6 %slice-start.2 = ((s8[16777216]{0:T(1024)(128)(4,1)}), s8[4194304]{0:T(1024)(128)(4,1)S(1)}, s32[]{:S(2)}) async-start(s8[16777216]{0:T(1024)(128)(4,1)} %bitcast.5), calls=%async_computation.5 | async-start | bytes 8388608
  18.7 28.6 %slice-start.3 = ((s8[16777216]{0:T(1024)(128)(4,1)}), s8[4194304]{0:T(1024)(128)(4,1)S(1)}, s32[]{:S(2)}) async-start(s8[16777216]{0:T(1024)(128)(4,1)} %bitcast.5), calls=%async_computation.6 | async-start | bytes 8388608
  48.9 2.2 %collective-permute-start.1 = (f32[8,2,2048]{2,1,0:T(2,128)S(1)}, f32[8,2,2048]{2,1,0:T(2,128)S(1)}, u32[]{:S(2)}, u32[]{:S(2)}) collective-permute-start(f32[8,2,2048]{2,1,0:T(2,128)S(1)} %get-tuple-element.18), channel_id=1, source_target_pairs={{0,1},{1,0},{2,3},{3,2},{4,5},{5,4},{6,7},{7,6},{8,9},{9,8},{10,11... | collective-permute-start | bytes 393224 | tf_op jit(solution)/shard_map/ppermute | solution.py:213
  50.6 1.5 %collective-permute-start.3 = (f32[8,2,2048]{2,1,0:T(2,128)S(1)}, f32[8,2,2048]{2,1,0:T(2,128)S(1)}, u32[]{:S(2)}, u32[]{:S(2)}) collective-permute-start(f32[8,2,2048]{2,1,0:T(2,128)S(1)} %get-tuple-element.22), channel_id=1, source_target_pairs={{0,1},{1,0},{2,3},{3,2},{4,5},{5,4},{6,7},{7,6},{8,9},{9,8},{10,11... | collective-permute-start | bytes 393224 | tf_op jit(solution)/shard_map/ppermute | solution.py:213
  51.2 4.7 %collective-permute-start.2 = (f32[4,1,2,2048]{3,2,1,0:T(2,128)S(1)}, f32[4,1,2,2048]{3,2,1,0:T(2,128)S(1)}, u32[]{:S(2)}, u32[]{:S(2)}) collective-permute-start(f32[4,1,2,2048]{3,2,1,0:T(2,128)S(1)} %get-tuple-element.20), channel_id=1, source_target_pairs={{0,2},{2,0},{1,3},{3,1},{4,6},{6,4},{5,7},{7,5},{8,10},{10,8},{9,1... | collective-permute-start | bytes 196616 | tf_op jit(solution)/shard_map/ppermute | solution.py:213
  52.2 4.8 %collective-permute-start.4 = (f32[4,1,2,2048]{3,2,1,0:T(2,128)S(1)}, f32[4,1,2,2048]{3,2,1,0:T(2,128)S(1)}, u32[]{:S(2)}, u32[]{:S(2)}) collective-permute-start(f32[4,1,2,2048]{3,2,1,0:T(2,128)S(1)} %get-tuple-element.24), channel_id=1, source_target_pairs={{0,2},{2,0},{1,3},{3,1},{4,6},{6,4},{5,7},{7,5},{8,10},{10,8},{9,1... | collective-permute-start | bytes 196616 | tf_op jit(solution)/shard_map/ppermute | solution.py:213
  57.0 5.6 %collective-permute-start.5 = (bf16[2,4096]{1,0:T(2,128)(2,1)S(1)}, bf16[2,4096]{1,0:T(2,128)(2,1)S(1)}, u32[]{:S(2)}, u32[]{:S(2)}) collective-permute-start(bf16[2,4096]{1,0:T(2,128)(2,1)S(1)} %get-tuple-element.25), channel_id=1, source_target_pairs={{0,12},{4,8},{8,4},{12,0},{1,13},{5,9},{9,5},{13,1},{2,14},{6,10},... | collective-permute-start | bytes 49160 | tf_op jit(solution)/shard_map/ppermute | solution.py:213
  57.8 4.8 %collective-permute-start.6 = (bf16[2,4096]{1,0:T(2,128)(2,1)S(1)}, bf16[2,4096]{1,0:T(2,128)(2,1)S(1)}, u32[]{:S(2)}, u32[]{:S(2)}) collective-permute-start(bf16[2,4096]{1,0:T(2,128)(2,1)S(1)} %get-tuple-element.26), channel_id=1, source_target_pairs={{0,8},{4,12},{8,0},{12,4},{1,9},{5,13},{9,1},{13,5},{2,10},{6,14},... | collective-permute-start | bytes 49160 | tf_op jit(solution)/shard_map/ppermute | solution.py:213
  58.3 4.9 %collective-permute-start.7 = (bf16[2,4096]{1,0:T(2,128)(2,1)S(1)}, bf16[2,4096]{1,0:T(2,128)(2,1)S(1)}, u32[]{:S(2)}, u32[]{:S(2)}) collective-permute-start(bf16[2,4096]{1,0:T(2,128)(2,1)S(1)} %get-tuple-element.27), channel_id=1, source_target_pairs={{0,4},{4,0},{8,12},{12,8},{1,5},{5,1},{9,13},{13,9},{2,6},{6,2},{1... | collective-permute-start | bytes 49160 | tf_op jit(solution)/shard_map/ppermute | solution.py:213

commit v8 on v6

--- a/solution.py
+++ b/solution.py
@@ -31,7 +31,7 @@
             blocks_ref[i * plane + j] = normed[:, at : at + half]
 
 
-def project_kernel(own, wide, plane, rows_ref, query_ref, key_ref, value_ref, _, *refs):
+def project_kernel(own, wide, plane, rows_ref, query_ref, key_ref, value_ref, *refs):
     owners, rows, half = rows_ref.shape
     core = lax.axis_index("gz")
     at_row = pl.multiple_of((core if own else 1 - core) * half, half)
@@ -50,7 +50,7 @@
             if own:
                 sums_ref[:, at : at + step] = part
             else:
-                part = part + refs[0][:, at : at + step]
+                part = part + refs[1][:, at : at + step]
                 sums_ref[:, :, at : at + step] = part.reshape(owners, rows, step)
             at += step
     if not own:
@@ -58,32 +58,56 @@
         own_plane = 2 * lax.axis_index("gy") + core
         for k in range(wide):
             for l in range(plane):
-                refs[1 + k][l] = sums_ref[(own_wide ^ k) * plane + (own_plane ^ l)]
-
-
-def share_kernel(plane, lengths_ref, keys_ref, values_ref, _, *blocks):
-    rows, slots, _ = keys_ref.shape
-    cols = blocks[0].shape[1]
-    own_plane = 2 * lax.axis_index("gy") + lax.axis_index("gz")
-    at_row = lax.broadcasted_iota(jnp.int32, (16, cols), 0)
-    filled = jnp.zeros((16, cols), jnp.float32)
+                refs[2 + k][l] = sums_ref[(own_wide ^ k) * plane + (own_plane ^ l)]
+
+
+def own_place():
+    return 2 * lax.axis_index("gy") + lax.axis_index("gz")
+
+
+def write_heads(cache_ref, block_ref, start, owner):
+    rows, slots, _ = cache_ref.shape
+    cols = block_ref.shape[1]
+    at = pl.multiple_of(owner * cols, cols)
+    for r in range(rows):
+        block_ref[start + r * slots : start + (r + 1) * slots] = cache_ref[r, :, pl.ds(at, cols)]
+
+
+def write_lengths(rows, lengths_ref, block_ref):
+    at_row = lax.broadcasted_iota(jnp.int32, (16, block_ref.shape[1]), 0)
+    filled = jnp.zeros(at_row.shape, jnp.float32)
     for r in range(rows):
         filled = jnp.where(at_row == r, lengths_ref[r].astype(jnp.float32), filled)
-    for l in range(plane):
-        at = pl.multiple_of((own_plane ^ l) * cols, cols)
-        for c, cache in enumerate((keys_ref, values_ref)):
-            for r in range(rows):
-                to = (c * rows + r) * slots
-                blocks[l][to : to + slots] = cache[r, :, pl.ds(at, cols)]
-        blocks[l][2 * rows * slots :] = filled.astype(jnp.bfloat16)
-
-
-def attend_kernel(wide, plane, query_cols, frequency_ref, *refs):
-    partials, shared, attended_ref = refs[wide - 1 :: -1], refs[wide:-1], refs[-1]
-    rows, cols = partials[0].shape[1:]
+    block_ref[block_ref.shape[0] - 16 :] = filled.astype(jnp.bfloat16)
+
+
+def first_kernel(lengths_ref, keys_ref, _, *blocks):
+    for s, block in enumerate(blocks):
+        write_heads(keys_ref, block, 0, own_place() ^ (2 * s + 2))
+        write_lengths(keys_ref.shape[0], lengths_ref, block)
+
+
+def rest_kernel(even, lengths_ref, keys_ref, values_ref, _, *refs):
+    rows, slots, _ = keys_ref.shape
+    blocks, count = refs[even:], even
+    for s, block in enumerate(blocks[:count]):
+        write_heads(values_ref, block, 0, own_place() ^ (2 * s + 2))
+    for s, block in enumerate(blocks[count:]):
+        write_heads(keys_ref, block, 0, own_place() ^ (2 * s + 1))
+        write_heads(values_ref, block, rows * slots, own_place() ^ (2 * s + 1))
+        write_lengths(rows, lengths_ref, block)
+
+
+def attend_kernel(
+    wide, plane, query_cols, lengths_ref, keys_ref, values_ref, frequency_ref, *refs
+):
+    partials, held, attended_ref = refs[wide - 1 :: -1], refs[wide:-1], refs[-1]
+    even = plane // 2 - 1
+    even_keys, even_values, odd = held[:even], held[even : 2 * even], held[2 * even :]
+    rows, slots, _ = keys_ref.shape
+    cols = partials[0].shape[-1]
     kv_cols = (cols - query_cols) // 2
     kv_heads, group = kv_cols // HD, query_cols // kv_cols
-    slots = (shared[0].shape[0] - 16) // (2 * rows)
     pairs = plane * rows
     count = pairs * kv_heads
     heads = count * group
@@ -92,12 +116,26 @@
     for k in range(1, wide):
         total = total + partials[k][...]
     total = total.reshape(pairs, cols).astype(jnp.bfloat16).astype(jnp.float32)
-
-    filled = [
-        shared[p // rows][2 * rows * slots : 2 * rows * slots + 16, :HD]
-        .astype(jnp.float32)[p % rows : p % rows + 1]
-        for p in range(pairs)
-    ]
+    own_at = pl.multiple_of(own_place() * kv_cols, kv_cols)
+
+    def cached(cache_ref, even_blocks, start):
+        parts = []
+        for p in range(pairs):
+            l, r = p // rows, p % rows
+            if l == 0:
+                parts.append(cache_ref[r, :, pl.ds(own_at, kv_cols)])
+            elif l % 2:
+                at = start + r * slots
+                parts.append(odd[l // 2][at : at + slots])
+            else:
+                parts.append(even_blocks[l // 2 - 1][r * slots : (r + 1) * slots])
+        return jnp.concatenate(parts, 1)
+
+    filled = [jnp.full((1, HD), lengths_ref[r].astype(jnp.float32)) for r in range(rows)]
+    for l in range(1, plane):
+        block = odd[l // 2] if l % 2 else even_keys[l // 2 - 1]
+        last = block[block.shape[0] - 16 :, :HD].astype(jnp.float32)
+        filled += [last[r : r + 1] for r in range(rows)]
     angles = jnp.concatenate(filled, 0) * frequency_ref[...]
     cosine, sine = jnp.cos(angles), jnp.sin(angles)
     front = lax.broadcasted_iota(jnp.int32, (1, HD), 1) < HD // 2
@@ -120,21 +158,12 @@
     key_new = jnp.stack(key_new, 1).reshape(count, HD).astype(jnp.bfloat16)
     value_new = jnp.stack(value_new, 1).reshape(count, HD)
 
-    def cached(c):
-        return jnp.concatenate(
-            [
-                shared[p // rows][(c * rows + p % rows) * slots : (c * rows + p % rows + 1) * slots]
-                for p in range(pairs)
-            ],
-            1,
-        )
-
     head_pair = lax.broadcasted_iota(jnp.int32, (1, heads), 1) // group
     by_pair = jnp.concatenate(
         [jnp.where(head_pair == b, turned_query, jnp.zeros_like(turned_query)) for b in range(count)],
         0,
     )
-    scores = scale * jnp.dot(cached(0), by_pair, preferred_element_type=jnp.float32)
+    scores = scale * jnp.dot(cached(keys_ref, even_keys, 0), by_pair, preferred_element_type=jnp.float32)
     own = scale * jnp.dot(key_new, turned_query, preferred_element_type=jnp.float32)
     of_pair = lax.broadcasted_iota(jnp.int32, (count, 1), 0) == head_pair
     own = jnp.sum(jnp.where(of_pair, own, 0.0), 0, keepdims=True)
@@ -151,7 +180,7 @@
     own_prob = (own_weight / denominator).astype(jnp.bfloat16)
     contract_rows = (((0,), (0,)), ((), ()))
     mixed = lax.dot_general(
-        probability, cached(1), contract_rows, preferred_element_type=jnp.float32
+        probability, cached(values_ref, even_values, rows * slots), contract_rows, preferred_element_type=jnp.float32
     )
     own_prob = jnp.where(of_pair, own_prob.astype(jnp.float32), 0.0).astype(jnp.bfloat16)
     fresh = lax.dot_general(
@@ -171,7 +200,7 @@
 
 
 def output_kernel(at, cols, weight_ref, *refs):
-    blocks, keep_ref, give_ref = refs[:-2], refs[-2], refs[-1]
+    blocks, keep_ref, give_ref = refs[-3::-1], refs[-2], refs[-1]
     wide = len(blocks)
     plane, rows, depth = blocks[0].shape
     attended = jnp.concatenate(
@@ -270,27 +299,42 @@
         out_specs=IN_VMEM,
         compiler_params=params(8),
     )(scaled, norm_gain.reshape(1, -1))
-    shared_rows = 2 * rows * cache_keys.shape[1] + 16
-    shared = pl.pallas_call(
-        functools.partial(share_kernel, plane),
-        out_shape=[jax.ShapeDtypeStruct((shared_rows, kv_cols), jnp.bfloat16)] * plane,
-        in_specs=[IN_SMEM] + [IN_VMEM] * 3,
-        out_specs=[IN_VMEM] * plane,
-        compiler_params=params(8),
-    )(lengths, cache_keys, cache_values, normed)
-    shared = [shared[0]] + [swap_plane(shared[l], l) for l in range(1, plane)]
+    block_rows = rows * cache_keys.shape[1]
+    even = plane // 2 - 1
+
+    def block_of(count):
+        return jax.ShapeDtypeStruct((count, kv_cols), jnp.bfloat16)
+
+    keys = pl.pallas_call(
+        first_kernel,
+        out_shape=[block_of(block_rows + 16)] * even,
+        in_specs=[IN_SMEM] + [IN_VMEM] * 2,
+        out_specs=[IN_VMEM] * even,
+        compiler_params=params(8),
+    )(lengths, cache_keys, normed)
+    keys = [swap_plane(keys[s], 2 * s + 2) for s in range(even)]
     own_half = swap_blocks(normed, ROW_AXES)
     other_half = swap_pairs(own_half, "gz", 1)
+    rest = pl.pallas_call(
+        functools.partial(rest_kernel, even),
+        out_shape=[block_of(block_rows)] * even + [block_of(2 * block_rows + 16)] * (even + 1),
+        in_specs=[IN_SMEM] + [IN_VMEM] * (3 + even),
+        out_specs=[IN_VMEM] * (2 * even + 1),
+        compiler_params=params(8),
+    )(lengths, cache_keys, cache_values, own_half, *keys)
+    values = [swap_plane(rest[s], 2 * s + 2) for s in range(even)]
+    odd = [swap_plane(rest[even + s], 2 * s + 1) for s in range(even + 1)]
+    held = [*keys, *values, *odd]
     weights = (query_weight, key_weight, value_weight)
     half_cost = cost(owners * rows * width * cols, width * cols)
     partial = pl.pallas_call(
         functools.partial(project_kernel, True, wide, plane),
         out_shape=jax.ShapeDtypeStruct((owners * rows, cols), jnp.float32),
-        in_specs=[IN_VMEM] * 5,
+        in_specs=[IN_VMEM] * 4,
         out_specs=IN_VMEM,
         compiler_params=params(8),
         cost_estimate=half_cost,
-    )(own_half, *weights, shared[1])
+    )(own_half, *weights)
     partial = pl.pallas_call(
         functools.partial(project_kernel, False, wide, plane),
         out_shape=[jax.ShapeDtypeStruct((plane, rows, cols), jnp.float32)] * wide,
@@ -299,7 +343,7 @@
         scratch_shapes=[pltpu.VMEM((owners, rows, cols), jnp.float32)],
         compiler_params=params(8),
         cost_estimate=half_cost,
-    )(other_half, *weights, shared[1], partial)
+    )(other_half, *weights, odd[0], partial)
     partial = swap_wide(partial)
 
     half_dim = HD // 2
@@ -308,11 +352,11 @@
     attended = pl.pallas_call(
         functools.partial(attend_kernel, wide, plane, query_cols),
         out_shape=jax.ShapeDtypeStruct((plane, rows, query_cols), jnp.bfloat16),
-        in_specs=[IN_VMEM] * (1 + wide + plane),
+        in_specs=[IN_SMEM] + [IN_VMEM] * (3 + wide + len(held)),
         out_specs=IN_VMEM,
         compiler_params=params(8),
         cost_estimate=cost(10**9, 4 * MIB),
-    )(jnp.asarray(frequency), *partial[::-1], *shared)
+    )(lengths, cache_keys, cache_values, jnp.asarray(frequency), *partial[::-1], *held)
     head_rows = swap_wide([attended] * wide)
     parts = 2
     part_cols = out_cols // parts
@@ -327,7 +371,7 @@
             out_specs=(IN_VMEM, IN_VMEM),
             compiler_params=params(8),
             cost_estimate=cost(2 * owners * rows * depth * part_cols, 2 * depth * part_cols),
-        )(out_weight, *head_rows)
+        )(out_weight, *head_rows[::-1])
         give = swap_plane(give, 1)
         step = 2
         while step < plane:

time: 72 us -> 64.6 us (0.90)
  blocking collectives: 25.4 us -> 13 us
  waiting for transfers between devices: 15.1 us -> 18.2 us
  Pallas kernels: 9.94 us -> 11 us
  starting transfers between devices: 20 us -> 21 us
    all_to_all x1, blocking collectives: 25.4 us -> 13 us  [swap_blocks(): return lax.all_to_all(blocks, axes, split_axis=0, concat_axis=0, tiled=True)]
    ppermute x7 -> x8, waiting for transfers between devices: 3.37 us -> 13.5 us  [swap_plane(): lax.ppermute(value, PLANE, [(i, i ^ step) for i in range(lax.axis_size(PL...]
    ppermute x10, waiting for transfers between devices: 11.7 us -> 4.74 us  [swap_pairs(): lax.ppermute(value, axis, [(i, i ^ step) for i in range(lax.axis_size(axi...]
    ppermute x7 -> x8, starting transfers between devices: 6.37 us -> 7.59 us  [swap_plane(): lax.ppermute(value, PLANE, [(i, i ^ step) for i in range(lax.axis_size(PL...]
  transfers between devices with their start and end apart: 17 -> 18, of which waited for: 8 -> 9; matrix products, arithmetic and copies ran while one was open for 0% -> 0% of each run, Pallas kernels for 8% -> 8%
where the time goes in v8:
time: 64.6 us; the launch traced here: 64.4 us
  starting transfers between devices  21 us (33%)
  waiting for transfers between devices  18.2 us (28%)
  blocking collectives  13 us (20%)
  Pallas kernels  11 us (17%)
  local copies, waits for them, and re-layouts  1.04 us (2%)
    ppermute x8, waiting for transfers between devices, swap_plane(): lax.ppermute(value, PLANE, [(i, i ^ step) for i in range(lax.axis_size(PL...  13.5 us
    ppermute x10, starting transfers between devices, swap_pairs(): lax.ppermute(value, axis, [(i, i ^ step) for i in range(lax.axis_size(axi...  13.4 us
    all_to_all x1, blocking collectives, swap_blocks(): return lax.all_to_all(blocks, axes, split_axis=0, concat_axis=0, tiled=True)  13 us
    ppermute x8, starting transfers between devices, swap_plane(): lax.ppermute(value, PLANE, [(i, i ^ step) for i in range(lax.axis_size(PL...  7.59 us
    ppermute x10, waiting for transfers between devices, swap_pairs(): lax.ppermute(value, axis, [(i, i ^ step) for i in range(lax.axis_size(axi...  4.74 us
    pallas_call x2, Pallas kernels, shards(): pl.pallas_call(functools.partial(output_kernel, p * part_cols, part_cols)...  3.09 us
    pallas_call x1, Pallas kernels, shards(): pl.pallas_call(functools.partial(project_kernel, False, wide, plane), out...  1.97 us
    pallas_call x1, Pallas kernels, shards(): pl.pallas_call(functools.partial(project_kernel, True, wide, plane), out_...  1.9 us
  transfers between devices with their start and end apart: 18, of which 9 were waited for; matrix products, arithmetic and copies ran while one was open for 0% of the time, Pallas kernels for 8%

profile of v8, /device:TPU:0, one launch (start us, length us, event | category | flops | bytes accessed | tf_op | source)
XLA Modules:
  0.0 64.4 jit_solution(7850784461349736017)
XLA Ops:
  0.0 0.0 copy-start.2
  0.0 0.0 copy-start.3
  0.0 0.0 copy-start.8
  0.0 1.0 %copy-done.8 = bf16[2,16384]{1,0:T(2,128)(2,1)S(1)} copy-done((bf16[2,16384]{1,0:T(2,128)(2,1)S(1)}, bf16[2,16384]{1,0:T(2,128)(2,1)}, u32[]{:S(2)}) %copy-start.8) | copy-done | bytes 65560
  1.0 0.2 shard_map.100.scaled_ref
  1.3 0.0 copy-done.5
  1.3 0.1 shard_map.101._
  1.4 0.0 copy-done.6
  1.4 0.0 copy-done.1
  1.4 0.6 shard_map.102
  2.0 3.0 %collective-permute-start.1 = (bf16[528,256]{1,0:T(8,128)(2,1)S(1)}, bf16[528,256]{1,0:T(8,128)(2,1)S(1)}, u32[]{:S(2)}, u32[]{:S(2)}) collective-permute-start(bf16[528,256]{1,0:T(8,128)(2,1)S(1)} %shard_map.102), channel_id=1, source_target_pairs={{0,2},{1,3},{2,0},{3,1},{4,6},{5,7},{6,4},{7,5},{8,10},{9,11},{10,... | collective-permute-start | bytes 811016 | tf_op jit(solution)/shard_map/ppermute | solution.py:252
  5.0 13.0 %all_to_all.5._.rows_ref = bf16[16,2,2048]{2,1,0:T(2,128)(2,1)S(1)} all-to-all(bf16[16,2,2048]{2,1,0:T(2,128)(2,1)S(1)} %shard_map.101._), channel_id=1, replica_groups=mesh['groups'=2,'gx'=4,'gy'=2,'gz'=2] {'gx','gy','gz'}, dimensions={0} | all-to-all | bytes 262144 | tf_op jit(solution)/shard_map/all_to_all | solution.py:244
  18.0 0.0 collective-permute-done.1.refs_0_.refs_4_
  18.0 0.0 copy-done.4
  18.0 0.7 %shard_map.103 = (bf16[512,256]{1,0:T(8,128)(2,1)S(1)}, bf16[1040,256]{1,0:T(8,128)(2,1)S(1)}, bf16[1040,256]{1,0:T(8,128)(2,1)S(1)}) custom-call(s32[2]{0:T(128)S(1)} %copy-done.6, bf16[2,256,1024]{2,1,0:T(8,128)(2,1)S(1)} %copy-done.1, bf16[2,256,1024]{2,1,0:T(8,128)(2,1)S(1)} %copy-done.4, bf16[16,2,2048]{2,1,0:T(2,128)(2,1)S(1)} %all_to_all.5._.rows_ref, ...), custom_call_target="tpu_custom_call" | custom-call | tf_op jit(solution)/shard_map/pallas_call | solution.py:318
  18.7 0.1 collective-permute-start.2
  18.8 0.1 collective-permute-start.7
  18.9 0.0 copy-start.7
  18.9 2.1 %collective-permute-start.6 = (bf16[512,256]{1,0:T(8,128)(2,1)S(1)}, bf16[512,256]{1,0:T(8,128)(2,1)S(1)}, u32[]{:S(2)}, u32[]{:S(2)}) collective-permute-start(bf16[512,256]{1,0:T(8,128)(2,1)S(1)} %get-tuple-element.29), channel_id=1, source_target_pairs={{0,2},{1,3},{2,0},{3,1},{4,6},{5,7},{6,4},{7,5},{8,10},{9,11},{10,... | collective-permute-start | bytes 786440 | tf_op jit(solution)/shard_map/ppermute | solution.py:252
  20.9 0.0 collective-permute-start
  20.9 0.0 copy-done
  20.9 0.0 copy-done.2
  20.9 0.0 copy-done.3
  21.0 0.0 slice-start
  21.0 0.0 slice-start.1
  21.0 1.9 %shard_map.104.refs_1_ = f32[32,2560]{1,0:T(8,128)S(1)} custom-call(bf16[16,2,2048]{2,1,0:T(2,128)(2,1)S(1)} %all_to_all.5._.rows_ref, bf16[4096,2048]{1,0:T(8,128)(2,1)S(1)} %copy-done, bf16[4096,256]{1,0:T(8,128)(2,1)S(1)} %copy-done.2, bf16[4096,256]{1,0:T(8,128)(2,1)S(1)} %copy-done.3), custom_call_target="tpu_custom_call" | custom-call | flops 335544320 | bytes 10485760 | tf_op jit(solution)/shard_map/pallas_call | solution.py:330
  22.9 0.0 collective-permute-done.rows_ref
  22.9 0.0 collective-permute-done.2.refs_0_.refs_6_
  22.9 2.0 %shard_map.105 = (f32[4,2,2560]{2,1,0:T(2,128)S(1)}, f32[4,2,2560]{2,1,0:T(2,128)S(1)}, f32[4,2,2560]{2,1,0:T(2,128)S(1)}, f32[4,2,2560]{2,1,0:T(2,128)S(1)}) custom-call(bf16[16,2,2048]{2,1,0:T(2,128)(2,1)S(1)} %collective-permute-done.rows_ref, bf16[4096,2048]{1,0:T(8,128)(2,1)S(1)} %copy-done, bf16[4096,256]{1,0:T(8,128)(2,1)S(1)} %copy-done.2, ...), custom_call_target="tpu_custom_call" | custom-call | flops 335544320 | bytes 10485760 | tf_op jit(solution)/shard_map/pallas_call | solution.py:338
  24.9 0.8 %collective-permute-start.3 = (f32[4,2,2560]{2,1,0:T(2,128)S(1)}, f32[4,2,2560]{2,1,0:T(2,128)S(1)}, u32[]{:S(2)}, u32[]{:S(2)}) collective-permute-start(f32[4,2,2560]{2,1,0:T(2,128)S(1)} %get-tuple-element.25), channel_id=1, source_target_pairs={{0,12},{4,8},{8,4},{12,0},{1,13},{5,9},{9,5},{13,1},{2,14},{6,10},... | collective-permute-start | bytes 245768 | tf_op jit(solution)/shard_map/ppermute | solution.py:248
  25.7 0.5 collective-permute-start.4
  26.2 3.2 %collective-permute-start.5 = (f32[4,2,2560]{2,1,0:T(2,128)S(1)}, f32[4,2,2560]{2,1,0:T(2,128)S(1)}, u32[]{:S(2)}, u32[]{:S(2)}) collective-permute-start(f32[4,2,2560]{2,1,0:T(2,128)S(1)} %get-tuple-element.27), channel_id=1, source_target_pairs={{0,4},{4,0},{8,12},{12,8},{1,5},{5,1},{9,13},{13,9},{2,6},{6,2},{1... | collective-permute-start | bytes 245768 | tf_op jit(solution)/shard_map/ppermute | solution.py:248
  29.3 9.5 %collective-permute-done.6.refs_5_ = bf16[512,256]{1,0:T(8,128)(2,1)S(1)} collective-permute-done((bf16[512,256]{1,0:T(8,128)(2,1)S(1)}, bf16[512,256]{1,0:T(8,128)(2,1)S(1)}, u32[]{:S(2)}, u32[]{:S(2)}) %collective-permute-start.6) | collective-permute-done | bytes 262176 | tf_op jit(solution)/shard_map/ppermute | solution.py:252
  38.9 0.0 collective-permute-done.7.refs_7_
  38.9 0.0 collective-permute-done.3.refs_0_
  38.9 0.0 collective-permute-done.4.refs_1_
  38.9 0.0 collective-permute-done.5.refs_2_
  38.9 0.0 copy-done.7
  38.9 1.7 %shard_map.106.refs_3_ = bf16[4,2,2048]{2,1,0:T(2,128)(2,1)S(1)} custom-call(s32[2]{0:T(128)S(1)} %copy-done.6, bf16[2,256,1024]{2,1,0:T(8,128)(2,1)S(1)} %copy-done.1, bf16[2,256,1024]{2,1,0:T(8,128)(2,1)S(1)} %copy-done.4, f32[1,128]{1,0:T(1,128)S(1)} %copy-done.7, f32[4,2,2560]{2,1,0:T(2,128)S(1)} %collective-permute-done.3.refs_0_, ...), custom_call_target="tpu_custom_call" | custom-call | flops 1000000000 | bytes 4194304 | tf_op jit(solution)/shard_map/pallas_call | solution.py:352
  40.6 0.9 %collective-permute-start.8 = (bf16[4,2,2048]{2,1,0:T(2,128)(2,1)S(1)}, bf16[4,2,2048]{2,1,0:T(2,128)(2,1)S(1)}, u32[]{:S(2)}, u32[]{:S(2)}) collective-permute-start(bf16[4,2,2048]{2,1,0:T(2,128)(2,1)S(1)} %shard_map.106.refs_3_), channel_id=1, source_target_pairs={{0,12},{4,8},{8,4},{12,0},{1,13},{5,9},{9,5},{13,1},{2,14},{6,10},... | collective-permute-start | bytes 98312 | tf_op jit(solution)/shard_map/ppermute | solution.py:248
  41.4 0.6 collective-permute-start.9
  42.0 3.0 %collective-permute-start.10 = (bf16[4,2,2048]{2,1,0:T(2,128)(2,1)S(1)}, bf16[4,2,2048]{2,1,0:T(2,128)(2,1)S(1)}, u32[]{:S(2)}, u32[]{:S(2)}) collective-permute-start(bf16[4,2,2048]{2,1,0:T(2,128)(2,1)S(1)} %shard_map.106.refs_3_), channel_id=1, source_target_pairs={{0,4},{4,0},{8,12},{12,8},{1,5},{5,1},{9,13},{13,9},{2,6},{6,2},{1... | collective-permute-start | bytes 98312 | tf_op jit(solution)/shard_map/ppermute | solution.py:248
  45.0 1.4 %collective-permute-done.8.refs_0_ = bf16[4,2,2048]{2,1,0:T(2,128)(2,1)S(1)} collective-permute-done((bf16[4,2,2048]{2,1,0:T(2,128)(2,1)S(1)}, bf16[4,2,2048]{2,1,0:T(2,128)(2,1)S(1)}, u32[]{:S(2)}, u32[]{:S(2)}) %collective-permute-start.8) | collective-permute-done | bytes 32800 | tf_op jit(solution)/shard_map/ppermute | solution.py:248
  46.4 0.6 collective-permute-done.9.refs_1_
  47.1 0.0 collective-permute-done.10.refs_2_
  47.1 0.0 slice-done.3
  47.1 1.5 %shard_map.107 = (f32[8,2,2048]{2,1,0:T(2,128)S(1)}, f32[8,2,2048]{2,1,0:T(2,128)S(1)}) custom-call(bf16[2048,4096]{1,0:T(8,128)(2,1)S(1)} %bitcast.2, bf16[4,2,2048]{2,1,0:T(2,128)(2,1)S(1)} %collective-permute-done.8.refs_0_, bf16[4,2,2048]{2,1,0:T(2,128)(2,1)S(1)} %collective-permute-done.9.refs_1_, ...), custom_call_target="tpu_custom_call" | custom-call | flops 268435456 | bytes 8388608 | tf_op jit(solution)/shard_map/pallas_call | solution.py:367
  48.7 0.1 collective-permute-start.11
  48.7 1.5 %shard_map.109 = (f32[8,2,2048]{2,1,0:T(2,128)S(1)}, f32[8,2,2048]{2,1,0:T(2,128)S(1)}) custom-call(bf16[2048,4096]{1,0:T(8,128)(2,1)S(1)} %bitcast.2, bf16[4,2,2048]{2,1,0:T(2,128)(2,1)S(1)} %collective-permute-done.8.refs_0_, bf16[4,2,2048]{2,1,0:T(2,128)(2,1)S(1)} %collective-permute-done.9.refs_1_, ...), custom_call_target="tpu_custom_call" | custom-call | flops 268435456 | bytes 8388608 | tf_op jit(solution)/shard_map/pallas_call | solution.py:367
  50.3 0.6 collective-permute-start.13
  50.9 0.0 collective-permute-done.11.b_ref
  50.9 0.6 collective-permute-start.12
  51.4 0.4 collective-permute-done.13.b_ref
  51.9 1.2 %collective-permute-start.14 = (f32[4,2,2048]{2,1,0:T(2,128)S(1)}, f32[4,2,2048]{2,1,0:T(2,128)S(1)}, u32[]{:S(2)}, u32[]{:S(2)}) collective-permute-start(f32[4,2,2048]{2,1,0:T(2,128)S(1)} %get-tuple-element.38), channel_id=1, source_target_pairs={{0,2},{1,3},{2,0},{3,1},{4,6},{5,7},{6,4},{7,5},{8,10},{9,11},{10,... | collective-permute-start | bytes 196616 | tf_op jit(solution)/shard_map/ppermute | solution.py:252
  53.1 2.6 %collective-permute-done.12.refs_1_ = f32[4,2,2048]{2,1,0:T(2,128)S(1)} collective-permute-done((f32[4,2,2048]{2,1,0:T(2,128)S(1)}, f32[4,2,2048]{2,1,0:T(2,128)S(1)}, u32[]{:S(2)}, u32[]{:S(2)}) %collective-permute-start.12) | collective-permute-done | bytes 65568 | tf_op jit(solution)/shard_map/ppermute | solution.py:252
  55.6 1.0 %collective-permute-done.14.refs_3_ = f32[4,2,2048]{2,1,0:T(2,128)S(1)} collective-permute-done((f32[4,2,2048]{2,1,0:T(2,128)S(1)}, f32[4,2,2048]{2,1,0:T(2,128)S(1)}, u32[]{:S(2)}, u32[]{:S(2)}) %collective-permute-start.14) | collective-permute-done | bytes 65568 | tf_op jit(solution)/shard_map/ppermute | solution.py:252
  56.6 0.1 shard_map.111
  56.7 2.3 %collective-permute-start.15 = (bf16[2,4096]{1,0:T(2,128)(2,1)S(1)}, bf16[2,4096]{1,0:T(2,128)(2,1)S(1)}, u32[]{:S(2)}, u32[]{:S(2)}) collective-permute-start(bf16[2,4096]{1,0:T(2,128)(2,1)S(1)} %get-tuple-element.39), channel_id=1, source_target_pairs={{0,12},{4,8},{8,4},{12,0},{1,13},{5,9},{9,5},{13,1},{2,14},{6,10},... | collective-permute-start | bytes 49160 | tf_op jit(solution)/shard_map/ppermute | solution.py:248
  58.9 1.1 %collective-permute-start.16 = (bf16[2,4096]{1,0:T(2,128)(2,1)S(1)}, bf16[2,4096]{1,0:T(2,128)(2,1)S(1)}, u32[]{:S(2)}, u32[]{:S(2)}) collective-permute-start(bf16[2,4096]{1,0:T(2,128)(2,1)S(1)} %get-tuple-element.40), channel_id=1, source_target_pairs={{0,8},{4,12},{8,0},{12,4},{1,9},{5,13},{9,1},{13,5},{2,10},{6,14},... | collective-permute-start | bytes 49160 | tf_op jit(solution)/shard_map/ppermute | solution.py:248
  60.1 1.1 %collective-permute-start.17 = (bf16[2,4096]{1,0:T(2,128)(2,1)S(1)}, bf16[2,4096]{1,0:T(2,128)(2,1)S(1)}, u32[]{:S(2)}, u32[]{:S(2)}) collective-permute-start(bf16[2,4096]{1,0:T(2,128)(2,1)S(1)} %get-tuple-element.41), channel_id=1, source_target_pairs={{0,4},{4,0},{8,12},{12,8},{1,5},{5,1},{9,13},{13,9},{2,6},{6,2},{1... | collective-permute-start | bytes 49160 | tf_op jit(solution)/shard_map/ppermute | solution.py:248
  61.1 1.2 %collective-permute-done.15.refs_0_ = bf16[2,4096]{1,0:T(2,128)(2,1)S(1)} collective-permute-done((bf16[2,4096]{1,0:T(2,128)(2,1)S(1)}, bf16[2,4096]{1,0:T(2,128)(2,1)S(1)}, u32[]{:S(2)}, u32[]{:S(2)}) %collective-permute-start.15) | collective-permute-done | bytes 16416 | tf_op jit(solution)/shard_map/ppermute | solution.py:248
  62.3 1.3 %collective-permute-done.16.refs_1_ = bf16[2,4096]{1,0:T(2,128)(2,1)S(1)} collective-permute-done((bf16[2,4096]{1,0:T(2,128)(2,1)S(1)}, bf16[2,4096]{1,0:T(2,128)(2,1)S(1)}, u32[]{:S(2)}, u32[]{:S(2)}) %collective-permute-start.16) | collective-permute-done | bytes 16416 | tf_op jit(solution)/shard_map/ppermute | solution.py:248
  63.6 0.2 collective-permute-done.17.refs_2_
  63.8 0.6 shard_map.112
  (13 shorter events, 0.0 us)
Async XLA Ops:
  0.0 1.3 %copy-start.5 = (f32[16384]{0:T(1024)S(1)}, f32[16384]{0:T(1024)}, u32[]{:S(2)}) copy-start(f32[16384]{0:T(1024)} %param.11) | copy-start | bytes 196612
  0.0 1.4 %copy-start.6 = (s32[2]{0:T(128)S(1)}, s32[2]{0:T(128)}, u32[]{:S(2)}) copy-start(s32[2]{0:T(128)} %lengths_ref.5) | copy-start | bytes 28
  0.0 1.4 %copy-start.1 = (bf16[2,256,1024]{2,1,0:T(8,128)(2,1)S(1)}, bf16[2,256,1024]{2,1,0:T(8,128)(2,1)}, u32[]{:S(2)}) copy-start(bf16[2,256,1024]{2,1,0:T(8,128)(2,1)} %keys_ref.5) | copy-start | bytes 3145732
  0.0 18.0 %copy-start.4 = (bf16[2,256,1024]{2,1,0:T(8,128)(2,1)S(1)}, bf16[2,256,1024]{2,1,0:T(8,128)(2,1)}, u32[]{:S(2)}) copy-start(bf16[2,256,1024]{2,1,0:T(8,128)(2,1)} %values_ref.3) | copy-start | bytes 3145732
  0.0 20.9 %copy-start = (bf16[4096,2048]{1,0:T(8,128)(2,1)S(1)}, bf16[4096,2048]{1,0:T(8,128)(2,1)}, u32[]{:S(2)}) copy-start(bf16[4096,2048]{1,0:T(8,128)(2,1)} %query_ref.3) | copy-start | bytes 50331652
  0.0 20.9 %copy-start.2 = (bf16[4096,256]{1,0:T(8,128)(2,1)S(1)}, bf16[4096,256]{1,0:T(8,128)(2,1)}, u32[]{:S(2)}) copy-start(bf16[4096,256]{1,0:T(8,128)(2,1)} %key_ref.3) | copy-start | bytes 6291460
  0.0 20.9 %copy-start.3 = (bf16[4096,256]{1,0:T(8,128)(2,1)S(1)}, bf16[4096,256]{1,0:T(8,128)(2,1)}, u32[]{:S(2)}) copy-start(bf16[4096,256]{1,0:T(8,128)(2,1)} %value_ref.3) | copy-start | bytes 6291460
  0.0 1.0 %copy-start.8 = (bf16[2,16384]{1,0:T(2,128)(2,1)S(1)}, bf16[2,16384]{1,0:T(2,128)(2,1)}, u32[]{:S(2)}) copy-start(bf16[2,16384]{1,0:T(2,128)(2,1)} %tokens_ref.1) | copy-start | bytes 196612
  2.0 16.0 %collective-permute-start.1 = (bf16[528,256]{1,0:T(8,128)(2,1)S(1)}, bf16[528,256]{1,0:T(8,128)(2,1)S(1)}, u32[]{:S(2)}, u32[]{:S(2)}) collective-permute-start(bf16[528,256]{1,0:T(8,128)(2,1)S(1)} %shard_map.102), channel_id=1, source_target_pairs={{0,2},{1,3},{2,0},{3,1},{4,6},{5,7},{6,4},{7,5},{8,10},{9,11},{10,... | collective-permute-start | bytes 811016 | tf_op jit(solution)/shard_map/ppermute | solution.py:252
  18.7 4.2 %collective-permute-start.2 = (bf16[1040,256]{1,0:T(8,128)(2,1)S(1)}, bf16[1040,256]{1,0:T(8,128)(2,1)S(1)}, u32[]{:S(2)}, u32[]{:S(2)}) collective-permute-start(bf16[1040,256]{1,0:T(8,128)(2,1)S(1)} %get-tuple-element.24), channel_id=1, source_target_pairs={{0,1},{1,0},{2,3},{3,2},{4,5},{5,4},{6,7},{7,6},{8,9},{9,8},{10,11... | collective-permute-start | bytes 1597448 | tf_op jit(solution)/shard_map/ppermute | solution.py:252
  18.8 20.1 %collective-permute-start.7 = (bf16[1040,256]{1,0:T(8,128)(2,1)S(1)}, bf16[1040,256]{1,0:T(8,128)(2,1)S(1)}, u32[]{:S(2)}, u32[]{:S(2)}) collective-permute-start(bf16[1040,256]{1,0:T(8,128)(2,1)S(1)} %get-tuple-element.30), channel_id=1, source_target_pairs={{0,3},{1,2},{2,1},{3,0},{4,7},{5,6},{6,5},{7,4},{8,11},{9,10},{10,... | collective-permute-start | bytes 1597448 | tf_op jit(solution)/shard_map/ppermute | solution.py:252
  18.9 20.0 %copy-start.7 = (f32[1,128]{1,0:T(1,128)S(1)}, f32[1,128]{1,0:T(1,128)}, u32[]{:S(2)}) copy-start(f32[1,128]{1,0:T(1,128)} %constant.2.clone.frequency_ref) | copy-start | bytes 1540
  18.9 20.0 %collective-permute-start.6 = (bf16[512,256]{1,0:T(8,128)(2,1)S(1)}, bf16[512,256]{1,0:T(8,128)(2,1)S(1)}, u32[]{:S(2)}, u32[]{:S(2)}) collective-permute-start(bf16[512,256]{1,0:T(8,128)(2,1)S(1)} %get-tuple-element.29), channel_id=1, source_target_pairs={{0,2},{1,3},{2,0},{3,1},{4,6},{5,7},{6,4},{7,5},{8,10},{9,11},{10,... | collective-permute-start | bytes 786440 | tf_op jit(solution)/shard_map/ppermute | solution.py:252
  20.9 2.0 %collective-permute-start = (bf16[16,2,2048]{2,1,0:T(2,128)(2,1)S(1)}, bf16[16,2,2048]{2,1,0:T(2,128)(2,1)S(1)}, u32[]{:S(2)}, u32[]{:S(2)}) collective-permute-start(bf16[16,2,2048]{2,1,0:T(2,128)(2,1)S(1)} %all_to_all.5._.rows_ref), channel_id=1, source_target_pairs={{0,1},{1,0},{2,3},{3,2},{4,5},{5,4},{6,7},{7,6},{8,9},{9,8},{10,11... | collective-permute-start | bytes 393224 | tf_op jit(solution)/shard_map/ppermute | solution.py:248
  21.0 26.1 %slice-start = ((s8[16777216]{0:T(1024)(128)(4,1)}), s8[4194304]{0:T(1024)(128)(4,1)S(1)}, s32[]{:S(2)}) async-start(s8[16777216]{0:T(1024)(128)(4,1)} %bitcast.1), calls=%async_computation.1 | async-start | bytes 8388608
  21.0 26.1 %slice-start.1 = ((s8[16777216]{0:T(1024)(128)(4,1)}), s8[4194304]{0:T(1024)(128)(4,1)S(1)}, s32[]{:S(2)}) async-start(s8[16777216]{0:T(1024)(128)(4,1)} %bitcast.1), calls=%async_computation.2 | async-start | bytes 8388608
  22.9 24.2 %slice-start.2 = ((s8[16777216]{0:T(1024)(128)(4,1)}), s8[4194304]{0:T(1024)(128)(4,1)S(1)}, s32[]{:S(2)}) async-start(s8[16777216]{0:T(1024)(128)(4,1)} %bitcast.1), calls=%async_computation.3 | async-start | bytes 8388608
  22.9 24.2 %slice-start.3 = ((s8[16777216]{0:T(1024)(128)(4,1)}), s8[4194304]{0:T(1024)(128)(4,1)S(1)}, s32[]{:S(2)}) async-start(s8[16777216]{0:T(1024)(128)(4,1)} %bitcast.1), calls=%async_computation.4 | async-start | bytes 8388608
  24.9 14.0 %collective-permute-start.3 = (f32[4,2,2560]{2,1,0:T(2,128)S(1)}, f32[4,2,2560]{2,1,0:T(2,128)S(1)}, u32[]{:S(2)}, u32[]{:S(2)}) collective-permute-start(f32[4,2,2560]{2,1,0:T(2,128)S(1)} %get-tuple-element.25), channel_id=1, source_target_pairs={{0,12},{4,8},{8,4},{12,0},{1,13},{5,9},{9,5},{13,1},{2,14},{6,10},... | collective-permute-start | bytes 245768 | tf_op jit(solution)/shard_map/ppermute | solution.py:248
  25.7 13.2 %collective-permute-start.4 = (f32[4,2,2560]{2,1,0:T(2,128)S(1)}, f32[4,2,2560]{2,1,0:T(2,128)S(1)}, u32[]{:S(2)}, u32[]{:S(2)}) collective-permute-start(f32[4,2,2560]{2,1,0:T(2,128)S(1)} %get-tuple-element.26), channel_id=1, source_target_pairs={{0,8},{4,12},{8,0},{12,4},{1,9},{5,13},{9,1},{13,5},{2,10},{6,14},... | collective-permute-start | bytes 245768 | tf_op jit(solution)/shard_map/ppermute | solution.py:248
  26.2 12.7 %collective-permute-start.5 = (f32[4,2,2560]{2,1,0:T(2,128)S(1)}, f32[4,2,2560]{2,1,0:T(2,128)S(1)}, u32[]{:S(2)}, u32[]{:S(2)}) collective-permute-start(f32[4,2,2560]{2,1,0:T(2,128)S(1)} %get-tuple-element.27), channel_id=1, source_target_pairs={{0,4},{4,0},{8,12},{12,8},{1,5},{5,1},{9,13},{13,9},{2,6},{6,2},{1... | collective-permute-start | bytes 245768 | tf_op jit(solution)/shard_map/ppermute | solution.py:248
  40.6 5.9 %collective-permute-start.8 = (bf16[4,2,2048]{2,1,0:T(2,128)(2,1)S(1)}, bf16[4,2,2048]{2,1,0:T(2,128)(2,1)S(1)}, u32[]{:S(2)}, u32[]{:S(2)}) collective-permute-start(bf16[4,2,2048]{2,1,0:T(2,128)(2,1)S(1)} %shard_map.106.refs_3_), channel_id=1, source_target_pairs={{0,12},{4,8},{8,4},{12,0},{1,13},{5,9},{9,5},{13,1},{2,14},{6,10},... | collective-permute-start | bytes 98312 | tf_op jit(solution)/shard_map/ppermute | solution.py:248
  41.4 5.6 %collective-permute-start.9 = (bf16[4,2,2048]{2,1,0:T(2,128)(2,1)S(1)}, bf16[4,2,2048]{2,1,0:T(2,128)(2,1)S(1)}, u32[]{:S(2)}, u32[]{:S(2)}) collective-permute-start(bf16[4,2,2048]{2,1,0:T(2,128)(2,1)S(1)} %shard_map.106.refs_3_), channel_id=1, source_target_pairs={{0,8},{4,12},{8,0},{12,4},{1,9},{5,13},{9,1},{13,5},{2,10},{6,14},... | collective-permute-start | bytes 98312 | tf_op jit(solution)/shard_map/ppermute | solution.py:248
  42.0 5.0 %collective-permute-start.10 = (bf16[4,2,2048]{2,1,0:T(2,128)(2,1)S(1)}, bf16[4,2,2048]{2,1,0:T(2,128)(2,1)S(1)}, u32[]{:S(2)}, u32[]{:S(2)}) collective-permute-start(bf16[4,2,2048]{2,1,0:T(2,128)(2,1)S(1)} %shard_map.106.refs_3_), channel_id=1, source_target_pairs={{0,4},{4,0},{8,12},{12,8},{1,5},{5,1},{9,13},{13,9},{2,6},{6,2},{1... | collective-permute-start | bytes 98312 | tf_op jit(solution)/shard_map/ppermute | solution.py:248
  48.7 2.2 %collective-permute-start.11 = (f32[8,2,2048]{2,1,0:T(2,128)S(1)}, f32[8,2,2048]{2,1,0:T(2,128)S(1)}, u32[]{:S(2)}, u32[]{:S(2)}) collective-permute-start(f32[8,2,2048]{2,1,0:T(2,128)S(1)} %get-tuple-element.32), channel_id=1, source_target_pairs={{0,1},{1,0},{2,3},{3,2},{4,5},{5,4},{6,7},{7,6},{8,9},{9,8},{10,11... | collective-permute-start | bytes 393224 | tf_op jit(solution)/shard_map/ppermute | solution.py:252
  50.3 1.5 %collective-permute-start.13 = (f32[8,2,2048]{2,1,0:T(2,128)S(1)}, f32[8,2,2048]{2,1,0:T(2,128)S(1)}, u32[]{:S(2)}, u32[]{:S(2)}) collective-permute-start(f32[8,2,2048]{2,1,0:T(2,128)S(1)} %get-tuple-element.36), channel_id=1, source_target_pairs={{0,1},{1,0},{2,3},{3,2},{4,5},{5,4},{6,7},{7,6},{8,9},{9,8},{10,11... | collective-permute-start | bytes 393224 | tf_op jit(solution)/shard_map/ppermute | solution.py:252
  50.9 4.7 %collective-permute-start.12 = (f32[4,2,2048]{2,1,0:T(2,128)S(1)}, f32[4,2,2048]{2,1,0:T(2,128)S(1)}, u32[]{:S(2)}, u32[]{:S(2)}) collective-permute-start(f32[4,2,2048]{2,1,0:T(2,128)S(1)} %get-tuple-element.34), channel_id=1, source_target_pairs={{0,2},{1,3},{2,0},{3,1},{4,6},{5,7},{6,4},{7,5},{8,10},{9,11},{10,... | collective-permute-start | bytes 196616 | tf_op jit(solution)/shard_map/ppermute | solution.py:252
  51.9 4.8 %collective-permute-start.14 = (f32[4,2,2048]{2,1,0:T(2,128)S(1)}, f32[4,2,2048]{2,1,0:T(2,128)S(1)}, u32[]{:S(2)}, u32[]{:S(2)}) collective-permute-start(f32[4,2,2048]{2,1,0:T(2,128)S(1)} %get-tuple-element.38), channel_id=1, source_target_pairs={{0,2},{1,3},{2,0},{3,1},{4,6},{5,7},{6,4},{7,5},{8,10},{9,11},{10,... | collective-permute-start | bytes 196616 | tf_op jit(solution)/shard_map/ppermute | solution.py:252
  56.7 5.6 %collective-permute-start.15 = (bf16[2,4096]{1,0:T(2,128)(2,1)S(1)}, bf16[2,4096]{1,0:T(2,128)(2,1)S(1)}, u32[]{:S(2)}, u32[]{:S(2)}) collective-permute-start(bf16[2,4096]{1,0:T(2,128)(2,1)S(1)} %get-tuple-element.39), channel_id=1, source_target_pairs={{0,12},{4,8},{8,4},{12,0},{1,13},{5,9},{9,5},{13,1},{2,14},{6,10},... | collective-permute-start | bytes 49160 | tf_op jit(solution)/shard_map/ppermute | solution.py:248
  58.9 4.6 %collective-permute-start.16 = (bf16[2,4096]{1,0:T(2,128)(2,1)S(1)}, bf16[2,4096]{1,0:T(2,128)(2,1)S(1)}, u32[]{:S(2)}, u32[]{:S(2)}) collective-permute-start(bf16[2,4096]{1,0:T(2,128)(2,1)S(1)} %get-tuple-element.40), channel_id=1, source_target_pairs={{0,8},{4,12},{8,0},{12,4},{1,9},{5,13},{9,1},{13,5},{2,10},{6,14},... | collective-permute-start | bytes 49160 | tf_op jit(solution)/shard_map/ppermute | solution.py:248
  60.1 3.7 %collective-permute-start.17 = (bf16[2,4096]{1,0:T(2,128)(2,1)S(1)}, bf16[2,4096]{1,0:T(2,128)(2,1)S(1)}, u32[]{:S(2)}, u32[]{:S(2)}) collective-permute-start(bf16[2,4096]{1,0:T(2,128)(2,1)S(1)} %get-tuple-element.41), channel_id=1, source_target_pairs={{0,4},{4,0},{8,12},{12,8},{1,5},{5,1},{9,13},{13,9},{2,6},{6,2},{1... | collective-permute-start | bytes 49160 | tf_op jit(solution)/shard_map/ppermute | solution.py:248

commit v9 on v6

--- a/solution.py
+++ b/solution.py
@@ -31,7 +31,7 @@
             blocks_ref[i * plane + j] = normed[:, at : at + half]
 
 
-def project_kernel(own, wide, plane, rows_ref, query_ref, key_ref, value_ref, _, *refs):
+def project_kernel(own, wide, plane, rows_ref, query_ref, key_ref, value_ref, *refs):
     owners, rows, half = rows_ref.shape
     core = lax.axis_index("gz")
     at_row = pl.multiple_of((core if own else 1 - core) * half, half)
@@ -61,43 +61,75 @@
                 refs[1 + k][l] = sums_ref[(own_wide ^ k) * plane + (own_plane ^ l)]
 
 
-def share_kernel(plane, lengths_ref, keys_ref, values_ref, _, *blocks):
-    rows, slots, _ = keys_ref.shape
-    cols = blocks[0].shape[1]
-    own_plane = 2 * lax.axis_index("gy") + lax.axis_index("gz")
-    at_row = lax.broadcasted_iota(jnp.int32, (16, cols), 0)
-    filled = jnp.zeros((16, cols), jnp.float32)
+def own_place():
+    return 2 * lax.axis_index("gy") + lax.axis_index("gz")
+
+
+def write_heads(cache_ref, block_ref, start, owner):
+    rows, slots, _ = cache_ref.shape
+    cols = block_ref.shape[1]
+    at = pl.multiple_of(owner * cols, cols)
+    for r in range(rows):
+        block_ref[start + r * slots : start + (r + 1) * slots] = cache_ref[r, :, pl.ds(at, cols)]
+
+
+def write_lengths(rows, lengths_ref, block_ref):
+    at_row = lax.broadcasted_iota(jnp.int32, (16, block_ref.shape[1]), 0)
+    filled = jnp.zeros(at_row.shape, jnp.float32)
     for r in range(rows):
         filled = jnp.where(at_row == r, lengths_ref[r].astype(jnp.float32), filled)
-    for l in range(plane):
-        at = pl.multiple_of((own_plane ^ l) * cols, cols)
-        for c, cache in enumerate((keys_ref, values_ref)):
-            for r in range(rows):
-                to = (c * rows + r) * slots
-                blocks[l][to : to + slots] = cache[r, :, pl.ds(at, cols)]
-        blocks[l][2 * rows * slots :] = filled.astype(jnp.bfloat16)
-
-
-def attend_kernel(wide, plane, query_cols, frequency_ref, *refs):
-    partials, shared, attended_ref = refs[wide - 1 :: -1], refs[wide:-1], refs[-1]
-    rows, cols = partials[0].shape[1:]
+    block_ref[block_ref.shape[0] - 16 :] = filled.astype(jnp.bfloat16)
+
+
+def cut_kernel(side, lengths_ref, keys_ref, values_ref, _, *blocks):
+    rows, slots, _ = keys_ref.shape
+    for s, block in enumerate(blocks):
+        write_heads(keys_ref, block, 0, own_place() ^ (2 * s + side))
+        write_heads(values_ref, block, rows * slots, own_place() ^ (2 * s + side))
+        write_lengths(rows, lengths_ref, block)
+
+
+def round_kernel(wide, *refs):
+    partials, outs = refs[wide - 1 :: -1], refs[wide:]
+    for s, out in enumerate(outs):
+        total = partials[0][2 * s : 2 * s + 2]
+        for k in range(1, wide):
+            total = total + partials[k][2 * s : 2 * s + 2]
+        out[...] = total.astype(jnp.bfloat16)
+
+
+def pair_kernel(*refs):
+    for s, block in enumerate(refs[:-1]):
+        refs[-1][2 * s : 2 * s + 2] = block[...]
+
+
+def attend_kernel(
+    query_cols, frequency_ref, heads_ref, mine_ref, mate_ref, attended_ref
+):
+    chip, rows, cols = heads_ref.shape
     kv_cols = (cols - query_cols) // 2
     kv_heads, group = kv_cols // HD, query_cols // kv_cols
-    slots = (shared[0].shape[0] - 16) // (2 * rows)
-    pairs = plane * rows
+    slots = (mine_ref.shape[0] - 16) // (2 * rows)
+    pairs = chip * rows
     count = pairs * kv_heads
     heads = count * group
     scale = 1.0 / HD**0.5
-    total = partials[0][...]
-    for k in range(1, wide):
-        total = total + partials[k][...]
-    total = total.reshape(pairs, cols).astype(jnp.bfloat16).astype(jnp.float32)
-
-    filled = [
-        shared[p // rows][2 * rows * slots : 2 * rows * slots + 16, :HD]
-        .astype(jnp.float32)[p % rows : p % rows + 1]
-        for p in range(pairs)
-    ]
+    total = heads_ref[...].reshape(pairs, cols).astype(jnp.float32)
+
+    def cached(start):
+        return jnp.concatenate(
+            [
+                ref[start + r * slots : start + (r + 1) * slots]
+                for ref in (mine_ref, mate_ref)
+                for r in range(rows)
+            ],
+            1,
+        )
+
+    filled = []
+    for ref in (mine_ref, mate_ref):
+        last = ref[ref.shape[0] - 16 :, :HD].astype(jnp.float32)
+        filled += [last[r : r + 1] for r in range(rows)]
     angles = jnp.concatenate(filled, 0) * frequency_ref[...]
     cosine, sine = jnp.cos(angles), jnp.sin(angles)
     front = lax.broadcasted_iota(jnp.int32, (1, HD), 1) < HD // 2
@@ -119,15 +151,6 @@
     turned_query = query.T.astype(jnp.bfloat16)
     key_new = jnp.stack(key_new, 1).reshape(count, HD).astype(jnp.bfloat16)
     value_new = jnp.stack(value_new, 1).reshape(count, HD)
-
-    def cached(c):
-        return jnp.concatenate(
-            [
-                shared[p // rows][(c * rows + p % rows) * slots : (c * rows + p % rows + 1) * slots]
-                for p in range(pairs)
-            ],
-            1,
-        )
 
     head_pair = lax.broadcasted_iota(jnp.int32, (1, heads), 1) // group
     by_pair = jnp.concatenate(
@@ -151,7 +174,7 @@
     own_prob = (own_weight / denominator).astype(jnp.bfloat16)
     contract_rows = (((0,), (0,)), ((), ()))
     mixed = lax.dot_general(
-        probability, cached(1), contract_rows, preferred_element_type=jnp.float32
+        probability, cached(rows * slots), contract_rows, preferred_element_type=jnp.float32
     )
     own_prob = jnp.where(of_pair, own_prob.astype(jnp.float32), 0.0).astype(jnp.bfloat16)
     fresh = lax.dot_general(
@@ -167,7 +190,7 @@
         by_head = jnp.swapaxes(jnp.stack(mixed[h::kv_heads], 0), 0, 1)
         attended += [by_head[g] for g in range(group)]
     attended = jnp.concatenate(attended, 1)
-    attended_ref[...] = attended.reshape(plane, rows, query_cols).astype(jnp.bfloat16)
+    attended_ref[...] = attended.reshape(chip, rows, query_cols).astype(jnp.bfloat16)
 
 
 def output_kernel(at, cols, weight_ref, *refs):
@@ -270,49 +293,78 @@
         out_specs=IN_VMEM,
         compiler_params=params(8),
     )(scaled, norm_gain.reshape(1, -1))
-    shared_rows = 2 * rows * cache_keys.shape[1] + 16
-    shared = pl.pallas_call(
-        functools.partial(share_kernel, plane),
-        out_shape=[jax.ShapeDtypeStruct((shared_rows, kv_cols), jnp.bfloat16)] * plane,
-        in_specs=[IN_SMEM] + [IN_VMEM] * 3,
-        out_specs=[IN_VMEM] * plane,
-        compiler_params=params(8),
-    )(lengths, cache_keys, cache_values, normed)
-    shared = [shared[0]] + [swap_plane(shared[l], l) for l in range(1, plane)]
     own_half = swap_blocks(normed, ROW_AXES)
     other_half = swap_pairs(own_half, "gz", 1)
+    chips = plane // 2
+    block = jax.ShapeDtypeStruct(
+        (2 * rows * cache_keys.shape[1] + 16, kv_cols), cache_keys.dtype
+    )
+
+    def cut(side, after):
+        return pl.pallas_call(
+            functools.partial(cut_kernel, side),
+            out_shape=[block] * chips,
+            in_specs=[IN_SMEM] + [IN_VMEM] * 3,
+            out_specs=[IN_VMEM] * chips,
+            compiler_params=params(8),
+        )(lengths, cache_keys, cache_values, after)
+
+    mates = [swap_plane(value, 1) for value in cut(1, normed)]
+    mine = cut(0, own_half)
     weights = (query_weight, key_weight, value_weight)
     half_cost = cost(owners * rows * width * cols, width * cols)
     partial = pl.pallas_call(
         functools.partial(project_kernel, True, wide, plane),
         out_shape=jax.ShapeDtypeStruct((owners * rows, cols), jnp.float32),
-        in_specs=[IN_VMEM] * 5,
+        in_specs=[IN_VMEM] * 4,
         out_specs=IN_VMEM,
         compiler_params=params(8),
         cost_estimate=half_cost,
-    )(own_half, *weights, shared[1])
+    )(own_half, *weights)
     partial = pl.pallas_call(
         functools.partial(project_kernel, False, wide, plane),
         out_shape=[jax.ShapeDtypeStruct((plane, rows, cols), jnp.float32)] * wide,
-        in_specs=[IN_VMEM] * 6,
+        in_specs=[IN_VMEM] * 5,
         out_specs=[IN_VMEM] * wide,
         scratch_shapes=[pltpu.VMEM((owners, rows, cols), jnp.float32)],
         compiler_params=params(8),
         cost_estimate=half_cost,
-    )(other_half, *weights, shared[1], partial)
+    )(other_half, *weights, partial)
     partial = swap_wide(partial)
 
     half_dim = HD // 2
     frequency = 500000.0 ** (-np.arange(half_dim, dtype=np.float64) / half_dim)
     frequency = np.tile(frequency.astype(np.float32), 2).reshape(1, HD)
+    heads = pl.pallas_call(
+        functools.partial(round_kernel, wide),
+        out_shape=[jax.ShapeDtypeStruct((2, rows, cols), jnp.bfloat16)] * chips,
+        in_specs=[IN_VMEM] * wide,
+        out_specs=[IN_VMEM] * chips,
+        compiler_params=params(8),
+    )(*partial[::-1])
+    attended = []
+    for s in range(chips):
+        chip_rows = pl.pallas_call(
+            functools.partial(attend_kernel, query_cols),
+            out_shape=jax.ShapeDtypeStruct((2, rows, query_cols), jnp.bfloat16),
+            in_specs=[IN_VMEM] * 4,
+            out_specs=IN_VMEM,
+            compiler_params=params(8),
+            cost_estimate=cost(10**9, 2 * MIB),
+        )(
+            jnp.asarray(frequency),
+            swap_plane(heads[s], 2 * s) if s else heads[s],
+            mine[s],
+            mates[s],
+        )
+        attended.append(swap_plane(chip_rows, 2 * s) if s else chip_rows)
     attended = pl.pallas_call(
-        functools.partial(attend_kernel, wide, plane, query_cols),
+        pair_kernel,
         out_shape=jax.ShapeDtypeStruct((plane, rows, query_cols), jnp.bfloat16),
-        in_specs=[IN_VMEM] * (1 + wide + plane),
+        in_specs=[IN_VMEM] * chips,
         out_specs=IN_VMEM,
         compiler_params=params(8),
-        cost_estimate=cost(10**9, 4 * MIB),
-    )(jnp.asarray(frequency), *partial[::-1], *shared)
+    )(*attended)
     head_rows = swap_wide([attended] * wide)
     parts = 2
     part_cols = out_cols // parts

time: 72 us -> 78.8 us (1.094)
  blocking collectives: 25.4 us -> 0 us
  local copies, waits for them, and re-layouts: 1.27 us -> 13 us
  waiting for transfers between devices: 15.1 us -> 26.4 us
  Pallas kernels: 9.94 us -> 15 us
  starting transfers between devices: 20 us -> 23.9 us
    all_to_all x1 -> x0, blocking collectives: 25.4 us -> none  [swap_blocks(): return lax.all_to_all(blocks, axes, split_axis=0, concat_axis=0, tiled=True)]
    unnamed x26 -> x32, local copies, waits for them, and re-layouts: 1.27 us -> 13 us
    all_to_all x0 -> x1, waiting for transfers between devices: none -> 7.52 us  [swap_blocks(): return lax.all_to_all(blocks, axes, split_axis=0, concat_axis=0, tiled=True)]
    all_to_all x0 -> x1, starting transfers between devices: none -> 7.02 us  [swap_blocks(): return lax.all_to_all(blocks, axes, split_axis=0, concat_axis=0, tiled=True)]
    ppermute x7 -> x8, waiting for transfers between devices: 3.37 us -> 8.78 us  [swap_plane(): lax.ppermute(value, PLANE, [(i, i ^ step) for i in range(lax.axis_size(PL...]
    pallas_call x2 -> x6, Pallas kernels: 1.93 us -> 6.33 us  [the longest x2 3.71 us: shards(): pl.pallas_call(functools.partial(attend_kernel, query_cols), out_shape=ja...]
    ppermute x7 -> x8, starting transfers between devices: 6.37 us -> 3.54 us  [swap_plane(): lax.ppermute(value, PLANE, [(i, i ^ step) for i in range(lax.axis_size(PL...]
    ppermute x10, waiting for transfers between devices: 11.7 us -> 10.1 us  [swap_pairs(): lax.ppermute(value, axis, [(i, i ^ step) for i in range(lax.axis_size(axi...]
  transfers between devices with their start and end apart: 17 -> 19, of which waited for: 8 -> 13; matrix products, arithmetic and copies ran while one was open for 0% -> 0% of each run, Pallas kernels for 8% -> 13%
where the time goes in v9:
time: 78.8 us; the launch traced here: 78.5 us
  waiting for transfers between devices  26.4 us (34%)
  starting transfers between devices  23.9 us (30%)
  Pallas kernels  15 us (19%)
  local copies, waits for them, and re-layouts  13 us (16%)
    ppermute x10, starting transfers between devices, swap_pairs(): lax.ppermute(value, axis, [(i, i ^ step) for i in range(lax.axis_size(axi...  13.3 us
    unnamed x32, local copies, waits for them, and re-layouts  13 us
    ppermute x10, waiting for transfers between devices, swap_pairs(): lax.ppermute(value, axis, [(i, i ^ step) for i in range(lax.axis_size(axi...  10.1 us
    ppermute x8, waiting for transfers between devices, swap_plane(): lax.ppermute(value, PLANE, [(i, i ^ step) for i in range(lax.axis_size(PL...  8.78 us
    all_to_all x1, waiting for transfers between devices, swap_blocks(): return lax.all_to_all(blocks, axes, split_axis=0, concat_axis=0, tiled=True)  7.52 us
    all_to_all x1, starting transfers between devices, swap_blocks(): return lax.all_to_all(blocks, axes, split_axis=0, concat_axis=0, tiled=True)  7.02 us
    pallas_call x2, Pallas kernels, shards(): pl.pallas_call(functools.partial(attend_kernel, query_cols), out_shape=ja...  3.71 us
    ppermute x8, starting transfers between devices, swap_plane(): lax.ppermute(value, PLANE, [(i, i ^ step) for i in range(lax.axis_size(PL...  3.54 us
  transfers between devices with their start and end apart: 19, of which 13 were waited for; matrix products, arithmetic and copies ran while one was open for 0% of the time, Pallas kernels for 13%

profile of v9, /device:TPU:0, one launch (start us, length us, event | category | flops | bytes accessed | tf_op | source)
XLA Modules:
  0.0 78.5 jit_solution(1743229845959891869)
XLA Ops:
  0.0 0.0 copy-start.10
  0.0 1.0 %copy-done.10 = bf16[2,16384]{1,0:T(2,128)(2,1)S(1)} copy-done((bf16[2,16384]{1,0:T(2,128)(2,1)S(1)}, bf16[2,16384]{1,0:T(2,128)(2,1)}, u32[]{:S(2)}) %copy-start.10) | copy-done | bytes 65560
  1.0 0.2 shard_map.100.scaled_ref
  1.2 0.0 copy-done.7
  1.3 0.7 shard_map.101._
  2.0 0.0 copy-done.8
  2.0 0.0 copy-done.5
  2.0 1.9 %shard_map.106 = (bf16[1040,256]{1,0:T(8,128)(2,1)S(1)}, bf16[1040,256]{1,0:T(8,128)(2,1)}) custom-call(s32[2]{0:T(128)S(1)} %copy-done.8, bf16[2,256,1024]{2,1,0:T(8,128)(2,1)S(1)} %copy-done.4, bf16[2,256,1024]{2,1,0:T(8,128)(2,1)S(1)} %copy-done.5, bf16[16,2,2048]{2,1,0:T(2,128)(2,1)} %shard_map.101._), custom_call_target="tpu_custom_call" | custom-call | tf_op jit(solution)/shard_map/pallas_call | solution.py:304
  3.9 0.8 %copy-done.9 = bf16[1040,256]{1,0:T(8,128)(2,1)} copy-done((bf16[1040,256]{1,0:T(8,128)(2,1)}, bf16[1040,256]{1,0:T(8,128)(2,1)S(1)}, u32[]{:S(2)}) %copy-start.9) | copy-done | bytes 532504
  4.7 0.5 collective-permute-start.6
  5.2 7.0 %all-to-all-start = ((bf16[16,2,2048]{2,1,0:T(2,128)(2,1)}), bf16[16,2,2048]{2,1,0:T(2,128)(2,1)S(1)}, u32[]{:S(2)}, u32[]{:S(2)}) async-start(bf16[16,2,2048]{2,1,0:T(2,128)(2,1)} %shard_map.101._), calls=%async_computation | async-start | bytes 262144 | tf_op jit(solution)/shard_map/all_to_all | solution.py:238
  12.2 0.4 collective-permute-start.4
  12.6 7.5 %all-to-all-done.rows_ref._ = bf16[16,2,2048]{2,1,0:T(2,128)(2,1)S(1)} async-done(((bf16[16,2,2048]{2,1,0:T(2,128)(2,1)}), bf16[16,2,2048]{2,1,0:T(2,128)(2,1)S(1)}, u32[]{:S(2)}, u32[]{:S(2)}) %all-to-all-start) | async-done | bytes 131104 | tf_op jit(solution)/shard_map/all_to_all | solution.py:238
  20.1 0.0 collective-permute-start
  20.1 0.0 copy-done.2
  20.1 5.8 %copy-done = bf16[4096,2048]{1,0:T(8,128)(2,1)S(1)} copy-done((bf16[4096,2048]{1,0:T(8,128)(2,1)S(1)}, bf16[4096,2048]{1,0:T(8,128)(2,1)}, u32[]{:S(2)}) %copy-start) | copy-done | bytes 16777240
  25.9 1.6 %copy-done.3 = bf16[4096,256]{1,0:T(8,128)(2,1)S(1)} copy-done((bf16[4096,256]{1,0:T(8,128)(2,1)S(1)}, bf16[4096,256]{1,0:T(8,128)(2,1)}, u32[]{:S(2)}) %copy-start.3) | copy-done | bytes 2097176
  27.5 1.9 %shard_map.102.refs_0_ = f32[32,2560]{1,0:T(8,128)S(1)} custom-call(bf16[16,2,2048]{2,1,0:T(2,128)(2,1)S(1)} %all-to-all-done.rows_ref._, bf16[4096,2048]{1,0:T(8,128)(2,1)S(1)} %copy-done, bf16[4096,256]{1,0:T(8,128)(2,1)S(1)} %copy-done.2, bf16[4096,256]{1,0:T(8,128)(2,1)S(1)} %copy-done.3), custom_call_target="tpu_custom_call" | custom-call | flops 335544320 | bytes 10485760 | tf_op jit(solution)/shard_map/pallas_call | solution.py:316
  29.4 0.0 slice-start.1
  29.4 0.0 slice-start.2
  29.4 0.0 collective-permute-done.rows_ref
  29.4 3.8 %copy-done.1 = bf16[4096,2048]{1,0:T(8,128)(2,1)S(1)} copy-done((bf16[4096,2048]{1,0:T(8,128)(2,1)S(1)}, bf16[4096,2048]{1,0:T(8,128)(2,1)}, u32[]{:S(2)}) %copy-start.1) | copy-done | bytes 16777240
  33.3 2.0 %shard_map.103 = (f32[4,2,2560]{2,1,0:T(2,128)S(1)}, f32[4,2,2560]{2,1,0:T(2,128)S(1)}, f32[4,2,2560]{2,1,0:T(2,128)S(1)}, f32[4,2,2560]{2,1,0:T(2,128)S(1)}) custom-call(bf16[16,2,2048]{2,1,0:T(2,128)(2,1)S(1)} %collective-permute-done.rows_ref, bf16[4096,2048]{1,0:T(8,128)(2,1)S(1)} %copy-done.1, bf16[4096,256]{1,0:T(8,128)(2,1)S(1)} %copy-done.2, ...), custom_call_target="tpu_custom_call" | custom-call | flops 335544320 | bytes 10485760 | tf_op jit(solution)/shard_map/pallas_call | solution.py:324
  35.2 1.0 %collective-permute-start.1 = (f32[4,2,2560]{2,1,0:T(2,128)S(1)}, f32[4,2,2560]{2,1,0:T(2,128)S(1)}, u32[]{:S(2)}, u32[]{:S(2)}) collective-permute-start(f32[4,2,2560]{2,1,0:T(2,128)S(1)} %get-tuple-element.27), channel_id=1, source_target_pairs={{0,12},{4,8},{8,4},{12,0},{1,13},{5,9},{9,5},{13,1},{2,14},{6,10},... | collective-permute-start | bytes 245768 | tf_op jit(solution)/shard_map/ppermute | solution.py:242
  36.2 0.6 collective-permute-start.2
  36.8 2.9 %collective-permute-start.3 = (f32[4,2,2560]{2,1,0:T(2,128)S(1)}, f32[4,2,2560]{2,1,0:T(2,128)S(1)}, u32[]{:S(2)}, u32[]{:S(2)}) collective-permute-start(f32[4,2,2560]{2,1,0:T(2,128)S(1)} %get-tuple-element.29), channel_id=1, source_target_pairs={{0,4},{4,0},{8,12},{12,8},{1,5},{5,1},{9,13},{13,9},{2,6},{6,2},{1... | collective-permute-start | bytes 245768 | tf_op jit(solution)/shard_map/ppermute | solution.py:242
  39.7 2.7 %collective-permute-done.1.refs_0_ = f32[4,2,2560]{2,1,0:T(2,128)S(1)} collective-permute-done((f32[4,2,2560]{2,1,0:T(2,128)S(1)}, f32[4,2,2560]{2,1,0:T(2,128)S(1)}, u32[]{:S(2)}, u32[]{:S(2)}) %collective-permute-start.1) | collective-permute-done | bytes 81952 | tf_op jit(solution)/shard_map/ppermute | solution.py:242
  42.4 2.6 %collective-permute-done.2.refs_1_ = f32[4,2,2560]{2,1,0:T(2,128)S(1)} collective-permute-done((f32[4,2,2560]{2,1,0:T(2,128)S(1)}, f32[4,2,2560]{2,1,0:T(2,128)S(1)}, u32[]{:S(2)}, u32[]{:S(2)}) %collective-permute-start.2) | collective-permute-done | bytes 81952 | tf_op jit(solution)/shard_map/ppermute | solution.py:242
  45.0 0.0 collective-permute-done.3.refs_2_
  45.1 0.0 slice-start.3
  45.1 0.3 collective-permute-start.5
  45.3 0.7 shard_map.105
  46.0 2.9 %collective-permute-done.5.heads_ref = bf16[2,2,2560]{2,1,0:T(2,128)(2,1)S(1)} collective-permute-done((bf16[2,2,2560]{2,1,0:T(2,128)(2,1)S(1)}, bf16[2,2,2560]{2,1,0:T(2,128)(2,1)S(1)}, u32[]{:S(2)}, u32[]{:S(2)}) %collective-permute-start.5) | collective-permute-done | bytes 20512 | tf_op jit(solution)/shard_map/ppermute | solution.py:246
  48.9 0.0 collective-permute-done.6.mate_ref
  48.9 1.9 %shard_map.108 = bf16[2,2,2048]{2,1,0:T(2,128)(2,1)S(1)} custom-call(f32[1,128]{1,0:T(1,128)S(1)} %copy-done.11, bf16[2,2,2560]{2,1,0:T(2,128)(2,1)S(1)} %collective-permute-done.5.heads_ref, bf16[1040,256]{1,0:T(8,128)(2,1)S(1)} %get-tuple-element.35.mine_ref, bf16[1040,256]{1,0:T(8,128)(2,1)} %collective-permute-done.6.mate_ref), custom_call_target="tpu_custom_call" | custom-call | flops 1000000000 | bytes 2097152 | tf_op jit(solution)/shard_map/pallas_call | solution.py:347
  50.8 0.3 collective-permute-start.7
  51.1 0.0 collective-permute-done.4.mate_ref
  51.1 1.9 %shard_map.107.refs_0_ = bf16[2,2,2048]{2,1,0:T(2,128)(2,1)S(1)} custom-call(f32[1,128]{1,0:T(1,128)S(1)} %copy-done.11, bf16[2,2,2560]{2,1,0:T(2,128)(2,1)S(1)} %get-tuple-element.31.heads_ref, bf16[1040,256]{1,0:T(8,128)(2,1)S(1)} %get-tuple-element.32.mine_ref, bf16[1040,256]{1,0:T(8,128)(2,1)} %collective-permute-done.4.mate_ref), custom_call_target="tpu_custom_call" | custom-call | flops 1000000000 | bytes 2097152 | tf_op jit(solution)/shard_map/pallas_call | solution.py:347
  52.9 1.7 %collective-permute-done.7.refs_1_ = bf16[2,2,2048]{2,1,0:T(2,128)(2,1)S(1)} collective-permute-done((bf16[2,2,2048]{2,1,0:T(2,128)(2,1)S(1)}, bf16[2,2,2048]{2,1,0:T(2,128)(2,1)S(1)}, u32[]{:S(2)}, u32[]{:S(2)}) %collective-permute-start.7) | collective-permute-done | bytes 16416 | tf_op jit(solution)/shard_map/ppermute | solution.py:246
  54.6 1.7 %collective-permute-start.10 = (bf16[4,2,2048]{2,1,0:T(2,128)(2,1)S(1)}, bf16[4,2,2048]{2,1,0:T(2,128)(2,1)S(1)}, u32[]{:S(2)}, u32[]{:S(2)}) collective-permute-start(bf16[4,2,2048]{2,1,0:T(2,128)(2,1)S(1)} %shard_map.109.refs_0_), channel_id=1, source_target_pairs={{0,12},{4,8},{8,4},{12,0},{1,13},{5,9},{9,5},{13,1},{2,14},{6,10},... | collective-permute-start | bytes 98312 | tf_op jit(solution)/shard_map/ppermute | solution.py:242
  56.3 0.0 collective-permute-start.9
  56.3 2.6 %collective-permute-start.8 = (bf16[4,2,2048]{2,1,0:T(2,128)(2,1)S(1)}, bf16[4,2,2048]{2,1,0:T(2,128)(2,1)S(1)}, u32[]{:S(2)}, u32[]{:S(2)}) collective-permute-start(bf16[4,2,2048]{2,1,0:T(2,128)(2,1)S(1)} %shard_map.109.refs_0_), channel_id=1, source_target_pairs={{0,4},{4,0},{8,12},{12,8},{1,5},{5,1},{9,13},{13,9},{2,6},{6,2},{1... | collective-permute-start | bytes 98312 | tf_op jit(solution)/shard_map/ppermute | solution.py:242
  59.0 1.3 %collective-permute-done.10.refs_3_ = bf16[4,2,2048]{2,1,0:T(2,128)(2,1)S(1)} collective-permute-done((bf16[4,2,2048]{2,1,0:T(2,128)(2,1)S(1)}, bf16[4,2,2048]{2,1,0:T(2,128)(2,1)S(1)}, u32[]{:S(2)}, u32[]{:S(2)}) %collective-permute-start.10) | collective-permute-done | bytes 32800 | tf_op jit(solution)/shard_map/ppermute | solution.py:242
  60.3 0.9 %collective-permute-done.9.refs_2_ = bf16[4,2,2048]{2,1,0:T(2,128)(2,1)S(1)} collective-permute-done((bf16[4,2,2048]{2,1,0:T(2,128)(2,1)S(1)}, bf16[4,2,2048]{2,1,0:T(2,128)(2,1)S(1)}, u32[]{:S(2)}, u32[]{:S(2)}) %collective-permute-start.9) | collective-permute-done | bytes 32800 | tf_op jit(solution)/shard_map/ppermute | solution.py:242
  61.2 0.0 collective-permute-done.8.refs_1_
  61.2 0.0 slice-done
  61.3 1.5 %shard_map.110 = (f32[8,2,2048]{2,1,0:T(2,128)S(1)}, f32[8,2,2048]{2,1,0:T(2,128)S(1)}) custom-call(bf16[2048,4096]{1,0:T(8,128)(2,1)S(1)} %bitcast.2, bf16[4,2,2048]{2,1,0:T(2,128)(2,1)S(1)} %shard_map.109.refs_0_, bf16[4,2,2048]{2,1,0:T(2,128)(2,1)S(1)} %collective-permute-done.8.refs_1_, bf16[4,2,2048]{2,1,0:T(2,128)(2,1)S(1)} %collective-permute-done.9.refs_2_, ...), custom_call_target="tpu_custom_call" | custom-call | flops 268435456 | bytes 8388608 | tf_op jit(solution)/shard_map/pallas_call | solution.py:375
  62.8 0.1 collective-permute-start.11
  62.9 1.5 %shard_map.112 = (f32[8,2,2048]{2,1,0:T(2,128)S(1)}, f32[8,2,2048]{2,1,0:T(2,128)S(1)}) custom-call(bf16[2048,4096]{1,0:T(8,128)(2,1)S(1)} %bitcast.2, bf16[4,2,2048]{2,1,0:T(2,128)(2,1)S(1)} %shard_map.109.refs_0_, bf16[4,2,2048]{2,1,0:T(2,128)(2,1)S(1)} %collective-permute-done.8.refs_1_, bf16[4,2,2048]{2,1,0:T(2,128)(2,1)S(1)} %collective-permute-done.9.refs_2_, ...), custom_call_target="tpu_custom_call" | custom-call | flops 268435456 | bytes 8388608 | tf_op jit(solution)/shard_map/pallas_call | solution.py:375
  64.5 0.6 collective-permute-start.13
  65.0 0.0 collective-permute-done.11.b_ref
  65.0 0.3 collective-permute-start.12
  65.3 0.7 collective-permute-done.13.b_ref
  66.0 1.2 %collective-permute-start.14 = (f32[4,2,2048]{2,1,0:T(2,128)S(1)}, f32[4,2,2048]{2,1,0:T(2,128)S(1)}, u32[]{:S(2)}, u32[]{:S(2)}) collective-permute-start(f32[4,2,2048]{2,1,0:T(2,128)S(1)} %get-tuple-element.44), channel_id=1, source_target_pairs={{0,2},{1,3},{2,0},{3,1},{4,6},{5,7},{6,4},{7,5},{8,10},{9,11},{10,... | collective-permute-start | bytes 196616 | tf_op jit(solution)/shard_map/ppermute | solution.py:246
  67.2 2.6 %collective-permute-done.12.refs_1_ = f32[4,2,2048]{2,1,0:T(2,128)S(1)} collective-permute-done((f32[4,2,2048]{2,1,0:T(2,128)S(1)}, f32[4,2,2048]{2,1,0:T(2,128)S(1)}, u32[]{:S(2)}, u32[]{:S(2)}) %collective-permute-start.12) | collective-permute-done | bytes 65568 | tf_op jit(solution)/shard_map/ppermute | solution.py:246
  69.8 1.0 %collective-permute-done.14.refs_3_ = f32[4,2,2048]{2,1,0:T(2,128)S(1)} collective-permute-done((f32[4,2,2048]{2,1,0:T(2,128)S(1)}, f32[4,2,2048]{2,1,0:T(2,128)S(1)}, u32[]{:S(2)}, u32[]{:S(2)}) %collective-permute-start.14) | collective-permute-done | bytes 65568 | tf_op jit(solution)/shard_map/ppermute | solution.py:246
  70.8 0.1 shard_map.114
  70.8 2.1 %collective-permute-start.15 = (bf16[2,4096]{1,0:T(2,128)(2,1)S(1)}, bf16[2,4096]{1,0:T(2,128)(2,1)S(1)}, u32[]{:S(2)}, u32[]{:S(2)}) collective-permute-start(bf16[2,4096]{1,0:T(2,128)(2,1)S(1)} %get-tuple-element.45), channel_id=1, source_target_pairs={{0,12},{4,8},{8,4},{12,0},{1,13},{5,9},{9,5},{13,1},{2,14},{6,10},... | collective-permute-start | bytes 49160 | tf_op jit(solution)/shard_map/ppermute | solution.py:242
  72.9 1.1 %collective-permute-start.16 = (bf16[2,4096]{1,0:T(2,128)(2,1)S(1)}, bf16[2,4096]{1,0:T(2,128)(2,1)S(1)}, u32[]{:S(2)}, u32[]{:S(2)}) collective-permute-start(bf16[2,4096]{1,0:T(2,128)(2,1)S(1)} %get-tuple-element.46), channel_id=1, source_target_pairs={{0,8},{4,12},{8,0},{12,4},{1,9},{5,13},{9,1},{13,5},{2,10},{6,14},... | collective-permute-start | bytes 49160 | tf_op jit(solution)/shard_map/ppermute | solution.py:242
  74.0 1.3 %collective-permute-start.17 = (bf16[2,4096]{1,0:T(2,128)(2,1)S(1)}, bf16[2,4096]{1,0:T(2,128)(2,1)S(1)}, u32[]{:S(2)}, u32[]{:S(2)}) collective-permute-start(bf16[2,4096]{1,0:T(2,128)(2,1)S(1)} %get-tuple-element.47), channel_id=1, source_target_pairs={{0,4},{4,0},{8,12},{12,8},{1,5},{5,1},{9,13},{13,9},{2,6},{6,2},{1... | collective-permute-start | bytes 49160 | tf_op jit(solution)/shard_map/ppermute | solution.py:242
  75.3 1.1 %collective-permute-done.15.refs_0_ = bf16[2,4096]{1,0:T(2,128)(2,1)S(1)} collective-permute-done((bf16[2,4096]{1,0:T(2,128)(2,1)S(1)}, bf16[2,4096]{1,0:T(2,128)(2,1)S(1)}, u32[]{:S(2)}, u32[]{:S(2)}) %collective-permute-start.15) | collective-permute-done | bytes 16416 | tf_op jit(solution)/shard_map/ppermute | solution.py:242
  76.4 1.2 %collective-permute-done.16.refs_1_ = bf16[2,4096]{1,0:T(2,128)(2,1)S(1)} collective-permute-done((bf16[2,4096]{1,0:T(2,128)(2,1)S(1)}, bf16[2,4096]{1,0:T(2,128)(2,1)S(1)}, u32[]{:S(2)}, u32[]{:S(2)}) %collective-permute-start.16) | collective-permute-done | bytes 16416 | tf_op jit(solution)/shard_map/ppermute | solution.py:242
  77.7 0.2 collective-permute-done.17.refs_2_
  77.8 0.6 shard_map.115
  (23 shorter events, 0.1 us)
Async XLA Ops:
  0.0 1.2 %copy-start.7 = (f32[16384]{0:T(1024)S(1)}, f32[16384]{0:T(1024)}, u32[]{:S(2)}) copy-start(f32[16384]{0:T(1024)} %param.11) | copy-start | bytes 196612
  0.0 2.0 %copy-start.8 = (s32[2]{0:T(128)S(1)}, s32[2]{0:T(128)}, u32[]{:S(2)}) copy-start(s32[2]{0:T(128)} %lengths_ref.3) | copy-start | bytes 28
  0.0 2.0 %copy-start.5 = (bf16[2,256,1024]{2,1,0:T(8,128)(2,1)S(1)}, bf16[2,256,1024]{2,1,0:T(8,128)(2,1)}, u32[]{:S(2)}) copy-start(bf16[2,256,1024]{2,1,0:T(8,128)(2,1)} %values_ref.3) | copy-start | bytes 3145732
  0.0 2.0 %copy-start.4 = (bf16[2,256,1024]{2,1,0:T(8,128)(2,1)S(1)}, bf16[2,256,1024]{2,1,0:T(8,128)(2,1)}, u32[]{:S(2)}) copy-start(bf16[2,256,1024]{2,1,0:T(8,128)(2,1)} %keys_ref.3) | copy-start | bytes 3145732
  0.0 20.1 %copy-start.2 = (bf16[4096,256]{1,0:T(8,128)(2,1)S(1)}, bf16[4096,256]{1,0:T(8,128)(2,1)}, u32[]{:S(2)}) copy-start(bf16[4096,256]{1,0:T(8,128)(2,1)} %key_ref.3) | copy-start | bytes 6291460
  0.0 1.0 %copy-start.10 = (bf16[2,16384]{1,0:T(2,128)(2,1)S(1)}, bf16[2,16384]{1,0:T(2,128)(2,1)}, u32[]{:S(2)}) copy-start(bf16[2,16384]{1,0:T(2,128)(2,1)} %tokens_ref.1) | copy-start | bytes 196612
  3.9 0.8 %copy-start.9 = (bf16[1040,256]{1,0:T(8,128)(2,1)}, bf16[1040,256]{1,0:T(8,128)(2,1)S(1)}, u32[]{:S(2)}) copy-start(bf16[1040,256]{1,0:T(8,128)(2,1)S(1)} %get-tuple-element.33) | copy-start | bytes 1597444
  4.7 44.2 %collective-permute-start.6 = (bf16[1040,256]{1,0:T(8,128)(2,1)}, bf16[1040,256]{1,0:T(8,128)(2,1)}, u32[]{:S(2)}, u32[]{:S(2)}) collective-permute-start(bf16[1040,256]{1,0:T(8,128)(2,1)} %get-tuple-element.36), channel_id=1, source_target_pairs={{0,1},{1,0},{2,3},{3,2},{4,5},{5,4},{6,7},{7,6},{8,9},{9,8},{10,11... | collective-permute-start | bytes 1597448 | tf_op jit(solution)/shard_map/ppermute | solution.py:246
  5.2 15.0 %all-to-all-start = ((bf16[16,2,2048]{2,1,0:T(2,128)(2,1)}), bf16[16,2,2048]{2,1,0:T(2,128)(2,1)S(1)}, u32[]{:S(2)}, u32[]{:S(2)}) async-start(bf16[16,2,2048]{2,1,0:T(2,128)(2,1)} %shard_map.101._), calls=%async_computation | async-start | bytes 262144 | tf_op jit(solution)/shard_map/all_to_all | solution.py:238
  12.2 38.9 %collective-permute-start.4 = (bf16[1040,256]{1,0:T(8,128)(2,1)}, bf16[1040,256]{1,0:T(8,128)(2,1)}, u32[]{:S(2)}, u32[]{:S(2)}) collective-permute-start(bf16[1040,256]{1,0:T(8,128)(2,1)} %copy-done.9), channel_id=1, source_target_pairs={{0,1},{1,0},{2,3},{3,2},{4,5},{5,4},{6,7},{7,6},{8,9},{9,8},{10,11... | collective-permute-start | bytes 1597448 | tf_op jit(solution)/shard_map/ppermute | solution.py:246
  20.1 9.3 %collective-permute-start = (bf16[16,2,2048]{2,1,0:T(2,128)(2,1)S(1)}, bf16[16,2,2048]{2,1,0:T(2,128)(2,1)S(1)}, u32[]{:S(2)}, u32[]{:S(2)}) collective-permute-start(bf16[16,2,2048]{2,1,0:T(2,128)(2,1)S(1)} %all-to-all-done.rows_ref._), channel_id=1, source_target_pairs={{0,1},{1,0},{2,3},{3,2},{4,5},{5,4},{6,7},{7,6},{8,9},{9,8},{10,11... | collective-permute-start | bytes 393224 | tf_op jit(solution)/shard_map/ppermute | solution.py:242
  20.1 5.8 %copy-start = (bf16[4096,2048]{1,0:T(8,128)(2,1)S(1)}, bf16[4096,2048]{1,0:T(8,128)(2,1)}, u32[]{:S(2)}) copy-start(bf16[4096,2048]{1,0:T(8,128)(2,1)} %query_ref.3) | copy-start | bytes 50331652
  25.9 1.6 %copy-start.3 = (bf16[4096,256]{1,0:T(8,128)(2,1)S(1)}, bf16[4096,256]{1,0:T(8,128)(2,1)}, u32[]{:S(2)}) copy-start(bf16[4096,256]{1,0:T(8,128)(2,1)} %value_ref.3) | copy-start | bytes 6291460
  27.5 5.8 %copy-start.1 = (bf16[4096,2048]{1,0:T(8,128)(2,1)S(1)}, bf16[4096,2048]{1,0:T(8,128)(2,1)}, u32[]{:S(2)}) copy-start(bf16[4096,2048]{1,0:T(8,128)(2,1)} %query_ref.3) | copy-start | bytes 50331652
  27.5 17.9 %copy-start.6 = (bf16[2,256,1024]{2,1,0:T(8,128)(2,1)S(1)}, bf16[2,256,1024]{2,1,0:T(8,128)(2,1)}, u32[]{:S(2)}) copy-start(bf16[2,256,1024]{2,1,0:T(8,128)(2,1)} %values_ref.3) | copy-start | bytes 3145732
  29.4 19.5 %copy-start.11 = (f32[1,128]{1,0:T(1,128)S(1)}, f32[1,128]{1,0:T(1,128)}, u32[]{:S(2)}) copy-start(f32[1,128]{1,0:T(1,128)} %constant.2.clone.frequency_ref) | copy-start | bytes 1540
  29.4 31.9 %slice-start = ((s8[16777216]{0:T(1024)(128)(4,1)}), s8[4194304]{0:T(1024)(128)(4,1)S(1)}, s32[]{:S(2)}) async-start(s8[16777216]{0:T(1024)(128)(4,1)} %bitcast.1), calls=%async_computation.1 | async-start | bytes 8388608
  29.4 31.8 %slice-start.1 = ((s8[16777216]{0:T(1024)(128)(4,1)}), s8[4194304]{0:T(1024)(128)(4,1)S(1)}, s32[]{:S(2)}) async-start(s8[16777216]{0:T(1024)(128)(4,1)} %bitcast.1), calls=%async_computation.2 | async-start | bytes 8388608
  29.4 31.8 %slice-start.2 = ((s8[16777216]{0:T(1024)(128)(4,1)}), s8[4194304]{0:T(1024)(128)(4,1)S(1)}, s32[]{:S(2)}) async-start(s8[16777216]{0:T(1024)(128)(4,1)} %bitcast.1), calls=%async_computation.3 | async-start | bytes 8388608
  35.2 7.2 %collective-permute-start.1 = (f32[4,2,2560]{2,1,0:T(2,128)S(1)}, f32[4,2,2560]{2,1,0:T(2,128)S(1)}, u32[]{:S(2)}, u32[]{:S(2)}) collective-permute-start(f32[4,2,2560]{2,1,0:T(2,128)S(1)} %get-tuple-element.27), channel_id=1, source_target_pairs={{0,12},{4,8},{8,4},{12,0},{1,13},{5,9},{9,5},{13,1},{2,14},{6,10},... | collective-permute-start | bytes 245768 | tf_op jit(solution)/shard_map/ppermute | solution.py:242
  36.2 8.8 %collective-permute-start.2 = (f32[4,2,2560]{2,1,0:T(2,128)S(1)}, f32[4,2,2560]{2,1,0:T(2,128)S(1)}, u32[]{:S(2)}, u32[]{:S(2)}) collective-permute-start(f32[4,2,2560]{2,1,0:T(2,128)S(1)} %get-tuple-element.28), channel_id=1, source_target_pairs={{0,8},{4,12},{8,0},{12,4},{1,9},{5,13},{9,1},{13,5},{2,10},{6,14},... | collective-permute-start | bytes 245768 | tf_op jit(solution)/shard_map/ppermute | solution.py:242
  36.8 8.2 %collective-permute-start.3 = (f32[4,2,2560]{2,1,0:T(2,128)S(1)}, f32[4,2,2560]{2,1,0:T(2,128)S(1)}, u32[]{:S(2)}, u32[]{:S(2)}) collective-permute-start(f32[4,2,2560]{2,1,0:T(2,128)S(1)} %get-tuple-element.29), channel_id=1, source_target_pairs={{0,4},{4,0},{8,12},{12,8},{1,5},{5,1},{9,13},{13,9},{2,6},{6,2},{1... | collective-permute-start | bytes 245768 | tf_op jit(solution)/shard_map/ppermute | solution.py:242
  45.1 16.2 %slice-start.3 = ((s8[16777216]{0:T(1024)(128)(4,1)}), s8[4194304]{0:T(1024)(128)(4,1)S(1)}, s32[]{:S(2)}) async-start(s8[16777216]{0:T(1024)(128)(4,1)} %bitcast.1), calls=%async_computation.4 | async-start | bytes 8388608
  45.1 3.8 %collective-permute-start.5 = (bf16[2,2,2560]{2,1,0:T(2,128)(2,1)S(1)}, bf16[2,2,2560]{2,1,0:T(2,128)(2,1)S(1)}, u32[]{:S(2)}, u32[]{:S(2)}) collective-permute-start(bf16[2,2,2560]{2,1,0:T(2,128)(2,1)S(1)} %get-tuple-element.34), channel_id=1, source_target_pairs={{0,2},{1,3},{2,0},{3,1},{4,6},{5,7},{6,4},{7,5},{8,10},{9,11},{10,... | collective-permute-start | bytes 61448 | tf_op jit(solution)/shard_map/ppermute | solution.py:246
  50.8 3.8 %collective-permute-start.7 = (bf16[2,2,2048]{2,1,0:T(2,128)(2,1)S(1)}, bf16[2,2,2048]{2,1,0:T(2,128)(2,1)S(1)}, u32[]{:S(2)}, u32[]{:S(2)}) collective-permute-start(bf16[2,2,2048]{2,1,0:T(2,128)(2,1)S(1)} %shard_map.108), channel_id=1, source_target_pairs={{0,2},{1,3},{2,0},{3,1},{4,6},{5,7},{6,4},{7,5},{8,10},{9,11},{10,... | collective-permute-start | bytes 49160 | tf_op jit(solution)/shard_map/ppermute | solution.py:246
  54.6 5.7 %collective-permute-start.10 = (bf16[4,2,2048]{2,1,0:T(2,128)(2,1)S(1)}, bf16[4,2,2048]{2,1,0:T(2,128)(2,1)S(1)}, u32[]{:S(2)}, u32[]{:S(2)}) collective-permute-start(bf16[4,2,2048]{2,1,0:T(2,128)(2,1)S(1)} %shard_map.109.refs_0_), channel_id=1, source_target_pairs={{0,12},{4,8},{8,4},{12,0},{1,13},{5,9},{9,5},{13,1},{2,14},{6,10},... | collective-permute-start | bytes 98312 | tf_op jit(solution)/shard_map/ppermute | solution.py:242
  56.3 4.9 %collective-permute-start.9 = (bf16[4,2,2048]{2,1,0:T(2,128)(2,1)S(1)}, bf16[4,2,2048]{2,1,0:T(2,128)(2,1)S(1)}, u32[]{:S(2)}, u32[]{:S(2)}) collective-permute-start(bf16[4,2,2048]{2,1,0:T(2,128)(2,1)S(1)} %shard_map.109.refs_0_), channel_id=1, source_target_pairs={{0,8},{4,12},{8,0},{12,4},{1,9},{5,13},{9,1},{13,5},{2,10},{6,14},... | collective-permute-start | bytes 98312 | tf_op jit(solution)/shard_map/ppermute | solution.py:242
  56.3 4.9 %collective-permute-start.8 = (bf16[4,2,2048]{2,1,0:T(2,128)(2,1)S(1)}, bf16[4,2,2048]{2,1,0:T(2,128)(2,1)S(1)}, u32[]{:S(2)}, u32[]{:S(2)}) collective-permute-start(bf16[4,2,2048]{2,1,0:T(2,128)(2,1)S(1)} %shard_map.109.refs_0_), channel_id=1, source_target_pairs={{0,4},{4,0},{8,12},{12,8},{1,5},{5,1},{9,13},{13,9},{2,6},{6,2},{1... | collective-permute-start | bytes 98312 | tf_op jit(solution)/shard_map/ppermute | solution.py:242
  62.8 2.2 %collective-permute-start.11 = (f32[8,2,2048]{2,1,0:T(2,128)S(1)}, f32[8,2,2048]{2,1,0:T(2,128)S(1)}, u32[]{:S(2)}, u32[]{:S(2)}) collective-permute-start(f32[8,2,2048]{2,1,0:T(2,128)S(1)} %get-tuple-element.38), channel_id=1, source_target_pairs={{0,1},{1,0},{2,3},{3,2},{4,5},{5,4},{6,7},{7,6},{8,9},{9,8},{10,11... | collective-permute-start | bytes 393224 | tf_op jit(solution)/shard_map/ppermute | solution.py:246
  64.5 1.5 %collective-permute-start.13 = (f32[8,2,2048]{2,1,0:T(2,128)S(1)}, f32[8,2,2048]{2,1,0:T(2,128)S(1)}, u32[]{:S(2)}, u32[]{:S(2)}) collective-permute-start(f32[8,2,2048]{2,1,0:T(2,128)S(1)} %get-tuple-element.42), channel_id=1, source_target_pairs={{0,1},{1,0},{2,3},{3,2},{4,5},{5,4},{6,7},{7,6},{8,9},{9,8},{10,11... | collective-permute-start | bytes 393224 | tf_op jit(solution)/shard_map/ppermute | solution.py:246
  65.0 4.7 %collective-permute-start.12 = (f32[4,2,2048]{2,1,0:T(2,128)S(1)}, f32[4,2,2048]{2,1,0:T(2,128)S(1)}, u32[]{:S(2)}, u32[]{:S(2)}) collective-permute-start(f32[4,2,2048]{2,1,0:T(2,128)S(1)} %get-tuple-element.40), channel_id=1, source_target_pairs={{0,2},{1,3},{2,0},{3,1},{4,6},{5,7},{6,4},{7,5},{8,10},{9,11},{10,... | collective-permute-start | bytes 196616 | tf_op jit(solution)/shard_map/ppermute | solution.py:246
  66.0 4.8 %collective-permute-start.14 = (f32[4,2,2048]{2,1,0:T(2,128)S(1)}, f32[4,2,2048]{2,1,0:T(2,128)S(1)}, u32[]{:S(2)}, u32[]{:S(2)}) collective-permute-start(f32[4,2,2048]{2,1,0:T(2,128)S(1)} %get-tuple-element.44), channel_id=1, source_target_pairs={{0,2},{1,3},{2,0},{3,1},{4,6},{5,7},{6,4},{7,5},{8,10},{9,11},{10,... | collective-permute-start | bytes 196616 | tf_op jit(solution)/shard_map/ppermute | solution.py:246
  70.8 5.6 %collective-permute-start.15 = (bf16[2,4096]{1,0:T(2,128)(2,1)S(1)}, bf16[2,4096]{1,0:T(2,128)(2,1)S(1)}, u32[]{:S(2)}, u32[]{:S(2)}) collective-permute-start(bf16[2,4096]{1,0:T(2,128)(2,1)S(1)} %get-tuple-element.45), channel_id=1, source_target_pairs={{0,12},{4,8},{8,4},{12,0},{1,13},{5,9},{9,5},{13,1},{2,14},{6,10},... | collective-permute-start | bytes 49160 | tf_op jit(solution)/shard_map/ppermute | solution.py:242
  72.9 4.7 %collective-permute-start.16 = (bf16[2,4096]{1,0:T(2,128)(2,1)S(1)}, bf16[2,4096]{1,0:T(2,128)(2,1)S(1)}, u32[]{:S(2)}, u32[]{:S(2)}) collective-permute-start(bf16[2,4096]{1,0:T(2,128)(2,1)S(1)} %get-tuple-element.46), channel_id=1, source_target_pairs={{0,8},{4,12},{8,0},{12,4},{1,9},{5,13},{9,1},{13,5},{2,10},{6,14},... | collective-permute-start | bytes 49160 | tf_op jit(solution)/shard_map/ppermute | solution.py:242
  74.0 3.8 %collective-permute-start.17 = (bf16[2,4096]{1,0:T(2,128)(2,1)S(1)}, bf16[2,4096]{1,0:T(2,128)(2,1)S(1)}, u32[]{:S(2)}, u32[]{:S(2)}) collective-permute-start(bf16[2,4096]{1,0:T(2,128)(2,1)S(1)} %get-tuple-element.47), channel_id=1, source_target_pairs={{0,4},{4,0},{8,12},{12,8},{1,5},{5,1},{9,13},{13,9},{2,6},{6,2},{1... | collective-permute-start | bytes 49160 | tf_op jit(solution)/shard_map/ppermute | solution.py:242

commit v10 on v9

--- a/solution.py
+++ b/solution.py
@@ -73,20 +73,21 @@
         block_ref[start + r * slots : start + (r + 1) * slots] = cache_ref[r, :, pl.ds(at, cols)]
 
 
-def write_lengths(rows, lengths_ref, block_ref):
+def write_lengths(rows, lengths_ref, block_ref, end):
     at_row = lax.broadcasted_iota(jnp.int32, (16, block_ref.shape[1]), 0)
     filled = jnp.zeros(at_row.shape, jnp.float32)
     for r in range(rows):
         filled = jnp.where(at_row == r, lengths_ref[r].astype(jnp.float32), filled)
-    block_ref[block_ref.shape[0] - 16 :] = filled.astype(jnp.bfloat16)
-
-
-def cut_kernel(side, lengths_ref, keys_ref, values_ref, _, *blocks):
+    block_ref[end - 16 : end] = filled.astype(jnp.bfloat16)
+
+
+def cut_kernel(side, lengths_ref, keys_ref, values_ref, _, block_ref):
     rows, slots, _ = keys_ref.shape
-    for s, block in enumerate(blocks):
-        write_heads(keys_ref, block, 0, own_place() ^ (2 * s + side))
-        write_heads(values_ref, block, rows * slots, own_place() ^ (2 * s + side))
-        write_lengths(rows, lengths_ref, block)
+    size = 2 * rows * slots + 16
+    for s in range(block_ref.shape[0] // size):
+        write_heads(keys_ref, block_ref, s * size, own_place() ^ (2 * s + side))
+        write_heads(values_ref, block_ref, s * size + rows * slots, own_place() ^ (2 * s + side))
+        write_lengths(rows, lengths_ref, block_ref, (s + 1) * size)
 
 
 def round_kernel(wide, *refs):
@@ -104,12 +105,12 @@
 
 
 def attend_kernel(
-    query_cols, frequency_ref, heads_ref, mine_ref, mate_ref, attended_ref
+    query_cols, block, size, frequency_ref, heads_ref, mine_ref, mate_ref, attended_ref
 ):
     chip, rows, cols = heads_ref.shape
     kv_cols = (cols - query_cols) // 2
     kv_heads, group = kv_cols // HD, query_cols // kv_cols
-    slots = (mine_ref.shape[0] - 16) // (2 * rows)
+    slots = (size - 16) // (2 * rows)
     pairs = chip * rows
     count = pairs * kv_heads
     heads = count * group
@@ -117,9 +118,10 @@
     total = heads_ref[...].reshape(pairs, cols).astype(jnp.float32)
 
     def cached(start):
+        at = block * size + start
         return jnp.concatenate(
             [
-                ref[start + r * slots : start + (r + 1) * slots]
+                ref[at + r * slots : at + (r + 1) * slots]
                 for ref in (mine_ref, mate_ref)
                 for r in range(rows)
             ],
@@ -128,7 +130,7 @@
 
     filled = []
     for ref in (mine_ref, mate_ref):
-        last = ref[ref.shape[0] - 16 :, :HD].astype(jnp.float32)
+        last = ref[(block + 1) * size - 16 : (block + 1) * size, :HD].astype(jnp.float32)
         filled += [last[r : r + 1] for r in range(rows)]
     angles = jnp.concatenate(filled, 0) * frequency_ref[...]
     cosine, sine = jnp.cos(angles), jnp.sin(angles)
@@ -296,20 +298,18 @@
     own_half = swap_blocks(normed, ROW_AXES)
     other_half = swap_pairs(own_half, "gz", 1)
     chips = plane // 2
-    block = jax.ShapeDtypeStruct(
-        (2 * rows * cache_keys.shape[1] + 16, kv_cols), cache_keys.dtype
-    )
+    size = 2 * rows * cache_keys.shape[1] + 16
 
     def cut(side, after):
         return pl.pallas_call(
             functools.partial(cut_kernel, side),
-            out_shape=[block] * chips,
+            out_shape=jax.ShapeDtypeStruct((chips * size, kv_cols), cache_keys.dtype),
             in_specs=[IN_SMEM] + [IN_VMEM] * 3,
-            out_specs=[IN_VMEM] * chips,
+            out_specs=IN_VMEM,
             compiler_params=params(8),
         )(lengths, cache_keys, cache_values, after)
 
-    mates = [swap_plane(value, 1) for value in cut(1, normed)]
+    mates = swap_plane(cut(1, normed), 1)
     mine = cut(0, own_half)
     weights = (query_weight, key_weight, value_weight)
     half_cost = cost(owners * rows * width * cols, width * cols)
@@ -345,7 +345,7 @@
     attended = []
     for s in range(chips):
         chip_rows = pl.pallas_call(
-            functools.partial(attend_kernel, query_cols),
+            functools.partial(attend_kernel, query_cols, s, size),
             out_shape=jax.ShapeDtypeStruct((2, rows, query_cols), jnp.bfloat16),
             in_specs=[IN_VMEM] * 4,
             out_specs=IN_VMEM,
@@ -354,8 +354,8 @@
         )(
             jnp.asarray(frequency),
             swap_plane(heads[s], 2 * s) if s else heads[s],
-            mine[s],
-            mates[s],
+            mine,
+            mates,
         )
         attended.append(swap_plane(chip_rows, 2 * s) if s else chip_rows)
     attended = pl.pallas_call(

time: 78.8 us -> 64.1 us (0.81)
  blocking collectives: 0 us -> 15 us
  local copies, waits for them, and re-layouts: 13 us -> 1.3 us
  starting transfers between devices: 23.9 us -> 16.5 us
  waiting for transfers between devices: 26.4 us -> 19.9 us
  Pallas kernels: 15 us -> 11.1 us
    all_to_all x0 -> x1, blocking collectives: none -> 15 us  [swap_blocks(): return lax.all_to_all(blocks, axes, split_axis=0, concat_axis=0, tiled=True)]
    unnamed x32 -> x26, local copies, waits for them, and re-layouts: 13 us -> 1.3 us
    all_to_all x1 -> x0, waiting for transfers between devices: 7.52 us -> none  [swap_blocks(): return lax.all_to_all(blocks, axes, split_axis=0, concat_axis=0, tiled=True)]
    all_to_all x1 -> x0, starting transfers between devices: 7.02 us -> none  [swap_blocks(): return lax.all_to_all(blocks, axes, split_axis=0, concat_axis=0, tiled=True)]
    pallas_call x4, Pallas kernels: 6.28 us -> 3.01 us  [the longest x2 1.63 us: shards(): pl.pallas_call(functools.partial(attend_kernel, query_cols, s, size), out...]
    ppermute x8 -> x7, waiting for transfers between devices: 8.78 us -> 9.84 us  [swap_plane(): lax.ppermute(value, PLANE, [(i, i ^ step) for i in range(lax.axis_size(PL...]
    ppermute x8 -> x7, starting transfers between devices: 3.54 us -> 3.16 us  [swap_plane(): lax.ppermute(value, PLANE, [(i, i ^ step) for i in range(lax.axis_size(PL...]
  transfers between devices with their start and end apart: 19 -> 17, of which waited for: 13 -> 12; matrix products, arithmetic and copies ran while one was open for 0% -> 0% of each run, Pallas kernels for 13% -> 11%
where the time goes in v10:
time: 64.1 us; the launch traced here: 64 us
  waiting for transfers between devices  19.9 us (31%)
  starting transfers between devices  16.5 us (26%)
  blocking collectives  15 us (23%)
  Pallas kernels  11.1 us (17%)
  local copies, waits for them, and re-layouts  1.3 us (2%)
    all_to_all x1, blocking collectives, swap_blocks(): return lax.all_to_all(blocks, axes, split_axis=0, concat_axis=0, tiled=True)  15 us
    ppermute x10, starting transfers between devices, swap_pairs(): lax.ppermute(value, axis, [(i, i ^ step) for i in range(lax.axis_size(axi...  13.3 us
    ppermute x10, waiting for transfers between devices, swap_pairs(): lax.ppermute(value, axis, [(i, i ^ step) for i in range(lax.axis_size(axi...  10.1 us
    ppermute x7, waiting for transfers between devices, swap_plane(): lax.ppermute(value, PLANE, [(i, i ^ step) for i in range(lax.axis_size(PL...  9.84 us
    ppermute x7, starting transfers between devices, swap_plane(): lax.ppermute(value, PLANE, [(i, i ^ step) for i in range(lax.axis_size(PL...  3.16 us
    pallas_call x2, Pallas kernels, shards(): pl.pallas_call(functools.partial(output_kernel, p * part_cols, part_cols)...  3.09 us
    pallas_call x1, Pallas kernels, shards(): pl.pallas_call(functools.partial(project_kernel, False, wide, plane), out...  1.97 us
    pallas_call x1, Pallas kernels, shards(): pl.pallas_call(functools.partial(project_kernel, True, wide, plane), out_...  1.89 us
  transfers between devices with their start and end apart: 17, of which 12 were waited for; matrix products, arithmetic and copies ran while one was open for 0% of the time, Pallas kernels for 11%

profile of v10, /device:TPU:0, one launch (start us, length us, event | category | flops | bytes accessed | tf_op | source)
XLA Modules:
  0.0 64.0 jit_solution(14379066667578898086)
XLA Ops:
  0.0 1.0 %copy-done.7 = bf16[2,16384]{1,0:T(2,128)(2,1)S(1)} copy-done((bf16[2,16384]{1,0:T(2,128)(2,1)S(1)}, bf16[2,16384]{1,0:T(2,128)(2,1)}, u32[]{:S(2)}) %copy-start.7) | copy-done | bytes 65560
  1.0 0.2 shard_map.100.scaled_ref
  1.2 0.0 copy-start.1
  1.3 0.0 copy-done.5
  1.3 0.1 shard_map.101._
  1.4 0.0 copy-done.6
  1.4 0.0 copy-done.4
  1.4 0.3 copy-done.3
  1.6 0.7 %shard_map.106 = bf16[2080,256]{1,0:T(8,128)(2,1)S(1)} custom-call(s32[2]{0:T(128)S(1)} %copy-done.6, bf16[2,256,1024]{2,1,0:T(8,128)(2,1)S(1)} %copy-done.3, bf16[2,256,1024]{2,1,0:T(8,128)(2,1)S(1)} %copy-done.4, bf16[16,2,2048]{2,1,0:T(2,128)(2,1)S(1)} %shard_map.101._), custom_call_target="tpu_custom_call" | custom-call | tf_op jit(solution)/shard_map/pallas_call | solution.py:304
  2.3 0.5 collective-permute-start.4
  2.8 15.0 %all_to_all.5.rows_ref._ = bf16[16,2,2048]{2,1,0:T(2,128)(2,1)S(1)} all-to-all(bf16[16,2,2048]{2,1,0:T(2,128)(2,1)S(1)} %shard_map.101._), channel_id=1, replica_groups=mesh['groups'=2,'gx'=4,'gy'=2,'gz'=2] {'gx','gy','gz'}, dimensions={0} | all-to-all | bytes 262144 | tf_op jit(solution)/shard_map/all_to_all | solution.py:240
  17.8 0.0 collective-permute-start
  17.9 0.0 copy-done
  17.9 0.0 copy-done.2
  17.9 0.0 copy-done.1
  17.9 1.9 %shard_map.102.refs_0_ = f32[32,2560]{1,0:T(8,128)S(1)} custom-call(bf16[16,2,2048]{2,1,0:T(2,128)(2,1)S(1)} %all_to_all.5.rows_ref._, bf16[4096,2048]{1,0:T(8,128)(2,1)S(1)} %copy-done, bf16[4096,256]{1,0:T(8,128)(2,1)S(1)} %copy-done.1, bf16[4096,256]{1,0:T(8,128)(2,1)S(1)} %copy-done.2), custom_call_target="tpu_custom_call" | custom-call | flops 335544320 | bytes 10485760 | tf_op jit(solution)/shard_map/pallas_call | solution.py:316
  19.8 0.0 collective-permute-done.rows_ref
  19.8 0.0 slice-start
  19.8 0.0 slice-start.1
  19.8 0.0 slice-start.2
  19.8 2.0 %shard_map.103 = (f32[4,2,2560]{2,1,0:T(2,128)S(1)}, f32[4,2,2560]{2,1,0:T(2,128)S(1)}, f32[4,2,2560]{2,1,0:T(2,128)S(1)}, f32[4,2,2560]{2,1,0:T(2,128)S(1)}) custom-call(bf16[16,2,2048]{2,1,0:T(2,128)(2,1)S(1)} %collective-permute-done.rows_ref, bf16[4096,2048]{1,0:T(8,128)(2,1)S(1)} %copy-done, bf16[4096,256]{1,0:T(8,128)(2,1)S(1)} %copy-done.1, ...), custom_call_target="tpu_custom_call" | custom-call | flops 335544320 | bytes 10485760 | tf_op jit(solution)/shard_map/pallas_call | solution.py:324
  21.8 0.0 copy-start.8
  21.8 1.0 %collective-permute-start.1 = (f32[4,2,2560]{2,1,0:T(2,128)S(1)}, f32[4,2,2560]{2,1,0:T(2,128)S(1)}, u32[]{:S(2)}, u32[]{:S(2)}) collective-permute-start(f32[4,2,2560]{2,1,0:T(2,128)S(1)} %get-tuple-element.23), channel_id=1, source_target_pairs={{0,12},{4,8},{8,4},{12,0},{1,13},{5,9},{9,5},{13,1},{2,14},{6,10},... | collective-permute-start | bytes 245768 | tf_op jit(solution)/shard_map/ppermute | solution.py:244
  22.8 0.6 collective-permute-start.2
  23.3 2.9 %collective-permute-start.3 = (f32[4,2,2560]{2,1,0:T(2,128)S(1)}, f32[4,2,2560]{2,1,0:T(2,128)S(1)}, u32[]{:S(2)}, u32[]{:S(2)}) collective-permute-start(f32[4,2,2560]{2,1,0:T(2,128)S(1)} %get-tuple-element.25), channel_id=1, source_target_pairs={{0,4},{4,0},{8,12},{12,8},{1,5},{5,1},{9,13},{13,9},{2,6},{6,2},{1... | collective-permute-start | bytes 245768 | tf_op jit(solution)/shard_map/ppermute | solution.py:244
  26.2 2.7 %collective-permute-done.1.refs_0_ = f32[4,2,2560]{2,1,0:T(2,128)S(1)} collective-permute-done((f32[4,2,2560]{2,1,0:T(2,128)S(1)}, f32[4,2,2560]{2,1,0:T(2,128)S(1)}, u32[]{:S(2)}, u32[]{:S(2)}) %collective-permute-start.1) | collective-permute-done | bytes 81952 | tf_op jit(solution)/shard_map/ppermute | solution.py:244
  29.0 2.6 %collective-permute-done.2.refs_1_ = f32[4,2,2560]{2,1,0:T(2,128)S(1)} collective-permute-done((f32[4,2,2560]{2,1,0:T(2,128)S(1)}, f32[4,2,2560]{2,1,0:T(2,128)S(1)}, u32[]{:S(2)}, u32[]{:S(2)}) %collective-permute-start.2) | collective-permute-done | bytes 81952 | tf_op jit(solution)/shard_map/ppermute | solution.py:244
  31.6 0.0 collective-permute-done.3.refs_2_
  31.6 0.0 slice-start.3
  31.6 0.3 collective-permute-start.5
  31.9 0.7 %shard_map.105.mine_ref = bf16[2080,256]{1,0:T(8,128)(2,1)S(1)} custom-call(s32[2]{0:T(128)S(1)} %copy-done.6, bf16[2,256,1024]{2,1,0:T(8,128)(2,1)S(1)} %copy-done.3, bf16[2,256,1024]{2,1,0:T(8,128)(2,1)S(1)} %copy-done.4, bf16[16,2,2048]{2,1,0:T(2,128)(2,1)S(1)} %all_to_all.5.rows_ref._), custom_call_target="tpu_custom_call" | custom-call | tf_op jit(solution)/shard_map/pallas_call | solution.py:304
  32.6 2.9 %collective-permute-done.5.heads_ref = bf16[2,2,2560]{2,1,0:T(2,128)(2,1)S(1)} collective-permute-done((bf16[2,2,2560]{2,1,0:T(2,128)(2,1)S(1)}, bf16[2,2,2560]{2,1,0:T(2,128)(2,1)S(1)}, u32[]{:S(2)}, u32[]{:S(2)}) %collective-permute-start.5) | collective-permute-done | bytes 20512 | tf_op jit(solution)/shard_map/ppermute | solution.py:248
  35.5 0.0 collective-permute-done.4.mate_ref
  35.5 0.0 copy-done.8
  35.5 0.8 %shard_map.108 = bf16[2,2,2048]{2,1,0:T(2,128)(2,1)S(1)} custom-call(f32[1,128]{1,0:T(1,128)S(1)} %copy-done.8, bf16[2,2,2560]{2,1,0:T(2,128)(2,1)S(1)} %collective-permute-done.5.heads_ref, bf16[2080,256]{1,0:T(8,128)(2,1)S(1)} %shard_map.105.mine_ref, bf16[2080,256]{1,0:T(8,128)(2,1)S(1)} %collective-permute-done.4.mate_ref), custom_call_target="tpu_custom_call" | custom-call | flops 1000000000 | bytes 2097152 | tf_op jit(solution)/shard_map/pallas_call | solution.py:347
  36.3 0.3 collective-permute-start.6
  36.6 0.8 %shard_map.107.refs_0_ = bf16[2,2,2048]{2,1,0:T(2,128)(2,1)S(1)} custom-call(f32[1,128]{1,0:T(1,128)S(1)} %copy-done.8, bf16[2,2,2560]{2,1,0:T(2,128)(2,1)S(1)} %get-tuple-element.27.heads_ref, bf16[2080,256]{1,0:T(8,128)(2,1)S(1)} %shard_map.105.mine_ref, bf16[2080,256]{1,0:T(8,128)(2,1)S(1)} %collective-permute-done.4.mate_ref), custom_call_target="tpu_custom_call" | custom-call | flops 1000000000 | bytes 2097152 | tf_op jit(solution)/shard_map/pallas_call | solution.py:347
  37.4 2.7 %collective-permute-done.6.refs_1_ = bf16[2,2,2048]{2,1,0:T(2,128)(2,1)S(1)} collective-permute-done((bf16[2,2,2048]{2,1,0:T(2,128)(2,1)S(1)}, bf16[2,2,2048]{2,1,0:T(2,128)(2,1)S(1)}, u32[]{:S(2)}, u32[]{:S(2)}) %collective-permute-start.6) | collective-permute-done | bytes 16416 | tf_op jit(solution)/shard_map/ppermute | solution.py:248
  40.1 1.7 %collective-permute-start.9 = (bf16[4,2,2048]{2,1,0:T(2,128)(2,1)S(1)}, bf16[4,2,2048]{2,1,0:T(2,128)(2,1)S(1)}, u32[]{:S(2)}, u32[]{:S(2)}) collective-permute-start(bf16[4,2,2048]{2,1,0:T(2,128)(2,1)S(1)} %shard_map.109.refs_0_), channel_id=1, source_target_pairs={{0,12},{4,8},{8,4},{12,0},{1,13},{5,9},{9,5},{13,1},{2,14},{6,10},... | collective-permute-start | bytes 98312 | tf_op jit(solution)/shard_map/ppermute | solution.py:244
  41.8 0.0 collective-permute-start.8
  41.9 2.6 %collective-permute-start.7 = (bf16[4,2,2048]{2,1,0:T(2,128)(2,1)S(1)}, bf16[4,2,2048]{2,1,0:T(2,128)(2,1)S(1)}, u32[]{:S(2)}, u32[]{:S(2)}) collective-permute-start(bf16[4,2,2048]{2,1,0:T(2,128)(2,1)S(1)} %shard_map.109.refs_0_), channel_id=1, source_target_pairs={{0,4},{4,0},{8,12},{12,8},{1,5},{5,1},{9,13},{13,9},{2,6},{6,2},{1... | collective-permute-start | bytes 98312 | tf_op jit(solution)/shard_map/ppermute | solution.py:244
  44.5 1.3 %collective-permute-done.9.refs_3_ = bf16[4,2,2048]{2,1,0:T(2,128)(2,1)S(1)} collective-permute-done((bf16[4,2,2048]{2,1,0:T(2,128)(2,1)S(1)}, bf16[4,2,2048]{2,1,0:T(2,128)(2,1)S(1)}, u32[]{:S(2)}, u32[]{:S(2)}) %collective-permute-start.9) | collective-permute-done | bytes 32800 | tf_op jit(solution)/shard_map/ppermute | solution.py:244
  45.8 0.9 %collective-permute-done.8.refs_2_ = bf16[4,2,2048]{2,1,0:T(2,128)(2,1)S(1)} collective-permute-done((bf16[4,2,2048]{2,1,0:T(2,128)(2,1)S(1)}, bf16[4,2,2048]{2,1,0:T(2,128)(2,1)S(1)}, u32[]{:S(2)}, u32[]{:S(2)}) %collective-permute-start.8) | collective-permute-done | bytes 32800 | tf_op jit(solution)/shard_map/ppermute | solution.py:244
  46.7 0.0 collective-permute-done.7.refs_1_
  46.7 0.0 slice-done
  46.7 0.0 slice-done.1
  46.8 1.5 %shard_map.110 = (f32[8,2,2048]{2,1,0:T(2,128)S(1)}, f32[8,2,2048]{2,1,0:T(2,128)S(1)}) custom-call(bf16[2048,4096]{1,0:T(8,128)(2,1)S(1)} %bitcast.2, bf16[4,2,2048]{2,1,0:T(2,128)(2,1)S(1)} %shard_map.109.refs_0_, bf16[4,2,2048]{2,1,0:T(2,128)(2,1)S(1)} %collective-permute-done.7.refs_1_, bf16[4,2,2048]{2,1,0:T(2,128)(2,1)S(1)} %collective-permute-done.8.refs_2_, ...), custom_call_target="tpu_custom_call" | custom-call | flops 268435456 | bytes 8388608 | tf_op jit(solution)/shard_map/pallas_call | solution.py:375
  48.3 0.1 collective-permute-start.10
  48.4 1.5 %shard_map.112 = (f32[8,2,2048]{2,1,0:T(2,128)S(1)}, f32[8,2,2048]{2,1,0:T(2,128)S(1)}) custom-call(bf16[2048,4096]{1,0:T(8,128)(2,1)S(1)} %bitcast.2, bf16[4,2,2048]{2,1,0:T(2,128)(2,1)S(1)} %shard_map.109.refs_0_, bf16[4,2,2048]{2,1,0:T(2,128)(2,1)S(1)} %collective-permute-done.7.refs_1_, bf16[4,2,2048]{2,1,0:T(2,128)(2,1)S(1)} %collective-permute-done.8.refs_2_, ...), custom_call_target="tpu_custom_call" | custom-call | flops 268435456 | bytes 8388608 | tf_op jit(solution)/shard_map/pallas_call | solution.py:375
  50.0 0.6 collective-permute-start.12
  50.5 0.0 collective-permute-done.10.b_ref
  50.6 0.3 collective-permute-start.11
  50.8 0.7 %collective-permute-done.12.b_ref = f32[8,2,2048]{2,1,0:T(2,128)S(1)} collective-permute-done((f32[8,2,2048]{2,1,0:T(2,128)S(1)}, f32[8,2,2048]{2,1,0:T(2,128)S(1)}, u32[]{:S(2)}, u32[]{:S(2)}) %collective-permute-start.12) | collective-permute-done | bytes 131104 | tf_op jit(solution)/shard_map/ppermute | solution.py:248
  51.5 1.2 %collective-permute-start.13 = (f32[4,2,2048]{2,1,0:T(2,128)S(1)}, f32[4,2,2048]{2,1,0:T(2,128)S(1)}, u32[]{:S(2)}, u32[]{:S(2)}) collective-permute-start(f32[4,2,2048]{2,1,0:T(2,128)S(1)} %get-tuple-element.36), channel_id=1, source_target_pairs={{0,2},{1,3},{2,0},{3,1},{4,6},{5,7},{6,4},{7,5},{8,10},{9,11},{10,... | collective-permute-start | bytes 196616 | tf_op jit(solution)/shard_map/ppermute | solution.py:248
  52.7 2.6 %collective-permute-done.11.refs_1_ = f32[4,2,2048]{2,1,0:T(2,128)S(1)} collective-permute-done((f32[4,2,2048]{2,1,0:T(2,128)S(1)}, f32[4,2,2048]{2,1,0:T(2,128)S(1)}, u32[]{:S(2)}, u32[]{:S(2)}) %collective-permute-start.11) | collective-permute-done | bytes 65568 | tf_op jit(solution)/shard_map/ppermute | solution.py:248
  55.3 1.0 %collective-permute-done.13.refs_3_ = f32[4,2,2048]{2,1,0:T(2,128)S(1)} collective-permute-done((f32[4,2,2048]{2,1,0:T(2,128)S(1)}, f32[4,2,2048]{2,1,0:T(2,128)S(1)}, u32[]{:S(2)}, u32[]{:S(2)}) %collective-permute-start.13) | collective-permute-done | bytes 65568 | tf_op jit(solution)/shard_map/ppermute | solution.py:248
  56.3 0.1 shard_map.114
  56.4 2.1 %collective-permute-start.14 = (bf16[2,4096]{1,0:T(2,128)(2,1)S(1)}, bf16[2,4096]{1,0:T(2,128)(2,1)S(1)}, u32[]{:S(2)}, u32[]{:S(2)}) collective-permute-start(bf16[2,4096]{1,0:T(2,128)(2,1)S(1)} %get-tuple-element.37), channel_id=1, source_target_pairs={{0,12},{4,8},{8,4},{12,0},{1,13},{5,9},{9,5},{13,1},{2,14},{6,10},... | collective-permute-start | bytes 49160 | tf_op jit(solution)/shard_map/ppermute | solution.py:244
  58.4 1.1 %collective-permute-start.15 = (bf16[2,4096]{1,0:T(2,128)(2,1)S(1)}, bf16[2,4096]{1,0:T(2,128)(2,1)S(1)}, u32[]{:S(2)}, u32[]{:S(2)}) collective-permute-start(bf16[2,4096]{1,0:T(2,128)(2,1)S(1)} %get-tuple-element.38), channel_id=1, source_target_pairs={{0,8},{4,12},{8,0},{12,4},{1,9},{5,13},{9,1},{13,5},{2,10},{6,14},... | collective-permute-start | bytes 49160 | tf_op jit(solution)/shard_map/ppermute | solution.py:244
  59.5 1.3 %collective-permute-start.16 = (bf16[2,4096]{1,0:T(2,128)(2,1)S(1)}, bf16[2,4096]{1,0:T(2,128)(2,1)S(1)}, u32[]{:S(2)}, u32[]{:S(2)}) collective-permute-start(bf16[2,4096]{1,0:T(2,128)(2,1)S(1)} %get-tuple-element.39), channel_id=1, source_target_pairs={{0,4},{4,0},{8,12},{12,8},{1,5},{5,1},{9,13},{13,9},{2,6},{6,2},{1... | collective-permute-start | bytes 49160 | tf_op jit(solution)/shard_map/ppermute | solution.py:244
  60.8 1.1 %collective-permute-done.14.refs_0_ = bf16[2,4096]{1,0:T(2,128)(2,1)S(1)} collective-permute-done((bf16[2,4096]{1,0:T(2,128)(2,1)S(1)}, bf16[2,4096]{1,0:T(2,128)(2,1)S(1)}, u32[]{:S(2)}, u32[]{:S(2)}) %collective-permute-start.14) | collective-permute-done | bytes 16416 | tf_op jit(solution)/shard_map/ppermute | solution.py:244
  62.0 1.2 %collective-permute-done.15.refs_1_ = bf16[2,4096]{1,0:T(2,128)(2,1)S(1)} collective-permute-done((bf16[2,4096]{1,0:T(2,128)(2,1)S(1)}, bf16[2,4096]{1,0:T(2,128)(2,1)S(1)}, u32[]{:S(2)}, u32[]{:S(2)}) %collective-permute-start.15) | collective-permute-done | bytes 16416 | tf_op jit(solution)/shard_map/ppermute | solution.py:244
  63.2 0.2 collective-permute-done.16.refs_2_
  63.3 0.6 shard_map.115
  (14 shorter events, 0.1 us)
Async XLA Ops:
  0.0 1.3 %copy-start.5 = (f32[16384]{0:T(1024)S(1)}, f32[16384]{0:T(1024)}, u32[]{:S(2)}) copy-start(f32[16384]{0:T(1024)} %param.11) | copy-start | bytes 196612
  0.0 1.4 %copy-start.6 = (s32[2]{0:T(128)S(1)}, s32[2]{0:T(128)}, u32[]{:S(2)}) copy-start(s32[2]{0:T(128)} %lengths_ref.3) | copy-start | bytes 28
  0.0 1.4 %copy-start.4 = (bf16[2,256,1024]{2,1,0:T(8,128)(2,1)S(1)}, bf16[2,256,1024]{2,1,0:T(8,128)(2,1)}, u32[]{:S(2)}) copy-start(bf16[2,256,1024]{2,1,0:T(8,128)(2,1)} %values_ref.3) | copy-start | bytes 3145732
  0.0 1.6 %copy-start.3 = (bf16[2,256,1024]{2,1,0:T(8,128)(2,1)S(1)}, bf16[2,256,1024]{2,1,0:T(8,128)(2,1)}, u32[]{:S(2)}) copy-start(bf16[2,256,1024]{2,1,0:T(8,128)(2,1)} %keys_ref.3) | copy-start | bytes 3145732
  0.0 1.0 %copy-start.7 = (bf16[2,16384]{1,0:T(2,128)(2,1)S(1)}, bf16[2,16384]{1,0:T(2,128)(2,1)}, u32[]{:S(2)}) copy-start(bf16[2,16384]{1,0:T(2,128)(2,1)} %tokens_ref.1) | copy-start | bytes 196612
  1.0 16.9 %copy-start = (bf16[4096,2048]{1,0:T(8,128)(2,1)S(1)}, bf16[4096,2048]{1,0:T(8,128)(2,1)}, u32[]{:S(2)}) copy-start(bf16[4096,2048]{1,0:T(8,128)(2,1)} %query_ref.3) | copy-start | bytes 50331652
  1.0 16.9 %copy-start.2 = (bf16[4096,256]{1,0:T(8,128)(2,1)S(1)}, bf16[4096,256]{1,0:T(8,128)(2,1)}, u32[]{:S(2)}) copy-start(bf16[4096,256]{1,0:T(8,128)(2,1)} %value_ref.3) | copy-start | bytes 6291460
  1.2 16.6 %copy-start.1 = (bf16[4096,256]{1,0:T(8,128)(2,1)S(1)}, bf16[4096,256]{1,0:T(8,128)(2,1)}, u32[]{:S(2)}) copy-start(bf16[4096,256]{1,0:T(8,128)(2,1)} %key_ref.3) | copy-start | bytes 6291460
  2.3 33.2 %collective-permute-start.4 = (bf16[2080,256]{1,0:T(8,128)(2,1)S(1)}, bf16[2080,256]{1,0:T(8,128)(2,1)S(1)}, u32[]{:S(2)}, u32[]{:S(2)}) collective-permute-start(bf16[2080,256]{1,0:T(8,128)(2,1)S(1)} %shard_map.106), channel_id=1, source_target_pairs={{0,1},{1,0},{2,3},{3,2},{4,5},{5,4},{6,7},{7,6},{8,9},{9,8},{10,11... | collective-permute-start | bytes 3194888 | tf_op jit(solution)/shard_map/ppermute | solution.py:248
  17.8 1.9 %collective-permute-start = (bf16[16,2,2048]{2,1,0:T(2,128)(2,1)S(1)}, bf16[16,2,2048]{2,1,0:T(2,128)(2,1)S(1)}, u32[]{:S(2)}, u32[]{:S(2)}) collective-permute-start(bf16[16,2,2048]{2,1,0:T(2,128)(2,1)S(1)} %all_to_all.5.rows_ref._), channel_id=1, source_target_pairs={{0,1},{1,0},{2,3},{3,2},{4,5},{5,4},{6,7},{7,6},{8,9},{9,8},{10,11... | collective-permute-start | bytes 393224 | tf_op jit(solution)/shard_map/ppermute | solution.py:244
  19.8 27.0 %slice-start = ((s8[16777216]{0:T(1024)(128)(4,1)}), s8[4194304]{0:T(1024)(128)(4,1)S(1)}, s32[]{:S(2)}) async-start(s8[16777216]{0:T(1024)(128)(4,1)} %bitcast.1), calls=%async_computation.1 | async-start | bytes 8388608
  19.8 27.0 %slice-start.1 = ((s8[16777216]{0:T(1024)(128)(4,1)}), s8[4194304]{0:T(1024)(128)(4,1)S(1)}, s32[]{:S(2)}) async-start(s8[16777216]{0:T(1024)(128)(4,1)} %bitcast.1), calls=%async_computation.2 | async-start | bytes 8388608
  19.8 27.0 %slice-start.2 = ((s8[16777216]{0:T(1024)(128)(4,1)}), s8[4194304]{0:T(1024)(128)(4,1)S(1)}, s32[]{:S(2)}) async-start(s8[16777216]{0:T(1024)(128)(4,1)} %bitcast.1), calls=%async_computation.3 | async-start | bytes 8388608
  21.8 13.7 %copy-start.8 = (f32[1,128]{1,0:T(1,128)S(1)}, f32[1,128]{1,0:T(1,128)}, u32[]{:S(2)}) copy-start(f32[1,128]{1,0:T(1,128)} %constant.2.clone.frequency_ref) | copy-start | bytes 1540
  21.8 7.2 %collective-permute-start.1 = (f32[4,2,2560]{2,1,0:T(2,128)S(1)}, f32[4,2,2560]{2,1,0:T(2,128)S(1)}, u32[]{:S(2)}, u32[]{:S(2)}) collective-permute-start(f32[4,2,2560]{2,1,0:T(2,128)S(1)} %get-tuple-element.23), channel_id=1, source_target_pairs={{0,12},{4,8},{8,4},{12,0},{1,13},{5,9},{9,5},{13,1},{2,14},{6,10},... | collective-permute-start | bytes 245768 | tf_op jit(solution)/shard_map/ppermute | solution.py:244
  22.8 8.8 %collective-permute-start.2 = (f32[4,2,2560]{2,1,0:T(2,128)S(1)}, f32[4,2,2560]{2,1,0:T(2,128)S(1)}, u32[]{:S(2)}, u32[]{:S(2)}) collective-permute-start(f32[4,2,2560]{2,1,0:T(2,128)S(1)} %get-tuple-element.24), channel_id=1, source_target_pairs={{0,8},{4,12},{8,0},{12,4},{1,9},{5,13},{9,1},{13,5},{2,10},{6,14},... | collective-permute-start | bytes 245768 | tf_op jit(solution)/shard_map/ppermute | solution.py:244
  23.3 8.2 %collective-permute-start.3 = (f32[4,2,2560]{2,1,0:T(2,128)S(1)}, f32[4,2,2560]{2,1,0:T(2,128)S(1)}, u32[]{:S(2)}, u32[]{:S(2)}) collective-permute-start(f32[4,2,2560]{2,1,0:T(2,128)S(1)} %get-tuple-element.25), channel_id=1, source_target_pairs={{0,4},{4,0},{8,12},{12,8},{1,5},{5,1},{9,13},{13,9},{2,6},{6,2},{1... | collective-permute-start | bytes 245768 | tf_op jit(solution)/shard_map/ppermute | solution.py:244
  31.6 15.2 %slice-start.3 = ((s8[16777216]{0:T(1024)(128)(4,1)}), s8[4194304]{0:T(1024)(128)(4,1)S(1)}, s32[]{:S(2)}) async-start(s8[16777216]{0:T(1024)(128)(4,1)} %bitcast.1), calls=%async_computation.4 | async-start | bytes 8388608
  31.6 3.8 %collective-permute-start.5 = (bf16[2,2,2560]{2,1,0:T(2,128)(2,1)S(1)}, bf16[2,2,2560]{2,1,0:T(2,128)(2,1)S(1)}, u32[]{:S(2)}, u32[]{:S(2)}) collective-permute-start(bf16[2,2,2560]{2,1,0:T(2,128)(2,1)S(1)} %get-tuple-element.28), channel_id=1, source_target_pairs={{0,2},{1,3},{2,0},{3,1},{4,6},{5,7},{6,4},{7,5},{8,10},{9,11},{10,... | collective-permute-start | bytes 61448 | tf_op jit(solution)/shard_map/ppermute | solution.py:248
  36.3 3.8 %collective-permute-start.6 = (bf16[2,2,2048]{2,1,0:T(2,128)(2,1)S(1)}, bf16[2,2,2048]{2,1,0:T(2,128)(2,1)S(1)}, u32[]{:S(2)}, u32[]{:S(2)}) collective-permute-start(bf16[2,2,2048]{2,1,0:T(2,128)(2,1)S(1)} %shard_map.108), channel_id=1, source_target_pairs={{0,2},{1,3},{2,0},{3,1},{4,6},{5,7},{6,4},{7,5},{8,10},{9,11},{10,... | collective-permute-start | bytes 49160 | tf_op jit(solution)/shard_map/ppermute | solution.py:248
  40.1 5.7 %collective-permute-start.9 = (bf16[4,2,2048]{2,1,0:T(2,128)(2,1)S(1)}, bf16[4,2,2048]{2,1,0:T(2,128)(2,1)S(1)}, u32[]{:S(2)}, u32[]{:S(2)}) collective-permute-start(bf16[4,2,2048]{2,1,0:T(2,128)(2,1)S(1)} %shard_map.109.refs_0_), channel_id=1, source_target_pairs={{0,12},{4,8},{8,4},{12,0},{1,13},{5,9},{9,5},{13,1},{2,14},{6,10},... | collective-permute-start | bytes 98312 | tf_op jit(solution)/shard_map/ppermute | solution.py:244
  41.8 4.9 %collective-permute-start.8 = (bf16[4,2,2048]{2,1,0:T(2,128)(2,1)S(1)}, bf16[4,2,2048]{2,1,0:T(2,128)(2,1)S(1)}, u32[]{:S(2)}, u32[]{:S(2)}) collective-permute-start(bf16[4,2,2048]{2,1,0:T(2,128)(2,1)S(1)} %shard_map.109.refs_0_), channel_id=1, source_target_pairs={{0,8},{4,12},{8,0},{12,4},{1,9},{5,13},{9,1},{13,5},{2,10},{6,14},... | collective-permute-start | bytes 98312 | tf_op jit(solution)/shard_map/ppermute | solution.py:244
  41.9 4.9 %collective-permute-start.7 = (bf16[4,2,2048]{2,1,0:T(2,128)(2,1)S(1)}, bf16[4,2,2048]{2,1,0:T(2,128)(2,1)S(1)}, u32[]{:S(2)}, u32[]{:S(2)}) collective-permute-start(bf16[4,2,2048]{2,1,0:T(2,128)(2,1)S(1)} %shard_map.109.refs_0_), channel_id=1, source_target_pairs={{0,4},{4,0},{8,12},{12,8},{1,5},{5,1},{9,13},{13,9},{2,6},{6,2},{1... | collective-permute-start | bytes 98312 | tf_op jit(solution)/shard_map/ppermute | solution.py:244
  48.3 2.2 %collective-permute-start.10 = (f32[8,2,2048]{2,1,0:T(2,128)S(1)}, f32[8,2,2048]{2,1,0:T(2,128)S(1)}, u32[]{:S(2)}, u32[]{:S(2)}) collective-permute-start(f32[8,2,2048]{2,1,0:T(2,128)S(1)} %get-tuple-element.30), channel_id=1, source_target_pairs={{0,1},{1,0},{2,3},{3,2},{4,5},{5,4},{6,7},{7,6},{8,9},{9,8},{10,11... | collective-permute-start | bytes 393224 | tf_op jit(solution)/shard_map/ppermute | solution.py:248
  50.0 1.5 %collective-permute-start.12 = (f32[8,2,2048]{2,1,0:T(2,128)S(1)}, f32[8,2,2048]{2,1,0:T(2,128)S(1)}, u32[]{:S(2)}, u32[]{:S(2)}) collective-permute-start(f32[8,2,2048]{2,1,0:T(2,128)S(1)} %get-tuple-element.34), channel_id=1, source_target_pairs={{0,1},{1,0},{2,3},{3,2},{4,5},{5,4},{6,7},{7,6},{8,9},{9,8},{10,11... | collective-permute-start | bytes 393224 | tf_op jit(solution)/shard_map/ppermute | solution.py:248
  50.6 4.7 %collective-permute-start.11 = (f32[4,2,2048]{2,1,0:T(2,128)S(1)}, f32[4,2,2048]{2,1,0:T(2,128)S(1)}, u32[]{:S(2)}, u32[]{:S(2)}) collective-permute-start(f32[4,2,2048]{2,1,0:T(2,128)S(1)} %get-tuple-element.32), channel_id=1, source_target_pairs={{0,2},{1,3},{2,0},{3,1},{4,6},{5,7},{6,4},{7,5},{8,10},{9,11},{10,... | collective-permute-start | bytes 196616 | tf_op jit(solution)/shard_map/ppermute | solution.py:248
  51.5 4.8 %collective-permute-start.13 = (f32[4,2,2048]{2,1,0:T(2,128)S(1)}, f32[4,2,2048]{2,1,0:T(2,128)S(1)}, u32[]{:S(2)}, u32[]{:S(2)}) collective-permute-start(f32[4,2,2048]{2,1,0:T(2,128)S(1)} %get-tuple-element.36), channel_id=1, source_target_pairs={{0,2},{1,3},{2,0},{3,1},{4,6},{5,7},{6,4},{7,5},{8,10},{9,11},{10,... | collective-permute-start | bytes 196616 | tf_op jit(solution)/shard_map/ppermute | solution.py:248
  56.4 5.6 %collective-permute-start.14 = (bf16[2,4096]{1,0:T(2,128)(2,1)S(1)}, bf16[2,4096]{1,0:T(2,128)(2,1)S(1)}, u32[]{:S(2)}, u32[]{:S(2)}) collective-permute-start(bf16[2,4096]{1,0:T(2,128)(2,1)S(1)} %get-tuple-element.37), channel_id=1, source_target_pairs={{0,12},{4,8},{8,4},{12,0},{1,13},{5,9},{9,5},{13,1},{2,14},{6,10},... | collective-permute-start | bytes 49160 | tf_op jit(solution)/shard_map/ppermute | solution.py:244
  58.4 4.7 %collective-permute-start.15 = (bf16[2,4096]{1,0:T(2,128)(2,1)S(1)}, bf16[2,4096]{1,0:T(2,128)(2,1)S(1)}, u32[]{:S(2)}, u32[]{:S(2)}) collective-permute-start(bf16[2,4096]{1,0:T(2,128)(2,1)S(1)} %get-tuple-element.38), channel_id=1, source_target_pairs={{0,8},{4,12},{8,0},{12,4},{1,9},{5,13},{9,1},{13,5},{2,10},{6,14},... | collective-permute-start | bytes 49160 | tf_op jit(solution)/shard_map/ppermute | solution.py:244
  59.5 3.8 %collective-permute-start.16 = (bf16[2,4096]{1,0:T(2,128)(2,1)S(1)}, bf16[2,4096]{1,0:T(2,128)(2,1)S(1)}, u32[]{:S(2)}, u32[]{:S(2)}) collective-permute-start(bf16[2,4096]{1,0:T(2,128)(2,1)S(1)} %get-tuple-element.39), channel_id=1, source_target_pairs={{0,4},{4,0},{8,12},{12,8},{1,5},{5,1},{9,13},{13,9},{2,6},{6,2},{1... | collective-permute-start | bytes 49160 | tf_op jit(solution)/shard_map/ppermute | solution.py:244

commit v11 on v8

--- a/solution.py
+++ b/solution.py
@@ -13,7 +13,7 @@
 PLANE = ("gy", "gz")
 MIB = 1024 * 1024
 IN_VMEM = pl.BlockSpec(memory_space=pltpu.VMEM)
-IN_SMEM = pl.BlockSpec(memory_space=pltpu.SMEM)
+ANYWHERE = pl.BlockSpec(memory_space=pl.ANY)
 
 
 def scale_kernel(tokens_ref, scaled_ref):
@@ -77,34 +77,31 @@
     at_row = lax.broadcasted_iota(jnp.int32, (16, block_ref.shape[1]), 0)
     filled = jnp.zeros(at_row.shape, jnp.float32)
     for r in range(rows):
-        filled = jnp.where(at_row == r, lengths_ref[r].astype(jnp.float32), filled)
+        filled = jnp.where(at_row == r, lengths_ref[:, r : r + 1].astype(jnp.float32), filled)
     block_ref[block_ref.shape[0] - 16 :] = filled.astype(jnp.bfloat16)
 
 
-def first_kernel(lengths_ref, keys_ref, _, *blocks):
-    for s, block in enumerate(blocks):
-        write_heads(keys_ref, block, 0, own_place() ^ (2 * s + 2))
-        write_lengths(keys_ref.shape[0], lengths_ref, block)
-
-
-def rest_kernel(even, lengths_ref, keys_ref, values_ref, _, *refs):
+def cut_kernel(plan, lengths_ref, keys_ref, values_ref, _, *blocks):
     rows, slots, _ = keys_ref.shape
-    blocks, count = refs[even:], even
-    for s, block in enumerate(blocks[:count]):
-        write_heads(values_ref, block, 0, own_place() ^ (2 * s + 2))
-    for s, block in enumerate(blocks[count:]):
-        write_heads(keys_ref, block, 0, own_place() ^ (2 * s + 1))
-        write_heads(values_ref, block, rows * slots, own_place() ^ (2 * s + 1))
-        write_lengths(rows, lengths_ref, block)
-
-
-def attend_kernel(
-    wide, plane, query_cols, lengths_ref, keys_ref, values_ref, frequency_ref, *refs
-):
+    for (slot, parts), block in zip(plan, blocks):
+        start = 0
+        for part, cache in (("k", keys_ref), ("v", values_ref)):
+            if part in parts:
+                write_heads(cache, block, start, own_place() ^ slot)
+                start += rows * slots
+        if "n" in parts:
+            write_lengths(rows, lengths_ref, block)
+
+
+def pass_kernel(*refs):
+    pass
+
+
+def attend_kernel(wide, plane, rows, query_cols, frequency_ref, *refs):
     partials, held, attended_ref = refs[wide - 1 :: -1], refs[wide:-1], refs[-1]
     even = plane // 2 - 1
-    even_keys, even_values, odd = held[:even], held[even : 2 * even], held[2 * even :]
-    rows, slots, _ = keys_ref.shape
+    split_keys, split_values, whole = held[:even], held[even : 2 * even], held[2 * even :]
+    slots = (whole[0].shape[0] - 16) // (2 * rows)
     cols = partials[0].shape[-1]
     kv_cols = (cols - query_cols) // 2
     kv_heads, group = kv_cols // HD, query_cols // kv_cols
@@ -116,24 +113,21 @@
     for k in range(1, wide):
         total = total + partials[k][...]
     total = total.reshape(pairs, cols).astype(jnp.bfloat16).astype(jnp.float32)
-    own_at = pl.multiple_of(own_place() * kv_cols, kv_cols)
-
-    def cached(cache_ref, even_blocks, start):
+
+    def cached(split, start):
         parts = []
         for p in range(pairs):
             l, r = p // rows, p % rows
-            if l == 0:
-                parts.append(cache_ref[r, :, pl.ds(own_at, kv_cols)])
-            elif l % 2:
+            if l % 2 == 0 and l:
+                parts.append(split[l // 2 - 1][r * slots : (r + 1) * slots])
+            else:
                 at = start + r * slots
-                parts.append(odd[l // 2][at : at + slots])
-            else:
-                parts.append(even_blocks[l // 2 - 1][r * slots : (r + 1) * slots])
+                parts.append(whole[(l + 1) // 2][at : at + slots])
         return jnp.concatenate(parts, 1)
 
-    filled = [jnp.full((1, HD), lengths_ref[r].astype(jnp.float32)) for r in range(rows)]
-    for l in range(1, plane):
-        block = odd[l // 2] if l % 2 else even_keys[l // 2 - 1]
+    filled = []
+    for l in range(plane):
+        block = split_values[l // 2 - 1] if l % 2 == 0 and l else whole[(l + 1) // 2]
         last = block[block.shape[0] - 16 :, :HD].astype(jnp.float32)
         filled += [last[r : r + 1] for r in range(rows)]
     angles = jnp.concatenate(filled, 0) * frequency_ref[...]
@@ -163,7 +157,7 @@
         [jnp.where(head_pair == b, turned_query, jnp.zeros_like(turned_query)) for b in range(count)],
         0,
     )
-    scores = scale * jnp.dot(cached(keys_ref, even_keys, 0), by_pair, preferred_element_type=jnp.float32)
+    scores = scale * jnp.dot(cached(split_keys, 0), by_pair, preferred_element_type=jnp.float32)
     own = scale * jnp.dot(key_new, turned_query, preferred_element_type=jnp.float32)
     of_pair = lax.broadcasted_iota(jnp.int32, (count, 1), 0) == head_pair
     own = jnp.sum(jnp.where(of_pair, own, 0.0), 0, keepdims=True)
@@ -180,7 +174,7 @@
     own_prob = (own_weight / denominator).astype(jnp.bfloat16)
     contract_rows = (((0,), (0,)), ((), ()))
     mixed = lax.dot_general(
-        probability, cached(values_ref, even_values, rows * slots), contract_rows, preferred_element_type=jnp.float32
+        probability, cached(split_values, rows * slots), contract_rows, preferred_element_type=jnp.float32
     )
     own_prob = jnp.where(of_pair, own_prob.astype(jnp.float32), 0.0).astype(jnp.bfloat16)
     fresh = lax.dot_general(
@@ -199,8 +193,8 @@
     attended_ref[...] = attended.reshape(plane, rows, query_cols).astype(jnp.bfloat16)
 
 
-def output_kernel(at, cols, weight_ref, *refs):
-    blocks, keep_ref, give_ref = refs[-3::-1], refs[-2], refs[-1]
+def output_kernel(at, cols, order, weight_ref, *refs):
+    blocks, keep_ref, give_ref = [refs[n] for n in order], refs[-2], refs[-1]
     wide = len(blocks)
     plane, rows, depth = blocks[0].shape
     attended = jnp.concatenate(
@@ -302,29 +296,39 @@
     block_rows = rows * cache_keys.shape[1]
     even = plane // 2 - 1
 
-    def block_of(count):
-        return jax.ShapeDtypeStruct((count, kv_cols), jnp.bfloat16)
-
-    keys = pl.pallas_call(
-        first_kernel,
-        out_shape=[block_of(block_rows + 16)] * even,
-        in_specs=[IN_SMEM] + [IN_VMEM] * 2,
-        out_specs=[IN_VMEM] * even,
-        compiler_params=params(8),
-    )(lengths, cache_keys, normed)
+    def cut(plan, after):
+        return pl.pallas_call(
+            functools.partial(cut_kernel, plan),
+            out_shape=[
+                jax.ShapeDtypeStruct(
+                    (("k" in parts) * block_rows + ("v" in parts) * block_rows + ("n" in parts) * 16, kv_cols),
+                    cache_keys.dtype,
+                )
+                for _, parts in plan
+            ],
+            in_specs=[IN_VMEM] * 4,
+            out_specs=[IN_VMEM] * len(plan),
+            compiler_params=params(8),
+        )(lengths.reshape(1, -1), cache_keys, cache_values, after)
+
+    plan = [(l, "k") for l in range(2, plane, 2)] + [(l, "vn") for l in range(2, plane, 2)]
+    plan += [(l, "kvn") for l in range(1, plane, 2)]
+    blocks = cut(plan, normed)
+    keys, rest = blocks[:even], blocks[even:]
     keys = [swap_plane(keys[s], 2 * s + 2) for s in range(even)]
     own_half = swap_blocks(normed, ROW_AXES)
     other_half = swap_pairs(own_half, "gz", 1)
     rest = pl.pallas_call(
-        functools.partial(rest_kernel, even),
-        out_shape=[block_of(block_rows)] * even + [block_of(2 * block_rows + 16)] * (even + 1),
-        in_specs=[IN_SMEM] + [IN_VMEM] * (3 + even),
-        out_specs=[IN_VMEM] * (2 * even + 1),
-        compiler_params=params(8),
-    )(lengths, cache_keys, cache_values, own_half, *keys)
+        pass_kernel,
+        out_shape=[jax.ShapeDtypeStruct(value.shape, value.dtype) for value in rest],
+        in_specs=[ANYWHERE] * (len(rest) + even + 1),
+        out_specs=[ANYWHERE] * len(rest),
+        input_output_aliases={n: n for n in range(len(rest))},
+    )(*rest, own_half, *keys)
     values = [swap_plane(rest[s], 2 * s + 2) for s in range(even)]
     odd = [swap_plane(rest[even + s], 2 * s + 1) for s in range(even + 1)]
-    held = [*keys, *values, *odd]
+    (mine,) = cut([(0, "kvn")], own_half)
+    held = [*keys, *values, mine, *odd]
     weights = (query_weight, key_weight, value_weight)
     half_cost = cost(owners * rows * width * cols, width * cols)
     partial = pl.pallas_call(
@@ -350,28 +354,29 @@
     frequency = 500000.0 ** (-np.arange(half_dim, dtype=np.float64) / half_dim)
     frequency = np.tile(frequency.astype(np.float32), 2).reshape(1, HD)
     attended = pl.pallas_call(
-        functools.partial(attend_kernel, wide, plane, query_cols),
+        functools.partial(attend_kernel, wide, plane, rows, query_cols),
         out_shape=jax.ShapeDtypeStruct((plane, rows, query_cols), jnp.bfloat16),
-        in_specs=[IN_SMEM] + [IN_VMEM] * (3 + wide + len(held)),
+        in_specs=[IN_VMEM] * (1 + wide + len(held)),
         out_specs=IN_VMEM,
         compiler_params=params(8),
-        cost_estimate=cost(10**9, 4 * MIB),
-    )(lengths, cache_keys, cache_values, jnp.asarray(frequency), *partial[::-1], *held)
+        cost_estimate=cost(10**10, 4 * MIB),
+    )(jnp.asarray(frequency), *partial[::-1], *held)
     head_rows = swap_wide([attended] * wide)
     parts = 2
+    order = [0, *range(wide - 2, 0, -1), wide - 1]
     part_cols = out_cols // parts
     sums = []
     for p in range(parts):
         count = owners // 2
         shape = jax.ShapeDtypeStruct((count, rows, part_cols), jnp.float32)
         keep, give = pl.pallas_call(
-            functools.partial(output_kernel, p * part_cols, part_cols),
+            functools.partial(output_kernel, p * part_cols, part_cols, order),
             out_shape=(shape, shape),
             in_specs=[IN_VMEM] * (1 + wide),
             out_specs=(IN_VMEM, IN_VMEM),
             compiler_params=params(8),
             cost_estimate=cost(2 * owners * rows * depth * part_cols, 2 * depth * part_cols),
-        )(out_weight, *head_rows[::-1])
+        )(out_weight, *[head_rows[k] for k in order])
         give = swap_plane(give, 1)
         step = 2
         while step < plane:

time: 64.6 us -> 73.9 us (1.14)
  local copies, waits for them, and re-layouts: 1.04 us -> 16.4 us
  waiting for transfers between devices: 18.2 us -> 13.9 us
  Pallas kernels: 11 us -> 9.41 us
    unnamed x26 -> x44, local copies, waits for them, and re-layouts: 1.04 us -> 16.4 us
    ppermute x8, waiting for transfers between devices: 13.5 us -> 3.9 us  [swap_plane(): lax.ppermute(value, PLANE, [(i, i ^ step) for i in range(lax.axis_size(PL...]
    ppermute x10, waiting for transfers between devices: 4.74 us -> 9.99 us  [swap_pairs(): lax.ppermute(value, axis, [(i, i ^ step) for i in range(lax.axis_size(axi...]
    pallas_call x5 -> x6, Pallas kernels: 6.06 us -> 4.49 us  [the longest x2 3.09 us: shards(): pl.pallas_call(functools.partial(output_kernel, p * part_cols, part_cols,...]
  transfers between devices with their start and end apart: 18 -> 18, of which waited for: 9 -> 10; matrix products, arithmetic and copies ran while one was open for 0% -> 0% of each run, Pallas kernels for 8% -> 8%
where the time goes in v11:
time: 73.9 us; the launch traced here: 73.6 us
  starting transfers between devices  20.9 us (28%)
  local copies, waits for them, and re-layouts  16.4 us (22%)
  waiting for transfers between devices  13.9 us (19%)
  blocking collectives  12.8 us (17%)
  Pallas kernels  9.41 us (13%)
    unnamed x44, local copies, waits for them, and re-layouts  16.4 us
    ppermute x10, starting transfers between devices, swap_pairs(): lax.ppermute(value, axis, [(i, i ^ step) for i in range(lax.axis_size(axi...  13.4 us
    all_to_all x1, blocking collectives, swap_blocks(): return lax.all_to_all(blocks, axes, split_axis=0, concat_axis=0, tiled=True)  12.8 us
    ppermute x10, waiting for transfers between devices, swap_pairs(): lax.ppermute(value, axis, [(i, i ^ step) for i in range(lax.axis_size(axi...  9.99 us
    ppermute x8, starting transfers between devices, swap_plane(): lax.ppermute(value, PLANE, [(i, i ^ step) for i in range(lax.axis_size(PL...  7.54 us
    ppermute x8, waiting for transfers between devices, swap_plane(): lax.ppermute(value, PLANE, [(i, i ^ step) for i in range(lax.axis_size(PL...  3.9 us
    pallas_call x2, Pallas kernels, shards(): pl.pallas_call(functools.partial(output_kernel, p * part_cols, part_cols,...  3.09 us
    pallas_call x1, Pallas kernels, shards(): pl.pallas_call(functools.partial(project_kernel, False, wide, plane), out...  1.97 us
  transfers between devices with their start and end apart: 18, of which 10 were waited for; matrix products, arithmetic and copies ran while one was open for 0% of the time, Pallas kernels for 8%

profile of v11, /device:TPU:0, one launch (start us, length us, event | category | flops | bytes accessed | tf_op | source)
XLA Modules:
  0.0 73.6 jit_solution(17826606667872867437)
XLA Ops:
  0.0 0.0 copy-start.16
  0.0 1.0 %copy-done.16 = bf16[2,16384]{1,0:T(2,128)(2,1)S(1)} copy-done((bf16[2,16384]{1,0:T(2,128)(2,1)S(1)}, bf16[2,16384]{1,0:T(2,128)(2,1)}, u32[]{:S(2)}) %copy-start.16) | copy-done | bytes 65560
  1.0 0.2 shard_map.100.scaled_ref
  1.2 0.0 copy-done.14
  1.3 0.1 shard_map.101._
  1.3 0.0 copy-done.15
  1.4 0.3 copy-done.5
  1.6 0.2 shard_map.102
  1.9 0.8 %copy-done.9 = bf16[1040,256]{1,0:T(8,128)(2,1)} copy-done((bf16[1040,256]{1,0:T(8,128)(2,1)}, bf16[1040,256]{1,0:T(8,128)(2,1)S(1)}, u32[]{:S(2)}) %copy-start.9) | copy-done | bytes 532504
  2.6 0.8 %copy-done.10 = bf16[1040,256]{1,0:T(8,128)(2,1)} copy-done((bf16[1040,256]{1,0:T(8,128)(2,1)}, bf16[1040,256]{1,0:T(8,128)(2,1)S(1)}, u32[]{:S(2)}) %copy-start.10) | copy-done | bytes 532504
  3.5 0.7 copy-done.11
  4.2 2.9 %collective-permute-start.1 = (bf16[512,256]{1,0:T(8,128)(2,1)S(1)}, bf16[512,256]{1,0:T(8,128)(2,1)S(1)}, u32[]{:S(2)}, u32[]{:S(2)}) collective-permute-start(bf16[512,256]{1,0:T(8,128)(2,1)S(1)} %get-tuple-element.31), channel_id=1, source_target_pairs={{0,2},{1,3},{2,0},{3,1},{4,6},{5,7},{6,4},{7,5},{8,10},{9,11},{10,... | collective-permute-start | bytes 786440 | tf_op jit(solution)/shard_map/ppermute | solution.py:246
  7.1 12.8 %all_to_all.5.refs_3_.rows_ref._ = bf16[16,2,2048]{2,1,0:T(2,128)(2,1)} all-to-all(bf16[16,2,2048]{2,1,0:T(2,128)(2,1)S(1)} %shard_map.101._), channel_id=1, replica_groups=mesh['groups'=2,'gx'=4,'gy'=2,'gz'=2] {'gx','gy','gz'}, dimensions={0} | all-to-all | bytes 262144 | tf_op jit(solution)/shard_map/all_to_all | solution.py:238
  19.9 0.0 collective-permute-done.1.refs_4_
  19.9 0.7 copy-done.12
  20.6 0.0 collective-permute-start.2
  20.6 0.0 collective-permute-start.7
  20.6 2.1 %collective-permute-start.6 = (bf16[528,256]{1,0:T(8,128)(2,1)}, bf16[528,256]{1,0:T(8,128)(2,1)S(1)}, u32[]{:S(2)}, u32[]{:S(2)}) collective-permute-start(bf16[528,256]{1,0:T(8,128)(2,1)} %get-tuple-element.37), channel_id=1, source_target_pairs={{0,2},{1,3},{2,0},{3,1},{4,6},{5,7},{6,4},{7,5},{8,10},{9,11},{10,... | collective-permute-start | bytes 811016 | tf_op jit(solution)/shard_map/ppermute | solution.py:246
  22.8 0.0 collective-permute-start
  22.8 5.8 %copy-done = bf16[4096,2048]{1,0:T(8,128)(2,1)S(1)} copy-done((bf16[4096,2048]{1,0:T(8,128)(2,1)S(1)}, bf16[4096,2048]{1,0:T(8,128)(2,1)}, u32[]{:S(2)}) %copy-start) | copy-done | bytes 16777240
  28.5 1.6 %copy-done.3 = bf16[4096,256]{1,0:T(8,128)(2,1)S(1)} copy-done((bf16[4096,256]{1,0:T(8,128)(2,1)S(1)}, bf16[4096,256]{1,0:T(8,128)(2,1)}, u32[]{:S(2)}) %copy-start.3) | copy-done | bytes 2097176
  30.1 0.9 %copy-done.7 = bf16[16,2,2048]{2,1,0:T(2,128)(2,1)S(1)} copy-done((bf16[16,2,2048]{2,1,0:T(2,128)(2,1)S(1)}, bf16[16,2,2048]{2,1,0:T(2,128)(2,1)}, u32[]{:S(2)}) %copy-start.7) | copy-done | bytes 131096
  31.0 1.9 %shard_map.104.refs_1_ = f32[32,2560]{1,0:T(8,128)S(1)} custom-call(bf16[16,2,2048]{2,1,0:T(2,128)(2,1)S(1)} %copy-done.7, bf16[4096,2048]{1,0:T(8,128)(2,1)S(1)} %copy-done, bf16[4096,256]{1,0:T(8,128)(2,1)S(1)} %copy-done.2, bf16[4096,256]{1,0:T(8,128)(2,1)S(1)} %copy-done.3), custom_call_target="tpu_custom_call" | custom-call | flops 335544320 | bytes 10485760 | tf_op jit(solution)/shard_map/pallas_call | solution.py:334
  32.9 0.0 collective-permute-done.rows_ref
  33.0 0.0 collective-permute-done.2.refs_0_.refs_7_
  33.0 3.8 %copy-done.1 = bf16[4096,2048]{1,0:T(8,128)(2,1)S(1)} copy-done((bf16[4096,2048]{1,0:T(8,128)(2,1)S(1)}, bf16[4096,2048]{1,0:T(8,128)(2,1)}, u32[]{:S(2)}) %copy-start.1) | copy-done | bytes 16777240
  36.8 2.0 %shard_map.105 = (f32[4,2,2560]{2,1,0:T(2,128)S(1)}, f32[4,2,2560]{2,1,0:T(2,128)S(1)}, f32[4,2,2560]{2,1,0:T(2,128)S(1)}, f32[4,2,2560]{2,1,0:T(2,128)S(1)}) custom-call(bf16[16,2,2048]{2,1,0:T(2,128)(2,1)S(1)} %collective-permute-done.rows_ref, bf16[4096,2048]{1,0:T(8,128)(2,1)S(1)} %copy-done.1, bf16[4096,256]{1,0:T(8,128)(2,1)S(1)} %copy-done.2, ...), custom_call_target="tpu_custom_call" | custom-call | flops 335544320 | bytes 10485760 | tf_op jit(solution)/shard_map/pallas_call | solution.py:342
  38.8 0.8 %collective-permute-start.3 = (f32[4,2,2560]{2,1,0:T(2,128)S(1)}, f32[4,2,2560]{2,1,0:T(2,128)S(1)}, u32[]{:S(2)}, u32[]{:S(2)}) collective-permute-start(f32[4,2,2560]{2,1,0:T(2,128)S(1)} %get-tuple-element.33), channel_id=1, source_target_pairs={{0,12},{4,8},{8,4},{12,0},{1,13},{5,9},{9,5},{13,1},{2,14},{6,10},... | collective-permute-start | bytes 245768 | tf_op jit(solution)/shard_map/ppermute | solution.py:242
  39.6 0.5 collective-permute-start.4
  40.1 3.2 %collective-permute-start.5 = (f32[4,2,2560]{2,1,0:T(2,128)S(1)}, f32[4,2,2560]{2,1,0:T(2,128)S(1)}, u32[]{:S(2)}, u32[]{:S(2)}) collective-permute-start(f32[4,2,2560]{2,1,0:T(2,128)S(1)} %get-tuple-element.35), channel_id=1, source_target_pairs={{0,4},{4,0},{8,12},{12,8},{1,5},{5,1},{9,13},{13,9},{2,6},{6,2},{1... | collective-permute-start | bytes 245768 | tf_op jit(solution)/shard_map/ppermute | solution.py:242
  43.2 0.1 shard_map.106.refs_6_
  43.3 0.0 collective-permute-done.6.refs_5_
  43.3 0.0 collective-permute-done.7.refs_8_
  43.4 2.6 %collective-permute-done.3.refs_0_ = f32[4,2,2560]{2,1,0:T(2,128)S(1)} collective-permute-done((f32[4,2,2560]{2,1,0:T(2,128)S(1)}, f32[4,2,2560]{2,1,0:T(2,128)S(1)}, u32[]{:S(2)}, u32[]{:S(2)}) %collective-permute-start.3) | collective-permute-done | bytes 81952 | tf_op jit(solution)/shard_map/ppermute | solution.py:242
  46.0 2.6 %collective-permute-done.4.refs_1_ = f32[4,2,2560]{2,1,0:T(2,128)S(1)} collective-permute-done((f32[4,2,2560]{2,1,0:T(2,128)S(1)}, f32[4,2,2560]{2,1,0:T(2,128)S(1)}, u32[]{:S(2)}, u32[]{:S(2)}) %collective-permute-start.4) | collective-permute-done | bytes 81952 | tf_op jit(solution)/shard_map/ppermute | solution.py:242
  48.6 0.0 collective-permute-done.5.refs_2_
  48.6 0.0 slice-start.1
  48.6 0.0 slice-start.2
  48.6 0.0 slice-start.3
  48.6 1.1 %shard_map.107.refs_0_ = bf16[4,2,2048]{2,1,0:T(2,128)(2,1)S(1)} custom-call(f32[1,128]{1,0:T(1,128)S(1)} %copy-done.17, f32[4,2,2560]{2,1,0:T(2,128)S(1)} %collective-permute-done.3.refs_0_, f32[4,2,2560]{2,1,0:T(2,128)S(1)} %collective-permute-done.4.refs_1_, f32[4,2,2560]{2,1,0:T(2,128)S(1)} %collective-permute-done.5.refs_2_, ...), custom_call_target="tpu_custom_call" | custom-call | flops 10000000000 | bytes 4194304 | tf_op jit(solution)/shard_map/pallas_call | solution.py:356
  49.7 1.8 %collective-permute-start.10 = (bf16[4,2,2048]{2,1,0:T(2,128)(2,1)S(1)}, bf16[4,2,2048]{2,1,0:T(2,128)(2,1)S(1)}, u32[]{:S(2)}, u32[]{:S(2)}) collective-permute-start(bf16[4,2,2048]{2,1,0:T(2,128)(2,1)S(1)} %shard_map.107.refs_0_), channel_id=1, source_target_pairs={{0,12},{4,8},{8,4},{12,0},{1,13},{5,9},{9,5},{13,1},{2,14},{6,10},... | collective-permute-start | bytes 98312 | tf_op jit(solution)/shard_map/ppermute | solution.py:242
  51.5 0.0 collective-permute-start.8
  51.5 2.7 %collective-permute-start.9 = (bf16[4,2,2048]{2,1,0:T(2,128)(2,1)S(1)}, bf16[4,2,2048]{2,1,0:T(2,128)(2,1)S(1)}, u32[]{:S(2)}, u32[]{:S(2)}) collective-permute-start(bf16[4,2,2048]{2,1,0:T(2,128)(2,1)S(1)} %shard_map.107.refs_0_), channel_id=1, source_target_pairs={{0,4},{4,0},{8,12},{12,8},{1,5},{5,1},{9,13},{13,9},{2,6},{6,2},{1... | collective-permute-start | bytes 98312 | tf_op jit(solution)/shard_map/ppermute | solution.py:242
  54.2 1.3 %collective-permute-done.10.refs_3_ = bf16[4,2,2048]{2,1,0:T(2,128)(2,1)S(1)} collective-permute-done((bf16[4,2,2048]{2,1,0:T(2,128)(2,1)S(1)}, bf16[4,2,2048]{2,1,0:T(2,128)(2,1)S(1)}, u32[]{:S(2)}, u32[]{:S(2)}) %collective-permute-start.10) | collective-permute-done | bytes 32800 | tf_op jit(solution)/shard_map/ppermute | solution.py:242
  55.5 0.9 %collective-permute-done.8.refs_1_ = bf16[4,2,2048]{2,1,0:T(2,128)(2,1)S(1)} collective-permute-done((bf16[4,2,2048]{2,1,0:T(2,128)(2,1)S(1)}, bf16[4,2,2048]{2,1,0:T(2,128)(2,1)S(1)}, u32[]{:S(2)}, u32[]{:S(2)}) %collective-permute-start.8) | collective-permute-done | bytes 32800 | tf_op jit(solution)/shard_map/ppermute | solution.py:242
  56.4 0.0 collective-permute-done.9.refs_2_
  56.5 1.5 %shard_map.110 = (f32[8,2,2048]{2,1,0:T(2,128)S(1)}, f32[8,2,2048]{2,1,0:T(2,128)S(1)}) custom-call(bf16[2048,4096]{1,0:T(8,128)(2,1)S(1)} %bitcast.3, bf16[4,2,2048]{2,1,0:T(2,128)(2,1)S(1)} %shard_map.107.refs_0_, bf16[4,2,2048]{2,1,0:T(2,128)(2,1)S(1)} %collective-permute-done.8.refs_1_, bf16[4,2,2048]{2,1,0:T(2,128)(2,1)S(1)} %collective-permute-done.9.refs_2_, ...), custom_call_target="tpu_custom_call" | custom-call | flops 268435456 | bytes 8388608 | tf_op jit(solution)/shard_map/pallas_call | solution.py:372
  58.0 0.1 collective-permute-start.13
  58.1 1.5 %shard_map.108 = (f32[8,2,2048]{2,1,0:T(2,128)S(1)}, f32[8,2,2048]{2,1,0:T(2,128)S(1)}) custom-call(bf16[2048,4096]{1,0:T(8,128)(2,1)S(1)} %bitcast.3, bf16[4,2,2048]{2,1,0:T(2,128)(2,1)S(1)} %shard_map.107.refs_0_, bf16[4,2,2048]{2,1,0:T(2,128)(2,1)S(1)} %collective-permute-done.8.refs_1_, bf16[4,2,2048]{2,1,0:T(2,128)(2,1)S(1)} %collective-permute-done.9.refs_2_, ...), custom_call_target="tpu_custom_call" | custom-call | flops 268435456 | bytes 8388608 | tf_op jit(solution)/shard_map/pallas_call | solution.py:372
  59.6 0.6 collective-permute-start.11
  60.2 0.0 collective-permute-done.13.b_ref
  60.2 0.6 collective-permute-start.14
  60.9 0.3 collective-permute-done.11.b_ref
  61.2 1.2 %collective-permute-start.12 = (f32[4,2,2048]{2,1,0:T(2,128)S(1)}, f32[4,2,2048]{2,1,0:T(2,128)S(1)}, u32[]{:S(2)}, u32[]{:S(2)}) collective-permute-start(f32[4,2,2048]{2,1,0:T(2,128)S(1)} %get-tuple-element.42), channel_id=1, source_target_pairs={{0,2},{1,3},{2,0},{3,1},{4,6},{5,7},{6,4},{7,5},{8,10},{9,11},{10,... | collective-permute-start | bytes 196616 | tf_op jit(solution)/shard_map/ppermute | solution.py:246
  62.4 2.6 %collective-permute-done.14.refs_3_ = f32[4,2,2048]{2,1,0:T(2,128)S(1)} collective-permute-done((f32[4,2,2048]{2,1,0:T(2,128)S(1)}, f32[4,2,2048]{2,1,0:T(2,128)S(1)}, u32[]{:S(2)}, u32[]{:S(2)}) %collective-permute-start.14) | collective-permute-done | bytes 65568 | tf_op jit(solution)/shard_map/ppermute | solution.py:246
  65.0 1.0 %collective-permute-done.12.refs_1_ = f32[4,2,2048]{2,1,0:T(2,128)S(1)} collective-permute-done((f32[4,2,2048]{2,1,0:T(2,128)S(1)}, f32[4,2,2048]{2,1,0:T(2,128)S(1)}, u32[]{:S(2)}, u32[]{:S(2)}) %collective-permute-start.12) | collective-permute-done | bytes 65568 | tf_op jit(solution)/shard_map/ppermute | solution.py:246
  66.0 0.1 shard_map.112
  66.0 2.1 %collective-permute-start.15 = (bf16[2,4096]{1,0:T(2,128)(2,1)S(1)}, bf16[2,4096]{1,0:T(2,128)(2,1)S(1)}, u32[]{:S(2)}, u32[]{:S(2)}) collective-permute-start(bf16[2,4096]{1,0:T(2,128)(2,1)S(1)} %get-tuple-element.47), channel_id=1, source_target_pairs={{0,12},{4,8},{8,4},{12,0},{1,13},{5,9},{9,5},{13,1},{2,14},{6,10},... | collective-permute-start | bytes 49160 | tf_op jit(solution)/shard_map/ppermute | solution.py:242
  68.1 1.1 %collective-permute-start.16 = (bf16[2,4096]{1,0:T(2,128)(2,1)S(1)}, bf16[2,4096]{1,0:T(2,128)(2,1)S(1)}, u32[]{:S(2)}, u32[]{:S(2)}) collective-permute-start(bf16[2,4096]{1,0:T(2,128)(2,1)S(1)} %get-tuple-element.48), channel_id=1, source_target_pairs={{0,8},{4,12},{8,0},{12,4},{1,9},{5,13},{9,1},{13,5},{2,10},{6,14},... | collective-permute-start | bytes 49160 | tf_op jit(solution)/shard_map/ppermute | solution.py:242
  69.2 1.3 %collective-permute-start.17 = (bf16[2,4096]{1,0:T(2,128)(2,1)S(1)}, bf16[2,4096]{1,0:T(2,128)(2,1)S(1)}, u32[]{:S(2)}, u32[]{:S(2)}) collective-permute-start(bf16[2,4096]{1,0:T(2,128)(2,1)S(1)} %get-tuple-element.49), channel_id=1, source_target_pairs={{0,4},{4,0},{8,12},{12,8},{1,5},{5,1},{9,13},{13,9},{2,6},{6,2},{1... | collective-permute-start | bytes 49160 | tf_op jit(solution)/shard_map/ppermute | solution.py:242
  70.5 1.1 %collective-permute-done.15.refs_0_ = bf16[2,4096]{1,0:T(2,128)(2,1)S(1)} collective-permute-done((bf16[2,4096]{1,0:T(2,128)(2,1)S(1)}, bf16[2,4096]{1,0:T(2,128)(2,1)S(1)}, u32[]{:S(2)}, u32[]{:S(2)}) %collective-permute-start.15) | collective-permute-done | bytes 16416 | tf_op jit(solution)/shard_map/ppermute | solution.py:242
  71.6 1.2 %collective-permute-done.16.refs_1_ = bf16[2,4096]{1,0:T(2,128)(2,1)S(1)} collective-permute-done((bf16[2,4096]{1,0:T(2,128)(2,1)S(1)}, bf16[2,4096]{1,0:T(2,128)(2,1)S(1)}, u32[]{:S(2)}, u32[]{:S(2)}) %collective-permute-start.16) | collective-permute-done | bytes 16416 | tf_op jit(solution)/shard_map/ppermute | solution.py:242
  72.8 0.2 collective-permute-done.17.refs_2_
  73.0 0.6 shard_map.113
  (32 shorter events, 0.1 us)
Async XLA Ops:
  0.0 1.2 %copy-start.14 = (f32[16384]{0:T(1024)S(1)}, f32[16384]{0:T(1024)}, u32[]{:S(2)}) copy-start(f32[16384]{0:T(1024)} %param.11) | copy-start | bytes 196612
  0.0 1.3 %copy-start.15 = (s32[2]{0:T(128)S(1)}, s32[2]{0:T(128)}, u32[]{:S(2)}) copy-start(s32[2]{0:T(128)} %param.18) | copy-start | bytes 28
  0.0 1.4 %copy-start.4 = (bf16[2,256,1024]{2,1,0:T(8,128)(2,1)S(1)}, bf16[2,256,1024]{2,1,0:T(8,128)(2,1)}, u32[]{:S(2)}) copy-start(bf16[2,256,1024]{2,1,0:T(8,128)(2,1)} %keys_ref.3) | copy-start | bytes 3145732
  0.0 1.6 %copy-start.5 = (bf16[2,256,1024]{2,1,0:T(8,128)(2,1)S(1)}, bf16[2,256,1024]{2,1,0:T(8,128)(2,1)}, u32[]{:S(2)}) copy-start(bf16[2,256,1024]{2,1,0:T(8,128)(2,1)} %values_ref.3) | copy-start | bytes 3145732
  0.0 22.8 %copy-start.2 = (bf16[4096,256]{1,0:T(8,128)(2,1)S(1)}, bf16[4096,256]{1,0:T(8,128)(2,1)}, u32[]{:S(2)}) copy-start(bf16[4096,256]{1,0:T(8,128)(2,1)} %key_ref.3) | copy-start | bytes 6291460
  0.0 1.0 %copy-start.16 = (bf16[2,16384]{1,0:T(2,128)(2,1)S(1)}, bf16[2,16384]{1,0:T(2,128)(2,1)}, u32[]{:S(2)}) copy-start(bf16[2,16384]{1,0:T(2,128)(2,1)} %tokens_ref.1) | copy-start | bytes 196612
  1.8 0.8 %copy-start.9 = (bf16[1040,256]{1,0:T(8,128)(2,1)}, bf16[1040,256]{1,0:T(8,128)(2,1)S(1)}, u32[]{:S(2)}) copy-start(bf16[1040,256]{1,0:T(8,128)(2,1)S(1)} %get-tuple-element.29.refs_1_) | copy-start | bytes 1597444
  2.6 0.8 %copy-start.10 = (bf16[1040,256]{1,0:T(8,128)(2,1)}, bf16[1040,256]{1,0:T(8,128)(2,1)S(1)}, u32[]{:S(2)}) copy-start(bf16[1040,256]{1,0:T(8,128)(2,1)S(1)} %get-tuple-element.30.refs_2_) | copy-start | bytes 1597444
  3.5 0.7 copy-start.11
  4.2 15.8 %collective-permute-start.1 = (bf16[512,256]{1,0:T(8,128)(2,1)S(1)}, bf16[512,256]{1,0:T(8,128)(2,1)S(1)}, u32[]{:S(2)}, u32[]{:S(2)}) collective-permute-start(bf16[512,256]{1,0:T(8,128)(2,1)S(1)} %get-tuple-element.31), channel_id=1, source_target_pairs={{0,2},{1,3},{2,0},{3,1},{4,6},{5,7},{6,4},{7,5},{8,10},{9,11},{10,... | collective-permute-start | bytes 786440 | tf_op jit(solution)/shard_map/ppermute | solution.py:246
  19.9 0.7 copy-start.12
  20.6 12.3 %collective-permute-start.2 = (bf16[1040,256]{1,0:T(8,128)(2,1)}, bf16[1040,256]{1,0:T(8,128)(2,1)S(1)}, u32[]{:S(2)}, u32[]{:S(2)}) collective-permute-start(bf16[1040,256]{1,0:T(8,128)(2,1)} %get-tuple-element.32), channel_id=1, source_target_pairs={{0,1},{1,0},{2,3},{3,2},{4,5},{5,4},{6,7},{7,6},{8,9},{9,8},{10,11... | collective-permute-start | bytes 1597448 | tf_op jit(solution)/shard_map/ppermute | solution.py:246
  20.6 22.7 %collective-permute-start.7 = (bf16[1040,256]{1,0:T(8,128)(2,1)}, bf16[1040,256]{1,0:T(8,128)(2,1)S(1)}, u32[]{:S(2)}, u32[]{:S(2)}) collective-permute-start(bf16[1040,256]{1,0:T(8,128)(2,1)} %get-tuple-element.38), channel_id=1, source_target_pairs={{0,3},{1,2},{2,1},{3,0},{4,7},{5,6},{6,5},{7,4},{8,11},{9,10},{10,... | collective-permute-start | bytes 1597448 | tf_op jit(solution)/shard_map/ppermute | solution.py:246
  20.6 22.7 %collective-permute-start.6 = (bf16[528,256]{1,0:T(8,128)(2,1)}, bf16[528,256]{1,0:T(8,128)(2,1)S(1)}, u32[]{:S(2)}, u32[]{:S(2)}) collective-permute-start(bf16[528,256]{1,0:T(8,128)(2,1)} %get-tuple-element.37), channel_id=1, source_target_pairs={{0,2},{1,3},{2,0},{3,1},{4,6},{5,7},{6,4},{7,5},{8,10},{9,11},{10,... | collective-permute-start | bytes 811016 | tf_op jit(solution)/shard_map/ppermute | solution.py:246
  22.8 10.2 %collective-permute-start = (bf16[16,2,2048]{2,1,0:T(2,128)(2,1)}, bf16[16,2,2048]{2,1,0:T(2,128)(2,1)S(1)}, u32[]{:S(2)}, u32[]{:S(2)}) collective-permute-start(bf16[16,2,2048]{2,1,0:T(2,128)(2,1)} %all_to_all.5.refs_3_.rows_ref._), channel_id=1, source_target_pairs={{0,1},{1,0},{2,3},{3,2},{4,5},{5,4},{6,7},{7,6},{8,9},{9,8},{10,11... | collective-permute-start | bytes 393224 | tf_op jit(solution)/shard_map/ppermute | solution.py:242
  22.8 5.8 %copy-start = (bf16[4096,2048]{1,0:T(8,128)(2,1)S(1)}, bf16[4096,2048]{1,0:T(8,128)(2,1)}, u32[]{:S(2)}) copy-start(bf16[4096,2048]{1,0:T(8,128)(2,1)} %query_ref.3) | copy-start | bytes 50331652
  28.5 1.6 %copy-start.3 = (bf16[4096,256]{1,0:T(8,128)(2,1)S(1)}, bf16[4096,256]{1,0:T(8,128)(2,1)}, u32[]{:S(2)}) copy-start(bf16[4096,256]{1,0:T(8,128)(2,1)} %value_ref.3) | copy-start | bytes 6291460
  30.1 0.9 %copy-start.7 = (bf16[16,2,2048]{2,1,0:T(2,128)(2,1)S(1)}, bf16[16,2,2048]{2,1,0:T(2,128)(2,1)}, u32[]{:S(2)}) copy-start(bf16[16,2,2048]{2,1,0:T(2,128)(2,1)} %all_to_all.5.refs_3_.rows_ref._) | copy-start | bytes 393220
  31.0 5.8 %copy-start.1 = (bf16[4096,2048]{1,0:T(8,128)(2,1)S(1)}, bf16[4096,2048]{1,0:T(8,128)(2,1)}, u32[]{:S(2)}) copy-start(bf16[4096,2048]{1,0:T(8,128)(2,1)} %query_ref.3) | copy-start | bytes 50331652
  31.0 12.2 %copy-start.6 = (bf16[2,256,1024]{2,1,0:T(8,128)(2,1)S(1)}, bf16[2,256,1024]{2,1,0:T(8,128)(2,1)}, u32[]{:S(2)}) copy-start(bf16[2,256,1024]{2,1,0:T(8,128)(2,1)} %values_ref.3) | copy-start | bytes 3145732
  31.0 12.2 %copy-start.8 = (bf16[16,2,2048]{2,1,0:T(2,128)(2,1)S(1)}, bf16[16,2,2048]{2,1,0:T(2,128)(2,1)}, u32[]{:S(2)}) copy-start(bf16[16,2,2048]{2,1,0:T(2,128)(2,1)} %all_to_all.5.refs_3_.rows_ref._) | copy-start | bytes 393220
  32.9 15.6 %copy-start.13 = (bf16[512,256]{1,0:T(8,128)(2,1)S(1)}, bf16[512,256]{1,0:T(8,128)(2,1)}, u32[]{:S(2)}) copy-start(bf16[512,256]{1,0:T(8,128)(2,1)} %copy-done.12) | copy-start | bytes 786436
  32.9 15.6 %copy-start.17 = (f32[1,128]{1,0:T(1,128)S(1)}, f32[1,128]{1,0:T(1,128)}, u32[]{:S(2)}) copy-start(f32[1,128]{1,0:T(1,128)} %constant.2.clone.frequency_ref) | copy-start | bytes 1540
  38.8 7.2 %collective-permute-start.3 = (f32[4,2,2560]{2,1,0:T(2,128)S(1)}, f32[4,2,2560]{2,1,0:T(2,128)S(1)}, u32[]{:S(2)}, u32[]{:S(2)}) collective-permute-start(f32[4,2,2560]{2,1,0:T(2,128)S(1)} %get-tuple-element.33), channel_id=1, source_target_pairs={{0,12},{4,8},{8,4},{12,0},{1,13},{5,9},{9,5},{13,1},{2,14},{6,10},... | collective-permute-start | bytes 245768 | tf_op jit(solution)/shard_map/ppermute | solution.py:242
  39.6 9.0 %collective-permute-start.4 = (f32[4,2,2560]{2,1,0:T(2,128)S(1)}, f32[4,2,2560]{2,1,0:T(2,128)S(1)}, u32[]{:S(2)}, u32[]{:S(2)}) collective-permute-start(f32[4,2,2560]{2,1,0:T(2,128)S(1)} %get-tuple-element.34), channel_id=1, source_target_pairs={{0,8},{4,12},{8,0},{12,4},{1,9},{5,13},{9,1},{13,5},{2,10},{6,14},... | collective-permute-start | bytes 245768 | tf_op jit(solution)/shard_map/ppermute | solution.py:242
  40.1 8.5 %collective-permute-start.5 = (f32[4,2,2560]{2,1,0:T(2,128)S(1)}, f32[4,2,2560]{2,1,0:T(2,128)S(1)}, u32[]{:S(2)}, u32[]{:S(2)}) collective-permute-start(f32[4,2,2560]{2,1,0:T(2,128)S(1)} %get-tuple-element.35), channel_id=1, source_target_pairs={{0,4},{4,0},{8,12},{12,8},{1,5},{5,1},{9,13},{13,9},{2,6},{6,2},{1... | collective-permute-start | bytes 245768 | tf_op jit(solution)/shard_map/ppermute | solution.py:242
  43.2 13.2 %slice-start = ((s8[16777216]{0:T(1024)(128)(4,1)}), s8[4194304]{0:T(1024)(128)(4,1)S(1)}, s32[]{:S(2)}) async-start(s8[16777216]{0:T(1024)(128)(4,1)} %bitcast.2), calls=%async_computation.1 | async-start | bytes 8388608
  48.6 7.9 %slice-start.1 = ((s8[16777216]{0:T(1024)(128)(4,1)}), s8[4194304]{0:T(1024)(128)(4,1)S(1)}, s32[]{:S(2)}) async-start(s8[16777216]{0:T(1024)(128)(4,1)} %bitcast.2), calls=%async_computation.2 | async-start | bytes 8388608
  48.6 7.8 %slice-start.2 = ((s8[16777216]{0:T(1024)(128)(4,1)}), s8[4194304]{0:T(1024)(128)(4,1)S(1)}, s32[]{:S(2)}) async-start(s8[16777216]{0:T(1024)(128)(4,1)} %bitcast.2), calls=%async_computation.3 | async-start | bytes 8388608
  48.6 7.8 %slice-start.3 = ((s8[16777216]{0:T(1024)(128)(4,1)}), s8[4194304]{0:T(1024)(128)(4,1)S(1)}, s32[]{:S(2)}) async-start(s8[16777216]{0:T(1024)(128)(4,1)} %bitcast.2), calls=%async_computation.4 | async-start | bytes 8388608
  49.7 5.8 %collective-permute-start.10 = (bf16[4,2,2048]{2,1,0:T(2,128)(2,1)S(1)}, bf16[4,2,2048]{2,1,0:T(2,128)(2,1)S(1)}, u32[]{:S(2)}, u32[]{:S(2)}) collective-permute-start(bf16[4,2,2048]{2,1,0:T(2,128)(2,1)S(1)} %shard_map.107.refs_0_), channel_id=1, source_target_pairs={{0,12},{4,8},{8,4},{12,0},{1,13},{5,9},{9,5},{13,1},{2,14},{6,10},... | collective-permute-start | bytes 98312 | tf_op jit(solution)/shard_map/ppermute | solution.py:242
  51.5 4.9 %collective-permute-start.8 = (bf16[4,2,2048]{2,1,0:T(2,128)(2,1)S(1)}, bf16[4,2,2048]{2,1,0:T(2,128)(2,1)S(1)}, u32[]{:S(2)}, u32[]{:S(2)}) collective-permute-start(bf16[4,2,2048]{2,1,0:T(2,128)(2,1)S(1)} %shard_map.107.refs_0_), channel_id=1, source_target_pairs={{0,8},{4,12},{8,0},{12,4},{1,9},{5,13},{9,1},{13,5},{2,10},{6,14},... | collective-permute-start | bytes 98312 | tf_op jit(solution)/shard_map/ppermute | solution.py:242
  51.5 4.9 %collective-permute-start.9 = (bf16[4,2,2048]{2,1,0:T(2,128)(2,1)S(1)}, bf16[4,2,2048]{2,1,0:T(2,128)(2,1)S(1)}, u32[]{:S(2)}, u32[]{:S(2)}) collective-permute-start(bf16[4,2,2048]{2,1,0:T(2,128)(2,1)S(1)} %shard_map.107.refs_0_), channel_id=1, source_target_pairs={{0,4},{4,0},{8,12},{12,8},{1,5},{5,1},{9,13},{13,9},{2,6},{6,2},{1... | collective-permute-start | bytes 98312 | tf_op jit(solution)/shard_map/ppermute | solution.py:242
  58.0 2.2 %collective-permute-start.13 = (f32[8,2,2048]{2,1,0:T(2,128)S(1)}, f32[8,2,2048]{2,1,0:T(2,128)S(1)}, u32[]{:S(2)}, u32[]{:S(2)}) collective-permute-start(f32[8,2,2048]{2,1,0:T(2,128)S(1)} %get-tuple-element.44), channel_id=1, source_target_pairs={{0,1},{1,0},{2,3},{3,2},{4,5},{5,4},{6,7},{7,6},{8,9},{9,8},{10,11... | collective-permute-start | bytes 393224 | tf_op jit(solution)/shard_map/ppermute | solution.py:246
  59.6 1.5 %collective-permute-start.11 = (f32[8,2,2048]{2,1,0:T(2,128)S(1)}, f32[8,2,2048]{2,1,0:T(2,128)S(1)}, u32[]{:S(2)}, u32[]{:S(2)}) collective-permute-start(f32[8,2,2048]{2,1,0:T(2,128)S(1)} %get-tuple-element.40), channel_id=1, source_target_pairs={{0,1},{1,0},{2,3},{3,2},{4,5},{5,4},{6,7},{7,6},{8,9},{9,8},{10,11... | collective-permute-start | bytes 393224 | tf_op jit(solution)/shard_map/ppermute | solution.py:246
  60.2 4.7 %collective-permute-start.14 = (f32[4,2,2048]{2,1,0:T(2,128)S(1)}, f32[4,2,2048]{2,1,0:T(2,128)S(1)}, u32[]{:S(2)}, u32[]{:S(2)}) collective-permute-start(f32[4,2,2048]{2,1,0:T(2,128)S(1)} %get-tuple-element.46), channel_id=1, source_target_pairs={{0,2},{1,3},{2,0},{3,1},{4,6},{5,7},{6,4},{7,5},{8,10},{9,11},{10,... | collective-permute-start | bytes 196616 | tf_op jit(solution)/shard_map/ppermute | solution.py:246
  61.2 4.8 %collective-permute-start.12 = (f32[4,2,2048]{2,1,0:T(2,128)S(1)}, f32[4,2,2048]{2,1,0:T(2,128)S(1)}, u32[]{:S(2)}, u32[]{:S(2)}) collective-permute-start(f32[4,2,2048]{2,1,0:T(2,128)S(1)} %get-tuple-element.42), channel_id=1, source_target_pairs={{0,2},{1,3},{2,0},{3,1},{4,6},{5,7},{6,4},{7,5},{8,10},{9,11},{10,... | collective-permute-start | bytes 196616 | tf_op jit(solution)/shard_map/ppermute | solution.py:246
  66.0 5.6 %collective-permute-start.15 = (bf16[2,4096]{1,0:T(2,128)(2,1)S(1)}, bf16[2,4096]{1,0:T(2,128)(2,1)S(1)}, u32[]{:S(2)}, u32[]{:S(2)}) collective-permute-start(bf16[2,4096]{1,0:T(2,128)(2,1)S(1)} %get-tuple-element.47), channel_id=1, source_target_pairs={{0,12},{4,8},{8,4},{12,0},{1,13},{5,9},{9,5},{13,1},{2,14},{6,10},... | collective-permute-start | bytes 49160 | tf_op jit(solution)/shard_map/ppermute | solution.py:242
  68.1 4.7 %collective-permute-start.16 = (bf16[2,4096]{1,0:T(2,128)(2,1)S(1)}, bf16[2,4096]{1,0:T(2,128)(2,1)S(1)}, u32[]{:S(2)}, u32[]{:S(2)}) collective-permute-start(bf16[2,4096]{1,0:T(2,128)(2,1)S(1)} %get-tuple-element.48), channel_id=1, source_target_pairs={{0,8},{4,12},{8,0},{12,4},{1,9},{5,13},{9,1},{13,5},{2,10},{6,14},... | collective-permute-start | bytes 49160 | tf_op jit(solution)/shard_map/ppermute | solution.py:242
  69.2 3.8 %collective-permute-start.17 = (bf16[2,4096]{1,0:T(2,128)(2,1)S(1)}, bf16[2,4096]{1,0:T(2,128)(2,1)S(1)}, u32[]{:S(2)}, u32[]{:S(2)}) collective-permute-start(bf16[2,4096]{1,0:T(2,128)(2,1)S(1)} %get-tuple-element.49), channel_id=1, source_target_pairs={{0,4},{4,0},{8,12},{12,8},{1,5},{5,1},{9,13},{13,9},{2,6},{6,2},{1... | collective-permute-start | bytes 49160 | tf_op jit(solution)/shard_map/ppermute | solution.py:242

commit v12 on v11

--- a/solution.py
+++ b/solution.py
@@ -324,6 +324,7 @@
         in_specs=[ANYWHERE] * (len(rest) + even + 1),
         out_specs=[ANYWHERE] * len(rest),
         input_output_aliases={n: n for n in range(len(rest))},
+        compiler_params=params(1),
     )(*rest, own_half, *keys)
     values = [swap_plane(rest[s], 2 * s + 2) for s in range(even)]
     odd = [swap_plane(rest[even + s], 2 * s + 1) for s in range(even + 1)]

time: 73.9 us -> 63.3 us (0.86)
  local copies, waits for them, and re-layouts: 16.4 us -> 1.27 us
  waiting for transfers between devices: 13.9 us -> 18.4 us
    unnamed x44 -> x26, local copies, waits for them, and re-layouts: 16.4 us -> 1.27 us
    ppermute x8, waiting for transfers between devices: 3.9 us -> 13.6 us  [swap_plane(): lax.ppermute(value, PLANE, [(i, i ^ step) for i in range(lax.axis_size(PL...]
    ppermute x10, waiting for transfers between devices: 9.99 us -> 4.74 us  [swap_pairs(): lax.ppermute(value, axis, [(i, i ^ step) for i in range(lax.axis_size(axi...]
  transfers between devices with their start and end apart: 18 -> 18, of which waited for: 10 -> 9; matrix products, arithmetic and copies ran while one was open for 0% -> 0% of each run, Pallas kernels for 8% -> 9%
where the time goes in v12:
time: 63.3 us; the launch traced here: 63.1 us
  starting transfers between devices  20.9 us (33%)
  waiting for transfers between devices  18.4 us (29%)
  blocking collectives  13 us (21%)
  Pallas kernels  9.4 us (15%)
  local copies, waits for them, and re-layouts  1.27 us (2%)
    ppermute x8, waiting for transfers between devices, swap_plane(): lax.ppermute(value, PLANE, [(i, i ^ step) for i in range(lax.axis_size(PL...  13.6 us
    ppermute x10, starting transfers between devices, swap_pairs(): lax.ppermute(value, axis, [(i, i ^ step) for i in range(lax.axis_size(axi...  13.4 us
    all_to_all x1, blocking collectives, swap_blocks(): return lax.all_to_all(blocks, axes, split_axis=0, concat_axis=0, tiled=True)  13 us
    ppermute x8, starting transfers between devices, swap_plane(): lax.ppermute(value, PLANE, [(i, i ^ step) for i in range(lax.axis_size(PL...  7.51 us
    ppermute x10, waiting for transfers between devices, swap_pairs(): lax.ppermute(value, axis, [(i, i ^ step) for i in range(lax.axis_size(axi...  4.74 us
    pallas_call x2, Pallas kernels, shards(): pl.pallas_call(functools.partial(output_kernel, p * part_cols, part_cols,...  3.09 us
    pallas_call x1, Pallas kernels, shards(): pl.pallas_call(functools.partial(project_kernel, False, wide, plane), out...  1.97 us
    pallas_call x1, Pallas kernels, shards(): pl.pallas_call(functools.partial(project_kernel, True, wide, plane), out_...  1.9 us
  transfers between devices with their start and end apart: 18, of which 9 were waited for; matrix products, arithmetic and copies ran while one was open for 0% of the time, Pallas kernels for 9%

profile of v12, /device:TPU:0, one launch (start us, length us, event | category | flops | bytes accessed | tf_op | source)
XLA Modules:
  0.0 63.1 jit_solution(5694862281956636498)
XLA Ops:
  0.0 0.0 copy-start.1
  0.0 0.0 copy-start.2
  0.0 0.0 copy-start.7
  0.0 1.0 %copy-done.7 = bf16[2,16384]{1,0:T(2,128)(2,1)S(1)} copy-done((bf16[2,16384]{1,0:T(2,128)(2,1)S(1)}, bf16[2,16384]{1,0:T(2,128)(2,1)}, u32[]{:S(2)}) %copy-start.7) | copy-done | bytes 65560
  1.0 0.2 shard_map.100.scaled_ref
  1.3 0.0 copy-done.5
  1.3 0.1 shard_map.101._
  1.4 0.0 copy-done.6
  1.4 0.0 copy-done.3
  1.4 0.2 copy-done.4
  1.6 0.2 shard_map.102
  1.8 3.0 %collective-permute-start.1 = (bf16[512,256]{1,0:T(8,128)(2,1)S(1)}, bf16[512,256]{1,0:T(8,128)(2,1)S(1)}, u32[]{:S(2)}, u32[]{:S(2)}) collective-permute-start(bf16[512,256]{1,0:T(8,128)(2,1)S(1)} %get-tuple-element.31), channel_id=1, source_target_pairs={{0,2},{1,3},{2,0},{3,1},{4,6},{5,7},{6,4},{7,5},{8,10},{9,11},{10,... | collective-permute-start | bytes 786440 | tf_op jit(solution)/shard_map/ppermute | solution.py:246
  4.9 13.0 %all_to_all.5.refs_3_.rows_ref._ = bf16[16,2,2048]{2,1,0:T(2,128)(2,1)S(1)} all-to-all(bf16[16,2,2048]{2,1,0:T(2,128)(2,1)S(1)} %shard_map.101._), channel_id=1, replica_groups=mesh['groups'=2,'gx'=4,'gy'=2,'gz'=2] {'gx','gy','gz'}, dimensions={0} | all-to-all | bytes 262144 | tf_op jit(solution)/shard_map/all_to_all | solution.py:238
  17.8 0.0 collective-permute-done.1.refs_4_
  17.8 0.0 collective-permute-start.2
  17.8 0.1 collective-permute-start.7
  17.9 2.1 %collective-permute-start.6 = (bf16[528,256]{1,0:T(8,128)(2,1)S(1)}, bf16[528,256]{1,0:T(8,128)(2,1)S(1)}, u32[]{:S(2)}, u32[]{:S(2)}) collective-permute-start(bf16[528,256]{1,0:T(8,128)(2,1)S(1)} %get-tuple-element.37), channel_id=1, source_target_pairs={{0,2},{1,3},{2,0},{3,1},{4,6},{5,7},{6,4},{7,5},{8,10},{9,11},{10,... | collective-permute-start | bytes 811016 | tf_op jit(solution)/shard_map/ppermute | solution.py:246
  20.0 0.0 collective-permute-start
  20.0 0.0 copy-done
  20.0 0.0 copy-done.1
  20.0 0.0 copy-done.2
  20.0 1.9 %shard_map.104.refs_1_ = f32[32,2560]{1,0:T(8,128)S(1)} custom-call(bf16[16,2,2048]{2,1,0:T(2,128)(2,1)S(1)} %all_to_all.5.refs_3_.rows_ref._, bf16[4096,2048]{1,0:T(8,128)(2,1)S(1)} %copy-done, bf16[4096,256]{1,0:T(8,128)(2,1)S(1)} %copy-done.1, bf16[4096,256]{1,0:T(8,128)(2,1)S(1)} %copy-done.2), custom_call_target="tpu_custom_call" | custom-call | flops 335544320 | bytes 10485760 | tf_op jit(solution)/shard_map/pallas_call | solution.py:335
  21.9 0.0 collective-permute-done.rows_ref
  21.9 0.0 collective-permute-done.2.refs_0_.refs_7_
  21.9 2.0 %shard_map.105 = (f32[4,2,2560]{2,1,0:T(2,128)S(1)}, f32[4,2,2560]{2,1,0:T(2,128)S(1)}, f32[4,2,2560]{2,1,0:T(2,128)S(1)}, f32[4,2,2560]{2,1,0:T(2,128)S(1)}) custom-call(bf16[16,2,2048]{2,1,0:T(2,128)(2,1)S(1)} %collective-permute-done.rows_ref, bf16[4096,2048]{1,0:T(8,128)(2,1)S(1)} %copy-done, bf16[4096,256]{1,0:T(8,128)(2,1)S(1)} %copy-done.1, ...), custom_call_target="tpu_custom_call" | custom-call | flops 335544320 | bytes 10485760 | tf_op jit(solution)/shard_map/pallas_call | solution.py:343
  23.9 0.8 %collective-permute-start.3 = (f32[4,2,2560]{2,1,0:T(2,128)S(1)}, f32[4,2,2560]{2,1,0:T(2,128)S(1)}, u32[]{:S(2)}, u32[]{:S(2)}) collective-permute-start(f32[4,2,2560]{2,1,0:T(2,128)S(1)} %get-tuple-element.33), channel_id=1, source_target_pairs={{0,12},{4,8},{8,4},{12,0},{1,13},{5,9},{9,5},{13,1},{2,14},{6,10},... | collective-permute-start | bytes 245768 | tf_op jit(solution)/shard_map/ppermute | solution.py:242
  24.7 0.5 collective-permute-start.4
  25.2 3.2 %collective-permute-start.5 = (f32[4,2,2560]{2,1,0:T(2,128)S(1)}, f32[4,2,2560]{2,1,0:T(2,128)S(1)}, u32[]{:S(2)}, u32[]{:S(2)}) collective-permute-start(f32[4,2,2560]{2,1,0:T(2,128)S(1)} %get-tuple-element.35), channel_id=1, source_target_pairs={{0,4},{4,0},{8,12},{12,8},{1,5},{5,1},{9,13},{13,9},{2,6},{6,2},{1... | collective-permute-start | bytes 245768 | tf_op jit(solution)/shard_map/ppermute | solution.py:242
  28.4 0.1 shard_map.106.refs_6_
  28.4 9.6 %collective-permute-done.6.refs_5_ = bf16[528,256]{1,0:T(8,128)(2,1)S(1)} collective-permute-done((bf16[528,256]{1,0:T(8,128)(2,1)S(1)}, bf16[528,256]{1,0:T(8,128)(2,1)S(1)}, u32[]{:S(2)}, u32[]{:S(2)}) %collective-permute-start.6) | collective-permute-done | bytes 270368 | tf_op jit(solution)/shard_map/ppermute | solution.py:246
  38.1 0.0 collective-permute-done.7.refs_8_
  38.1 0.0 collective-permute-done.3.refs_0_
  38.1 0.0 collective-permute-done.4.refs_1_
  38.1 0.0 collective-permute-done.5.refs_2_
  38.1 0.0 copy-done.8
  38.1 0.0 slice-start.1
  38.1 0.0 slice-start.2
  38.1 0.0 slice-start.3
  38.2 1.1 %shard_map.107.refs_0_ = bf16[4,2,2048]{2,1,0:T(2,128)(2,1)S(1)} custom-call(f32[1,128]{1,0:T(1,128)S(1)} %copy-done.8, f32[4,2,2560]{2,1,0:T(2,128)S(1)} %collective-permute-done.3.refs_0_, f32[4,2,2560]{2,1,0:T(2,128)S(1)} %collective-permute-done.4.refs_1_, f32[4,2,2560]{2,1,0:T(2,128)S(1)} %collective-permute-done.5.refs_2_, ...), custom_call_target="tpu_custom_call" | custom-call | flops 10000000000 | bytes 4194304 | tf_op jit(solution)/shard_map/pallas_call | solution.py:357
  39.3 0.9 %collective-permute-start.10 = (bf16[4,2,2048]{2,1,0:T(2,128)(2,1)S(1)}, bf16[4,2,2048]{2,1,0:T(2,128)(2,1)S(1)}, u32[]{:S(2)}, u32[]{:S(2)}) collective-permute-start(bf16[4,2,2048]{2,1,0:T(2,128)(2,1)S(1)} %shard_map.107.refs_0_), channel_id=1, source_target_pairs={{0,12},{4,8},{8,4},{12,0},{1,13},{5,9},{9,5},{13,1},{2,14},{6,10},... | collective-permute-start | bytes 98312 | tf_op jit(solution)/shard_map/ppermute | solution.py:242
  40.2 0.6 collective-permute-start.8
  40.8 3.0 %collective-permute-start.9 = (bf16[4,2,2048]{2,1,0:T(2,128)(2,1)S(1)}, bf16[4,2,2048]{2,1,0:T(2,128)(2,1)S(1)}, u32[]{:S(2)}, u32[]{:S(2)}) collective-permute-start(bf16[4,2,2048]{2,1,0:T(2,128)(2,1)S(1)} %shard_map.107.refs_0_), channel_id=1, source_target_pairs={{0,4},{4,0},{8,12},{12,8},{1,5},{5,1},{9,13},{13,9},{2,6},{6,2},{1... | collective-permute-start | bytes 98312 | tf_op jit(solution)/shard_map/ppermute | solution.py:242
  43.7 1.4 %collective-permute-done.10.refs_3_ = bf16[4,2,2048]{2,1,0:T(2,128)(2,1)S(1)} collective-permute-done((bf16[4,2,2048]{2,1,0:T(2,128)(2,1)S(1)}, bf16[4,2,2048]{2,1,0:T(2,128)(2,1)S(1)}, u32[]{:S(2)}, u32[]{:S(2)}) %collective-permute-start.10) | collective-permute-done | bytes 32800 | tf_op jit(solution)/shard_map/ppermute | solution.py:242
  45.1 0.7 %collective-permute-done.8.refs_1_ = bf16[4,2,2048]{2,1,0:T(2,128)(2,1)S(1)} collective-permute-done((bf16[4,2,2048]{2,1,0:T(2,128)(2,1)S(1)}, bf16[4,2,2048]{2,1,0:T(2,128)(2,1)S(1)}, u32[]{:S(2)}, u32[]{:S(2)}) %collective-permute-start.8) | collective-permute-done | bytes 32800 | tf_op jit(solution)/shard_map/ppermute | solution.py:242
  45.8 0.0 collective-permute-done.9.refs_2_
  45.8 0.0 slice-done
  45.8 1.5 %shard_map.110 = (f32[8,2,2048]{2,1,0:T(2,128)S(1)}, f32[8,2,2048]{2,1,0:T(2,128)S(1)}) custom-call(bf16[2048,4096]{1,0:T(8,128)(2,1)S(1)} %bitcast.3, bf16[4,2,2048]{2,1,0:T(2,128)(2,1)S(1)} %shard_map.107.refs_0_, bf16[4,2,2048]{2,1,0:T(2,128)(2,1)S(1)} %collective-permute-done.8.refs_1_, bf16[4,2,2048]{2,1,0:T(2,128)(2,1)S(1)} %collective-permute-done.9.refs_2_, ...), custom_call_target="tpu_custom_call" | custom-call | flops 268435456 | bytes 8388608 | tf_op jit(solution)/shard_map/pallas_call | solution.py:373
  47.4 0.1 collective-permute-start.13
  47.5 1.5 %shard_map.108 = (f32[8,2,2048]{2,1,0:T(2,128)S(1)}, f32[8,2,2048]{2,1,0:T(2,128)S(1)}) custom-call(bf16[2048,4096]{1,0:T(8,128)(2,1)S(1)} %bitcast.3, bf16[4,2,2048]{2,1,0:T(2,128)(2,1)S(1)} %shard_map.107.refs_0_, bf16[4,2,2048]{2,1,0:T(2,128)(2,1)S(1)} %collective-permute-done.8.refs_1_, bf16[4,2,2048]{2,1,0:T(2,128)(2,1)S(1)} %collective-permute-done.9.refs_2_, ...), custom_call_target="tpu_custom_call" | custom-call | flops 268435456 | bytes 8388608 | tf_op jit(solution)/shard_map/pallas_call | solution.py:373
  49.0 0.6 collective-permute-start.11
  49.6 0.0 collective-permute-done.13.b_ref
  49.6 0.5 collective-permute-start.14
  50.1 0.4 collective-permute-done.11.b_ref
  50.6 1.2 %collective-permute-start.12 = (f32[4,2,2048]{2,1,0:T(2,128)S(1)}, f32[4,2,2048]{2,1,0:T(2,128)S(1)}, u32[]{:S(2)}, u32[]{:S(2)}) collective-permute-start(f32[4,2,2048]{2,1,0:T(2,128)S(1)} %get-tuple-element.42), channel_id=1, source_target_pairs={{0,2},{1,3},{2,0},{3,1},{4,6},{5,7},{6,4},{7,5},{8,10},{9,11},{10,... | collective-permute-start | bytes 196616 | tf_op jit(solution)/shard_map/ppermute | solution.py:246
  51.8 2.6 %collective-permute-done.14.refs_3_ = f32[4,2,2048]{2,1,0:T(2,128)S(1)} collective-permute-done((f32[4,2,2048]{2,1,0:T(2,128)S(1)}, f32[4,2,2048]{2,1,0:T(2,128)S(1)}, u32[]{:S(2)}, u32[]{:S(2)}) %collective-permute-start.14) | collective-permute-done | bytes 65568 | tf_op jit(solution)/shard_map/ppermute | solution.py:246
  54.3 1.0 %collective-permute-done.12.refs_1_ = f32[4,2,2048]{2,1,0:T(2,128)S(1)} collective-permute-done((f32[4,2,2048]{2,1,0:T(2,128)S(1)}, f32[4,2,2048]{2,1,0:T(2,128)S(1)}, u32[]{:S(2)}, u32[]{:S(2)}) %collective-permute-start.12) | collective-permute-done | bytes 65568 | tf_op jit(solution)/shard_map/ppermute | solution.py:246
  55.3 0.1 shard_map.112
  55.4 2.2 %collective-permute-start.15 = (bf16[2,4096]{1,0:T(2,128)(2,1)S(1)}, bf16[2,4096]{1,0:T(2,128)(2,1)S(1)}, u32[]{:S(2)}, u32[]{:S(2)}) collective-permute-start(bf16[2,4096]{1,0:T(2,128)(2,1)S(1)} %get-tuple-element.47), channel_id=1, source_target_pairs={{0,12},{4,8},{8,4},{12,0},{1,13},{5,9},{9,5},{13,1},{2,14},{6,10},... | collective-permute-start | bytes 49160 | tf_op jit(solution)/shard_map/ppermute | solution.py:242
  57.6 1.1 %collective-permute-start.16 = (bf16[2,4096]{1,0:T(2,128)(2,1)S(1)}, bf16[2,4096]{1,0:T(2,128)(2,1)S(1)}, u32[]{:S(2)}, u32[]{:S(2)}) collective-permute-start(bf16[2,4096]{1,0:T(2,128)(2,1)S(1)} %get-tuple-element.48), channel_id=1, source_target_pairs={{0,8},{4,12},{8,0},{12,4},{1,9},{5,13},{9,1},{13,5},{2,10},{6,14},... | collective-permute-start | bytes 49160 | tf_op jit(solution)/shard_map/ppermute | solution.py:242
  58.8 1.1 %collective-permute-start.17 = (bf16[2,4096]{1,0:T(2,128)(2,1)S(1)}, bf16[2,4096]{1,0:T(2,128)(2,1)S(1)}, u32[]{:S(2)}, u32[]{:S(2)}) collective-permute-start(bf16[2,4096]{1,0:T(2,128)(2,1)S(1)} %get-tuple-element.49), channel_id=1, source_target_pairs={{0,4},{4,0},{8,12},{12,8},{1,5},{5,1},{9,13},{13,9},{2,6},{6,2},{1... | collective-permute-start | bytes 49160 | tf_op jit(solution)/shard_map/ppermute | solution.py:242
  59.9 1.2 %collective-permute-done.15.refs_0_ = bf16[2,4096]{1,0:T(2,128)(2,1)S(1)} collective-permute-done((bf16[2,4096]{1,0:T(2,128)(2,1)S(1)}, bf16[2,4096]{1,0:T(2,128)(2,1)S(1)}, u32[]{:S(2)}, u32[]{:S(2)}) %collective-permute-start.15) | collective-permute-done | bytes 16416 | tf_op jit(solution)/shard_map/ppermute | solution.py:242
  61.0 1.3 %collective-permute-done.16.refs_1_ = bf16[2,4096]{1,0:T(2,128)(2,1)S(1)} collective-permute-done((bf16[2,4096]{1,0:T(2,128)(2,1)S(1)}, bf16[2,4096]{1,0:T(2,128)(2,1)S(1)}, u32[]{:S(2)}, u32[]{:S(2)}) %collective-permute-start.16) | collective-permute-done | bytes 16416 | tf_op jit(solution)/shard_map/ppermute | solution.py:242
  62.3 0.2 collective-permute-done.17.refs_2_
  62.5 0.6 %shard_map.113 = bf16[2,16384]{1,0:T(2,128)(2,1)} custom-call(bf16[2,4096]{1,0:T(2,128)(2,1)S(1)} %collective-permute-done.15.refs_0_, bf16[2,4096]{1,0:T(2,128)(2,1)S(1)} %collective-permute-done.16.refs_1_, bf16[2,4096]{1,0:T(2,128)(2,1)S(1)} %collective-permute-done.17.refs_2_, bf16[2,4096]{1,0:T(2,128)(2,1)S(1)} %get-tuple-element.50.refs_3_), custom_call_target="tpu_custom_call" | custom-call | tf_op jit(solution)/shard_map/pallas_call | solution.py:404
  (14 shorter events, 0.0 us)
Async XLA Ops:
  0.0 1.3 %copy-start.5 = (f32[16384]{0:T(1024)S(1)}, f32[16384]{0:T(1024)}, u32[]{:S(2)}) copy-start(f32[16384]{0:T(1024)} %param.11) | copy-start | bytes 196612
  0.0 1.4 %copy-start.6 = (s32[2]{0:T(128)S(1)}, s32[2]{0:T(128)}, u32[]{:S(2)}) copy-start(s32[2]{0:T(128)} %param.18) | copy-start | bytes 28
  0.0 1.4 %copy-start.3 = (bf16[2,256,1024]{2,1,0:T(8,128)(2,1)S(1)}, bf16[2,256,1024]{2,1,0:T(8,128)(2,1)}, u32[]{:S(2)}) copy-start(bf16[2,256,1024]{2,1,0:T(8,128)(2,1)} %keys_ref.3) | copy-start | bytes 3145732
  0.0 1.6 %copy-start.4 = (bf16[2,256,1024]{2,1,0:T(8,128)(2,1)S(1)}, bf16[2,256,1024]{2,1,0:T(8,128)(2,1)}, u32[]{:S(2)}) copy-start(bf16[2,256,1024]{2,1,0:T(8,128)(2,1)} %values_ref.3) | copy-start | bytes 3145732
  0.0 20.0 %copy-start = (bf16[4096,2048]{1,0:T(8,128)(2,1)S(1)}, bf16[4096,2048]{1,0:T(8,128)(2,1)}, u32[]{:S(2)}) copy-start(bf16[4096,2048]{1,0:T(8,128)(2,1)} %query_ref.3) | copy-start | bytes 50331652
  0.0 20.0 %copy-start.1 = (bf16[4096,256]{1,0:T(8,128)(2,1)S(1)}, bf16[4096,256]{1,0:T(8,128)(2,1)}, u32[]{:S(2)}) copy-start(bf16[4096,256]{1,0:T(8,128)(2,1)} %key_ref.3) | copy-start | bytes 6291460
  0.0 20.0 %copy-start.2 = (bf16[4096,256]{1,0:T(8,128)(2,1)S(1)}, bf16[4096,256]{1,0:T(8,128)(2,1)}, u32[]{:S(2)}) copy-start(bf16[4096,256]{1,0:T(8,128)(2,1)} %value_ref.3) | copy-start | bytes 6291460
  0.0 1.0 %copy-start.7 = (bf16[2,16384]{1,0:T(2,128)(2,1)S(1)}, bf16[2,16384]{1,0:T(2,128)(2,1)}, u32[]{:S(2)}) copy-start(bf16[2,16384]{1,0:T(2,128)(2,1)} %tokens_ref.1) | copy-start | bytes 196612
  1.8 16.0 %collective-permute-start.1 = (bf16[512,256]{1,0:T(8,128)(2,1)S(1)}, bf16[512,256]{1,0:T(8,128)(2,1)S(1)}, u32[]{:S(2)}, u32[]{:S(2)}) collective-permute-start(bf16[512,256]{1,0:T(8,128)(2,1)S(1)} %get-tuple-element.31), channel_id=1, source_target_pairs={{0,2},{1,3},{2,0},{3,1},{4,6},{5,7},{6,4},{7,5},{8,10},{9,11},{10,... | collective-permute-start | bytes 786440 | tf_op jit(solution)/shard_map/ppermute | solution.py:246
  17.8 4.1 %collective-permute-start.2 = (bf16[1040,256]{1,0:T(8,128)(2,1)S(1)}, bf16[1040,256]{1,0:T(8,128)(2,1)S(1)}, u32[]{:S(2)}, u32[]{:S(2)}) collective-permute-start(bf16[1040,256]{1,0:T(8,128)(2,1)S(1)} %get-tuple-element.32), channel_id=1, source_target_pairs={{0,1},{1,0},{2,3},{3,2},{4,5},{5,4},{6,7},{7,6},{8,9},{9,8},{10,11... | collective-permute-start | bytes 1597448 | tf_op jit(solution)/shard_map/ppermute | solution.py:246
  17.8 20.3 %collective-permute-start.7 = (bf16[1040,256]{1,0:T(8,128)(2,1)S(1)}, bf16[1040,256]{1,0:T(8,128)(2,1)S(1)}, u32[]{:S(2)}, u32[]{:S(2)}) collective-permute-start(bf16[1040,256]{1,0:T(8,128)(2,1)S(1)} %get-tuple-element.38), channel_id=1, source_target_pairs={{0,3},{1,2},{2,1},{3,0},{4,7},{5,6},{6,5},{7,4},{8,11},{9,10},{10,... | collective-permute-start | bytes 1597448 | tf_op jit(solution)/shard_map/ppermute | solution.py:246
  17.9 20.2 %collective-permute-start.6 = (bf16[528,256]{1,0:T(8,128)(2,1)S(1)}, bf16[528,256]{1,0:T(8,128)(2,1)S(1)}, u32[]{:S(2)}, u32[]{:S(2)}) collective-permute-start(bf16[528,256]{1,0:T(8,128)(2,1)S(1)} %get-tuple-element.37), channel_id=1, source_target_pairs={{0,2},{1,3},{2,0},{3,1},{4,6},{5,7},{6,4},{7,5},{8,10},{9,11},{10,... | collective-permute-start | bytes 811016 | tf_op jit(solution)/shard_map/ppermute | solution.py:246
  20.0 1.9 %collective-permute-start = (bf16[16,2,2048]{2,1,0:T(2,128)(2,1)S(1)}, bf16[16,2,2048]{2,1,0:T(2,128)(2,1)S(1)}, u32[]{:S(2)}, u32[]{:S(2)}) collective-permute-start(bf16[16,2,2048]{2,1,0:T(2,128)(2,1)S(1)} %all_to_all.5.refs_3_.rows_ref._), channel_id=1, source_target_pairs={{0,1},{1,0},{2,3},{3,2},{4,5},{5,4},{6,7},{7,6},{8,9},{9,8},{10,11... | collective-permute-start | bytes 393224 | tf_op jit(solution)/shard_map/ppermute | solution.py:242
  21.9 16.2 %copy-start.8 = (f32[1,128]{1,0:T(1,128)S(1)}, f32[1,128]{1,0:T(1,128)}, u32[]{:S(2)}) copy-start(f32[1,128]{1,0:T(1,128)} %constant.2.clone.frequency_ref) | copy-start | bytes 1540
  23.9 14.2 %collective-permute-start.3 = (f32[4,2,2560]{2,1,0:T(2,128)S(1)}, f32[4,2,2560]{2,1,0:T(2,128)S(1)}, u32[]{:S(2)}, u32[]{:S(2)}) collective-permute-start(f32[4,2,2560]{2,1,0:T(2,128)S(1)} %get-tuple-element.33), channel_id=1, source_target_pairs={{0,12},{4,8},{8,4},{12,0},{1,13},{5,9},{9,5},{13,1},{2,14},{6,10},... | collective-permute-start | bytes 245768 | tf_op jit(solution)/shard_map/ppermute | solution.py:242
  24.7 13.4 %collective-permute-start.4 = (f32[4,2,2560]{2,1,0:T(2,128)S(1)}, f32[4,2,2560]{2,1,0:T(2,128)S(1)}, u32[]{:S(2)}, u32[]{:S(2)}) collective-permute-start(f32[4,2,2560]{2,1,0:T(2,128)S(1)} %get-tuple-element.34), channel_id=1, source_target_pairs={{0,8},{4,12},{8,0},{12,4},{1,9},{5,13},{9,1},{13,5},{2,10},{6,14},... | collective-permute-start | bytes 245768 | tf_op jit(solution)/shard_map/ppermute | solution.py:242
  25.2 12.9 %collective-permute-start.5 = (f32[4,2,2560]{2,1,0:T(2,128)S(1)}, f32[4,2,2560]{2,1,0:T(2,128)S(1)}, u32[]{:S(2)}, u32[]{:S(2)}) collective-permute-start(f32[4,2,2560]{2,1,0:T(2,128)S(1)} %get-tuple-element.35), channel_id=1, source_target_pairs={{0,4},{4,0},{8,12},{12,8},{1,5},{5,1},{9,13},{13,9},{2,6},{6,2},{1... | collective-permute-start | bytes 245768 | tf_op jit(solution)/shard_map/ppermute | solution.py:242
  28.4 17.5 %slice-start = ((s8[16777216]{0:T(1024)(128)(4,1)}), s8[4194304]{0:T(1024)(128)(4,1)S(1)}, s32[]{:S(2)}) async-start(s8[16777216]{0:T(1024)(128)(4,1)} %bitcast.2), calls=%async_computation.1 | async-start | bytes 8388608
  38.1 7.7 %slice-start.1 = ((s8[16777216]{0:T(1024)(128)(4,1)}), s8[4194304]{0:T(1024)(128)(4,1)S(1)}, s32[]{:S(2)}) async-start(s8[16777216]{0:T(1024)(128)(4,1)} %bitcast.2), calls=%async_computation.2 | async-start | bytes 8388608
  38.1 7.7 %slice-start.2 = ((s8[16777216]{0:T(1024)(128)(4,1)}), s8[4194304]{0:T(1024)(128)(4,1)S(1)}, s32[]{:S(2)}) async-start(s8[16777216]{0:T(1024)(128)(4,1)} %bitcast.2), calls=%async_computation.3 | async-start | bytes 8388608
  38.1 7.7 %slice-start.3 = ((s8[16777216]{0:T(1024)(128)(4,1)}), s8[4194304]{0:T(1024)(128)(4,1)S(1)}, s32[]{:S(2)}) async-start(s8[16777216]{0:T(1024)(128)(4,1)} %bitcast.2), calls=%async_computation.4 | async-start | bytes 8388608
  39.3 5.9 %collective-permute-start.10 = (bf16[4,2,2048]{2,1,0:T(2,128)(2,1)S(1)}, bf16[4,2,2048]{2,1,0:T(2,128)(2,1)S(1)}, u32[]{:S(2)}, u32[]{:S(2)}) collective-permute-start(bf16[4,2,2048]{2,1,0:T(2,128)(2,1)S(1)} %shard_map.107.refs_0_), channel_id=1, source_target_pairs={{0,12},{4,8},{8,4},{12,0},{1,13},{5,9},{9,5},{13,1},{2,14},{6,10},... | collective-permute-start | bytes 98312 | tf_op jit(solution)/shard_map/ppermute | solution.py:242
  40.2 5.6 %collective-permute-start.8 = (bf16[4,2,2048]{2,1,0:T(2,128)(2,1)S(1)}, bf16[4,2,2048]{2,1,0:T(2,128)(2,1)S(1)}, u32[]{:S(2)}, u32[]{:S(2)}) collective-permute-start(bf16[4,2,2048]{2,1,0:T(2,128)(2,1)S(1)} %shard_map.107.refs_0_), channel_id=1, source_target_pairs={{0,8},{4,12},{8,0},{12,4},{1,9},{5,13},{9,1},{13,5},{2,10},{6,14},... | collective-permute-start | bytes 98312 | tf_op jit(solution)/shard_map/ppermute | solution.py:242
  40.8 5.0 %collective-permute-start.9 = (bf16[4,2,2048]{2,1,0:T(2,128)(2,1)S(1)}, bf16[4,2,2048]{2,1,0:T(2,128)(2,1)S(1)}, u32[]{:S(2)}, u32[]{:S(2)}) collective-permute-start(bf16[4,2,2048]{2,1,0:T(2,128)(2,1)S(1)} %shard_map.107.refs_0_), channel_id=1, source_target_pairs={{0,4},{4,0},{8,12},{12,8},{1,5},{5,1},{9,13},{13,9},{2,6},{6,2},{1... | collective-permute-start | bytes 98312 | tf_op jit(solution)/shard_map/ppermute | solution.py:242
  47.4 2.2 %collective-permute-start.13 = (f32[8,2,2048]{2,1,0:T(2,128)S(1)}, f32[8,2,2048]{2,1,0:T(2,128)S(1)}, u32[]{:S(2)}, u32[]{:S(2)}) collective-permute-start(f32[8,2,2048]{2,1,0:T(2,128)S(1)} %get-tuple-element.44), channel_id=1, source_target_pairs={{0,1},{1,0},{2,3},{3,2},{4,5},{5,4},{6,7},{7,6},{8,9},{9,8},{10,11... | collective-permute-start | bytes 393224 | tf_op jit(solution)/shard_map/ppermute | solution.py:246
  49.0 1.5 %collective-permute-start.11 = (f32[8,2,2048]{2,1,0:T(2,128)S(1)}, f32[8,2,2048]{2,1,0:T(2,128)S(1)}, u32[]{:S(2)}, u32[]{:S(2)}) collective-permute-start(f32[8,2,2048]{2,1,0:T(2,128)S(1)} %get-tuple-element.40), channel_id=1, source_target_pairs={{0,1},{1,0},{2,3},{3,2},{4,5},{5,4},{6,7},{7,6},{8,9},{9,8},{10,11... | collective-permute-start | bytes 393224 | tf_op jit(solution)/shard_map/ppermute | solution.py:246
  49.6 4.7 %collective-permute-start.14 = (f32[4,2,2048]{2,1,0:T(2,128)S(1)}, f32[4,2,2048]{2,1,0:T(2,128)S(1)}, u32[]{:S(2)}, u32[]{:S(2)}) collective-permute-start(f32[4,2,2048]{2,1,0:T(2,128)S(1)} %get-tuple-element.46), channel_id=1, source_target_pairs={{0,2},{1,3},{2,0},{3,1},{4,6},{5,7},{6,4},{7,5},{8,10},{9,11},{10,... | collective-permute-start | bytes 196616 | tf_op jit(solution)/shard_map/ppermute | solution.py:246
  50.6 4.8 %collective-permute-start.12 = (f32[4,2,2048]{2,1,0:T(2,128)S(1)}, f32[4,2,2048]{2,1,0:T(2,128)S(1)}, u32[]{:S(2)}, u32[]{:S(2)}) collective-permute-start(f32[4,2,2048]{2,1,0:T(2,128)S(1)} %get-tuple-element.42), channel_id=1, source_target_pairs={{0,2},{1,3},{2,0},{3,1},{4,6},{5,7},{6,4},{7,5},{8,10},{9,11},{10,... | collective-permute-start | bytes 196616 | tf_op jit(solution)/shard_map/ppermute | solution.py:246
  55.4 5.6 %collective-permute-start.15 = (bf16[2,4096]{1,0:T(2,128)(2,1)S(1)}, bf16[2,4096]{1,0:T(2,128)(2,1)S(1)}, u32[]{:S(2)}, u32[]{:S(2)}) collective-permute-start(bf16[2,4096]{1,0:T(2,128)(2,1)S(1)} %get-tuple-element.47), channel_id=1, source_target_pairs={{0,12},{4,8},{8,4},{12,0},{1,13},{5,9},{9,5},{13,1},{2,14},{6,10},... | collective-permute-start | bytes 49160 | tf_op jit(solution)/shard_map/ppermute | solution.py:242
  57.6 4.6 %collective-permute-start.16 = (bf16[2,4096]{1,0:T(2,128)(2,1)S(1)}, bf16[2,4096]{1,0:T(2,128)(2,1)S(1)}, u32[]{:S(2)}, u32[]{:S(2)}) collective-permute-start(bf16[2,4096]{1,0:T(2,128)(2,1)S(1)} %get-tuple-element.48), channel_id=1, source_target_pairs={{0,8},{4,12},{8,0},{12,4},{1,9},{5,13},{9,1},{13,5},{2,10},{6,14},... | collective-permute-start | bytes 49160 | tf_op jit(solution)/shard_map/ppermute | solution.py:242
  58.8 3.7 %collective-permute-start.17 = (bf16[2,4096]{1,0:T(2,128)(2,1)S(1)}, bf16[2,4096]{1,0:T(2,128)(2,1)S(1)}, u32[]{:S(2)}, u32[]{:S(2)}) collective-permute-start(bf16[2,4096]{1,0:T(2,128)(2,1)S(1)} %get-tuple-element.49), channel_id=1, source_target_pairs={{0,4},{4,0},{8,12},{12,8},{1,5},{5,1},{9,13},{13,9},{2,6},{6,2},{1... | collective-permute-start | bytes 49160 | tf_op jit(solution)/shard_map/ppermute | solution.py:242

commit v13 on v12

--- a/solution.py
+++ b/solution.py
@@ -65,14 +65,6 @@
     return 2 * lax.axis_index("gy") + lax.axis_index("gz")
 
 
-def write_heads(cache_ref, block_ref, start, owner):
-    rows, slots, _ = cache_ref.shape
-    cols = block_ref.shape[1]
-    at = pl.multiple_of(owner * cols, cols)
-    for r in range(rows):
-        block_ref[start + r * slots : start + (r + 1) * slots] = cache_ref[r, :, pl.ds(at, cols)]
-
-
 def write_lengths(rows, lengths_ref, block_ref):
     at_row = lax.broadcasted_iota(jnp.int32, (16, block_ref.shape[1]), 0)
     filled = jnp.zeros(at_row.shape, jnp.float32)
@@ -83,13 +75,15 @@
 
 def cut_kernel(plan, lengths_ref, keys_ref, values_ref, _, *blocks):
     rows, slots, _ = keys_ref.shape
-    for (slot, parts), block in zip(plan, blocks):
+    cols = blocks[0].shape[1]
+    for (slot, key_rows, value_rows, with_lengths), block in zip(plan, blocks):
+        at = pl.multiple_of((own_place() ^ slot) * cols, cols)
         start = 0
-        for part, cache in (("k", keys_ref), ("v", values_ref)):
-            if part in parts:
-                write_heads(cache, block, start, own_place() ^ slot)
-                start += rows * slots
-        if "n" in parts:
+        for cache_ref, wanted in ((keys_ref, key_rows), (values_ref, value_rows)):
+            for r in wanted:
+                block[start : start + slots] = cache_ref[r, :, pl.ds(at, cols)]
+                start += slots
+        if with_lengths:
             write_lengths(rows, lengths_ref, block)
 
 
@@ -97,10 +91,10 @@
     pass
 
 
-def attend_kernel(wide, plane, rows, query_cols, frequency_ref, *refs):
+def attend_kernel(wide, plane, rows, early, query_cols, frequency_ref, *refs):
     partials, held, attended_ref = refs[wide - 1 :: -1], refs[wide:-1], refs[-1]
     even = plane // 2 - 1
-    split_keys, split_values, whole = held[:even], held[even : 2 * even], held[2 * even :]
+    firsts, lasts, whole = held[:even], held[even : 2 * even], held[2 * even :]
     slots = (whole[0].shape[0] - 16) // (2 * rows)
     cols = partials[0].shape[-1]
     kv_cols = (cols - query_cols) // 2
@@ -114,20 +108,21 @@
         total = total + partials[k][...]
     total = total.reshape(pairs, cols).astype(jnp.bfloat16).astype(jnp.float32)
 
-    def cached(split, start):
+    def cached(values):
         parts = []
         for p in range(pairs):
             l, r = p // rows, p % rows
+            ref, at = whole[(l + 1) // 2], values * rows + r
             if l % 2 == 0 and l:
-                parts.append(split[l // 2 - 1][r * slots : (r + 1) * slots])
-            else:
-                at = start + r * slots
-                parts.append(whole[(l + 1) // 2][at : at + slots])
+                ref = firsts[l // 2 - 1]
+                if at >= rows + early:
+                    ref, at = lasts[l // 2 - 1], at - rows - early
+            parts.append(ref[at * slots : (at + 1) * slots])
         return jnp.concatenate(parts, 1)
 
     filled = []
     for l in range(plane):
-        block = split_values[l // 2 - 1] if l % 2 == 0 and l else whole[(l + 1) // 2]
+        block = lasts[l // 2 - 1] if l % 2 == 0 and l else whole[(l + 1) // 2]
         last = block[block.shape[0] - 16 :, :HD].astype(jnp.float32)
         filled += [last[r : r + 1] for r in range(rows)]
     angles = jnp.concatenate(filled, 0) * frequency_ref[...]
@@ -157,7 +152,7 @@
         [jnp.where(head_pair == b, turned_query, jnp.zeros_like(turned_query)) for b in range(count)],
         0,
     )
-    scores = scale * jnp.dot(cached(split_keys, 0), by_pair, preferred_element_type=jnp.float32)
+    scores = scale * jnp.dot(cached(0), by_pair, preferred_element_type=jnp.float32)
     own = scale * jnp.dot(key_new, turned_query, preferred_element_type=jnp.float32)
     of_pair = lax.broadcasted_iota(jnp.int32, (count, 1), 0) == head_pair
     own = jnp.sum(jnp.where(of_pair, own, 0.0), 0, keepdims=True)
@@ -174,7 +169,7 @@
     own_prob = (own_weight / denominator).astype(jnp.bfloat16)
     contract_rows = (((0,), (0,)), ((), ()))
     mixed = lax.dot_general(
-        probability, cached(split_values, rows * slots), contract_rows, preferred_element_type=jnp.float32
+        probability, cached(1), contract_rows, preferred_element_type=jnp.float32
     )
     own_prob = jnp.where(of_pair, own_prob.astype(jnp.float32), 0.0).astype(jnp.bfloat16)
     fresh = lax.dot_general(
@@ -293,29 +288,32 @@
         out_specs=IN_VMEM,
         compiler_params=params(8),
     )(scaled, norm_gain.reshape(1, -1))
-    block_rows = rows * cache_keys.shape[1]
+    slots = cache_keys.shape[1]
     even = plane // 2 - 1
+    early = rows // 2
+    every = range(rows)
 
     def cut(plan, after):
         return pl.pallas_call(
             functools.partial(cut_kernel, plan),
             out_shape=[
                 jax.ShapeDtypeStruct(
-                    (("k" in parts) * block_rows + ("v" in parts) * block_rows + ("n" in parts) * 16, kv_cols),
+                    ((len(key_rows) + len(value_rows)) * slots + 16 * with_lengths, kv_cols),
                     cache_keys.dtype,
                 )
-                for _, parts in plan
+                for _, key_rows, value_rows, with_lengths in plan
             ],
             in_specs=[IN_VMEM] * 4,
             out_specs=[IN_VMEM] * len(plan),
             compiler_params=params(8),
         )(lengths.reshape(1, -1), cache_keys, cache_values, after)
 
-    plan = [(l, "k") for l in range(2, plane, 2)] + [(l, "vn") for l in range(2, plane, 2)]
-    plan += [(l, "kvn") for l in range(1, plane, 2)]
+    plan = [(l, every, every[:early], False) for l in range(2, plane, 2)]
+    plan += [(l, (), every[early:], True) for l in range(2, plane, 2)]
+    plan += [(l, every, every, True) for l in range(1, plane, 2)]
     blocks = cut(plan, normed)
-    keys, rest = blocks[:even], blocks[even:]
-    keys = [swap_plane(keys[s], 2 * s + 2) for s in range(even)]
+    firsts, rest = blocks[:even], blocks[even:]
+    firsts = [swap_plane(firsts[s], 2 * s + 2) for s in range(even)]
     own_half = swap_blocks(normed, ROW_AXES)
     other_half = swap_pairs(own_half, "gz", 1)
     rest = pl.pallas_call(
@@ -325,11 +323,11 @@
         out_specs=[ANYWHERE] * len(rest),
         input_output_aliases={n: n for n in range(len(rest))},
         compiler_params=params(1),
-    )(*rest, own_half, *keys)
-    values = [swap_plane(rest[s], 2 * s + 2) for s in range(even)]
+    )(*rest, own_half, *firsts)
+    lasts = [swap_plane(rest[s], 2 * s + 2) for s in range(even)]
     odd = [swap_plane(rest[even + s], 2 * s + 1) for s in range(even + 1)]
-    (mine,) = cut([(0, "kvn")], own_half)
-    held = [*keys, *values, mine, *odd]
+    (mine,) = cut([(0, every, every, True)], own_half)
+    held = [*firsts, *lasts, mine, *odd]
     weights = (query_weight, key_weight, value_weight)
     half_cost = cost(owners * rows * width * cols, width * cols)
     partial = pl.pallas_call(
@@ -355,7 +353,7 @@
     frequency = 500000.0 ** (-np.arange(half_dim, dtype=np.float64) / half_dim)
     frequency = np.tile(frequency.astype(np.float32), 2).reshape(1, HD)
     attended = pl.pallas_call(
-        functools.partial(attend_kernel, wide, plane, rows, query_cols),
+        functools.partial(attend_kernel, wide, plane, rows, early, query_cols),
         out_shape=jax.ShapeDtypeStruct((plane, rows, query_cols), jnp.bfloat16),
         in_specs=[IN_VMEM] * (1 + wide + len(held)),
         out_specs=IN_VMEM,

time: 63.3 us -> 60.5 us (0.956)
  waiting for transfers between devices: 18.4 us -> 15.1 us
    ppermute x8, waiting for transfers between devices: 13.6 us -> 10.4 us  [swap_plane(): lax.ppermute(value, PLANE, [(i, i ^ step) for i in range(lax.axis_size(PL...]
  transfers between devices with their start and end apart: 18 -> 18, of which waited for: 9 -> 8; matrix products, arithmetic and copies ran while one was open for 0% -> 0% of each run, Pallas kernels for 9% -> 9%
where the time goes in v13:
time: 60.5 us; the launch traced here: 60.3 us
  starting transfers between devices  21.3 us (35%)
  waiting for transfers between devices  15.1 us (25%)
  blocking collectives  13 us (21%)
  Pallas kernels  9.41 us (16%)
  local copies, waits for them, and re-layouts  1.27 us (2%)
    ppermute x10, starting transfers between devices, swap_pairs(): lax.ppermute(value, axis, [(i, i ^ step) for i in range(lax.axis_size(axi...  13.8 us
    all_to_all x1, blocking collectives, swap_blocks(): return lax.all_to_all(blocks, axes, split_axis=0, concat_axis=0, tiled=True)  13 us
    ppermute x8, waiting for transfers between devices, swap_plane(): lax.ppermute(value, PLANE, [(i, i ^ step) for i in range(lax.axis_size(PL...  10.4 us
    ppermute x8, starting transfers between devices, swap_plane(): lax.ppermute(value, PLANE, [(i, i ^ step) for i in range(lax.axis_size(PL...  7.55 us
    ppermute x10, waiting for transfers between devices, swap_pairs(): lax.ppermute(value, axis, [(i, i ^ step) for i in range(lax.axis_size(axi...  4.74 us
    pallas_call x2, Pallas kernels, shards(): pl.pallas_call(functools.partial(output_kernel, p * part_cols, part_cols,...  3.09 us
    pallas_call x1, Pallas kernels, shards(): pl.pallas_call(functools.partial(project_kernel, False, wide, plane), out...  1.97 us
    pallas_call x1, Pallas kernels, shards(): pl.pallas_call(functools.partial(project_kernel, True, wide, plane), out_...  1.9 us
  transfers between devices with their start and end apart: 18, of which 8 were waited for; matrix products, arithmetic and copies ran while one was open for 0% of the time, Pallas kernels for 9%

profile of v13, /device:TPU:0, one launch (start us, length us, event | category | flops | bytes accessed | tf_op | source)
XLA Modules:
  0.0 60.3 jit_solution(1323211690531276980)
XLA Ops:
  0.0 0.0 copy-start.1
  0.0 0.0 copy-start.2
  0.0 0.0 copy-start.7
  0.0 1.0 %copy-done.7 = bf16[2,16384]{1,0:T(2,128)(2,1)S(1)} copy-done((bf16[2,16384]{1,0:T(2,128)(2,1)S(1)}, bf16[2,16384]{1,0:T(2,128)(2,1)}, u32[]{:S(2)}) %copy-start.7) | copy-done | bytes 65560
  1.0 0.2 shard_map.100.scaled_ref
  1.3 0.0 copy-done.5
  1.3 0.1 shard_map.101._
  1.4 0.0 copy-done.6
  1.4 0.0 copy-done.3
  1.4 0.2 copy-done.4
  1.6 0.2 shard_map.102
  1.8 3.0 %collective-permute-start.1 = (bf16[768,256]{1,0:T(8,128)(2,1)S(1)}, bf16[768,256]{1,0:T(8,128)(2,1)S(1)}, u32[]{:S(2)}, u32[]{:S(2)}) collective-permute-start(bf16[768,256]{1,0:T(8,128)(2,1)S(1)} %get-tuple-element.31), channel_id=1, source_target_pairs={{0,2},{1,3},{2,0},{3,1},{4,6},{5,7},{6,4},{7,5},{8,10},{9,11},{10,... | collective-permute-start | bytes 1179656 | tf_op jit(solution)/shard_map/ppermute | solution.py:241
  4.9 13.0 %all_to_all.5.refs_3_.rows_ref._ = bf16[16,2,2048]{2,1,0:T(2,128)(2,1)S(1)} all-to-all(bf16[16,2,2048]{2,1,0:T(2,128)(2,1)S(1)} %shard_map.101._), channel_id=1, replica_groups=mesh['groups'=2,'gx'=4,'gy'=2,'gz'=2] {'gx','gy','gz'}, dimensions={0} | all-to-all | bytes 262144 | tf_op jit(solution)/shard_map/all_to_all | solution.py:233
  17.8 0.0 collective-permute-done.1.refs_4_
  17.8 0.0 collective-permute-start.2
  17.8 0.1 collective-permute-start.7
  17.9 0.4 collective-permute-start
  18.3 1.7 %collective-permute-start.6 = (bf16[272,256]{1,0:T(8,128)(2,1)S(1)}, bf16[272,256]{1,0:T(8,128)(2,1)S(1)}, u32[]{:S(2)}, u32[]{:S(2)}) collective-permute-start(bf16[272,256]{1,0:T(8,128)(2,1)S(1)} %get-tuple-element.37), channel_id=1, source_target_pairs={{0,2},{1,3},{2,0},{3,1},{4,6},{5,7},{6,4},{7,5},{8,10},{9,11},{10,... | collective-permute-start | bytes 417800 | tf_op jit(solution)/shard_map/ppermute | solution.py:241
  20.0 0.0 copy-done
  20.0 0.0 copy-done.1
  20.0 0.0 copy-done.2
  20.0 1.9 %shard_map.104.refs_1_ = f32[32,2560]{1,0:T(8,128)S(1)} custom-call(bf16[16,2,2048]{2,1,0:T(2,128)(2,1)S(1)} %all_to_all.5.refs_3_.rows_ref._, bf16[4096,2048]{1,0:T(8,128)(2,1)S(1)} %copy-done, bf16[4096,256]{1,0:T(8,128)(2,1)S(1)} %copy-done.1, bf16[4096,256]{1,0:T(8,128)(2,1)S(1)} %copy-done.2), custom_call_target="tpu_custom_call" | custom-call | flops 335544320 | bytes 10485760 | tf_op jit(solution)/shard_map/pallas_call | solution.py:333
  21.9 0.0 collective-permute-done.rows_ref
  22.0 0.0 collective-permute-done.2.refs_0_.refs_7_
  22.0 2.0 %shard_map.105 = (f32[4,2,2560]{2,1,0:T(2,128)S(1)}, f32[4,2,2560]{2,1,0:T(2,128)S(1)}, f32[4,2,2560]{2,1,0:T(2,128)S(1)}, f32[4,2,2560]{2,1,0:T(2,128)S(1)}) custom-call(bf16[16,2,2048]{2,1,0:T(2,128)(2,1)S(1)} %collective-permute-done.rows_ref, bf16[4096,2048]{1,0:T(8,128)(2,1)S(1)} %copy-done, bf16[4096,256]{1,0:T(8,128)(2,1)S(1)} %copy-done.1, ...), custom_call_target="tpu_custom_call" | custom-call | flops 335544320 | bytes 10485760 | tf_op jit(solution)/shard_map/pallas_call | solution.py:341
  24.0 1.5 %collective-permute-start.3 = (f32[4,2,2560]{2,1,0:T(2,128)S(1)}, f32[4,2,2560]{2,1,0:T(2,128)S(1)}, u32[]{:S(2)}, u32[]{:S(2)}) collective-permute-start(f32[4,2,2560]{2,1,0:T(2,128)S(1)} %get-tuple-element.33), channel_id=1, source_target_pairs={{0,12},{4,8},{8,4},{12,0},{1,13},{5,9},{9,5},{13,1},{2,14},{6,10},... | collective-permute-start | bytes 245768 | tf_op jit(solution)/shard_map/ppermute | solution.py:237
  25.4 0.0 collective-permute-start.4
  25.5 3.0 %collective-permute-start.5 = (f32[4,2,2560]{2,1,0:T(2,128)S(1)}, f32[4,2,2560]{2,1,0:T(2,128)S(1)}, u32[]{:S(2)}, u32[]{:S(2)}) collective-permute-start(f32[4,2,2560]{2,1,0:T(2,128)S(1)} %get-tuple-element.35), channel_id=1, source_target_pairs={{0,4},{4,0},{8,12},{12,8},{1,5},{5,1},{9,13},{13,9},{2,6},{6,2},{1... | collective-permute-start | bytes 245768 | tf_op jit(solution)/shard_map/ppermute | solution.py:237
  28.4 0.1 shard_map.106.refs_6_
  28.5 6.8 %collective-permute-done.6.refs_5_ = bf16[272,256]{1,0:T(8,128)(2,1)S(1)} collective-permute-done((bf16[272,256]{1,0:T(8,128)(2,1)S(1)}, bf16[272,256]{1,0:T(8,128)(2,1)S(1)}, u32[]{:S(2)}, u32[]{:S(2)}) %collective-permute-start.6) | collective-permute-done | bytes 139296 | tf_op jit(solution)/shard_map/ppermute | solution.py:241
  35.3 0.0 collective-permute-done.7.refs_8_
  35.3 0.0 collective-permute-done.3.refs_0_
  35.3 0.0 collective-permute-done.4.refs_1_
  35.3 0.0 collective-permute-done.5.refs_2_
  35.3 0.0 copy-done.8
  35.3 0.0 slice-start.1
  35.3 0.0 slice-start.2
  35.3 0.0 slice-start.3
  35.3 1.1 %shard_map.107.refs_0_ = bf16[4,2,2048]{2,1,0:T(2,128)(2,1)S(1)} custom-call(f32[1,128]{1,0:T(1,128)S(1)} %copy-done.8, f32[4,2,2560]{2,1,0:T(2,128)S(1)} %collective-permute-done.3.refs_0_, f32[4,2,2560]{2,1,0:T(2,128)S(1)} %collective-permute-done.4.refs_1_, f32[4,2,2560]{2,1,0:T(2,128)S(1)} %collective-permute-done.5.refs_2_, ...), custom_call_target="tpu_custom_call" | custom-call | flops 10000000000 | bytes 4194304 | tf_op jit(solution)/shard_map/pallas_call | solution.py:355
  36.5 1.5 %collective-permute-start.10 = (bf16[4,2,2048]{2,1,0:T(2,128)(2,1)S(1)}, bf16[4,2,2048]{2,1,0:T(2,128)(2,1)S(1)}, u32[]{:S(2)}, u32[]{:S(2)}) collective-permute-start(bf16[4,2,2048]{2,1,0:T(2,128)(2,1)S(1)} %shard_map.107.refs_0_), channel_id=1, source_target_pairs={{0,12},{4,8},{8,4},{12,0},{1,13},{5,9},{9,5},{13,1},{2,14},{6,10},... | collective-permute-start | bytes 98312 | tf_op jit(solution)/shard_map/ppermute | solution.py:237
  37.9 0.0 collective-permute-start.8
  38.0 3.0 %collective-permute-start.9 = (bf16[4,2,2048]{2,1,0:T(2,128)(2,1)S(1)}, bf16[4,2,2048]{2,1,0:T(2,128)(2,1)S(1)}, u32[]{:S(2)}, u32[]{:S(2)}) collective-permute-start(bf16[4,2,2048]{2,1,0:T(2,128)(2,1)S(1)} %shard_map.107.refs_0_), channel_id=1, source_target_pairs={{0,4},{4,0},{8,12},{12,8},{1,5},{5,1},{9,13},{13,9},{2,6},{6,2},{1... | collective-permute-start | bytes 98312 | tf_op jit(solution)/shard_map/ppermute | solution.py:237
  40.9 1.6 %collective-permute-done.10.refs_3_ = bf16[4,2,2048]{2,1,0:T(2,128)(2,1)S(1)} collective-permute-done((bf16[4,2,2048]{2,1,0:T(2,128)(2,1)S(1)}, bf16[4,2,2048]{2,1,0:T(2,128)(2,1)S(1)}, u32[]{:S(2)}, u32[]{:S(2)}) %collective-permute-start.10) | collective-permute-done | bytes 32800 | tf_op jit(solution)/shard_map/ppermute | solution.py:237
  42.5 0.6 %collective-permute-done.8.refs_1_ = bf16[4,2,2048]{2,1,0:T(2,128)(2,1)S(1)} collective-permute-done((bf16[4,2,2048]{2,1,0:T(2,128)(2,1)S(1)}, bf16[4,2,2048]{2,1,0:T(2,128)(2,1)S(1)}, u32[]{:S(2)}, u32[]{:S(2)}) %collective-permute-start.8) | collective-permute-done | bytes 32800 | tf_op jit(solution)/shard_map/ppermute | solution.py:237
  43.2 0.0 collective-permute-done.9.refs_2_
  43.2 0.0 slice-done.1
  43.2 1.5 %shard_map.110 = (f32[8,2,2048]{2,1,0:T(2,128)S(1)}, f32[8,2,2048]{2,1,0:T(2,128)S(1)}) custom-call(bf16[2048,4096]{1,0:T(8,128)(2,1)S(1)} %bitcast.3, bf16[4,2,2048]{2,1,0:T(2,128)(2,1)S(1)} %shard_map.107.refs_0_, bf16[4,2,2048]{2,1,0:T(2,128)(2,1)S(1)} %collective-permute-done.8.refs_1_, bf16[4,2,2048]{2,1,0:T(2,128)(2,1)S(1)} %collective-permute-done.9.refs_2_, ...), custom_call_target="tpu_custom_call" | custom-call | flops 268435456 | bytes 8388608 | tf_op jit(solution)/shard_map/pallas_call | solution.py:371
  44.8 0.1 collective-permute-start.13
  44.8 1.5 %shard_map.108 = (f32[8,2,2048]{2,1,0:T(2,128)S(1)}, f32[8,2,2048]{2,1,0:T(2,128)S(1)}) custom-call(bf16[2048,4096]{1,0:T(8,128)(2,1)S(1)} %bitcast.3, bf16[4,2,2048]{2,1,0:T(2,128)(2,1)S(1)} %shard_map.107.refs_0_, bf16[4,2,2048]{2,1,0:T(2,128)(2,1)S(1)} %collective-permute-done.8.refs_1_, bf16[4,2,2048]{2,1,0:T(2,128)(2,1)S(1)} %collective-permute-done.9.refs_2_, ...), custom_call_target="tpu_custom_call" | custom-call | flops 268435456 | bytes 8388608 | tf_op jit(solution)/shard_map/pallas_call | solution.py:371
  46.4 0.6 collective-permute-start.11
  46.9 0.0 collective-permute-done.13.b_ref
  47.0 1.1 %collective-permute-start.14 = (f32[4,2,2048]{2,1,0:T(2,128)S(1)}, f32[4,2,2048]{2,1,0:T(2,128)S(1)}, u32[]{:S(2)}, u32[]{:S(2)}) collective-permute-start(f32[4,2,2048]{2,1,0:T(2,128)S(1)} %get-tuple-element.46), channel_id=1, source_target_pairs={{0,2},{1,3},{2,0},{3,1},{4,6},{5,7},{6,4},{7,5},{8,10},{9,11},{10,... | collective-permute-start | bytes 196616 | tf_op jit(solution)/shard_map/ppermute | solution.py:241
  48.1 0.0 collective-permute-done.11.b_ref
  48.1 1.0 %collective-permute-start.12 = (f32[4,2,2048]{2,1,0:T(2,128)S(1)}, f32[4,2,2048]{2,1,0:T(2,128)S(1)}, u32[]{:S(2)}, u32[]{:S(2)}) collective-permute-start(f32[4,2,2048]{2,1,0:T(2,128)S(1)} %get-tuple-element.42), channel_id=1, source_target_pairs={{0,2},{1,3},{2,0},{3,1},{4,6},{5,7},{6,4},{7,5},{8,10},{9,11},{10,... | collective-permute-start | bytes 196616 | tf_op jit(solution)/shard_map/ppermute | solution.py:241
  49.1 2.6 %collective-permute-done.14.refs_3_ = f32[4,2,2048]{2,1,0:T(2,128)S(1)} collective-permute-done((f32[4,2,2048]{2,1,0:T(2,128)S(1)}, f32[4,2,2048]{2,1,0:T(2,128)S(1)}, u32[]{:S(2)}, u32[]{:S(2)}) %collective-permute-start.14) | collective-permute-done | bytes 65568 | tf_op jit(solution)/shard_map/ppermute | solution.py:241
  51.7 1.0 %collective-permute-done.12.refs_1_ = f32[4,2,2048]{2,1,0:T(2,128)S(1)} collective-permute-done((f32[4,2,2048]{2,1,0:T(2,128)S(1)}, f32[4,2,2048]{2,1,0:T(2,128)S(1)}, u32[]{:S(2)}, u32[]{:S(2)}) %collective-permute-start.12) | collective-permute-done | bytes 65568 | tf_op jit(solution)/shard_map/ppermute | solution.py:241
  52.7 0.1 shard_map.112
  52.8 2.1 %collective-permute-start.15 = (bf16[2,4096]{1,0:T(2,128)(2,1)S(1)}, bf16[2,4096]{1,0:T(2,128)(2,1)S(1)}, u32[]{:S(2)}, u32[]{:S(2)}) collective-permute-start(bf16[2,4096]{1,0:T(2,128)(2,1)S(1)} %get-tuple-element.47), channel_id=1, source_target_pairs={{0,12},{4,8},{8,4},{12,0},{1,13},{5,9},{9,5},{13,1},{2,14},{6,10},... | collective-permute-start | bytes 49160 | tf_op jit(solution)/shard_map/ppermute | solution.py:237
  54.8 1.1 %collective-permute-start.16 = (bf16[2,4096]{1,0:T(2,128)(2,1)S(1)}, bf16[2,4096]{1,0:T(2,128)(2,1)S(1)}, u32[]{:S(2)}, u32[]{:S(2)}) collective-permute-start(bf16[2,4096]{1,0:T(2,128)(2,1)S(1)} %get-tuple-element.48), channel_id=1, source_target_pairs={{0,8},{4,12},{8,0},{12,4},{1,9},{5,13},{9,1},{13,5},{2,10},{6,14},... | collective-permute-start | bytes 49160 | tf_op jit(solution)/shard_map/ppermute | solution.py:237
  56.0 1.3 %collective-permute-start.17 = (bf16[2,4096]{1,0:T(2,128)(2,1)S(1)}, bf16[2,4096]{1,0:T(2,128)(2,1)S(1)}, u32[]{:S(2)}, u32[]{:S(2)}) collective-permute-start(bf16[2,4096]{1,0:T(2,128)(2,1)S(1)} %get-tuple-element.49), channel_id=1, source_target_pairs={{0,4},{4,0},{8,12},{12,8},{1,5},{5,1},{9,13},{13,9},{2,6},{6,2},{1... | collective-permute-start | bytes 49160 | tf_op jit(solution)/shard_map/ppermute | solution.py:237
  57.2 1.1 %collective-permute-done.15.refs_0_ = bf16[2,4096]{1,0:T(2,128)(2,1)S(1)} collective-permute-done((bf16[2,4096]{1,0:T(2,128)(2,1)S(1)}, bf16[2,4096]{1,0:T(2,128)(2,1)S(1)}, u32[]{:S(2)}, u32[]{:S(2)}) %collective-permute-start.15) | collective-permute-done | bytes 16416 | tf_op jit(solution)/shard_map/ppermute | solution.py:237
  58.4 1.1 %collective-permute-done.16.refs_1_ = bf16[2,4096]{1,0:T(2,128)(2,1)S(1)} collective-permute-done((bf16[2,4096]{1,0:T(2,128)(2,1)S(1)}, bf16[2,4096]{1,0:T(2,128)(2,1)S(1)}, u32[]{:S(2)}, u32[]{:S(2)}) %collective-permute-start.16) | collective-permute-done | bytes 16416 | tf_op jit(solution)/shard_map/ppermute | solution.py:237
  59.5 0.2 collective-permute-done.17.refs_2_
  59.7 0.6 %shard_map.113 = bf16[2,16384]{1,0:T(2,128)(2,1)} custom-call(bf16[2,4096]{1,0:T(2,128)(2,1)S(1)} %collective-permute-done.15.refs_0_, bf16[2,4096]{1,0:T(2,128)(2,1)S(1)} %collective-permute-done.16.refs_1_, bf16[2,4096]{1,0:T(2,128)(2,1)S(1)} %collective-permute-done.17.refs_2_, bf16[2,4096]{1,0:T(2,128)(2,1)S(1)} %get-tuple-element.50.refs_3_), custom_call_target="tpu_custom_call" | custom-call | tf_op jit(solution)/shard_map/pallas_call | solution.py:402
  (14 shorter events, 0.0 us)
Async XLA Ops:
  0.0 1.3 %copy-start.5 = (f32[16384]{0:T(1024)S(1)}, f32[16384]{0:T(1024)}, u32[]{:S(2)}) copy-start(f32[16384]{0:T(1024)} %param.11) | copy-start | bytes 196612
  0.0 1.4 %copy-start.6 = (s32[2]{0:T(128)S(1)}, s32[2]{0:T(128)}, u32[]{:S(2)}) copy-start(s32[2]{0:T(128)} %param.18) | copy-start | bytes 28
  0.0 1.4 %copy-start.3 = (bf16[2,256,1024]{2,1,0:T(8,128)(2,1)S(1)}, bf16[2,256,1024]{2,1,0:T(8,128)(2,1)}, u32[]{:S(2)}) copy-start(bf16[2,256,1024]{2,1,0:T(8,128)(2,1)} %keys_ref.3) | copy-start | bytes 3145732
  0.0 1.6 %copy-start.4 = (bf16[2,256,1024]{2,1,0:T(8,128)(2,1)S(1)}, bf16[2,256,1024]{2,1,0:T(8,128)(2,1)}, u32[]{:S(2)}) copy-start(bf16[2,256,1024]{2,1,0:T(8,128)(2,1)} %values_ref.3) | copy-start | bytes 3145732
  0.0 20.0 %copy-start = (bf16[4096,2048]{1,0:T(8,128)(2,1)S(1)}, bf16[4096,2048]{1,0:T(8,128)(2,1)}, u32[]{:S(2)}) copy-start(bf16[4096,2048]{1,0:T(8,128)(2,1)} %query_ref.3) | copy-start | bytes 50331652
  0.0 20.0 %copy-start.1 = (bf16[4096,256]{1,0:T(8,128)(2,1)S(1)}, bf16[4096,256]{1,0:T(8,128)(2,1)}, u32[]{:S(2)}) copy-start(bf16[4096,256]{1,0:T(8,128)(2,1)} %key_ref.3) | copy-start | bytes 6291460
  0.0 20.0 %copy-start.2 = (bf16[4096,256]{1,0:T(8,128)(2,1)S(1)}, bf16[4096,256]{1,0:T(8,128)(2,1)}, u32[]{:S(2)}) copy-start(bf16[4096,256]{1,0:T(8,128)(2,1)} %value_ref.3) | copy-start | bytes 6291460
  0.0 1.0 %copy-start.7 = (bf16[2,16384]{1,0:T(2,128)(2,1)S(1)}, bf16[2,16384]{1,0:T(2,128)(2,1)}, u32[]{:S(2)}) copy-start(bf16[2,16384]{1,0:T(2,128)(2,1)} %tokens_ref.1) | copy-start | bytes 196612
  1.8 16.0 %collective-permute-start.1 = (bf16[768,256]{1,0:T(8,128)(2,1)S(1)}, bf16[768,256]{1,0:T(8,128)(2,1)S(1)}, u32[]{:S(2)}, u32[]{:S(2)}) collective-permute-start(bf16[768,256]{1,0:T(8,128)(2,1)S(1)} %get-tuple-element.31), channel_id=1, source_target_pairs={{0,2},{1,3},{2,0},{3,1},{4,6},{5,7},{6,4},{7,5},{8,10},{9,11},{10,... | collective-permute-start | bytes 1179656 | tf_op jit(solution)/shard_map/ppermute | solution.py:241
  17.8 4.1 %collective-permute-start.2 = (bf16[1040,256]{1,0:T(8,128)(2,1)S(1)}, bf16[1040,256]{1,0:T(8,128)(2,1)S(1)}, u32[]{:S(2)}, u32[]{:S(2)}) collective-permute-start(bf16[1040,256]{1,0:T(8,128)(2,1)S(1)} %get-tuple-element.32), channel_id=1, source_target_pairs={{0,1},{1,0},{2,3},{3,2},{4,5},{5,4},{6,7},{7,6},{8,9},{9,8},{10,11... | collective-permute-start | bytes 1597448 | tf_op jit(solution)/shard_map/ppermute | solution.py:241
  17.8 17.4 %collective-permute-start.7 = (bf16[1040,256]{1,0:T(8,128)(2,1)S(1)}, bf16[1040,256]{1,0:T(8,128)(2,1)S(1)}, u32[]{:S(2)}, u32[]{:S(2)}) collective-permute-start(bf16[1040,256]{1,0:T(8,128)(2,1)S(1)} %get-tuple-element.38), channel_id=1, source_target_pairs={{0,3},{1,2},{2,1},{3,0},{4,7},{5,6},{6,5},{7,4},{8,11},{9,10},{10,... | collective-permute-start | bytes 1597448 | tf_op jit(solution)/shard_map/ppermute | solution.py:241
  17.9 4.0 %collective-permute-start = (bf16[16,2,2048]{2,1,0:T(2,128)(2,1)S(1)}, bf16[16,2,2048]{2,1,0:T(2,128)(2,1)S(1)}, u32[]{:S(2)}, u32[]{:S(2)}) collective-permute-start(bf16[16,2,2048]{2,1,0:T(2,128)(2,1)S(1)} %all_to_all.5.refs_3_.rows_ref._), channel_id=1, source_target_pairs={{0,1},{1,0},{2,3},{3,2},{4,5},{5,4},{6,7},{7,6},{8,9},{9,8},{10,11... | collective-permute-start | bytes 393224 | tf_op jit(solution)/shard_map/ppermute | solution.py:237
  18.3 16.9 %collective-permute-start.6 = (bf16[272,256]{1,0:T(8,128)(2,1)S(1)}, bf16[272,256]{1,0:T(8,128)(2,1)S(1)}, u32[]{:S(2)}, u32[]{:S(2)}) collective-permute-start(bf16[272,256]{1,0:T(8,128)(2,1)S(1)} %get-tuple-element.37), channel_id=1, source_target_pairs={{0,2},{1,3},{2,0},{3,1},{4,6},{5,7},{6,4},{7,5},{8,10},{9,11},{10,... | collective-permute-start | bytes 417800 | tf_op jit(solution)/shard_map/ppermute | solution.py:241
  21.9 13.4 %copy-start.8 = (f32[1,128]{1,0:T(1,128)S(1)}, f32[1,128]{1,0:T(1,128)}, u32[]{:S(2)}) copy-start(f32[1,128]{1,0:T(1,128)} %constant.2.clone.frequency_ref) | copy-start | bytes 1540
  24.0 11.3 %collective-permute-start.3 = (f32[4,2,2560]{2,1,0:T(2,128)S(1)}, f32[4,2,2560]{2,1,0:T(2,128)S(1)}, u32[]{:S(2)}, u32[]{:S(2)}) collective-permute-start(f32[4,2,2560]{2,1,0:T(2,128)S(1)} %get-tuple-element.33), channel_id=1, source_target_pairs={{0,12},{4,8},{8,4},{12,0},{1,13},{5,9},{9,5},{13,1},{2,14},{6,10},... | collective-permute-start | bytes 245768 | tf_op jit(solution)/shard_map/ppermute | solution.py:237
  25.4 9.9 %collective-permute-start.4 = (f32[4,2,2560]{2,1,0:T(2,128)S(1)}, f32[4,2,2560]{2,1,0:T(2,128)S(1)}, u32[]{:S(2)}, u32[]{:S(2)}) collective-permute-start(f32[4,2,2560]{2,1,0:T(2,128)S(1)} %get-tuple-element.34), channel_id=1, source_target_pairs={{0,8},{4,12},{8,0},{12,4},{1,9},{5,13},{9,1},{13,5},{2,10},{6,14},... | collective-permute-start | bytes 245768 | tf_op jit(solution)/shard_map/ppermute | solution.py:237
  25.5 9.8 %collective-permute-start.5 = (f32[4,2,2560]{2,1,0:T(2,128)S(1)}, f32[4,2,2560]{2,1,0:T(2,128)S(1)}, u32[]{:S(2)}, u32[]{:S(2)}) collective-permute-start(f32[4,2,2560]{2,1,0:T(2,128)S(1)} %get-tuple-element.35), channel_id=1, source_target_pairs={{0,4},{4,0},{8,12},{12,8},{1,5},{5,1},{9,13},{13,9},{2,6},{6,2},{1... | collective-permute-start | bytes 245768 | tf_op jit(solution)/shard_map/ppermute | solution.py:237
  28.4 14.8 %slice-start = ((s8[16777216]{0:T(1024)(128)(4,1)}), s8[4194304]{0:T(1024)(128)(4,1)S(1)}, s32[]{:S(2)}) async-start(s8[16777216]{0:T(1024)(128)(4,1)} %bitcast.2), calls=%async_computation.1 | async-start | bytes 8388608
  35.3 7.9 %slice-start.1 = ((s8[16777216]{0:T(1024)(128)(4,1)}), s8[4194304]{0:T(1024)(128)(4,1)S(1)}, s32[]{:S(2)}) async-start(s8[16777216]{0:T(1024)(128)(4,1)} %bitcast.2), calls=%async_computation.2 | async-start | bytes 8388608
  35.3 7.9 %slice-start.2 = ((s8[16777216]{0:T(1024)(128)(4,1)}), s8[4194304]{0:T(1024)(128)(4,1)S(1)}, s32[]{:S(2)}) async-start(s8[16777216]{0:T(1024)(128)(4,1)} %bitcast.2), calls=%async_computation.3 | async-start | bytes 8388608
  35.3 7.9 %slice-start.3 = ((s8[16777216]{0:T(1024)(128)(4,1)}), s8[4194304]{0:T(1024)(128)(4,1)S(1)}, s32[]{:S(2)}) async-start(s8[16777216]{0:T(1024)(128)(4,1)} %bitcast.2), calls=%async_computation.4 | async-start | bytes 8388608
  36.5 6.1 %collective-permute-start.10 = (bf16[4,2,2048]{2,1,0:T(2,128)(2,1)S(1)}, bf16[4,2,2048]{2,1,0:T(2,128)(2,1)S(1)}, u32[]{:S(2)}, u32[]{:S(2)}) collective-permute-start(bf16[4,2,2048]{2,1,0:T(2,128)(2,1)S(1)} %shard_map.107.refs_0_), channel_id=1, source_target_pairs={{0,12},{4,8},{8,4},{12,0},{1,13},{5,9},{9,5},{13,1},{2,14},{6,10},... | collective-permute-start | bytes 98312 | tf_op jit(solution)/shard_map/ppermute | solution.py:237
  37.9 5.2 %collective-permute-start.8 = (bf16[4,2,2048]{2,1,0:T(2,128)(2,1)S(1)}, bf16[4,2,2048]{2,1,0:T(2,128)(2,1)S(1)}, u32[]{:S(2)}, u32[]{:S(2)}) collective-permute-start(bf16[4,2,2048]{2,1,0:T(2,128)(2,1)S(1)} %shard_map.107.refs_0_), channel_id=1, source_target_pairs={{0,8},{4,12},{8,0},{12,4},{1,9},{5,13},{9,1},{13,5},{2,10},{6,14},... | collective-permute-start | bytes 98312 | tf_op jit(solution)/shard_map/ppermute | solution.py:237
  38.0 5.2 %collective-permute-start.9 = (bf16[4,2,2048]{2,1,0:T(2,128)(2,1)S(1)}, bf16[4,2,2048]{2,1,0:T(2,128)(2,1)S(1)}, u32[]{:S(2)}, u32[]{:S(2)}) collective-permute-start(bf16[4,2,2048]{2,1,0:T(2,128)(2,1)S(1)} %shard_map.107.refs_0_), channel_id=1, source_target_pairs={{0,4},{4,0},{8,12},{12,8},{1,5},{5,1},{9,13},{13,9},{2,6},{6,2},{1... | collective-permute-start | bytes 98312 | tf_op jit(solution)/shard_map/ppermute | solution.py:237
  44.8 2.2 %collective-permute-start.13 = (f32[8,2,2048]{2,1,0:T(2,128)S(1)}, f32[8,2,2048]{2,1,0:T(2,128)S(1)}, u32[]{:S(2)}, u32[]{:S(2)}) collective-permute-start(f32[8,2,2048]{2,1,0:T(2,128)S(1)} %get-tuple-element.44), channel_id=1, source_target_pairs={{0,1},{1,0},{2,3},{3,2},{4,5},{5,4},{6,7},{7,6},{8,9},{9,8},{10,11... | collective-permute-start | bytes 393224 | tf_op jit(solution)/shard_map/ppermute | solution.py:241
  46.4 1.7 %collective-permute-start.11 = (f32[8,2,2048]{2,1,0:T(2,128)S(1)}, f32[8,2,2048]{2,1,0:T(2,128)S(1)}, u32[]{:S(2)}, u32[]{:S(2)}) collective-permute-start(f32[8,2,2048]{2,1,0:T(2,128)S(1)} %get-tuple-element.40), channel_id=1, source_target_pairs={{0,1},{1,0},{2,3},{3,2},{4,5},{5,4},{6,7},{7,6},{8,9},{9,8},{10,11... | collective-permute-start | bytes 393224 | tf_op jit(solution)/shard_map/ppermute | solution.py:241
  47.0 4.7 %collective-permute-start.14 = (f32[4,2,2048]{2,1,0:T(2,128)S(1)}, f32[4,2,2048]{2,1,0:T(2,128)S(1)}, u32[]{:S(2)}, u32[]{:S(2)}) collective-permute-start(f32[4,2,2048]{2,1,0:T(2,128)S(1)} %get-tuple-element.46), channel_id=1, source_target_pairs={{0,2},{1,3},{2,0},{3,1},{4,6},{5,7},{6,4},{7,5},{8,10},{9,11},{10,... | collective-permute-start | bytes 196616 | tf_op jit(solution)/shard_map/ppermute | solution.py:241
  48.1 4.6 %collective-permute-start.12 = (f32[4,2,2048]{2,1,0:T(2,128)S(1)}, f32[4,2,2048]{2,1,0:T(2,128)S(1)}, u32[]{:S(2)}, u32[]{:S(2)}) collective-permute-start(f32[4,2,2048]{2,1,0:T(2,128)S(1)} %get-tuple-element.42), channel_id=1, source_target_pairs={{0,2},{1,3},{2,0},{3,1},{4,6},{5,7},{6,4},{7,5},{8,10},{9,11},{10,... | collective-permute-start | bytes 196616 | tf_op jit(solution)/shard_map/ppermute | solution.py:241
  52.8 5.6 %collective-permute-start.15 = (bf16[2,4096]{1,0:T(2,128)(2,1)S(1)}, bf16[2,4096]{1,0:T(2,128)(2,1)S(1)}, u32[]{:S(2)}, u32[]{:S(2)}) collective-permute-start(bf16[2,4096]{1,0:T(2,128)(2,1)S(1)} %get-tuple-element.47), channel_id=1, source_target_pairs={{0,12},{4,8},{8,4},{12,0},{1,13},{5,9},{9,5},{13,1},{2,14},{6,10},... | collective-permute-start | bytes 49160 | tf_op jit(solution)/shard_map/ppermute | solution.py:237
  54.8 4.6 %collective-permute-start.16 = (bf16[2,4096]{1,0:T(2,128)(2,1)S(1)}, bf16[2,4096]{1,0:T(2,128)(2,1)S(1)}, u32[]{:S(2)}, u32[]{:S(2)}) collective-permute-start(bf16[2,4096]{1,0:T(2,128)(2,1)S(1)} %get-tuple-element.48), channel_id=1, source_target_pairs={{0,8},{4,12},{8,0},{12,4},{1,9},{5,13},{9,1},{13,5},{2,10},{6,14},... | collective-permute-start | bytes 49160 | tf_op jit(solution)/shard_map/ppermute | solution.py:237
  56.0 3.7 %collective-permute-start.17 = (bf16[2,4096]{1,0:T(2,128)(2,1)S(1)}, bf16[2,4096]{1,0:T(2,128)(2,1)S(1)}, u32[]{:S(2)}, u32[]{:S(2)}) collective-permute-start(bf16[2,4096]{1,0:T(2,128)(2,1)S(1)} %get-tuple-element.49), channel_id=1, source_target_pairs={{0,4},{4,0},{8,12},{12,8},{1,5},{5,1},{9,13},{13,9},{2,6},{6,2},{1... | collective-permute-start | bytes 49160 | tf_op jit(solution)/shard_map/ppermute | solution.py:237

commit v14 on v13

--- a/solution.py
+++ b/solution.py
@@ -87,6 +87,28 @@
             write_lengths(rows, lengths_ref, block)
 
 
+def early_kernel(early, keys_hbm, values_hbm, *refs):
+    blocks, sems = refs[:-1], refs[-1]
+    rows, slots, _ = keys_hbm.shape
+    cols = blocks[0].shape[1]
+    copies = []
+    for s, block in enumerate(blocks):
+        at = pl.multiple_of((own_place() ^ (2 * s + 2)) * cols, cols)
+        wanted = [(keys_hbm, r) for r in range(rows)] + [(values_hbm, r) for r in range(early)]
+        for n, (cache, r) in enumerate(wanted):
+            copies.append(
+                pltpu.make_async_copy(
+                    cache.at[r, :, pl.ds(at, cols)],
+                    block.at[pl.ds(n * slots, slots)],
+                    sems.at[s, n],
+                )
+            )
+    for copy in copies:
+        copy.start()
+    for copy in copies:
+        copy.wait()
+
+
 def pass_kernel(*refs):
     pass
 
@@ -273,6 +295,23 @@
         return pl.CostEstimate(flops=flops, bytes_accessed=size, transcendentals=0)
 
     half = width // 2
+    slots = cache_keys.shape[1]
+    even = plane // 2 - 1
+    early = rows // 2
+    every = range(rows)
+
+    firsts = pl.pallas_call(
+        functools.partial(early_kernel, early),
+        out_shape=[
+            jax.ShapeDtypeStruct(((rows + early) * slots, kv_cols), cache_keys.dtype)
+        ] * even,
+        in_specs=[ANYWHERE] * 2,
+        out_specs=[ANYWHERE] * even,
+        scratch_shapes=[pltpu.SemaphoreType.DMA((even, rows + early))],
+        compiler_params=params(62),
+        cost_estimate=cost(40 * 10**9, MIB),
+    )(cache_keys, cache_values)
+    firsts = [swap_plane(firsts[s], 2 * s + 2) for s in range(even)]
     scaled = pl.pallas_call(
         scale_kernel,
         out_shape=jax.ShapeDtypeStruct(tokens.shape, jnp.float32),
@@ -288,11 +327,6 @@
         out_specs=IN_VMEM,
         compiler_params=params(8),
     )(scaled, norm_gain.reshape(1, -1))
-    slots = cache_keys.shape[1]
-    even = plane // 2 - 1
-    early = rows // 2
-    every = range(rows)
-
     def cut(plan, after):
         return pl.pallas_call(
             functools.partial(cut_kernel, plan),
@@ -308,12 +342,9 @@
             compiler_params=params(8),
         )(lengths.reshape(1, -1), cache_keys, cache_values, after)
 
-    plan = [(l, every, every[:early], False) for l in range(2, plane, 2)]
-    plan += [(l, (), every[early:], True) for l in range(2, plane, 2)]
+    plan = [(l, (), every[early:], True) for l in range(2, plane, 2)]
     plan += [(l, every, every, True) for l in range(1, plane, 2)]
-    blocks = cut(plan, normed)
-    firsts, rest = blocks[:even], blocks[even:]
-    firsts = [swap_plane(firsts[s], 2 * s + 2) for s in range(even)]
+    rest = cut(plan, normed)
     own_half = swap_blocks(normed, ROW_AXES)
     other_half = swap_pairs(own_half, "gz", 1)
     rest = pl.pallas_call(

time: 60.5 us -> 89.1 us (1.47)
  local copies, waits for them, and re-layouts: 1.27 us -> 19.7 us
  Pallas kernels: 9.41 us -> 25.1 us
  blocking collectives: 13 us -> 0 us
  starting transfers between devices: 21.3 us -> 26.2 us
  waiting for transfers between devices: 15.1 us -> 17.4 us
    unnamed x26 -> x42, local copies, waits for them, and re-layouts: 1.27 us -> 19.7 us
    pallas_call x0 -> x1, Pallas kernels: none -> 13 us  [shards(): pl.pallas_call(functools.partial(early_kernel, early), out_shape=[jax.Sha...]
    all_to_all x1 -> x0, blocking collectives: 13 us -> none  [swap_blocks(): return lax.all_to_all(blocks, axes, split_axis=0, concat_axis=0, tiled=True)]
    ppermute x8, waiting for transfers between devices: 10.4 us -> 3.65 us  [swap_plane(): lax.ppermute(value, PLANE, [(i, i ^ step) for i in range(lax.axis_size(PL...]
    all_to_all x0 -> x1, starting transfers between devices: none -> 4.98 us  [swap_blocks(): return lax.all_to_all(blocks, axes, split_axis=0, concat_axis=0, tiled=True)]
    ppermute x10, waiting for transfers between devices: 4.74 us -> 9.72 us  [swap_pairs(): lax.ppermute(value, axis, [(i, i ^ step) for i in range(lax.axis_size(axi...]
    all_to_all x0 -> x1, waiting for transfers between devices: none -> 4.02 us  [swap_blocks(): return lax.all_to_all(blocks, axes, split_axis=0, concat_axis=0, tiled=True)]
    pallas_call x1, Pallas kernels: 1.12 us -> 2.26 us  [shards(): pl.pallas_call(functools.partial(attend_kernel, wide, plane, rows, early,...]
  transfers between devices with their start and end apart: 18 -> 19, of which waited for: 8 -> 11; matrix products, arithmetic and copies ran while one was open for 0% -> 0% of each run, Pallas kernels for 9% -> 9%
where the time goes in v14:
time: 89.1 us; the launch traced here: 88.6 us
  starting transfers between devices  26.2 us (29%)
  Pallas kernels  25.1 us (28%)
  local copies, waits for them, and re-layouts  19.7 us (22%)
  waiting for transfers between devices  17.4 us (20%)
    unnamed x42, local copies, waits for them, and re-layouts  19.7 us
    ppermute x10, starting transfers between devices, swap_pairs(): lax.ppermute(value, axis, [(i, i ^ step) for i in range(lax.axis_size(axi...  13.9 us
    pallas_call x1, Pallas kernels, shards(): pl.pallas_call(functools.partial(early_kernel, early), out_shape=[jax.Sha...  13 us
    ppermute x10, waiting for transfers between devices, swap_pairs(): lax.ppermute(value, axis, [(i, i ^ step) for i in range(lax.axis_size(axi...  9.72 us
    ppermute x8, starting transfers between devices, swap_plane(): lax.ppermute(value, PLANE, [(i, i ^ step) for i in range(lax.axis_size(PL...  7.36 us
    all_to_all x1, starting transfers between devices, swap_blocks(): return lax.all_to_all(blocks, axes, split_axis=0, concat_axis=0, tiled=True)  4.98 us
    all_to_all x1, waiting for transfers between devices, swap_blocks(): return lax.all_to_all(blocks, axes, split_axis=0, concat_axis=0, tiled=True)  4.02 us
    ppermute x8, waiting for transfers between devices, swap_plane(): lax.ppermute(value, PLANE, [(i, i ^ step) for i in range(lax.axis_size(PL...  3.65 us
  transfers between devices with their start and end apart: 19, of which 11 were waited for; matrix products, arithmetic and copies ran while one was open for 0% of the time, Pallas kernels for 9%

profile of v14, /device:TPU:0, one launch (start us, length us, event | category | flops | bytes accessed | tf_op | source)
XLA Modules:
  0.0 88.6 jit_solution(1282176373884556315)
XLA Ops:
  0.0 13.0 %shard_map.103 = bf16[768,256]{1,0:T(8,128)(2,1)} custom-call(bf16[2,256,1024]{2,1,0:T(8,128)(2,1)} %keys_ref.3, bf16[2,256,1024]{2,1,0:T(8,128)(2,1)} %values_ref.3), custom_call_target="tpu_custom_call" | custom-call | flops 40000000000 | bytes 1048576 | tf_op jit(solution)/shard_map/pallas_call | solution.py:303
  13.0 0.0 copy-start.13
  13.1 0.0 copy-start.4
  13.1 0.0 copy-start.14
  13.1 0.0 copy-start.2
  13.1 3.0 %collective-permute-start.1 = (bf16[768,256]{1,0:T(8,128)(2,1)}, bf16[768,256]{1,0:T(8,128)(2,1)}, u32[]{:S(2)}, u32[]{:S(2)}) collective-permute-start(bf16[768,256]{1,0:T(8,128)(2,1)} %shard_map.103), channel_id=1, source_target_pairs={{0,2},{1,3},{2,0},{3,1},{4,6},{5,7},{6,4},{7,5},{8,10},{9,11},{10,... | collective-permute-start | bytes 1179656 | tf_op jit(solution)/shard_map/ppermute | solution.py:263
  16.1 0.2 shard_map.100.scaled_ref
  16.4 0.8 shard_map.101._
  17.1 5.0 %all-to-all-start = ((bf16[16,2,2048]{2,1,0:T(2,128)(2,1)}), bf16[16,2,2048]{2,1,0:T(2,128)(2,1)S(1)}, u32[]{:S(2)}, u32[]{:S(2)}) async-start(bf16[16,2,2048]{2,1,0:T(2,128)(2,1)} %shard_map.101._), calls=%async_computation | async-start | bytes 262144 | tf_op jit(solution)/shard_map/all_to_all | solution.py:255
  22.1 0.0 copy-start.5
  22.1 1.2 %copy-done.5 = bf16[2,256,1024]{2,1,0:T(8,128)(2,1)S(1)} copy-done((bf16[2,256,1024]{2,1,0:T(8,128)(2,1)S(1)}, bf16[2,256,1024]{2,1,0:T(8,128)(2,1)}, u32[]{:S(2)}) %copy-start.5) | copy-done | bytes 1048600
  23.3 1.1 %shard_map.102 = (bf16[272,256]{1,0:T(8,128)(2,1)S(1)}, bf16[1040,256]{1,0:T(8,128)(2,1)S(1)}, bf16[1040,256]{1,0:T(8,128)(2,1)S(1)}) custom-call(s32[1,2]{1,0:T(1,128)S(1)} %bitcast.5, bf16[2,256,1024]{2,1,0:T(8,128)(2,1)S(1)} %copy-done.4, bf16[2,256,1024]{2,1,0:T(8,128)(2,1)S(1)} %copy-done.5, bf16[16,2,2048]{2,1,0:T(2,128)(2,1)} %shard_map.101._), custom_call_target="tpu_custom_call" | custom-call | tf_op jit(solution)/shard_map/pallas_call | solution.py:331
  24.4 0.8 copy-done.7
  25.2 0.8 copy-done.10
  26.0 4.0 %all-to-all-done.refs_3_.rows_ref._ = bf16[16,2,2048]{2,1,0:T(2,128)(2,1)S(1)} async-done(((bf16[16,2,2048]{2,1,0:T(2,128)(2,1)}), bf16[16,2,2048]{2,1,0:T(2,128)(2,1)S(1)}, u32[]{:S(2)}, u32[]{:S(2)}) %all-to-all-start) | async-done | bytes 131104 | tf_op jit(solution)/shard_map/all_to_all | solution.py:255
  30.0 0.0 collective-permute-done.1.refs_4_
  30.0 1.0 %copy-done.8 = bf16[1040,256]{1,0:T(8,128)(2,1)S(1)} copy-done((bf16[1040,256]{1,0:T(8,128)(2,1)S(1)}, bf16[1040,256]{1,0:T(8,128)(2,1)}, u32[]{:S(2)}) %copy-start.8) | copy-done | bytes 532504
  31.1 1.0 %copy-done.11 = bf16[1040,256]{1,0:T(8,128)(2,1)S(1)} copy-done((bf16[1040,256]{1,0:T(8,128)(2,1)S(1)}, bf16[1040,256]{1,0:T(8,128)(2,1)}, u32[]{:S(2)}) %copy-start.11) | copy-done | bytes 532504
  32.1 0.8 copy-done.9
  32.9 0.8 copy-done.12
  33.7 0.0 collective-permute-start.2
  33.7 0.0 collective-permute-start.7
  33.7 0.5 collective-permute-start
  34.2 1.6 %collective-permute-start.6 = (bf16[272,256]{1,0:T(8,128)(2,1)S(1)}, bf16[272,256]{1,0:T(8,128)(2,1)S(1)}, u32[]{:S(2)}, u32[]{:S(2)}) collective-permute-start(bf16[272,256]{1,0:T(8,128)(2,1)S(1)} %get-tuple-element.35), channel_id=1, source_target_pairs={{0,2},{1,3},{2,0},{3,1},{4,6},{5,7},{6,4},{7,5},{8,10},{9,11},{10,... | collective-permute-start | bytes 417800 | tf_op jit(solution)/shard_map/ppermute | solution.py:263
  35.9 5.8 %copy-done = bf16[4096,2048]{1,0:T(8,128)(2,1)S(1)} copy-done((bf16[4096,2048]{1,0:T(8,128)(2,1)S(1)}, bf16[4096,2048]{1,0:T(8,128)(2,1)}, u32[]{:S(2)}) %copy-start) | copy-done | bytes 16777240
  41.6 1.6 %copy-done.3 = bf16[4096,256]{1,0:T(8,128)(2,1)S(1)} copy-done((bf16[4096,256]{1,0:T(8,128)(2,1)S(1)}, bf16[4096,256]{1,0:T(8,128)(2,1)}, u32[]{:S(2)}) %copy-start.3) | copy-done | bytes 2097176
  43.2 1.9 %shard_map.105.refs_1_ = f32[32,2560]{1,0:T(8,128)S(1)} custom-call(bf16[16,2,2048]{2,1,0:T(2,128)(2,1)S(1)} %all-to-all-done.refs_3_.rows_ref._, bf16[4096,2048]{1,0:T(8,128)(2,1)S(1)} %copy-done, bf16[4096,256]{1,0:T(8,128)(2,1)S(1)} %copy-done.2, bf16[4096,256]{1,0:T(8,128)(2,1)S(1)} %copy-done.3), custom_call_target="tpu_custom_call" | custom-call | flops 335544320 | bytes 10485760 | tf_op jit(solution)/shard_map/pallas_call | solution.py:364
  45.1 0.0 collective-permute-done.rows_ref
  45.1 0.0 collective-permute-done.2.refs_0_.refs_7_
  45.2 0.0 copy-start.1
  45.2 5.8 %copy-done.1 = bf16[4096,2048]{1,0:T(8,128)(2,1)S(1)} copy-done((bf16[4096,2048]{1,0:T(8,128)(2,1)S(1)}, bf16[4096,2048]{1,0:T(8,128)(2,1)}, u32[]{:S(2)}) %copy-start.1) | copy-done | bytes 16777240
  50.9 2.0 %shard_map.106 = (f32[4,2,2560]{2,1,0:T(2,128)S(1)}, f32[4,2,2560]{2,1,0:T(2,128)S(1)}, f32[4,2,2560]{2,1,0:T(2,128)S(1)}, f32[4,2,2560]{2,1,0:T(2,128)S(1)}) custom-call(bf16[16,2,2048]{2,1,0:T(2,128)(2,1)S(1)} %collective-permute-done.rows_ref, bf16[4096,2048]{1,0:T(8,128)(2,1)S(1)} %copy-done.1, bf16[4096,256]{1,0:T(8,128)(2,1)S(1)} %copy-done.2, ...), custom_call_target="tpu_custom_call" | custom-call | flops 335544320 | bytes 10485760 | tf_op jit(solution)/shard_map/pallas_call | solution.py:372
  52.9 1.0 %collective-permute-start.3 = (f32[4,2,2560]{2,1,0:T(2,128)S(1)}, f32[4,2,2560]{2,1,0:T(2,128)S(1)}, u32[]{:S(2)}, u32[]{:S(2)}) collective-permute-start(f32[4,2,2560]{2,1,0:T(2,128)S(1)} %get-tuple-element.31), channel_id=1, source_target_pairs={{0,12},{4,8},{8,4},{12,0},{1,13},{5,9},{9,5},{13,1},{2,14},{6,10},... | collective-permute-start | bytes 245768 | tf_op jit(solution)/shard_map/ppermute | solution.py:259
  53.9 0.6 collective-permute-start.4
  54.5 2.9 %collective-permute-start.5 = (f32[4,2,2560]{2,1,0:T(2,128)S(1)}, f32[4,2,2560]{2,1,0:T(2,128)S(1)}, u32[]{:S(2)}, u32[]{:S(2)}) collective-permute-start(f32[4,2,2560]{2,1,0:T(2,128)S(1)} %get-tuple-element.33), channel_id=1, source_target_pairs={{0,4},{4,0},{8,12},{12,8},{1,5},{5,1},{9,13},{13,9},{2,6},{6,2},{1... | collective-permute-start | bytes 245768 | tf_op jit(solution)/shard_map/ppermute | solution.py:259
  57.4 0.1 shard_map.107.refs_6_
  57.5 0.0 collective-permute-done.6.refs_5_
  57.5 0.0 collective-permute-done.7.refs_8_
  57.5 2.7 %collective-permute-done.3.refs_0_ = f32[4,2,2560]{2,1,0:T(2,128)S(1)} collective-permute-done((f32[4,2,2560]{2,1,0:T(2,128)S(1)}, f32[4,2,2560]{2,1,0:T(2,128)S(1)}, u32[]{:S(2)}, u32[]{:S(2)}) %collective-permute-start.3) | collective-permute-done | bytes 81952 | tf_op jit(solution)/shard_map/ppermute | solution.py:259
  60.2 2.3 %collective-permute-done.4.refs_1_ = f32[4,2,2560]{2,1,0:T(2,128)S(1)} collective-permute-done((f32[4,2,2560]{2,1,0:T(2,128)S(1)}, f32[4,2,2560]{2,1,0:T(2,128)S(1)}, u32[]{:S(2)}, u32[]{:S(2)}) %collective-permute-start.4) | collective-permute-done | bytes 81952 | tf_op jit(solution)/shard_map/ppermute | solution.py:259
  62.4 0.0 collective-permute-done.5.refs_2_
  62.4 2.3 %shard_map.108.refs_0_ = bf16[4,2,2048]{2,1,0:T(2,128)(2,1)S(1)} custom-call(f32[1,128]{1,0:T(1,128)S(1)} %copy-done.16, f32[4,2,2560]{2,1,0:T(2,128)S(1)} %collective-permute-done.3.refs_0_, f32[4,2,2560]{2,1,0:T(2,128)S(1)} %collective-permute-done.4.refs_1_, f32[4,2,2560]{2,1,0:T(2,128)S(1)} %collective-permute-done.5.refs_2_, ...), custom_call_target="tpu_custom_call" | custom-call | flops 10000000000 | bytes 4194304 | tf_op jit(solution)/shard_map/pallas_call | solution.py:386
  64.7 1.8 %collective-permute-start.10 = (bf16[4,2,2048]{2,1,0:T(2,128)(2,1)S(1)}, bf16[4,2,2048]{2,1,0:T(2,128)(2,1)S(1)}, u32[]{:S(2)}, u32[]{:S(2)}) collective-permute-start(bf16[4,2,2048]{2,1,0:T(2,128)(2,1)S(1)} %shard_map.108.refs_0_), channel_id=1, source_target_pairs={{0,12},{4,8},{8,4},{12,0},{1,13},{5,9},{9,5},{13,1},{2,14},{6,10},... | collective-permute-start | bytes 98312 | tf_op jit(solution)/shard_map/ppermute | solution.py:259
  66.5 2.6 %collective-permute-start.9 = (bf16[4,2,2048]{2,1,0:T(2,128)(2,1)S(1)}, bf16[4,2,2048]{2,1,0:T(2,128)(2,1)S(1)}, u32[]{:S(2)}, u32[]{:S(2)}) collective-permute-start(bf16[4,2,2048]{2,1,0:T(2,128)(2,1)S(1)} %shard_map.108.refs_0_), channel_id=1, source_target_pairs={{0,4},{4,0},{8,12},{12,8},{1,5},{5,1},{9,13},{13,9},{2,6},{6,2},{1... | collective-permute-start | bytes 98312 | tf_op jit(solution)/shard_map/ppermute | solution.py:259
  69.1 1.3 %collective-permute-done.10.refs_3_ = bf16[4,2,2048]{2,1,0:T(2,128)(2,1)S(1)} collective-permute-done((bf16[4,2,2048]{2,1,0:T(2,128)(2,1)S(1)}, bf16[4,2,2048]{2,1,0:T(2,128)(2,1)S(1)}, u32[]{:S(2)}, u32[]{:S(2)}) %collective-permute-start.10) | collective-permute-done | bytes 32800 | tf_op jit(solution)/shard_map/ppermute | solution.py:259
  70.5 0.9 %collective-permute-done.8.refs_1_ = bf16[4,2,2048]{2,1,0:T(2,128)(2,1)S(1)} collective-permute-done((bf16[4,2,2048]{2,1,0:T(2,128)(2,1)S(1)}, bf16[4,2,2048]{2,1,0:T(2,128)(2,1)S(1)}, u32[]{:S(2)}, u32[]{:S(2)}) %collective-permute-start.8) | collective-permute-done | bytes 32800 | tf_op jit(solution)/shard_map/ppermute | solution.py:259
  71.4 1.5 %shard_map.111 = (f32[8,2,2048]{2,1,0:T(2,128)S(1)}, f32[8,2,2048]{2,1,0:T(2,128)S(1)}) custom-call(bf16[2048,4096]{1,0:T(8,128)(2,1)S(1)} %bitcast.3, bf16[4,2,2048]{2,1,0:T(2,128)(2,1)S(1)} %shard_map.108.refs_0_, bf16[4,2,2048]{2,1,0:T(2,128)(2,1)S(1)} %collective-permute-done.8.refs_1_, bf16[4,2,2048]{2,1,0:T(2,128)(2,1)S(1)} %collective-permute-done.9.refs_2_, ...), custom_call_target="tpu_custom_call" | custom-call | flops 268435456 | bytes 8388608 | tf_op jit(solution)/shard_map/pallas_call | solution.py:402
  73.0 0.1 collective-permute-start.13
  73.1 1.5 %shard_map.109 = (f32[8,2,2048]{2,1,0:T(2,128)S(1)}, f32[8,2,2048]{2,1,0:T(2,128)S(1)}) custom-call(bf16[2048,4096]{1,0:T(8,128)(2,1)S(1)} %bitcast.3, bf16[4,2,2048]{2,1,0:T(2,128)(2,1)S(1)} %shard_map.108.refs_0_, bf16[4,2,2048]{2,1,0:T(2,128)(2,1)S(1)} %collective-permute-done.8.refs_1_, bf16[4,2,2048]{2,1,0:T(2,128)(2,1)S(1)} %collective-permute-done.9.refs_2_, ...), custom_call_target="tpu_custom_call" | custom-call | flops 268435456 | bytes 8388608 | tf_op jit(solution)/shard_map/pallas_call | solution.py:402
  74.6 0.6 collective-permute-start.11
  75.2 0.0 collective-permute-done.13.b_ref
  75.2 0.9 %collective-permute-start.14 = (f32[4,2,2048]{2,1,0:T(2,128)S(1)}, f32[4,2,2048]{2,1,0:T(2,128)S(1)}, u32[]{:S(2)}, u32[]{:S(2)}) collective-permute-start(f32[4,2,2048]{2,1,0:T(2,128)S(1)} %get-tuple-element.44), channel_id=1, source_target_pairs={{0,2},{1,3},{2,0},{3,1},{4,6},{5,7},{6,4},{7,5},{8,10},{9,11},{10,... | collective-permute-start | bytes 196616 | tf_op jit(solution)/shard_map/ppermute | solution.py:263
  76.1 0.1 collective-permute-done.11.b_ref
  76.2 1.2 %collective-permute-start.12 = (f32[4,2,2048]{2,1,0:T(2,128)S(1)}, f32[4,2,2048]{2,1,0:T(2,128)S(1)}, u32[]{:S(2)}, u32[]{:S(2)}) collective-permute-start(f32[4,2,2048]{2,1,0:T(2,128)S(1)} %get-tuple-element.40), channel_id=1, source_target_pairs={{0,2},{1,3},{2,0},{3,1},{4,6},{5,7},{6,4},{7,5},{8,10},{9,11},{10,... | collective-permute-start | bytes 196616 | tf_op jit(solution)/shard_map/ppermute | solution.py:263
  77.4 2.6 %collective-permute-done.14.refs_3_ = f32[4,2,2048]{2,1,0:T(2,128)S(1)} collective-permute-done((f32[4,2,2048]{2,1,0:T(2,128)S(1)}, f32[4,2,2048]{2,1,0:T(2,128)S(1)}, u32[]{:S(2)}, u32[]{:S(2)}) %collective-permute-start.14) | collective-permute-done | bytes 65568 | tf_op jit(solution)/shard_map/ppermute | solution.py:263
  79.9 1.0 %collective-permute-done.12.refs_1_ = f32[4,2,2048]{2,1,0:T(2,128)S(1)} collective-permute-done((f32[4,2,2048]{2,1,0:T(2,128)S(1)}, f32[4,2,2048]{2,1,0:T(2,128)S(1)}, u32[]{:S(2)}, u32[]{:S(2)}) %collective-permute-start.12) | collective-permute-done | bytes 65568 | tf_op jit(solution)/shard_map/ppermute | solution.py:263
  80.9 0.1 shard_map.113
  81.0 2.1 %collective-permute-start.15 = (bf16[2,4096]{1,0:T(2,128)(2,1)S(1)}, bf16[2,4096]{1,0:T(2,128)(2,1)S(1)}, u32[]{:S(2)}, u32[]{:S(2)}) collective-permute-start(bf16[2,4096]{1,0:T(2,128)(2,1)S(1)} %get-tuple-element.45), channel_id=1, source_target_pairs={{0,12},{4,8},{8,4},{12,0},{1,13},{5,9},{9,5},{13,1},{2,14},{6,10},... | collective-permute-start | bytes 49160 | tf_op jit(solution)/shard_map/ppermute | solution.py:259
  83.1 1.1 %collective-permute-start.16 = (bf16[2,4096]{1,0:T(2,128)(2,1)S(1)}, bf16[2,4096]{1,0:T(2,128)(2,1)S(1)}, u32[]{:S(2)}, u32[]{:S(2)}) collective-permute-start(bf16[2,4096]{1,0:T(2,128)(2,1)S(1)} %get-tuple-element.46), channel_id=1, source_target_pairs={{0,8},{4,12},{8,0},{12,4},{1,9},{5,13},{9,1},{13,5},{2,10},{6,14},... | collective-permute-start | bytes 49160 | tf_op jit(solution)/shard_map/ppermute | solution.py:259
  84.2 1.3 %collective-permute-start.17 = (bf16[2,4096]{1,0:T(2,128)(2,1)S(1)}, bf16[2,4096]{1,0:T(2,128)(2,1)S(1)}, u32[]{:S(2)}, u32[]{:S(2)}) collective-permute-start(bf16[2,4096]{1,0:T(2,128)(2,1)S(1)} %get-tuple-element.47), channel_id=1, source_target_pairs={{0,4},{4,0},{8,12},{12,8},{1,5},{5,1},{9,13},{13,9},{2,6},{6,2},{1... | collective-permute-start | bytes 49160 | tf_op jit(solution)/shard_map/ppermute | solution.py:259
  85.5 1.1 %collective-permute-done.15.refs_0_ = bf16[2,4096]{1,0:T(2,128)(2,1)S(1)} collective-permute-done((bf16[2,4096]{1,0:T(2,128)(2,1)S(1)}, bf16[2,4096]{1,0:T(2,128)(2,1)S(1)}, u32[]{:S(2)}, u32[]{:S(2)}) %collective-permute-start.15) | collective-permute-done | bytes 16416 | tf_op jit(solution)/shard_map/ppermute | solution.py:259
  86.6 1.2 %collective-permute-done.16.refs_1_ = bf16[2,4096]{1,0:T(2,128)(2,1)S(1)} collective-permute-done((bf16[2,4096]{1,0:T(2,128)(2,1)S(1)}, bf16[2,4096]{1,0:T(2,128)(2,1)S(1)}, u32[]{:S(2)}, u32[]{:S(2)}) %collective-permute-start.16) | collective-permute-done | bytes 16416 | tf_op jit(solution)/shard_map/ppermute | solution.py:259
  87.8 0.2 collective-permute-done.17.refs_2_
  88.0 0.6 shard_map.114
  (32 shorter events, 0.1 us)
Async XLA Ops:
  0.0 16.1 %copy-start.15 = (bf16[2,16384]{1,0:T(2,128)(2,1)S(1)}, bf16[2,16384]{1,0:T(2,128)(2,1)}, u32[]{:S(2)}) copy-start(bf16[2,16384]{1,0:T(2,128)(2,1)} %tokens_ref.1) | copy-start | bytes 196612
  13.0 3.3 %copy-start.13 = (f32[16384]{0:T(1024)S(1)}, f32[16384]{0:T(1024)}, u32[]{:S(2)}) copy-start(f32[16384]{0:T(1024)} %param.11) | copy-start | bytes 196612
  13.1 9.0 %copy-start.4 = (bf16[2,256,1024]{2,1,0:T(8,128)(2,1)S(1)}, bf16[2,256,1024]{2,1,0:T(8,128)(2,1)}, u32[]{:S(2)}) copy-start(bf16[2,256,1024]{2,1,0:T(8,128)(2,1)} %keys_ref.3) | copy-start | bytes 3145732
  13.1 9.0 %copy-start.14 = (s32[2]{0:T(128)S(1)}, s32[2]{0:T(128)}, u32[]{:S(2)}) copy-start(s32[2]{0:T(128)} %param.18) | copy-start | bytes 28
  13.1 22.8 %copy-start.2 = (bf16[4096,256]{1,0:T(8,128)(2,1)S(1)}, bf16[4096,256]{1,0:T(8,128)(2,1)}, u32[]{:S(2)}) copy-start(bf16[4096,256]{1,0:T(8,128)(2,1)} %key_ref.3) | copy-start | bytes 6291460
  13.1 16.9 %collective-permute-start.1 = (bf16[768,256]{1,0:T(8,128)(2,1)}, bf16[768,256]{1,0:T(8,128)(2,1)}, u32[]{:S(2)}, u32[]{:S(2)}) collective-permute-start(bf16[768,256]{1,0:T(8,128)(2,1)} %shard_map.103), channel_id=1, source_target_pairs={{0,2},{1,3},{2,0},{3,1},{4,6},{5,7},{6,4},{7,5},{8,10},{9,11},{10,... | collective-permute-start | bytes 1179656 | tf_op jit(solution)/shard_map/ppermute | solution.py:263
  17.1 12.9 %all-to-all-start = ((bf16[16,2,2048]{2,1,0:T(2,128)(2,1)}), bf16[16,2,2048]{2,1,0:T(2,128)(2,1)S(1)}, u32[]{:S(2)}, u32[]{:S(2)}) async-start(bf16[16,2,2048]{2,1,0:T(2,128)(2,1)} %shard_map.101._), calls=%async_computation | async-start | bytes 262144 | tf_op jit(solution)/shard_map/all_to_all | solution.py:255
  22.1 1.2 %copy-start.5 = (bf16[2,256,1024]{2,1,0:T(8,128)(2,1)S(1)}, bf16[2,256,1024]{2,1,0:T(8,128)(2,1)}, u32[]{:S(2)}) copy-start(bf16[2,256,1024]{2,1,0:T(8,128)(2,1)} %values_ref.3) | copy-start | bytes 3145732
  24.4 0.8 copy-start.7
  25.2 0.8 copy-start.10
  30.0 1.0 %copy-start.8 = (bf16[1040,256]{1,0:T(8,128)(2,1)S(1)}, bf16[1040,256]{1,0:T(8,128)(2,1)}, u32[]{:S(2)}) copy-start(bf16[1040,256]{1,0:T(8,128)(2,1)} %copy-done.7) | copy-start | bytes 1597444
  31.1 1.0 %copy-start.11 = (bf16[1040,256]{1,0:T(8,128)(2,1)S(1)}, bf16[1040,256]{1,0:T(8,128)(2,1)}, u32[]{:S(2)}) copy-start(bf16[1040,256]{1,0:T(8,128)(2,1)} %copy-done.10) | copy-start | bytes 1597444
  32.1 0.8 copy-start.9
  32.9 0.8 copy-start.12
  33.7 11.4 %collective-permute-start.2 = (bf16[1040,256]{1,0:T(8,128)(2,1)}, bf16[1040,256]{1,0:T(8,128)(2,1)S(1)}, u32[]{:S(2)}, u32[]{:S(2)}) collective-permute-start(bf16[1040,256]{1,0:T(8,128)(2,1)} %copy-done.9), channel_id=1, source_target_pairs={{0,1},{1,0},{2,3},{3,2},{4,5},{5,4},{6,7},{7,6},{8,9},{9,8},{10,11... | collective-permute-start | bytes 1597448 | tf_op jit(solution)/shard_map/ppermute | solution.py:263
  33.7 23.7 %collective-permute-start.7 = (bf16[1040,256]{1,0:T(8,128)(2,1)}, bf16[1040,256]{1,0:T(8,128)(2,1)S(1)}, u32[]{:S(2)}, u32[]{:S(2)}) collective-permute-start(bf16[1040,256]{1,0:T(8,128)(2,1)} %copy-done.12), channel_id=1, source_target_pairs={{0,3},{1,2},{2,1},{3,0},{4,7},{5,6},{6,5},{7,4},{8,11},{9,10},{10,... | collective-permute-start | bytes 1597448 | tf_op jit(solution)/shard_map/ppermute | solution.py:263
  33.7 11.4 %collective-permute-start = (bf16[16,2,2048]{2,1,0:T(2,128)(2,1)S(1)}, bf16[16,2,2048]{2,1,0:T(2,128)(2,1)S(1)}, u32[]{:S(2)}, u32[]{:S(2)}) collective-permute-start(bf16[16,2,2048]{2,1,0:T(2,128)(2,1)S(1)} %all-to-all-done.refs_3_.rows_ref._), channel_id=1, source_target_pairs={{0,1},{1,0},{2,3},{3,2},{4,5},{5,4},{6,7},{7,6},{8,9},{9,8},{10,11... | collective-permute-start | bytes 393224 | tf_op jit(solution)/shard_map/ppermute | solution.py:259
  34.2 23.2 %collective-permute-start.6 = (bf16[272,256]{1,0:T(8,128)(2,1)S(1)}, bf16[272,256]{1,0:T(8,128)(2,1)S(1)}, u32[]{:S(2)}, u32[]{:S(2)}) collective-permute-start(bf16[272,256]{1,0:T(8,128)(2,1)S(1)} %get-tuple-element.35), channel_id=1, source_target_pairs={{0,2},{1,3},{2,0},{3,1},{4,6},{5,7},{6,4},{7,5},{8,10},{9,11},{10,... | collective-permute-start | bytes 417800 | tf_op jit(solution)/shard_map/ppermute | solution.py:263
  35.9 5.8 %copy-start = (bf16[4096,2048]{1,0:T(8,128)(2,1)S(1)}, bf16[4096,2048]{1,0:T(8,128)(2,1)}, u32[]{:S(2)}) copy-start(bf16[4096,2048]{1,0:T(8,128)(2,1)} %query_ref.3) | copy-start | bytes 50331652
  41.6 1.6 %copy-start.3 = (bf16[4096,256]{1,0:T(8,128)(2,1)S(1)}, bf16[4096,256]{1,0:T(8,128)(2,1)}, u32[]{:S(2)}) copy-start(bf16[4096,256]{1,0:T(8,128)(2,1)} %value_ref.3) | copy-start | bytes 6291460
  43.2 14.1 %copy-start.6 = (bf16[2,256,1024]{2,1,0:T(8,128)(2,1)S(1)}, bf16[2,256,1024]{2,1,0:T(8,128)(2,1)}, u32[]{:S(2)}) copy-start(bf16[2,256,1024]{2,1,0:T(8,128)(2,1)} %values_ref.3) | copy-start | bytes 3145732
  43.2 19.2 %copy-start.16 = (f32[1,128]{1,0:T(1,128)S(1)}, f32[1,128]{1,0:T(1,128)}, u32[]{:S(2)}) copy-start(f32[1,128]{1,0:T(1,128)} %constant.2.clone.frequency_ref) | copy-start | bytes 1540
  45.2 5.8 %copy-start.1 = (bf16[4096,2048]{1,0:T(8,128)(2,1)S(1)}, bf16[4096,2048]{1,0:T(8,128)(2,1)}, u32[]{:S(2)}) copy-start(bf16[4096,2048]{1,0:T(8,128)(2,1)} %query_ref.3) | copy-start | bytes 50331652
  50.9 20.5 %slice-start = ((s8[16777216]{0:T(1024)(128)(4,1)}), s8[4194304]{0:T(1024)(128)(4,1)S(1)}, s32[]{:S(2)}) async-start(s8[16777216]{0:T(1024)(128)(4,1)} %bitcast.2), calls=%async_computation.1 | async-start | bytes 8388608
  50.9 20.5 %slice-start.1 = ((s8[16777216]{0:T(1024)(128)(4,1)}), s8[4194304]{0:T(1024)(128)(4,1)S(1)}, s32[]{:S(2)}) async-start(s8[16777216]{0:T(1024)(128)(4,1)} %bitcast.2), calls=%async_computation.2 | async-start | bytes 8388608
  52.9 7.2 %collective-permute-start.3 = (f32[4,2,2560]{2,1,0:T(2,128)S(1)}, f32[4,2,2560]{2,1,0:T(2,128)S(1)}, u32[]{:S(2)}, u32[]{:S(2)}) collective-permute-start(f32[4,2,2560]{2,1,0:T(2,128)S(1)} %get-tuple-element.31), channel_id=1, source_target_pairs={{0,12},{4,8},{8,4},{12,0},{1,13},{5,9},{9,5},{13,1},{2,14},{6,10},... | collective-permute-start | bytes 245768 | tf_op jit(solution)/shard_map/ppermute | solution.py:259
  53.9 8.5 %collective-permute-start.4 = (f32[4,2,2560]{2,1,0:T(2,128)S(1)}, f32[4,2,2560]{2,1,0:T(2,128)S(1)}, u32[]{:S(2)}, u32[]{:S(2)}) collective-permute-start(f32[4,2,2560]{2,1,0:T(2,128)S(1)} %get-tuple-element.32), channel_id=1, source_target_pairs={{0,8},{4,12},{8,0},{12,4},{1,9},{5,13},{9,1},{13,5},{2,10},{6,14},... | collective-permute-start | bytes 245768 | tf_op jit(solution)/shard_map/ppermute | solution.py:259
  54.5 7.9 %collective-permute-start.5 = (f32[4,2,2560]{2,1,0:T(2,128)S(1)}, f32[4,2,2560]{2,1,0:T(2,128)S(1)}, u32[]{:S(2)}, u32[]{:S(2)}) collective-permute-start(f32[4,2,2560]{2,1,0:T(2,128)S(1)} %get-tuple-element.33), channel_id=1, source_target_pairs={{0,4},{4,0},{8,12},{12,8},{1,5},{5,1},{9,13},{13,9},{2,6},{6,2},{1... | collective-permute-start | bytes 245768 | tf_op jit(solution)/shard_map/ppermute | solution.py:259
  62.4 9.0 %slice-start.2 = ((s8[16777216]{0:T(1024)(128)(4,1)}), s8[4194304]{0:T(1024)(128)(4,1)S(1)}, s32[]{:S(2)}) async-start(s8[16777216]{0:T(1024)(128)(4,1)} %bitcast.2), calls=%async_computation.3 | async-start | bytes 8388608
  62.4 9.0 %slice-start.3 = ((s8[16777216]{0:T(1024)(128)(4,1)}), s8[4194304]{0:T(1024)(128)(4,1)S(1)}, s32[]{:S(2)}) async-start(s8[16777216]{0:T(1024)(128)(4,1)} %bitcast.2), calls=%async_computation.4 | async-start | bytes 8388608
  64.7 5.8 %collective-permute-start.10 = (bf16[4,2,2048]{2,1,0:T(2,128)(2,1)S(1)}, bf16[4,2,2048]{2,1,0:T(2,128)(2,1)S(1)}, u32[]{:S(2)}, u32[]{:S(2)}) collective-permute-start(bf16[4,2,2048]{2,1,0:T(2,128)(2,1)S(1)} %shard_map.108.refs_0_), channel_id=1, source_target_pairs={{0,12},{4,8},{8,4},{12,0},{1,13},{5,9},{9,5},{13,1},{2,14},{6,10},... | collective-permute-start | bytes 98312 | tf_op jit(solution)/shard_map/ppermute | solution.py:259
  66.5 4.9 %collective-permute-start.8 = (bf16[4,2,2048]{2,1,0:T(2,128)(2,1)S(1)}, bf16[4,2,2048]{2,1,0:T(2,128)(2,1)S(1)}, u32[]{:S(2)}, u32[]{:S(2)}) collective-permute-start(bf16[4,2,2048]{2,1,0:T(2,128)(2,1)S(1)} %shard_map.108.refs_0_), channel_id=1, source_target_pairs={{0,8},{4,12},{8,0},{12,4},{1,9},{5,13},{9,1},{13,5},{2,10},{6,14},... | collective-permute-start | bytes 98312 | tf_op jit(solution)/shard_map/ppermute | solution.py:259
  66.5 4.9 %collective-permute-start.9 = (bf16[4,2,2048]{2,1,0:T(2,128)(2,1)S(1)}, bf16[4,2,2048]{2,1,0:T(2,128)(2,1)S(1)}, u32[]{:S(2)}, u32[]{:S(2)}) collective-permute-start(bf16[4,2,2048]{2,1,0:T(2,128)(2,1)S(1)} %shard_map.108.refs_0_), channel_id=1, source_target_pairs={{0,4},{4,0},{8,12},{12,8},{1,5},{5,1},{9,13},{13,9},{2,6},{6,2},{1... | collective-permute-start | bytes 98312 | tf_op jit(solution)/shard_map/ppermute | solution.py:259
  73.0 2.2 %collective-permute-start.13 = (f32[8,2,2048]{2,1,0:T(2,128)S(1)}, f32[8,2,2048]{2,1,0:T(2,128)S(1)}, u32[]{:S(2)}, u32[]{:S(2)}) collective-permute-start(f32[8,2,2048]{2,1,0:T(2,128)S(1)} %get-tuple-element.42), channel_id=1, source_target_pairs={{0,1},{1,0},{2,3},{3,2},{4,5},{5,4},{6,7},{7,6},{8,9},{9,8},{10,11... | collective-permute-start | bytes 393224 | tf_op jit(solution)/shard_map/ppermute | solution.py:263
  74.6 1.5 %collective-permute-start.11 = (f32[8,2,2048]{2,1,0:T(2,128)S(1)}, f32[8,2,2048]{2,1,0:T(2,128)S(1)}, u32[]{:S(2)}, u32[]{:S(2)}) collective-permute-start(f32[8,2,2048]{2,1,0:T(2,128)S(1)} %get-tuple-element.38), channel_id=1, source_target_pairs={{0,1},{1,0},{2,3},{3,2},{4,5},{5,4},{6,7},{7,6},{8,9},{9,8},{10,11... | collective-permute-start | bytes 393224 | tf_op jit(solution)/shard_map/ppermute | solution.py:263
  75.2 4.7 %collective-permute-start.14 = (f32[4,2,2048]{2,1,0:T(2,128)S(1)}, f32[4,2,2048]{2,1,0:T(2,128)S(1)}, u32[]{:S(2)}, u32[]{:S(2)}) collective-permute-start(f32[4,2,2048]{2,1,0:T(2,128)S(1)} %get-tuple-element.44), channel_id=1, source_target_pairs={{0,2},{1,3},{2,0},{3,1},{4,6},{5,7},{6,4},{7,5},{8,10},{9,11},{10,... | collective-permute-start | bytes 196616 | tf_op jit(solution)/shard_map/ppermute | solution.py:263
  76.2 4.8 %collective-permute-start.12 = (f32[4,2,2048]{2,1,0:T(2,128)S(1)}, f32[4,2,2048]{2,1,0:T(2,128)S(1)}, u32[]{:S(2)}, u32[]{:S(2)}) collective-permute-start(f32[4,2,2048]{2,1,0:T(2,128)S(1)} %get-tuple-element.40), channel_id=1, source_target_pairs={{0,2},{1,3},{2,0},{3,1},{4,6},{5,7},{6,4},{7,5},{8,10},{9,11},{10,... | collective-permute-start | bytes 196616 | tf_op jit(solution)/shard_map/ppermute | solution.py:263
  81.0 5.6 %collective-permute-start.15 = (bf16[2,4096]{1,0:T(2,128)(2,1)S(1)}, bf16[2,4096]{1,0:T(2,128)(2,1)S(1)}, u32[]{:S(2)}, u32[]{:S(2)}) collective-permute-start(bf16[2,4096]{1,0:T(2,128)(2,1)S(1)} %get-tuple-element.45), channel_id=1, source_target_pairs={{0,12},{4,8},{8,4},{12,0},{1,13},{5,9},{9,5},{13,1},{2,14},{6,10},... | collective-permute-start | bytes 49160 | tf_op jit(solution)/shard_map/ppermute | solution.py:259
  83.1 4.7 %collective-permute-start.16 = (bf16[2,4096]{1,0:T(2,128)(2,1)S(1)}, bf16[2,4096]{1,0:T(2,128)(2,1)S(1)}, u32[]{:S(2)}, u32[]{:S(2)}) collective-permute-start(bf16[2,4096]{1,0:T(2,128)(2,1)S(1)} %get-tuple-element.46), channel_id=1, source_target_pairs={{0,8},{4,12},{8,0},{12,4},{1,9},{5,13},{9,1},{13,5},{2,10},{6,14},... | collective-permute-start | bytes 49160 | tf_op jit(solution)/shard_map/ppermute | solution.py:259
  84.2 3.8 %collective-permute-start.17 = (bf16[2,4096]{1,0:T(2,128)(2,1)S(1)}, bf16[2,4096]{1,0:T(2,128)(2,1)S(1)}, u32[]{:S(2)}, u32[]{:S(2)}) collective-permute-start(bf16[2,4096]{1,0:T(2,128)(2,1)S(1)} %get-tuple-element.47), channel_id=1, source_target_pairs={{0,4},{4,0},{8,12},{12,8},{1,5},{5,1},{9,13},{13,9},{2,6},{6,2},{1... | collective-permute-start | bytes 49160 | tf_op jit(solution)/shard_map/ppermute | solution.py:259

commit v15 on v13

--- a/solution.py
+++ b/solution.py
@@ -22,7 +22,7 @@
     scaled_ref[...] = tokens * lax.rsqrt(mean_square + 1e-05)
 
 
-def gain_kernel(wide, plane, scaled_ref, gain_ref, blocks_ref):
+def gain_kernel(wide, plane, scaled_ref, gain_ref, _, blocks_ref):
     normed = (scaled_ref[...] * gain_ref[...]).astype(jnp.bfloat16)
     half = normed.shape[1] // wide // 2
     for i in range(wide):
@@ -87,6 +87,32 @@
             write_lengths(rows, lengths_ref, block)
 
 
+def early_kernel(early, keys_ref, *blocks):
+    rows, slots, _ = keys_ref.shape
+    cols = blocks[0].shape[1]
+    for s, block in enumerate(blocks):
+        wanted = [(2 * s + 2, r) for r in range(rows)] + [(2 * s + 3, r) for r in range(early)]
+        for n, (slot, r) in enumerate(wanted):
+            at = pl.multiple_of((own_place() ^ slot) * cols, cols)
+            block[n * slots : (n + 1) * slots] = keys_ref[r, :, pl.ds(at, cols)]
+
+
+def near_kernel(early, lengths_ref, keys_ref, values_ref, _, *refs):
+    firsts, near_ref = refs[:-1], refs[-1]
+    rows, slots, _ = keys_ref.shape
+    cols = near_ref.shape[1]
+    at = pl.multiple_of((own_place() ^ 1) * cols, cols)
+    n = 0
+    for cache_ref in (keys_ref, values_ref):
+        for r in range(rows):
+            near_ref[n * slots : (n + 1) * slots] = cache_ref[r, :, pl.ds(at, cols)]
+            n += 1
+    for first in firsts:
+        near_ref[n * slots : (n + early) * slots] = first[rows * slots :]
+        n += early
+    write_lengths(rows, lengths_ref, near_ref)
+
+
 def pass_kernel(*refs):
     pass
 
@@ -94,8 +120,20 @@
 def attend_kernel(wide, plane, rows, early, query_cols, frequency_ref, *refs):
     partials, held, attended_ref = refs[wide - 1 :: -1], refs[wide:-1], refs[-1]
     even = plane // 2 - 1
-    firsts, lasts, whole = held[:even], held[even : 2 * even], held[2 * even :]
-    slots = (whole[0].shape[0] - 16) // (2 * rows)
+    mine, near = held[:2]
+    firsts, lasts, odds = held[2 : 2 + even], held[2 + even : 2 + 2 * even], held[2 + 2 * even :]
+    slots = (mine.shape[0] - 16) // (2 * rows)
+
+    def place(l, values, r):
+        s = l // 2 - 1
+        if l < 2:
+            return (mine, near)[l], values * rows + r
+        if l % 2 == 0:
+            return (lasts if values else firsts)[s], r
+        if values:
+            return odds[s], rows - early + r
+        return (near, 2 * rows + s * early + r) if r < early else (odds[s], r - early)
+
     cols = partials[0].shape[-1]
     kv_cols = (cols - query_cols) // 2
     kv_heads, group = kv_cols // HD, query_cols // kv_cols
@@ -111,18 +149,13 @@
     def cached(values):
         parts = []
         for p in range(pairs):
-            l, r = p // rows, p % rows
-            ref, at = whole[(l + 1) // 2], values * rows + r
-            if l % 2 == 0 and l:
-                ref = firsts[l // 2 - 1]
-                if at >= rows + early:
-                    ref, at = lasts[l // 2 - 1], at - rows - early
+            ref, at = place(p // rows, values, p % rows)
             parts.append(ref[at * slots : (at + 1) * slots])
         return jnp.concatenate(parts, 1)
 
     filled = []
     for l in range(plane):
-        block = lasts[l // 2 - 1] if l % 2 == 0 and l else whole[(l + 1) // 2]
+        block = place(l, 1, 0)[0]
         last = block[block.shape[0] - 16 :, :HD].astype(jnp.float32)
         filled += [last[r : r + 1] for r in range(rows)]
     angles = jnp.concatenate(filled, 0) * frequency_ref[...]
@@ -273,6 +306,22 @@
         return pl.CostEstimate(flops=flops, bytes_accessed=size, transcendentals=0)
 
     half = width // 2
+    slots = cache_keys.shape[1]
+    even = plane // 2 - 1
+    early = rows // 2
+    every = range(rows)
+
+    firsts = pl.pallas_call(
+        functools.partial(early_kernel, early),
+        out_shape=[
+            jax.ShapeDtypeStruct(((rows + early) * slots, kv_cols), cache_keys.dtype)
+        ] * even,
+        in_specs=[IN_VMEM],
+        out_specs=[IN_VMEM] * even,
+        compiler_params=params(8),
+        cost_estimate=cost(40 * 10**9, MIB),
+    )(cache_keys)
+    firsts = [swap_plane(firsts[s], 2 * s + 2) for s in range(even)]
     scaled = pl.pallas_call(
         scale_kernel,
         out_shape=jax.ShapeDtypeStruct(tokens.shape, jnp.float32),
@@ -281,18 +330,6 @@
         compiler_params=params(8),
         cost_estimate=cost(40 * 10**9, MIB),
     )(tokens)
-    normed = pl.pallas_call(
-        functools.partial(gain_kernel, wide, plane),
-        out_shape=jax.ShapeDtypeStruct((owners, rows, half), jnp.bfloat16),
-        in_specs=[IN_VMEM, IN_VMEM],
-        out_specs=IN_VMEM,
-        compiler_params=params(8),
-    )(scaled, norm_gain.reshape(1, -1))
-    slots = cache_keys.shape[1]
-    even = plane // 2 - 1
-    early = rows // 2
-    every = range(rows)
-
     def cut(plan, after):
         return pl.pallas_call(
             functools.partial(cut_kernel, plan),
@@ -308,12 +345,16 @@
             compiler_params=params(8),
         )(lengths.reshape(1, -1), cache_keys, cache_values, after)
 
-    plan = [(l, every, every[:early], False) for l in range(2, plane, 2)]
-    plan += [(l, (), every[early:], True) for l in range(2, plane, 2)]
-    plan += [(l, every, every, True) for l in range(1, plane, 2)]
-    blocks = cut(plan, normed)
-    firsts, rest = blocks[:even], blocks[even:]
-    firsts = [swap_plane(firsts[s], 2 * s + 2) for s in range(even)]
+    plan = [(l, (), every, True) for l in range(2, plane, 2)]
+    plan += [(l, every[early:], every, True) for l in range(3, plane, 2)]
+    rest = cut(plan, scaled)
+    normed = pl.pallas_call(
+        functools.partial(gain_kernel, wide, plane),
+        out_shape=jax.ShapeDtypeStruct((owners, rows, half), jnp.bfloat16),
+        in_specs=[IN_VMEM] * 3,
+        out_specs=IN_VMEM,
+        compiler_params=params(8),
+    )(scaled, norm_gain.reshape(1, -1), rest[0])
     own_half = swap_blocks(normed, ROW_AXES)
     other_half = swap_pairs(own_half, "gz", 1)
     rest = pl.pallas_call(
@@ -325,9 +366,19 @@
         compiler_params=params(1),
     )(*rest, own_half, *firsts)
     lasts = [swap_plane(rest[s], 2 * s + 2) for s in range(even)]
-    odd = [swap_plane(rest[even + s], 2 * s + 1) for s in range(even + 1)]
+    odds = [swap_plane(rest[even + s], 2 * s + 3) for s in range(even)]
+    near = pl.pallas_call(
+        functools.partial(near_kernel, early),
+        out_shape=jax.ShapeDtypeStruct(
+            ((2 * rows + even * early) * slots + 16, kv_cols), cache_keys.dtype
+        ),
+        in_specs=[IN_VMEM] * (4 + even),
+        out_specs=IN_VMEM,
+        compiler_params=params(8),
+    )(lengths.reshape(1, -1), cache_keys, cache_values, rest[0], *firsts)
+    near = swap_plane(near, 1)
     (mine,) = cut([(0, every, every, True)], own_half)
-    held = [*firsts, *lasts, mine, *odd]
+    held = [mine, near, *firsts, *lasts, *odds]
     weights = (query_weight, key_weight, value_weight)
     half_cost = cost(owners * rows * width * cols, width * cols)
     partial = pl.pallas_call(
@@ -346,7 +397,7 @@
         scratch_shapes=[pltpu.VMEM((owners, rows, cols), jnp.float32)],
         compiler_params=params(8),
         cost_estimate=half_cost,
-    )(other_half, *weights, odd[0], partial)
+    )(other_half, *weights, near, partial)
     partial = swap_wide(partial)
 
     half_dim = HD // 2

time: 60.5 us -> 61.4 us (1.015)
  blocking collectives: 13 us -> 13.7 us
    all_to_all x1, blocking collectives: 13 us -> 13.7 us  [swap_blocks(): return lax.all_to_all(blocks, axes, split_axis=0, concat_axis=0, tiled=True)]
    unnamed x26 -> x34, local copies, waits for them, and re-layouts: 1.27 us -> 1.32 us
  transfers between devices with their start and end apart: 18 -> 18, of which waited for: 8 -> 9; matrix products, arithmetic and copies ran while one was open for 0% -> 0% of each run, Pallas kernels for 9% -> 10%
where the time goes in v15:
time: 61.4 us; the launch traced here: 61.2 us
  starting transfers between devices  20.9 us (34%)
  waiting for transfers between devices  15.5 us (25%)
  blocking collectives  13.7 us (22%)
  Pallas kernels  9.43 us (15%)
  local copies, waits for them, and re-layouts  1.32 us (2%)
    all_to_all x1, blocking collectives, swap_blocks(): return lax.all_to_all(blocks, axes, split_axis=0, concat_axis=0, tiled=True)  13.7 us
    ppermute x10, starting transfers between devices, swap_pairs(): lax.ppermute(value, axis, [(i, i ^ step) for i in range(lax.axis_size(axi...  13.4 us
    ppermute x8, waiting for transfers between devices, swap_plane(): lax.ppermute(value, PLANE, [(i, i ^ step) for i in range(lax.axis_size(PL...  10.8 us
    ppermute x8, starting transfers between devices, swap_plane(): lax.ppermute(value, PLANE, [(i, i ^ step) for i in range(lax.axis_size(PL...  7.59 us
    ppermute x10, waiting for transfers between devices, swap_pairs(): lax.ppermute(value, axis, [(i, i ^ step) for i in range(lax.axis_size(axi...  4.75 us
    pallas_call x2, Pallas kernels, shards(): pl.pallas_call(functools.partial(output_kernel, p * part_cols, part_cols,...  3.1 us
    pallas_call x1, Pallas kernels, shards(): pl.pallas_call(functools.partial(project_kernel, False, wide, plane), out...  1.97 us
    pallas_call x1, Pallas kernels, shards(): pl.pallas_call(functools.partial(project_kernel, True, wide, plane), out_...  1.89 us
  transfers between devices with their start and end apart: 18, of which 9 were waited for; matrix products, arithmetic and copies ran while one was open for 0% of the time, Pallas kernels for 10%

profile of v15, /device:TPU:0, one launch (start us, length us, event | category | flops | bytes accessed | tf_op | source)
XLA Modules:
  0.0 61.2 jit_solution(11802823779251002156)
XLA Ops:
  0.0 1.2 %copy-done = bf16[2,256,1024]{2,1,0:T(8,128)(2,1)S(1)} copy-done((bf16[2,256,1024]{2,1,0:T(8,128)(2,1)S(1)}, bf16[2,256,1024]{2,1,0:T(8,128)(2,1)}, u32[]{:S(2)}) %copy-start) | copy-done | bytes 1048600
  1.2 0.1 shard_map.103
  1.3 0.0 copy-start.1
  1.3 0.0 copy-start.2
  1.3 0.0 copy-start.6
  1.3 0.0 copy-start.5
  1.3 0.0 slice-start.2
  1.3 0.0 slice-start.3
  1.4 0.0 copy-start.3
  1.4 0.0 copy-start.4
  1.4 3.0 %collective-permute-start.1 = (bf16[768,256]{1,0:T(8,128)(2,1)S(1)}, bf16[768,256]{1,0:T(8,128)(2,1)S(1)}, u32[]{:S(2)}, u32[]{:S(2)}) collective-permute-start(bf16[768,256]{1,0:T(8,128)(2,1)S(1)} %shard_map.103), channel_id=1, source_target_pairs={{0,2},{1,3},{2,0},{3,1},{4,6},{5,7},{6,4},{7,5},{8,10},{9,11},{10,... | collective-permute-start | bytes 1179656 | tf_op jit(solution)/shard_map/ppermute | solution.py:274
  4.4 0.2 shard_map.100._.scaled_ref
  4.7 0.1 shard_map.101
  4.8 0.1 shard_map.102
  4.9 13.7 %all_to_all.5.refs_2_.rows_ref._ = bf16[16,2,2048]{2,1,0:T(2,128)(2,1)S(1)} all-to-all(bf16[16,2,2048]{2,1,0:T(2,128)(2,1)S(1)} %shard_map.102), channel_id=1, replica_groups=mesh['groups'=2,'gx'=4,'gy'=2,'gz'=2] {'gx','gy','gz'}, dimensions={0} | all-to-all | bytes 262144 | tf_op jit(solution)/shard_map/all_to_all | solution.py:266
  18.5 0.0 collective-permute-done.1.refs_3_.refs_0_.refs_6_
  18.5 0.1 shard_map.105
  18.6 0.1 collective-permute-start.2
  18.7 0.1 collective-permute-start.7
  18.8 2.1 %collective-permute-start.6 = (bf16[528,256]{1,0:T(8,128)(2,1)S(1)}, bf16[528,256]{1,0:T(8,128)(2,1)S(1)}, u32[]{:S(2)}, u32[]{:S(2)}) collective-permute-start(bf16[528,256]{1,0:T(8,128)(2,1)S(1)} %get-tuple-element.27._), channel_id=1, source_target_pairs={{0,2},{1,3},{2,0},{3,1},{4,6},{5,7},{6,4},{7,5},{8,10},{9,11},{10,... | collective-permute-start | bytes 811016 | tf_op jit(solution)/shard_map/ppermute | solution.py:274
  20.9 0.0 collective-permute-start
  20.9 1.9 %shard_map.106.refs_1_ = f32[32,2560]{1,0:T(8,128)S(1)} custom-call(bf16[16,2,2048]{2,1,0:T(2,128)(2,1)S(1)} %all_to_all.5.refs_2_.rows_ref._, bf16[4096,2048]{1,0:T(8,128)(2,1)S(1)} %bitcast.3, bf16[4096,256]{1,0:T(8,128)(2,1)S(1)} %copy-done.3, bf16[4096,256]{1,0:T(8,128)(2,1)S(1)} %copy-done.4), custom_call_target="tpu_custom_call" | custom-call | flops 335544320 | bytes 10485760 | tf_op jit(solution)/shard_map/pallas_call | solution.py:384
  22.8 0.0 collective-permute-done.rows_ref
  22.8 0.0 collective-permute-done.2.refs_0_.refs_5_
  22.8 0.0 slice-start.4
  22.9 0.0 slice-start.5
  22.9 2.0 %shard_map.107 = (f32[4,2,2560]{2,1,0:T(2,128)S(1)}, f32[4,2,2560]{2,1,0:T(2,128)S(1)}, f32[4,2,2560]{2,1,0:T(2,128)S(1)}, f32[4,2,2560]{2,1,0:T(2,128)S(1)}) custom-call(bf16[16,2,2048]{2,1,0:T(2,128)(2,1)S(1)} %collective-permute-done.rows_ref, bf16[4096,2048]{1,0:T(8,128)(2,1)S(1)} %bitcast.3, bf16[4096,256]{1,0:T(8,128)(2,1)S(1)} %copy-done.3, ...), custom_call_target="tpu_custom_call" | custom-call | flops 335544320 | bytes 10485760 | tf_op jit(solution)/shard_map/pallas_call | solution.py:392
  24.8 0.8 %collective-permute-start.3 = (f32[4,2,2560]{2,1,0:T(2,128)S(1)}, f32[4,2,2560]{2,1,0:T(2,128)S(1)}, u32[]{:S(2)}, u32[]{:S(2)}) collective-permute-start(f32[4,2,2560]{2,1,0:T(2,128)S(1)} %get-tuple-element.28), channel_id=1, source_target_pairs={{0,12},{4,8},{8,4},{12,0},{1,13},{5,9},{9,5},{13,1},{2,14},{6,10},... | collective-permute-start | bytes 245768 | tf_op jit(solution)/shard_map/ppermute | solution.py:270
  25.6 0.5 collective-permute-start.4
  26.1 3.2 %collective-permute-start.5 = (f32[4,2,2560]{2,1,0:T(2,128)S(1)}, f32[4,2,2560]{2,1,0:T(2,128)S(1)}, u32[]{:S(2)}, u32[]{:S(2)}) collective-permute-start(f32[4,2,2560]{2,1,0:T(2,128)S(1)} %get-tuple-element.30), channel_id=1, source_target_pairs={{0,4},{4,0},{8,12},{12,8},{1,5},{5,1},{9,13},{13,9},{2,6},{6,2},{1... | collective-permute-start | bytes 245768 | tf_op jit(solution)/shard_map/ppermute | solution.py:270
  29.3 0.1 shard_map.108.refs_4_
  29.4 6.8 %collective-permute-done.6.refs_7_ = bf16[528,256]{1,0:T(8,128)(2,1)S(1)} collective-permute-done((bf16[528,256]{1,0:T(8,128)(2,1)S(1)}, bf16[528,256]{1,0:T(8,128)(2,1)S(1)}, u32[]{:S(2)}, u32[]{:S(2)}) %collective-permute-start.6) | collective-permute-done | bytes 270368 | tf_op jit(solution)/shard_map/ppermute | solution.py:274
  36.2 0.0 collective-permute-done.7.refs_8_
  36.2 0.0 collective-permute-done.3.refs_0_
  36.2 0.0 collective-permute-done.4.refs_1_
  36.2 0.0 collective-permute-done.5.refs_2_
  36.2 0.0 slice-start.6
  36.2 0.0 slice-start.7
  36.2 1.1 %shard_map.109.refs_0_ = bf16[4,2,2048]{2,1,0:T(2,128)(2,1)S(1)} custom-call(f32[1,128]{1,0:T(1,128)S(1)} %copy-done.8, f32[4,2,2560]{2,1,0:T(2,128)S(1)} %collective-permute-done.3.refs_0_, f32[4,2,2560]{2,1,0:T(2,128)S(1)} %collective-permute-done.4.refs_1_, f32[4,2,2560]{2,1,0:T(2,128)S(1)} %collective-permute-done.5.refs_2_, ...), custom_call_target="tpu_custom_call" | custom-call | flops 10000000000 | bytes 4194304 | tf_op jit(solution)/shard_map/pallas_call | solution.py:406
  37.3 0.9 %collective-permute-start.10 = (bf16[4,2,2048]{2,1,0:T(2,128)(2,1)S(1)}, bf16[4,2,2048]{2,1,0:T(2,128)(2,1)S(1)}, u32[]{:S(2)}, u32[]{:S(2)}) collective-permute-start(bf16[4,2,2048]{2,1,0:T(2,128)(2,1)S(1)} %shard_map.109.refs_0_), channel_id=1, source_target_pairs={{0,12},{4,8},{8,4},{12,0},{1,13},{5,9},{9,5},{13,1},{2,14},{6,10},... | collective-permute-start | bytes 98312 | tf_op jit(solution)/shard_map/ppermute | solution.py:270
  38.2 0.6 collective-permute-start.8
  38.8 3.0 %collective-permute-start.9 = (bf16[4,2,2048]{2,1,0:T(2,128)(2,1)S(1)}, bf16[4,2,2048]{2,1,0:T(2,128)(2,1)S(1)}, u32[]{:S(2)}, u32[]{:S(2)}) collective-permute-start(bf16[4,2,2048]{2,1,0:T(2,128)(2,1)S(1)} %shard_map.109.refs_0_), channel_id=1, source_target_pairs={{0,4},{4,0},{8,12},{12,8},{1,5},{5,1},{9,13},{13,9},{2,6},{6,2},{1... | collective-permute-start | bytes 98312 | tf_op jit(solution)/shard_map/ppermute | solution.py:270
  41.8 1.4 %collective-permute-done.10.refs_3_ = bf16[4,2,2048]{2,1,0:T(2,128)(2,1)S(1)} collective-permute-done((bf16[4,2,2048]{2,1,0:T(2,128)(2,1)S(1)}, bf16[4,2,2048]{2,1,0:T(2,128)(2,1)S(1)}, u32[]{:S(2)}, u32[]{:S(2)}) %collective-permute-start.10) | collective-permute-done | bytes 32800 | tf_op jit(solution)/shard_map/ppermute | solution.py:270
  43.2 0.6 %collective-permute-done.8.refs_1_ = bf16[4,2,2048]{2,1,0:T(2,128)(2,1)S(1)} collective-permute-done((bf16[4,2,2048]{2,1,0:T(2,128)(2,1)S(1)}, bf16[4,2,2048]{2,1,0:T(2,128)(2,1)S(1)}, u32[]{:S(2)}, u32[]{:S(2)}) %collective-permute-start.8) | collective-permute-done | bytes 32800 | tf_op jit(solution)/shard_map/ppermute | solution.py:270
  43.9 0.0 collective-permute-done.9.refs_2_
  43.9 0.0 slice-done.6
  43.9 1.5 %shard_map.112 = (f32[8,2,2048]{2,1,0:T(2,128)S(1)}, f32[8,2,2048]{2,1,0:T(2,128)S(1)}) custom-call(bf16[2048,4096]{1,0:T(8,128)(2,1)S(1)} %bitcast.5, bf16[4,2,2048]{2,1,0:T(2,128)(2,1)S(1)} %shard_map.109.refs_0_, bf16[4,2,2048]{2,1,0:T(2,128)(2,1)S(1)} %collective-permute-done.8.refs_1_, bf16[4,2,2048]{2,1,0:T(2,128)(2,1)S(1)} %collective-permute-done.9.refs_2_, ...), custom_call_target="tpu_custom_call" | custom-call | flops 268435456 | bytes 8388608 | tf_op jit(solution)/shard_map/pallas_call | solution.py:422
  45.5 0.1 collective-permute-start.13
  45.5 1.5 %shard_map.110 = (f32[8,2,2048]{2,1,0:T(2,128)S(1)}, f32[8,2,2048]{2,1,0:T(2,128)S(1)}) custom-call(bf16[2048,4096]{1,0:T(8,128)(2,1)S(1)} %bitcast.5, bf16[4,2,2048]{2,1,0:T(2,128)(2,1)S(1)} %shard_map.109.refs_0_, bf16[4,2,2048]{2,1,0:T(2,128)(2,1)S(1)} %collective-permute-done.8.refs_1_, bf16[4,2,2048]{2,1,0:T(2,128)(2,1)S(1)} %collective-permute-done.9.refs_2_, ...), custom_call_target="tpu_custom_call" | custom-call | flops 268435456 | bytes 8388608 | tf_op jit(solution)/shard_map/pallas_call | solution.py:422
  47.1 0.6 collective-permute-start.11
  47.6 0.0 collective-permute-done.13.b_ref
  47.7 0.6 collective-permute-start.14
  48.2 0.4 collective-permute-done.11.b_ref
  48.7 1.2 %collective-permute-start.12 = (f32[4,2,2048]{2,1,0:T(2,128)S(1)}, f32[4,2,2048]{2,1,0:T(2,128)S(1)}, u32[]{:S(2)}, u32[]{:S(2)}) collective-permute-start(f32[4,2,2048]{2,1,0:T(2,128)S(1)} %get-tuple-element.36), channel_id=1, source_target_pairs={{0,2},{1,3},{2,0},{3,1},{4,6},{5,7},{6,4},{7,5},{8,10},{9,11},{10,... | collective-permute-start | bytes 196616 | tf_op jit(solution)/shard_map/ppermute | solution.py:274
  49.8 2.6 %collective-permute-done.14.refs_3_ = f32[4,2,2048]{2,1,0:T(2,128)S(1)} collective-permute-done((f32[4,2,2048]{2,1,0:T(2,128)S(1)}, f32[4,2,2048]{2,1,0:T(2,128)S(1)}, u32[]{:S(2)}, u32[]{:S(2)}) %collective-permute-start.14) | collective-permute-done | bytes 65568 | tf_op jit(solution)/shard_map/ppermute | solution.py:274
  52.4 1.0 %collective-permute-done.12.refs_1_ = f32[4,2,2048]{2,1,0:T(2,128)S(1)} collective-permute-done((f32[4,2,2048]{2,1,0:T(2,128)S(1)}, f32[4,2,2048]{2,1,0:T(2,128)S(1)}, u32[]{:S(2)}, u32[]{:S(2)}) %collective-permute-start.12) | collective-permute-done | bytes 65568 | tf_op jit(solution)/shard_map/ppermute | solution.py:274
  53.4 0.1 shard_map.114
  53.5 2.3 %collective-permute-start.15 = (bf16[2,4096]{1,0:T(2,128)(2,1)S(1)}, bf16[2,4096]{1,0:T(2,128)(2,1)S(1)}, u32[]{:S(2)}, u32[]{:S(2)}) collective-permute-start(bf16[2,4096]{1,0:T(2,128)(2,1)S(1)} %get-tuple-element.41), channel_id=1, source_target_pairs={{0,12},{4,8},{8,4},{12,0},{1,13},{5,9},{9,5},{13,1},{2,14},{6,10},... | collective-permute-start | bytes 49160 | tf_op jit(solution)/shard_map/ppermute | solution.py:270
  55.7 1.1 %collective-permute-start.16 = (bf16[2,4096]{1,0:T(2,128)(2,1)S(1)}, bf16[2,4096]{1,0:T(2,128)(2,1)S(1)}, u32[]{:S(2)}, u32[]{:S(2)}) collective-permute-start(bf16[2,4096]{1,0:T(2,128)(2,1)S(1)} %get-tuple-element.42), channel_id=1, source_target_pairs={{0,8},{4,12},{8,0},{12,4},{1,9},{5,13},{9,1},{13,5},{2,10},{6,14},... | collective-permute-start | bytes 49160 | tf_op jit(solution)/shard_map/ppermute | solution.py:270
  56.8 1.1 %collective-permute-start.17 = (bf16[2,4096]{1,0:T(2,128)(2,1)S(1)}, bf16[2,4096]{1,0:T(2,128)(2,1)S(1)}, u32[]{:S(2)}, u32[]{:S(2)}) collective-permute-start(bf16[2,4096]{1,0:T(2,128)(2,1)S(1)} %get-tuple-element.43), channel_id=1, source_target_pairs={{0,4},{4,0},{8,12},{12,8},{1,5},{5,1},{9,13},{13,9},{2,6},{6,2},{1... | collective-permute-start | bytes 49160 | tf_op jit(solution)/shard_map/ppermute | solution.py:270
  57.9 1.2 %collective-permute-done.15.refs_0_ = bf16[2,4096]{1,0:T(2,128)(2,1)S(1)} collective-permute-done((bf16[2,4096]{1,0:T(2,128)(2,1)S(1)}, bf16[2,4096]{1,0:T(2,128)(2,1)S(1)}, u32[]{:S(2)}, u32[]{:S(2)}) %collective-permute-start.15) | collective-permute-done | bytes 16416 | tf_op jit(solution)/shard_map/ppermute | solution.py:270
  59.1 1.3 %collective-permute-done.16.refs_1_ = bf16[2,4096]{1,0:T(2,128)(2,1)S(1)} collective-permute-done((bf16[2,4096]{1,0:T(2,128)(2,1)S(1)}, bf16[2,4096]{1,0:T(2,128)(2,1)S(1)}, u32[]{:S(2)}, u32[]{:S(2)}) %collective-permute-start.16) | collective-permute-done | bytes 16416 | tf_op jit(solution)/shard_map/ppermute | solution.py:270
  60.4 0.2 collective-permute-done.17.refs_2_
  60.6 0.6 %shard_map.115 = bf16[2,16384]{1,0:T(2,128)(2,1)} custom-call(bf16[2,4096]{1,0:T(2,128)(2,1)S(1)} %collective-permute-done.15.refs_0_, bf16[2,4096]{1,0:T(2,128)(2,1)S(1)} %collective-permute-done.16.refs_1_, bf16[2,4096]{1,0:T(2,128)(2,1)S(1)} %collective-permute-done.17.refs_2_, bf16[2,4096]{1,0:T(2,128)(2,1)S(1)} %get-tuple-element.44.refs_3_), custom_call_target="tpu_custom_call" | custom-call | tf_op jit(solution)/shard_map/pallas_call | solution.py:453
  (25 shorter events, 0.1 us)
Async XLA Ops:
  0.0 1.2 %copy-start = (bf16[2,256,1024]{2,1,0:T(8,128)(2,1)S(1)}, bf16[2,256,1024]{2,1,0:T(8,128)(2,1)}, u32[]{:S(2)}) copy-start(bf16[2,256,1024]{2,1,0:T(8,128)(2,1)} %keys_ref.7) | copy-start | bytes 3145732
  1.2 3.2 %copy-start.7 = (bf16[2,16384]{1,0:T(2,128)(2,1)S(1)}, bf16[2,16384]{1,0:T(2,128)(2,1)}, u32[]{:S(2)}) copy-start(bf16[2,16384]{1,0:T(2,128)(2,1)} %tokens_ref.1) | copy-start | bytes 196612
  1.2 19.6 %slice-start = ((s8[16777216]{0:T(1024)(128)(4,1)}), s8[4194304]{0:T(1024)(128)(4,1)S(1)}, s32[]{:S(2)}) async-start(s8[16777216]{0:T(1024)(128)(4,1)} %bitcast.2), calls=%async_computation.1 | async-start | bytes 8388608
  1.2 19.6 %slice-start.1 = ((s8[16777216]{0:T(1024)(128)(4,1)}), s8[4194304]{0:T(1024)(128)(4,1)S(1)}, s32[]{:S(2)}) async-start(s8[16777216]{0:T(1024)(128)(4,1)} %bitcast.2), calls=%async_computation.2 | async-start | bytes 8388608
  1.3 3.3 %copy-start.1 = (bf16[2,256,1024]{2,1,0:T(8,128)(2,1)S(1)}, bf16[2,256,1024]{2,1,0:T(8,128)(2,1)}, u32[]{:S(2)}) copy-start(bf16[2,256,1024]{2,1,0:T(8,128)(2,1)} %keys_ref.7) | copy-start | bytes 3145732
  1.3 3.3 %copy-start.2 = (bf16[2,256,1024]{2,1,0:T(8,128)(2,1)S(1)}, bf16[2,256,1024]{2,1,0:T(8,128)(2,1)}, u32[]{:S(2)}) copy-start(bf16[2,256,1024]{2,1,0:T(8,128)(2,1)} %values_ref.5) | copy-start | bytes 3145732
  1.3 3.3 %copy-start.6 = (s32[2]{0:T(128)S(1)}, s32[2]{0:T(128)}, u32[]{:S(2)}) copy-start(s32[2]{0:T(128)} %param.18) | copy-start | bytes 28
  1.3 3.4 %copy-start.5 = (f32[16384]{0:T(1024)S(1)}, f32[16384]{0:T(1024)}, u32[]{:S(2)}) copy-start(f32[16384]{0:T(1024)} %param.11) | copy-start | bytes 196612
  1.3 19.5 %slice-start.2 = ((s8[16777216]{0:T(1024)(128)(4,1)}), s8[4194304]{0:T(1024)(128)(4,1)S(1)}, s32[]{:S(2)}) async-start(s8[16777216]{0:T(1024)(128)(4,1)} %bitcast.2), calls=%async_computation.3 | async-start | bytes 8388608
  1.3 19.5 %slice-start.3 = ((s8[16777216]{0:T(1024)(128)(4,1)}), s8[4194304]{0:T(1024)(128)(4,1)S(1)}, s32[]{:S(2)}) async-start(s8[16777216]{0:T(1024)(128)(4,1)} %bitcast.2), calls=%async_computation.4 | async-start | bytes 8388608
  1.4 19.5 %copy-start.3 = (bf16[4096,256]{1,0:T(8,128)(2,1)S(1)}, bf16[4096,256]{1,0:T(8,128)(2,1)}, u32[]{:S(2)}) copy-start(bf16[4096,256]{1,0:T(8,128)(2,1)} %key_ref.3) | copy-start | bytes 6291460
  1.4 19.5 %copy-start.4 = (bf16[4096,256]{1,0:T(8,128)(2,1)S(1)}, bf16[4096,256]{1,0:T(8,128)(2,1)}, u32[]{:S(2)}) copy-start(bf16[4096,256]{1,0:T(8,128)(2,1)} %value_ref.3) | copy-start | bytes 6291460
  1.4 17.2 %collective-permute-start.1 = (bf16[768,256]{1,0:T(8,128)(2,1)S(1)}, bf16[768,256]{1,0:T(8,128)(2,1)S(1)}, u32[]{:S(2)}, u32[]{:S(2)}) collective-permute-start(bf16[768,256]{1,0:T(8,128)(2,1)S(1)} %shard_map.103), channel_id=1, source_target_pairs={{0,2},{1,3},{2,0},{3,1},{4,6},{5,7},{6,4},{7,5},{8,10},{9,11},{10,... | collective-permute-start | bytes 1179656 | tf_op jit(solution)/shard_map/ppermute | solution.py:274
  18.6 4.2 %collective-permute-start.2 = (bf16[1296,256]{1,0:T(8,128)(2,1)S(1)}, bf16[1296,256]{1,0:T(8,128)(2,1)S(1)}, u32[]{:S(2)}, u32[]{:S(2)}) collective-permute-start(bf16[1296,256]{1,0:T(8,128)(2,1)S(1)} %shard_map.105), channel_id=1, source_target_pairs={{0,1},{1,0},{2,3},{3,2},{4,5},{5,4},{6,7},{7,6},{8,9},{9,8},{10,11... | collective-permute-start | bytes 1990664 | tf_op jit(solution)/shard_map/ppermute | solution.py:274
  18.7 17.5 %collective-permute-start.7 = (bf16[784,256]{1,0:T(8,128)(2,1)S(1)}, bf16[784,256]{1,0:T(8,128)(2,1)S(1)}, u32[]{:S(2)}, u32[]{:S(2)}) collective-permute-start(bf16[784,256]{1,0:T(8,128)(2,1)S(1)} %get-tuple-element.32), channel_id=1, source_target_pairs={{0,3},{1,2},{2,1},{3,0},{4,7},{5,6},{6,5},{7,4},{8,11},{9,10},{10,... | collective-permute-start | bytes 1204232 | tf_op jit(solution)/shard_map/ppermute | solution.py:274
  18.8 17.4 %collective-permute-start.6 = (bf16[528,256]{1,0:T(8,128)(2,1)S(1)}, bf16[528,256]{1,0:T(8,128)(2,1)S(1)}, u32[]{:S(2)}, u32[]{:S(2)}) collective-permute-start(bf16[528,256]{1,0:T(8,128)(2,1)S(1)} %get-tuple-element.27._), channel_id=1, source_target_pairs={{0,2},{1,3},{2,0},{3,1},{4,6},{5,7},{6,4},{7,5},{8,10},{9,11},{10,... | collective-permute-start | bytes 811016 | tf_op jit(solution)/shard_map/ppermute | solution.py:274
  20.9 2.0 %collective-permute-start = (bf16[16,2,2048]{2,1,0:T(2,128)(2,1)S(1)}, bf16[16,2,2048]{2,1,0:T(2,128)(2,1)S(1)}, u32[]{:S(2)}, u32[]{:S(2)}) collective-permute-start(bf16[16,2,2048]{2,1,0:T(2,128)(2,1)S(1)} %all_to_all.5.refs_2_.rows_ref._), channel_id=1, source_target_pairs={{0,1},{1,0},{2,3},{3,2},{4,5},{5,4},{6,7},{7,6},{8,9},{9,8},{10,11... | collective-permute-start | bytes 393224 | tf_op jit(solution)/shard_map/ppermute | solution.py:270
  22.8 13.4 %copy-start.8 = (f32[1,128]{1,0:T(1,128)S(1)}, f32[1,128]{1,0:T(1,128)}, u32[]{:S(2)}) copy-start(f32[1,128]{1,0:T(1,128)} %constant.2.clone.frequency_ref) | copy-start | bytes 1540
  22.8 21.0 %slice-start.4 = ((s8[16777216]{0:T(1024)(128)(4,1)}), s8[4194304]{0:T(1024)(128)(4,1)S(1)}, s32[]{:S(2)}) async-start(s8[16777216]{0:T(1024)(128)(4,1)} %bitcast.4), calls=%async_computation.5 | async-start | bytes 8388608
  22.9 21.0 %slice-start.5 = ((s8[16777216]{0:T(1024)(128)(4,1)}), s8[4194304]{0:T(1024)(128)(4,1)S(1)}, s32[]{:S(2)}) async-start(s8[16777216]{0:T(1024)(128)(4,1)} %bitcast.4), calls=%async_computation.6 | async-start | bytes 8388608
  24.8 11.3 %collective-permute-start.3 = (f32[4,2,2560]{2,1,0:T(2,128)S(1)}, f32[4,2,2560]{2,1,0:T(2,128)S(1)}, u32[]{:S(2)}, u32[]{:S(2)}) collective-permute-start(f32[4,2,2560]{2,1,0:T(2,128)S(1)} %get-tuple-element.28), channel_id=1, source_target_pairs={{0,12},{4,8},{8,4},{12,0},{1,13},{5,9},{9,5},{13,1},{2,14},{6,10},... | collective-permute-start | bytes 245768 | tf_op jit(solution)/shard_map/ppermute | solution.py:270
  25.6 10.6 %collective-permute-start.4 = (f32[4,2,2560]{2,1,0:T(2,128)S(1)}, f32[4,2,2560]{2,1,0:T(2,128)S(1)}, u32[]{:S(2)}, u32[]{:S(2)}) collective-permute-start(f32[4,2,2560]{2,1,0:T(2,128)S(1)} %get-tuple-element.29), channel_id=1, source_target_pairs={{0,8},{4,12},{8,0},{12,4},{1,9},{5,13},{9,1},{13,5},{2,10},{6,14},... | collective-permute-start | bytes 245768 | tf_op jit(solution)/shard_map/ppermute | solution.py:270
  26.1 10.1 %collective-permute-start.5 = (f32[4,2,2560]{2,1,0:T(2,128)S(1)}, f32[4,2,2560]{2,1,0:T(2,128)S(1)}, u32[]{:S(2)}, u32[]{:S(2)}) collective-permute-start(f32[4,2,2560]{2,1,0:T(2,128)S(1)} %get-tuple-element.30), channel_id=1, source_target_pairs={{0,4},{4,0},{8,12},{12,8},{1,5},{5,1},{9,13},{13,9},{2,6},{6,2},{1... | collective-permute-start | bytes 245768 | tf_op jit(solution)/shard_map/ppermute | solution.py:270
  36.2 7.7 %slice-start.6 = ((s8[16777216]{0:T(1024)(128)(4,1)}), s8[4194304]{0:T(1024)(128)(4,1)S(1)}, s32[]{:S(2)}) async-start(s8[16777216]{0:T(1024)(128)(4,1)} %bitcast.4), calls=%async_computation.7 | async-start | bytes 8388608
  36.2 7.7 %slice-start.7 = ((s8[16777216]{0:T(1024)(128)(4,1)}), s8[4194304]{0:T(1024)(128)(4,1)S(1)}, s32[]{:S(2)}) async-start(s8[16777216]{0:T(1024)(128)(4,1)} %bitcast.4), calls=%async_computation.8 | async-start | bytes 8388608
  37.3 5.9 %collective-permute-start.10 = (bf16[4,2,2048]{2,1,0:T(2,128)(2,1)S(1)}, bf16[4,2,2048]{2,1,0:T(2,128)(2,1)S(1)}, u32[]{:S(2)}, u32[]{:S(2)}) collective-permute-start(bf16[4,2,2048]{2,1,0:T(2,128)(2,1)S(1)} %shard_map.109.refs_0_), channel_id=1, source_target_pairs={{0,12},{4,8},{8,4},{12,0},{1,13},{5,9},{9,5},{13,1},{2,14},{6,10},... | collective-permute-start | bytes 98312 | tf_op jit(solution)/shard_map/ppermute | solution.py:270
  38.2 5.6 %collective-permute-start.8 = (bf16[4,2,2048]{2,1,0:T(2,128)(2,1)S(1)}, bf16[4,2,2048]{2,1,0:T(2,128)(2,1)S(1)}, u32[]{:S(2)}, u32[]{:S(2)}) collective-permute-start(bf16[4,2,2048]{2,1,0:T(2,128)(2,1)S(1)} %shard_map.109.refs_0_), channel_id=1, source_target_pairs={{0,8},{4,12},{8,0},{12,4},{1,9},{5,13},{9,1},{13,5},{2,10},{6,14},... | collective-permute-start | bytes 98312 | tf_op jit(solution)/shard_map/ppermute | solution.py:270
  38.8 5.0 %collective-permute-start.9 = (bf16[4,2,2048]{2,1,0:T(2,128)(2,1)S(1)}, bf16[4,2,2048]{2,1,0:T(2,128)(2,1)S(1)}, u32[]{:S(2)}, u32[]{:S(2)}) collective-permute-start(bf16[4,2,2048]{2,1,0:T(2,128)(2,1)S(1)} %shard_map.109.refs_0_), channel_id=1, source_target_pairs={{0,4},{4,0},{8,12},{12,8},{1,5},{5,1},{9,13},{13,9},{2,6},{6,2},{1... | collective-permute-start | bytes 98312 | tf_op jit(solution)/shard_map/ppermute | solution.py:270
  45.5 2.2 %collective-permute-start.13 = (f32[8,2,2048]{2,1,0:T(2,128)S(1)}, f32[8,2,2048]{2,1,0:T(2,128)S(1)}, u32[]{:S(2)}, u32[]{:S(2)}) collective-permute-start(f32[8,2,2048]{2,1,0:T(2,128)S(1)} %get-tuple-element.38), channel_id=1, source_target_pairs={{0,1},{1,0},{2,3},{3,2},{4,5},{5,4},{6,7},{7,6},{8,9},{9,8},{10,11... | collective-permute-start | bytes 393224 | tf_op jit(solution)/shard_map/ppermute | solution.py:274
  47.1 1.5 %collective-permute-start.11 = (f32[8,2,2048]{2,1,0:T(2,128)S(1)}, f32[8,2,2048]{2,1,0:T(2,128)S(1)}, u32[]{:S(2)}, u32[]{:S(2)}) collective-permute-start(f32[8,2,2048]{2,1,0:T(2,128)S(1)} %get-tuple-element.34), channel_id=1, source_target_pairs={{0,1},{1,0},{2,3},{3,2},{4,5},{5,4},{6,7},{7,6},{8,9},{9,8},{10,11... | collective-permute-start | bytes 393224 | tf_op jit(solution)/shard_map/ppermute | solution.py:274
  47.7 4.7 %collective-permute-start.14 = (f32[4,2,2048]{2,1,0:T(2,128)S(1)}, f32[4,2,2048]{2,1,0:T(2,128)S(1)}, u32[]{:S(2)}, u32[]{:S(2)}) collective-permute-start(f32[4,2,2048]{2,1,0:T(2,128)S(1)} %get-tuple-element.40), channel_id=1, source_target_pairs={{0,2},{1,3},{2,0},{3,1},{4,6},{5,7},{6,4},{7,5},{8,10},{9,11},{10,... | collective-permute-start | bytes 196616 | tf_op jit(solution)/shard_map/ppermute | solution.py:274
  48.7 4.8 %collective-permute-start.12 = (f32[4,2,2048]{2,1,0:T(2,128)S(1)}, f32[4,2,2048]{2,1,0:T(2,128)S(1)}, u32[]{:S(2)}, u32[]{:S(2)}) collective-permute-start(f32[4,2,2048]{2,1,0:T(2,128)S(1)} %get-tuple-element.36), channel_id=1, source_target_pairs={{0,2},{1,3},{2,0},{3,1},{4,6},{5,7},{6,4},{7,5},{8,10},{9,11},{10,... | collective-permute-start | bytes 196616 | tf_op jit(solution)/shard_map/ppermute | solution.py:274
  53.5 5.6 %collective-permute-start.15 = (bf16[2,4096]{1,0:T(2,128)(2,1)S(1)}, bf16[2,4096]{1,0:T(2,128)(2,1)S(1)}, u32[]{:S(2)}, u32[]{:S(2)}) collective-permute-start(bf16[2,4096]{1,0:T(2,128)(2,1)S(1)} %get-tuple-element.41), channel_id=1, source_target_pairs={{0,12},{4,8},{8,4},{12,0},{1,13},{5,9},{9,5},{13,1},{2,14},{6,10},... | collective-permute-start | bytes 49160 | tf_op jit(solution)/shard_map/ppermute | solution.py:270
  55.7 4.6 %collective-permute-start.16 = (bf16[2,4096]{1,0:T(2,128)(2,1)S(1)}, bf16[2,4096]{1,0:T(2,128)(2,1)S(1)}, u32[]{:S(2)}, u32[]{:S(2)}) collective-permute-start(bf16[2,4096]{1,0:T(2,128)(2,1)S(1)} %get-tuple-element.42), channel_id=1, source_target_pairs={{0,8},{4,12},{8,0},{12,4},{1,9},{5,13},{9,1},{13,5},{2,10},{6,14},... | collective-permute-start | bytes 49160 | tf_op jit(solution)/shard_map/ppermute | solution.py:270
  56.8 3.7 %collective-permute-start.17 = (bf16[2,4096]{1,0:T(2,128)(2,1)S(1)}, bf16[2,4096]{1,0:T(2,128)(2,1)S(1)}, u32[]{:S(2)}, u32[]{:S(2)}) collective-permute-start(bf16[2,4096]{1,0:T(2,128)(2,1)S(1)} %get-tuple-element.43), channel_id=1, source_target_pairs={{0,4},{4,0},{8,12},{12,8},{1,5},{5,1},{9,13},{13,9},{2,6},{6,2},{1... | collective-permute-start | bytes 49160 | tf_op jit(solution)/shard_map/ppermute | solution.py:270

commit v16 on v13

--- a/solution.py
+++ b/solution.py
@@ -314,6 +314,8 @@
     blocks = cut(plan, normed)
     firsts, rest = blocks[:even], blocks[even:]
     firsts = [swap_plane(firsts[s], 2 * s + 2) for s in range(even)]
+    near = swap_plane(rest[even], 1)
+    rest = [*rest[:even], *rest[even + 1 :]]
     own_half = swap_blocks(normed, ROW_AXES)
     other_half = swap_pairs(own_half, "gz", 1)
     rest = pl.pallas_call(
@@ -325,7 +327,7 @@
         compiler_params=params(1),
     )(*rest, own_half, *firsts)
     lasts = [swap_plane(rest[s], 2 * s + 2) for s in range(even)]
-    odd = [swap_plane(rest[even + s], 2 * s + 1) for s in range(even + 1)]
+    odd = [near, *[swap_plane(rest[even + s], 2 * s + 3) for s in range(even)]]
     (mine,) = cut([(0, every, every, True)], own_half)
     held = [*firsts, *lasts, mine, *odd]
     weights = (query_weight, key_weight, value_weight)

time: 60.5 us -> 77.7 us (1.28)
  local copies, waits for them, and re-layouts: 1.27 us -> 15.7 us
  blocking collectives: 13 us -> 0 us
  starting transfers between devices: 21.3 us -> 27.1 us
  waiting for transfers between devices: 15.1 us -> 20.3 us
  Pallas kernels: 9.41 us -> 14.1 us
    unnamed x26 -> x38, local copies, waits for them, and re-layouts: 1.27 us -> 15.7 us
    all_to_all x1 -> x0, blocking collectives: 13 us -> none  [swap_blocks(): return lax.all_to_all(blocks, axes, split_axis=0, concat_axis=0, tiled=True)]
    all_to_all x0 -> x1, waiting for transfers between devices: none -> 7.52 us  [swap_blocks(): return lax.all_to_all(blocks, axes, split_axis=0, concat_axis=0, tiled=True)]
    ppermute x8, waiting for transfers between devices: 10.4 us -> 3.37 us  [swap_plane(): lax.ppermute(value, PLANE, [(i, i ^ step) for i in range(lax.axis_size(PL...]
    all_to_all x0 -> x1, starting transfers between devices: none -> 4.98 us  [swap_blocks(): return lax.all_to_all(blocks, axes, split_axis=0, concat_axis=0, tiled=True)]
    ppermute x10, waiting for transfers between devices: 4.74 us -> 9.41 us  [swap_pairs(): lax.ppermute(value, axis, [(i, i ^ step) for i in range(lax.axis_size(axi...]
    pallas_call x2, Pallas kernels: 0.29 us -> 1.96 us  [cut(): pl.pallas_call(functools.partial(cut_kernel, plan), out_shape=[jax.ShapeD...]
    pallas_call x1, Pallas kernels: 1.12 us -> 2.42 us  [shards(): pl.pallas_call(functools.partial(attend_kernel, wide, plane, rows, early,...]
  transfers between devices with their start and end apart: 18 -> 19, of which waited for: 8 -> 10; matrix products, arithmetic and copies ran while one was open for 0% -> 0% of each run, Pallas kernels for 9% -> 8%
where the time goes in v16:
time: 77.7 us; the launch traced here: 77.4 us
  starting transfers between devices  27.1 us (35%)
  waiting for transfers between devices  20.3 us (26%)
  local copies, waits for them, and re-layouts  15.7 us (20%)
  Pallas kernels  14.1 us (18%)
    unnamed x38, local copies, waits for them, and re-layouts  15.7 us
    ppermute x10, starting transfers between devices, swap_pairs(): lax.ppermute(value, axis, [(i, i ^ step) for i in range(lax.axis_size(axi...  13.4 us
    ppermute x10, waiting for transfers between devices, swap_pairs(): lax.ppermute(value, axis, [(i, i ^ step) for i in range(lax.axis_size(axi...  9.41 us
    ppermute x8, starting transfers between devices, swap_plane(): lax.ppermute(value, PLANE, [(i, i ^ step) for i in range(lax.axis_size(PL...  8.71 us
    all_to_all x1, waiting for transfers between devices, swap_blocks(): return lax.all_to_all(blocks, axes, split_axis=0, concat_axis=0, tiled=True)  7.52 us
    all_to_all x1, starting transfers between devices, swap_blocks(): return lax.all_to_all(blocks, axes, split_axis=0, concat_axis=0, tiled=True)  4.98 us
    ppermute x8, waiting for transfers between devices, swap_plane(): lax.ppermute(value, PLANE, [(i, i ^ step) for i in range(lax.axis_size(PL...  3.37 us
    pallas_call x2, Pallas kernels, shards(): pl.pallas_call(functools.partial(output_kernel, p * part_cols, part_cols,...  3.09 us
  transfers between devices with their start and end apart: 19, of which 10 were waited for; matrix products, arithmetic and copies ran while one was open for 0% of the time, Pallas kernels for 8%

profile of v16, /device:TPU:0, one launch (start us, length us, event | category | flops | bytes accessed | tf_op | source)
XLA Modules:
  0.0 77.4 jit_solution(6568174916057470956)
XLA Ops:
  0.0 0.0 copy-start.13
  0.0 1.0 %copy-done.13 = bf16[2,16384]{1,0:T(2,128)(2,1)S(1)} copy-done((bf16[2,16384]{1,0:T(2,128)(2,1)S(1)}, bf16[2,16384]{1,0:T(2,128)(2,1)}, u32[]{:S(2)}) %copy-start.13) | copy-done | bytes 65560
  1.0 0.2 shard_map.100.scaled_ref
  1.2 0.0 copy-done.10
  1.3 0.7 shard_map.101._
  2.0 0.0 copy-done.11
  2.0 0.0 copy-done.4
  2.0 1.9 %shard_map.102 = (bf16[768,256]{1,0:T(8,128)(2,1)}, bf16[272,256]{1,0:T(8,128)(2,1)S(1)}, bf16[1040,256]{1,0:T(8,128)(2,1)S(1)}, bf16[1040,256]{1,0:T(8,128)(2,1)S(1)}) custom-call(s32[1,2]{1,0:T(1,128)S(1)} %bitcast.5, bf16[2,256,1024]{2,1,0:T(8,128)(2,1)S(1)} %copy-done.4, bf16[2,256,1024]{2,1,0:T(8,128)(2,1)S(1)} %copy-done.5, ...), custom_call_target="tpu_custom_call" | custom-call | tf_op jit(solution)/shard_map/pallas_call | solution.py:297
  3.9 0.8 %copy-done.7 = bf16[1040,256]{1,0:T(8,128)(2,1)} copy-done((bf16[1040,256]{1,0:T(8,128)(2,1)}, bf16[1040,256]{1,0:T(8,128)(2,1)S(1)}, u32[]{:S(2)}) %copy-start.7) | copy-done | bytes 532504
  4.7 0.8 %copy-done.12 = bf16[1040,256]{1,0:T(8,128)(2,1)} copy-done((bf16[1040,256]{1,0:T(8,128)(2,1)}, bf16[1040,256]{1,0:T(8,128)(2,1)S(1)}, u32[]{:S(2)}) %copy-start.12) | copy-done | bytes 532504
  5.5 3.0 %collective-permute-start.5 = (bf16[768,256]{1,0:T(8,128)(2,1)}, bf16[768,256]{1,0:T(8,128)(2,1)}, u32[]{:S(2)}, u32[]{:S(2)}) collective-permute-start(bf16[768,256]{1,0:T(8,128)(2,1)} %get-tuple-element.32), channel_id=1, source_target_pairs={{0,2},{1,3},{2,0},{3,1},{4,6},{5,7},{6,4},{7,5},{8,10},{9,11},{10,... | collective-permute-start | bytes 1179656 | tf_op jit(solution)/shard_map/ppermute | solution.py:241
  8.5 5.0 %all-to-all-start = ((bf16[16,2,2048]{2,1,0:T(2,128)(2,1)}), bf16[16,2,2048]{2,1,0:T(2,128)(2,1)S(1)}, u32[]{:S(2)}, u32[]{:S(2)}) async-start(bf16[16,2,2048]{2,1,0:T(2,128)(2,1)} %shard_map.101._), calls=%async_computation | async-start | bytes 262144 | tf_op jit(solution)/shard_map/all_to_all | solution.py:233
  13.5 0.4 collective-permute-start.1
  13.9 7.5 %all-to-all-done.rows_ref.refs_2_._ = bf16[16,2,2048]{2,1,0:T(2,128)(2,1)S(1)} async-done(((bf16[16,2,2048]{2,1,0:T(2,128)(2,1)}), bf16[16,2,2048]{2,1,0:T(2,128)(2,1)S(1)}, u32[]{:S(2)}, u32[]{:S(2)}) %all-to-all-start) | async-done | bytes 131104 | tf_op jit(solution)/shard_map/all_to_all | solution.py:233
  21.4 0.0 collective-permute-done.5.refs_3_.refs_4_
  21.4 1.0 %copy-done.8 = bf16[1040,256]{1,0:T(8,128)(2,1)S(1)} copy-done((bf16[1040,256]{1,0:T(8,128)(2,1)S(1)}, bf16[1040,256]{1,0:T(8,128)(2,1)}, u32[]{:S(2)}) %copy-start.8) | copy-done | bytes 532504
  22.5 0.8 %copy-done.9 = bf16[1040,256]{1,0:T(8,128)(2,1)} copy-done((bf16[1040,256]{1,0:T(8,128)(2,1)}, bf16[1040,256]{1,0:T(8,128)(2,1)S(1)}, u32[]{:S(2)}) %copy-start.9) | copy-done | bytes 532504
  23.3 0.0 collective-permute-start.7
  23.3 0.0 collective-permute-start
  23.3 2.1 %collective-permute-start.6 = (bf16[272,256]{1,0:T(8,128)(2,1)S(1)}, bf16[272,256]{1,0:T(8,128)(2,1)S(1)}, u32[]{:S(2)}, u32[]{:S(2)}) collective-permute-start(bf16[272,256]{1,0:T(8,128)(2,1)S(1)} %get-tuple-element.35), channel_id=1, source_target_pairs={{0,2},{1,3},{2,0},{3,1},{4,6},{5,7},{6,4},{7,5},{8,10},{9,11},{10,... | collective-permute-start | bytes 417800 | tf_op jit(solution)/shard_map/ppermute | solution.py:241
  25.4 5.8 %copy-done = bf16[4096,2048]{1,0:T(8,128)(2,1)S(1)} copy-done((bf16[4096,2048]{1,0:T(8,128)(2,1)S(1)}, bf16[4096,2048]{1,0:T(8,128)(2,1)}, u32[]{:S(2)}) %copy-start) | copy-done | bytes 16777240
  31.2 1.6 %copy-done.3 = bf16[4096,256]{1,0:T(8,128)(2,1)S(1)} copy-done((bf16[4096,256]{1,0:T(8,128)(2,1)S(1)}, bf16[4096,256]{1,0:T(8,128)(2,1)}, u32[]{:S(2)}) %copy-start.3) | copy-done | bytes 2097176
  32.8 1.9 %shard_map.103.refs_1_ = f32[32,2560]{1,0:T(8,128)S(1)} custom-call(bf16[16,2,2048]{2,1,0:T(2,128)(2,1)S(1)} %all-to-all-done.rows_ref.refs_2_._, bf16[4096,2048]{1,0:T(8,128)(2,1)S(1)} %copy-done, bf16[4096,256]{1,0:T(8,128)(2,1)S(1)} %copy-done.2, bf16[4096,256]{1,0:T(8,128)(2,1)S(1)} %copy-done.3), custom_call_target="tpu_custom_call" | custom-call | flops 335544320 | bytes 10485760 | tf_op jit(solution)/shard_map/pallas_call | solution.py:335
  34.7 0.0 collective-permute-done.rows_ref
  34.7 0.0 collective-permute-done.1.refs_0_.refs_7_
  34.7 3.8 %copy-done.1 = bf16[4096,2048]{1,0:T(8,128)(2,1)S(1)} copy-done((bf16[4096,2048]{1,0:T(8,128)(2,1)S(1)}, bf16[4096,2048]{1,0:T(8,128)(2,1)}, u32[]{:S(2)}) %copy-start.1) | copy-done | bytes 16777240
  38.6 3.0 %shard_map.104 = (f32[4,2,2560]{2,1,0:T(2,128)S(1)}, f32[4,2,2560]{2,1,0:T(2,128)S(1)}, f32[4,2,2560]{2,1,0:T(2,128)S(1)}, f32[4,2,2560]{2,1,0:T(2,128)S(1)}) custom-call(bf16[16,2,2048]{2,1,0:T(2,128)(2,1)S(1)} %collective-permute-done.rows_ref, bf16[4096,2048]{1,0:T(8,128)(2,1)S(1)} %copy-done.1, bf16[4096,256]{1,0:T(8,128)(2,1)S(1)} %copy-done.2, ...), custom_call_target="tpu_custom_call" | custom-call | flops 335544320 | bytes 10485760 | tf_op jit(solution)/shard_map/pallas_call | solution.py:343
  41.6 1.7 %collective-permute-start.2 = (f32[4,2,2560]{2,1,0:T(2,128)S(1)}, f32[4,2,2560]{2,1,0:T(2,128)S(1)}, u32[]{:S(2)}, u32[]{:S(2)}) collective-permute-start(f32[4,2,2560]{2,1,0:T(2,128)S(1)} %get-tuple-element.28), channel_id=1, source_target_pairs={{0,12},{4,8},{8,4},{12,0},{1,13},{5,9},{9,5},{13,1},{2,14},{6,10},... | collective-permute-start | bytes 245768 | tf_op jit(solution)/shard_map/ppermute | solution.py:237
  43.2 0.0 collective-permute-start.3
  43.2 2.8 %collective-permute-start.4 = (f32[4,2,2560]{2,1,0:T(2,128)S(1)}, f32[4,2,2560]{2,1,0:T(2,128)S(1)}, u32[]{:S(2)}, u32[]{:S(2)}) collective-permute-start(f32[4,2,2560]{2,1,0:T(2,128)S(1)} %get-tuple-element.30), channel_id=1, source_target_pairs={{0,4},{4,0},{8,12},{12,8},{1,5},{5,1},{9,13},{13,9},{2,6},{6,2},{1... | collective-permute-start | bytes 245768 | tf_op jit(solution)/shard_map/ppermute | solution.py:237
  46.0 0.1 shard_map.106.refs_6_
  46.1 0.0 collective-permute-done.6.refs_5_
  46.1 2.7 %collective-permute-done.2.refs_0_ = f32[4,2,2560]{2,1,0:T(2,128)S(1)} collective-permute-done((f32[4,2,2560]{2,1,0:T(2,128)S(1)}, f32[4,2,2560]{2,1,0:T(2,128)S(1)}, u32[]{:S(2)}, u32[]{:S(2)}) %collective-permute-start.2) | collective-permute-done | bytes 81952 | tf_op jit(solution)/shard_map/ppermute | solution.py:237
  48.9 2.2 %collective-permute-done.3.refs_1_ = f32[4,2,2560]{2,1,0:T(2,128)S(1)} collective-permute-done((f32[4,2,2560]{2,1,0:T(2,128)S(1)}, f32[4,2,2560]{2,1,0:T(2,128)S(1)}, u32[]{:S(2)}, u32[]{:S(2)}) %collective-permute-start.3) | collective-permute-done | bytes 81952 | tf_op jit(solution)/shard_map/ppermute | solution.py:237
  51.0 0.0 collective-permute-done.4.refs_2_
  51.0 0.0 collective-permute-done.7.refs_8_
  51.0 0.0 slice-start.1
  51.1 0.0 slice-start.2
  51.1 0.0 slice-start.3
  51.1 2.4 %shard_map.107.refs_0_ = bf16[4,2,2048]{2,1,0:T(2,128)(2,1)S(1)} custom-call(f32[1,128]{1,0:T(1,128)S(1)} %copy-done.14, f32[4,2,2560]{2,1,0:T(2,128)S(1)} %collective-permute-done.2.refs_0_, f32[4,2,2560]{2,1,0:T(2,128)S(1)} %collective-permute-done.3.refs_1_, f32[4,2,2560]{2,1,0:T(2,128)S(1)} %collective-permute-done.4.refs_2_, ...), custom_call_target="tpu_custom_call" | custom-call | flops 10000000000 | bytes 4194304 | tf_op jit(solution)/shard_map/pallas_call | solution.py:357
  53.5 1.9 %collective-permute-start.10 = (bf16[4,2,2048]{2,1,0:T(2,128)(2,1)S(1)}, bf16[4,2,2048]{2,1,0:T(2,128)(2,1)S(1)}, u32[]{:S(2)}, u32[]{:S(2)}) collective-permute-start(bf16[4,2,2048]{2,1,0:T(2,128)(2,1)S(1)} %shard_map.107.refs_0_), channel_id=1, source_target_pairs={{0,12},{4,8},{8,4},{12,0},{1,13},{5,9},{9,5},{13,1},{2,14},{6,10},... | collective-permute-start | bytes 98312 | tf_op jit(solution)/shard_map/ppermute | solution.py:237
  55.4 0.0 collective-permute-start.8
  55.4 2.6 %collective-permute-start.9 = (bf16[4,2,2048]{2,1,0:T(2,128)(2,1)S(1)}, bf16[4,2,2048]{2,1,0:T(2,128)(2,1)S(1)}, u32[]{:S(2)}, u32[]{:S(2)}) collective-permute-start(bf16[4,2,2048]{2,1,0:T(2,128)(2,1)S(1)} %shard_map.107.refs_0_), channel_id=1, source_target_pairs={{0,4},{4,0},{8,12},{12,8},{1,5},{5,1},{9,13},{13,9},{2,6},{6,2},{1... | collective-permute-start | bytes 98312 | tf_op jit(solution)/shard_map/ppermute | solution.py:237
  58.0 1.4 %collective-permute-done.10.refs_3_ = bf16[4,2,2048]{2,1,0:T(2,128)(2,1)S(1)} collective-permute-done((bf16[4,2,2048]{2,1,0:T(2,128)(2,1)S(1)}, bf16[4,2,2048]{2,1,0:T(2,128)(2,1)S(1)}, u32[]{:S(2)}, u32[]{:S(2)}) %collective-permute-start.10) | collective-permute-done | bytes 32800 | tf_op jit(solution)/shard_map/ppermute | solution.py:237
  59.4 0.8 %collective-permute-done.8.refs_1_ = bf16[4,2,2048]{2,1,0:T(2,128)(2,1)S(1)} collective-permute-done((bf16[4,2,2048]{2,1,0:T(2,128)(2,1)S(1)}, bf16[4,2,2048]{2,1,0:T(2,128)(2,1)S(1)}, u32[]{:S(2)}, u32[]{:S(2)}) %collective-permute-start.8) | collective-permute-done | bytes 32800 | tf_op jit(solution)/shard_map/ppermute | solution.py:237
  60.2 0.0 collective-permute-done.9.refs_2_
  60.2 1.5 %shard_map.110 = (f32[8,2,2048]{2,1,0:T(2,128)S(1)}, f32[8,2,2048]{2,1,0:T(2,128)S(1)}) custom-call(bf16[2048,4096]{1,0:T(8,128)(2,1)S(1)} %bitcast.3, bf16[4,2,2048]{2,1,0:T(2,128)(2,1)S(1)} %shard_map.107.refs_0_, bf16[4,2,2048]{2,1,0:T(2,128)(2,1)S(1)} %collective-permute-done.8.refs_1_, bf16[4,2,2048]{2,1,0:T(2,128)(2,1)S(1)} %collective-permute-done.9.refs_2_, ...), custom_call_target="tpu_custom_call" | custom-call | flops 268435456 | bytes 8388608 | tf_op jit(solution)/shard_map/pallas_call | solution.py:373
  61.8 0.1 collective-permute-start.13
  61.9 1.5 %shard_map.108 = (f32[8,2,2048]{2,1,0:T(2,128)S(1)}, f32[8,2,2048]{2,1,0:T(2,128)S(1)}) custom-call(bf16[2048,4096]{1,0:T(8,128)(2,1)S(1)} %bitcast.3, bf16[4,2,2048]{2,1,0:T(2,128)(2,1)S(1)} %shard_map.107.refs_0_, bf16[4,2,2048]{2,1,0:T(2,128)(2,1)S(1)} %collective-permute-done.8.refs_1_, bf16[4,2,2048]{2,1,0:T(2,128)(2,1)S(1)} %collective-permute-done.9.refs_2_, ...), custom_call_target="tpu_custom_call" | custom-call | flops 268435456 | bytes 8388608 | tf_op jit(solution)/shard_map/pallas_call | solution.py:373
  63.4 0.6 collective-permute-start.11
  64.0 0.0 collective-permute-done.13.b_ref
  64.0 1.6 %collective-permute-start.14 = (f32[4,2,2048]{2,1,0:T(2,128)S(1)}, f32[4,2,2048]{2,1,0:T(2,128)S(1)}, u32[]{:S(2)}, u32[]{:S(2)}) collective-permute-start(f32[4,2,2048]{2,1,0:T(2,128)S(1)} %get-tuple-element.44), channel_id=1, source_target_pairs={{0,2},{1,3},{2,0},{3,1},{4,6},{5,7},{6,4},{7,5},{8,10},{9,11},{10,... | collective-permute-start | bytes 196616 | tf_op jit(solution)/shard_map/ppermute | solution.py:241
  65.6 0.0 collective-permute-done.11.b_ref
  65.6 1.0 %collective-permute-start.12 = (f32[4,2,2048]{2,1,0:T(2,128)S(1)}, f32[4,2,2048]{2,1,0:T(2,128)S(1)}, u32[]{:S(2)}, u32[]{:S(2)}) collective-permute-start(f32[4,2,2048]{2,1,0:T(2,128)S(1)} %get-tuple-element.40), channel_id=1, source_target_pairs={{0,2},{1,3},{2,0},{3,1},{4,6},{5,7},{6,4},{7,5},{8,10},{9,11},{10,... | collective-permute-start | bytes 196616 | tf_op jit(solution)/shard_map/ppermute | solution.py:241
  66.6 2.1 %collective-permute-done.14.refs_3_ = f32[4,2,2048]{2,1,0:T(2,128)S(1)} collective-permute-done((f32[4,2,2048]{2,1,0:T(2,128)S(1)}, f32[4,2,2048]{2,1,0:T(2,128)S(1)}, u32[]{:S(2)}, u32[]{:S(2)}) %collective-permute-start.14) | collective-permute-done | bytes 65568 | tf_op jit(solution)/shard_map/ppermute | solution.py:241
  68.7 1.2 %collective-permute-done.12.refs_1_ = f32[4,2,2048]{2,1,0:T(2,128)S(1)} collective-permute-done((f32[4,2,2048]{2,1,0:T(2,128)S(1)}, f32[4,2,2048]{2,1,0:T(2,128)S(1)}, u32[]{:S(2)}, u32[]{:S(2)}) %collective-permute-start.12) | collective-permute-done | bytes 65568 | tf_op jit(solution)/shard_map/ppermute | solution.py:241
  70.0 0.1 shard_map.112
  70.0 1.8 %collective-permute-start.15 = (bf16[2,4096]{1,0:T(2,128)(2,1)S(1)}, bf16[2,4096]{1,0:T(2,128)(2,1)S(1)}, u32[]{:S(2)}, u32[]{:S(2)}) collective-permute-start(bf16[2,4096]{1,0:T(2,128)(2,1)S(1)} %get-tuple-element.45), channel_id=1, source_target_pairs={{0,12},{4,8},{8,4},{12,0},{1,13},{5,9},{9,5},{13,1},{2,14},{6,10},... | collective-permute-start | bytes 49160 | tf_op jit(solution)/shard_map/ppermute | solution.py:237
  71.9 1.1 %collective-permute-start.16 = (bf16[2,4096]{1,0:T(2,128)(2,1)S(1)}, bf16[2,4096]{1,0:T(2,128)(2,1)S(1)}, u32[]{:S(2)}, u32[]{:S(2)}) collective-permute-start(bf16[2,4096]{1,0:T(2,128)(2,1)S(1)} %get-tuple-element.46), channel_id=1, source_target_pairs={{0,8},{4,12},{8,0},{12,4},{1,9},{5,13},{9,1},{13,5},{2,10},{6,14},... | collective-permute-start | bytes 49160 | tf_op jit(solution)/shard_map/ppermute | solution.py:237
  73.0 1.5 %collective-permute-start.17 = (bf16[2,4096]{1,0:T(2,128)(2,1)S(1)}, bf16[2,4096]{1,0:T(2,128)(2,1)S(1)}, u32[]{:S(2)}, u32[]{:S(2)}) collective-permute-start(bf16[2,4096]{1,0:T(2,128)(2,1)S(1)} %get-tuple-element.47), channel_id=1, source_target_pairs={{0,4},{4,0},{8,12},{12,8},{1,5},{5,1},{9,13},{13,9},{2,6},{6,2},{1... | collective-permute-start | bytes 49160 | tf_op jit(solution)/shard_map/ppermute | solution.py:237
  74.5 1.1 %collective-permute-done.15.refs_0_ = bf16[2,4096]{1,0:T(2,128)(2,1)S(1)} collective-permute-done((bf16[2,4096]{1,0:T(2,128)(2,1)S(1)}, bf16[2,4096]{1,0:T(2,128)(2,1)S(1)}, u32[]{:S(2)}, u32[]{:S(2)}) %collective-permute-start.15) | collective-permute-done | bytes 16416 | tf_op jit(solution)/shard_map/ppermute | solution.py:237
  75.6 0.9 %collective-permute-done.16.refs_1_ = bf16[2,4096]{1,0:T(2,128)(2,1)S(1)} collective-permute-done((bf16[2,4096]{1,0:T(2,128)(2,1)S(1)}, bf16[2,4096]{1,0:T(2,128)(2,1)S(1)}, u32[]{:S(2)}, u32[]{:S(2)}) %collective-permute-start.16) | collective-permute-done | bytes 16416 | tf_op jit(solution)/shard_map/ppermute | solution.py:237
  76.5 0.2 collective-permute-done.17.refs_2_
  76.7 0.6 shard_map.113
  (27 shorter events, 0.1 us)
Async XLA Ops:
  0.0 1.2 %copy-start.10 = (f32[16384]{0:T(1024)S(1)}, f32[16384]{0:T(1024)}, u32[]{:S(2)}) copy-start(f32[16384]{0:T(1024)} %param.11) | copy-start | bytes 196612
  0.0 2.0 %copy-start.11 = (s32[2]{0:T(128)S(1)}, s32[2]{0:T(128)}, u32[]{:S(2)}) copy-start(s32[2]{0:T(128)} %param.18) | copy-start | bytes 28
  0.0 2.0 %copy-start.4 = (bf16[2,256,1024]{2,1,0:T(8,128)(2,1)S(1)}, bf16[2,256,1024]{2,1,0:T(8,128)(2,1)}, u32[]{:S(2)}) copy-start(bf16[2,256,1024]{2,1,0:T(8,128)(2,1)} %keys_ref.3) | copy-start | bytes 3145732
  0.0 2.0 %copy-start.5 = (bf16[2,256,1024]{2,1,0:T(8,128)(2,1)S(1)}, bf16[2,256,1024]{2,1,0:T(8,128)(2,1)}, u32[]{:S(2)}) copy-start(bf16[2,256,1024]{2,1,0:T(8,128)(2,1)} %values_ref.3) | copy-start | bytes 3145732
  0.0 25.4 %copy-start.2 = (bf16[4096,256]{1,0:T(8,128)(2,1)S(1)}, bf16[4096,256]{1,0:T(8,128)(2,1)}, u32[]{:S(2)}) copy-start(bf16[4096,256]{1,0:T(8,128)(2,1)} %key_ref.3) | copy-start | bytes 6291460
  0.0 1.0 %copy-start.13 = (bf16[2,16384]{1,0:T(2,128)(2,1)S(1)}, bf16[2,16384]{1,0:T(2,128)(2,1)}, u32[]{:S(2)}) copy-start(bf16[2,16384]{1,0:T(2,128)(2,1)} %tokens_ref.1) | copy-start | bytes 196612
  3.9 0.8 %copy-start.7 = (bf16[1040,256]{1,0:T(8,128)(2,1)}, bf16[1040,256]{1,0:T(8,128)(2,1)S(1)}, u32[]{:S(2)}) copy-start(bf16[1040,256]{1,0:T(8,128)(2,1)S(1)} %get-tuple-element.34.refs_1_) | copy-start | bytes 1597444
  4.7 0.8 %copy-start.12 = (bf16[1040,256]{1,0:T(8,128)(2,1)}, bf16[1040,256]{1,0:T(8,128)(2,1)S(1)}, u32[]{:S(2)}) copy-start(bf16[1040,256]{1,0:T(8,128)(2,1)S(1)} %get-tuple-element.27) | copy-start | bytes 1597444
  5.5 15.9 %collective-permute-start.5 = (bf16[768,256]{1,0:T(8,128)(2,1)}, bf16[768,256]{1,0:T(8,128)(2,1)}, u32[]{:S(2)}, u32[]{:S(2)}) collective-permute-start(bf16[768,256]{1,0:T(8,128)(2,1)} %get-tuple-element.32), channel_id=1, source_target_pairs={{0,2},{1,3},{2,0},{3,1},{4,6},{5,7},{6,4},{7,5},{8,10},{9,11},{10,... | collective-permute-start | bytes 1179656 | tf_op jit(solution)/shard_map/ppermute | solution.py:241
  8.5 12.9 %all-to-all-start = ((bf16[16,2,2048]{2,1,0:T(2,128)(2,1)}), bf16[16,2,2048]{2,1,0:T(2,128)(2,1)S(1)}, u32[]{:S(2)}, u32[]{:S(2)}) async-start(bf16[16,2,2048]{2,1,0:T(2,128)(2,1)} %shard_map.101._), calls=%async_computation | async-start | bytes 262144 | tf_op jit(solution)/shard_map/all_to_all | solution.py:233
  13.5 21.2 %collective-permute-start.1 = (bf16[1040,256]{1,0:T(8,128)(2,1)}, bf16[1040,256]{1,0:T(8,128)(2,1)}, u32[]{:S(2)}, u32[]{:S(2)}) collective-permute-start(bf16[1040,256]{1,0:T(8,128)(2,1)} %copy-done.12), channel_id=1, source_target_pairs={{0,1},{1,0},{2,3},{3,2},{4,5},{5,4},{6,7},{7,6},{8,9},{9,8},{10,11... | collective-permute-start | bytes 1597448 | tf_op jit(solution)/shard_map/ppermute | solution.py:241
  21.4 1.0 %copy-start.8 = (bf16[1040,256]{1,0:T(8,128)(2,1)S(1)}, bf16[1040,256]{1,0:T(8,128)(2,1)}, u32[]{:S(2)}) copy-start(bf16[1040,256]{1,0:T(8,128)(2,1)} %copy-done.7) | copy-start | bytes 1597444
  22.5 0.8 %copy-start.9 = (bf16[1040,256]{1,0:T(8,128)(2,1)}, bf16[1040,256]{1,0:T(8,128)(2,1)S(1)}, u32[]{:S(2)}) copy-start(bf16[1040,256]{1,0:T(8,128)(2,1)S(1)} %get-tuple-element.36) | copy-start | bytes 1597444
  23.3 27.8 %collective-permute-start.7 = (bf16[1040,256]{1,0:T(8,128)(2,1)}, bf16[1040,256]{1,0:T(8,128)(2,1)S(1)}, u32[]{:S(2)}, u32[]{:S(2)}) collective-permute-start(bf16[1040,256]{1,0:T(8,128)(2,1)} %copy-done.9), channel_id=1, source_target_pairs={{0,3},{1,2},{2,1},{3,0},{4,7},{5,6},{6,5},{7,4},{8,11},{9,10},{10,... | collective-permute-start | bytes 1597448 | tf_op jit(solution)/shard_map/ppermute | solution.py:241
  23.3 11.4 %collective-permute-start = (bf16[16,2,2048]{2,1,0:T(2,128)(2,1)S(1)}, bf16[16,2,2048]{2,1,0:T(2,128)(2,1)S(1)}, u32[]{:S(2)}, u32[]{:S(2)}) collective-permute-start(bf16[16,2,2048]{2,1,0:T(2,128)(2,1)S(1)} %all-to-all-done.rows_ref.refs_2_._), channel_id=1, source_target_pairs={{0,1},{1,0},{2,3},{3,2},{4,5},{5,4},{6,7},{7,6},{8,9},{9,8},{10,11... | collective-permute-start | bytes 393224 | tf_op jit(solution)/shard_map/ppermute | solution.py:237
  23.3 22.8 %collective-permute-start.6 = (bf16[272,256]{1,0:T(8,128)(2,1)S(1)}, bf16[272,256]{1,0:T(8,128)(2,1)S(1)}, u32[]{:S(2)}, u32[]{:S(2)}) collective-permute-start(bf16[272,256]{1,0:T(8,128)(2,1)S(1)} %get-tuple-element.35), channel_id=1, source_target_pairs={{0,2},{1,3},{2,0},{3,1},{4,6},{5,7},{6,4},{7,5},{8,10},{9,11},{10,... | collective-permute-start | bytes 417800 | tf_op jit(solution)/shard_map/ppermute | solution.py:241
  25.4 5.8 %copy-start = (bf16[4096,2048]{1,0:T(8,128)(2,1)S(1)}, bf16[4096,2048]{1,0:T(8,128)(2,1)}, u32[]{:S(2)}) copy-start(bf16[4096,2048]{1,0:T(8,128)(2,1)} %query_ref.3) | copy-start | bytes 50331652
  31.2 1.6 %copy-start.3 = (bf16[4096,256]{1,0:T(8,128)(2,1)S(1)}, bf16[4096,256]{1,0:T(8,128)(2,1)}, u32[]{:S(2)}) copy-start(bf16[4096,256]{1,0:T(8,128)(2,1)} %value_ref.3) | copy-start | bytes 6291460
  32.8 5.8 %copy-start.1 = (bf16[4096,2048]{1,0:T(8,128)(2,1)S(1)}, bf16[4096,2048]{1,0:T(8,128)(2,1)}, u32[]{:S(2)}) copy-start(bf16[4096,2048]{1,0:T(8,128)(2,1)} %query_ref.3) | copy-start | bytes 50331652
  32.8 13.2 %copy-start.6 = (bf16[2,256,1024]{2,1,0:T(8,128)(2,1)S(1)}, bf16[2,256,1024]{2,1,0:T(8,128)(2,1)}, u32[]{:S(2)}) copy-start(bf16[2,256,1024]{2,1,0:T(8,128)(2,1)} %values_ref.3) | copy-start | bytes 3145732
  34.7 16.3 %copy-start.14 = (f32[1,128]{1,0:T(1,128)S(1)}, f32[1,128]{1,0:T(1,128)}, u32[]{:S(2)}) copy-start(f32[1,128]{1,0:T(1,128)} %constant.2.clone.frequency_ref) | copy-start | bytes 1540
  41.6 7.3 %collective-permute-start.2 = (f32[4,2,2560]{2,1,0:T(2,128)S(1)}, f32[4,2,2560]{2,1,0:T(2,128)S(1)}, u32[]{:S(2)}, u32[]{:S(2)}) collective-permute-start(f32[4,2,2560]{2,1,0:T(2,128)S(1)} %get-tuple-element.28), channel_id=1, source_target_pairs={{0,12},{4,8},{8,4},{12,0},{1,13},{5,9},{9,5},{13,1},{2,14},{6,10},... | collective-permute-start | bytes 245768 | tf_op jit(solution)/shard_map/ppermute | solution.py:237
  43.2 7.8 %collective-permute-start.3 = (f32[4,2,2560]{2,1,0:T(2,128)S(1)}, f32[4,2,2560]{2,1,0:T(2,128)S(1)}, u32[]{:S(2)}, u32[]{:S(2)}) collective-permute-start(f32[4,2,2560]{2,1,0:T(2,128)S(1)} %get-tuple-element.29), channel_id=1, source_target_pairs={{0,8},{4,12},{8,0},{12,4},{1,9},{5,13},{9,1},{13,5},{2,10},{6,14},... | collective-permute-start | bytes 245768 | tf_op jit(solution)/shard_map/ppermute | solution.py:237
  43.2 7.8 %collective-permute-start.4 = (f32[4,2,2560]{2,1,0:T(2,128)S(1)}, f32[4,2,2560]{2,1,0:T(2,128)S(1)}, u32[]{:S(2)}, u32[]{:S(2)}) collective-permute-start(f32[4,2,2560]{2,1,0:T(2,128)S(1)} %get-tuple-element.30), channel_id=1, source_target_pairs={{0,4},{4,0},{8,12},{12,8},{1,5},{5,1},{9,13},{13,9},{2,6},{6,2},{1... | collective-permute-start | bytes 245768 | tf_op jit(solution)/shard_map/ppermute | solution.py:237
  46.0 14.2 %slice-start = ((s8[16777216]{0:T(1024)(128)(4,1)}), s8[4194304]{0:T(1024)(128)(4,1)S(1)}, s32[]{:S(2)}) async-start(s8[16777216]{0:T(1024)(128)(4,1)} %bitcast.2), calls=%async_computation.1 | async-start | bytes 8388608
  51.0 9.2 %slice-start.1 = ((s8[16777216]{0:T(1024)(128)(4,1)}), s8[4194304]{0:T(1024)(128)(4,1)S(1)}, s32[]{:S(2)}) async-start(s8[16777216]{0:T(1024)(128)(4,1)} %bitcast.2), calls=%async_computation.2 | async-start | bytes 8388608
  51.1 9.2 %slice-start.2 = ((s8[16777216]{0:T(1024)(128)(4,1)}), s8[4194304]{0:T(1024)(128)(4,1)S(1)}, s32[]{:S(2)}) async-start(s8[16777216]{0:T(1024)(128)(4,1)} %bitcast.2), calls=%async_computation.3 | async-start | bytes 8388608
  51.1 9.2 %slice-start.3 = ((s8[16777216]{0:T(1024)(128)(4,1)}), s8[4194304]{0:T(1024)(128)(4,1)S(1)}, s32[]{:S(2)}) async-start(s8[16777216]{0:T(1024)(128)(4,1)} %bitcast.2), calls=%async_computation.4 | async-start | bytes 8388608
  53.5 5.9 %collective-permute-start.10 = (bf16[4,2,2048]{2,1,0:T(2,128)(2,1)S(1)}, bf16[4,2,2048]{2,1,0:T(2,128)(2,1)S(1)}, u32[]{:S(2)}, u32[]{:S(2)}) collective-permute-start(bf16[4,2,2048]{2,1,0:T(2,128)(2,1)S(1)} %shard_map.107.refs_0_), channel_id=1, source_target_pairs={{0,12},{4,8},{8,4},{12,0},{1,13},{5,9},{9,5},{13,1},{2,14},{6,10},... | collective-permute-start | bytes 98312 | tf_op jit(solution)/shard_map/ppermute | solution.py:237
  55.4 4.8 %collective-permute-start.8 = (bf16[4,2,2048]{2,1,0:T(2,128)(2,1)S(1)}, bf16[4,2,2048]{2,1,0:T(2,128)(2,1)S(1)}, u32[]{:S(2)}, u32[]{:S(2)}) collective-permute-start(bf16[4,2,2048]{2,1,0:T(2,128)(2,1)S(1)} %shard_map.107.refs_0_), channel_id=1, source_target_pairs={{0,8},{4,12},{8,0},{12,4},{1,9},{5,13},{9,1},{13,5},{2,10},{6,14},... | collective-permute-start | bytes 98312 | tf_op jit(solution)/shard_map/ppermute | solution.py:237
  55.4 4.8 %collective-permute-start.9 = (bf16[4,2,2048]{2,1,0:T(2,128)(2,1)S(1)}, bf16[4,2,2048]{2,1,0:T(2,128)(2,1)S(1)}, u32[]{:S(2)}, u32[]{:S(2)}) collective-permute-start(bf16[4,2,2048]{2,1,0:T(2,128)(2,1)S(1)} %shard_map.107.refs_0_), channel_id=1, source_target_pairs={{0,4},{4,0},{8,12},{12,8},{1,5},{5,1},{9,13},{13,9},{2,6},{6,2},{1... | collective-permute-start | bytes 98312 | tf_op jit(solution)/shard_map/ppermute | solution.py:237
  61.8 2.2 %collective-permute-start.13 = (f32[8,2,2048]{2,1,0:T(2,128)S(1)}, f32[8,2,2048]{2,1,0:T(2,128)S(1)}, u32[]{:S(2)}, u32[]{:S(2)}) collective-permute-start(f32[8,2,2048]{2,1,0:T(2,128)S(1)} %get-tuple-element.42), channel_id=1, source_target_pairs={{0,1},{1,0},{2,3},{3,2},{4,5},{5,4},{6,7},{7,6},{8,9},{9,8},{10,11... | collective-permute-start | bytes 393224 | tf_op jit(solution)/shard_map/ppermute | solution.py:241
  63.4 2.2 %collective-permute-start.11 = (f32[8,2,2048]{2,1,0:T(2,128)S(1)}, f32[8,2,2048]{2,1,0:T(2,128)S(1)}, u32[]{:S(2)}, u32[]{:S(2)}) collective-permute-start(f32[8,2,2048]{2,1,0:T(2,128)S(1)} %get-tuple-element.38), channel_id=1, source_target_pairs={{0,1},{1,0},{2,3},{3,2},{4,5},{5,4},{6,7},{7,6},{8,9},{9,8},{10,11... | collective-permute-start | bytes 393224 | tf_op jit(solution)/shard_map/ppermute | solution.py:241
  64.0 4.7 %collective-permute-start.14 = (f32[4,2,2048]{2,1,0:T(2,128)S(1)}, f32[4,2,2048]{2,1,0:T(2,128)S(1)}, u32[]{:S(2)}, u32[]{:S(2)}) collective-permute-start(f32[4,2,2048]{2,1,0:T(2,128)S(1)} %get-tuple-element.44), channel_id=1, source_target_pairs={{0,2},{1,3},{2,0},{3,1},{4,6},{5,7},{6,4},{7,5},{8,10},{9,11},{10,... | collective-permute-start | bytes 196616 | tf_op jit(solution)/shard_map/ppermute | solution.py:241
  65.6 4.3 %collective-permute-start.12 = (f32[4,2,2048]{2,1,0:T(2,128)S(1)}, f32[4,2,2048]{2,1,0:T(2,128)S(1)}, u32[]{:S(2)}, u32[]{:S(2)}) collective-permute-start(f32[4,2,2048]{2,1,0:T(2,128)S(1)} %get-tuple-element.40), channel_id=1, source_target_pairs={{0,2},{1,3},{2,0},{3,1},{4,6},{5,7},{6,4},{7,5},{8,10},{9,11},{10,... | collective-permute-start | bytes 196616 | tf_op jit(solution)/shard_map/ppermute | solution.py:241
  70.0 5.6 %collective-permute-start.15 = (bf16[2,4096]{1,0:T(2,128)(2,1)S(1)}, bf16[2,4096]{1,0:T(2,128)(2,1)S(1)}, u32[]{:S(2)}, u32[]{:S(2)}) collective-permute-start(bf16[2,4096]{1,0:T(2,128)(2,1)S(1)} %get-tuple-element.45), channel_id=1, source_target_pairs={{0,12},{4,8},{8,4},{12,0},{1,13},{5,9},{9,5},{13,1},{2,14},{6,10},... | collective-permute-start | bytes 49160 | tf_op jit(solution)/shard_map/ppermute | solution.py:237
  71.9 4.6 %collective-permute-start.16 = (bf16[2,4096]{1,0:T(2,128)(2,1)S(1)}, bf16[2,4096]{1,0:T(2,128)(2,1)S(1)}, u32[]{:S(2)}, u32[]{:S(2)}) collective-permute-start(bf16[2,4096]{1,0:T(2,128)(2,1)S(1)} %get-tuple-element.46), channel_id=1, source_target_pairs={{0,8},{4,12},{8,0},{12,4},{1,9},{5,13},{9,1},{13,5},{2,10},{6,14},... | collective-permute-start | bytes 49160 | tf_op jit(solution)/shard_map/ppermute | solution.py:237
  73.0 3.7 %collective-permute-start.17 = (bf16[2,4096]{1,0:T(2,128)(2,1)S(1)}, bf16[2,4096]{1,0:T(2,128)(2,1)S(1)}, u32[]{:S(2)}, u32[]{:S(2)}) collective-permute-start(bf16[2,4096]{1,0:T(2,128)(2,1)S(1)} %get-tuple-element.47), channel_id=1, source_target_pairs={{0,4},{4,0},{8,12},{12,8},{1,5},{5,1},{9,13},{13,9},{2,6},{6,2},{1... | collective-permute-start | bytes 49160 | tf_op jit(solution)/shard_map/ppermute | solution.py:237

commit v17 on v13

--- a/solution.py
+++ b/solution.py
@@ -91,27 +91,28 @@
     pass
 
 
-def attend_kernel(wide, plane, rows, early, query_cols, frequency_ref, *refs):
+def attend_kernel(wide, plane, members, rows, early, query_cols, frequency_ref, *refs):
     partials, held, attended_ref = refs[wide - 1 :: -1], refs[wide:-1], refs[-1]
-    even = plane // 2 - 1
+    even = plane // 2 - 1 if members[0] else 0
     firsts, lasts, whole = held[:even], held[even : 2 * even], held[2 * even :]
     slots = (whole[0].shape[0] - 16) // (2 * rows)
     cols = partials[0].shape[-1]
     kv_cols = (cols - query_cols) // 2
     kv_heads, group = kv_cols // HD, query_cols // kv_cols
-    pairs = plane * rows
+    pairs = len(members) * rows
     count = pairs * kv_heads
     heads = count * group
     scale = 1.0 / HD**0.5
-    total = partials[0][...]
+    own = slice(members[0], members[-1] + 1)
+    total = partials[0][own]
     for k in range(1, wide):
-        total = total + partials[k][...]
+        total = total + partials[k][own]
     total = total.reshape(pairs, cols).astype(jnp.bfloat16).astype(jnp.float32)
 
     def cached(values):
         parts = []
         for p in range(pairs):
-            l, r = p // rows, p % rows
+            l, r = members[p // rows], p % rows
             ref, at = whole[(l + 1) // 2], values * rows + r
             if l % 2 == 0 and l:
                 ref = firsts[l // 2 - 1]
@@ -121,7 +122,7 @@
         return jnp.concatenate(parts, 1)
 
     filled = []
-    for l in range(plane):
+    for l in members:
         block = lasts[l // 2 - 1] if l % 2 == 0 and l else whole[(l + 1) // 2]
         last = block[block.shape[0] - 16 :, :HD].astype(jnp.float32)
         filled += [last[r : r + 1] for r in range(rows)]
@@ -185,7 +186,14 @@
         by_head = jnp.swapaxes(jnp.stack(mixed[h::kv_heads], 0), 0, 1)
         attended += [by_head[g] for g in range(group)]
     attended = jnp.concatenate(attended, 1)
-    attended_ref[...] = attended.reshape(plane, rows, query_cols).astype(jnp.bfloat16)
+    attended_ref[...] = attended.reshape(len(members), rows, query_cols).astype(jnp.bfloat16)
+
+
+def join_kernel(*refs):
+    at = 0
+    for block in refs[:-1]:
+        refs[-1][at : at + block.shape[0]] = block[...]
+        at += block.shape[0]
 
 
 def output_kernel(at, cols, order, weight_ref, *refs):
@@ -352,14 +360,26 @@
     half_dim = HD // 2
     frequency = 500000.0 ** (-np.arange(half_dim, dtype=np.float64) / half_dim)
     frequency = np.tile(frequency.astype(np.float32), 2).reshape(1, HD)
+    attended = []
+    for members in (range(2), range(2, plane)):
+        used = held if members[0] else held[2 * even : 2 * even + 2]
+        attended.append(
+            pl.pallas_call(
+                functools.partial(attend_kernel, wide, plane, members, rows, early, query_cols),
+                out_shape=jax.ShapeDtypeStruct((len(members), rows, query_cols), jnp.bfloat16),
+                in_specs=[IN_VMEM] * (1 + wide + len(used)),
+                out_specs=IN_VMEM,
+                compiler_params=params(8),
+                cost_estimate=cost(10**10, 4 * MIB) if members[0] else cost(1, 1),
+            )(jnp.asarray(frequency), *partial[::-1], *used)
+        )
     attended = pl.pallas_call(
-        functools.partial(attend_kernel, wide, plane, rows, early, query_cols),
+        join_kernel,
         out_shape=jax.ShapeDtypeStruct((plane, rows, query_cols), jnp.bfloat16),
-        in_specs=[IN_VMEM] * (1 + wide + len(held)),
+        in_specs=[IN_VMEM, IN_VMEM],
         out_specs=IN_VMEM,
         compiler_params=params(8),
-        cost_estimate=cost(10**10, 4 * MIB),
-    )(jnp.asarray(frequency), *partial[::-1], *held)
+    )(*attended)
     head_rows = swap_wide([attended] * wide)
     parts = 2
     order = [0, *range(wide - 2, 0, -1), wide - 1]

time: 60.5 us -> 60.2 us (level)
  waiting for transfers between devices: 15.1 us -> 14.2 us
    ppermute x8, waiting for transfers between devices: 10.4 us -> 4.12 us  [swap_plane(): lax.ppermute(value, PLANE, [(i, i ^ step) for i in range(lax.axis_size(PL...]
    ppermute x10, waiting for transfers between devices: 4.74 us -> 10.1 us  [swap_pairs(): lax.ppermute(value, axis, [(i, i ^ step) for i in range(lax.axis_size(axi...]
    pallas_call x1 -> x3, Pallas kernels: 1.12 us -> 1.67 us  [the longest x2 1.66 us: shards(): pl.pallas_call(functools.partial(attend_kernel, wide, plane, members, row...]
  transfers between devices with their start and end apart: 18 -> 18, of which waited for: 8 -> 10; matrix products, arithmetic and copies ran while one was open for 0% -> 0% of each run, Pallas kernels for 9% -> 11%
where the time goes in v17:
time: 60.2 us; the launch traced here: 60 us
  starting transfers between devices  21.3 us (35%)
  waiting for transfers between devices  14.2 us (24%)
  blocking collectives  13 us (22%)
  Pallas kernels  9.97 us (17%)
  local copies, waits for them, and re-layouts  1.27 us (2%)
    ppermute x10, starting transfers between devices, swap_pairs(): lax.ppermute(value, axis, [(i, i ^ step) for i in range(lax.axis_size(axi...  13.8 us
    all_to_all x1, blocking collectives, swap_blocks(): return lax.all_to_all(blocks, axes, split_axis=0, concat_axis=0, tiled=True)  13 us
    ppermute x10, waiting for transfers between devices, swap_pairs(): lax.ppermute(value, axis, [(i, i ^ step) for i in range(lax.axis_size(axi...  10.1 us
    ppermute x8, starting transfers between devices, swap_plane(): lax.ppermute(value, PLANE, [(i, i ^ step) for i in range(lax.axis_size(PL...  7.55 us
    ppermute x8, waiting for transfers between devices, swap_plane(): lax.ppermute(value, PLANE, [(i, i ^ step) for i in range(lax.axis_size(PL...  4.12 us
    pallas_call x2, Pallas kernels, shards(): pl.pallas_call(functools.partial(output_kernel, p * part_cols, part_cols,...  3.09 us
    pallas_call x1, Pallas kernels, shards(): pl.pallas_call(functools.partial(project_kernel, False, wide, plane), out...  1.98 us
    pallas_call x1, Pallas kernels, shards(): pl.pallas_call(functools.partial(project_kernel, True, wide, plane), out_...  1.9 us
  transfers between devices with their start and end apart: 18, of which 10 were waited for; matrix products, arithmetic and copies ran while one was open for 0% of the time, Pallas kernels for 11%

profile of v17, /device:TPU:0, one launch (start us, length us, event | category | flops | bytes accessed | tf_op | source)
XLA Modules:
  0.0 60.0 jit_solution(15961508638840674565)
XLA Ops:
  0.0 0.0 copy-start.1
  0.0 0.0 copy-start.2
  0.0 0.0 copy-start.8
  0.0 1.0 %copy-done.8 = bf16[2,16384]{1,0:T(2,128)(2,1)S(1)} copy-done((bf16[2,16384]{1,0:T(2,128)(2,1)S(1)}, bf16[2,16384]{1,0:T(2,128)(2,1)}, u32[]{:S(2)}) %copy-start.8) | copy-done | bytes 65560
  1.0 0.2 shard_map.100.scaled_ref
  1.3 0.0 copy-done.5
  1.3 0.1 shard_map.101._
  1.4 0.0 copy-done.6
  1.4 0.0 copy-done.3
  1.4 0.2 copy-done.4
  1.6 0.2 shard_map.102
  1.8 3.0 %collective-permute-start.1 = (bf16[768,256]{1,0:T(8,128)(2,1)S(1)}, bf16[768,256]{1,0:T(8,128)(2,1)S(1)}, u32[]{:S(2)}, u32[]{:S(2)}) collective-permute-start(bf16[768,256]{1,0:T(8,128)(2,1)S(1)} %get-tuple-element.31), channel_id=1, source_target_pairs={{0,2},{1,3},{2,0},{3,1},{4,6},{5,7},{6,4},{7,5},{8,10},{9,11},{10,... | collective-permute-start | bytes 1179656 | tf_op jit(solution)/shard_map/ppermute | solution.py:249
  4.9 13.0 %all_to_all.5.refs_3_.rows_ref._ = bf16[16,2,2048]{2,1,0:T(2,128)(2,1)S(1)} all-to-all(bf16[16,2,2048]{2,1,0:T(2,128)(2,1)S(1)} %shard_map.101._), channel_id=1, replica_groups=mesh['groups'=2,'gx'=4,'gy'=2,'gz'=2] {'gx','gy','gz'}, dimensions={0} | all-to-all | bytes 262144 | tf_op jit(solution)/shard_map/all_to_all | solution.py:241
  17.8 0.0 collective-permute-done.1.refs_4_
  17.8 0.0 collective-permute-start.2
  17.8 0.1 collective-permute-start.7
  17.9 0.4 collective-permute-start
  18.3 1.7 %collective-permute-start.6 = (bf16[272,256]{1,0:T(8,128)(2,1)S(1)}, bf16[272,256]{1,0:T(8,128)(2,1)S(1)}, u32[]{:S(2)}, u32[]{:S(2)}) collective-permute-start(bf16[272,256]{1,0:T(8,128)(2,1)S(1)} %get-tuple-element.37), channel_id=1, source_target_pairs={{0,2},{1,3},{2,0},{3,1},{4,6},{5,7},{6,4},{7,5},{8,10},{9,11},{10,... | collective-permute-start | bytes 417800 | tf_op jit(solution)/shard_map/ppermute | solution.py:249
  20.0 0.0 copy-done
  20.0 0.0 copy-done.1
  20.0 0.0 copy-done.2
  20.0 1.9 %shard_map.104.refs_1_ = f32[32,2560]{1,0:T(8,128)S(1)} custom-call(bf16[16,2,2048]{2,1,0:T(2,128)(2,1)S(1)} %all_to_all.5.refs_3_.rows_ref._, bf16[4096,2048]{1,0:T(8,128)(2,1)S(1)} %copy-done, bf16[4096,256]{1,0:T(8,128)(2,1)S(1)} %copy-done.1, bf16[4096,256]{1,0:T(8,128)(2,1)S(1)} %copy-done.2), custom_call_target="tpu_custom_call" | custom-call | flops 335544320 | bytes 10485760 | tf_op jit(solution)/shard_map/pallas_call | solution.py:341
  21.9 0.0 collective-permute-done.rows_ref
  22.0 0.0 collective-permute-done.2.refs_0_.refs_5_.refs_7_
  22.0 2.0 %shard_map.105 = (f32[4,2,2560]{2,1,0:T(2,128)S(1)}, f32[4,2,2560]{2,1,0:T(2,128)S(1)}, f32[4,2,2560]{2,1,0:T(2,128)S(1)}, f32[4,2,2560]{2,1,0:T(2,128)S(1)}) custom-call(bf16[16,2,2048]{2,1,0:T(2,128)(2,1)S(1)} %collective-permute-done.rows_ref, bf16[4096,2048]{1,0:T(8,128)(2,1)S(1)} %copy-done, bf16[4096,256]{1,0:T(8,128)(2,1)S(1)} %copy-done.1, ...), custom_call_target="tpu_custom_call" | custom-call | flops 335544320 | bytes 10485760 | tf_op jit(solution)/shard_map/pallas_call | solution.py:349
  24.0 1.5 %collective-permute-start.3 = (f32[4,2,2560]{2,1,0:T(2,128)S(1)}, f32[4,2,2560]{2,1,0:T(2,128)S(1)}, u32[]{:S(2)}, u32[]{:S(2)}) collective-permute-start(f32[4,2,2560]{2,1,0:T(2,128)S(1)} %get-tuple-element.33), channel_id=1, source_target_pairs={{0,12},{4,8},{8,4},{12,0},{1,13},{5,9},{9,5},{13,1},{2,14},{6,10},... | collective-permute-start | bytes 245768 | tf_op jit(solution)/shard_map/ppermute | solution.py:245
  25.4 0.0 collective-permute-start.4
  25.5 3.0 %collective-permute-start.5 = (f32[4,2,2560]{2,1,0:T(2,128)S(1)}, f32[4,2,2560]{2,1,0:T(2,128)S(1)}, u32[]{:S(2)}, u32[]{:S(2)}) collective-permute-start(f32[4,2,2560]{2,1,0:T(2,128)S(1)} %get-tuple-element.35), channel_id=1, source_target_pairs={{0,4},{4,0},{8,12},{12,8},{1,5},{5,1},{9,13},{13,9},{2,6},{6,2},{1... | collective-permute-start | bytes 245768 | tf_op jit(solution)/shard_map/ppermute | solution.py:245
  28.4 0.1 shard_map.106.refs_4_.refs_6_
  28.5 2.7 %collective-permute-done.3.refs_0_ = f32[4,2,2560]{2,1,0:T(2,128)S(1)} collective-permute-done((f32[4,2,2560]{2,1,0:T(2,128)S(1)}, f32[4,2,2560]{2,1,0:T(2,128)S(1)}, u32[]{:S(2)}, u32[]{:S(2)}) %collective-permute-start.3) | collective-permute-done | bytes 81952 | tf_op jit(solution)/shard_map/ppermute | solution.py:245
  31.2 2.6 %collective-permute-done.4.refs_1_ = f32[4,2,2560]{2,1,0:T(2,128)S(1)} collective-permute-done((f32[4,2,2560]{2,1,0:T(2,128)S(1)}, f32[4,2,2560]{2,1,0:T(2,128)S(1)}, u32[]{:S(2)}, u32[]{:S(2)}) %collective-permute-start.4) | collective-permute-done | bytes 81952 | tf_op jit(solution)/shard_map/ppermute | solution.py:245
  33.8 0.0 collective-permute-done.5.refs_2_
  33.9 0.0 copy-done.7
  33.9 0.8 %shard_map.107.refs_0_ = bf16[2,2,2048]{2,1,0:T(2,128)(2,1)S(1)} custom-call(f32[1,128]{1,0:T(1,128)S(1)} %copy-done.7, f32[4,2,2560]{2,1,0:T(2,128)S(1)} %collective-permute-done.3.refs_0_, f32[4,2,2560]{2,1,0:T(2,128)S(1)} %collective-permute-done.4.refs_1_, f32[4,2,2560]{2,1,0:T(2,128)S(1)} %collective-permute-done.5.refs_2_, ...), custom_call_target="tpu_custom_call" | custom-call | flops 1 | bytes 1 | tf_op jit(solution)/shard_map/pallas_call | solution.py:367
  34.7 0.0 slice-start.1
  34.7 0.0 slice-start.2
  34.7 0.0 slice-start.3
  34.7 0.5 collective-permute-done.6.refs_5_
  35.3 0.0 collective-permute-done.7.refs_8_
  35.3 0.8 %shard_map.108.refs_1_ = bf16[2,2,2048]{2,1,0:T(2,128)(2,1)S(1)} custom-call(f32[1,128]{1,0:T(1,128)S(1)} %copy-done.7, f32[4,2,2560]{2,1,0:T(2,128)S(1)} %collective-permute-done.3.refs_0_, f32[4,2,2560]{2,1,0:T(2,128)S(1)} %collective-permute-done.4.refs_1_, f32[4,2,2560]{2,1,0:T(2,128)S(1)} %collective-permute-done.5.refs_2_, ...), custom_call_target="tpu_custom_call" | custom-call | flops 10000000000 | bytes 4194304 | tf_op jit(solution)/shard_map/pallas_call | solution.py:367
  36.1 1.5 %collective-permute-start.10 = (bf16[4,2,2048]{2,1,0:T(2,128)(2,1)S(1)}, bf16[4,2,2048]{2,1,0:T(2,128)(2,1)S(1)}, u32[]{:S(2)}, u32[]{:S(2)}) collective-permute-start(bf16[4,2,2048]{2,1,0:T(2,128)(2,1)S(1)} %shard_map.109.refs_0_), channel_id=1, source_target_pairs={{0,12},{4,8},{8,4},{12,0},{1,13},{5,9},{9,5},{13,1},{2,14},{6,10},... | collective-permute-start | bytes 98312 | tf_op jit(solution)/shard_map/ppermute | solution.py:245
  37.6 0.0 collective-permute-start.8
  37.6 3.0 %collective-permute-start.9 = (bf16[4,2,2048]{2,1,0:T(2,128)(2,1)S(1)}, bf16[4,2,2048]{2,1,0:T(2,128)(2,1)S(1)}, u32[]{:S(2)}, u32[]{:S(2)}) collective-permute-start(bf16[4,2,2048]{2,1,0:T(2,128)(2,1)S(1)} %shard_map.109.refs_0_), channel_id=1, source_target_pairs={{0,4},{4,0},{8,12},{12,8},{1,5},{5,1},{9,13},{13,9},{2,6},{6,2},{1... | collective-permute-start | bytes 98312 | tf_op jit(solution)/shard_map/ppermute | solution.py:245
  40.6 1.6 %collective-permute-done.10.refs_3_ = bf16[4,2,2048]{2,1,0:T(2,128)(2,1)S(1)} collective-permute-done((bf16[4,2,2048]{2,1,0:T(2,128)(2,1)S(1)}, bf16[4,2,2048]{2,1,0:T(2,128)(2,1)S(1)}, u32[]{:S(2)}, u32[]{:S(2)}) %collective-permute-start.10) | collective-permute-done | bytes 32800 | tf_op jit(solution)/shard_map/ppermute | solution.py:245
  42.2 0.6 %collective-permute-done.8.refs_1_ = bf16[4,2,2048]{2,1,0:T(2,128)(2,1)S(1)} collective-permute-done((bf16[4,2,2048]{2,1,0:T(2,128)(2,1)S(1)}, bf16[4,2,2048]{2,1,0:T(2,128)(2,1)S(1)}, u32[]{:S(2)}, u32[]{:S(2)}) %collective-permute-start.8) | collective-permute-done | bytes 32800 | tf_op jit(solution)/shard_map/ppermute | solution.py:245
  42.8 0.0 collective-permute-done.9.refs_2_
  42.9 1.5 %shard_map.112 = (f32[8,2,2048]{2,1,0:T(2,128)S(1)}, f32[8,2,2048]{2,1,0:T(2,128)S(1)}) custom-call(bf16[2048,4096]{1,0:T(8,128)(2,1)S(1)} %bitcast.3, bf16[4,2,2048]{2,1,0:T(2,128)(2,1)S(1)} %shard_map.109.refs_0_, bf16[4,2,2048]{2,1,0:T(2,128)(2,1)S(1)} %collective-permute-done.8.refs_1_, bf16[4,2,2048]{2,1,0:T(2,128)(2,1)S(1)} %collective-permute-done.9.refs_2_, ...), custom_call_target="tpu_custom_call" | custom-call | flops 268435456 | bytes 8388608 | tf_op jit(solution)/shard_map/pallas_call | solution.py:391
  44.4 0.1 collective-permute-start.13
  44.5 1.5 %shard_map.110 = (f32[8,2,2048]{2,1,0:T(2,128)S(1)}, f32[8,2,2048]{2,1,0:T(2,128)S(1)}) custom-call(bf16[2048,4096]{1,0:T(8,128)(2,1)S(1)} %bitcast.3, bf16[4,2,2048]{2,1,0:T(2,128)(2,1)S(1)} %shard_map.109.refs_0_, bf16[4,2,2048]{2,1,0:T(2,128)(2,1)S(1)} %collective-permute-done.8.refs_1_, bf16[4,2,2048]{2,1,0:T(2,128)(2,1)S(1)} %collective-permute-done.9.refs_2_, ...), custom_call_target="tpu_custom_call" | custom-call | flops 268435456 | bytes 8388608 | tf_op jit(solution)/shard_map/pallas_call | solution.py:391
  46.1 0.6 collective-permute-start.11
  46.6 0.0 collective-permute-done.13.b_ref
  46.6 1.1 %collective-permute-start.14 = (f32[4,2,2048]{2,1,0:T(2,128)S(1)}, f32[4,2,2048]{2,1,0:T(2,128)S(1)}, u32[]{:S(2)}, u32[]{:S(2)}) collective-permute-start(f32[4,2,2048]{2,1,0:T(2,128)S(1)} %get-tuple-element.46), channel_id=1, source_target_pairs={{0,2},{1,3},{2,0},{3,1},{4,6},{5,7},{6,4},{7,5},{8,10},{9,11},{10,... | collective-permute-start | bytes 196616 | tf_op jit(solution)/shard_map/ppermute | solution.py:249
  47.8 0.0 collective-permute-done.11.b_ref
  47.8 1.0 %collective-permute-start.12 = (f32[4,2,2048]{2,1,0:T(2,128)S(1)}, f32[4,2,2048]{2,1,0:T(2,128)S(1)}, u32[]{:S(2)}, u32[]{:S(2)}) collective-permute-start(f32[4,2,2048]{2,1,0:T(2,128)S(1)} %get-tuple-element.42), channel_id=1, source_target_pairs={{0,2},{1,3},{2,0},{3,1},{4,6},{5,7},{6,4},{7,5},{8,10},{9,11},{10,... | collective-permute-start | bytes 196616 | tf_op jit(solution)/shard_map/ppermute | solution.py:249
  48.8 2.6 %collective-permute-done.14.refs_3_ = f32[4,2,2048]{2,1,0:T(2,128)S(1)} collective-permute-done((f32[4,2,2048]{2,1,0:T(2,128)S(1)}, f32[4,2,2048]{2,1,0:T(2,128)S(1)}, u32[]{:S(2)}, u32[]{:S(2)}) %collective-permute-start.14) | collective-permute-done | bytes 65568 | tf_op jit(solution)/shard_map/ppermute | solution.py:249
  51.4 1.0 %collective-permute-done.12.refs_1_ = f32[4,2,2048]{2,1,0:T(2,128)S(1)} collective-permute-done((f32[4,2,2048]{2,1,0:T(2,128)S(1)}, f32[4,2,2048]{2,1,0:T(2,128)S(1)}, u32[]{:S(2)}, u32[]{:S(2)}) %collective-permute-start.12) | collective-permute-done | bytes 65568 | tf_op jit(solution)/shard_map/ppermute | solution.py:249
  52.4 0.1 shard_map.114
  52.4 2.1 %collective-permute-start.15 = (bf16[2,4096]{1,0:T(2,128)(2,1)S(1)}, bf16[2,4096]{1,0:T(2,128)(2,1)S(1)}, u32[]{:S(2)}, u32[]{:S(2)}) collective-permute-start(bf16[2,4096]{1,0:T(2,128)(2,1)S(1)} %get-tuple-element.47), channel_id=1, source_target_pairs={{0,12},{4,8},{8,4},{12,0},{1,13},{5,9},{9,5},{13,1},{2,14},{6,10},... | collective-permute-start | bytes 49160 | tf_op jit(solution)/shard_map/ppermute | solution.py:245
  54.5 1.1 %collective-permute-start.16 = (bf16[2,4096]{1,0:T(2,128)(2,1)S(1)}, bf16[2,4096]{1,0:T(2,128)(2,1)S(1)}, u32[]{:S(2)}, u32[]{:S(2)}) collective-permute-start(bf16[2,4096]{1,0:T(2,128)(2,1)S(1)} %get-tuple-element.48), channel_id=1, source_target_pairs={{0,8},{4,12},{8,0},{12,4},{1,9},{5,13},{9,1},{13,5},{2,10},{6,14},... | collective-permute-start | bytes 49160 | tf_op jit(solution)/shard_map/ppermute | solution.py:245
  55.6 1.3 %collective-permute-start.17 = (bf16[2,4096]{1,0:T(2,128)(2,1)S(1)}, bf16[2,4096]{1,0:T(2,128)(2,1)S(1)}, u32[]{:S(2)}, u32[]{:S(2)}) collective-permute-start(bf16[2,4096]{1,0:T(2,128)(2,1)S(1)} %get-tuple-element.49), channel_id=1, source_target_pairs={{0,4},{4,0},{8,12},{12,8},{1,5},{5,1},{9,13},{13,9},{2,6},{6,2},{1... | collective-permute-start | bytes 49160 | tf_op jit(solution)/shard_map/ppermute | solution.py:245
  56.9 1.1 %collective-permute-done.15.refs_0_ = bf16[2,4096]{1,0:T(2,128)(2,1)S(1)} collective-permute-done((bf16[2,4096]{1,0:T(2,128)(2,1)S(1)}, bf16[2,4096]{1,0:T(2,128)(2,1)S(1)}, u32[]{:S(2)}, u32[]{:S(2)}) %collective-permute-start.15) | collective-permute-done | bytes 16416 | tf_op jit(solution)/shard_map/ppermute | solution.py:245
  58.0 1.1 %collective-permute-done.16.refs_1_ = bf16[2,4096]{1,0:T(2,128)(2,1)S(1)} collective-permute-done((bf16[2,4096]{1,0:T(2,128)(2,1)S(1)}, bf16[2,4096]{1,0:T(2,128)(2,1)S(1)}, u32[]{:S(2)}, u32[]{:S(2)}) %collective-permute-start.16) | collective-permute-done | bytes 16416 | tf_op jit(solution)/shard_map/ppermute | solution.py:245
  59.1 0.2 collective-permute-done.17.refs_2_
  59.4 0.6 %shard_map.115 = bf16[2,16384]{1,0:T(2,128)(2,1)} custom-call(bf16[2,4096]{1,0:T(2,128)(2,1)S(1)} %collective-permute-done.15.refs_0_, bf16[2,4096]{1,0:T(2,128)(2,1)S(1)} %collective-permute-done.16.refs_1_, bf16[2,4096]{1,0:T(2,128)(2,1)S(1)} %collective-permute-done.17.refs_2_, bf16[2,4096]{1,0:T(2,128)(2,1)S(1)} %get-tuple-element.50.refs_3_), custom_call_target="tpu_custom_call" | custom-call | tf_op jit(solution)/shard_map/pallas_call | solution.py:422
  (16 shorter events, 0.1 us)
Async XLA Ops:
  0.0 1.3 %copy-start.5 = (f32[16384]{0:T(1024)S(1)}, f32[16384]{0:T(1024)}, u32[]{:S(2)}) copy-start(f32[16384]{0:T(1024)} %param.11) | copy-start | bytes 196612
  0.0 1.4 %copy-start.6 = (s32[2]{0:T(128)S(1)}, s32[2]{0:T(128)}, u32[]{:S(2)}) copy-start(s32[2]{0:T(128)} %param.18) | copy-start | bytes 28
  0.0 1.4 %copy-start.3 = (bf16[2,256,1024]{2,1,0:T(8,128)(2,1)S(1)}, bf16[2,256,1024]{2,1,0:T(8,128)(2,1)}, u32[]{:S(2)}) copy-start(bf16[2,256,1024]{2,1,0:T(8,128)(2,1)} %keys_ref.3) | copy-start | bytes 3145732
  0.0 1.6 %copy-start.4 = (bf16[2,256,1024]{2,1,0:T(8,128)(2,1)S(1)}, bf16[2,256,1024]{2,1,0:T(8,128)(2,1)}, u32[]{:S(2)}) copy-start(bf16[2,256,1024]{2,1,0:T(8,128)(2,1)} %values_ref.3) | copy-start | bytes 3145732
  0.0 20.0 %copy-start = (bf16[4096,2048]{1,0:T(8,128)(2,1)S(1)}, bf16[4096,2048]{1,0:T(8,128)(2,1)}, u32[]{:S(2)}) copy-start(bf16[4096,2048]{1,0:T(8,128)(2,1)} %query_ref.3) | copy-start | bytes 50331652
  0.0 20.0 %copy-start.1 = (bf16[4096,256]{1,0:T(8,128)(2,1)S(1)}, bf16[4096,256]{1,0:T(8,128)(2,1)}, u32[]{:S(2)}) copy-start(bf16[4096,256]{1,0:T(8,128)(2,1)} %key_ref.3) | copy-start | bytes 6291460
  0.0 20.0 %copy-start.2 = (bf16[4096,256]{1,0:T(8,128)(2,1)S(1)}, bf16[4096,256]{1,0:T(8,128)(2,1)}, u32[]{:S(2)}) copy-start(bf16[4096,256]{1,0:T(8,128)(2,1)} %value_ref.3) | copy-start | bytes 6291460
  0.0 1.0 %copy-start.8 = (bf16[2,16384]{1,0:T(2,128)(2,1)S(1)}, bf16[2,16384]{1,0:T(2,128)(2,1)}, u32[]{:S(2)}) copy-start(bf16[2,16384]{1,0:T(2,128)(2,1)} %tokens_ref.1) | copy-start | bytes 196612
  1.8 16.0 %collective-permute-start.1 = (bf16[768,256]{1,0:T(8,128)(2,1)S(1)}, bf16[768,256]{1,0:T(8,128)(2,1)S(1)}, u32[]{:S(2)}, u32[]{:S(2)}) collective-permute-start(bf16[768,256]{1,0:T(8,128)(2,1)S(1)} %get-tuple-element.31), channel_id=1, source_target_pairs={{0,2},{1,3},{2,0},{3,1},{4,6},{5,7},{6,4},{7,5},{8,10},{9,11},{10,... | collective-permute-start | bytes 1179656 | tf_op jit(solution)/shard_map/ppermute | solution.py:249
  17.8 4.1 %collective-permute-start.2 = (bf16[1040,256]{1,0:T(8,128)(2,1)S(1)}, bf16[1040,256]{1,0:T(8,128)(2,1)S(1)}, u32[]{:S(2)}, u32[]{:S(2)}) collective-permute-start(bf16[1040,256]{1,0:T(8,128)(2,1)S(1)} %get-tuple-element.32), channel_id=1, source_target_pairs={{0,1},{1,0},{2,3},{3,2},{4,5},{5,4},{6,7},{7,6},{8,9},{9,8},{10,11... | collective-permute-start | bytes 1597448 | tf_op jit(solution)/shard_map/ppermute | solution.py:249
  17.8 17.4 %collective-permute-start.7 = (bf16[1040,256]{1,0:T(8,128)(2,1)S(1)}, bf16[1040,256]{1,0:T(8,128)(2,1)S(1)}, u32[]{:S(2)}, u32[]{:S(2)}) collective-permute-start(bf16[1040,256]{1,0:T(8,128)(2,1)S(1)} %get-tuple-element.38), channel_id=1, source_target_pairs={{0,3},{1,2},{2,1},{3,0},{4,7},{5,6},{6,5},{7,4},{8,11},{9,10},{10,... | collective-permute-start | bytes 1597448 | tf_op jit(solution)/shard_map/ppermute | solution.py:249
  17.9 4.0 %collective-permute-start = (bf16[16,2,2048]{2,1,0:T(2,128)(2,1)S(1)}, bf16[16,2,2048]{2,1,0:T(2,128)(2,1)S(1)}, u32[]{:S(2)}, u32[]{:S(2)}) collective-permute-start(bf16[16,2,2048]{2,1,0:T(2,128)(2,1)S(1)} %all_to_all.5.refs_3_.rows_ref._), channel_id=1, source_target_pairs={{0,1},{1,0},{2,3},{3,2},{4,5},{5,4},{6,7},{7,6},{8,9},{9,8},{10,11... | collective-permute-start | bytes 393224 | tf_op jit(solution)/shard_map/ppermute | solution.py:245
  18.3 16.9 %collective-permute-start.6 = (bf16[272,256]{1,0:T(8,128)(2,1)S(1)}, bf16[272,256]{1,0:T(8,128)(2,1)S(1)}, u32[]{:S(2)}, u32[]{:S(2)}) collective-permute-start(bf16[272,256]{1,0:T(8,128)(2,1)S(1)} %get-tuple-element.37), channel_id=1, source_target_pairs={{0,2},{1,3},{2,0},{3,1},{4,6},{5,7},{6,4},{7,5},{8,10},{9,11},{10,... | collective-permute-start | bytes 417800 | tf_op jit(solution)/shard_map/ppermute | solution.py:249
  21.9 11.9 %copy-start.7 = (f32[1,128]{1,0:T(1,128)S(1)}, f32[1,128]{1,0:T(1,128)}, u32[]{:S(2)}) copy-start(f32[1,128]{1,0:T(1,128)} %constant.2.clone.frequency_ref) | copy-start | bytes 1540
  24.0 7.3 %collective-permute-start.3 = (f32[4,2,2560]{2,1,0:T(2,128)S(1)}, f32[4,2,2560]{2,1,0:T(2,128)S(1)}, u32[]{:S(2)}, u32[]{:S(2)}) collective-permute-start(f32[4,2,2560]{2,1,0:T(2,128)S(1)} %get-tuple-element.33), channel_id=1, source_target_pairs={{0,12},{4,8},{8,4},{12,0},{1,13},{5,9},{9,5},{13,1},{2,14},{6,10},... | collective-permute-start | bytes 245768 | tf_op jit(solution)/shard_map/ppermute | solution.py:245
  25.4 8.4 %collective-permute-start.4 = (f32[4,2,2560]{2,1,0:T(2,128)S(1)}, f32[4,2,2560]{2,1,0:T(2,128)S(1)}, u32[]{:S(2)}, u32[]{:S(2)}) collective-permute-start(f32[4,2,2560]{2,1,0:T(2,128)S(1)} %get-tuple-element.34), channel_id=1, source_target_pairs={{0,8},{4,12},{8,0},{12,4},{1,9},{5,13},{9,1},{13,5},{2,10},{6,14},... | collective-permute-start | bytes 245768 | tf_op jit(solution)/shard_map/ppermute | solution.py:245
  25.5 8.4 %collective-permute-start.5 = (f32[4,2,2560]{2,1,0:T(2,128)S(1)}, f32[4,2,2560]{2,1,0:T(2,128)S(1)}, u32[]{:S(2)}, u32[]{:S(2)}) collective-permute-start(f32[4,2,2560]{2,1,0:T(2,128)S(1)} %get-tuple-element.35), channel_id=1, source_target_pairs={{0,4},{4,0},{8,12},{12,8},{1,5},{5,1},{9,13},{13,9},{2,6},{6,2},{1... | collective-permute-start | bytes 245768 | tf_op jit(solution)/shard_map/ppermute | solution.py:245
  33.9 9.0 %slice-start = ((s8[16777216]{0:T(1024)(128)(4,1)}), s8[4194304]{0:T(1024)(128)(4,1)S(1)}, s32[]{:S(2)}) async-start(s8[16777216]{0:T(1024)(128)(4,1)} %bitcast.2), calls=%async_computation.1 | async-start | bytes 8388608
  34.7 8.1 %slice-start.1 = ((s8[16777216]{0:T(1024)(128)(4,1)}), s8[4194304]{0:T(1024)(128)(4,1)S(1)}, s32[]{:S(2)}) async-start(s8[16777216]{0:T(1024)(128)(4,1)} %bitcast.2), calls=%async_computation.2 | async-start | bytes 8388608
  34.7 8.1 %slice-start.2 = ((s8[16777216]{0:T(1024)(128)(4,1)}), s8[4194304]{0:T(1024)(128)(4,1)S(1)}, s32[]{:S(2)}) async-start(s8[16777216]{0:T(1024)(128)(4,1)} %bitcast.2), calls=%async_computation.3 | async-start | bytes 8388608
  34.7 8.1 %slice-start.3 = ((s8[16777216]{0:T(1024)(128)(4,1)}), s8[4194304]{0:T(1024)(128)(4,1)S(1)}, s32[]{:S(2)}) async-start(s8[16777216]{0:T(1024)(128)(4,1)} %bitcast.2), calls=%async_computation.4 | async-start | bytes 8388608
  36.1 6.1 %collective-permute-start.10 = (bf16[4,2,2048]{2,1,0:T(2,128)(2,1)S(1)}, bf16[4,2,2048]{2,1,0:T(2,128)(2,1)S(1)}, u32[]{:S(2)}, u32[]{:S(2)}) collective-permute-start(bf16[4,2,2048]{2,1,0:T(2,128)(2,1)S(1)} %shard_map.109.refs_0_), channel_id=1, source_target_pairs={{0,12},{4,8},{8,4},{12,0},{1,13},{5,9},{9,5},{13,1},{2,14},{6,10},... | collective-permute-start | bytes 98312 | tf_op jit(solution)/shard_map/ppermute | solution.py:245
  37.6 5.2 %collective-permute-start.8 = (bf16[4,2,2048]{2,1,0:T(2,128)(2,1)S(1)}, bf16[4,2,2048]{2,1,0:T(2,128)(2,1)S(1)}, u32[]{:S(2)}, u32[]{:S(2)}) collective-permute-start(bf16[4,2,2048]{2,1,0:T(2,128)(2,1)S(1)} %shard_map.109.refs_0_), channel_id=1, source_target_pairs={{0,8},{4,12},{8,0},{12,4},{1,9},{5,13},{9,1},{13,5},{2,10},{6,14},... | collective-permute-start | bytes 98312 | tf_op jit(solution)/shard_map/ppermute | solution.py:245
  37.6 5.2 %collective-permute-start.9 = (bf16[4,2,2048]{2,1,0:T(2,128)(2,1)S(1)}, bf16[4,2,2048]{2,1,0:T(2,128)(2,1)S(1)}, u32[]{:S(2)}, u32[]{:S(2)}) collective-permute-start(bf16[4,2,2048]{2,1,0:T(2,128)(2,1)S(1)} %shard_map.109.refs_0_), channel_id=1, source_target_pairs={{0,4},{4,0},{8,12},{12,8},{1,5},{5,1},{9,13},{13,9},{2,6},{6,2},{1... | collective-permute-start | bytes 98312 | tf_op jit(solution)/shard_map/ppermute | solution.py:245
  44.4 2.2 %collective-permute-start.13 = (f32[8,2,2048]{2,1,0:T(2,128)S(1)}, f32[8,2,2048]{2,1,0:T(2,128)S(1)}, u32[]{:S(2)}, u32[]{:S(2)}) collective-permute-start(f32[8,2,2048]{2,1,0:T(2,128)S(1)} %get-tuple-element.44), channel_id=1, source_target_pairs={{0,1},{1,0},{2,3},{3,2},{4,5},{5,4},{6,7},{7,6},{8,9},{9,8},{10,11... | collective-permute-start | bytes 393224 | tf_op jit(solution)/shard_map/ppermute | solution.py:249
  46.1 1.7 %collective-permute-start.11 = (f32[8,2,2048]{2,1,0:T(2,128)S(1)}, f32[8,2,2048]{2,1,0:T(2,128)S(1)}, u32[]{:S(2)}, u32[]{:S(2)}) collective-permute-start(f32[8,2,2048]{2,1,0:T(2,128)S(1)} %get-tuple-element.40), channel_id=1, source_target_pairs={{0,1},{1,0},{2,3},{3,2},{4,5},{5,4},{6,7},{7,6},{8,9},{9,8},{10,11... | collective-permute-start | bytes 393224 | tf_op jit(solution)/shard_map/ppermute | solution.py:249
  46.6 4.7 %collective-permute-start.14 = (f32[4,2,2048]{2,1,0:T(2,128)S(1)}, f32[4,2,2048]{2,1,0:T(2,128)S(1)}, u32[]{:S(2)}, u32[]{:S(2)}) collective-permute-start(f32[4,2,2048]{2,1,0:T(2,128)S(1)} %get-tuple-element.46), channel_id=1, source_target_pairs={{0,2},{1,3},{2,0},{3,1},{4,6},{5,7},{6,4},{7,5},{8,10},{9,11},{10,... | collective-permute-start | bytes 196616 | tf_op jit(solution)/shard_map/ppermute | solution.py:249
  47.8 4.6 %collective-permute-start.12 = (f32[4,2,2048]{2,1,0:T(2,128)S(1)}, f32[4,2,2048]{2,1,0:T(2,128)S(1)}, u32[]{:S(2)}, u32[]{:S(2)}) collective-permute-start(f32[4,2,2048]{2,1,0:T(2,128)S(1)} %get-tuple-element.42), channel_id=1, source_target_pairs={{0,2},{1,3},{2,0},{3,1},{4,6},{5,7},{6,4},{7,5},{8,10},{9,11},{10,... | collective-permute-start | bytes 196616 | tf_op jit(solution)/shard_map/ppermute | solution.py:249
  52.4 5.6 %collective-permute-start.15 = (bf16[2,4096]{1,0:T(2,128)(2,1)S(1)}, bf16[2,4096]{1,0:T(2,128)(2,1)S(1)}, u32[]{:S(2)}, u32[]{:S(2)}) collective-permute-start(bf16[2,4096]{1,0:T(2,128)(2,1)S(1)} %get-tuple-element.47), channel_id=1, source_target_pairs={{0,12},{4,8},{8,4},{12,0},{1,13},{5,9},{9,5},{13,1},{2,14},{6,10},... | collective-permute-start | bytes 49160 | tf_op jit(solution)/shard_map/ppermute | solution.py:245
  54.5 4.6 %collective-permute-start.16 = (bf16[2,4096]{1,0:T(2,128)(2,1)S(1)}, bf16[2,4096]{1,0:T(2,128)(2,1)S(1)}, u32[]{:S(2)}, u32[]{:S(2)}) collective-permute-start(bf16[2,4096]{1,0:T(2,128)(2,1)S(1)} %get-tuple-element.48), channel_id=1, source_target_pairs={{0,8},{4,12},{8,0},{12,4},{1,9},{5,13},{9,1},{13,5},{2,10},{6,14},... | collective-permute-start | bytes 49160 | tf_op jit(solution)/shard_map/ppermute | solution.py:245
  55.6 3.7 %collective-permute-start.17 = (bf16[2,4096]{1,0:T(2,128)(2,1)S(1)}, bf16[2,4096]{1,0:T(2,128)(2,1)S(1)}, u32[]{:S(2)}, u32[]{:S(2)}) collective-permute-start(bf16[2,4096]{1,0:T(2,128)(2,1)S(1)} %get-tuple-element.49), channel_id=1, source_target_pairs={{0,4},{4,0},{8,12},{12,8},{1,5},{5,1},{9,13},{13,9},{2,6},{6,2},{1... | collective-permute-start | bytes 49160 | tf_op jit(solution)/shard_map/ppermute | solution.py:245

commit v18 on v17

--- a/solution.py
+++ b/solution.py
@@ -287,7 +287,7 @@
         in_specs=[IN_VMEM],
         out_specs=IN_VMEM,
         compiler_params=params(8),
-        cost_estimate=cost(40 * 10**9, MIB),
+        cost_estimate=cost(6 * 10**9, MIB),
     )(tokens)
     normed = pl.pallas_call(
         functools.partial(gain_kernel, wide, plane),
@@ -314,6 +314,7 @@
             in_specs=[IN_VMEM] * 4,
             out_specs=[IN_VMEM] * len(plan),
             compiler_params=params(8),
+            cost_estimate=cost(40 * 10**9 if plan[0][0] else 1, MIB),
         )(lengths.reshape(1, -1), cache_keys, cache_values, after)
 
     plan = [(l, every, every[:early], False) for l in range(2, plane, 2)]

time: 60.2 us -> 60.2 us (level)
    unnamed x26 -> x32, local copies, waits for them, and re-layouts: 1.27 us -> 1.31 us
where the time goes in v18:
time: 60.2 us; the launch traced here: 60 us
  starting transfers between devices  21.3 us (35%)
  waiting for transfers between devices  14.2 us (24%)
  blocking collectives  13 us (22%)
  Pallas kernels  9.97 us (17%)
  local copies, waits for them, and re-layouts  1.31 us (2%)
    ppermute x10, starting transfers between devices, swap_pairs(): lax.ppermute(value, axis, [(i, i ^ step) for i in range(lax.axis_size(axi...  13.8 us
    all_to_all x1, blocking collectives, swap_blocks(): return lax.all_to_all(blocks, axes, split_axis=0, concat_axis=0, tiled=True)  13 us
    ppermute x10, waiting for transfers between devices, swap_pairs(): lax.ppermute(value, axis, [(i, i ^ step) for i in range(lax.axis_size(axi...  10.1 us
    ppermute x8, starting transfers between devices, swap_plane(): lax.ppermute(value, PLANE, [(i, i ^ step) for i in range(lax.axis_size(PL...  7.55 us
    ppermute x8, waiting for transfers between devices, swap_plane(): lax.ppermute(value, PLANE, [(i, i ^ step) for i in range(lax.axis_size(PL...  4.08 us
    pallas_call x2, Pallas kernels, shards(): pl.pallas_call(functools.partial(output_kernel, p * part_cols, part_cols,...  3.09 us
    pallas_call x1, Pallas kernels, shards(): pl.pallas_call(functools.partial(project_kernel, False, wide, plane), out...  1.98 us
    pallas_call x1, Pallas kernels, shards(): pl.pallas_call(functools.partial(project_kernel, True, wide, plane), out_...  1.9 us
  transfers between devices with their start and end apart: 18, of which 10 were waited for; matrix products, arithmetic and copies ran while one was open for 0% of the time, Pallas kernels for 11%

profile of v18, /device:TPU:0, one launch (start us, length us, event | category | flops | bytes accessed | tf_op | source)
XLA Modules:
  0.0 60.0 jit_solution(10162608903845481546)
XLA Ops:
  0.0 1.0 %copy-done.7 = bf16[2,16384]{1,0:T(2,128)(2,1)S(1)} copy-done((bf16[2,16384]{1,0:T(2,128)(2,1)S(1)}, bf16[2,16384]{1,0:T(2,128)(2,1)}, u32[]{:S(2)}) %copy-start.7) | copy-done | bytes 65560
  1.0 0.2 shard_map.100.scaled_ref
  1.2 0.0 copy-done.4
  1.2 0.1 shard_map.101._
  1.3 0.0 copy-done.6
  1.4 0.0 copy-done.2
  1.4 0.3 copy-done.3
  1.6 0.0 copy-start.1
  1.6 0.2 shard_map.102
  1.9 3.0 %collective-permute-start.1 = (bf16[768,256]{1,0:T(8,128)(2,1)S(1)}, bf16[768,256]{1,0:T(8,128)(2,1)S(1)}, u32[]{:S(2)}, u32[]{:S(2)}) collective-permute-start(bf16[768,256]{1,0:T(8,128)(2,1)S(1)} %get-tuple-element.31), channel_id=1, source_target_pairs={{0,2},{1,3},{2,0},{3,1},{4,6},{5,7},{6,4},{7,5},{8,10},{9,11},{10,... | collective-permute-start | bytes 1179656 | tf_op jit(solution)/shard_map/ppermute | solution.py:249
  4.9 13.0 %all_to_all.5.refs_3_.rows_ref._ = bf16[16,2,2048]{2,1,0:T(2,128)(2,1)S(1)} all-to-all(bf16[16,2,2048]{2,1,0:T(2,128)(2,1)S(1)} %shard_map.101._), channel_id=1, replica_groups=mesh['groups'=2,'gx'=4,'gy'=2,'gz'=2] {'gx','gy','gz'}, dimensions={0} | all-to-all | bytes 262144 | tf_op jit(solution)/shard_map/all_to_all | solution.py:241
  17.9 0.0 collective-permute-done.1.refs_4_
  17.9 0.0 collective-permute-start.2
  17.9 0.1 collective-permute-start.7
  17.9 0.4 collective-permute-start
  18.4 1.7 %collective-permute-start.6 = (bf16[272,256]{1,0:T(8,128)(2,1)S(1)}, bf16[272,256]{1,0:T(8,128)(2,1)S(1)}, u32[]{:S(2)}, u32[]{:S(2)}) collective-permute-start(bf16[272,256]{1,0:T(8,128)(2,1)S(1)} %get-tuple-element.37), channel_id=1, source_target_pairs={{0,2},{1,3},{2,0},{3,1},{4,6},{5,7},{6,4},{7,5},{8,10},{9,11},{10,... | collective-permute-start | bytes 417800 | tf_op jit(solution)/shard_map/ppermute | solution.py:249
  20.1 0.0 slice-done
  20.1 0.0 slice-done.1
  20.1 0.0 slice-done.2
  20.1 0.0 slice-done.3
  20.1 0.0 copy-done
  20.1 0.0 copy-done.1
  20.1 1.9 %shard_map.104.refs_1_ = f32[32,2560]{1,0:T(8,128)S(1)} custom-call(bf16[16,2,2048]{2,1,0:T(2,128)(2,1)S(1)} %all_to_all.5.refs_3_.rows_ref._, bf16[4096,2048]{1,0:T(8,128)(2,1)S(1)} %bitcast.3, bf16[4096,256]{1,0:T(8,128)(2,1)S(1)} %copy-done, bf16[4096,256]{1,0:T(8,128)(2,1)S(1)} %copy-done.1), custom_call_target="tpu_custom_call" | custom-call | flops 335544320 | bytes 10485760 | tf_op jit(solution)/shard_map/pallas_call | solution.py:342
  22.0 0.0 collective-permute-done.rows_ref
  22.0 0.0 collective-permute-done.2.refs_0_.refs_5_.refs_7_
  22.0 2.0 %shard_map.105 = (f32[4,2,2560]{2,1,0:T(2,128)S(1)}, f32[4,2,2560]{2,1,0:T(2,128)S(1)}, f32[4,2,2560]{2,1,0:T(2,128)S(1)}, f32[4,2,2560]{2,1,0:T(2,128)S(1)}) custom-call(bf16[16,2,2048]{2,1,0:T(2,128)(2,1)S(1)} %collective-permute-done.rows_ref, bf16[4096,2048]{1,0:T(8,128)(2,1)S(1)} %bitcast.3, bf16[4096,256]{1,0:T(8,128)(2,1)S(1)} %copy-done, ...), custom_call_target="tpu_custom_call" | custom-call | flops 335544320 | bytes 10485760 | tf_op jit(solution)/shard_map/pallas_call | solution.py:350
  24.0 1.5 %collective-permute-start.3 = (f32[4,2,2560]{2,1,0:T(2,128)S(1)}, f32[4,2,2560]{2,1,0:T(2,128)S(1)}, u32[]{:S(2)}, u32[]{:S(2)}) collective-permute-start(f32[4,2,2560]{2,1,0:T(2,128)S(1)} %get-tuple-element.33), channel_id=1, source_target_pairs={{0,12},{4,8},{8,4},{12,0},{1,13},{5,9},{9,5},{13,1},{2,14},{6,10},... | collective-permute-start | bytes 245768 | tf_op jit(solution)/shard_map/ppermute | solution.py:245
  25.5 0.0 collective-permute-start.4
  25.5 3.0 %collective-permute-start.5 = (f32[4,2,2560]{2,1,0:T(2,128)S(1)}, f32[4,2,2560]{2,1,0:T(2,128)S(1)}, u32[]{:S(2)}, u32[]{:S(2)}) collective-permute-start(f32[4,2,2560]{2,1,0:T(2,128)S(1)} %get-tuple-element.35), channel_id=1, source_target_pairs={{0,4},{4,0},{8,12},{12,8},{1,5},{5,1},{9,13},{13,9},{2,6},{6,2},{1... | collective-permute-start | bytes 245768 | tf_op jit(solution)/shard_map/ppermute | solution.py:245
  28.5 0.1 shard_map.106.refs_4_.refs_6_
  28.6 2.7 %collective-permute-done.3.refs_0_ = f32[4,2,2560]{2,1,0:T(2,128)S(1)} collective-permute-done((f32[4,2,2560]{2,1,0:T(2,128)S(1)}, f32[4,2,2560]{2,1,0:T(2,128)S(1)}, u32[]{:S(2)}, u32[]{:S(2)}) %collective-permute-start.3) | collective-permute-done | bytes 81952 | tf_op jit(solution)/shard_map/ppermute | solution.py:245
  31.3 2.6 %collective-permute-done.4.refs_1_ = f32[4,2,2560]{2,1,0:T(2,128)S(1)} collective-permute-done((f32[4,2,2560]{2,1,0:T(2,128)S(1)}, f32[4,2,2560]{2,1,0:T(2,128)S(1)}, u32[]{:S(2)}, u32[]{:S(2)}) %collective-permute-start.4) | collective-permute-done | bytes 81952 | tf_op jit(solution)/shard_map/ppermute | solution.py:245
  33.9 0.0 collective-permute-done.5.refs_2_
  33.9 0.8 %shard_map.107.refs_0_ = bf16[2,2,2048]{2,1,0:T(2,128)(2,1)S(1)} custom-call(f32[1,128]{1,0:T(1,128)S(1)} %copy-done.5, f32[4,2,2560]{2,1,0:T(2,128)S(1)} %collective-permute-done.3.refs_0_, f32[4,2,2560]{2,1,0:T(2,128)S(1)} %collective-permute-done.4.refs_1_, f32[4,2,2560]{2,1,0:T(2,128)S(1)} %collective-permute-done.5.refs_2_, ...), custom_call_target="tpu_custom_call" | custom-call | flops 1 | bytes 1 | tf_op jit(solution)/shard_map/pallas_call | solution.py:368
  34.8 0.0 slice-start.5
  34.8 0.0 slice-start.6
  34.8 0.0 slice-start.7
  34.8 0.5 collective-permute-done.6.refs_5_
  35.3 0.0 collective-permute-done.7.refs_8_
  35.3 0.8 %shard_map.108.refs_1_ = bf16[2,2,2048]{2,1,0:T(2,128)(2,1)S(1)} custom-call(f32[1,128]{1,0:T(1,128)S(1)} %copy-done.5, f32[4,2,2560]{2,1,0:T(2,128)S(1)} %collective-permute-done.3.refs_0_, f32[4,2,2560]{2,1,0:T(2,128)S(1)} %collective-permute-done.4.refs_1_, f32[4,2,2560]{2,1,0:T(2,128)S(1)} %collective-permute-done.5.refs_2_, ...), custom_call_target="tpu_custom_call" | custom-call | flops 10000000000 | bytes 4194304 | tf_op jit(solution)/shard_map/pallas_call | solution.py:368
  36.2 1.5 %collective-permute-start.10 = (bf16[4,2,2048]{2,1,0:T(2,128)(2,1)S(1)}, bf16[4,2,2048]{2,1,0:T(2,128)(2,1)S(1)}, u32[]{:S(2)}, u32[]{:S(2)}) collective-permute-start(bf16[4,2,2048]{2,1,0:T(2,128)(2,1)S(1)} %shard_map.109.refs_0_), channel_id=1, source_target_pairs={{0,12},{4,8},{8,4},{12,0},{1,13},{5,9},{9,5},{13,1},{2,14},{6,10},... | collective-permute-start | bytes 98312 | tf_op jit(solution)/shard_map/ppermute | solution.py:245
  37.6 0.0 collective-permute-start.8
  37.7 3.0 %collective-permute-start.9 = (bf16[4,2,2048]{2,1,0:T(2,128)(2,1)S(1)}, bf16[4,2,2048]{2,1,0:T(2,128)(2,1)S(1)}, u32[]{:S(2)}, u32[]{:S(2)}) collective-permute-start(bf16[4,2,2048]{2,1,0:T(2,128)(2,1)S(1)} %shard_map.109.refs_0_), channel_id=1, source_target_pairs={{0,4},{4,0},{8,12},{12,8},{1,5},{5,1},{9,13},{13,9},{2,6},{6,2},{1... | collective-permute-start | bytes 98312 | tf_op jit(solution)/shard_map/ppermute | solution.py:245
  40.6 1.6 %collective-permute-done.10.refs_3_ = bf16[4,2,2048]{2,1,0:T(2,128)(2,1)S(1)} collective-permute-done((bf16[4,2,2048]{2,1,0:T(2,128)(2,1)S(1)}, bf16[4,2,2048]{2,1,0:T(2,128)(2,1)S(1)}, u32[]{:S(2)}, u32[]{:S(2)}) %collective-permute-start.10) | collective-permute-done | bytes 32800 | tf_op jit(solution)/shard_map/ppermute | solution.py:245
  42.2 0.6 %collective-permute-done.8.refs_1_ = bf16[4,2,2048]{2,1,0:T(2,128)(2,1)S(1)} collective-permute-done((bf16[4,2,2048]{2,1,0:T(2,128)(2,1)S(1)}, bf16[4,2,2048]{2,1,0:T(2,128)(2,1)S(1)}, u32[]{:S(2)}, u32[]{:S(2)}) %collective-permute-start.8) | collective-permute-done | bytes 32800 | tf_op jit(solution)/shard_map/ppermute | solution.py:245
  42.8 0.0 collective-permute-done.9.refs_2_
  42.9 1.5 %shard_map.112 = (f32[8,2,2048]{2,1,0:T(2,128)S(1)}, f32[8,2,2048]{2,1,0:T(2,128)S(1)}) custom-call(bf16[2048,4096]{1,0:T(8,128)(2,1)S(1)} %bitcast.5, bf16[4,2,2048]{2,1,0:T(2,128)(2,1)S(1)} %shard_map.109.refs_0_, bf16[4,2,2048]{2,1,0:T(2,128)(2,1)S(1)} %collective-permute-done.8.refs_1_, bf16[4,2,2048]{2,1,0:T(2,128)(2,1)S(1)} %collective-permute-done.9.refs_2_, ...), custom_call_target="tpu_custom_call" | custom-call | flops 268435456 | bytes 8388608 | tf_op jit(solution)/shard_map/pallas_call | solution.py:392
  44.4 0.1 collective-permute-start.13
  44.5 1.5 %shard_map.110 = (f32[8,2,2048]{2,1,0:T(2,128)S(1)}, f32[8,2,2048]{2,1,0:T(2,128)S(1)}) custom-call(bf16[2048,4096]{1,0:T(8,128)(2,1)S(1)} %bitcast.5, bf16[4,2,2048]{2,1,0:T(2,128)(2,1)S(1)} %shard_map.109.refs_0_, bf16[4,2,2048]{2,1,0:T(2,128)(2,1)S(1)} %collective-permute-done.8.refs_1_, bf16[4,2,2048]{2,1,0:T(2,128)(2,1)S(1)} %collective-permute-done.9.refs_2_, ...), custom_call_target="tpu_custom_call" | custom-call | flops 268435456 | bytes 8388608 | tf_op jit(solution)/shard_map/pallas_call | solution.py:392
  46.1 0.6 collective-permute-start.11
  46.6 0.0 collective-permute-done.13.b_ref
  46.7 1.1 %collective-permute-start.14 = (f32[4,2,2048]{2,1,0:T(2,128)S(1)}, f32[4,2,2048]{2,1,0:T(2,128)S(1)}, u32[]{:S(2)}, u32[]{:S(2)}) collective-permute-start(f32[4,2,2048]{2,1,0:T(2,128)S(1)} %get-tuple-element.46), channel_id=1, source_target_pairs={{0,2},{1,3},{2,0},{3,1},{4,6},{5,7},{6,4},{7,5},{8,10},{9,11},{10,... | collective-permute-start | bytes 196616 | tf_op jit(solution)/shard_map/ppermute | solution.py:249
  47.8 0.0 collective-permute-done.11.b_ref
  47.8 1.0 %collective-permute-start.12 = (f32[4,2,2048]{2,1,0:T(2,128)S(1)}, f32[4,2,2048]{2,1,0:T(2,128)S(1)}, u32[]{:S(2)}, u32[]{:S(2)}) collective-permute-start(f32[4,2,2048]{2,1,0:T(2,128)S(1)} %get-tuple-element.42), channel_id=1, source_target_pairs={{0,2},{1,3},{2,0},{3,1},{4,6},{5,7},{6,4},{7,5},{8,10},{9,11},{10,... | collective-permute-start | bytes 196616 | tf_op jit(solution)/shard_map/ppermute | solution.py:249
  48.8 2.6 %collective-permute-done.14.refs_3_ = f32[4,2,2048]{2,1,0:T(2,128)S(1)} collective-permute-done((f32[4,2,2048]{2,1,0:T(2,128)S(1)}, f32[4,2,2048]{2,1,0:T(2,128)S(1)}, u32[]{:S(2)}, u32[]{:S(2)}) %collective-permute-start.14) | collective-permute-done | bytes 65568 | tf_op jit(solution)/shard_map/ppermute | solution.py:249
  51.4 1.0 %collective-permute-done.12.refs_1_ = f32[4,2,2048]{2,1,0:T(2,128)S(1)} collective-permute-done((f32[4,2,2048]{2,1,0:T(2,128)S(1)}, f32[4,2,2048]{2,1,0:T(2,128)S(1)}, u32[]{:S(2)}, u32[]{:S(2)}) %collective-permute-start.12) | collective-permute-done | bytes 65568 | tf_op jit(solution)/shard_map/ppermute | solution.py:249
  52.4 0.1 shard_map.114
  52.5 2.1 %collective-permute-start.15 = (bf16[2,4096]{1,0:T(2,128)(2,1)S(1)}, bf16[2,4096]{1,0:T(2,128)(2,1)S(1)}, u32[]{:S(2)}, u32[]{:S(2)}) collective-permute-start(bf16[2,4096]{1,0:T(2,128)(2,1)S(1)} %get-tuple-element.47), channel_id=1, source_target_pairs={{0,12},{4,8},{8,4},{12,0},{1,13},{5,9},{9,5},{13,1},{2,14},{6,10},... | collective-permute-start | bytes 49160 | tf_op jit(solution)/shard_map/ppermute | solution.py:245
  54.5 1.1 %collective-permute-start.16 = (bf16[2,4096]{1,0:T(2,128)(2,1)S(1)}, bf16[2,4096]{1,0:T(2,128)(2,1)S(1)}, u32[]{:S(2)}, u32[]{:S(2)}) collective-permute-start(bf16[2,4096]{1,0:T(2,128)(2,1)S(1)} %get-tuple-element.48), channel_id=1, source_target_pairs={{0,8},{4,12},{8,0},{12,4},{1,9},{5,13},{9,1},{13,5},{2,10},{6,14},... | collective-permute-start | bytes 49160 | tf_op jit(solution)/shard_map/ppermute | solution.py:245
  55.6 1.3 %collective-permute-start.17 = (bf16[2,4096]{1,0:T(2,128)(2,1)S(1)}, bf16[2,4096]{1,0:T(2,128)(2,1)S(1)}, u32[]{:S(2)}, u32[]{:S(2)}) collective-permute-start(bf16[2,4096]{1,0:T(2,128)(2,1)S(1)} %get-tuple-element.49), channel_id=1, source_target_pairs={{0,4},{4,0},{8,12},{12,8},{1,5},{5,1},{9,13},{13,9},{2,6},{6,2},{1... | collective-permute-start | bytes 49160 | tf_op jit(solution)/shard_map/ppermute | solution.py:245
  56.9 1.1 %collective-permute-done.15.refs_0_ = bf16[2,4096]{1,0:T(2,128)(2,1)S(1)} collective-permute-done((bf16[2,4096]{1,0:T(2,128)(2,1)S(1)}, bf16[2,4096]{1,0:T(2,128)(2,1)S(1)}, u32[]{:S(2)}, u32[]{:S(2)}) %collective-permute-start.15) | collective-permute-done | bytes 16416 | tf_op jit(solution)/shard_map/ppermute | solution.py:245
  58.1 1.1 %collective-permute-done.16.refs_1_ = bf16[2,4096]{1,0:T(2,128)(2,1)S(1)} collective-permute-done((bf16[2,4096]{1,0:T(2,128)(2,1)S(1)}, bf16[2,4096]{1,0:T(2,128)(2,1)S(1)}, u32[]{:S(2)}, u32[]{:S(2)}) %collective-permute-start.16) | collective-permute-done | bytes 16416 | tf_op jit(solution)/shard_map/ppermute | solution.py:245
  59.2 0.2 collective-permute-done.17.refs_2_
  59.4 0.6 %shard_map.115 = bf16[2,16384]{1,0:T(2,128)(2,1)} custom-call(bf16[2,4096]{1,0:T(2,128)(2,1)S(1)} %collective-permute-done.15.refs_0_, bf16[2,4096]{1,0:T(2,128)(2,1)S(1)} %collective-permute-done.16.refs_1_, bf16[2,4096]{1,0:T(2,128)(2,1)S(1)} %collective-permute-done.17.refs_2_, bf16[2,4096]{1,0:T(2,128)(2,1)S(1)} %get-tuple-element.50.refs_3_), custom_call_target="tpu_custom_call" | custom-call | tf_op jit(solution)/shard_map/pallas_call | solution.py:423
  (23 shorter events, 0.1 us)
Async XLA Ops:
  0.0 1.2 %copy-start.4 = (f32[16384]{0:T(1024)S(1)}, f32[16384]{0:T(1024)}, u32[]{:S(2)}) copy-start(f32[16384]{0:T(1024)} %param.11) | copy-start | bytes 196612
  0.0 1.3 %copy-start.6 = (s32[2]{0:T(128)S(1)}, s32[2]{0:T(128)}, u32[]{:S(2)}) copy-start(s32[2]{0:T(128)} %param.18) | copy-start | bytes 28
  0.0 1.3 %copy-start.2 = (bf16[2,256,1024]{2,1,0:T(8,128)(2,1)S(1)}, bf16[2,256,1024]{2,1,0:T(8,128)(2,1)}, u32[]{:S(2)}) copy-start(bf16[2,256,1024]{2,1,0:T(8,128)(2,1)} %keys_ref.3) | copy-start | bytes 3145732
  0.0 1.6 %copy-start.3 = (bf16[2,256,1024]{2,1,0:T(8,128)(2,1)S(1)}, bf16[2,256,1024]{2,1,0:T(8,128)(2,1)}, u32[]{:S(2)}) copy-start(bf16[2,256,1024]{2,1,0:T(8,128)(2,1)} %values_ref.3) | copy-start | bytes 3145732
  0.0 1.0 %copy-start.7 = (bf16[2,16384]{1,0:T(2,128)(2,1)S(1)}, bf16[2,16384]{1,0:T(2,128)(2,1)}, u32[]{:S(2)}) copy-start(bf16[2,16384]{1,0:T(2,128)(2,1)} %tokens_ref.1) | copy-start | bytes 196612
  1.0 19.1 %slice-start = ((s8[16777216]{0:T(1024)(128)(4,1)}), s8[4194304]{0:T(1024)(128)(4,1)S(1)}, s32[]{:S(2)}) async-start(s8[16777216]{0:T(1024)(128)(4,1)} %bitcast.2), calls=%async_computation.1 | async-start | bytes 8388608
  1.6 18.4 %slice-start.1 = ((s8[16777216]{0:T(1024)(128)(4,1)}), s8[4194304]{0:T(1024)(128)(4,1)S(1)}, s32[]{:S(2)}) async-start(s8[16777216]{0:T(1024)(128)(4,1)} %bitcast.2), calls=%async_computation.2 | async-start | bytes 8388608
  1.6 18.4 %slice-start.2 = ((s8[16777216]{0:T(1024)(128)(4,1)}), s8[4194304]{0:T(1024)(128)(4,1)S(1)}, s32[]{:S(2)}) async-start(s8[16777216]{0:T(1024)(128)(4,1)} %bitcast.2), calls=%async_computation.3 | async-start | bytes 8388608
  1.6 18.4 %slice-start.3 = ((s8[16777216]{0:T(1024)(128)(4,1)}), s8[4194304]{0:T(1024)(128)(4,1)S(1)}, s32[]{:S(2)}) async-start(s8[16777216]{0:T(1024)(128)(4,1)} %bitcast.2), calls=%async_computation.4 | async-start | bytes 8388608
  1.6 18.4 %copy-start = (bf16[4096,256]{1,0:T(8,128)(2,1)S(1)}, bf16[4096,256]{1,0:T(8,128)(2,1)}, u32[]{:S(2)}) copy-start(bf16[4096,256]{1,0:T(8,128)(2,1)} %key_ref.3) | copy-start | bytes 6291460
  1.6 18.5 %copy-start.1 = (bf16[4096,256]{1,0:T(8,128)(2,1)S(1)}, bf16[4096,256]{1,0:T(8,128)(2,1)}, u32[]{:S(2)}) copy-start(bf16[4096,256]{1,0:T(8,128)(2,1)} %value_ref.3) | copy-start | bytes 6291460
  1.9 16.0 %collective-permute-start.1 = (bf16[768,256]{1,0:T(8,128)(2,1)S(1)}, bf16[768,256]{1,0:T(8,128)(2,1)S(1)}, u32[]{:S(2)}, u32[]{:S(2)}) collective-permute-start(bf16[768,256]{1,0:T(8,128)(2,1)S(1)} %get-tuple-element.31), channel_id=1, source_target_pairs={{0,2},{1,3},{2,0},{3,1},{4,6},{5,7},{6,4},{7,5},{8,10},{9,11},{10,... | collective-permute-start | bytes 1179656 | tf_op jit(solution)/shard_map/ppermute | solution.py:249
  17.9 4.2 %collective-permute-start.2 = (bf16[1040,256]{1,0:T(8,128)(2,1)S(1)}, bf16[1040,256]{1,0:T(8,128)(2,1)S(1)}, u32[]{:S(2)}, u32[]{:S(2)}) collective-permute-start(bf16[1040,256]{1,0:T(8,128)(2,1)S(1)} %get-tuple-element.32), channel_id=1, source_target_pairs={{0,1},{1,0},{2,3},{3,2},{4,5},{5,4},{6,7},{7,6},{8,9},{9,8},{10,11... | collective-permute-start | bytes 1597448 | tf_op jit(solution)/shard_map/ppermute | solution.py:249
  17.9 17.4 %collective-permute-start.7 = (bf16[1040,256]{1,0:T(8,128)(2,1)S(1)}, bf16[1040,256]{1,0:T(8,128)(2,1)S(1)}, u32[]{:S(2)}, u32[]{:S(2)}) collective-permute-start(bf16[1040,256]{1,0:T(8,128)(2,1)S(1)} %get-tuple-element.38), channel_id=1, source_target_pairs={{0,3},{1,2},{2,1},{3,0},{4,7},{5,6},{6,5},{7,4},{8,11},{9,10},{10,... | collective-permute-start | bytes 1597448 | tf_op jit(solution)/shard_map/ppermute | solution.py:249
  17.9 4.1 %collective-permute-start = (bf16[16,2,2048]{2,1,0:T(2,128)(2,1)S(1)}, bf16[16,2,2048]{2,1,0:T(2,128)(2,1)S(1)}, u32[]{:S(2)}, u32[]{:S(2)}) collective-permute-start(bf16[16,2,2048]{2,1,0:T(2,128)(2,1)S(1)} %all_to_all.5.refs_3_.rows_ref._), channel_id=1, source_target_pairs={{0,1},{1,0},{2,3},{3,2},{4,5},{5,4},{6,7},{7,6},{8,9},{9,8},{10,11... | collective-permute-start | bytes 393224 | tf_op jit(solution)/shard_map/ppermute | solution.py:245
  18.4 16.9 %collective-permute-start.6 = (bf16[272,256]{1,0:T(8,128)(2,1)S(1)}, bf16[272,256]{1,0:T(8,128)(2,1)S(1)}, u32[]{:S(2)}, u32[]{:S(2)}) collective-permute-start(bf16[272,256]{1,0:T(8,128)(2,1)S(1)} %get-tuple-element.37), channel_id=1, source_target_pairs={{0,2},{1,3},{2,0},{3,1},{4,6},{5,7},{6,4},{7,5},{8,10},{9,11},{10,... | collective-permute-start | bytes 417800 | tf_op jit(solution)/shard_map/ppermute | solution.py:249
  22.0 11.9 %copy-start.5 = (f32[1,128]{1,0:T(1,128)S(1)}, f32[1,128]{1,0:T(1,128)}, u32[]{:S(2)}) copy-start(f32[1,128]{1,0:T(1,128)} %constant.2.clone.frequency_ref) | copy-start | bytes 1540
  24.0 7.2 %collective-permute-start.3 = (f32[4,2,2560]{2,1,0:T(2,128)S(1)}, f32[4,2,2560]{2,1,0:T(2,128)S(1)}, u32[]{:S(2)}, u32[]{:S(2)}) collective-permute-start(f32[4,2,2560]{2,1,0:T(2,128)S(1)} %get-tuple-element.33), channel_id=1, source_target_pairs={{0,12},{4,8},{8,4},{12,0},{1,13},{5,9},{9,5},{13,1},{2,14},{6,10},... | collective-permute-start | bytes 245768 | tf_op jit(solution)/shard_map/ppermute | solution.py:245
  25.5 8.4 %collective-permute-start.4 = (f32[4,2,2560]{2,1,0:T(2,128)S(1)}, f32[4,2,2560]{2,1,0:T(2,128)S(1)}, u32[]{:S(2)}, u32[]{:S(2)}) collective-permute-start(f32[4,2,2560]{2,1,0:T(2,128)S(1)} %get-tuple-element.34), channel_id=1, source_target_pairs={{0,8},{4,12},{8,0},{12,4},{1,9},{5,13},{9,1},{13,5},{2,10},{6,14},... | collective-permute-start | bytes 245768 | tf_op jit(solution)/shard_map/ppermute | solution.py:245
  25.5 8.4 %collective-permute-start.5 = (f32[4,2,2560]{2,1,0:T(2,128)S(1)}, f32[4,2,2560]{2,1,0:T(2,128)S(1)}, u32[]{:S(2)}, u32[]{:S(2)}) collective-permute-start(f32[4,2,2560]{2,1,0:T(2,128)S(1)} %get-tuple-element.35), channel_id=1, source_target_pairs={{0,4},{4,0},{8,12},{12,8},{1,5},{5,1},{9,13},{13,9},{2,6},{6,2},{1... | collective-permute-start | bytes 245768 | tf_op jit(solution)/shard_map/ppermute | solution.py:245
  33.9 8.9 %slice-start.4 = ((s8[16777216]{0:T(1024)(128)(4,1)}), s8[4194304]{0:T(1024)(128)(4,1)S(1)}, s32[]{:S(2)}) async-start(s8[16777216]{0:T(1024)(128)(4,1)} %bitcast.4), calls=%async_computation.5 | async-start | bytes 8388608
  34.8 8.1 %slice-start.5 = ((s8[16777216]{0:T(1024)(128)(4,1)}), s8[4194304]{0:T(1024)(128)(4,1)S(1)}, s32[]{:S(2)}) async-start(s8[16777216]{0:T(1024)(128)(4,1)} %bitcast.4), calls=%async_computation.6 | async-start | bytes 8388608
  34.8 8.1 %slice-start.6 = ((s8[16777216]{0:T(1024)(128)(4,1)}), s8[4194304]{0:T(1024)(128)(4,1)S(1)}, s32[]{:S(2)}) async-start(s8[16777216]{0:T(1024)(128)(4,1)} %bitcast.4), calls=%async_computation.7 | async-start | bytes 8388608
  34.8 8.1 %slice-start.7 = ((s8[16777216]{0:T(1024)(128)(4,1)}), s8[4194304]{0:T(1024)(128)(4,1)S(1)}, s32[]{:S(2)}) async-start(s8[16777216]{0:T(1024)(128)(4,1)} %bitcast.4), calls=%async_computation.8 | async-start | bytes 8388608
  36.2 6.1 %collective-permute-start.10 = (bf16[4,2,2048]{2,1,0:T(2,128)(2,1)S(1)}, bf16[4,2,2048]{2,1,0:T(2,128)(2,1)S(1)}, u32[]{:S(2)}, u32[]{:S(2)}) collective-permute-start(bf16[4,2,2048]{2,1,0:T(2,128)(2,1)S(1)} %shard_map.109.refs_0_), channel_id=1, source_target_pairs={{0,12},{4,8},{8,4},{12,0},{1,13},{5,9},{9,5},{13,1},{2,14},{6,10},... | collective-permute-start | bytes 98312 | tf_op jit(solution)/shard_map/ppermute | solution.py:245
  37.6 5.2 %collective-permute-start.8 = (bf16[4,2,2048]{2,1,0:T(2,128)(2,1)S(1)}, bf16[4,2,2048]{2,1,0:T(2,128)(2,1)S(1)}, u32[]{:S(2)}, u32[]{:S(2)}) collective-permute-start(bf16[4,2,2048]{2,1,0:T(2,128)(2,1)S(1)} %shard_map.109.refs_0_), channel_id=1, source_target_pairs={{0,8},{4,12},{8,0},{12,4},{1,9},{5,13},{9,1},{13,5},{2,10},{6,14},... | collective-permute-start | bytes 98312 | tf_op jit(solution)/shard_map/ppermute | solution.py:245
  37.7 5.2 %collective-permute-start.9 = (bf16[4,2,2048]{2,1,0:T(2,128)(2,1)S(1)}, bf16[4,2,2048]{2,1,0:T(2,128)(2,1)S(1)}, u32[]{:S(2)}, u32[]{:S(2)}) collective-permute-start(bf16[4,2,2048]{2,1,0:T(2,128)(2,1)S(1)} %shard_map.109.refs_0_), channel_id=1, source_target_pairs={{0,4},{4,0},{8,12},{12,8},{1,5},{5,1},{9,13},{13,9},{2,6},{6,2},{1... | collective-permute-start | bytes 98312 | tf_op jit(solution)/shard_map/ppermute | solution.py:245
  44.4 2.2 %collective-permute-start.13 = (f32[8,2,2048]{2,1,0:T(2,128)S(1)}, f32[8,2,2048]{2,1,0:T(2,128)S(1)}, u32[]{:S(2)}, u32[]{:S(2)}) collective-permute-start(f32[8,2,2048]{2,1,0:T(2,128)S(1)} %get-tuple-element.44), channel_id=1, source_target_pairs={{0,1},{1,0},{2,3},{3,2},{4,5},{5,4},{6,7},{7,6},{8,9},{9,8},{10,11... | collective-permute-start | bytes 393224 | tf_op jit(solution)/shard_map/ppermute | solution.py:249
  46.1 1.7 %collective-permute-start.11 = (f32[8,2,2048]{2,1,0:T(2,128)S(1)}, f32[8,2,2048]{2,1,0:T(2,128)S(1)}, u32[]{:S(2)}, u32[]{:S(2)}) collective-permute-start(f32[8,2,2048]{2,1,0:T(2,128)S(1)} %get-tuple-element.40), channel_id=1, source_target_pairs={{0,1},{1,0},{2,3},{3,2},{4,5},{5,4},{6,7},{7,6},{8,9},{9,8},{10,11... | collective-permute-start | bytes 393224 | tf_op jit(solution)/shard_map/ppermute | solution.py:249
  46.7 4.7 %collective-permute-start.14 = (f32[4,2,2048]{2,1,0:T(2,128)S(1)}, f32[4,2,2048]{2,1,0:T(2,128)S(1)}, u32[]{:S(2)}, u32[]{:S(2)}) collective-permute-start(f32[4,2,2048]{2,1,0:T(2,128)S(1)} %get-tuple-element.46), channel_id=1, source_target_pairs={{0,2},{1,3},{2,0},{3,1},{4,6},{5,7},{6,4},{7,5},{8,10},{9,11},{10,... | collective-permute-start | bytes 196616 | tf_op jit(solution)/shard_map/ppermute | solution.py:249
  47.8 4.6 %collective-permute-start.12 = (f32[4,2,2048]{2,1,0:T(2,128)S(1)}, f32[4,2,2048]{2,1,0:T(2,128)S(1)}, u32[]{:S(2)}, u32[]{:S(2)}) collective-permute-start(f32[4,2,2048]{2,1,0:T(2,128)S(1)} %get-tuple-element.42), channel_id=1, source_target_pairs={{0,2},{1,3},{2,0},{3,1},{4,6},{5,7},{6,4},{7,5},{8,10},{9,11},{10,... | collective-permute-start | bytes 196616 | tf_op jit(solution)/shard_map/ppermute | solution.py:249
  52.5 5.6 %collective-permute-start.15 = (bf16[2,4096]{1,0:T(2,128)(2,1)S(1)}, bf16[2,4096]{1,0:T(2,128)(2,1)S(1)}, u32[]{:S(2)}, u32[]{:S(2)}) collective-permute-start(bf16[2,4096]{1,0:T(2,128)(2,1)S(1)} %get-tuple-element.47), channel_id=1, source_target_pairs={{0,12},{4,8},{8,4},{12,0},{1,13},{5,9},{9,5},{13,1},{2,14},{6,10},... | collective-permute-start | bytes 49160 | tf_op jit(solution)/shard_map/ppermute | solution.py:245
  54.5 4.6 %collective-permute-start.16 = (bf16[2,4096]{1,0:T(2,128)(2,1)S(1)}, bf16[2,4096]{1,0:T(2,128)(2,1)S(1)}, u32[]{:S(2)}, u32[]{:S(2)}) collective-permute-start(bf16[2,4096]{1,0:T(2,128)(2,1)S(1)} %get-tuple-element.48), channel_id=1, source_target_pairs={{0,8},{4,12},{8,0},{12,4},{1,9},{5,13},{9,1},{13,5},{2,10},{6,14},... | collective-permute-start | bytes 49160 | tf_op jit(solution)/shard_map/ppermute | solution.py:245
  55.6 3.7 %collective-permute-start.17 = (bf16[2,4096]{1,0:T(2,128)(2,1)S(1)}, bf16[2,4096]{1,0:T(2,128)(2,1)S(1)}, u32[]{:S(2)}, u32[]{:S(2)}) collective-permute-start(bf16[2,4096]{1,0:T(2,128)(2,1)S(1)} %get-tuple-element.49), channel_id=1, source_target_pairs={{0,4},{4,0},{8,12},{12,8},{1,5},{5,1},{9,13},{13,9},{2,6},{6,2},{1... | collective-permute-start | bytes 49160 | tf_op jit(solution)/shard_map/ppermute | solution.py:245

commit v19 on v17

--- a/solution.py
+++ b/solution.py
@@ -32,10 +32,17 @@
 
 
 def project_kernel(own, wide, plane, rows_ref, query_ref, key_ref, value_ref, *refs):
-    owners, rows, half = rows_ref.shape
+    half = query_ref.shape[0] // 2
     core = lax.axis_index("gz")
     at_row = pl.multiple_of((core if own else 1 - core) * half, half)
-    normed = rows_ref[...].reshape(owners * rows, half)
+    if own:
+        normed = rows_ref[...].reshape(-1, half)
+    else:
+        count, cols = refs[0].shape[0], rows_ref.shape[1]
+        normed = jnp.concatenate(
+            [rows_ref[n * count : (n + 1) * count] for n in range(half // cols)], 1
+        )
+        owners, rows = refs[-1].shape[:2]
     sums_ref = refs[-1]
     at = 0
     for weight in (query_ref, key_ref, value_ref):
@@ -50,7 +57,7 @@
             if own:
                 sums_ref[:, at : at + step] = part
             else:
-                part = part + refs[1][:, at : at + step]
+                part = part + refs[0][:, at : at + step]
                 sums_ref[:, :, at : at + step] = part.reshape(owners, rows, step)
             at += step
     if not own:
@@ -58,7 +65,7 @@
         own_plane = 2 * lax.axis_index("gy") + core
         for k in range(wide):
             for l in range(plane):
-                refs[2 + k][l] = sums_ref[(own_wide ^ k) * plane + (own_plane ^ l)]
+                refs[1 + k][l] = sums_ref[(own_wide ^ k) * plane + (own_plane ^ l)]
 
 
 def own_place():
@@ -85,6 +92,24 @@
                 start += slots
         if with_lengths:
             write_lengths(rows, lengths_ref, block)
+
+
+def mate_kernel(lengths_ref, keys_ref, values_ref, rows_ref, mate_ref):
+    rows, slots, _ = keys_ref.shape
+    cols = mate_ref.shape[1]
+    half = rows_ref.shape[-1]
+    normed = rows_ref[...].reshape(-1, half)
+    count = normed.shape[0]
+    start = 0
+    for c in range(0, half, cols):
+        mate_ref[start : start + count] = normed[:, c : c + cols]
+        start += count
+    at = pl.multiple_of((own_place() ^ 1) * cols, cols)
+    for cache_ref in (keys_ref, values_ref):
+        for r in range(rows):
+            mate_ref[start : start + slots] = cache_ref[r, :, pl.ds(at, cols)]
+            start += slots
+    write_lengths(rows, lengths_ref, mate_ref)
 
 
 def pass_kernel(*refs):
@@ -114,11 +139,12 @@
         for p in range(pairs):
             l, r = members[p // rows], p % rows
             ref, at = whole[(l + 1) // 2], values * rows + r
+            shift = ref.shape[0] - whole[0].shape[0] if l == 1 else 0
             if l % 2 == 0 and l:
                 ref = firsts[l // 2 - 1]
                 if at >= rows + early:
                     ref, at = lasts[l // 2 - 1], at - rows - early
-            parts.append(ref[at * slots : (at + 1) * slots])
+            parts.append(ref[shift + at * slots : shift + (at + 1) * slots])
         return jnp.concatenate(parts, 1)
 
     filled = []
@@ -318,12 +344,22 @@
 
     plan = [(l, every, every[:early], False) for l in range(2, plane, 2)]
     plan += [(l, (), every[early:], True) for l in range(2, plane, 2)]
-    plan += [(l, every, every, True) for l in range(1, plane, 2)]
+    plan += [(l, every, every, True) for l in range(3, plane, 2)]
     blocks = cut(plan, normed)
     firsts, rest = blocks[:even], blocks[even:]
     firsts = [swap_plane(firsts[s], 2 * s + 2) for s in range(even)]
     own_half = swap_blocks(normed, ROW_AXES)
-    other_half = swap_pairs(own_half, "gz", 1)
+    pieces = half // kv_cols
+    mate = pl.pallas_call(
+        mate_kernel,
+        out_shape=jax.ShapeDtypeStruct(
+            (pieces * owners * rows + 2 * rows * slots + 16, kv_cols), cache_keys.dtype
+        ),
+        in_specs=[IN_VMEM] * 4,
+        out_specs=IN_VMEM,
+        compiler_params=params(8),
+    )(lengths.reshape(1, -1), cache_keys, cache_values, own_half)
+    mate = swap_plane(mate, 1)
     rest = pl.pallas_call(
         pass_kernel,
         out_shape=[jax.ShapeDtypeStruct(value.shape, value.dtype) for value in rest],
@@ -333,7 +369,7 @@
         compiler_params=params(1),
     )(*rest, own_half, *firsts)
     lasts = [swap_plane(rest[s], 2 * s + 2) for s in range(even)]
-    odd = [swap_plane(rest[even + s], 2 * s + 1) for s in range(even + 1)]
+    odd = [mate, *[swap_plane(rest[even + s], 2 * s + 3) for s in range(even)]]
     (mine,) = cut([(0, every, every, True)], own_half)
     held = [*firsts, *lasts, mine, *odd]
     weights = (query_weight, key_weight, value_weight)
@@ -349,12 +385,12 @@
     partial = pl.pallas_call(
         functools.partial(project_kernel, False, wide, plane),
         out_shape=[jax.ShapeDtypeStruct((plane, rows, cols), jnp.float32)] * wide,
-        in_specs=[IN_VMEM] * 6,
+        in_specs=[IN_VMEM] * 5,
         out_specs=[IN_VMEM] * wide,
         scratch_shapes=[pltpu.VMEM((owners, rows, cols), jnp.float32)],
         compiler_params=params(8),
         cost_estimate=half_cost,
-    )(other_half, *weights, odd[0], partial)
+    )(mate, *weights, partial)
     partial = swap_wide(partial)
 
     half_dim = HD // 2

time: 60.2 us -> 80.5 us (1.34)
  local copies, waits for them, and re-layouts: 1.27 us -> 14.4 us
  blocking collectives: 13 us -> 0 us
  waiting for transfers between devices: 14.2 us -> 26.3 us
  starting transfers between devices: 21.3 us -> 27 us
  Pallas kernels: 9.97 us -> 12.3 us
    unnamed x26 -> x32, local copies, waits for them, and re-layouts: 1.27 us -> 14.4 us
    all_to_all x1 -> x0, blocking collectives: 13 us -> none  [swap_blocks(): return lax.all_to_all(blocks, axes, split_axis=0, concat_axis=0, tiled=True)]
    all_to_all x0 -> x1, starting transfers between devices: none -> 7.37 us  [swap_blocks(): return lax.all_to_all(blocks, axes, split_axis=0, concat_axis=0, tiled=True)]
    ppermute x8, waiting for transfers between devices: 4.12 us -> 9.6 us  [swap_plane(): lax.ppermute(value, PLANE, [(i, i ^ step) for i in range(lax.axis_size(PL...]
    all_to_all x0 -> x1, waiting for transfers between devices: none -> 4.16 us  [swap_blocks(): return lax.all_to_all(blocks, axes, split_axis=0, concat_axis=0, tiled=True)]
    ppermute x10 -> x9, waiting for transfers between devices: 10.1 us -> 12.5 us  [swap_pairs(): lax.ppermute(value, axis, [(i, i ^ step) for i in range(lax.axis_size(axi...]
    pallas_call x2, Pallas kernels: 0.29 us -> 1.91 us  [cut(): pl.pallas_call(functools.partial(cut_kernel, plan), out_shape=[jax.ShapeD...]
    ppermute x8, starting transfers between devices: 7.55 us -> 6.23 us  [swap_plane(): lax.ppermute(value, PLANE, [(i, i ^ step) for i in range(lax.axis_size(PL...]
  transfers between devices with their start and end apart: 18 -> 18, of which waited for: 10 -> 11; matrix products, arithmetic and copies ran while one was open for 0% -> 0% of each run, Pallas kernels for 11% -> 10%
where the time goes in v19:
time: 80.5 us; the launch traced here: 80.2 us
  starting transfers between devices  27 us (34%)
  waiting for transfers between devices  26.3 us (33%)
  local copies, waits for them, and re-layouts  14.4 us (18%)
  Pallas kernels  12.3 us (15%)
    unnamed x32, local copies, waits for them, and re-layouts  14.4 us
    ppermute x9, starting transfers between devices, swap_pairs(): lax.ppermute(value, axis, [(i, i ^ step) for i in range(lax.axis_size(axi...  13.4 us
    ppermute x9, waiting for transfers between devices, swap_pairs(): lax.ppermute(value, axis, [(i, i ^ step) for i in range(lax.axis_size(axi...  12.5 us
    ppermute x8, waiting for transfers between devices, swap_plane(): lax.ppermute(value, PLANE, [(i, i ^ step) for i in range(lax.axis_size(PL...  9.6 us
    all_to_all x1, starting transfers between devices, swap_blocks(): return lax.all_to_all(blocks, axes, split_axis=0, concat_axis=0, tiled=True)  7.37 us
    ppermute x8, starting transfers between devices, swap_plane(): lax.ppermute(value, PLANE, [(i, i ^ step) for i in range(lax.axis_size(PL...  6.23 us
    all_to_all x1, waiting for transfers between devices, swap_blocks(): return lax.all_to_all(blocks, axes, split_axis=0, concat_axis=0, tiled=True)  4.16 us
    pallas_call x2, Pallas kernels, shards(): pl.pallas_call(functools.partial(output_kernel, p * part_cols, part_cols,...  3.09 us
  transfers between devices with their start and end apart: 18, of which 11 were waited for; matrix products, arithmetic and copies ran while one was open for 0% of the time, Pallas kernels for 10%

profile of v19, /device:TPU:0, one launch (start us, length us, event | category | flops | bytes accessed | tf_op | source)
XLA Modules:
  0.0 80.2 jit_solution(7201710259066715294)
XLA Ops:
  0.0 1.0 %copy-done.11 = bf16[2,16384]{1,0:T(2,128)(2,1)S(1)} copy-done((bf16[2,16384]{1,0:T(2,128)(2,1)S(1)}, bf16[2,16384]{1,0:T(2,128)(2,1)}, u32[]{:S(2)}) %copy-start.11) | copy-done | bytes 65560
  1.0 0.2 shard_map.100.scaled_ref
  1.2 0.0 copy-done.8
  1.2 0.7 shard_map.101._
  2.0 7.4 %all-to-all-start = ((bf16[16,2,2048]{2,1,0:T(2,128)(2,1)}), bf16[16,2,2048]{2,1,0:T(2,128)(2,1)S(1)}, u32[]{:S(2)}, u32[]{:S(2)}) async-start(bf16[16,2,2048]{2,1,0:T(2,128)(2,1)} %shard_map.101._), calls=%async_computation | async-start | bytes 262144 | tf_op jit(solution)/shard_map/all_to_all | solution.py:267
  9.4 0.0 copy-done.9
  9.4 0.0 copy-done.2
  9.4 0.0 copy-done.3
  9.4 1.8 %shard_map.107 = (bf16[768,256]{1,0:T(8,128)(2,1)}, bf16[272,256]{1,0:T(8,128)(2,1)S(1)}, bf16[1040,256]{1,0:T(8,128)(2,1)S(1)}) custom-call(s32[1,2]{1,0:T(1,128)S(1)} %bitcast.5, bf16[2,256,1024]{2,1,0:T(8,128)(2,1)S(1)} %copy-done.2, bf16[2,256,1024]{2,1,0:T(8,128)(2,1)S(1)} %copy-done.3, bf16[16,2,2048]{2,1,0:T(2,128)(2,1)} %shard_map.101._), custom_call_target="tpu_custom_call" | custom-call | tf_op jit(solution)/shard_map/pallas_call | solution.py:331
  11.2 1.9 %collective-permute-start.4 = (bf16[768,256]{1,0:T(8,128)(2,1)}, bf16[768,256]{1,0:T(8,128)(2,1)S(1)}, u32[]{:S(2)}, u32[]{:S(2)}) collective-permute-start(bf16[768,256]{1,0:T(8,128)(2,1)} %get-tuple-element.30), channel_id=1, source_target_pairs={{0,2},{1,3},{2,0},{3,1},{4,6},{5,7},{6,4},{7,5},{8,10},{9,11},{10,... | collective-permute-start | bytes 1179656 | tf_op jit(solution)/shard_map/ppermute | solution.py:275
  13.1 4.2 %all-to-all-done.rows_ref._.refs_2_ = bf16[16,2,2048]{2,1,0:T(2,128)(2,1)S(1)} async-done(((bf16[16,2,2048]{2,1,0:T(2,128)(2,1)}), bf16[16,2,2048]{2,1,0:T(2,128)(2,1)S(1)}, u32[]{:S(2)}, u32[]{:S(2)}) %all-to-all-start) | async-done | bytes 131104 | tf_op jit(solution)/shard_map/all_to_all | solution.py:267
  17.3 0.1 shard_map.102
  17.4 0.1 collective-permute-start
  17.5 6.0 %collective-permute-done.4.refs_3_.refs_4_ = bf16[768,256]{1,0:T(8,128)(2,1)S(1)} collective-permute-done((bf16[768,256]{1,0:T(8,128)(2,1)}, bf16[768,256]{1,0:T(8,128)(2,1)S(1)}, u32[]{:S(2)}, u32[]{:S(2)}) %collective-permute-start.4) | collective-permute-done | bytes 393248 | tf_op jit(solution)/shard_map/ppermute | solution.py:275
  23.5 0.5 collective-permute-start.6
  24.0 1.0 %collective-permute-start.5 = (bf16[272,256]{1,0:T(8,128)(2,1)S(1)}, bf16[272,256]{1,0:T(8,128)(2,1)S(1)}, u32[]{:S(2)}, u32[]{:S(2)}) collective-permute-start(bf16[272,256]{1,0:T(8,128)(2,1)S(1)} %get-tuple-element.33), channel_id=1, source_target_pairs={{0,2},{1,3},{2,0},{3,1},{4,6},{5,7},{6,4},{7,5},{8,10},{9,11},{10,... | collective-permute-start | bytes 417800 | tf_op jit(solution)/shard_map/ppermute | solution.py:275
  24.9 5.8 %copy-done = bf16[4096,2048]{1,0:T(8,128)(2,1)S(1)} copy-done((bf16[4096,2048]{1,0:T(8,128)(2,1)S(1)}, bf16[4096,2048]{1,0:T(8,128)(2,1)}, u32[]{:S(2)}) %copy-start) | copy-done | bytes 16777240
  30.7 1.6 %copy-done.4 = bf16[4096,256]{1,0:T(8,128)(2,1)S(1)} copy-done((bf16[4096,256]{1,0:T(8,128)(2,1)S(1)}, bf16[4096,256]{1,0:T(8,128)(2,1)}, u32[]{:S(2)}) %copy-start.4) | copy-done | bytes 2097176
  32.3 1.6 %copy-done.6 = bf16[4096,256]{1,0:T(8,128)(2,1)S(1)} copy-done((bf16[4096,256]{1,0:T(8,128)(2,1)S(1)}, bf16[4096,256]{1,0:T(8,128)(2,1)}, u32[]{:S(2)}) %copy-start.6) | copy-done | bytes 2097176
  33.9 1.9 %shard_map.103.refs_0_ = f32[32,2560]{1,0:T(8,128)S(1)} custom-call(bf16[16,2,2048]{2,1,0:T(2,128)(2,1)S(1)} %all-to-all-done.rows_ref._.refs_2_, bf16[4096,2048]{1,0:T(8,128)(2,1)S(1)} %copy-done, bf16[4096,256]{1,0:T(8,128)(2,1)S(1)} %copy-done.4, bf16[4096,256]{1,0:T(8,128)(2,1)S(1)} %copy-done.6), custom_call_target="tpu_custom_call" | custom-call | flops 335544320 | bytes 10485760 | tf_op jit(solution)/shard_map/pallas_call | solution.py:377
  35.8 0.0 collective-permute-done.rows_ref.refs_5_.refs_7_
  35.8 0.0 copy-done.5
  35.8 3.8 %copy-done.1 = bf16[4096,2048]{1,0:T(8,128)(2,1)S(1)} copy-done((bf16[4096,2048]{1,0:T(8,128)(2,1)S(1)}, bf16[4096,2048]{1,0:T(8,128)(2,1)}, u32[]{:S(2)}) %copy-start.1) | copy-done | bytes 16777240
  39.7 0.6 copy-done.7
  40.3 1.9 %shard_map.104 = (f32[4,2,2560]{2,1,0:T(2,128)S(1)}, f32[4,2,2560]{2,1,0:T(2,128)S(1)}, f32[4,2,2560]{2,1,0:T(2,128)S(1)}, f32[4,2,2560]{2,1,0:T(2,128)S(1)}) custom-call(bf16[1296,256]{1,0:T(8,128)(2,1)S(1)} %collective-permute-done.rows_ref.refs_5_.refs_7_, bf16[4096,2048]{1,0:T(8,128)(2,1)S(1)} %copy-done.1, bf16[4096,256]{1,0:T(8,128)(2,1)S(1)} %copy-done.5, ...), custom_call_target="tpu_custom_call" | custom-call | flops 335544320 | bytes 10485760 | tf_op jit(solution)/shard_map/pallas_call | solution.py:385
  42.2 3.0 %collective-permute-start.1 = (f32[4,2,2560]{2,1,0:T(2,128)S(1)}, f32[4,2,2560]{2,1,0:T(2,128)S(1)}, u32[]{:S(2)}, u32[]{:S(2)}) collective-permute-start(f32[4,2,2560]{2,1,0:T(2,128)S(1)} %get-tuple-element.26), channel_id=1, source_target_pairs={{0,12},{4,8},{8,4},{12,0},{1,13},{5,9},{9,5},{13,1},{2,14},{6,10},... | collective-permute-start | bytes 245768 | tf_op jit(solution)/shard_map/ppermute | solution.py:271
  45.2 0.0 collective-permute-start.2
  45.2 1.5 %collective-permute-start.3 = (f32[4,2,2560]{2,1,0:T(2,128)S(1)}, f32[4,2,2560]{2,1,0:T(2,128)S(1)}, u32[]{:S(2)}, u32[]{:S(2)}) collective-permute-start(f32[4,2,2560]{2,1,0:T(2,128)S(1)} %get-tuple-element.28), channel_id=1, source_target_pairs={{0,4},{4,0},{8,12},{12,8},{1,5},{5,1},{9,13},{13,9},{2,6},{6,2},{1... | collective-permute-start | bytes 245768 | tf_op jit(solution)/shard_map/ppermute | solution.py:271
  46.6 0.1 shard_map.105.refs_4_.refs_6_
  46.7 2.7 %collective-permute-done.1.refs_0_ = f32[4,2,2560]{2,1,0:T(2,128)S(1)} collective-permute-done((f32[4,2,2560]{2,1,0:T(2,128)S(1)}, f32[4,2,2560]{2,1,0:T(2,128)S(1)}, u32[]{:S(2)}, u32[]{:S(2)}) %collective-permute-start.1) | collective-permute-done | bytes 81952 | tf_op jit(solution)/shard_map/ppermute | solution.py:271
  49.4 3.7 %collective-permute-done.2.refs_1_ = f32[4,2,2560]{2,1,0:T(2,128)S(1)} collective-permute-done((f32[4,2,2560]{2,1,0:T(2,128)S(1)}, f32[4,2,2560]{2,1,0:T(2,128)S(1)}, u32[]{:S(2)}, u32[]{:S(2)}) %collective-permute-start.2) | collective-permute-done | bytes 81952 | tf_op jit(solution)/shard_map/ppermute | solution.py:271
  53.1 0.0 collective-permute-done.3.refs_2_
  53.1 0.8 %shard_map.106.refs_0_ = bf16[2,2,2048]{2,1,0:T(2,128)(2,1)S(1)} custom-call(f32[1,128]{1,0:T(1,128)S(1)} %copy-done.10, f32[4,2,2560]{2,1,0:T(2,128)S(1)} %collective-permute-done.1.refs_0_, f32[4,2,2560]{2,1,0:T(2,128)S(1)} %collective-permute-done.2.refs_1_, f32[4,2,2560]{2,1,0:T(2,128)S(1)} %collective-permute-done.3.refs_2_, ...), custom_call_target="tpu_custom_call" | custom-call | flops 1 | bytes 1 | tf_op jit(solution)/shard_map/pallas_call | solution.py:403
  54.0 0.0 slice-start.1
  54.0 0.0 slice-start.2
  54.0 0.0 slice-start.3
  54.0 0.0 collective-permute-done.5.refs_5_
  54.0 0.0 collective-permute-done.6.refs_8_
  54.0 0.8 %shard_map.109.refs_1_ = bf16[2,2,2048]{2,1,0:T(2,128)(2,1)S(1)} custom-call(f32[1,128]{1,0:T(1,128)S(1)} %copy-done.10, f32[4,2,2560]{2,1,0:T(2,128)S(1)} %collective-permute-done.1.refs_0_, f32[4,2,2560]{2,1,0:T(2,128)S(1)} %collective-permute-done.2.refs_1_, f32[4,2,2560]{2,1,0:T(2,128)S(1)} %collective-permute-done.3.refs_2_, ...), custom_call_target="tpu_custom_call" | custom-call | flops 10000000000 | bytes 4194304 | tf_op jit(solution)/shard_map/pallas_call | solution.py:403
  54.9 0.1 collective-permute-start.7
  55.0 2.9 %collective-permute-start.8 = (bf16[4,2,2048]{2,1,0:T(2,128)(2,1)S(1)}, bf16[4,2,2048]{2,1,0:T(2,128)(2,1)S(1)}, u32[]{:S(2)}, u32[]{:S(2)}) collective-permute-start(bf16[4,2,2048]{2,1,0:T(2,128)(2,1)S(1)} %shard_map.110.refs_0_), channel_id=1, source_target_pairs={{0,4},{4,0},{8,12},{12,8},{1,5},{5,1},{9,13},{13,9},{2,6},{6,2},{1... | collective-permute-start | bytes 98312 | tf_op jit(solution)/shard_map/ppermute | solution.py:271
  57.9 1.5 %collective-permute-start.9 = (bf16[4,2,2048]{2,1,0:T(2,128)(2,1)S(1)}, bf16[4,2,2048]{2,1,0:T(2,128)(2,1)S(1)}, u32[]{:S(2)}, u32[]{:S(2)}) collective-permute-start(bf16[4,2,2048]{2,1,0:T(2,128)(2,1)S(1)} %shard_map.110.refs_0_), channel_id=1, source_target_pairs={{0,12},{4,8},{8,4},{12,0},{1,13},{5,9},{9,5},{13,1},{2,14},{6,10},... | collective-permute-start | bytes 98312 | tf_op jit(solution)/shard_map/ppermute | solution.py:271
  59.3 1.0 %collective-permute-done.7.refs_1_ = bf16[4,2,2048]{2,1,0:T(2,128)(2,1)S(1)} collective-permute-done((bf16[4,2,2048]{2,1,0:T(2,128)(2,1)S(1)}, bf16[4,2,2048]{2,1,0:T(2,128)(2,1)S(1)}, u32[]{:S(2)}, u32[]{:S(2)}) %collective-permute-start.7) | collective-permute-done | bytes 32800 | tf_op jit(solution)/shard_map/ppermute | solution.py:271
  60.3 0.0 collective-permute-done.8.refs_2_
  60.3 3.2 %collective-permute-done.9.refs_3_ = bf16[4,2,2048]{2,1,0:T(2,128)(2,1)S(1)} collective-permute-done((bf16[4,2,2048]{2,1,0:T(2,128)(2,1)S(1)}, bf16[4,2,2048]{2,1,0:T(2,128)(2,1)S(1)}, u32[]{:S(2)}, u32[]{:S(2)}) %collective-permute-start.9) | collective-permute-done | bytes 32800 | tf_op jit(solution)/shard_map/ppermute | solution.py:271
  63.6 0.0 slice-done.1
  63.6 1.5 %shard_map.113 = (f32[8,2,2048]{2,1,0:T(2,128)S(1)}, f32[8,2,2048]{2,1,0:T(2,128)S(1)}) custom-call(bf16[2048,4096]{1,0:T(8,128)(2,1)S(1)} %bitcast.3, bf16[4,2,2048]{2,1,0:T(2,128)(2,1)S(1)} %shard_map.110.refs_0_, bf16[4,2,2048]{2,1,0:T(2,128)(2,1)S(1)} %collective-permute-done.7.refs_1_, bf16[4,2,2048]{2,1,0:T(2,128)(2,1)S(1)} %collective-permute-done.8.refs_2_, ...), custom_call_target="tpu_custom_call" | custom-call | flops 268435456 | bytes 8388608 | tf_op jit(solution)/shard_map/pallas_call | solution.py:427
  65.2 0.1 collective-permute-start.12
  65.2 1.5 %shard_map.111 = (f32[8,2,2048]{2,1,0:T(2,128)S(1)}, f32[8,2,2048]{2,1,0:T(2,128)S(1)}) custom-call(bf16[2048,4096]{1,0:T(8,128)(2,1)S(1)} %bitcast.3, bf16[4,2,2048]{2,1,0:T(2,128)(2,1)S(1)} %shard_map.110.refs_0_, bf16[4,2,2048]{2,1,0:T(2,128)(2,1)S(1)} %collective-permute-done.7.refs_1_, bf16[4,2,2048]{2,1,0:T(2,128)(2,1)S(1)} %collective-permute-done.8.refs_2_, ...), custom_call_target="tpu_custom_call" | custom-call | flops 268435456 | bytes 8388608 | tf_op jit(solution)/shard_map/pallas_call | solution.py:427
  66.8 0.6 collective-permute-start.10
  67.4 0.0 collective-permute-done.12.b_ref
  67.4 1.2 %collective-permute-start.13 = (f32[4,2,2048]{2,1,0:T(2,128)S(1)}, f32[4,2,2048]{2,1,0:T(2,128)S(1)}, u32[]{:S(2)}, u32[]{:S(2)}) collective-permute-start(f32[4,2,2048]{2,1,0:T(2,128)S(1)} %get-tuple-element.42), channel_id=1, source_target_pairs={{0,2},{1,3},{2,0},{3,1},{4,6},{5,7},{6,4},{7,5},{8,10},{9,11},{10,... | collective-permute-start | bytes 196616 | tf_op jit(solution)/shard_map/ppermute | solution.py:275
  68.6 0.0 collective-permute-done.10.b_ref
  68.6 1.0 %collective-permute-start.11 = (f32[4,2,2048]{2,1,0:T(2,128)S(1)}, f32[4,2,2048]{2,1,0:T(2,128)S(1)}, u32[]{:S(2)}, u32[]{:S(2)}) collective-permute-start(f32[4,2,2048]{2,1,0:T(2,128)S(1)} %get-tuple-element.38), channel_id=1, source_target_pairs={{0,2},{1,3},{2,0},{3,1},{4,6},{5,7},{6,4},{7,5},{8,10},{9,11},{10,... | collective-permute-start | bytes 196616 | tf_op jit(solution)/shard_map/ppermute | solution.py:275
  69.6 2.6 %collective-permute-done.13.refs_3_ = f32[4,2,2048]{2,1,0:T(2,128)S(1)} collective-permute-done((f32[4,2,2048]{2,1,0:T(2,128)S(1)}, f32[4,2,2048]{2,1,0:T(2,128)S(1)}, u32[]{:S(2)}, u32[]{:S(2)}) %collective-permute-start.13) | collective-permute-done | bytes 65568 | tf_op jit(solution)/shard_map/ppermute | solution.py:275
  72.1 1.0 %collective-permute-done.11.refs_1_ = f32[4,2,2048]{2,1,0:T(2,128)S(1)} collective-permute-done((f32[4,2,2048]{2,1,0:T(2,128)S(1)}, f32[4,2,2048]{2,1,0:T(2,128)S(1)}, u32[]{:S(2)}, u32[]{:S(2)}) %collective-permute-start.11) | collective-permute-done | bytes 65568 | tf_op jit(solution)/shard_map/ppermute | solution.py:275
  73.1 0.1 shard_map.115
  73.2 1.5 %collective-permute-start.14 = (bf16[2,4096]{1,0:T(2,128)(2,1)S(1)}, bf16[2,4096]{1,0:T(2,128)(2,1)S(1)}, u32[]{:S(2)}, u32[]{:S(2)}) collective-permute-start(bf16[2,4096]{1,0:T(2,128)(2,1)S(1)} %get-tuple-element.43), channel_id=1, source_target_pairs={{0,12},{4,8},{8,4},{12,0},{1,13},{5,9},{9,5},{13,1},{2,14},{6,10},... | collective-permute-start | bytes 49160 | tf_op jit(solution)/shard_map/ppermute | solution.py:271
  74.7 0.0 collective-permute-start.15
  74.7 2.9 %collective-permute-start.16 = (bf16[2,4096]{1,0:T(2,128)(2,1)S(1)}, bf16[2,4096]{1,0:T(2,128)(2,1)S(1)}, u32[]{:S(2)}, u32[]{:S(2)}) collective-permute-start(bf16[2,4096]{1,0:T(2,128)(2,1)S(1)} %get-tuple-element.45), channel_id=1, source_target_pairs={{0,4},{4,0},{8,12},{12,8},{1,5},{5,1},{9,13},{13,9},{2,6},{6,2},{1... | collective-permute-start | bytes 49160 | tf_op jit(solution)/shard_map/ppermute | solution.py:271
  77.6 1.3 %collective-permute-done.14.refs_0_ = bf16[2,4096]{1,0:T(2,128)(2,1)S(1)} collective-permute-done((bf16[2,4096]{1,0:T(2,128)(2,1)S(1)}, bf16[2,4096]{1,0:T(2,128)(2,1)S(1)}, u32[]{:S(2)}, u32[]{:S(2)}) %collective-permute-start.14) | collective-permute-done | bytes 16416 | tf_op jit(solution)/shard_map/ppermute | solution.py:271
  78.9 0.6 collective-permute-done.15.refs_1_
  79.5 0.1 collective-permute-done.16.refs_2_
  79.5 0.6 shard_map.116
  (22 shorter events, 0.1 us)
Async XLA Ops:
  0.0 1.2 %copy-start.8 = (f32[16384]{0:T(1024)S(1)}, f32[16384]{0:T(1024)}, u32[]{:S(2)}) copy-start(f32[16384]{0:T(1024)} %param.11) | copy-start | bytes 196612
  0.0 9.4 %copy-start.9 = (s32[2]{0:T(128)S(1)}, s32[2]{0:T(128)}, u32[]{:S(2)}) copy-start(s32[2]{0:T(128)} %param.18) | copy-start | bytes 28
  0.0 9.4 %copy-start.2 = (bf16[2,256,1024]{2,1,0:T(8,128)(2,1)S(1)}, bf16[2,256,1024]{2,1,0:T(8,128)(2,1)}, u32[]{:S(2)}) copy-start(bf16[2,256,1024]{2,1,0:T(8,128)(2,1)} %keys_ref.5) | copy-start | bytes 3145732
  0.0 9.4 %copy-start.3 = (bf16[2,256,1024]{2,1,0:T(8,128)(2,1)S(1)}, bf16[2,256,1024]{2,1,0:T(8,128)(2,1)}, u32[]{:S(2)}) copy-start(bf16[2,256,1024]{2,1,0:T(8,128)(2,1)} %values_ref.5) | copy-start | bytes 3145732
  0.0 1.0 %copy-start.11 = (bf16[2,16384]{1,0:T(2,128)(2,1)S(1)}, bf16[2,16384]{1,0:T(2,128)(2,1)}, u32[]{:S(2)}) copy-start(bf16[2,16384]{1,0:T(2,128)(2,1)} %tokens_ref.1) | copy-start | bytes 196612
  2.0 15.3 %all-to-all-start = ((bf16[16,2,2048]{2,1,0:T(2,128)(2,1)}), bf16[16,2,2048]{2,1,0:T(2,128)(2,1)S(1)}, u32[]{:S(2)}, u32[]{:S(2)}) async-start(bf16[16,2,2048]{2,1,0:T(2,128)(2,1)} %shard_map.101._), calls=%async_computation | async-start | bytes 262144 | tf_op jit(solution)/shard_map/all_to_all | solution.py:267
  11.2 12.3 %collective-permute-start.4 = (bf16[768,256]{1,0:T(8,128)(2,1)}, bf16[768,256]{1,0:T(8,128)(2,1)S(1)}, u32[]{:S(2)}, u32[]{:S(2)}) collective-permute-start(bf16[768,256]{1,0:T(8,128)(2,1)} %get-tuple-element.30), channel_id=1, source_target_pairs={{0,2},{1,3},{2,0},{3,1},{4,6},{5,7},{6,4},{7,5},{8,10},{9,11},{10,... | collective-permute-start | bytes 1179656 | tf_op jit(solution)/shard_map/ppermute | solution.py:275
  17.3 18.5 %copy-start.5 = (bf16[4096,256]{1,0:T(8,128)(2,1)S(1)}, bf16[4096,256]{1,0:T(8,128)(2,1)}, u32[]{:S(2)}) copy-start(bf16[4096,256]{1,0:T(8,128)(2,1)} %key_ref.3) | copy-start | bytes 6291460
  17.4 18.4 %collective-permute-start = (bf16[1296,256]{1,0:T(8,128)(2,1)S(1)}, bf16[1296,256]{1,0:T(8,128)(2,1)S(1)}, u32[]{:S(2)}, u32[]{:S(2)}) collective-permute-start(bf16[1296,256]{1,0:T(8,128)(2,1)S(1)} %shard_map.102), channel_id=1, source_target_pairs={{0,1},{1,0},{2,3},{3,2},{4,5},{5,4},{6,7},{7,6},{8,9},{9,8},{10,11... | collective-permute-start | bytes 1990664 | tf_op jit(solution)/shard_map/ppermute | solution.py:275
  23.5 30.5 %collective-permute-start.6 = (bf16[1040,256]{1,0:T(8,128)(2,1)S(1)}, bf16[1040,256]{1,0:T(8,128)(2,1)S(1)}, u32[]{:S(2)}, u32[]{:S(2)}) collective-permute-start(bf16[1040,256]{1,0:T(8,128)(2,1)S(1)} %get-tuple-element.34), channel_id=1, source_target_pairs={{0,3},{1,2},{2,1},{3,0},{4,7},{5,6},{6,5},{7,4},{8,11},{9,10},{10,... | collective-permute-start | bytes 1597448 | tf_op jit(solution)/shard_map/ppermute | solution.py:275
  24.0 30.0 %collective-permute-start.5 = (bf16[272,256]{1,0:T(8,128)(2,1)S(1)}, bf16[272,256]{1,0:T(8,128)(2,1)S(1)}, u32[]{:S(2)}, u32[]{:S(2)}) collective-permute-start(bf16[272,256]{1,0:T(8,128)(2,1)S(1)} %get-tuple-element.33), channel_id=1, source_target_pairs={{0,2},{1,3},{2,0},{3,1},{4,6},{5,7},{6,4},{7,5},{8,10},{9,11},{10,... | collective-permute-start | bytes 417800 | tf_op jit(solution)/shard_map/ppermute | solution.py:275
  24.9 5.8 %copy-start = (bf16[4096,2048]{1,0:T(8,128)(2,1)S(1)}, bf16[4096,2048]{1,0:T(8,128)(2,1)}, u32[]{:S(2)}) copy-start(bf16[4096,2048]{1,0:T(8,128)(2,1)} %query_ref.3) | copy-start | bytes 50331652
  30.7 1.6 %copy-start.4 = (bf16[4096,256]{1,0:T(8,128)(2,1)S(1)}, bf16[4096,256]{1,0:T(8,128)(2,1)}, u32[]{:S(2)}) copy-start(bf16[4096,256]{1,0:T(8,128)(2,1)} %key_ref.3) | copy-start | bytes 6291460
  32.3 1.6 %copy-start.6 = (bf16[4096,256]{1,0:T(8,128)(2,1)S(1)}, bf16[4096,256]{1,0:T(8,128)(2,1)}, u32[]{:S(2)}) copy-start(bf16[4096,256]{1,0:T(8,128)(2,1)} %value_ref.3) | copy-start | bytes 6291460
  33.9 5.8 %copy-start.1 = (bf16[4096,2048]{1,0:T(8,128)(2,1)S(1)}, bf16[4096,2048]{1,0:T(8,128)(2,1)}, u32[]{:S(2)}) copy-start(bf16[4096,2048]{1,0:T(8,128)(2,1)} %query_ref.3) | copy-start | bytes 50331652
  33.9 6.4 %copy-start.7 = (bf16[4096,256]{1,0:T(8,128)(2,1)S(1)}, bf16[4096,256]{1,0:T(8,128)(2,1)}, u32[]{:S(2)}) copy-start(bf16[4096,256]{1,0:T(8,128)(2,1)} %value_ref.3) | copy-start | bytes 6291460
  35.8 17.4 %copy-start.10 = (f32[1,128]{1,0:T(1,128)S(1)}, f32[1,128]{1,0:T(1,128)}, u32[]{:S(2)}) copy-start(f32[1,128]{1,0:T(1,128)} %constant.2.clone.frequency_ref) | copy-start | bytes 1540
  42.2 7.2 %collective-permute-start.1 = (f32[4,2,2560]{2,1,0:T(2,128)S(1)}, f32[4,2,2560]{2,1,0:T(2,128)S(1)}, u32[]{:S(2)}, u32[]{:S(2)}) collective-permute-start(f32[4,2,2560]{2,1,0:T(2,128)S(1)} %get-tuple-element.26), channel_id=1, source_target_pairs={{0,12},{4,8},{8,4},{12,0},{1,13},{5,9},{9,5},{13,1},{2,14},{6,10},... | collective-permute-start | bytes 245768 | tf_op jit(solution)/shard_map/ppermute | solution.py:271
  45.2 8.0 %collective-permute-start.2 = (f32[4,2,2560]{2,1,0:T(2,128)S(1)}, f32[4,2,2560]{2,1,0:T(2,128)S(1)}, u32[]{:S(2)}, u32[]{:S(2)}) collective-permute-start(f32[4,2,2560]{2,1,0:T(2,128)S(1)} %get-tuple-element.27), channel_id=1, source_target_pairs={{0,8},{4,12},{8,0},{12,4},{1,9},{5,13},{9,1},{13,5},{2,10},{6,14},... | collective-permute-start | bytes 245768 | tf_op jit(solution)/shard_map/ppermute | solution.py:271
  45.2 8.0 %collective-permute-start.3 = (f32[4,2,2560]{2,1,0:T(2,128)S(1)}, f32[4,2,2560]{2,1,0:T(2,128)S(1)}, u32[]{:S(2)}, u32[]{:S(2)}) collective-permute-start(f32[4,2,2560]{2,1,0:T(2,128)S(1)} %get-tuple-element.28), channel_id=1, source_target_pairs={{0,4},{4,0},{8,12},{12,8},{1,5},{5,1},{9,13},{13,9},{2,6},{6,2},{1... | collective-permute-start | bytes 245768 | tf_op jit(solution)/shard_map/ppermute | solution.py:271
  53.1 10.4 %slice-start = ((s8[16777216]{0:T(1024)(128)(4,1)}), s8[4194304]{0:T(1024)(128)(4,1)S(1)}, s32[]{:S(2)}) async-start(s8[16777216]{0:T(1024)(128)(4,1)} %bitcast.2), calls=%async_computation.1 | async-start | bytes 8388608
  54.0 9.6 %slice-start.1 = ((s8[16777216]{0:T(1024)(128)(4,1)}), s8[4194304]{0:T(1024)(128)(4,1)S(1)}, s32[]{:S(2)}) async-start(s8[16777216]{0:T(1024)(128)(4,1)} %bitcast.2), calls=%async_computation.2 | async-start | bytes 8388608
  54.0 9.6 %slice-start.2 = ((s8[16777216]{0:T(1024)(128)(4,1)}), s8[4194304]{0:T(1024)(128)(4,1)S(1)}, s32[]{:S(2)}) async-start(s8[16777216]{0:T(1024)(128)(4,1)} %bitcast.2), calls=%async_computation.3 | async-start | bytes 8388608
  54.0 9.6 %slice-start.3 = ((s8[16777216]{0:T(1024)(128)(4,1)}), s8[4194304]{0:T(1024)(128)(4,1)S(1)}, s32[]{:S(2)}) async-start(s8[16777216]{0:T(1024)(128)(4,1)} %bitcast.2), calls=%async_computation.4 | async-start | bytes 8388608
  54.9 5.4 %collective-permute-start.7 = (bf16[4,2,2048]{2,1,0:T(2,128)(2,1)S(1)}, bf16[4,2,2048]{2,1,0:T(2,128)(2,1)S(1)}, u32[]{:S(2)}, u32[]{:S(2)}) collective-permute-start(bf16[4,2,2048]{2,1,0:T(2,128)(2,1)S(1)} %shard_map.110.refs_0_), channel_id=1, source_target_pairs={{0,8},{4,12},{8,0},{12,4},{1,9},{5,13},{9,1},{13,5},{2,10},{6,14},... | collective-permute-start | bytes 98312 | tf_op jit(solution)/shard_map/ppermute | solution.py:271
  55.0 5.4 %collective-permute-start.8 = (bf16[4,2,2048]{2,1,0:T(2,128)(2,1)S(1)}, bf16[4,2,2048]{2,1,0:T(2,128)(2,1)S(1)}, u32[]{:S(2)}, u32[]{:S(2)}) collective-permute-start(bf16[4,2,2048]{2,1,0:T(2,128)(2,1)S(1)} %shard_map.110.refs_0_), channel_id=1, source_target_pairs={{0,4},{4,0},{8,12},{12,8},{1,5},{5,1},{9,13},{13,9},{2,6},{6,2},{1... | collective-permute-start | bytes 98312 | tf_op jit(solution)/shard_map/ppermute | solution.py:271
  57.9 5.7 %collective-permute-start.9 = (bf16[4,2,2048]{2,1,0:T(2,128)(2,1)S(1)}, bf16[4,2,2048]{2,1,0:T(2,128)(2,1)S(1)}, u32[]{:S(2)}, u32[]{:S(2)}) collective-permute-start(bf16[4,2,2048]{2,1,0:T(2,128)(2,1)S(1)} %shard_map.110.refs_0_), channel_id=1, source_target_pairs={{0,12},{4,8},{8,4},{12,0},{1,13},{5,9},{9,5},{13,1},{2,14},{6,10},... | collective-permute-start | bytes 98312 | tf_op jit(solution)/shard_map/ppermute | solution.py:271
  65.2 2.2 %collective-permute-start.12 = (f32[8,2,2048]{2,1,0:T(2,128)S(1)}, f32[8,2,2048]{2,1,0:T(2,128)S(1)}, u32[]{:S(2)}, u32[]{:S(2)}) collective-permute-start(f32[8,2,2048]{2,1,0:T(2,128)S(1)} %get-tuple-element.40), channel_id=1, source_target_pairs={{0,1},{1,0},{2,3},{3,2},{4,5},{5,4},{6,7},{7,6},{8,9},{9,8},{10,11... | collective-permute-start | bytes 393224 | tf_op jit(solution)/shard_map/ppermute | solution.py:275
  66.8 1.8 %collective-permute-start.10 = (f32[8,2,2048]{2,1,0:T(2,128)S(1)}, f32[8,2,2048]{2,1,0:T(2,128)S(1)}, u32[]{:S(2)}, u32[]{:S(2)}) collective-permute-start(f32[8,2,2048]{2,1,0:T(2,128)S(1)} %get-tuple-element.36), channel_id=1, source_target_pairs={{0,1},{1,0},{2,3},{3,2},{4,5},{5,4},{6,7},{7,6},{8,9},{9,8},{10,11... | collective-permute-start | bytes 393224 | tf_op jit(solution)/shard_map/ppermute | solution.py:275
  67.4 4.7 %collective-permute-start.13 = (f32[4,2,2048]{2,1,0:T(2,128)S(1)}, f32[4,2,2048]{2,1,0:T(2,128)S(1)}, u32[]{:S(2)}, u32[]{:S(2)}) collective-permute-start(f32[4,2,2048]{2,1,0:T(2,128)S(1)} %get-tuple-element.42), channel_id=1, source_target_pairs={{0,2},{1,3},{2,0},{3,1},{4,6},{5,7},{6,4},{7,5},{8,10},{9,11},{10,... | collective-permute-start | bytes 196616 | tf_op jit(solution)/shard_map/ppermute | solution.py:275
  68.6 4.5 %collective-permute-start.11 = (f32[4,2,2048]{2,1,0:T(2,128)S(1)}, f32[4,2,2048]{2,1,0:T(2,128)S(1)}, u32[]{:S(2)}, u32[]{:S(2)}) collective-permute-start(f32[4,2,2048]{2,1,0:T(2,128)S(1)} %get-tuple-element.38), channel_id=1, source_target_pairs={{0,2},{1,3},{2,0},{3,1},{4,6},{5,7},{6,4},{7,5},{8,10},{9,11},{10,... | collective-permute-start | bytes 196616 | tf_op jit(solution)/shard_map/ppermute | solution.py:275
  73.2 5.7 %collective-permute-start.14 = (bf16[2,4096]{1,0:T(2,128)(2,1)S(1)}, bf16[2,4096]{1,0:T(2,128)(2,1)S(1)}, u32[]{:S(2)}, u32[]{:S(2)}) collective-permute-start(bf16[2,4096]{1,0:T(2,128)(2,1)S(1)} %get-tuple-element.43), channel_id=1, source_target_pairs={{0,12},{4,8},{8,4},{12,0},{1,13},{5,9},{9,5},{13,1},{2,14},{6,10},... | collective-permute-start | bytes 49160 | tf_op jit(solution)/shard_map/ppermute | solution.py:271
  74.7 4.7 %collective-permute-start.15 = (bf16[2,4096]{1,0:T(2,128)(2,1)S(1)}, bf16[2,4096]{1,0:T(2,128)(2,1)S(1)}, u32[]{:S(2)}, u32[]{:S(2)}) collective-permute-start(bf16[2,4096]{1,0:T(2,128)(2,1)S(1)} %get-tuple-element.44), channel_id=1, source_target_pairs={{0,8},{4,12},{8,0},{12,4},{1,9},{5,13},{9,1},{13,5},{2,10},{6,14},... | collective-permute-start | bytes 49160 | tf_op jit(solution)/shard_map/ppermute | solution.py:271
  74.7 4.8 %collective-permute-start.16 = (bf16[2,4096]{1,0:T(2,128)(2,1)S(1)}, bf16[2,4096]{1,0:T(2,128)(2,1)S(1)}, u32[]{:S(2)}, u32[]{:S(2)}) collective-permute-start(bf16[2,4096]{1,0:T(2,128)(2,1)S(1)} %get-tuple-element.45), channel_id=1, source_target_pairs={{0,4},{4,0},{8,12},{12,8},{1,5},{5,1},{9,13},{13,9},{2,6},{6,2},{1... | collective-permute-start | bytes 49160 | tf_op jit(solution)/shard_map/ppermute | solution.py:271

commit v20 on v19

--- a/solution.py
+++ b/solution.py
@@ -22,7 +22,7 @@
     scaled_ref[...] = tokens * lax.rsqrt(mean_square + 1e-05)
 
 
-def gain_kernel(wide, plane, scaled_ref, gain_ref, blocks_ref):
+def gain_kernel(wide, plane, scaled_ref, gain_ref, _, blocks_ref):
     normed = (scaled_ref[...] * gain_ref[...]).astype(jnp.bfloat16)
     half = normed.shape[1] // wide // 2
     for i in range(wide):
@@ -315,13 +315,6 @@
         compiler_params=params(8),
         cost_estimate=cost(40 * 10**9, MIB),
     )(tokens)
-    normed = pl.pallas_call(
-        functools.partial(gain_kernel, wide, plane),
-        out_shape=jax.ShapeDtypeStruct((owners, rows, half), jnp.bfloat16),
-        in_specs=[IN_VMEM, IN_VMEM],
-        out_specs=IN_VMEM,
-        compiler_params=params(8),
-    )(scaled, norm_gain.reshape(1, -1))
     slots = cache_keys.shape[1]
     even = plane // 2 - 1
     early = rows // 2
@@ -345,9 +338,16 @@
     plan = [(l, every, every[:early], False) for l in range(2, plane, 2)]
     plan += [(l, (), every[early:], True) for l in range(2, plane, 2)]
     plan += [(l, every, every, True) for l in range(3, plane, 2)]
-    blocks = cut(plan, normed)
+    blocks = cut(plan, scaled)
     firsts, rest = blocks[:even], blocks[even:]
     firsts = [swap_plane(firsts[s], 2 * s + 2) for s in range(even)]
+    normed = pl.pallas_call(
+        functools.partial(gain_kernel, wide, plane),
+        out_shape=jax.ShapeDtypeStruct((owners, rows, half), jnp.bfloat16),
+        in_specs=[IN_VMEM] * 3,
+        out_specs=IN_VMEM,
+        compiler_params=params(8),
+    )(scaled, norm_gain.reshape(1, -1), rest[0])
     own_half = swap_blocks(normed, ROW_AXES)
     pieces = half // kv_cols
     mate = pl.pallas_call(

time: 80.5 us -> 80.7 us (level)
  Pallas kernels: 12.3 us -> 10.6 us
  local copies, waits for them, and re-layouts: 14.4 us -> 15.5 us
  waiting for transfers between devices: 26.3 us -> 27.2 us
    all_to_all x1, waiting for transfers between devices: 4.16 us -> 6.02 us  [swap_blocks(): return lax.all_to_all(blocks, axes, split_axis=0, concat_axis=0, tiled=True)]
    pallas_call x2, Pallas kernels: 1.91 us -> 0.22 us  [cut(): pl.pallas_call(functools.partial(cut_kernel, plan), out_shape=[jax.ShapeD...]
    ppermute x8, waiting for transfers between devices: 9.6 us -> 8.43 us  [swap_plane(): lax.ppermute(value, PLANE, [(i, i ^ step) for i in range(lax.axis_size(PL...]
    unnamed x32 -> x34, local copies, waits for them, and re-layouts: 14.4 us -> 15.5 us
  transfers between devices with their start and end apart: 18 -> 18, of which waited for: 11 -> 10; matrix products, arithmetic and copies ran while one was open for 0% -> 0% of each run, Pallas kernels for 10% -> 8%
where the time goes in v20:
time: 80.7 us; the launch traced here: 80.3 us
  waiting for transfers between devices  27.2 us (34%)
  starting transfers between devices  26.8 us (33%)
  local copies, waits for them, and re-layouts  15.5 us (19%)
  Pallas kernels  10.6 us (13%)
    unnamed x34, local copies, waits for them, and re-layouts  15.5 us
    ppermute x9, starting transfers between devices, swap_pairs(): lax.ppermute(value, axis, [(i, i ^ step) for i in range(lax.axis_size(axi...  13.4 us
    ppermute x9, waiting for transfers between devices, swap_pairs(): lax.ppermute(value, axis, [(i, i ^ step) for i in range(lax.axis_size(axi...  12.8 us
    ppermute x8, waiting for transfers between devices, swap_plane(): lax.ppermute(value, PLANE, [(i, i ^ step) for i in range(lax.axis_size(PL...  8.43 us
    all_to_all x1, starting transfers between devices, swap_blocks(): return lax.all_to_all(blocks, axes, split_axis=0, concat_axis=0, tiled=True)  7.36 us
    ppermute x8, starting transfers between devices, swap_plane(): lax.ppermute(value, PLANE, [(i, i ^ step) for i in range(lax.axis_size(PL...  6.1 us
    all_to_all x1, waiting for transfers between devices, swap_blocks(): return lax.all_to_all(blocks, axes, split_axis=0, concat_axis=0, tiled=True)  6.02 us
    pallas_call x2, Pallas kernels, shards(): pl.pallas_call(functools.partial(output_kernel, p * part_cols, part_cols,...  3.11 us
  transfers between devices with their start and end apart: 18, of which 10 were waited for; matrix products, arithmetic and copies ran while one was open for 0% of the time, Pallas kernels for 8%

profile of v20, /device:TPU:0, one launch (start us, length us, event | category | flops | bytes accessed | tf_op | source)
XLA Modules:
  0.0 80.3 jit_solution(5427714004855813670)
XLA Ops:
  0.0 1.0 %copy-done.12 = bf16[2,16384]{1,0:T(2,128)(2,1)S(1)} copy-done((bf16[2,16384]{1,0:T(2,128)(2,1)S(1)}, bf16[2,16384]{1,0:T(2,128)(2,1)}, u32[]{:S(2)}) %copy-start.12) | copy-done | bytes 65560
  1.0 0.2 shard_map.100._.scaled_ref
  1.2 0.0 copy-done.9
  1.2 0.0 copy-done.2
  1.3 0.3 copy-done.3
  1.6 0.1 shard_map.101
  1.7 0.7 copy-done.11
  2.5 0.7 shard_map.102
  3.2 7.4 %all-to-all-start = ((bf16[16,2,2048]{2,1,0:T(2,128)(2,1)}), bf16[16,2,2048]{2,1,0:T(2,128)(2,1)S(1)}, u32[]{:S(2)}, u32[]{:S(2)}) async-start(bf16[16,2,2048]{2,1,0:T(2,128)(2,1)} %shard_map.102), calls=%async_computation | async-start | bytes 262144 | tf_op jit(solution)/shard_map/all_to_all | solution.py:267
  10.6 1.9 %collective-permute-start.4 = (bf16[768,256]{1,0:T(8,128)(2,1)}, bf16[768,256]{1,0:T(8,128)(2,1)S(1)}, u32[]{:S(2)}, u32[]{:S(2)}) collective-permute-start(bf16[768,256]{1,0:T(8,128)(2,1)} %copy-done.11), channel_id=1, source_target_pairs={{0,2},{1,3},{2,0},{3,1},{4,6},{5,7},{6,4},{7,5},{8,10},{9,11},{10,... | collective-permute-start | bytes 1179656 | tf_op jit(solution)/shard_map/ppermute | solution.py:275
  12.5 6.0 %all-to-all-done.rows_ref._.refs_2_ = bf16[16,2,2048]{2,1,0:T(2,128)(2,1)S(1)} async-done(((bf16[16,2,2048]{2,1,0:T(2,128)(2,1)}), bf16[16,2,2048]{2,1,0:T(2,128)(2,1)S(1)}, u32[]{:S(2)}, u32[]{:S(2)}) %all-to-all-start) | async-done | bytes 131104 | tf_op jit(solution)/shard_map/all_to_all | solution.py:267
  18.5 0.1 shard_map.103
  18.6 0.1 collective-permute-start
  18.7 4.8 %collective-permute-done.4.refs_3_.refs_4_ = bf16[768,256]{1,0:T(8,128)(2,1)S(1)} collective-permute-done((bf16[768,256]{1,0:T(8,128)(2,1)}, bf16[768,256]{1,0:T(8,128)(2,1)S(1)}, u32[]{:S(2)}, u32[]{:S(2)}) %collective-permute-start.4) | collective-permute-done | bytes 393248 | tf_op jit(solution)/shard_map/ppermute | solution.py:275
  23.5 0.5 collective-permute-start.6
  24.1 0.8 collective-permute-start.5
  24.9 5.8 %copy-done = bf16[4096,2048]{1,0:T(8,128)(2,1)S(1)} copy-done((bf16[4096,2048]{1,0:T(8,128)(2,1)S(1)}, bf16[4096,2048]{1,0:T(8,128)(2,1)}, u32[]{:S(2)}) %copy-start) | copy-done | bytes 16777240
  30.6 1.6 %copy-done.4 = bf16[4096,256]{1,0:T(8,128)(2,1)S(1)} copy-done((bf16[4096,256]{1,0:T(8,128)(2,1)S(1)}, bf16[4096,256]{1,0:T(8,128)(2,1)}, u32[]{:S(2)}) %copy-start.4) | copy-done | bytes 2097176
  32.2 1.6 %copy-done.6 = bf16[4096,256]{1,0:T(8,128)(2,1)S(1)} copy-done((bf16[4096,256]{1,0:T(8,128)(2,1)S(1)}, bf16[4096,256]{1,0:T(8,128)(2,1)}, u32[]{:S(2)}) %copy-start.6) | copy-done | bytes 2097176
  33.8 1.9 %shard_map.104.refs_0_ = f32[32,2560]{1,0:T(8,128)S(1)} custom-call(bf16[16,2,2048]{2,1,0:T(2,128)(2,1)S(1)} %all-to-all-done.rows_ref._.refs_2_, bf16[4096,2048]{1,0:T(8,128)(2,1)S(1)} %copy-done, bf16[4096,256]{1,0:T(8,128)(2,1)S(1)} %copy-done.4, bf16[4096,256]{1,0:T(8,128)(2,1)S(1)} %copy-done.6), custom_call_target="tpu_custom_call" | custom-call | flops 335544320 | bytes 10485760 | tf_op jit(solution)/shard_map/pallas_call | solution.py:377
  35.7 0.0 collective-permute-done.rows_ref.refs_5_.refs_7_
  35.7 3.8 %copy-done.1 = bf16[4096,2048]{1,0:T(8,128)(2,1)S(1)} copy-done((bf16[4096,2048]{1,0:T(8,128)(2,1)S(1)}, bf16[4096,2048]{1,0:T(8,128)(2,1)}, u32[]{:S(2)}) %copy-start.1) | copy-done | bytes 16777240
  39.6 0.6 copy-done.7
  40.2 2.0 %shard_map.105 = (f32[4,2,2560]{2,1,0:T(2,128)S(1)}, f32[4,2,2560]{2,1,0:T(2,128)S(1)}, f32[4,2,2560]{2,1,0:T(2,128)S(1)}, f32[4,2,2560]{2,1,0:T(2,128)S(1)}) custom-call(bf16[1296,256]{1,0:T(8,128)(2,1)S(1)} %collective-permute-done.rows_ref.refs_5_.refs_7_, bf16[4096,2048]{1,0:T(8,128)(2,1)S(1)} %copy-done.1, bf16[4096,256]{1,0:T(8,128)(2,1)S(1)} %copy-done.5, ...), custom_call_target="tpu_custom_call" | custom-call | flops 335544320 | bytes 10485760 | tf_op jit(solution)/shard_map/pallas_call | solution.py:385
  42.1 3.5 %collective-permute-start.1 = (f32[4,2,2560]{2,1,0:T(2,128)S(1)}, f32[4,2,2560]{2,1,0:T(2,128)S(1)}, u32[]{:S(2)}, u32[]{:S(2)}) collective-permute-start(f32[4,2,2560]{2,1,0:T(2,128)S(1)} %get-tuple-element.27), channel_id=1, source_target_pairs={{0,12},{4,8},{8,4},{12,0},{1,13},{5,9},{9,5},{13,1},{2,14},{6,10},... | collective-permute-start | bytes 245768 | tf_op jit(solution)/shard_map/ppermute | solution.py:271
  45.6 0.0 collective-permute-start.2
  45.6 1.0 %collective-permute-start.3 = (f32[4,2,2560]{2,1,0:T(2,128)S(1)}, f32[4,2,2560]{2,1,0:T(2,128)S(1)}, u32[]{:S(2)}, u32[]{:S(2)}) collective-permute-start(f32[4,2,2560]{2,1,0:T(2,128)S(1)} %get-tuple-element.29), channel_id=1, source_target_pairs={{0,4},{4,0},{8,12},{12,8},{1,5},{5,1},{9,13},{13,9},{2,6},{6,2},{1... | collective-permute-start | bytes 245768 | tf_op jit(solution)/shard_map/ppermute | solution.py:271
  46.6 0.1 shard_map.106.refs_4_.refs_6_
  46.7 2.7 %collective-permute-done.1.refs_0_ = f32[4,2,2560]{2,1,0:T(2,128)S(1)} collective-permute-done((f32[4,2,2560]{2,1,0:T(2,128)S(1)}, f32[4,2,2560]{2,1,0:T(2,128)S(1)}, u32[]{:S(2)}, u32[]{:S(2)}) %collective-permute-start.1) | collective-permute-done | bytes 81952 | tf_op jit(solution)/shard_map/ppermute | solution.py:271
  49.3 4.0 %collective-permute-done.2.refs_1_ = f32[4,2,2560]{2,1,0:T(2,128)S(1)} collective-permute-done((f32[4,2,2560]{2,1,0:T(2,128)S(1)}, f32[4,2,2560]{2,1,0:T(2,128)S(1)}, u32[]{:S(2)}, u32[]{:S(2)}) %collective-permute-start.2) | collective-permute-done | bytes 81952 | tf_op jit(solution)/shard_map/ppermute | solution.py:271
  53.4 0.0 collective-permute-done.3.refs_2_
  53.4 0.0 copy-done.10
  53.4 0.8 %shard_map.107.refs_0_ = bf16[2,2,2048]{2,1,0:T(2,128)(2,1)S(1)} custom-call(f32[1,128]{1,0:T(1,128)S(1)} %copy-done.10, f32[4,2,2560]{2,1,0:T(2,128)S(1)} %collective-permute-done.1.refs_0_, f32[4,2,2560]{2,1,0:T(2,128)S(1)} %collective-permute-done.2.refs_1_, f32[4,2,2560]{2,1,0:T(2,128)S(1)} %collective-permute-done.3.refs_2_, ...), custom_call_target="tpu_custom_call" | custom-call | flops 1 | bytes 1 | tf_op jit(solution)/shard_map/pallas_call | solution.py:403
  54.2 0.0 slice-start.1
  54.2 0.0 slice-start.2
  54.2 0.0 slice-start.3
  54.3 0.0 collective-permute-done.5.refs_5_
  54.3 0.0 collective-permute-done.6.refs_8_
  54.3 0.8 %shard_map.109.refs_1_ = bf16[2,2,2048]{2,1,0:T(2,128)(2,1)S(1)} custom-call(f32[1,128]{1,0:T(1,128)S(1)} %copy-done.10, f32[4,2,2560]{2,1,0:T(2,128)S(1)} %collective-permute-done.1.refs_0_, f32[4,2,2560]{2,1,0:T(2,128)S(1)} %collective-permute-done.2.refs_1_, f32[4,2,2560]{2,1,0:T(2,128)S(1)} %collective-permute-done.3.refs_2_, ...), custom_call_target="tpu_custom_call" | custom-call | flops 10000000000 | bytes 4194304 | tf_op jit(solution)/shard_map/pallas_call | solution.py:403
  55.1 0.3 collective-permute-start.7
  55.4 2.6 %collective-permute-start.8 = (bf16[4,2,2048]{2,1,0:T(2,128)(2,1)S(1)}, bf16[4,2,2048]{2,1,0:T(2,128)(2,1)S(1)}, u32[]{:S(2)}, u32[]{:S(2)}) collective-permute-start(bf16[4,2,2048]{2,1,0:T(2,128)(2,1)S(1)} %shard_map.110.refs_0_), channel_id=1, source_target_pairs={{0,4},{4,0},{8,12},{12,8},{1,5},{5,1},{9,13},{13,9},{2,6},{6,2},{1... | collective-permute-start | bytes 98312 | tf_op jit(solution)/shard_map/ppermute | solution.py:271
  58.0 1.5 %collective-permute-start.9 = (bf16[4,2,2048]{2,1,0:T(2,128)(2,1)S(1)}, bf16[4,2,2048]{2,1,0:T(2,128)(2,1)S(1)}, u32[]{:S(2)}, u32[]{:S(2)}) collective-permute-start(bf16[4,2,2048]{2,1,0:T(2,128)(2,1)S(1)} %shard_map.110.refs_0_), channel_id=1, source_target_pairs={{0,12},{4,8},{8,4},{12,0},{1,13},{5,9},{9,5},{13,1},{2,14},{6,10},... | collective-permute-start | bytes 98312 | tf_op jit(solution)/shard_map/ppermute | solution.py:271
  59.6 1.0 %collective-permute-done.7.refs_1_ = bf16[4,2,2048]{2,1,0:T(2,128)(2,1)S(1)} collective-permute-done((bf16[4,2,2048]{2,1,0:T(2,128)(2,1)S(1)}, bf16[4,2,2048]{2,1,0:T(2,128)(2,1)S(1)}, u32[]{:S(2)}, u32[]{:S(2)}) %collective-permute-start.7) | collective-permute-done | bytes 32800 | tf_op jit(solution)/shard_map/ppermute | solution.py:271
  60.6 0.0 collective-permute-done.8.refs_2_
  60.6 3.1 %collective-permute-done.9.refs_3_ = bf16[4,2,2048]{2,1,0:T(2,128)(2,1)S(1)} collective-permute-done((bf16[4,2,2048]{2,1,0:T(2,128)(2,1)S(1)}, bf16[4,2,2048]{2,1,0:T(2,128)(2,1)S(1)}, u32[]{:S(2)}, u32[]{:S(2)}) %collective-permute-start.9) | collective-permute-done | bytes 32800 | tf_op jit(solution)/shard_map/ppermute | solution.py:271
  63.7 0.0 slice-done
  63.8 1.6 %shard_map.113 = (f32[8,2,2048]{2,1,0:T(2,128)S(1)}, f32[8,2,2048]{2,1,0:T(2,128)S(1)}) custom-call(bf16[2048,4096]{1,0:T(8,128)(2,1)S(1)} %bitcast.3, bf16[4,2,2048]{2,1,0:T(2,128)(2,1)S(1)} %shard_map.110.refs_0_, bf16[4,2,2048]{2,1,0:T(2,128)(2,1)S(1)} %collective-permute-done.7.refs_1_, bf16[4,2,2048]{2,1,0:T(2,128)(2,1)S(1)} %collective-permute-done.8.refs_2_, ...), custom_call_target="tpu_custom_call" | custom-call | flops 268435456 | bytes 8388608 | tf_op jit(solution)/shard_map/pallas_call | solution.py:427
  65.3 0.1 collective-permute-start.12
  65.4 1.6 %shard_map.111 = (f32[8,2,2048]{2,1,0:T(2,128)S(1)}, f32[8,2,2048]{2,1,0:T(2,128)S(1)}) custom-call(bf16[2048,4096]{1,0:T(8,128)(2,1)S(1)} %bitcast.3, bf16[4,2,2048]{2,1,0:T(2,128)(2,1)S(1)} %shard_map.110.refs_0_, bf16[4,2,2048]{2,1,0:T(2,128)(2,1)S(1)} %collective-permute-done.7.refs_1_, bf16[4,2,2048]{2,1,0:T(2,128)(2,1)S(1)} %collective-permute-done.8.refs_2_, ...), custom_call_target="tpu_custom_call" | custom-call | flops 268435456 | bytes 8388608 | tf_op jit(solution)/shard_map/pallas_call | solution.py:427
  67.0 0.6 collective-permute-start.10
  67.5 0.0 collective-permute-done.12.b_ref
  67.6 1.2 %collective-permute-start.13 = (f32[4,2,2048]{2,1,0:T(2,128)S(1)}, f32[4,2,2048]{2,1,0:T(2,128)S(1)}, u32[]{:S(2)}, u32[]{:S(2)}) collective-permute-start(f32[4,2,2048]{2,1,0:T(2,128)S(1)} %get-tuple-element.42), channel_id=1, source_target_pairs={{0,2},{1,3},{2,0},{3,1},{4,6},{5,7},{6,4},{7,5},{8,10},{9,11},{10,... | collective-permute-start | bytes 196616 | tf_op jit(solution)/shard_map/ppermute | solution.py:275
  68.7 0.0 collective-permute-done.10.b_ref
  68.8 1.0 %collective-permute-start.11 = (f32[4,2,2048]{2,1,0:T(2,128)S(1)}, f32[4,2,2048]{2,1,0:T(2,128)S(1)}, u32[]{:S(2)}, u32[]{:S(2)}) collective-permute-start(f32[4,2,2048]{2,1,0:T(2,128)S(1)} %get-tuple-element.38), channel_id=1, source_target_pairs={{0,2},{1,3},{2,0},{3,1},{4,6},{5,7},{6,4},{7,5},{8,10},{9,11},{10,... | collective-permute-start | bytes 196616 | tf_op jit(solution)/shard_map/ppermute | solution.py:275
  69.7 2.6 %collective-permute-done.13.refs_3_ = f32[4,2,2048]{2,1,0:T(2,128)S(1)} collective-permute-done((f32[4,2,2048]{2,1,0:T(2,128)S(1)}, f32[4,2,2048]{2,1,0:T(2,128)S(1)}, u32[]{:S(2)}, u32[]{:S(2)}) %collective-permute-start.13) | collective-permute-done | bytes 65568 | tf_op jit(solution)/shard_map/ppermute | solution.py:275
  72.3 1.0 %collective-permute-done.11.refs_1_ = f32[4,2,2048]{2,1,0:T(2,128)S(1)} collective-permute-done((f32[4,2,2048]{2,1,0:T(2,128)S(1)}, f32[4,2,2048]{2,1,0:T(2,128)S(1)}, u32[]{:S(2)}, u32[]{:S(2)}) %collective-permute-start.11) | collective-permute-done | bytes 65568 | tf_op jit(solution)/shard_map/ppermute | solution.py:275
  73.3 0.1 shard_map.115
  73.4 1.6 %collective-permute-start.14 = (bf16[2,4096]{1,0:T(2,128)(2,1)S(1)}, bf16[2,4096]{1,0:T(2,128)(2,1)S(1)}, u32[]{:S(2)}, u32[]{:S(2)}) collective-permute-start(bf16[2,4096]{1,0:T(2,128)(2,1)S(1)} %get-tuple-element.43), channel_id=1, source_target_pairs={{0,12},{4,8},{8,4},{12,0},{1,13},{5,9},{9,5},{13,1},{2,14},{6,10},... | collective-permute-start | bytes 49160 | tf_op jit(solution)/shard_map/ppermute | solution.py:271
  75.0 0.0 collective-permute-start.15
  75.0 2.8 %collective-permute-start.16 = (bf16[2,4096]{1,0:T(2,128)(2,1)S(1)}, bf16[2,4096]{1,0:T(2,128)(2,1)S(1)}, u32[]{:S(2)}, u32[]{:S(2)}) collective-permute-start(bf16[2,4096]{1,0:T(2,128)(2,1)S(1)} %get-tuple-element.45), channel_id=1, source_target_pairs={{0,4},{4,0},{8,12},{12,8},{1,5},{5,1},{9,13},{13,9},{2,6},{6,2},{1... | collective-permute-start | bytes 49160 | tf_op jit(solution)/shard_map/ppermute | solution.py:271
  77.8 1.1 %collective-permute-done.14.refs_0_ = bf16[2,4096]{1,0:T(2,128)(2,1)S(1)} collective-permute-done((bf16[2,4096]{1,0:T(2,128)(2,1)S(1)}, bf16[2,4096]{1,0:T(2,128)(2,1)S(1)}, u32[]{:S(2)}, u32[]{:S(2)}) %collective-permute-start.14) | collective-permute-done | bytes 16416 | tf_op jit(solution)/shard_map/ppermute | solution.py:271
  79.0 0.7 collective-permute-done.15.refs_1_
  79.7 0.0 collective-permute-done.16.refs_2_
  79.7 0.6 shard_map.116
  (24 shorter events, 0.1 us)
Async XLA Ops:
  0.0 1.2 %copy-start.9 = (s32[2]{0:T(128)S(1)}, s32[2]{0:T(128)}, u32[]{:S(2)}) copy-start(s32[2]{0:T(128)} %param.18) | copy-start | bytes 28
  0.0 1.3 %copy-start.2 = (bf16[2,256,1024]{2,1,0:T(8,128)(2,1)S(1)}, bf16[2,256,1024]{2,1,0:T(8,128)(2,1)}, u32[]{:S(2)}) copy-start(bf16[2,256,1024]{2,1,0:T(8,128)(2,1)} %keys_ref.5) | copy-start | bytes 3145732
  0.0 1.6 %copy-start.3 = (bf16[2,256,1024]{2,1,0:T(8,128)(2,1)S(1)}, bf16[2,256,1024]{2,1,0:T(8,128)(2,1)}, u32[]{:S(2)}) copy-start(bf16[2,256,1024]{2,1,0:T(8,128)(2,1)} %values_ref.5) | copy-start | bytes 3145732
  0.0 2.5 %copy-start.8 = (f32[16384]{0:T(1024)S(1)}, f32[16384]{0:T(1024)}, u32[]{:S(2)}) copy-start(f32[16384]{0:T(1024)} %param.11) | copy-start | bytes 196612
  0.0 1.0 %copy-start.12 = (bf16[2,16384]{1,0:T(2,128)(2,1)S(1)}, bf16[2,16384]{1,0:T(2,128)(2,1)}, u32[]{:S(2)}) copy-start(bf16[2,16384]{1,0:T(2,128)(2,1)} %tokens_ref.1) | copy-start | bytes 196612
  1.7 0.7 copy-start.11
  3.2 15.3 %all-to-all-start = ((bf16[16,2,2048]{2,1,0:T(2,128)(2,1)}), bf16[16,2,2048]{2,1,0:T(2,128)(2,1)S(1)}, u32[]{:S(2)}, u32[]{:S(2)}) async-start(bf16[16,2,2048]{2,1,0:T(2,128)(2,1)} %shard_map.102), calls=%async_computation | async-start | bytes 262144 | tf_op jit(solution)/shard_map/all_to_all | solution.py:267
  10.6 13.0 %collective-permute-start.4 = (bf16[768,256]{1,0:T(8,128)(2,1)}, bf16[768,256]{1,0:T(8,128)(2,1)S(1)}, u32[]{:S(2)}, u32[]{:S(2)}) collective-permute-start(bf16[768,256]{1,0:T(8,128)(2,1)} %copy-done.11), channel_id=1, source_target_pairs={{0,2},{1,3},{2,0},{3,1},{4,6},{5,7},{6,4},{7,5},{8,10},{9,11},{10,... | collective-permute-start | bytes 1179656 | tf_op jit(solution)/shard_map/ppermute | solution.py:275
  18.5 17.2 %copy-start.5 = (bf16[4096,256]{1,0:T(8,128)(2,1)S(1)}, bf16[4096,256]{1,0:T(8,128)(2,1)}, u32[]{:S(2)}) copy-start(bf16[4096,256]{1,0:T(8,128)(2,1)} %key_ref.3) | copy-start | bytes 6291460
  18.6 17.1 %collective-permute-start = (bf16[1296,256]{1,0:T(8,128)(2,1)S(1)}, bf16[1296,256]{1,0:T(8,128)(2,1)S(1)}, u32[]{:S(2)}, u32[]{:S(2)}) collective-permute-start(bf16[1296,256]{1,0:T(8,128)(2,1)S(1)} %shard_map.103), channel_id=1, source_target_pairs={{0,1},{1,0},{2,3},{3,2},{4,5},{5,4},{6,7},{7,6},{8,9},{9,8},{10,11... | collective-permute-start | bytes 1990664 | tf_op jit(solution)/shard_map/ppermute | solution.py:275
  23.5 30.7 %collective-permute-start.6 = (bf16[1040,256]{1,0:T(8,128)(2,1)S(1)}, bf16[1040,256]{1,0:T(8,128)(2,1)S(1)}, u32[]{:S(2)}, u32[]{:S(2)}) collective-permute-start(bf16[1040,256]{1,0:T(8,128)(2,1)S(1)} %get-tuple-element.34), channel_id=1, source_target_pairs={{0,3},{1,2},{2,1},{3,0},{4,7},{5,6},{6,5},{7,4},{8,11},{9,10},{10,... | collective-permute-start | bytes 1597448 | tf_op jit(solution)/shard_map/ppermute | solution.py:275
  24.1 30.2 %collective-permute-start.5 = (bf16[272,256]{1,0:T(8,128)(2,1)S(1)}, bf16[272,256]{1,0:T(8,128)(2,1)S(1)}, u32[]{:S(2)}, u32[]{:S(2)}) collective-permute-start(bf16[272,256]{1,0:T(8,128)(2,1)S(1)} %get-tuple-element.33), channel_id=1, source_target_pairs={{0,2},{1,3},{2,0},{3,1},{4,6},{5,7},{6,4},{7,5},{8,10},{9,11},{10,... | collective-permute-start | bytes 417800 | tf_op jit(solution)/shard_map/ppermute | solution.py:275
  24.9 5.8 %copy-start = (bf16[4096,2048]{1,0:T(8,128)(2,1)S(1)}, bf16[4096,2048]{1,0:T(8,128)(2,1)}, u32[]{:S(2)}) copy-start(bf16[4096,2048]{1,0:T(8,128)(2,1)} %query_ref.3) | copy-start | bytes 50331652
  30.6 1.6 %copy-start.4 = (bf16[4096,256]{1,0:T(8,128)(2,1)S(1)}, bf16[4096,256]{1,0:T(8,128)(2,1)}, u32[]{:S(2)}) copy-start(bf16[4096,256]{1,0:T(8,128)(2,1)} %key_ref.3) | copy-start | bytes 6291460
  32.2 1.6 %copy-start.6 = (bf16[4096,256]{1,0:T(8,128)(2,1)S(1)}, bf16[4096,256]{1,0:T(8,128)(2,1)}, u32[]{:S(2)}) copy-start(bf16[4096,256]{1,0:T(8,128)(2,1)} %value_ref.3) | copy-start | bytes 6291460
  33.8 5.8 %copy-start.1 = (bf16[4096,2048]{1,0:T(8,128)(2,1)S(1)}, bf16[4096,2048]{1,0:T(8,128)(2,1)}, u32[]{:S(2)}) copy-start(bf16[4096,2048]{1,0:T(8,128)(2,1)} %query_ref.3) | copy-start | bytes 50331652
  33.8 6.4 %copy-start.7 = (bf16[4096,256]{1,0:T(8,128)(2,1)S(1)}, bf16[4096,256]{1,0:T(8,128)(2,1)}, u32[]{:S(2)}) copy-start(bf16[4096,256]{1,0:T(8,128)(2,1)} %value_ref.3) | copy-start | bytes 6291460
  35.7 17.7 %copy-start.10 = (f32[1,128]{1,0:T(1,128)S(1)}, f32[1,128]{1,0:T(1,128)}, u32[]{:S(2)}) copy-start(f32[1,128]{1,0:T(1,128)} %constant.2.clone.frequency_ref) | copy-start | bytes 1540
  42.1 7.2 %collective-permute-start.1 = (f32[4,2,2560]{2,1,0:T(2,128)S(1)}, f32[4,2,2560]{2,1,0:T(2,128)S(1)}, u32[]{:S(2)}, u32[]{:S(2)}) collective-permute-start(f32[4,2,2560]{2,1,0:T(2,128)S(1)} %get-tuple-element.27), channel_id=1, source_target_pairs={{0,12},{4,8},{8,4},{12,0},{1,13},{5,9},{9,5},{13,1},{2,14},{6,10},... | collective-permute-start | bytes 245768 | tf_op jit(solution)/shard_map/ppermute | solution.py:271
  45.6 7.8 %collective-permute-start.2 = (f32[4,2,2560]{2,1,0:T(2,128)S(1)}, f32[4,2,2560]{2,1,0:T(2,128)S(1)}, u32[]{:S(2)}, u32[]{:S(2)}) collective-permute-start(f32[4,2,2560]{2,1,0:T(2,128)S(1)} %get-tuple-element.28), channel_id=1, source_target_pairs={{0,8},{4,12},{8,0},{12,4},{1,9},{5,13},{9,1},{13,5},{2,10},{6,14},... | collective-permute-start | bytes 245768 | tf_op jit(solution)/shard_map/ppermute | solution.py:271
  45.6 7.8 %collective-permute-start.3 = (f32[4,2,2560]{2,1,0:T(2,128)S(1)}, f32[4,2,2560]{2,1,0:T(2,128)S(1)}, u32[]{:S(2)}, u32[]{:S(2)}) collective-permute-start(f32[4,2,2560]{2,1,0:T(2,128)S(1)} %get-tuple-element.29), channel_id=1, source_target_pairs={{0,4},{4,0},{8,12},{12,8},{1,5},{5,1},{9,13},{13,9},{2,6},{6,2},{1... | collective-permute-start | bytes 245768 | tf_op jit(solution)/shard_map/ppermute | solution.py:271
  53.4 10.4 %slice-start = ((s8[16777216]{0:T(1024)(128)(4,1)}), s8[4194304]{0:T(1024)(128)(4,1)S(1)}, s32[]{:S(2)}) async-start(s8[16777216]{0:T(1024)(128)(4,1)} %bitcast.2), calls=%async_computation.1 | async-start | bytes 8388608
  54.2 9.5 %slice-start.1 = ((s8[16777216]{0:T(1024)(128)(4,1)}), s8[4194304]{0:T(1024)(128)(4,1)S(1)}, s32[]{:S(2)}) async-start(s8[16777216]{0:T(1024)(128)(4,1)} %bitcast.2), calls=%async_computation.2 | async-start | bytes 8388608
  54.2 9.5 %slice-start.2 = ((s8[16777216]{0:T(1024)(128)(4,1)}), s8[4194304]{0:T(1024)(128)(4,1)S(1)}, s32[]{:S(2)}) async-start(s8[16777216]{0:T(1024)(128)(4,1)} %bitcast.2), calls=%async_computation.3 | async-start | bytes 8388608
  54.2 9.5 %slice-start.3 = ((s8[16777216]{0:T(1024)(128)(4,1)}), s8[4194304]{0:T(1024)(128)(4,1)S(1)}, s32[]{:S(2)}) async-start(s8[16777216]{0:T(1024)(128)(4,1)} %bitcast.2), calls=%async_computation.4 | async-start | bytes 8388608
  55.1 5.5 %collective-permute-start.7 = (bf16[4,2,2048]{2,1,0:T(2,128)(2,1)S(1)}, bf16[4,2,2048]{2,1,0:T(2,128)(2,1)S(1)}, u32[]{:S(2)}, u32[]{:S(2)}) collective-permute-start(bf16[4,2,2048]{2,1,0:T(2,128)(2,1)S(1)} %shard_map.110.refs_0_), channel_id=1, source_target_pairs={{0,8},{4,12},{8,0},{12,4},{1,9},{5,13},{9,1},{13,5},{2,10},{6,14},... | collective-permute-start | bytes 98312 | tf_op jit(solution)/shard_map/ppermute | solution.py:271
  55.4 5.2 %collective-permute-start.8 = (bf16[4,2,2048]{2,1,0:T(2,128)(2,1)S(1)}, bf16[4,2,2048]{2,1,0:T(2,128)(2,1)S(1)}, u32[]{:S(2)}, u32[]{:S(2)}) collective-permute-start(bf16[4,2,2048]{2,1,0:T(2,128)(2,1)S(1)} %shard_map.110.refs_0_), channel_id=1, source_target_pairs={{0,4},{4,0},{8,12},{12,8},{1,5},{5,1},{9,13},{13,9},{2,6},{6,2},{1... | collective-permute-start | bytes 98312 | tf_op jit(solution)/shard_map/ppermute | solution.py:271
  58.0 5.7 %collective-permute-start.9 = (bf16[4,2,2048]{2,1,0:T(2,128)(2,1)S(1)}, bf16[4,2,2048]{2,1,0:T(2,128)(2,1)S(1)}, u32[]{:S(2)}, u32[]{:S(2)}) collective-permute-start(bf16[4,2,2048]{2,1,0:T(2,128)(2,1)S(1)} %shard_map.110.refs_0_), channel_id=1, source_target_pairs={{0,12},{4,8},{8,4},{12,0},{1,13},{5,9},{9,5},{13,1},{2,14},{6,10},... | collective-permute-start | bytes 98312 | tf_op jit(solution)/shard_map/ppermute | solution.py:271
  65.3 2.2 %collective-permute-start.12 = (f32[8,2,2048]{2,1,0:T(2,128)S(1)}, f32[8,2,2048]{2,1,0:T(2,128)S(1)}, u32[]{:S(2)}, u32[]{:S(2)}) collective-permute-start(f32[8,2,2048]{2,1,0:T(2,128)S(1)} %get-tuple-element.40), channel_id=1, source_target_pairs={{0,1},{1,0},{2,3},{3,2},{4,5},{5,4},{6,7},{7,6},{8,9},{9,8},{10,11... | collective-permute-start | bytes 393224 | tf_op jit(solution)/shard_map/ppermute | solution.py:275
  67.0 1.8 %collective-permute-start.10 = (f32[8,2,2048]{2,1,0:T(2,128)S(1)}, f32[8,2,2048]{2,1,0:T(2,128)S(1)}, u32[]{:S(2)}, u32[]{:S(2)}) collective-permute-start(f32[8,2,2048]{2,1,0:T(2,128)S(1)} %get-tuple-element.36), channel_id=1, source_target_pairs={{0,1},{1,0},{2,3},{3,2},{4,5},{5,4},{6,7},{7,6},{8,9},{9,8},{10,11... | collective-permute-start | bytes 393224 | tf_op jit(solution)/shard_map/ppermute | solution.py:275
  67.6 4.7 %collective-permute-start.13 = (f32[4,2,2048]{2,1,0:T(2,128)S(1)}, f32[4,2,2048]{2,1,0:T(2,128)S(1)}, u32[]{:S(2)}, u32[]{:S(2)}) collective-permute-start(f32[4,2,2048]{2,1,0:T(2,128)S(1)} %get-tuple-element.42), channel_id=1, source_target_pairs={{0,2},{1,3},{2,0},{3,1},{4,6},{5,7},{6,4},{7,5},{8,10},{9,11},{10,... | collective-permute-start | bytes 196616 | tf_op jit(solution)/shard_map/ppermute | solution.py:275
  68.8 4.5 %collective-permute-start.11 = (f32[4,2,2048]{2,1,0:T(2,128)S(1)}, f32[4,2,2048]{2,1,0:T(2,128)S(1)}, u32[]{:S(2)}, u32[]{:S(2)}) collective-permute-start(f32[4,2,2048]{2,1,0:T(2,128)S(1)} %get-tuple-element.38), channel_id=1, source_target_pairs={{0,2},{1,3},{2,0},{3,1},{4,6},{5,7},{6,4},{7,5},{8,10},{9,11},{10,... | collective-permute-start | bytes 196616 | tf_op jit(solution)/shard_map/ppermute | solution.py:275
  73.4 5.6 %collective-permute-start.14 = (bf16[2,4096]{1,0:T(2,128)(2,1)S(1)}, bf16[2,4096]{1,0:T(2,128)(2,1)S(1)}, u32[]{:S(2)}, u32[]{:S(2)}) collective-permute-start(bf16[2,4096]{1,0:T(2,128)(2,1)S(1)} %get-tuple-element.43), channel_id=1, source_target_pairs={{0,12},{4,8},{8,4},{12,0},{1,13},{5,9},{9,5},{13,1},{2,14},{6,10},... | collective-permute-start | bytes 49160 | tf_op jit(solution)/shard_map/ppermute | solution.py:271
  75.0 4.7 %collective-permute-start.15 = (bf16[2,4096]{1,0:T(2,128)(2,1)S(1)}, bf16[2,4096]{1,0:T(2,128)(2,1)S(1)}, u32[]{:S(2)}, u32[]{:S(2)}) collective-permute-start(bf16[2,4096]{1,0:T(2,128)(2,1)S(1)} %get-tuple-element.44), channel_id=1, source_target_pairs={{0,8},{4,12},{8,0},{12,4},{1,9},{5,13},{9,1},{13,5},{2,10},{6,14},... | collective-permute-start | bytes 49160 | tf_op jit(solution)/shard_map/ppermute | solution.py:271
  75.0 4.7 %collective-permute-start.16 = (bf16[2,4096]{1,0:T(2,128)(2,1)S(1)}, bf16[2,4096]{1,0:T(2,128)(2,1)S(1)}, u32[]{:S(2)}, u32[]{:S(2)}) collective-permute-start(bf16[2,4096]{1,0:T(2,128)(2,1)S(1)} %get-tuple-element.45), channel_id=1, source_target_pairs={{0,4},{4,0},{8,12},{12,8},{1,5},{5,1},{9,13},{13,9},{2,6},{6,2},{1... | collective-permute-start | bytes 49160 | tf_op jit(solution)/shard_map/ppermute | solution.py:271

commit v21 on v17

--- a/solution.py
+++ b/solution.py
@@ -14,6 +14,10 @@
 MIB = 1024 * 1024
 IN_VMEM = pl.BlockSpec(memory_space=pltpu.VMEM)
 ANYWHERE = pl.BlockSpec(memory_space=pl.ANY)
+
+
+def sequence(wide):
+    return sorted(range(1, wide), key=lambda k: (k != wide // 2, -k))
 
 
 def scale_kernel(tokens_ref, scaled_ref):
@@ -197,7 +201,8 @@
 
 
 def output_kernel(at, cols, order, weight_ref, *refs):
-    blocks, keep_ref, give_ref = [refs[n] for n in order], refs[-2], refs[-1]
+    keep_ref, give_ref = refs[-2:]
+    blocks = [refs[order.index(k)] for k in range(len(order))]
     wide = len(blocks)
     plane, rows, depth = blocks[0].shape
     attended = jnp.concatenate(
@@ -229,7 +234,9 @@
 
 
 def finish_kernel(*refs):
-    blocks, result_ref = refs[-2::-1], refs[-1]
+    result_ref = refs[-1]
+    order = [*sequence(len(refs) - 1), 0]
+    blocks = [refs[order.index(k)] for k in range(len(order))]
     own = lax.axis_index("gx")
     cols = blocks[0].shape[-1]
     for k, block in enumerate(blocks):
@@ -382,7 +389,7 @@
     )(*attended)
     head_rows = swap_wide([attended] * wide)
     parts = 2
-    order = [0, *range(wide - 2, 0, -1), wide - 1]
+    order = [0, *sequence(wide)[1:], sequence(wide)[0]]
     part_cols = out_cols // parts
     sums = []
     for p in range(parts):
@@ -425,7 +432,7 @@
         in_specs=[IN_VMEM] * wide,
         out_specs=IN_VMEM,
         compiler_params=params(8),
-    )(*blocks[::-1])
+    )(*[blocks[k] for k in [*sequence(wide), 0]])
 
 
 def solution(mesh):

time: 60.2 us -> 60.2 us (level)
  starting transfers between devices: 21.3 us -> 19.5 us
  waiting for transfers between devices: 14.2 us -> 16 us
    ppermute x10, waiting for transfers between devices: 10.1 us -> 11.9 us  [swap_pairs(): lax.ppermute(value, axis, [(i, i ^ step) for i in range(lax.axis_size(axi...]
    ppermute x10, starting transfers between devices: 13.8 us -> 12 us  [swap_pairs(): lax.ppermute(value, axis, [(i, i ^ step) for i in range(lax.axis_size(axi...]
  transfers between devices with their start and end apart: 18 -> 18, of which waited for: 10 -> 11; matrix products, arithmetic and copies ran while one was open for 0% -> 0% of each run, Pallas kernels for 11% -> 11%
where the time goes in v21:
time: 60.2 us; the launch traced here: 60 us
  starting transfers between devices  19.5 us (32%)
  waiting for transfers between devices  16 us (27%)
  blocking collectives  13 us (22%)
  Pallas kernels  9.97 us (17%)
  local copies, waits for them, and re-layouts  1.27 us (2%)
    all_to_all x1, blocking collectives, swap_blocks(): return lax.all_to_all(blocks, axes, split_axis=0, concat_axis=0, tiled=True)  13 us
    ppermute x10, starting transfers between devices, swap_pairs(): lax.ppermute(value, axis, [(i, i ^ step) for i in range(lax.axis_size(axi...  12 us
    ppermute x10, waiting for transfers between devices, swap_pairs(): lax.ppermute(value, axis, [(i, i ^ step) for i in range(lax.axis_size(axi...  11.9 us
    ppermute x8, starting transfers between devices, swap_plane(): lax.ppermute(value, PLANE, [(i, i ^ step) for i in range(lax.axis_size(PL...  7.55 us
    ppermute x8, waiting for transfers between devices, swap_plane(): lax.ppermute(value, PLANE, [(i, i ^ step) for i in range(lax.axis_size(PL...  4.12 us
    pallas_call x2, Pallas kernels, shards(): pl.pallas_call(functools.partial(output_kernel, p * part_cols, part_cols,...  3.09 us
    pallas_call x1, Pallas kernels, shards(): pl.pallas_call(functools.partial(project_kernel, False, wide, plane), out...  1.98 us
    pallas_call x1, Pallas kernels, shards(): pl.pallas_call(functools.partial(project_kernel, True, wide, plane), out_...  1.9 us
  transfers between devices with their start and end apart: 18, of which 11 were waited for; matrix products, arithmetic and copies ran while one was open for 0% of the time, Pallas kernels for 11%

profile of v21, /device:TPU:0, one launch (start us, length us, event | category | flops | bytes accessed | tf_op | source)
XLA Modules:
  0.0 60.0 jit_solution(1491983922928327582)
XLA Ops:
  0.0 0.0 copy-start.1
  0.0 0.0 copy-start.2
  0.0 0.0 copy-start.8
  0.0 1.0 %copy-done.8 = bf16[2,16384]{1,0:T(2,128)(2,1)S(1)} copy-done((bf16[2,16384]{1,0:T(2,128)(2,1)S(1)}, bf16[2,16384]{1,0:T(2,128)(2,1)}, u32[]{:S(2)}) %copy-start.8) | copy-done | bytes 65560
  1.0 0.2 shard_map.100.scaled_ref
  1.3 0.0 copy-done.5
  1.3 0.1 shard_map.101._
  1.4 0.0 copy-done.6
  1.4 0.0 copy-done.3
  1.4 0.2 copy-done.4
  1.6 0.2 shard_map.102
  1.8 3.0 %collective-permute-start.1 = (bf16[768,256]{1,0:T(8,128)(2,1)S(1)}, bf16[768,256]{1,0:T(8,128)(2,1)S(1)}, u32[]{:S(2)}, u32[]{:S(2)}) collective-permute-start(bf16[768,256]{1,0:T(8,128)(2,1)S(1)} %get-tuple-element.31), channel_id=1, source_target_pairs={{0,2},{1,3},{2,0},{3,1},{4,6},{5,7},{6,4},{7,5},{8,10},{9,11},{10,... | collective-permute-start | bytes 1179656 | tf_op jit(solution)/shard_map/ppermute | solution.py:256
  4.9 13.0 %all_to_all.5.refs_3_.rows_ref._ = bf16[16,2,2048]{2,1,0:T(2,128)(2,1)S(1)} all-to-all(bf16[16,2,2048]{2,1,0:T(2,128)(2,1)S(1)} %shard_map.101._), channel_id=1, replica_groups=mesh['groups'=2,'gx'=4,'gy'=2,'gz'=2] {'gx','gy','gz'}, dimensions={0} | all-to-all | bytes 262144 | tf_op jit(solution)/shard_map/all_to_all | solution.py:248
  17.8 0.0 collective-permute-done.1.refs_4_
  17.8 0.0 collective-permute-start.2
  17.8 0.1 collective-permute-start.7
  17.9 0.4 collective-permute-start
  18.3 1.7 %collective-permute-start.6 = (bf16[272,256]{1,0:T(8,128)(2,1)S(1)}, bf16[272,256]{1,0:T(8,128)(2,1)S(1)}, u32[]{:S(2)}, u32[]{:S(2)}) collective-permute-start(bf16[272,256]{1,0:T(8,128)(2,1)S(1)} %get-tuple-element.37), channel_id=1, source_target_pairs={{0,2},{1,3},{2,0},{3,1},{4,6},{5,7},{6,4},{7,5},{8,10},{9,11},{10,... | collective-permute-start | bytes 417800 | tf_op jit(solution)/shard_map/ppermute | solution.py:256
  20.0 0.0 copy-done
  20.0 0.0 copy-done.1
  20.0 0.0 copy-done.2
  20.0 1.9 %shard_map.104.refs_1_ = f32[32,2560]{1,0:T(8,128)S(1)} custom-call(bf16[16,2,2048]{2,1,0:T(2,128)(2,1)S(1)} %all_to_all.5.refs_3_.rows_ref._, bf16[4096,2048]{1,0:T(8,128)(2,1)S(1)} %copy-done, bf16[4096,256]{1,0:T(8,128)(2,1)S(1)} %copy-done.1, bf16[4096,256]{1,0:T(8,128)(2,1)S(1)} %copy-done.2), custom_call_target="tpu_custom_call" | custom-call | flops 335544320 | bytes 10485760 | tf_op jit(solution)/shard_map/pallas_call | solution.py:348
  21.9 0.0 collective-permute-done.rows_ref
  22.0 0.0 collective-permute-done.2.refs_0_.refs_5_.refs_7_
  22.0 2.0 %shard_map.105 = (f32[4,2,2560]{2,1,0:T(2,128)S(1)}, f32[4,2,2560]{2,1,0:T(2,128)S(1)}, f32[4,2,2560]{2,1,0:T(2,128)S(1)}, f32[4,2,2560]{2,1,0:T(2,128)S(1)}) custom-call(bf16[16,2,2048]{2,1,0:T(2,128)(2,1)S(1)} %collective-permute-done.rows_ref, bf16[4096,2048]{1,0:T(8,128)(2,1)S(1)} %copy-done, bf16[4096,256]{1,0:T(8,128)(2,1)S(1)} %copy-done.1, ...), custom_call_target="tpu_custom_call" | custom-call | flops 335544320 | bytes 10485760 | tf_op jit(solution)/shard_map/pallas_call | solution.py:356
  24.0 1.5 %collective-permute-start.3 = (f32[4,2,2560]{2,1,0:T(2,128)S(1)}, f32[4,2,2560]{2,1,0:T(2,128)S(1)}, u32[]{:S(2)}, u32[]{:S(2)}) collective-permute-start(f32[4,2,2560]{2,1,0:T(2,128)S(1)} %get-tuple-element.33), channel_id=1, source_target_pairs={{0,12},{4,8},{8,4},{12,0},{1,13},{5,9},{9,5},{13,1},{2,14},{6,10},... | collective-permute-start | bytes 245768 | tf_op jit(solution)/shard_map/ppermute | solution.py:252
  25.4 0.0 collective-permute-start.4
  25.5 3.0 %collective-permute-start.5 = (f32[4,2,2560]{2,1,0:T(2,128)S(1)}, f32[4,2,2560]{2,1,0:T(2,128)S(1)}, u32[]{:S(2)}, u32[]{:S(2)}) collective-permute-start(f32[4,2,2560]{2,1,0:T(2,128)S(1)} %get-tuple-element.35), channel_id=1, source_target_pairs={{0,4},{4,0},{8,12},{12,8},{1,5},{5,1},{9,13},{13,9},{2,6},{6,2},{1... | collective-permute-start | bytes 245768 | tf_op jit(solution)/shard_map/ppermute | solution.py:252
  28.4 0.1 shard_map.106.refs_4_.refs_6_
  28.5 2.7 %collective-permute-done.3.refs_0_ = f32[4,2,2560]{2,1,0:T(2,128)S(1)} collective-permute-done((f32[4,2,2560]{2,1,0:T(2,128)S(1)}, f32[4,2,2560]{2,1,0:T(2,128)S(1)}, u32[]{:S(2)}, u32[]{:S(2)}) %collective-permute-start.3) | collective-permute-done | bytes 81952 | tf_op jit(solution)/shard_map/ppermute | solution.py:252
  31.2 2.6 %collective-permute-done.4.refs_1_ = f32[4,2,2560]{2,1,0:T(2,128)S(1)} collective-permute-done((f32[4,2,2560]{2,1,0:T(2,128)S(1)}, f32[4,2,2560]{2,1,0:T(2,128)S(1)}, u32[]{:S(2)}, u32[]{:S(2)}) %collective-permute-start.4) | collective-permute-done | bytes 81952 | tf_op jit(solution)/shard_map/ppermute | solution.py:252
  33.8 0.0 collective-permute-done.5.refs_2_
  33.9 0.8 %shard_map.107.refs_0_ = bf16[2,2,2048]{2,1,0:T(2,128)(2,1)S(1)} custom-call(f32[1,128]{1,0:T(1,128)S(1)} %copy-done.7, f32[4,2,2560]{2,1,0:T(2,128)S(1)} %collective-permute-done.3.refs_0_, f32[4,2,2560]{2,1,0:T(2,128)S(1)} %collective-permute-done.4.refs_1_, f32[4,2,2560]{2,1,0:T(2,128)S(1)} %collective-permute-done.5.refs_2_, ...), custom_call_target="tpu_custom_call" | custom-call | flops 1 | bytes 1 | tf_op jit(solution)/shard_map/pallas_call | solution.py:374
  34.7 0.0 slice-start.1
  34.7 0.0 slice-start.2
  34.7 0.0 slice-start.3
  34.7 0.5 collective-permute-done.6.refs_5_
  35.3 0.0 collective-permute-done.7.refs_8_
  35.3 0.8 %shard_map.108.refs_1_ = bf16[2,2,2048]{2,1,0:T(2,128)(2,1)S(1)} custom-call(f32[1,128]{1,0:T(1,128)S(1)} %copy-done.7, f32[4,2,2560]{2,1,0:T(2,128)S(1)} %collective-permute-done.3.refs_0_, f32[4,2,2560]{2,1,0:T(2,128)S(1)} %collective-permute-done.4.refs_1_, f32[4,2,2560]{2,1,0:T(2,128)S(1)} %collective-permute-done.5.refs_2_, ...), custom_call_target="tpu_custom_call" | custom-call | flops 10000000000 | bytes 4194304 | tf_op jit(solution)/shard_map/pallas_call | solution.py:374
  36.1 0.5 collective-permute-start.10
  36.6 1.9 %collective-permute-start.8 = (bf16[4,2,2048]{2,1,0:T(2,128)(2,1)S(1)}, bf16[4,2,2048]{2,1,0:T(2,128)(2,1)S(1)}, u32[]{:S(2)}, u32[]{:S(2)}) collective-permute-start(bf16[4,2,2048]{2,1,0:T(2,128)(2,1)S(1)} %shard_map.109.refs_0_), channel_id=1, source_target_pairs={{0,12},{4,8},{8,4},{12,0},{1,13},{5,9},{9,5},{13,1},{2,14},{6,10},... | collective-permute-start | bytes 98312 | tf_op jit(solution)/shard_map/ppermute | solution.py:252
  38.5 1.2 %collective-permute-start.9 = (bf16[4,2,2048]{2,1,0:T(2,128)(2,1)S(1)}, bf16[4,2,2048]{2,1,0:T(2,128)(2,1)S(1)}, u32[]{:S(2)}, u32[]{:S(2)}) collective-permute-start(bf16[4,2,2048]{2,1,0:T(2,128)(2,1)S(1)} %shard_map.109.refs_0_), channel_id=1, source_target_pairs={{0,4},{4,0},{8,12},{12,8},{1,5},{5,1},{9,13},{13,9},{2,6},{6,2},{1... | collective-permute-start | bytes 98312 | tf_op jit(solution)/shard_map/ppermute | solution.py:252
  39.7 1.5 %collective-permute-done.10.refs_3_ = bf16[4,2,2048]{2,1,0:T(2,128)(2,1)S(1)} collective-permute-done((bf16[4,2,2048]{2,1,0:T(2,128)(2,1)S(1)}, bf16[4,2,2048]{2,1,0:T(2,128)(2,1)S(1)}, u32[]{:S(2)}, u32[]{:S(2)}) %collective-permute-start.10) | collective-permute-done | bytes 32800 | tf_op jit(solution)/shard_map/ppermute | solution.py:252
  41.2 1.1 %collective-permute-done.8.refs_1_ = bf16[4,2,2048]{2,1,0:T(2,128)(2,1)S(1)} collective-permute-done((bf16[4,2,2048]{2,1,0:T(2,128)(2,1)S(1)}, bf16[4,2,2048]{2,1,0:T(2,128)(2,1)S(1)}, u32[]{:S(2)}, u32[]{:S(2)}) %collective-permute-start.8) | collective-permute-done | bytes 32800 | tf_op jit(solution)/shard_map/ppermute | solution.py:252
  42.3 0.3 collective-permute-done.9.refs_2_
  42.7 0.0 slice-done.3
  42.7 1.5 %shard_map.112 = (f32[8,2,2048]{2,1,0:T(2,128)S(1)}, f32[8,2,2048]{2,1,0:T(2,128)S(1)}) custom-call(bf16[2048,4096]{1,0:T(8,128)(2,1)S(1)} %bitcast.3, bf16[4,2,2048]{2,1,0:T(2,128)(2,1)S(1)} %shard_map.109.refs_0_, bf16[4,2,2048]{2,1,0:T(2,128)(2,1)S(1)} %collective-permute-done.8.refs_1_, bf16[4,2,2048]{2,1,0:T(2,128)(2,1)S(1)} %collective-permute-done.9.refs_2_, ...), custom_call_target="tpu_custom_call" | custom-call | flops 268435456 | bytes 8388608 | tf_op jit(solution)/shard_map/pallas_call | solution.py:398
  44.3 0.1 collective-permute-start.13
  44.3 1.5 %shard_map.110 = (f32[8,2,2048]{2,1,0:T(2,128)S(1)}, f32[8,2,2048]{2,1,0:T(2,128)S(1)}) custom-call(bf16[2048,4096]{1,0:T(8,128)(2,1)S(1)} %bitcast.3, bf16[4,2,2048]{2,1,0:T(2,128)(2,1)S(1)} %shard_map.109.refs_0_, bf16[4,2,2048]{2,1,0:T(2,128)(2,1)S(1)} %collective-permute-done.8.refs_1_, bf16[4,2,2048]{2,1,0:T(2,128)(2,1)S(1)} %collective-permute-done.9.refs_2_, ...), custom_call_target="tpu_custom_call" | custom-call | flops 268435456 | bytes 8388608 | tf_op jit(solution)/shard_map/pallas_call | solution.py:398
  45.9 0.6 collective-permute-start.11
  46.5 0.0 collective-permute-done.13.b_ref
  46.5 1.2 %collective-permute-start.14 = (f32[4,2,2048]{2,1,0:T(2,128)S(1)}, f32[4,2,2048]{2,1,0:T(2,128)S(1)}, u32[]{:S(2)}, u32[]{:S(2)}) collective-permute-start(f32[4,2,2048]{2,1,0:T(2,128)S(1)} %get-tuple-element.46), channel_id=1, source_target_pairs={{0,2},{1,3},{2,0},{3,1},{4,6},{5,7},{6,4},{7,5},{8,10},{9,11},{10,... | collective-permute-start | bytes 196616 | tf_op jit(solution)/shard_map/ppermute | solution.py:256
  47.7 0.0 collective-permute-done.11.b_ref
  47.7 1.0 %collective-permute-start.12 = (f32[4,2,2048]{2,1,0:T(2,128)S(1)}, f32[4,2,2048]{2,1,0:T(2,128)S(1)}, u32[]{:S(2)}, u32[]{:S(2)}) collective-permute-start(f32[4,2,2048]{2,1,0:T(2,128)S(1)} %get-tuple-element.42), channel_id=1, source_target_pairs={{0,2},{1,3},{2,0},{3,1},{4,6},{5,7},{6,4},{7,5},{8,10},{9,11},{10,... | collective-permute-start | bytes 196616 | tf_op jit(solution)/shard_map/ppermute | solution.py:256
  48.7 2.6 %collective-permute-done.14.refs_3_ = f32[4,2,2048]{2,1,0:T(2,128)S(1)} collective-permute-done((f32[4,2,2048]{2,1,0:T(2,128)S(1)}, f32[4,2,2048]{2,1,0:T(2,128)S(1)}, u32[]{:S(2)}, u32[]{:S(2)}) %collective-permute-start.14) | collective-permute-done | bytes 65568 | tf_op jit(solution)/shard_map/ppermute | solution.py:256
  51.2 1.0 %collective-permute-done.12.refs_1_ = f32[4,2,2048]{2,1,0:T(2,128)S(1)} collective-permute-done((f32[4,2,2048]{2,1,0:T(2,128)S(1)}, f32[4,2,2048]{2,1,0:T(2,128)S(1)}, u32[]{:S(2)}, u32[]{:S(2)}) %collective-permute-start.12) | collective-permute-done | bytes 65568 | tf_op jit(solution)/shard_map/ppermute | solution.py:256
  52.2 0.1 shard_map.114
  52.3 1.1 %collective-permute-start.15 = (bf16[2,4096]{1,0:T(2,128)(2,1)S(1)}, bf16[2,4096]{1,0:T(2,128)(2,1)S(1)}, u32[]{:S(2)}, u32[]{:S(2)}) collective-permute-start(bf16[2,4096]{1,0:T(2,128)(2,1)S(1)} %get-tuple-element.47), channel_id=1, source_target_pairs={{0,8},{4,12},{8,0},{12,4},{1,9},{5,13},{9,1},{13,5},{2,10},{6,14},... | collective-permute-start | bytes 49160 | tf_op jit(solution)/shard_map/ppermute | solution.py:252
  53.4 2.3 %collective-permute-start.16 = (bf16[2,4096]{1,0:T(2,128)(2,1)S(1)}, bf16[2,4096]{1,0:T(2,128)(2,1)S(1)}, u32[]{:S(2)}, u32[]{:S(2)}) collective-permute-start(bf16[2,4096]{1,0:T(2,128)(2,1)S(1)} %get-tuple-element.48), channel_id=1, source_target_pairs={{0,12},{4,8},{8,4},{12,0},{1,13},{5,9},{9,5},{13,1},{2,14},{6,10},... | collective-permute-start | bytes 49160 | tf_op jit(solution)/shard_map/ppermute | solution.py:252
  55.6 0.2 collective-permute-start.17
  55.8 1.1 %collective-permute-done.15.refs_0_ = bf16[2,4096]{1,0:T(2,128)(2,1)S(1)} collective-permute-done((bf16[2,4096]{1,0:T(2,128)(2,1)S(1)}, bf16[2,4096]{1,0:T(2,128)(2,1)S(1)}, u32[]{:S(2)}, u32[]{:S(2)}) %collective-permute-start.15) | collective-permute-done | bytes 16416 | tf_op jit(solution)/shard_map/ppermute | solution.py:252
  57.0 1.9 %collective-permute-done.16.refs_1_ = bf16[2,4096]{1,0:T(2,128)(2,1)S(1)} collective-permute-done((bf16[2,4096]{1,0:T(2,128)(2,1)S(1)}, bf16[2,4096]{1,0:T(2,128)(2,1)S(1)}, u32[]{:S(2)}, u32[]{:S(2)}) %collective-permute-start.16) | collective-permute-done | bytes 16416 | tf_op jit(solution)/shard_map/ppermute | solution.py:252
  58.9 0.5 collective-permute-done.17.refs_2_
  59.4 0.6 %shard_map.115 = bf16[2,16384]{1,0:T(2,128)(2,1)} custom-call(bf16[2,4096]{1,0:T(2,128)(2,1)S(1)} %collective-permute-done.15.refs_0_, bf16[2,4096]{1,0:T(2,128)(2,1)S(1)} %collective-permute-done.16.refs_1_, bf16[2,4096]{1,0:T(2,128)(2,1)S(1)} %collective-permute-done.17.refs_2_, bf16[2,4096]{1,0:T(2,128)(2,1)S(1)} %get-tuple-element.50.refs_3_), custom_call_target="tpu_custom_call" | custom-call | tf_op jit(solution)/shard_map/pallas_call | solution.py:429
  (16 shorter events, 0.1 us)
Async XLA Ops:
  0.0 1.3 %copy-start.5 = (f32[16384]{0:T(1024)S(1)}, f32[16384]{0:T(1024)}, u32[]{:S(2)}) copy-start(f32[16384]{0:T(1024)} %param.11) | copy-start | bytes 196612
  0.0 1.4 %copy-start.6 = (s32[2]{0:T(128)S(1)}, s32[2]{0:T(128)}, u32[]{:S(2)}) copy-start(s32[2]{0:T(128)} %param.18) | copy-start | bytes 28
  0.0 1.4 %copy-start.3 = (bf16[2,256,1024]{2,1,0:T(8,128)(2,1)S(1)}, bf16[2,256,1024]{2,1,0:T(8,128)(2,1)}, u32[]{:S(2)}) copy-start(bf16[2,256,1024]{2,1,0:T(8,128)(2,1)} %keys_ref.3) | copy-start | bytes 3145732
  0.0 1.6 %copy-start.4 = (bf16[2,256,1024]{2,1,0:T(8,128)(2,1)S(1)}, bf16[2,256,1024]{2,1,0:T(8,128)(2,1)}, u32[]{:S(2)}) copy-start(bf16[2,256,1024]{2,1,0:T(8,128)(2,1)} %values_ref.3) | copy-start | bytes 3145732
  0.0 20.0 %copy-start = (bf16[4096,2048]{1,0:T(8,128)(2,1)S(1)}, bf16[4096,2048]{1,0:T(8,128)(2,1)}, u32[]{:S(2)}) copy-start(bf16[4096,2048]{1,0:T(8,128)(2,1)} %query_ref.3) | copy-start | bytes 50331652
  0.0 20.0 %copy-start.1 = (bf16[4096,256]{1,0:T(8,128)(2,1)S(1)}, bf16[4096,256]{1,0:T(8,128)(2,1)}, u32[]{:S(2)}) copy-start(bf16[4096,256]{1,0:T(8,128)(2,1)} %key_ref.3) | copy-start | bytes 6291460
  0.0 20.0 %copy-start.2 = (bf16[4096,256]{1,0:T(8,128)(2,1)S(1)}, bf16[4096,256]{1,0:T(8,128)(2,1)}, u32[]{:S(2)}) copy-start(bf16[4096,256]{1,0:T(8,128)(2,1)} %value_ref.3) | copy-start | bytes 6291460
  0.0 1.0 %copy-start.8 = (bf16[2,16384]{1,0:T(2,128)(2,1)S(1)}, bf16[2,16384]{1,0:T(2,128)(2,1)}, u32[]{:S(2)}) copy-start(bf16[2,16384]{1,0:T(2,128)(2,1)} %tokens_ref.1) | copy-start | bytes 196612
  1.8 16.0 %collective-permute-start.1 = (bf16[768,256]{1,0:T(8,128)(2,1)S(1)}, bf16[768,256]{1,0:T(8,128)(2,1)S(1)}, u32[]{:S(2)}, u32[]{:S(2)}) collective-permute-start(bf16[768,256]{1,0:T(8,128)(2,1)S(1)} %get-tuple-element.31), channel_id=1, source_target_pairs={{0,2},{1,3},{2,0},{3,1},{4,6},{5,7},{6,4},{7,5},{8,10},{9,11},{10,... | collective-permute-start | bytes 1179656 | tf_op jit(solution)/shard_map/ppermute | solution.py:256
  17.8 4.1 %collective-permute-start.2 = (bf16[1040,256]{1,0:T(8,128)(2,1)S(1)}, bf16[1040,256]{1,0:T(8,128)(2,1)S(1)}, u32[]{:S(2)}, u32[]{:S(2)}) collective-permute-start(bf16[1040,256]{1,0:T(8,128)(2,1)S(1)} %get-tuple-element.32), channel_id=1, source_target_pairs={{0,1},{1,0},{2,3},{3,2},{4,5},{5,4},{6,7},{7,6},{8,9},{9,8},{10,11... | collective-permute-start | bytes 1597448 | tf_op jit(solution)/shard_map/ppermute | solution.py:256
  17.8 17.4 %collective-permute-start.7 = (bf16[1040,256]{1,0:T(8,128)(2,1)S(1)}, bf16[1040,256]{1,0:T(8,128)(2,1)S(1)}, u32[]{:S(2)}, u32[]{:S(2)}) collective-permute-start(bf16[1040,256]{1,0:T(8,128)(2,1)S(1)} %get-tuple-element.38), channel_id=1, source_target_pairs={{0,3},{1,2},{2,1},{3,0},{4,7},{5,6},{6,5},{7,4},{8,11},{9,10},{10,... | collective-permute-start | bytes 1597448 | tf_op jit(solution)/shard_map/ppermute | solution.py:256
  17.9 4.0 %collective-permute-start = (bf16[16,2,2048]{2,1,0:T(2,128)(2,1)S(1)}, bf16[16,2,2048]{2,1,0:T(2,128)(2,1)S(1)}, u32[]{:S(2)}, u32[]{:S(2)}) collective-permute-start(bf16[16,2,2048]{2,1,0:T(2,128)(2,1)S(1)} %all_to_all.5.refs_3_.rows_ref._), channel_id=1, source_target_pairs={{0,1},{1,0},{2,3},{3,2},{4,5},{5,4},{6,7},{7,6},{8,9},{9,8},{10,11... | collective-permute-start | bytes 393224 | tf_op jit(solution)/shard_map/ppermute | solution.py:252
  18.3 16.9 %collective-permute-start.6 = (bf16[272,256]{1,0:T(8,128)(2,1)S(1)}, bf16[272,256]{1,0:T(8,128)(2,1)S(1)}, u32[]{:S(2)}, u32[]{:S(2)}) collective-permute-start(bf16[272,256]{1,0:T(8,128)(2,1)S(1)} %get-tuple-element.37), channel_id=1, source_target_pairs={{0,2},{1,3},{2,0},{3,1},{4,6},{5,7},{6,4},{7,5},{8,10},{9,11},{10,... | collective-permute-start | bytes 417800 | tf_op jit(solution)/shard_map/ppermute | solution.py:256
  21.9 11.9 %copy-start.7 = (f32[1,128]{1,0:T(1,128)S(1)}, f32[1,128]{1,0:T(1,128)}, u32[]{:S(2)}) copy-start(f32[1,128]{1,0:T(1,128)} %constant.2.clone.frequency_ref) | copy-start | bytes 1540
  24.0 7.3 %collective-permute-start.3 = (f32[4,2,2560]{2,1,0:T(2,128)S(1)}, f32[4,2,2560]{2,1,0:T(2,128)S(1)}, u32[]{:S(2)}, u32[]{:S(2)}) collective-permute-start(f32[4,2,2560]{2,1,0:T(2,128)S(1)} %get-tuple-element.33), channel_id=1, source_target_pairs={{0,12},{4,8},{8,4},{12,0},{1,13},{5,9},{9,5},{13,1},{2,14},{6,10},... | collective-permute-start | bytes 245768 | tf_op jit(solution)/shard_map/ppermute | solution.py:252
  25.4 8.4 %collective-permute-start.4 = (f32[4,2,2560]{2,1,0:T(2,128)S(1)}, f32[4,2,2560]{2,1,0:T(2,128)S(1)}, u32[]{:S(2)}, u32[]{:S(2)}) collective-permute-start(f32[4,2,2560]{2,1,0:T(2,128)S(1)} %get-tuple-element.34), channel_id=1, source_target_pairs={{0,8},{4,12},{8,0},{12,4},{1,9},{5,13},{9,1},{13,5},{2,10},{6,14},... | collective-permute-start | bytes 245768 | tf_op jit(solution)/shard_map/ppermute | solution.py:252
  25.5 8.4 %collective-permute-start.5 = (f32[4,2,2560]{2,1,0:T(2,128)S(1)}, f32[4,2,2560]{2,1,0:T(2,128)S(1)}, u32[]{:S(2)}, u32[]{:S(2)}) collective-permute-start(f32[4,2,2560]{2,1,0:T(2,128)S(1)} %get-tuple-element.35), channel_id=1, source_target_pairs={{0,4},{4,0},{8,12},{12,8},{1,5},{5,1},{9,13},{13,9},{2,6},{6,2},{1... | collective-permute-start | bytes 245768 | tf_op jit(solution)/shard_map/ppermute | solution.py:252
  33.9 8.8 %slice-start = ((s8[16777216]{0:T(1024)(128)(4,1)}), s8[4194304]{0:T(1024)(128)(4,1)S(1)}, s32[]{:S(2)}) async-start(s8[16777216]{0:T(1024)(128)(4,1)} %bitcast.2), calls=%async_computation.1 | async-start | bytes 8388608
  34.7 8.0 %slice-start.1 = ((s8[16777216]{0:T(1024)(128)(4,1)}), s8[4194304]{0:T(1024)(128)(4,1)S(1)}, s32[]{:S(2)}) async-start(s8[16777216]{0:T(1024)(128)(4,1)} %bitcast.2), calls=%async_computation.2 | async-start | bytes 8388608
  34.7 8.0 %slice-start.2 = ((s8[16777216]{0:T(1024)(128)(4,1)}), s8[4194304]{0:T(1024)(128)(4,1)S(1)}, s32[]{:S(2)}) async-start(s8[16777216]{0:T(1024)(128)(4,1)} %bitcast.2), calls=%async_computation.3 | async-start | bytes 8388608
  34.7 8.0 %slice-start.3 = ((s8[16777216]{0:T(1024)(128)(4,1)}), s8[4194304]{0:T(1024)(128)(4,1)S(1)}, s32[]{:S(2)}) async-start(s8[16777216]{0:T(1024)(128)(4,1)} %bitcast.2), calls=%async_computation.4 | async-start | bytes 8388608
  36.1 5.1 %collective-permute-start.10 = (bf16[4,2,2048]{2,1,0:T(2,128)(2,1)S(1)}, bf16[4,2,2048]{2,1,0:T(2,128)(2,1)S(1)}, u32[]{:S(2)}, u32[]{:S(2)}) collective-permute-start(bf16[4,2,2048]{2,1,0:T(2,128)(2,1)S(1)} %shard_map.109.refs_0_), channel_id=1, source_target_pairs={{0,8},{4,12},{8,0},{12,4},{1,9},{5,13},{9,1},{13,5},{2,10},{6,14},... | collective-permute-start | bytes 98312 | tf_op jit(solution)/shard_map/ppermute | solution.py:252
  36.6 5.7 %collective-permute-start.8 = (bf16[4,2,2048]{2,1,0:T(2,128)(2,1)S(1)}, bf16[4,2,2048]{2,1,0:T(2,128)(2,1)S(1)}, u32[]{:S(2)}, u32[]{:S(2)}) collective-permute-start(bf16[4,2,2048]{2,1,0:T(2,128)(2,1)S(1)} %shard_map.109.refs_0_), channel_id=1, source_target_pairs={{0,12},{4,8},{8,4},{12,0},{1,13},{5,9},{9,5},{13,1},{2,14},{6,10},... | collective-permute-start | bytes 98312 | tf_op jit(solution)/shard_map/ppermute | solution.py:252
  38.5 4.2 %collective-permute-start.9 = (bf16[4,2,2048]{2,1,0:T(2,128)(2,1)S(1)}, bf16[4,2,2048]{2,1,0:T(2,128)(2,1)S(1)}, u32[]{:S(2)}, u32[]{:S(2)}) collective-permute-start(bf16[4,2,2048]{2,1,0:T(2,128)(2,1)S(1)} %shard_map.109.refs_0_), channel_id=1, source_target_pairs={{0,4},{4,0},{8,12},{12,8},{1,5},{5,1},{9,13},{13,9},{2,6},{6,2},{1... | collective-permute-start | bytes 98312 | tf_op jit(solution)/shard_map/ppermute | solution.py:252
  44.3 2.2 %collective-permute-start.13 = (f32[8,2,2048]{2,1,0:T(2,128)S(1)}, f32[8,2,2048]{2,1,0:T(2,128)S(1)}, u32[]{:S(2)}, u32[]{:S(2)}) collective-permute-start(f32[8,2,2048]{2,1,0:T(2,128)S(1)} %get-tuple-element.44), channel_id=1, source_target_pairs={{0,1},{1,0},{2,3},{3,2},{4,5},{5,4},{6,7},{7,6},{8,9},{9,8},{10,11... | collective-permute-start | bytes 393224 | tf_op jit(solution)/shard_map/ppermute | solution.py:256
  45.9 1.8 %collective-permute-start.11 = (f32[8,2,2048]{2,1,0:T(2,128)S(1)}, f32[8,2,2048]{2,1,0:T(2,128)S(1)}, u32[]{:S(2)}, u32[]{:S(2)}) collective-permute-start(f32[8,2,2048]{2,1,0:T(2,128)S(1)} %get-tuple-element.40), channel_id=1, source_target_pairs={{0,1},{1,0},{2,3},{3,2},{4,5},{5,4},{6,7},{7,6},{8,9},{9,8},{10,11... | collective-permute-start | bytes 393224 | tf_op jit(solution)/shard_map/ppermute | solution.py:256
  46.5 4.7 %collective-permute-start.14 = (f32[4,2,2048]{2,1,0:T(2,128)S(1)}, f32[4,2,2048]{2,1,0:T(2,128)S(1)}, u32[]{:S(2)}, u32[]{:S(2)}) collective-permute-start(f32[4,2,2048]{2,1,0:T(2,128)S(1)} %get-tuple-element.46), channel_id=1, source_target_pairs={{0,2},{1,3},{2,0},{3,1},{4,6},{5,7},{6,4},{7,5},{8,10},{9,11},{10,... | collective-permute-start | bytes 196616 | tf_op jit(solution)/shard_map/ppermute | solution.py:256
  47.7 4.5 %collective-permute-start.12 = (f32[4,2,2048]{2,1,0:T(2,128)S(1)}, f32[4,2,2048]{2,1,0:T(2,128)S(1)}, u32[]{:S(2)}, u32[]{:S(2)}) collective-permute-start(f32[4,2,2048]{2,1,0:T(2,128)S(1)} %get-tuple-element.42), channel_id=1, source_target_pairs={{0,2},{1,3},{2,0},{3,1},{4,6},{5,7},{6,4},{7,5},{8,10},{9,11},{10,... | collective-permute-start | bytes 196616 | tf_op jit(solution)/shard_map/ppermute | solution.py:256
  52.3 4.7 %collective-permute-start.15 = (bf16[2,4096]{1,0:T(2,128)(2,1)S(1)}, bf16[2,4096]{1,0:T(2,128)(2,1)S(1)}, u32[]{:S(2)}, u32[]{:S(2)}) collective-permute-start(bf16[2,4096]{1,0:T(2,128)(2,1)S(1)} %get-tuple-element.47), channel_id=1, source_target_pairs={{0,8},{4,12},{8,0},{12,4},{1,9},{5,13},{9,1},{13,5},{2,10},{6,14},... | collective-permute-start | bytes 49160 | tf_op jit(solution)/shard_map/ppermute | solution.py:252
  53.4 5.5 %collective-permute-start.16 = (bf16[2,4096]{1,0:T(2,128)(2,1)S(1)}, bf16[2,4096]{1,0:T(2,128)(2,1)S(1)}, u32[]{:S(2)}, u32[]{:S(2)}) collective-permute-start(bf16[2,4096]{1,0:T(2,128)(2,1)S(1)} %get-tuple-element.48), channel_id=1, source_target_pairs={{0,12},{4,8},{8,4},{12,0},{1,13},{5,9},{9,5},{13,1},{2,14},{6,10},... | collective-permute-start | bytes 49160 | tf_op jit(solution)/shard_map/ppermute | solution.py:252
  55.6 3.7 %collective-permute-start.17 = (bf16[2,4096]{1,0:T(2,128)(2,1)S(1)}, bf16[2,4096]{1,0:T(2,128)(2,1)S(1)}, u32[]{:S(2)}, u32[]{:S(2)}) collective-permute-start(bf16[2,4096]{1,0:T(2,128)(2,1)S(1)} %get-tuple-element.49), channel_id=1, source_target_pairs={{0,4},{4,0},{8,12},{12,8},{1,5},{5,1},{9,13},{13,9},{2,6},{6,2},{1... | collective-permute-start | bytes 49160 | tf_op jit(solution)/shard_map/ppermute | solution.py:252

commit v22 on v21

--- a/solution.py
+++ b/solution.py
@@ -226,11 +226,13 @@
 
 def total_kernel(parts, *refs):
     sums, blocks = refs[: 2 * parts], refs[2 * parts :]
-    cols = sums[0].shape[-1]
+    at = 0
     for p in range(parts):
+        cols = sums[2 * p].shape[-1]
         for k, block in enumerate(blocks):
             total = sums[2 * p][k] + sums[2 * p + 1][k]
-            block[:, p * cols : (p + 1) * cols] = total.astype(jnp.bfloat16)
+            block[:, at : at + cols] = total.astype(jnp.bfloat16)
+        at += cols
 
 
 def finish_kernel(*refs):
@@ -388,21 +390,21 @@
         compiler_params=params(8),
     )(*attended)
     head_rows = swap_wide([attended] * wide)
-    parts = 2
+    widths = (out_cols // 2, out_cols // 4, out_cols // 4)
     order = [0, *sequence(wide)[1:], sequence(wide)[0]]
-    part_cols = out_cols // parts
     sums = []
-    for p in range(parts):
+    for p, part_cols in enumerate(widths):
         count = owners // 2
+        behind = sums[:1] if p == len(widths) - 1 else []
         shape = jax.ShapeDtypeStruct((count, rows, part_cols), jnp.float32)
         keep, give = pl.pallas_call(
-            functools.partial(output_kernel, p * part_cols, part_cols, order),
+            functools.partial(output_kernel, sum(widths[:p]), part_cols, order),
             out_shape=(shape, shape),
-            in_specs=[IN_VMEM] * (1 + wide),
+            in_specs=[IN_VMEM] * (1 + wide) + [ANYWHERE] * len(behind),
             out_specs=(IN_VMEM, IN_VMEM),
             compiler_params=params(8),
             cost_estimate=cost(2 * owners * rows * depth * part_cols, 2 * depth * part_cols),
-        )(out_weight, *[head_rows[k] for k in order])
+        )(out_weight, *[head_rows[k] for k in order], *behind)
         give = swap_plane(give, 1)
         step = 2
         while step < plane:
@@ -419,7 +421,7 @@
             step *= 2
         sums += [keep, give]
     blocks = pl.pallas_call(
-        functools.partial(total_kernel, parts),
+        functools.partial(total_kernel, len(widths)),
         out_shape=[jax.ShapeDtypeStruct((rows, out_cols), jnp.bfloat16)] * wide,
         in_specs=[IN_VMEM] * len(sums),
         out_specs=[IN_VMEM] * wide,

time: 60.2 us -> 60.8 us (level)
  starting transfers between devices: 19.5 us -> 20.8 us
  waiting for transfers between devices: 16 us -> 15.3 us
    ppermute x8 -> x10, starting transfers between devices: 7.55 us -> 8.81 us  [swap_plane(): lax.ppermute(value, PLANE, [(i, i ^ step) for i in range(lax.axis_size(PL...]
    ppermute x8 -> x10, waiting for transfers between devices: 4.12 us -> 3.36 us  [swap_plane(): lax.ppermute(value, PLANE, [(i, i ^ step) for i in range(lax.axis_size(PL...]
    pallas_call x3 -> x4, Pallas kernels: 3.15 us -> 3.27 us  [the longest x3 3.21 us: shards(): pl.pallas_call(functools.partial(output_kernel, sum(widths[:p]), part_col...]
  transfers between devices with their start and end apart: 18 -> 20, of which waited for: 11 -> 11; matrix products, arithmetic and copies ran while one was open for 0% -> 0% of each run, Pallas kernels for 11% -> 11%
where the time goes in v22:
time: 60.8 us; the launch traced here: 60.6 us
  starting transfers between devices  20.8 us (34%)
  waiting for transfers between devices  15.3 us (25%)
  blocking collectives  13 us (21%)
  Pallas kernels  10.1 us (17%)
  local copies, waits for them, and re-layouts  1.27 us (2%)
    all_to_all x1, blocking collectives, swap_blocks(): return lax.all_to_all(blocks, axes, split_axis=0, concat_axis=0, tiled=True)  13 us
    ppermute x10, starting transfers between devices, swap_pairs(): lax.ppermute(value, axis, [(i, i ^ step) for i in range(lax.axis_size(axi...  12 us
    ppermute x10, waiting for transfers between devices, swap_pairs(): lax.ppermute(value, axis, [(i, i ^ step) for i in range(lax.axis_size(axi...  11.9 us
    ppermute x10, starting transfers between devices, swap_plane(): lax.ppermute(value, PLANE, [(i, i ^ step) for i in range(lax.axis_size(PL...  8.81 us
    ppermute x10, waiting for transfers between devices, swap_plane(): lax.ppermute(value, PLANE, [(i, i ^ step) for i in range(lax.axis_size(PL...  3.36 us
    pallas_call x3, Pallas kernels, shards(): pl.pallas_call(functools.partial(output_kernel, sum(widths[:p]), part_col...  3.21 us
    pallas_call x1, Pallas kernels, shards(): pl.pallas_call(functools.partial(project_kernel, False, wide, plane), out...  1.98 us
    pallas_call x1, Pallas kernels, shards(): pl.pallas_call(functools.partial(project_kernel, True, wide, plane), out_...  1.9 us
  transfers between devices with their start and end apart: 20, of which 11 were waited for; matrix products, arithmetic and copies ran while one was open for 0% of the time, Pallas kernels for 11%

profile of v22, /device:TPU:0, one launch (start us, length us, event | category | flops | bytes accessed | tf_op | source)
XLA Modules:
  0.0 60.6 jit_solution(14634652651664479576)
XLA Ops:
  0.0 0.0 copy-start.1
  0.0 0.0 copy-start.2
  0.0 0.0 copy-start.8
  0.0 1.0 %copy-done.8 = bf16[2,16384]{1,0:T(2,128)(2,1)S(1)} copy-done((bf16[2,16384]{1,0:T(2,128)(2,1)S(1)}, bf16[2,16384]{1,0:T(2,128)(2,1)}, u32[]{:S(2)}) %copy-start.8) | copy-done | bytes 65560
  1.0 0.2 shard_map.100.scaled_ref
  1.3 0.1 shard_map.101._
  1.4 0.2 copy-done.4
  1.6 0.2 shard_map.102
  1.8 3.0 %collective-permute-start.1 = (bf16[768,256]{1,0:T(8,128)(2,1)S(1)}, bf16[768,256]{1,0:T(8,128)(2,1)S(1)}, u32[]{:S(2)}, u32[]{:S(2)}) collective-permute-start(bf16[768,256]{1,0:T(8,128)(2,1)S(1)} %get-tuple-element.35), channel_id=1, source_target_pairs={{0,2},{1,3},{2,0},{3,1},{4,6},{5,7},{6,4},{7,5},{8,10},{9,11},{10,... | collective-permute-start | bytes 1179656 | tf_op jit(solution)/shard_map/ppermute | solution.py:258
  4.9 13.0 %all_to_all.5.refs_3_.rows_ref._ = bf16[16,2,2048]{2,1,0:T(2,128)(2,1)S(1)} all-to-all(bf16[16,2,2048]{2,1,0:T(2,128)(2,1)S(1)} %shard_map.101._), channel_id=1, replica_groups=mesh['groups'=2,'gx'=4,'gy'=2,'gz'=2] {'gx','gy','gz'}, dimensions={0} | all-to-all | bytes 262144 | tf_op jit(solution)/shard_map/all_to_all | solution.py:250
  17.8 0.0 collective-permute-done.1.refs_4_
  17.8 0.0 collective-permute-start.2
  17.8 0.1 collective-permute-start.7
  17.9 0.4 collective-permute-start
  18.3 1.7 %collective-permute-start.6 = (bf16[272,256]{1,0:T(8,128)(2,1)S(1)}, bf16[272,256]{1,0:T(8,128)(2,1)S(1)}, u32[]{:S(2)}, u32[]{:S(2)}) collective-permute-start(bf16[272,256]{1,0:T(8,128)(2,1)S(1)} %get-tuple-element.41), channel_id=1, source_target_pairs={{0,2},{1,3},{2,0},{3,1},{4,6},{5,7},{6,4},{7,5},{8,10},{9,11},{10,... | collective-permute-start | bytes 417800 | tf_op jit(solution)/shard_map/ppermute | solution.py:258
  20.0 0.0 copy-done
  20.0 1.9 %shard_map.104.refs_1_ = f32[32,2560]{1,0:T(8,128)S(1)} custom-call(bf16[16,2,2048]{2,1,0:T(2,128)(2,1)S(1)} %all_to_all.5.refs_3_.rows_ref._, bf16[4096,2048]{1,0:T(8,128)(2,1)S(1)} %copy-done, bf16[4096,256]{1,0:T(8,128)(2,1)S(1)} %copy-done.1, bf16[4096,256]{1,0:T(8,128)(2,1)S(1)} %copy-done.2), custom_call_target="tpu_custom_call" | custom-call | flops 335544320 | bytes 10485760 | tf_op jit(solution)/shard_map/pallas_call | solution.py:350
  21.9 0.0 collective-permute-done.rows_ref
  22.0 0.0 collective-permute-done.2.refs_0_.refs_5_.refs_7_
  22.0 2.0 %shard_map.105 = (f32[4,2,2560]{2,1,0:T(2,128)S(1)}, f32[4,2,2560]{2,1,0:T(2,128)S(1)}, f32[4,2,2560]{2,1,0:T(2,128)S(1)}, f32[4,2,2560]{2,1,0:T(2,128)S(1)}) custom-call(bf16[16,2,2048]{2,1,0:T(2,128)(2,1)S(1)} %collective-permute-done.rows_ref, bf16[4096,2048]{1,0:T(8,128)(2,1)S(1)} %copy-done, bf16[4096,256]{1,0:T(8,128)(2,1)S(1)} %copy-done.1, ...), custom_call_target="tpu_custom_call" | custom-call | flops 335544320 | bytes 10485760 | tf_op jit(solution)/shard_map/pallas_call | solution.py:358
  24.0 1.5 %collective-permute-start.3 = (f32[4,2,2560]{2,1,0:T(2,128)S(1)}, f32[4,2,2560]{2,1,0:T(2,128)S(1)}, u32[]{:S(2)}, u32[]{:S(2)}) collective-permute-start(f32[4,2,2560]{2,1,0:T(2,128)S(1)} %get-tuple-element.37), channel_id=1, source_target_pairs={{0,12},{4,8},{8,4},{12,0},{1,13},{5,9},{9,5},{13,1},{2,14},{6,10},... | collective-permute-start | bytes 245768 | tf_op jit(solution)/shard_map/ppermute | solution.py:254
  25.4 0.0 collective-permute-start.4
  25.5 3.0 %collective-permute-start.5 = (f32[4,2,2560]{2,1,0:T(2,128)S(1)}, f32[4,2,2560]{2,1,0:T(2,128)S(1)}, u32[]{:S(2)}, u32[]{:S(2)}) collective-permute-start(f32[4,2,2560]{2,1,0:T(2,128)S(1)} %get-tuple-element.39), channel_id=1, source_target_pairs={{0,4},{4,0},{8,12},{12,8},{1,5},{5,1},{9,13},{13,9},{2,6},{6,2},{1... | collective-permute-start | bytes 245768 | tf_op jit(solution)/shard_map/ppermute | solution.py:254
  28.4 0.1 shard_map.106.refs_4_.refs_6_
  28.5 2.7 %collective-permute-done.3.refs_0_ = f32[4,2,2560]{2,1,0:T(2,128)S(1)} collective-permute-done((f32[4,2,2560]{2,1,0:T(2,128)S(1)}, f32[4,2,2560]{2,1,0:T(2,128)S(1)}, u32[]{:S(2)}, u32[]{:S(2)}) %collective-permute-start.3) | collective-permute-done | bytes 81952 | tf_op jit(solution)/shard_map/ppermute | solution.py:254
  31.2 2.6 %collective-permute-done.4.refs_1_ = f32[4,2,2560]{2,1,0:T(2,128)S(1)} collective-permute-done((f32[4,2,2560]{2,1,0:T(2,128)S(1)}, f32[4,2,2560]{2,1,0:T(2,128)S(1)}, u32[]{:S(2)}, u32[]{:S(2)}) %collective-permute-start.4) | collective-permute-done | bytes 81952 | tf_op jit(solution)/shard_map/ppermute | solution.py:254
  33.8 0.0 collective-permute-done.5.refs_2_
  33.9 0.8 %shard_map.107.refs_0_ = bf16[2,2,2048]{2,1,0:T(2,128)(2,1)S(1)} custom-call(f32[1,128]{1,0:T(1,128)S(1)} %copy-done.7, f32[4,2,2560]{2,1,0:T(2,128)S(1)} %collective-permute-done.3.refs_0_, f32[4,2,2560]{2,1,0:T(2,128)S(1)} %collective-permute-done.4.refs_1_, f32[4,2,2560]{2,1,0:T(2,128)S(1)} %collective-permute-done.5.refs_2_, ...), custom_call_target="tpu_custom_call" | custom-call | flops 1 | bytes 1 | tf_op jit(solution)/shard_map/pallas_call | solution.py:376
  34.7 0.0 slice-start.1
  34.7 0.0 slice-start.2
  34.7 0.0 slice-start.3
  34.7 0.5 collective-permute-done.6.refs_5_
  35.3 0.0 collective-permute-done.7.refs_8_
  35.3 0.8 %shard_map.108.refs_1_ = bf16[2,2,2048]{2,1,0:T(2,128)(2,1)S(1)} custom-call(f32[1,128]{1,0:T(1,128)S(1)} %copy-done.7, f32[4,2,2560]{2,1,0:T(2,128)S(1)} %collective-permute-done.3.refs_0_, f32[4,2,2560]{2,1,0:T(2,128)S(1)} %collective-permute-done.4.refs_1_, f32[4,2,2560]{2,1,0:T(2,128)S(1)} %collective-permute-done.5.refs_2_, ...), custom_call_target="tpu_custom_call" | custom-call | flops 10000000000 | bytes 4194304 | tf_op jit(solution)/shard_map/pallas_call | solution.py:376
  36.1 0.5 collective-permute-start.10
  36.6 1.9 %collective-permute-start.8 = (bf16[4,2,2048]{2,1,0:T(2,128)(2,1)S(1)}, bf16[4,2,2048]{2,1,0:T(2,128)(2,1)S(1)}, u32[]{:S(2)}, u32[]{:S(2)}) collective-permute-start(bf16[4,2,2048]{2,1,0:T(2,128)(2,1)S(1)} %shard_map.109.refs_0_), channel_id=1, source_target_pairs={{0,12},{4,8},{8,4},{12,0},{1,13},{5,9},{9,5},{13,1},{2,14},{6,10},... | collective-permute-start | bytes 98312 | tf_op jit(solution)/shard_map/ppermute | solution.py:254
  38.5 1.2 %collective-permute-start.9 = (bf16[4,2,2048]{2,1,0:T(2,128)(2,1)S(1)}, bf16[4,2,2048]{2,1,0:T(2,128)(2,1)S(1)}, u32[]{:S(2)}, u32[]{:S(2)}) collective-permute-start(bf16[4,2,2048]{2,1,0:T(2,128)(2,1)S(1)} %shard_map.109.refs_0_), channel_id=1, source_target_pairs={{0,4},{4,0},{8,12},{12,8},{1,5},{5,1},{9,13},{13,9},{2,6},{6,2},{1... | collective-permute-start | bytes 98312 | tf_op jit(solution)/shard_map/ppermute | solution.py:254
  39.7 1.5 %collective-permute-done.10.refs_3_ = bf16[4,2,2048]{2,1,0:T(2,128)(2,1)S(1)} collective-permute-done((bf16[4,2,2048]{2,1,0:T(2,128)(2,1)S(1)}, bf16[4,2,2048]{2,1,0:T(2,128)(2,1)S(1)}, u32[]{:S(2)}, u32[]{:S(2)}) %collective-permute-start.10) | collective-permute-done | bytes 32800 | tf_op jit(solution)/shard_map/ppermute | solution.py:254
  41.2 1.1 %collective-permute-done.8.refs_1_ = bf16[4,2,2048]{2,1,0:T(2,128)(2,1)S(1)} collective-permute-done((bf16[4,2,2048]{2,1,0:T(2,128)(2,1)S(1)}, bf16[4,2,2048]{2,1,0:T(2,128)(2,1)S(1)}, u32[]{:S(2)}, u32[]{:S(2)}) %collective-permute-start.8) | collective-permute-done | bytes 32800 | tf_op jit(solution)/shard_map/ppermute | solution.py:254
  42.3 0.3 collective-permute-done.9.refs_2_
  42.7 0.0 slice-done.3
  42.7 1.5 %shard_map.110 = (f32[8,2,2048]{2,1,0:T(2,128)S(1)}, f32[8,2,2048]{2,1,0:T(2,128)S(1)}) custom-call(bf16[2048,4096]{1,0:T(8,128)(2,1)S(1)} %bitcast.3, bf16[4,2,2048]{2,1,0:T(2,128)(2,1)S(1)} %shard_map.109.refs_0_, bf16[4,2,2048]{2,1,0:T(2,128)(2,1)S(1)} %collective-permute-done.8.refs_1_, bf16[4,2,2048]{2,1,0:T(2,128)(2,1)S(1)} %collective-permute-done.9.refs_2_, ...), custom_call_target="tpu_custom_call" | custom-call | flops 268435456 | bytes 8388608 | tf_op jit(solution)/shard_map/pallas_call | solution.py:400
  44.3 0.1 collective-permute-start.11
  44.3 0.8 %shard_map.112 = (f32[8,2,1024]{2,1,0:T(2,128)S(1)}, f32[8,2,1024]{2,1,0:T(2,128)S(1)}) custom-call(bf16[2048,4096]{1,0:T(8,128)(2,1)S(1)} %bitcast.3, bf16[4,2,2048]{2,1,0:T(2,128)(2,1)S(1)} %shard_map.109.refs_0_, bf16[4,2,2048]{2,1,0:T(2,128)(2,1)S(1)} %collective-permute-done.8.refs_1_, bf16[4,2,2048]{2,1,0:T(2,128)(2,1)S(1)} %collective-permute-done.9.refs_2_, ...), custom_call_target="tpu_custom_call" | custom-call | flops 134217728 | bytes 4194304 | tf_op jit(solution)/shard_map/pallas_call | solution.py:400
  45.2 0.6 collective-permute-start.13
  45.7 0.0 collective-permute-done.11.b_ref
  45.8 0.8 %shard_map.114 = (f32[8,2,1024]{2,1,0:T(2,128)S(1)}, f32[8,2,1024]{2,1,0:T(2,128)S(1)}) custom-call(bf16[2048,4096]{1,0:T(8,128)(2,1)S(1)} %bitcast.3, bf16[4,2,2048]{2,1,0:T(2,128)(2,1)S(1)} %shard_map.109.refs_0_, bf16[4,2,2048]{2,1,0:T(2,128)(2,1)S(1)} %collective-permute-done.8.refs_1_, bf16[4,2,2048]{2,1,0:T(2,128)(2,1)S(1)} %collective-permute-done.9.refs_2_, ...), custom_call_target="tpu_custom_call" | custom-call | flops 134217728 | bytes 4194304 | tf_op jit(solution)/shard_map/pallas_call | solution.py:400
  46.6 0.1 collective-permute-start.15
  46.7 1.1 %collective-permute-start.12 = (f32[4,2,2048]{2,1,0:T(2,128)S(1)}, f32[4,2,2048]{2,1,0:T(2,128)S(1)}, u32[]{:S(2)}, u32[]{:S(2)}) collective-permute-start(f32[4,2,2048]{2,1,0:T(2,128)S(1)} %get-tuple-element.46), channel_id=1, source_target_pairs={{0,2},{1,3},{2,0},{3,1},{4,6},{5,7},{6,4},{7,5},{8,10},{9,11},{10,... | collective-permute-start | bytes 196616 | tf_op jit(solution)/shard_map/ppermute | solution.py:258
  47.9 0.0 collective-permute-done.13.b_ref
  47.9 1.0 %collective-permute-start.14 = (f32[4,2,1024]{2,1,0:T(2,128)S(1)}, f32[4,2,1024]{2,1,0:T(2,128)S(1)}, u32[]{:S(2)}, u32[]{:S(2)}) collective-permute-start(f32[4,2,1024]{2,1,0:T(2,128)S(1)} %get-tuple-element.50), channel_id=1, source_target_pairs={{0,2},{1,3},{2,0},{3,1},{4,6},{5,7},{6,4},{7,5},{8,10},{9,11},{10,... | collective-permute-start | bytes 98312 | tf_op jit(solution)/shard_map/ppermute | solution.py:258
  48.9 0.0 collective-permute-done.15.b_ref
  48.9 1.2 %collective-permute-start.16 = (f32[4,2,1024]{2,1,0:T(2,128)S(1)}, f32[4,2,1024]{2,1,0:T(2,128)S(1)}, u32[]{:S(2)}, u32[]{:S(2)}) collective-permute-start(f32[4,2,1024]{2,1,0:T(2,128)S(1)} %get-tuple-element.54), channel_id=1, source_target_pairs={{0,2},{1,3},{2,0},{3,1},{4,6},{5,7},{6,4},{7,5},{8,10},{9,11},{10,... | collective-permute-start | bytes 98312 | tf_op jit(solution)/shard_map/ppermute | solution.py:258
  50.1 2.2 %collective-permute-done.14.refs_3_ = f32[4,2,1024]{2,1,0:T(2,128)S(1)} collective-permute-done((f32[4,2,1024]{2,1,0:T(2,128)S(1)}, f32[4,2,1024]{2,1,0:T(2,128)S(1)}, u32[]{:S(2)}, u32[]{:S(2)}) %collective-permute-start.14) | collective-permute-done | bytes 32800 | tf_op jit(solution)/shard_map/ppermute | solution.py:258
  52.2 0.0 collective-permute-done.12.refs_1_
  52.2 0.6 collective-permute-done.16.refs_5_
  52.9 0.1 shard_map.116
  52.9 0.9 %collective-permute-start.17 = (bf16[2,4096]{1,0:T(2,128)(2,1)S(1)}, bf16[2,4096]{1,0:T(2,128)(2,1)S(1)}, u32[]{:S(2)}, u32[]{:S(2)}) collective-permute-start(bf16[2,4096]{1,0:T(2,128)(2,1)S(1)} %get-tuple-element.55), channel_id=1, source_target_pairs={{0,8},{4,12},{8,0},{12,4},{1,9},{5,13},{9,1},{13,5},{2,10},{6,14},... | collective-permute-start | bytes 49160 | tf_op jit(solution)/shard_map/ppermute | solution.py:254
  53.8 2.4 %collective-permute-start.18 = (bf16[2,4096]{1,0:T(2,128)(2,1)S(1)}, bf16[2,4096]{1,0:T(2,128)(2,1)S(1)}, u32[]{:S(2)}, u32[]{:S(2)}) collective-permute-start(bf16[2,4096]{1,0:T(2,128)(2,1)S(1)} %get-tuple-element.56), channel_id=1, source_target_pairs={{0,12},{4,8},{8,4},{12,0},{1,13},{5,9},{9,5},{13,1},{2,14},{6,10},... | collective-permute-start | bytes 49160 | tf_op jit(solution)/shard_map/ppermute | solution.py:254
  56.3 0.2 collective-permute-start.19
  56.5 1.1 %collective-permute-done.17.refs_0_ = bf16[2,4096]{1,0:T(2,128)(2,1)S(1)} collective-permute-done((bf16[2,4096]{1,0:T(2,128)(2,1)S(1)}, bf16[2,4096]{1,0:T(2,128)(2,1)S(1)}, u32[]{:S(2)}, u32[]{:S(2)}) %collective-permute-start.17) | collective-permute-done | bytes 16416 | tf_op jit(solution)/shard_map/ppermute | solution.py:254
  57.6 1.8 %collective-permute-done.18.refs_1_ = bf16[2,4096]{1,0:T(2,128)(2,1)S(1)} collective-permute-done((bf16[2,4096]{1,0:T(2,128)(2,1)S(1)}, bf16[2,4096]{1,0:T(2,128)(2,1)S(1)}, u32[]{:S(2)}, u32[]{:S(2)}) %collective-permute-start.18) | collective-permute-done | bytes 16416 | tf_op jit(solution)/shard_map/ppermute | solution.py:254
  59.4 0.6 %collective-permute-done.19.refs_2_ = bf16[2,4096]{1,0:T(2,128)(2,1)S(1)} collective-permute-done((bf16[2,4096]{1,0:T(2,128)(2,1)S(1)}, bf16[2,4096]{1,0:T(2,128)(2,1)S(1)}, u32[]{:S(2)}, u32[]{:S(2)}) %collective-permute-start.19) | collective-permute-done | bytes 16416 | tf_op jit(solution)/shard_map/ppermute | solution.py:254
  60.0 0.6 %shard_map.117 = bf16[2,16384]{1,0:T(2,128)(2,1)} custom-call(bf16[2,4096]{1,0:T(2,128)(2,1)S(1)} %collective-permute-done.17.refs_0_, bf16[2,4096]{1,0:T(2,128)(2,1)S(1)} %collective-permute-done.18.refs_1_, bf16[2,4096]{1,0:T(2,128)(2,1)S(1)} %collective-permute-done.19.refs_2_, bf16[2,4096]{1,0:T(2,128)(2,1)S(1)} %get-tuple-element.58.refs_3_), custom_call_target="tpu_custom_call" | custom-call | tf_op jit(solution)/shard_map/pallas_call | solution.py:431
  (22 shorter events, 0.1 us)
Async XLA Ops:
  0.0 1.3 %copy-start.5 = (f32[16384]{0:T(1024)S(1)}, f32[16384]{0:T(1024)}, u32[]{:S(2)}) copy-start(f32[16384]{0:T(1024)} %param.11) | copy-start | bytes 196612
  0.0 1.4 %copy-start.6 = (s32[2]{0:T(128)S(1)}, s32[2]{0:T(128)}, u32[]{:S(2)}) copy-start(s32[2]{0:T(128)} %param.18) | copy-start | bytes 28
  0.0 1.4 %copy-start.3 = (bf16[2,256,1024]{2,1,0:T(8,128)(2,1)S(1)}, bf16[2,256,1024]{2,1,0:T(8,128)(2,1)}, u32[]{:S(2)}) copy-start(bf16[2,256,1024]{2,1,0:T(8,128)(2,1)} %keys_ref.3) | copy-start | bytes 3145732
  0.0 1.6 %copy-start.4 = (bf16[2,256,1024]{2,1,0:T(8,128)(2,1)S(1)}, bf16[2,256,1024]{2,1,0:T(8,128)(2,1)}, u32[]{:S(2)}) copy-start(bf16[2,256,1024]{2,1,0:T(8,128)(2,1)} %values_ref.3) | copy-start | bytes 3145732
  0.0 20.0 %copy-start = (bf16[4096,2048]{1,0:T(8,128)(2,1)S(1)}, bf16[4096,2048]{1,0:T(8,128)(2,1)}, u32[]{:S(2)}) copy-start(bf16[4096,2048]{1,0:T(8,128)(2,1)} %query_ref.3) | copy-start | bytes 50331652
  0.0 20.0 %copy-start.1 = (bf16[4096,256]{1,0:T(8,128)(2,1)S(1)}, bf16[4096,256]{1,0:T(8,128)(2,1)}, u32[]{:S(2)}) copy-start(bf16[4096,256]{1,0:T(8,128)(2,1)} %key_ref.3) | copy-start | bytes 6291460
  0.0 20.0 %copy-start.2 = (bf16[4096,256]{1,0:T(8,128)(2,1)S(1)}, bf16[4096,256]{1,0:T(8,128)(2,1)}, u32[]{:S(2)}) copy-start(bf16[4096,256]{1,0:T(8,128)(2,1)} %value_ref.3) | copy-start | bytes 6291460
  0.0 1.0 %copy-start.8 = (bf16[2,16384]{1,0:T(2,128)(2,1)S(1)}, bf16[2,16384]{1,0:T(2,128)(2,1)}, u32[]{:S(2)}) copy-start(bf16[2,16384]{1,0:T(2,128)(2,1)} %tokens_ref.1) | copy-start | bytes 196612
  1.8 16.0 %collective-permute-start.1 = (bf16[768,256]{1,0:T(8,128)(2,1)S(1)}, bf16[768,256]{1,0:T(8,128)(2,1)S(1)}, u32[]{:S(2)}, u32[]{:S(2)}) collective-permute-start(bf16[768,256]{1,0:T(8,128)(2,1)S(1)} %get-tuple-element.35), channel_id=1, source_target_pairs={{0,2},{1,3},{2,0},{3,1},{4,6},{5,7},{6,4},{7,5},{8,10},{9,11},{10,... | collective-permute-start | bytes 1179656 | tf_op jit(solution)/shard_map/ppermute | solution.py:258
  17.8 4.1 %collective-permute-start.2 = (bf16[1040,256]{1,0:T(8,128)(2,1)S(1)}, bf16[1040,256]{1,0:T(8,128)(2,1)S(1)}, u32[]{:S(2)}, u32[]{:S(2)}) collective-permute-start(bf16[1040,256]{1,0:T(8,128)(2,1)S(1)} %get-tuple-element.36), channel_id=1, source_target_pairs={{0,1},{1,0},{2,3},{3,2},{4,5},{5,4},{6,7},{7,6},{8,9},{9,8},{10,11... | collective-permute-start | bytes 1597448 | tf_op jit(solution)/shard_map/ppermute | solution.py:258
  17.8 17.4 %collective-permute-start.7 = (bf16[1040,256]{1,0:T(8,128)(2,1)S(1)}, bf16[1040,256]{1,0:T(8,128)(2,1)S(1)}, u32[]{:S(2)}, u32[]{:S(2)}) collective-permute-start(bf16[1040,256]{1,0:T(8,128)(2,1)S(1)} %get-tuple-element.42), channel_id=1, source_target_pairs={{0,3},{1,2},{2,1},{3,0},{4,7},{5,6},{6,5},{7,4},{8,11},{9,10},{10,... | collective-permute-start | bytes 1597448 | tf_op jit(solution)/shard_map/ppermute | solution.py:258
  17.9 4.0 %collective-permute-start = (bf16[16,2,2048]{2,1,0:T(2,128)(2,1)S(1)}, bf16[16,2,2048]{2,1,0:T(2,128)(2,1)S(1)}, u32[]{:S(2)}, u32[]{:S(2)}) collective-permute-start(bf16[16,2,2048]{2,1,0:T(2,128)(2,1)S(1)} %all_to_all.5.refs_3_.rows_ref._), channel_id=1, source_target_pairs={{0,1},{1,0},{2,3},{3,2},{4,5},{5,4},{6,7},{7,6},{8,9},{9,8},{10,11... | collective-permute-start | bytes 393224 | tf_op jit(solution)/shard_map/ppermute | solution.py:254
  18.3 16.9 %collective-permute-start.6 = (bf16[272,256]{1,0:T(8,128)(2,1)S(1)}, bf16[272,256]{1,0:T(8,128)(2,1)S(1)}, u32[]{:S(2)}, u32[]{:S(2)}) collective-permute-start(bf16[272,256]{1,0:T(8,128)(2,1)S(1)} %get-tuple-element.41), channel_id=1, source_target_pairs={{0,2},{1,3},{2,0},{3,1},{4,6},{5,7},{6,4},{7,5},{8,10},{9,11},{10,... | collective-permute-start | bytes 417800 | tf_op jit(solution)/shard_map/ppermute | solution.py:258
  21.9 11.9 %copy-start.7 = (f32[1,128]{1,0:T(1,128)S(1)}, f32[1,128]{1,0:T(1,128)}, u32[]{:S(2)}) copy-start(f32[1,128]{1,0:T(1,128)} %constant.2.clone.frequency_ref) | copy-start | bytes 1540
  24.0 7.3 %collective-permute-start.3 = (f32[4,2,2560]{2,1,0:T(2,128)S(1)}, f32[4,2,2560]{2,1,0:T(2,128)S(1)}, u32[]{:S(2)}, u32[]{:S(2)}) collective-permute-start(f32[4,2,2560]{2,1,0:T(2,128)S(1)} %get-tuple-element.37), channel_id=1, source_target_pairs={{0,12},{4,8},{8,4},{12,0},{1,13},{5,9},{9,5},{13,1},{2,14},{6,10},... | collective-permute-start | bytes 245768 | tf_op jit(solution)/shard_map/ppermute | solution.py:254
  25.4 8.4 %collective-permute-start.4 = (f32[4,2,2560]{2,1,0:T(2,128)S(1)}, f32[4,2,2560]{2,1,0:T(2,128)S(1)}, u32[]{:S(2)}, u32[]{:S(2)}) collective-permute-start(f32[4,2,2560]{2,1,0:T(2,128)S(1)} %get-tuple-element.38), channel_id=1, source_target_pairs={{0,8},{4,12},{8,0},{12,4},{1,9},{5,13},{9,1},{13,5},{2,10},{6,14},... | collective-permute-start | bytes 245768 | tf_op jit(solution)/shard_map/ppermute | solution.py:254
  25.5 8.4 %collective-permute-start.5 = (f32[4,2,2560]{2,1,0:T(2,128)S(1)}, f32[4,2,2560]{2,1,0:T(2,128)S(1)}, u32[]{:S(2)}, u32[]{:S(2)}) collective-permute-start(f32[4,2,2560]{2,1,0:T(2,128)S(1)} %get-tuple-element.39), channel_id=1, source_target_pairs={{0,4},{4,0},{8,12},{12,8},{1,5},{5,1},{9,13},{13,9},{2,6},{6,2},{1... | collective-permute-start | bytes 245768 | tf_op jit(solution)/shard_map/ppermute | solution.py:254
  33.9 8.8 %slice-start = ((s8[16777216]{0:T(1024)(128)(4,1)}), s8[4194304]{0:T(1024)(128)(4,1)S(1)}, s32[]{:S(2)}) async-start(s8[16777216]{0:T(1024)(128)(4,1)} %bitcast.2), calls=%async_computation.1 | async-start | bytes 8388608
  34.7 8.0 %slice-start.1 = ((s8[16777216]{0:T(1024)(128)(4,1)}), s8[4194304]{0:T(1024)(128)(4,1)S(1)}, s32[]{:S(2)}) async-start(s8[16777216]{0:T(1024)(128)(4,1)} %bitcast.2), calls=%async_computation.2 | async-start | bytes 8388608
  34.7 8.0 %slice-start.2 = ((s8[16777216]{0:T(1024)(128)(4,1)}), s8[4194304]{0:T(1024)(128)(4,1)S(1)}, s32[]{:S(2)}) async-start(s8[16777216]{0:T(1024)(128)(4,1)} %bitcast.2), calls=%async_computation.3 | async-start | bytes 8388608
  34.7 8.0 %slice-start.3 = ((s8[16777216]{0:T(1024)(128)(4,1)}), s8[4194304]{0:T(1024)(128)(4,1)S(1)}, s32[]{:S(2)}) async-start(s8[16777216]{0:T(1024)(128)(4,1)} %bitcast.2), calls=%async_computation.4 | async-start | bytes 8388608
  36.1 5.1 %collective-permute-start.10 = (bf16[4,2,2048]{2,1,0:T(2,128)(2,1)S(1)}, bf16[4,2,2048]{2,1,0:T(2,128)(2,1)S(1)}, u32[]{:S(2)}, u32[]{:S(2)}) collective-permute-start(bf16[4,2,2048]{2,1,0:T(2,128)(2,1)S(1)} %shard_map.109.refs_0_), channel_id=1, source_target_pairs={{0,8},{4,12},{8,0},{12,4},{1,9},{5,13},{9,1},{13,5},{2,10},{6,14},... | collective-permute-start | bytes 98312 | tf_op jit(solution)/shard_map/ppermute | solution.py:254
  36.6 5.7 %collective-permute-start.8 = (bf16[4,2,2048]{2,1,0:T(2,128)(2,1)S(1)}, bf16[4,2,2048]{2,1,0:T(2,128)(2,1)S(1)}, u32[]{:S(2)}, u32[]{:S(2)}) collective-permute-start(bf16[4,2,2048]{2,1,0:T(2,128)(2,1)S(1)} %shard_map.109.refs_0_), channel_id=1, source_target_pairs={{0,12},{4,8},{8,4},{12,0},{1,13},{5,9},{9,5},{13,1},{2,14},{6,10},... | collective-permute-start | bytes 98312 | tf_op jit(solution)/shard_map/ppermute | solution.py:254
  38.5 4.2 %collective-permute-start.9 = (bf16[4,2,2048]{2,1,0:T(2,128)(2,1)S(1)}, bf16[4,2,2048]{2,1,0:T(2,128)(2,1)S(1)}, u32[]{:S(2)}, u32[]{:S(2)}) collective-permute-start(bf16[4,2,2048]{2,1,0:T(2,128)(2,1)S(1)} %shard_map.109.refs_0_), channel_id=1, source_target_pairs={{0,4},{4,0},{8,12},{12,8},{1,5},{5,1},{9,13},{13,9},{2,6},{6,2},{1... | collective-permute-start | bytes 98312 | tf_op jit(solution)/shard_map/ppermute | solution.py:254
  44.3 1.5 %collective-permute-start.11 = (f32[8,2,2048]{2,1,0:T(2,128)S(1)}, f32[8,2,2048]{2,1,0:T(2,128)S(1)}, u32[]{:S(2)}, u32[]{:S(2)}) collective-permute-start(f32[8,2,2048]{2,1,0:T(2,128)S(1)} %get-tuple-element.44), channel_id=1, source_target_pairs={{0,1},{1,0},{2,3},{3,2},{4,5},{5,4},{6,7},{7,6},{8,9},{9,8},{10,11... | collective-permute-start | bytes 393224 | tf_op jit(solution)/shard_map/ppermute | solution.py:258
  45.2 2.7 %collective-permute-start.13 = (f32[8,2,1024]{2,1,0:T(2,128)S(1)}, f32[8,2,1024]{2,1,0:T(2,128)S(1)}, u32[]{:S(2)}, u32[]{:S(2)}) collective-permute-start(f32[8,2,1024]{2,1,0:T(2,128)S(1)} %get-tuple-element.48), channel_id=1, source_target_pairs={{0,1},{1,0},{2,3},{3,2},{4,5},{5,4},{6,7},{7,6},{8,9},{9,8},{10,11... | collective-permute-start | bytes 196616 | tf_op jit(solution)/shard_map/ppermute | solution.py:258
  46.6 2.3 %collective-permute-start.15 = (f32[8,2,1024]{2,1,0:T(2,128)S(1)}, f32[8,2,1024]{2,1,0:T(2,128)S(1)}, u32[]{:S(2)}, u32[]{:S(2)}) collective-permute-start(f32[8,2,1024]{2,1,0:T(2,128)S(1)} %get-tuple-element.52), channel_id=1, source_target_pairs={{0,1},{1,0},{2,3},{3,2},{4,5},{5,4},{6,7},{7,6},{8,9},{9,8},{10,11... | collective-permute-start | bytes 196616 | tf_op jit(solution)/shard_map/ppermute | solution.py:258
  46.7 5.5 %collective-permute-start.12 = (f32[4,2,2048]{2,1,0:T(2,128)S(1)}, f32[4,2,2048]{2,1,0:T(2,128)S(1)}, u32[]{:S(2)}, u32[]{:S(2)}) collective-permute-start(f32[4,2,2048]{2,1,0:T(2,128)S(1)} %get-tuple-element.46), channel_id=1, source_target_pairs={{0,2},{1,3},{2,0},{3,1},{4,6},{5,7},{6,4},{7,5},{8,10},{9,11},{10,... | collective-permute-start | bytes 196616 | tf_op jit(solution)/shard_map/ppermute | solution.py:258
  47.9 4.4 %collective-permute-start.14 = (f32[4,2,1024]{2,1,0:T(2,128)S(1)}, f32[4,2,1024]{2,1,0:T(2,128)S(1)}, u32[]{:S(2)}, u32[]{:S(2)}) collective-permute-start(f32[4,2,1024]{2,1,0:T(2,128)S(1)} %get-tuple-element.50), channel_id=1, source_target_pairs={{0,2},{1,3},{2,0},{3,1},{4,6},{5,7},{6,4},{7,5},{8,10},{9,11},{10,... | collective-permute-start | bytes 98312 | tf_op jit(solution)/shard_map/ppermute | solution.py:258
  48.9 4.0 %collective-permute-start.16 = (f32[4,2,1024]{2,1,0:T(2,128)S(1)}, f32[4,2,1024]{2,1,0:T(2,128)S(1)}, u32[]{:S(2)}, u32[]{:S(2)}) collective-permute-start(f32[4,2,1024]{2,1,0:T(2,128)S(1)} %get-tuple-element.54), channel_id=1, source_target_pairs={{0,2},{1,3},{2,0},{3,1},{4,6},{5,7},{6,4},{7,5},{8,10},{9,11},{10,... | collective-permute-start | bytes 98312 | tf_op jit(solution)/shard_map/ppermute | solution.py:258
  52.9 4.7 %collective-permute-start.17 = (bf16[2,4096]{1,0:T(2,128)(2,1)S(1)}, bf16[2,4096]{1,0:T(2,128)(2,1)S(1)}, u32[]{:S(2)}, u32[]{:S(2)}) collective-permute-start(bf16[2,4096]{1,0:T(2,128)(2,1)S(1)} %get-tuple-element.55), channel_id=1, source_target_pairs={{0,8},{4,12},{8,0},{12,4},{1,9},{5,13},{9,1},{13,5},{2,10},{6,14},... | collective-permute-start | bytes 49160 | tf_op jit(solution)/shard_map/ppermute | solution.py:254
  53.8 5.5 %collective-permute-start.18 = (bf16[2,4096]{1,0:T(2,128)(2,1)S(1)}, bf16[2,4096]{1,0:T(2,128)(2,1)S(1)}, u32[]{:S(2)}, u32[]{:S(2)}) collective-permute-start(bf16[2,4096]{1,0:T(2,128)(2,1)S(1)} %get-tuple-element.56), channel_id=1, source_target_pairs={{0,12},{4,8},{8,4},{12,0},{1,13},{5,9},{9,5},{13,1},{2,14},{6,10},... | collective-permute-start | bytes 49160 | tf_op jit(solution)/shard_map/ppermute | solution.py:254
  56.3 3.7 %collective-permute-start.19 = (bf16[2,4096]{1,0:T(2,128)(2,1)S(1)}, bf16[2,4096]{1,0:T(2,128)(2,1)S(1)}, u32[]{:S(2)}, u32[]{:S(2)}) collective-permute-start(bf16[2,4096]{1,0:T(2,128)(2,1)S(1)} %get-tuple-element.57), channel_id=1, source_target_pairs={{0,4},{4,0},{8,12},{12,8},{1,5},{5,1},{9,13},{13,9},{2,6},{6,2},{1... | collective-permute-start | bytes 49160 | tf_op jit(solution)/shard_map/ppermute | solution.py:254

commit v23 on v21

--- a/solution.py
+++ b/solution.py
@@ -78,17 +78,16 @@
 
 
 def cut_kernel(plan, lengths_ref, keys_ref, values_ref, _, *blocks):
-    rows, slots, _ = keys_ref.shape
     cols = blocks[0].shape[1]
-    for (slot, key_rows, value_rows, with_lengths), block in zip(plan, blocks):
+    for (slot, keys, values, with_lengths), block in zip(plan, blocks):
         at = pl.multiple_of((own_place() ^ slot) * cols, cols)
         start = 0
-        for cache_ref, wanted in ((keys_ref, key_rows), (values_ref, value_rows)):
-            for r in wanted:
-                block[start : start + slots] = cache_ref[r, :, pl.ds(at, cols)]
-                start += slots
+        for cache_ref, wanted in ((keys_ref, keys), (values_ref, values)):
+            for r, low, high in wanted:
+                block[start : start + high - low] = cache_ref[r, low:high, pl.ds(at, cols)]
+                start += high - low
         if with_lengths:
-            write_lengths(rows, lengths_ref, block)
+            write_lengths(keys_ref.shape[0], lengths_ref, block)
 
 
 def pass_kernel(*refs):
@@ -117,12 +116,20 @@
         parts = []
         for p in range(pairs):
             l, r = members[p // rows], p % rows
-            ref, at = whole[(l + 1) // 2], values * rows + r
-            if l % 2 == 0 and l:
-                ref = firsts[l // 2 - 1]
-                if at >= rows + early:
-                    ref, at = lasts[l // 2 - 1], at - rows - early
-            parts.append(ref[at * slots : (at + 1) * slots])
+            if l % 2 or l == 0:
+                at = (values * rows + r) * slots
+                parts.append(whole[(l + 1) // 2][at : at + slots])
+                continue
+            first, last = firsts[l // 2 - 1], lasts[l // 2 - 1]
+            at = (values * rows + r) * slots
+            end = (rows + early) * slots + slots // 4
+            if at + slots <= end:
+                parts.append(first[at : at + slots])
+            elif at < end:
+                rest = last[: at + slots - end]
+                parts.append(jnp.concatenate([first[at:end], rest], 0))
+            else:
+                parts.append(last[at - end : at - end + slots])
         return jnp.concatenate(parts, 1)
 
     filled = []
@@ -306,25 +313,28 @@
     slots = cache_keys.shape[1]
     even = plane // 2 - 1
     early = rows // 2
-    every = range(rows)
+    every = [(r, 0, slots) for r in range(rows)]
+    cut_at = slots // 4
 
     def cut(plan, after):
         return pl.pallas_call(
             functools.partial(cut_kernel, plan),
             out_shape=[
                 jax.ShapeDtypeStruct(
-                    ((len(key_rows) + len(value_rows)) * slots + 16 * with_lengths, kv_cols),
+                    (sum(h - g for _, g, h in (*keys, *values)) + 16 * with_lengths, kv_cols),
                     cache_keys.dtype,
                 )
-                for _, key_rows, value_rows, with_lengths in plan
+                for _, keys, values, with_lengths in plan
             ],
             in_specs=[IN_VMEM] * 4,
             out_specs=[IN_VMEM] * len(plan),
             compiler_params=params(8),
         )(lengths.reshape(1, -1), cache_keys, cache_values, after)
 
-    plan = [(l, every, every[:early], False) for l in range(2, plane, 2)]
-    plan += [(l, (), every[early:], True) for l in range(2, plane, 2)]
+    early_values = [*every[:early], (early, 0, cut_at)]
+    late_values = [(early, cut_at, slots), *every[early + 1 :]]
+    plan = [(l, every, early_values, False) for l in range(2, plane, 2)]
+    plan += [(l, (), late_values, True) for l in range(2, plane, 2)]
     plan += [(l, every, every, True) for l in range(1, plane, 2)]
     blocks = cut(plan, normed)
     firsts, rest = blocks[:even], blocks[even:]

time: 60.2 us -> 59.8 us (level)
  waiting for transfers between devices: 16 us -> 15.2 us
    ppermute x8, waiting for transfers between devices: 4.12 us -> 3.37 us  [swap_plane(): lax.ppermute(value, PLANE, [(i, i ^ step) for i in range(lax.axis_size(PL...]
  transfers between devices with their start and end apart: 18 -> 18, of which waited for: 11 -> 9; matrix products, arithmetic and copies ran while one was open for 0% -> 0% of each run, Pallas kernels for 11% -> 11%
where the time goes in v23:
time: 59.8 us; the launch traced here: 59.6 us
  starting transfers between devices  20 us (33%)
  waiting for transfers between devices  15.2 us (25%)
  blocking collectives  13 us (22%)
  Pallas kernels  9.97 us (17%)
  local copies, waits for them, and re-layouts  1.27 us (2%)
    all_to_all x1, blocking collectives, swap_blocks(): return lax.all_to_all(blocks, axes, split_axis=0, concat_axis=0, tiled=True)  13 us
    ppermute x10, starting transfers between devices, swap_pairs(): lax.ppermute(value, axis, [(i, i ^ step) for i in range(lax.axis_size(axi...  12 us
    ppermute x10, waiting for transfers between devices, swap_pairs(): lax.ppermute(value, axis, [(i, i ^ step) for i in range(lax.axis_size(axi...  11.8 us
    ppermute x8, starting transfers between devices, swap_plane(): lax.ppermute(value, PLANE, [(i, i ^ step) for i in range(lax.axis_size(PL...  8.03 us
    ppermute x8, waiting for transfers between devices, swap_plane(): lax.ppermute(value, PLANE, [(i, i ^ step) for i in range(lax.axis_size(PL...  3.37 us
    pallas_call x2, Pallas kernels, shards(): pl.pallas_call(functools.partial(output_kernel, p * part_cols, part_cols,...  3.09 us
    pallas_call x1, Pallas kernels, shards(): pl.pallas_call(functools.partial(project_kernel, False, wide, plane), out...  1.97 us
    pallas_call x1, Pallas kernels, shards(): pl.pallas_call(functools.partial(project_kernel, True, wide, plane), out_...  1.9 us
  transfers between devices with their start and end apart: 18, of which 9 were waited for; matrix products, arithmetic and copies ran while one was open for 0% of the time, Pallas kernels for 11%

profile of v23, /device:TPU:0, one launch (start us, length us, event | category | flops | bytes accessed | tf_op | source)
XLA Modules:
  0.0 59.6 jit_solution(11104705464691530289)
XLA Ops:
  0.0 0.0 copy-start.1
  0.0 0.0 copy-start.2
  0.0 0.0 copy-start.8
  0.0 1.0 %copy-done.8 = bf16[2,16384]{1,0:T(2,128)(2,1)S(1)} copy-done((bf16[2,16384]{1,0:T(2,128)(2,1)S(1)}, bf16[2,16384]{1,0:T(2,128)(2,1)}, u32[]{:S(2)}) %copy-start.8) | copy-done | bytes 65560
  1.0 0.2 shard_map.100.scaled_ref
  1.3 0.0 copy-done.5
  1.3 0.1 shard_map.101._
  1.4 0.0 copy-done.6
  1.4 0.0 copy-done.3
  1.4 0.2 copy-done.4
  1.6 0.2 shard_map.102
  1.8 3.0 %collective-permute-start.1 = (bf16[832,256]{1,0:T(8,128)(2,1)S(1)}, bf16[832,256]{1,0:T(8,128)(2,1)S(1)}, u32[]{:S(2)}, u32[]{:S(2)}) collective-permute-start(bf16[832,256]{1,0:T(8,128)(2,1)S(1)} %get-tuple-element.31), channel_id=1, source_target_pairs={{0,2},{1,3},{2,0},{3,1},{4,6},{5,7},{6,4},{7,5},{8,10},{9,11},{10,... | collective-permute-start | bytes 1277960 | tf_op jit(solution)/shard_map/ppermute | solution.py:263
  4.9 13.0 %all_to_all.5.refs_3_.rows_ref._ = bf16[16,2,2048]{2,1,0:T(2,128)(2,1)S(1)} all-to-all(bf16[16,2,2048]{2,1,0:T(2,128)(2,1)S(1)} %shard_map.101._), channel_id=1, replica_groups=mesh['groups'=2,'gx'=4,'gy'=2,'gz'=2] {'gx','gy','gz'}, dimensions={0} | all-to-all | bytes 262144 | tf_op jit(solution)/shard_map/all_to_all | solution.py:255
  17.8 0.0 collective-permute-done.1.refs_4_
  17.8 0.0 collective-permute-start.2
  17.8 0.1 collective-permute-start.7
  17.9 0.4 collective-permute-start
  18.3 0.0 copy-done
  18.3 0.0 copy-done.1
  18.3 0.0 copy-done.2
  18.4 1.9 %shard_map.104.refs_1_ = f32[32,2560]{1,0:T(8,128)S(1)} custom-call(bf16[16,2,2048]{2,1,0:T(2,128)(2,1)S(1)} %all_to_all.5.refs_3_.rows_ref._, bf16[4096,2048]{1,0:T(8,128)(2,1)S(1)} %copy-done, bf16[4096,256]{1,0:T(8,128)(2,1)S(1)} %copy-done.1, bf16[4096,256]{1,0:T(8,128)(2,1)S(1)} %copy-done.2), custom_call_target="tpu_custom_call" | custom-call | flops 335544320 | bytes 10485760 | tf_op jit(solution)/shard_map/pallas_call | solution.py:358
  20.2 1.7 %collective-permute-start.6 = (bf16[208,256]{1,0:T(8,128)(2,1)S(1)}, bf16[208,256]{1,0:T(8,128)(2,1)S(1)}, u32[]{:S(2)}, u32[]{:S(2)}) collective-permute-start(bf16[208,256]{1,0:T(8,128)(2,1)S(1)} %get-tuple-element.37), channel_id=1, source_target_pairs={{0,2},{1,3},{2,0},{3,1},{4,6},{5,7},{6,4},{7,5},{8,10},{9,11},{10,... | collective-permute-start | bytes 319496 | tf_op jit(solution)/shard_map/ppermute | solution.py:263
  22.0 0.0 collective-permute-done.rows_ref
  22.0 0.0 collective-permute-done.2.refs_0_.refs_5_.refs_7_
  22.0 2.0 %shard_map.105 = (f32[4,2,2560]{2,1,0:T(2,128)S(1)}, f32[4,2,2560]{2,1,0:T(2,128)S(1)}, f32[4,2,2560]{2,1,0:T(2,128)S(1)}, f32[4,2,2560]{2,1,0:T(2,128)S(1)}) custom-call(bf16[16,2,2048]{2,1,0:T(2,128)(2,1)S(1)} %collective-permute-done.rows_ref, bf16[4096,2048]{1,0:T(8,128)(2,1)S(1)} %copy-done, bf16[4096,256]{1,0:T(8,128)(2,1)S(1)} %copy-done.1, ...), custom_call_target="tpu_custom_call" | custom-call | flops 335544320 | bytes 10485760 | tf_op jit(solution)/shard_map/pallas_call | solution.py:366
  23.9 2.2 %collective-permute-start.3 = (f32[4,2,2560]{2,1,0:T(2,128)S(1)}, f32[4,2,2560]{2,1,0:T(2,128)S(1)}, u32[]{:S(2)}, u32[]{:S(2)}) collective-permute-start(f32[4,2,2560]{2,1,0:T(2,128)S(1)} %get-tuple-element.33), channel_id=1, source_target_pairs={{0,12},{4,8},{8,4},{12,0},{1,13},{5,9},{9,5},{13,1},{2,14},{6,10},... | collective-permute-start | bytes 245768 | tf_op jit(solution)/shard_map/ppermute | solution.py:259
  26.1 0.0 collective-permute-start.4
  26.1 2.3 %collective-permute-start.5 = (f32[4,2,2560]{2,1,0:T(2,128)S(1)}, f32[4,2,2560]{2,1,0:T(2,128)S(1)}, u32[]{:S(2)}, u32[]{:S(2)}) collective-permute-start(f32[4,2,2560]{2,1,0:T(2,128)S(1)} %get-tuple-element.35), channel_id=1, source_target_pairs={{0,4},{4,0},{8,12},{12,8},{1,5},{5,1},{9,13},{13,9},{2,6},{6,2},{1... | collective-permute-start | bytes 245768 | tf_op jit(solution)/shard_map/ppermute | solution.py:259
  28.4 0.1 shard_map.106.refs_4_.refs_6_
  28.5 2.7 %collective-permute-done.3.refs_0_ = f32[4,2,2560]{2,1,0:T(2,128)S(1)} collective-permute-done((f32[4,2,2560]{2,1,0:T(2,128)S(1)}, f32[4,2,2560]{2,1,0:T(2,128)S(1)}, u32[]{:S(2)}, u32[]{:S(2)}) %collective-permute-start.3) | collective-permute-done | bytes 81952 | tf_op jit(solution)/shard_map/ppermute | solution.py:259
  31.2 2.6 %collective-permute-done.4.refs_1_ = f32[4,2,2560]{2,1,0:T(2,128)S(1)} collective-permute-done((f32[4,2,2560]{2,1,0:T(2,128)S(1)}, f32[4,2,2560]{2,1,0:T(2,128)S(1)}, u32[]{:S(2)}, u32[]{:S(2)}) %collective-permute-start.4) | collective-permute-done | bytes 81952 | tf_op jit(solution)/shard_map/ppermute | solution.py:259
  33.8 0.0 collective-permute-done.5.refs_2_
  33.8 0.8 %shard_map.107.refs_0_ = bf16[2,2,2048]{2,1,0:T(2,128)(2,1)S(1)} custom-call(f32[1,128]{1,0:T(1,128)S(1)} %copy-done.7, f32[4,2,2560]{2,1,0:T(2,128)S(1)} %collective-permute-done.3.refs_0_, f32[4,2,2560]{2,1,0:T(2,128)S(1)} %collective-permute-done.4.refs_1_, f32[4,2,2560]{2,1,0:T(2,128)S(1)} %collective-permute-done.5.refs_2_, ...), custom_call_target="tpu_custom_call" | custom-call | flops 1 | bytes 1 | tf_op jit(solution)/shard_map/pallas_call | solution.py:384
  34.7 0.0 slice-start.1
  34.7 0.0 slice-start.2
  34.7 0.0 slice-start.3
  34.7 0.0 collective-permute-done.6.refs_5_
  34.7 0.0 collective-permute-done.7.refs_8_
  34.7 0.8 %shard_map.108.refs_1_ = bf16[2,2,2048]{2,1,0:T(2,128)(2,1)S(1)} custom-call(f32[1,128]{1,0:T(1,128)S(1)} %copy-done.7, f32[4,2,2560]{2,1,0:T(2,128)S(1)} %collective-permute-done.3.refs_0_, f32[4,2,2560]{2,1,0:T(2,128)S(1)} %collective-permute-done.4.refs_1_, f32[4,2,2560]{2,1,0:T(2,128)S(1)} %collective-permute-done.5.refs_2_, ...), custom_call_target="tpu_custom_call" | custom-call | flops 10000000000 | bytes 4194304 | tf_op jit(solution)/shard_map/pallas_call | solution.py:384
  35.6 1.0 %collective-permute-start.10 = (bf16[4,2,2048]{2,1,0:T(2,128)(2,1)S(1)}, bf16[4,2,2048]{2,1,0:T(2,128)(2,1)S(1)}, u32[]{:S(2)}, u32[]{:S(2)}) collective-permute-start(bf16[4,2,2048]{2,1,0:T(2,128)(2,1)S(1)} %shard_map.109.refs_0_), channel_id=1, source_target_pairs={{0,8},{4,12},{8,0},{12,4},{1,9},{5,13},{9,1},{13,5},{2,10},{6,14},... | collective-permute-start | bytes 98312 | tf_op jit(solution)/shard_map/ppermute | solution.py:259
  36.6 1.7 %collective-permute-start.8 = (bf16[4,2,2048]{2,1,0:T(2,128)(2,1)S(1)}, bf16[4,2,2048]{2,1,0:T(2,128)(2,1)S(1)}, u32[]{:S(2)}, u32[]{:S(2)}) collective-permute-start(bf16[4,2,2048]{2,1,0:T(2,128)(2,1)S(1)} %shard_map.109.refs_0_), channel_id=1, source_target_pairs={{0,12},{4,8},{8,4},{12,0},{1,13},{5,9},{9,5},{13,1},{2,14},{6,10},... | collective-permute-start | bytes 98312 | tf_op jit(solution)/shard_map/ppermute | solution.py:259
  38.3 0.9 %collective-permute-start.9 = (bf16[4,2,2048]{2,1,0:T(2,128)(2,1)S(1)}, bf16[4,2,2048]{2,1,0:T(2,128)(2,1)S(1)}, u32[]{:S(2)}, u32[]{:S(2)}) collective-permute-start(bf16[4,2,2048]{2,1,0:T(2,128)(2,1)S(1)} %shard_map.109.refs_0_), channel_id=1, source_target_pairs={{0,4},{4,0},{8,12},{12,8},{1,5},{5,1},{9,13},{13,9},{2,6},{6,2},{1... | collective-permute-start | bytes 98312 | tf_op jit(solution)/shard_map/ppermute | solution.py:259
  39.1 2.1 %collective-permute-done.10.refs_3_ = bf16[4,2,2048]{2,1,0:T(2,128)(2,1)S(1)} collective-permute-done((bf16[4,2,2048]{2,1,0:T(2,128)(2,1)S(1)}, bf16[4,2,2048]{2,1,0:T(2,128)(2,1)S(1)}, u32[]{:S(2)}, u32[]{:S(2)}) %collective-permute-start.10) | collective-permute-done | bytes 32800 | tf_op jit(solution)/shard_map/ppermute | solution.py:259
  41.2 1.2 %collective-permute-done.8.refs_1_ = bf16[4,2,2048]{2,1,0:T(2,128)(2,1)S(1)} collective-permute-done((bf16[4,2,2048]{2,1,0:T(2,128)(2,1)S(1)}, bf16[4,2,2048]{2,1,0:T(2,128)(2,1)S(1)}, u32[]{:S(2)}, u32[]{:S(2)}) %collective-permute-start.8) | collective-permute-done | bytes 32800 | tf_op jit(solution)/shard_map/ppermute | solution.py:259
  42.4 0.1 collective-permute-done.9.refs_2_
  42.5 0.0 slice-done.3
  42.6 1.5 %shard_map.112 = (f32[8,2,2048]{2,1,0:T(2,128)S(1)}, f32[8,2,2048]{2,1,0:T(2,128)S(1)}) custom-call(bf16[2048,4096]{1,0:T(8,128)(2,1)S(1)} %bitcast.3, bf16[4,2,2048]{2,1,0:T(2,128)(2,1)S(1)} %shard_map.109.refs_0_, bf16[4,2,2048]{2,1,0:T(2,128)(2,1)S(1)} %collective-permute-done.8.refs_1_, bf16[4,2,2048]{2,1,0:T(2,128)(2,1)S(1)} %collective-permute-done.9.refs_2_, ...), custom_call_target="tpu_custom_call" | custom-call | flops 268435456 | bytes 8388608 | tf_op jit(solution)/shard_map/pallas_call | solution.py:408
  44.1 0.1 collective-permute-start.13
  44.2 1.5 %shard_map.110 = (f32[8,2,2048]{2,1,0:T(2,128)S(1)}, f32[8,2,2048]{2,1,0:T(2,128)S(1)}) custom-call(bf16[2048,4096]{1,0:T(8,128)(2,1)S(1)} %bitcast.3, bf16[4,2,2048]{2,1,0:T(2,128)(2,1)S(1)} %shard_map.109.refs_0_, bf16[4,2,2048]{2,1,0:T(2,128)(2,1)S(1)} %collective-permute-done.8.refs_1_, bf16[4,2,2048]{2,1,0:T(2,128)(2,1)S(1)} %collective-permute-done.9.refs_2_, ...), custom_call_target="tpu_custom_call" | custom-call | flops 268435456 | bytes 8388608 | tf_op jit(solution)/shard_map/pallas_call | solution.py:408
  45.8 0.6 collective-permute-start.11
  46.3 0.0 collective-permute-done.13.b_ref
  46.3 1.6 %collective-permute-start.14 = (f32[4,2,2048]{2,1,0:T(2,128)S(1)}, f32[4,2,2048]{2,1,0:T(2,128)S(1)}, u32[]{:S(2)}, u32[]{:S(2)}) collective-permute-start(f32[4,2,2048]{2,1,0:T(2,128)S(1)} %get-tuple-element.46), channel_id=1, source_target_pairs={{0,2},{1,3},{2,0},{3,1},{4,6},{5,7},{6,4},{7,5},{8,10},{9,11},{10,... | collective-permute-start | bytes 196616 | tf_op jit(solution)/shard_map/ppermute | solution.py:263
  48.0 0.0 collective-permute-done.11.b_ref
  48.0 1.0 %collective-permute-start.12 = (f32[4,2,2048]{2,1,0:T(2,128)S(1)}, f32[4,2,2048]{2,1,0:T(2,128)S(1)}, u32[]{:S(2)}, u32[]{:S(2)}) collective-permute-start(f32[4,2,2048]{2,1,0:T(2,128)S(1)} %get-tuple-element.42), channel_id=1, source_target_pairs={{0,2},{1,3},{2,0},{3,1},{4,6},{5,7},{6,4},{7,5},{8,10},{9,11},{10,... | collective-permute-start | bytes 196616 | tf_op jit(solution)/shard_map/ppermute | solution.py:263
  49.0 2.0 %collective-permute-done.14.refs_3_ = f32[4,2,2048]{2,1,0:T(2,128)S(1)} collective-permute-done((f32[4,2,2048]{2,1,0:T(2,128)S(1)}, f32[4,2,2048]{2,1,0:T(2,128)S(1)}, u32[]{:S(2)}, u32[]{:S(2)}) %collective-permute-start.14) | collective-permute-done | bytes 65568 | tf_op jit(solution)/shard_map/ppermute | solution.py:263
  51.0 1.3 %collective-permute-done.12.refs_1_ = f32[4,2,2048]{2,1,0:T(2,128)S(1)} collective-permute-done((f32[4,2,2048]{2,1,0:T(2,128)S(1)}, f32[4,2,2048]{2,1,0:T(2,128)S(1)}, u32[]{:S(2)}, u32[]{:S(2)}) %collective-permute-start.12) | collective-permute-done | bytes 65568 | tf_op jit(solution)/shard_map/ppermute | solution.py:263
  52.3 0.1 shard_map.114
  52.4 1.0 %collective-permute-start.15 = (bf16[2,4096]{1,0:T(2,128)(2,1)S(1)}, bf16[2,4096]{1,0:T(2,128)(2,1)S(1)}, u32[]{:S(2)}, u32[]{:S(2)}) collective-permute-start(bf16[2,4096]{1,0:T(2,128)(2,1)S(1)} %get-tuple-element.47), channel_id=1, source_target_pairs={{0,8},{4,12},{8,0},{12,4},{1,9},{5,13},{9,1},{13,5},{2,10},{6,14},... | collective-permute-start | bytes 49160 | tf_op jit(solution)/shard_map/ppermute | solution.py:259
  53.4 1.7 %collective-permute-start.16 = (bf16[2,4096]{1,0:T(2,128)(2,1)S(1)}, bf16[2,4096]{1,0:T(2,128)(2,1)S(1)}, u32[]{:S(2)}, u32[]{:S(2)}) collective-permute-start(bf16[2,4096]{1,0:T(2,128)(2,1)S(1)} %get-tuple-element.48), channel_id=1, source_target_pairs={{0,12},{4,8},{8,4},{12,0},{1,13},{5,9},{9,5},{13,1},{2,14},{6,10},... | collective-permute-start | bytes 49160 | tf_op jit(solution)/shard_map/ppermute | solution.py:259
  55.1 0.9 %collective-permute-start.17 = (bf16[2,4096]{1,0:T(2,128)(2,1)S(1)}, bf16[2,4096]{1,0:T(2,128)(2,1)S(1)}, u32[]{:S(2)}, u32[]{:S(2)}) collective-permute-start(bf16[2,4096]{1,0:T(2,128)(2,1)S(1)} %get-tuple-element.49), channel_id=1, source_target_pairs={{0,4},{4,0},{8,12},{12,8},{1,5},{5,1},{9,13},{13,9},{2,6},{6,2},{1... | collective-permute-start | bytes 49160 | tf_op jit(solution)/shard_map/ppermute | solution.py:259
  56.0 1.2 %collective-permute-done.15.refs_0_ = bf16[2,4096]{1,0:T(2,128)(2,1)S(1)} collective-permute-done((bf16[2,4096]{1,0:T(2,128)(2,1)S(1)}, bf16[2,4096]{1,0:T(2,128)(2,1)S(1)}, u32[]{:S(2)}, u32[]{:S(2)}) %collective-permute-start.15) | collective-permute-done | bytes 16416 | tf_op jit(solution)/shard_map/ppermute | solution.py:259
  57.2 1.8 %collective-permute-done.16.refs_1_ = bf16[2,4096]{1,0:T(2,128)(2,1)S(1)} collective-permute-done((bf16[2,4096]{1,0:T(2,128)(2,1)S(1)}, bf16[2,4096]{1,0:T(2,128)(2,1)S(1)}, u32[]{:S(2)}, u32[]{:S(2)}) %collective-permute-start.16) | collective-permute-done | bytes 16416 | tf_op jit(solution)/shard_map/ppermute | solution.py:259
  59.0 0.0 collective-permute-done.17.refs_2_
  59.0 0.6 %shard_map.115 = bf16[2,16384]{1,0:T(2,128)(2,1)} custom-call(bf16[2,4096]{1,0:T(2,128)(2,1)S(1)} %collective-permute-done.15.refs_0_, bf16[2,4096]{1,0:T(2,128)(2,1)S(1)} %collective-permute-done.16.refs_1_, bf16[2,4096]{1,0:T(2,128)(2,1)S(1)} %collective-permute-done.17.refs_2_, bf16[2,4096]{1,0:T(2,128)(2,1)S(1)} %get-tuple-element.50.refs_3_), custom_call_target="tpu_custom_call" | custom-call | tf_op jit(solution)/shard_map/pallas_call | solution.py:439
  (16 shorter events, 0.1 us)
Async XLA Ops:
  0.0 1.3 %copy-start.5 = (f32[16384]{0:T(1024)S(1)}, f32[16384]{0:T(1024)}, u32[]{:S(2)}) copy-start(f32[16384]{0:T(1024)} %param.11) | copy-start | bytes 196612
  0.0 1.4 %copy-start.6 = (s32[2]{0:T(128)S(1)}, s32[2]{0:T(128)}, u32[]{:S(2)}) copy-start(s32[2]{0:T(128)} %param.18) | copy-start | bytes 28
  0.0 1.4 %copy-start.3 = (bf16[2,256,1024]{2,1,0:T(8,128)(2,1)S(1)}, bf16[2,256,1024]{2,1,0:T(8,128)(2,1)}, u32[]{:S(2)}) copy-start(bf16[2,256,1024]{2,1,0:T(8,128)(2,1)} %keys_ref.3) | copy-start | bytes 3145732
  0.0 1.6 %copy-start.4 = (bf16[2,256,1024]{2,1,0:T(8,128)(2,1)S(1)}, bf16[2,256,1024]{2,1,0:T(8,128)(2,1)}, u32[]{:S(2)}) copy-start(bf16[2,256,1024]{2,1,0:T(8,128)(2,1)} %values_ref.3) | copy-start | bytes 3145732
  0.0 18.3 %copy-start = (bf16[4096,2048]{1,0:T(8,128)(2,1)S(1)}, bf16[4096,2048]{1,0:T(8,128)(2,1)}, u32[]{:S(2)}) copy-start(bf16[4096,2048]{1,0:T(8,128)(2,1)} %query_ref.3) | copy-start | bytes 50331652
  0.0 18.3 %copy-start.1 = (bf16[4096,256]{1,0:T(8,128)(2,1)S(1)}, bf16[4096,256]{1,0:T(8,128)(2,1)}, u32[]{:S(2)}) copy-start(bf16[4096,256]{1,0:T(8,128)(2,1)} %key_ref.3) | copy-start | bytes 6291460
  0.0 18.3 %copy-start.2 = (bf16[4096,256]{1,0:T(8,128)(2,1)S(1)}, bf16[4096,256]{1,0:T(8,128)(2,1)}, u32[]{:S(2)}) copy-start(bf16[4096,256]{1,0:T(8,128)(2,1)} %value_ref.3) | copy-start | bytes 6291460
  0.0 1.0 %copy-start.8 = (bf16[2,16384]{1,0:T(2,128)(2,1)S(1)}, bf16[2,16384]{1,0:T(2,128)(2,1)}, u32[]{:S(2)}) copy-start(bf16[2,16384]{1,0:T(2,128)(2,1)} %tokens_ref.1) | copy-start | bytes 196612
  1.8 16.0 %collective-permute-start.1 = (bf16[832,256]{1,0:T(8,128)(2,1)S(1)}, bf16[832,256]{1,0:T(8,128)(2,1)S(1)}, u32[]{:S(2)}, u32[]{:S(2)}) collective-permute-start(bf16[832,256]{1,0:T(8,128)(2,1)S(1)} %get-tuple-element.31), channel_id=1, source_target_pairs={{0,2},{1,3},{2,0},{3,1},{4,6},{5,7},{6,4},{7,5},{8,10},{9,11},{10,... | collective-permute-start | bytes 1277960 | tf_op jit(solution)/shard_map/ppermute | solution.py:263
  17.8 4.1 %collective-permute-start.2 = (bf16[1040,256]{1,0:T(8,128)(2,1)S(1)}, bf16[1040,256]{1,0:T(8,128)(2,1)S(1)}, u32[]{:S(2)}, u32[]{:S(2)}) collective-permute-start(bf16[1040,256]{1,0:T(8,128)(2,1)S(1)} %get-tuple-element.32), channel_id=1, source_target_pairs={{0,1},{1,0},{2,3},{3,2},{4,5},{5,4},{6,7},{7,6},{8,9},{9,8},{10,11... | collective-permute-start | bytes 1597448 | tf_op jit(solution)/shard_map/ppermute | solution.py:263
  17.8 16.9 %collective-permute-start.7 = (bf16[1040,256]{1,0:T(8,128)(2,1)S(1)}, bf16[1040,256]{1,0:T(8,128)(2,1)S(1)}, u32[]{:S(2)}, u32[]{:S(2)}) collective-permute-start(bf16[1040,256]{1,0:T(8,128)(2,1)S(1)} %get-tuple-element.38), channel_id=1, source_target_pairs={{0,3},{1,2},{2,1},{3,0},{4,7},{5,6},{6,5},{7,4},{8,11},{9,10},{10,... | collective-permute-start | bytes 1597448 | tf_op jit(solution)/shard_map/ppermute | solution.py:263
  17.9 4.1 %collective-permute-start = (bf16[16,2,2048]{2,1,0:T(2,128)(2,1)S(1)}, bf16[16,2,2048]{2,1,0:T(2,128)(2,1)S(1)}, u32[]{:S(2)}, u32[]{:S(2)}) collective-permute-start(bf16[16,2,2048]{2,1,0:T(2,128)(2,1)S(1)} %all_to_all.5.refs_3_.rows_ref._), channel_id=1, source_target_pairs={{0,1},{1,0},{2,3},{3,2},{4,5},{5,4},{6,7},{7,6},{8,9},{9,8},{10,11... | collective-permute-start | bytes 393224 | tf_op jit(solution)/shard_map/ppermute | solution.py:259
  20.2 13.6 %copy-start.7 = (f32[1,128]{1,0:T(1,128)S(1)}, f32[1,128]{1,0:T(1,128)}, u32[]{:S(2)}) copy-start(f32[1,128]{1,0:T(1,128)} %constant.2.clone.frequency_ref) | copy-start | bytes 1540
  20.2 14.5 %collective-permute-start.6 = (bf16[208,256]{1,0:T(8,128)(2,1)S(1)}, bf16[208,256]{1,0:T(8,128)(2,1)S(1)}, u32[]{:S(2)}, u32[]{:S(2)}) collective-permute-start(bf16[208,256]{1,0:T(8,128)(2,1)S(1)} %get-tuple-element.37), channel_id=1, source_target_pairs={{0,2},{1,3},{2,0},{3,1},{4,6},{5,7},{6,4},{7,5},{8,10},{9,11},{10,... | collective-permute-start | bytes 319496 | tf_op jit(solution)/shard_map/ppermute | solution.py:263
  23.9 7.2 %collective-permute-start.3 = (f32[4,2,2560]{2,1,0:T(2,128)S(1)}, f32[4,2,2560]{2,1,0:T(2,128)S(1)}, u32[]{:S(2)}, u32[]{:S(2)}) collective-permute-start(f32[4,2,2560]{2,1,0:T(2,128)S(1)} %get-tuple-element.33), channel_id=1, source_target_pairs={{0,12},{4,8},{8,4},{12,0},{1,13},{5,9},{9,5},{13,1},{2,14},{6,10},... | collective-permute-start | bytes 245768 | tf_op jit(solution)/shard_map/ppermute | solution.py:259
  26.1 7.7 %collective-permute-start.4 = (f32[4,2,2560]{2,1,0:T(2,128)S(1)}, f32[4,2,2560]{2,1,0:T(2,128)S(1)}, u32[]{:S(2)}, u32[]{:S(2)}) collective-permute-start(f32[4,2,2560]{2,1,0:T(2,128)S(1)} %get-tuple-element.34), channel_id=1, source_target_pairs={{0,8},{4,12},{8,0},{12,4},{1,9},{5,13},{9,1},{13,5},{2,10},{6,14},... | collective-permute-start | bytes 245768 | tf_op jit(solution)/shard_map/ppermute | solution.py:259
  26.1 7.7 %collective-permute-start.5 = (f32[4,2,2560]{2,1,0:T(2,128)S(1)}, f32[4,2,2560]{2,1,0:T(2,128)S(1)}, u32[]{:S(2)}, u32[]{:S(2)}) collective-permute-start(f32[4,2,2560]{2,1,0:T(2,128)S(1)} %get-tuple-element.35), channel_id=1, source_target_pairs={{0,4},{4,0},{8,12},{12,8},{1,5},{5,1},{9,13},{13,9},{2,6},{6,2},{1... | collective-permute-start | bytes 245768 | tf_op jit(solution)/shard_map/ppermute | solution.py:259
  33.8 8.7 %slice-start = ((s8[16777216]{0:T(1024)(128)(4,1)}), s8[4194304]{0:T(1024)(128)(4,1)S(1)}, s32[]{:S(2)}) async-start(s8[16777216]{0:T(1024)(128)(4,1)} %bitcast.2), calls=%async_computation.1 | async-start | bytes 8388608
  34.7 7.9 %slice-start.1 = ((s8[16777216]{0:T(1024)(128)(4,1)}), s8[4194304]{0:T(1024)(128)(4,1)S(1)}, s32[]{:S(2)}) async-start(s8[16777216]{0:T(1024)(128)(4,1)} %bitcast.2), calls=%async_computation.2 | async-start | bytes 8388608
  34.7 7.8 %slice-start.2 = ((s8[16777216]{0:T(1024)(128)(4,1)}), s8[4194304]{0:T(1024)(128)(4,1)S(1)}, s32[]{:S(2)}) async-start(s8[16777216]{0:T(1024)(128)(4,1)} %bitcast.2), calls=%async_computation.3 | async-start | bytes 8388608
  34.7 7.8 %slice-start.3 = ((s8[16777216]{0:T(1024)(128)(4,1)}), s8[4194304]{0:T(1024)(128)(4,1)S(1)}, s32[]{:S(2)}) async-start(s8[16777216]{0:T(1024)(128)(4,1)} %bitcast.2), calls=%async_computation.4 | async-start | bytes 8388608
  35.6 5.6 %collective-permute-start.10 = (bf16[4,2,2048]{2,1,0:T(2,128)(2,1)S(1)}, bf16[4,2,2048]{2,1,0:T(2,128)(2,1)S(1)}, u32[]{:S(2)}, u32[]{:S(2)}) collective-permute-start(bf16[4,2,2048]{2,1,0:T(2,128)(2,1)S(1)} %shard_map.109.refs_0_), channel_id=1, source_target_pairs={{0,8},{4,12},{8,0},{12,4},{1,9},{5,13},{9,1},{13,5},{2,10},{6,14},... | collective-permute-start | bytes 98312 | tf_op jit(solution)/shard_map/ppermute | solution.py:259
  36.6 5.8 %collective-permute-start.8 = (bf16[4,2,2048]{2,1,0:T(2,128)(2,1)S(1)}, bf16[4,2,2048]{2,1,0:T(2,128)(2,1)S(1)}, u32[]{:S(2)}, u32[]{:S(2)}) collective-permute-start(bf16[4,2,2048]{2,1,0:T(2,128)(2,1)S(1)} %shard_map.109.refs_0_), channel_id=1, source_target_pairs={{0,12},{4,8},{8,4},{12,0},{1,13},{5,9},{9,5},{13,1},{2,14},{6,10},... | collective-permute-start | bytes 98312 | tf_op jit(solution)/shard_map/ppermute | solution.py:259
  38.3 4.3 %collective-permute-start.9 = (bf16[4,2,2048]{2,1,0:T(2,128)(2,1)S(1)}, bf16[4,2,2048]{2,1,0:T(2,128)(2,1)S(1)}, u32[]{:S(2)}, u32[]{:S(2)}) collective-permute-start(bf16[4,2,2048]{2,1,0:T(2,128)(2,1)S(1)} %shard_map.109.refs_0_), channel_id=1, source_target_pairs={{0,4},{4,0},{8,12},{12,8},{1,5},{5,1},{9,13},{13,9},{2,6},{6,2},{1... | collective-permute-start | bytes 98312 | tf_op jit(solution)/shard_map/ppermute | solution.py:259
  44.1 2.2 %collective-permute-start.13 = (f32[8,2,2048]{2,1,0:T(2,128)S(1)}, f32[8,2,2048]{2,1,0:T(2,128)S(1)}, u32[]{:S(2)}, u32[]{:S(2)}) collective-permute-start(f32[8,2,2048]{2,1,0:T(2,128)S(1)} %get-tuple-element.44), channel_id=1, source_target_pairs={{0,1},{1,0},{2,3},{3,2},{4,5},{5,4},{6,7},{7,6},{8,9},{9,8},{10,11... | collective-permute-start | bytes 393224 | tf_op jit(solution)/shard_map/ppermute | solution.py:263
  45.8 2.2 %collective-permute-start.11 = (f32[8,2,2048]{2,1,0:T(2,128)S(1)}, f32[8,2,2048]{2,1,0:T(2,128)S(1)}, u32[]{:S(2)}, u32[]{:S(2)}) collective-permute-start(f32[8,2,2048]{2,1,0:T(2,128)S(1)} %get-tuple-element.40), channel_id=1, source_target_pairs={{0,1},{1,0},{2,3},{3,2},{4,5},{5,4},{6,7},{7,6},{8,9},{9,8},{10,11... | collective-permute-start | bytes 393224 | tf_op jit(solution)/shard_map/ppermute | solution.py:263
  46.3 4.7 %collective-permute-start.14 = (f32[4,2,2048]{2,1,0:T(2,128)S(1)}, f32[4,2,2048]{2,1,0:T(2,128)S(1)}, u32[]{:S(2)}, u32[]{:S(2)}) collective-permute-start(f32[4,2,2048]{2,1,0:T(2,128)S(1)} %get-tuple-element.46), channel_id=1, source_target_pairs={{0,2},{1,3},{2,0},{3,1},{4,6},{5,7},{6,4},{7,5},{8,10},{9,11},{10,... | collective-permute-start | bytes 196616 | tf_op jit(solution)/shard_map/ppermute | solution.py:263
  48.0 4.3 %collective-permute-start.12 = (f32[4,2,2048]{2,1,0:T(2,128)S(1)}, f32[4,2,2048]{2,1,0:T(2,128)S(1)}, u32[]{:S(2)}, u32[]{:S(2)}) collective-permute-start(f32[4,2,2048]{2,1,0:T(2,128)S(1)} %get-tuple-element.42), channel_id=1, source_target_pairs={{0,2},{1,3},{2,0},{3,1},{4,6},{5,7},{6,4},{7,5},{8,10},{9,11},{10,... | collective-permute-start | bytes 196616 | tf_op jit(solution)/shard_map/ppermute | solution.py:263
  52.4 4.8 %collective-permute-start.15 = (bf16[2,4096]{1,0:T(2,128)(2,1)S(1)}, bf16[2,4096]{1,0:T(2,128)(2,1)S(1)}, u32[]{:S(2)}, u32[]{:S(2)}) collective-permute-start(bf16[2,4096]{1,0:T(2,128)(2,1)S(1)} %get-tuple-element.47), channel_id=1, source_target_pairs={{0,8},{4,12},{8,0},{12,4},{1,9},{5,13},{9,1},{13,5},{2,10},{6,14},... | collective-permute-start | bytes 49160 | tf_op jit(solution)/shard_map/ppermute | solution.py:259
  53.4 5.6 %collective-permute-start.16 = (bf16[2,4096]{1,0:T(2,128)(2,1)S(1)}, bf16[2,4096]{1,0:T(2,128)(2,1)S(1)}, u32[]{:S(2)}, u32[]{:S(2)}) collective-permute-start(bf16[2,4096]{1,0:T(2,128)(2,1)S(1)} %get-tuple-element.48), channel_id=1, source_target_pairs={{0,12},{4,8},{8,4},{12,0},{1,13},{5,9},{9,5},{13,1},{2,14},{6,10},... | collective-permute-start | bytes 49160 | tf_op jit(solution)/shard_map/ppermute | solution.py:259
  55.1 3.9 %collective-permute-start.17 = (bf16[2,4096]{1,0:T(2,128)(2,1)S(1)}, bf16[2,4096]{1,0:T(2,128)(2,1)S(1)}, u32[]{:S(2)}, u32[]{:S(2)}) collective-permute-start(bf16[2,4096]{1,0:T(2,128)(2,1)S(1)} %get-tuple-element.49), channel_id=1, source_target_pairs={{0,4},{4,0},{8,12},{12,8},{1,5},{5,1},{9,13},{13,9},{2,6},{6,2},{1... | collective-permute-start | bytes 49160 | tf_op jit(solution)/shard_map/ppermute | solution.py:259

commit v24 on v23

--- a/solution.py
+++ b/solution.py
@@ -122,7 +122,7 @@
                 continue
             first, last = firsts[l // 2 - 1], lasts[l // 2 - 1]
             at = (values * rows + r) * slots
-            end = (rows + early) * slots + slots // 4
+            end = (rows + early) * slots + slots // 8
             if at + slots <= end:
                 parts.append(first[at : at + slots])
             elif at < end:
@@ -314,7 +314,7 @@
     even = plane // 2 - 1
     early = rows // 2
     every = [(r, 0, slots) for r in range(rows)]
-    cut_at = slots // 4
+    cut_at = slots // 8
 
     def cut(plan, after):
         return pl.pallas_call(

time: 59.8 us -> 59.9 us (level)
  transfers between devices with their start and end apart: 18 -> 18, of which waited for: 9 -> 10; matrix products, arithmetic and copies ran while one was open for 0% -> 0% of each run, Pallas kernels for 11% -> 11%
where the time goes in v24:
time: 59.9 us; the launch traced here: 59.7 us
  starting transfers between devices  19.8 us (33%)
  waiting for transfers between devices  15.5 us (26%)
  blocking collectives  13 us (22%)
  Pallas kernels  9.97 us (17%)
  local copies, waits for them, and re-layouts  1.27 us (2%)
    all_to_all x1, blocking collectives, swap_blocks(): return lax.all_to_all(blocks, axes, split_axis=0, concat_axis=0, tiled=True)  13 us
    ppermute x10, starting transfers between devices, swap_pairs(): lax.ppermute(value, axis, [(i, i ^ step) for i in range(lax.axis_size(axi...  12 us
    ppermute x10, waiting for transfers between devices, swap_pairs(): lax.ppermute(value, axis, [(i, i ^ step) for i in range(lax.axis_size(axi...  11.9 us
    ppermute x8, starting transfers between devices, swap_plane(): lax.ppermute(value, PLANE, [(i, i ^ step) for i in range(lax.axis_size(PL...  7.79 us
    ppermute x8, waiting for transfers between devices, swap_plane(): lax.ppermute(value, PLANE, [(i, i ^ step) for i in range(lax.axis_size(PL...  3.56 us
    pallas_call x2, Pallas kernels, shards(): pl.pallas_call(functools.partial(output_kernel, p * part_cols, part_cols,...  3.09 us
    pallas_call x1, Pallas kernels, shards(): pl.pallas_call(functools.partial(project_kernel, False, wide, plane), out...  1.98 us
    pallas_call x1, Pallas kernels, shards(): pl.pallas_call(functools.partial(project_kernel, True, wide, plane), out_...  1.9 us
  transfers between devices with their start and end apart: 18, of which 10 were waited for; matrix products, arithmetic and copies ran while one was open for 0% of the time, Pallas kernels for 11%

profile of v24, /device:TPU:0, one launch (start us, length us, event | category | flops | bytes accessed | tf_op | source)
XLA Modules:
  0.0 59.7 jit_solution(9888687204273360729)
XLA Ops:
  0.0 0.0 copy-start.1
  0.0 0.0 copy-start.2
  0.0 0.0 copy-start.8
  0.0 1.0 %copy-done.8 = bf16[2,16384]{1,0:T(2,128)(2,1)S(1)} copy-done((bf16[2,16384]{1,0:T(2,128)(2,1)S(1)}, bf16[2,16384]{1,0:T(2,128)(2,1)}, u32[]{:S(2)}) %copy-start.8) | copy-done | bytes 65560
  1.0 0.2 shard_map.100.scaled_ref
  1.3 0.0 copy-done.5
  1.3 0.1 shard_map.101._
  1.4 0.0 copy-done.6
  1.4 0.0 copy-done.3
  1.4 0.2 copy-done.4
  1.6 0.2 shard_map.102
  1.8 3.0 %collective-permute-start.1 = (bf16[800,256]{1,0:T(8,128)(2,1)S(1)}, bf16[800,256]{1,0:T(8,128)(2,1)S(1)}, u32[]{:S(2)}, u32[]{:S(2)}) collective-permute-start(bf16[800,256]{1,0:T(8,128)(2,1)S(1)} %get-tuple-element.31), channel_id=1, source_target_pairs={{0,2},{1,3},{2,0},{3,1},{4,6},{5,7},{6,4},{7,5},{8,10},{9,11},{10,... | collective-permute-start | bytes 1228808 | tf_op jit(solution)/shard_map/ppermute | solution.py:263
  4.9 13.0 %all_to_all.5.refs_3_.rows_ref._ = bf16[16,2,2048]{2,1,0:T(2,128)(2,1)S(1)} all-to-all(bf16[16,2,2048]{2,1,0:T(2,128)(2,1)S(1)} %shard_map.101._), channel_id=1, replica_groups=mesh['groups'=2,'gx'=4,'gy'=2,'gz'=2] {'gx','gy','gz'}, dimensions={0} | all-to-all | bytes 262144 | tf_op jit(solution)/shard_map/all_to_all | solution.py:255
  17.8 0.0 collective-permute-done.1.refs_4_
  17.8 0.0 collective-permute-start.2
  17.8 0.1 collective-permute-start.7
  17.9 0.4 collective-permute-start
  18.3 1.7 %collective-permute-start.6 = (bf16[240,256]{1,0:T(8,128)(2,1)S(1)}, bf16[240,256]{1,0:T(8,128)(2,1)S(1)}, u32[]{:S(2)}, u32[]{:S(2)}) collective-permute-start(bf16[240,256]{1,0:T(8,128)(2,1)S(1)} %get-tuple-element.37), channel_id=1, source_target_pairs={{0,2},{1,3},{2,0},{3,1},{4,6},{5,7},{6,4},{7,5},{8,10},{9,11},{10,... | collective-permute-start | bytes 368648 | tf_op jit(solution)/shard_map/ppermute | solution.py:263
  20.0 0.0 copy-done
  20.0 0.0 copy-done.1
  20.0 0.0 copy-done.2
  20.0 1.9 %shard_map.104.refs_1_ = f32[32,2560]{1,0:T(8,128)S(1)} custom-call(bf16[16,2,2048]{2,1,0:T(2,128)(2,1)S(1)} %all_to_all.5.refs_3_.rows_ref._, bf16[4096,2048]{1,0:T(8,128)(2,1)S(1)} %copy-done, bf16[4096,256]{1,0:T(8,128)(2,1)S(1)} %copy-done.1, bf16[4096,256]{1,0:T(8,128)(2,1)S(1)} %copy-done.2), custom_call_target="tpu_custom_call" | custom-call | flops 335544320 | bytes 10485760 | tf_op jit(solution)/shard_map/pallas_call | solution.py:358
  21.9 0.0 collective-permute-done.rows_ref
  22.0 0.0 collective-permute-done.2.refs_0_.refs_5_.refs_7_
  22.0 2.0 %shard_map.105 = (f32[4,2,2560]{2,1,0:T(2,128)S(1)}, f32[4,2,2560]{2,1,0:T(2,128)S(1)}, f32[4,2,2560]{2,1,0:T(2,128)S(1)}, f32[4,2,2560]{2,1,0:T(2,128)S(1)}) custom-call(bf16[16,2,2048]{2,1,0:T(2,128)(2,1)S(1)} %collective-permute-done.rows_ref, bf16[4096,2048]{1,0:T(8,128)(2,1)S(1)} %copy-done, bf16[4096,256]{1,0:T(8,128)(2,1)S(1)} %copy-done.1, ...), custom_call_target="tpu_custom_call" | custom-call | flops 335544320 | bytes 10485760 | tf_op jit(solution)/shard_map/pallas_call | solution.py:366
  24.0 1.8 %collective-permute-start.3 = (f32[4,2,2560]{2,1,0:T(2,128)S(1)}, f32[4,2,2560]{2,1,0:T(2,128)S(1)}, u32[]{:S(2)}, u32[]{:S(2)}) collective-permute-start(f32[4,2,2560]{2,1,0:T(2,128)S(1)} %get-tuple-element.33), channel_id=1, source_target_pairs={{0,12},{4,8},{8,4},{12,0},{1,13},{5,9},{9,5},{13,1},{2,14},{6,10},... | collective-permute-start | bytes 245768 | tf_op jit(solution)/shard_map/ppermute | solution.py:259
  25.8 0.0 collective-permute-start.4
  25.8 2.6 %collective-permute-start.5 = (f32[4,2,2560]{2,1,0:T(2,128)S(1)}, f32[4,2,2560]{2,1,0:T(2,128)S(1)}, u32[]{:S(2)}, u32[]{:S(2)}) collective-permute-start(f32[4,2,2560]{2,1,0:T(2,128)S(1)} %get-tuple-element.35), channel_id=1, source_target_pairs={{0,4},{4,0},{8,12},{12,8},{1,5},{5,1},{9,13},{13,9},{2,6},{6,2},{1... | collective-permute-start | bytes 245768 | tf_op jit(solution)/shard_map/ppermute | solution.py:259
  28.4 0.1 shard_map.106.refs_4_.refs_6_
  28.5 2.7 %collective-permute-done.3.refs_0_ = f32[4,2,2560]{2,1,0:T(2,128)S(1)} collective-permute-done((f32[4,2,2560]{2,1,0:T(2,128)S(1)}, f32[4,2,2560]{2,1,0:T(2,128)S(1)}, u32[]{:S(2)}, u32[]{:S(2)}) %collective-permute-start.3) | collective-permute-done | bytes 81952 | tf_op jit(solution)/shard_map/ppermute | solution.py:259
  31.2 2.6 %collective-permute-done.4.refs_1_ = f32[4,2,2560]{2,1,0:T(2,128)S(1)} collective-permute-done((f32[4,2,2560]{2,1,0:T(2,128)S(1)}, f32[4,2,2560]{2,1,0:T(2,128)S(1)}, u32[]{:S(2)}, u32[]{:S(2)}) %collective-permute-start.4) | collective-permute-done | bytes 81952 | tf_op jit(solution)/shard_map/ppermute | solution.py:259
  33.8 0.0 collective-permute-done.5.refs_2_
  33.9 0.8 %shard_map.107.refs_0_ = bf16[2,2,2048]{2,1,0:T(2,128)(2,1)S(1)} custom-call(f32[1,128]{1,0:T(1,128)S(1)} %copy-done.7, f32[4,2,2560]{2,1,0:T(2,128)S(1)} %collective-permute-done.3.refs_0_, f32[4,2,2560]{2,1,0:T(2,128)S(1)} %collective-permute-done.4.refs_1_, f32[4,2,2560]{2,1,0:T(2,128)S(1)} %collective-permute-done.5.refs_2_, ...), custom_call_target="tpu_custom_call" | custom-call | flops 1 | bytes 1 | tf_op jit(solution)/shard_map/pallas_call | solution.py:384
  34.7 0.0 slice-start.1
  34.7 0.0 slice-start.2
  34.7 0.0 slice-start.3
  34.7 0.2 collective-permute-done.6.refs_5_
  34.9 0.0 collective-permute-done.7.refs_8_
  34.9 0.8 %shard_map.108.refs_1_ = bf16[2,2,2048]{2,1,0:T(2,128)(2,1)S(1)} custom-call(f32[1,128]{1,0:T(1,128)S(1)} %copy-done.7, f32[4,2,2560]{2,1,0:T(2,128)S(1)} %collective-permute-done.3.refs_0_, f32[4,2,2560]{2,1,0:T(2,128)S(1)} %collective-permute-done.4.refs_1_, f32[4,2,2560]{2,1,0:T(2,128)S(1)} %collective-permute-done.5.refs_2_, ...), custom_call_target="tpu_custom_call" | custom-call | flops 10000000000 | bytes 4194304 | tf_op jit(solution)/shard_map/pallas_call | solution.py:384
  35.8 0.8 %collective-permute-start.10 = (bf16[4,2,2048]{2,1,0:T(2,128)(2,1)S(1)}, bf16[4,2,2048]{2,1,0:T(2,128)(2,1)S(1)}, u32[]{:S(2)}, u32[]{:S(2)}) collective-permute-start(bf16[4,2,2048]{2,1,0:T(2,128)(2,1)S(1)} %shard_map.109.refs_0_), channel_id=1, source_target_pairs={{0,8},{4,12},{8,0},{12,4},{1,9},{5,13},{9,1},{13,5},{2,10},{6,14},... | collective-permute-start | bytes 98312 | tf_op jit(solution)/shard_map/ppermute | solution.py:259
  36.6 1.6 %collective-permute-start.8 = (bf16[4,2,2048]{2,1,0:T(2,128)(2,1)S(1)}, bf16[4,2,2048]{2,1,0:T(2,128)(2,1)S(1)}, u32[]{:S(2)}, u32[]{:S(2)}) collective-permute-start(bf16[4,2,2048]{2,1,0:T(2,128)(2,1)S(1)} %shard_map.109.refs_0_), channel_id=1, source_target_pairs={{0,12},{4,8},{8,4},{12,0},{1,13},{5,9},{9,5},{13,1},{2,14},{6,10},... | collective-permute-start | bytes 98312 | tf_op jit(solution)/shard_map/ppermute | solution.py:259
  38.2 1.2 %collective-permute-start.9 = (bf16[4,2,2048]{2,1,0:T(2,128)(2,1)S(1)}, bf16[4,2,2048]{2,1,0:T(2,128)(2,1)S(1)}, u32[]{:S(2)}, u32[]{:S(2)}) collective-permute-start(bf16[4,2,2048]{2,1,0:T(2,128)(2,1)S(1)} %shard_map.109.refs_0_), channel_id=1, source_target_pairs={{0,4},{4,0},{8,12},{12,8},{1,5},{5,1},{9,13},{13,9},{2,6},{6,2},{1... | collective-permute-start | bytes 98312 | tf_op jit(solution)/shard_map/ppermute | solution.py:259
  39.3 1.8 %collective-permute-done.10.refs_3_ = bf16[4,2,2048]{2,1,0:T(2,128)(2,1)S(1)} collective-permute-done((bf16[4,2,2048]{2,1,0:T(2,128)(2,1)S(1)}, bf16[4,2,2048]{2,1,0:T(2,128)(2,1)S(1)}, u32[]{:S(2)}, u32[]{:S(2)}) %collective-permute-start.10) | collective-permute-done | bytes 32800 | tf_op jit(solution)/shard_map/ppermute | solution.py:259
  41.1 1.3 %collective-permute-done.8.refs_1_ = bf16[4,2,2048]{2,1,0:T(2,128)(2,1)S(1)} collective-permute-done((bf16[4,2,2048]{2,1,0:T(2,128)(2,1)S(1)}, bf16[4,2,2048]{2,1,0:T(2,128)(2,1)S(1)}, u32[]{:S(2)}, u32[]{:S(2)}) %collective-permute-start.8) | collective-permute-done | bytes 32800 | tf_op jit(solution)/shard_map/ppermute | solution.py:259
  42.4 0.0 collective-permute-done.9.refs_2_
  42.4 0.0 slice-done.1
  42.5 1.5 %shard_map.112 = (f32[8,2,2048]{2,1,0:T(2,128)S(1)}, f32[8,2,2048]{2,1,0:T(2,128)S(1)}) custom-call(bf16[2048,4096]{1,0:T(8,128)(2,1)S(1)} %bitcast.3, bf16[4,2,2048]{2,1,0:T(2,128)(2,1)S(1)} %shard_map.109.refs_0_, bf16[4,2,2048]{2,1,0:T(2,128)(2,1)S(1)} %collective-permute-done.8.refs_1_, bf16[4,2,2048]{2,1,0:T(2,128)(2,1)S(1)} %collective-permute-done.9.refs_2_, ...), custom_call_target="tpu_custom_call" | custom-call | flops 268435456 | bytes 8388608 | tf_op jit(solution)/shard_map/pallas_call | solution.py:408
  44.0 0.1 collective-permute-start.13
  44.1 1.5 %shard_map.110 = (f32[8,2,2048]{2,1,0:T(2,128)S(1)}, f32[8,2,2048]{2,1,0:T(2,128)S(1)}) custom-call(bf16[2048,4096]{1,0:T(8,128)(2,1)S(1)} %bitcast.3, bf16[4,2,2048]{2,1,0:T(2,128)(2,1)S(1)} %shard_map.109.refs_0_, bf16[4,2,2048]{2,1,0:T(2,128)(2,1)S(1)} %collective-permute-done.8.refs_1_, bf16[4,2,2048]{2,1,0:T(2,128)(2,1)S(1)} %collective-permute-done.9.refs_2_, ...), custom_call_target="tpu_custom_call" | custom-call | flops 268435456 | bytes 8388608 | tf_op jit(solution)/shard_map/pallas_call | solution.py:408
  45.7 0.6 collective-permute-start.11
  46.2 0.0 collective-permute-done.13.b_ref
  46.2 1.4 %collective-permute-start.14 = (f32[4,2,2048]{2,1,0:T(2,128)S(1)}, f32[4,2,2048]{2,1,0:T(2,128)S(1)}, u32[]{:S(2)}, u32[]{:S(2)}) collective-permute-start(f32[4,2,2048]{2,1,0:T(2,128)S(1)} %get-tuple-element.46), channel_id=1, source_target_pairs={{0,2},{1,3},{2,0},{3,1},{4,6},{5,7},{6,4},{7,5},{8,10},{9,11},{10,... | collective-permute-start | bytes 196616 | tf_op jit(solution)/shard_map/ppermute | solution.py:263
  47.7 0.0 collective-permute-done.11.b_ref
  47.7 1.0 %collective-permute-start.12 = (f32[4,2,2048]{2,1,0:T(2,128)S(1)}, f32[4,2,2048]{2,1,0:T(2,128)S(1)}, u32[]{:S(2)}, u32[]{:S(2)}) collective-permute-start(f32[4,2,2048]{2,1,0:T(2,128)S(1)} %get-tuple-element.42), channel_id=1, source_target_pairs={{0,2},{1,3},{2,0},{3,1},{4,6},{5,7},{6,4},{7,5},{8,10},{9,11},{10,... | collective-permute-start | bytes 196616 | tf_op jit(solution)/shard_map/ppermute | solution.py:263
  48.7 2.3 %collective-permute-done.14.refs_3_ = f32[4,2,2048]{2,1,0:T(2,128)S(1)} collective-permute-done((f32[4,2,2048]{2,1,0:T(2,128)S(1)}, f32[4,2,2048]{2,1,0:T(2,128)S(1)}, u32[]{:S(2)}, u32[]{:S(2)}) %collective-permute-start.14) | collective-permute-done | bytes 65568 | tf_op jit(solution)/shard_map/ppermute | solution.py:263
  51.0 1.0 %collective-permute-done.12.refs_1_ = f32[4,2,2048]{2,1,0:T(2,128)S(1)} collective-permute-done((f32[4,2,2048]{2,1,0:T(2,128)S(1)}, f32[4,2,2048]{2,1,0:T(2,128)S(1)}, u32[]{:S(2)}, u32[]{:S(2)}) %collective-permute-start.12) | collective-permute-done | bytes 65568 | tf_op jit(solution)/shard_map/ppermute | solution.py:263
  52.0 0.1 shard_map.114
  52.1 1.3 %collective-permute-start.15 = (bf16[2,4096]{1,0:T(2,128)(2,1)S(1)}, bf16[2,4096]{1,0:T(2,128)(2,1)S(1)}, u32[]{:S(2)}, u32[]{:S(2)}) collective-permute-start(bf16[2,4096]{1,0:T(2,128)(2,1)S(1)} %get-tuple-element.47), channel_id=1, source_target_pairs={{0,8},{4,12},{8,0},{12,4},{1,9},{5,13},{9,1},{13,5},{2,10},{6,14},... | collective-permute-start | bytes 49160 | tf_op jit(solution)/shard_map/ppermute | solution.py:259
  53.4 1.9 %collective-permute-start.16 = (bf16[2,4096]{1,0:T(2,128)(2,1)S(1)}, bf16[2,4096]{1,0:T(2,128)(2,1)S(1)}, u32[]{:S(2)}, u32[]{:S(2)}) collective-permute-start(bf16[2,4096]{1,0:T(2,128)(2,1)S(1)} %get-tuple-element.48), channel_id=1, source_target_pairs={{0,12},{4,8},{8,4},{12,0},{1,13},{5,9},{9,5},{13,1},{2,14},{6,10},... | collective-permute-start | bytes 49160 | tf_op jit(solution)/shard_map/ppermute | solution.py:259
  55.3 0.4 collective-permute-start.17
  55.6 1.2 %collective-permute-done.15.refs_0_ = bf16[2,4096]{1,0:T(2,128)(2,1)S(1)} collective-permute-done((bf16[2,4096]{1,0:T(2,128)(2,1)S(1)}, bf16[2,4096]{1,0:T(2,128)(2,1)S(1)}, u32[]{:S(2)}, u32[]{:S(2)}) %collective-permute-start.15) | collective-permute-done | bytes 16416 | tf_op jit(solution)/shard_map/ppermute | solution.py:259
  56.8 2.1 %collective-permute-done.16.refs_1_ = bf16[2,4096]{1,0:T(2,128)(2,1)S(1)} collective-permute-done((bf16[2,4096]{1,0:T(2,128)(2,1)S(1)}, bf16[2,4096]{1,0:T(2,128)(2,1)S(1)}, u32[]{:S(2)}, u32[]{:S(2)}) %collective-permute-start.16) | collective-permute-done | bytes 16416 | tf_op jit(solution)/shard_map/ppermute | solution.py:259
  58.9 0.2 collective-permute-done.17.refs_2_
  59.1 0.6 %shard_map.115 = bf16[2,16384]{1,0:T(2,128)(2,1)} custom-call(bf16[2,4096]{1,0:T(2,128)(2,1)S(1)} %collective-permute-done.15.refs_0_, bf16[2,4096]{1,0:T(2,128)(2,1)S(1)} %collective-permute-done.16.refs_1_, bf16[2,4096]{1,0:T(2,128)(2,1)S(1)} %collective-permute-done.17.refs_2_, bf16[2,4096]{1,0:T(2,128)(2,1)S(1)} %get-tuple-element.50.refs_3_), custom_call_target="tpu_custom_call" | custom-call | tf_op jit(solution)/shard_map/pallas_call | solution.py:439
  (16 shorter events, 0.1 us)
Async XLA Ops:
  0.0 1.3 %copy-start.5 = (f32[16384]{0:T(1024)S(1)}, f32[16384]{0:T(1024)}, u32[]{:S(2)}) copy-start(f32[16384]{0:T(1024)} %param.11) | copy-start | bytes 196612
  0.0 1.4 %copy-start.6 = (s32[2]{0:T(128)S(1)}, s32[2]{0:T(128)}, u32[]{:S(2)}) copy-start(s32[2]{0:T(128)} %param.18) | copy-start | bytes 28
  0.0 1.4 %copy-start.3 = (bf16[2,256,1024]{2,1,0:T(8,128)(2,1)S(1)}, bf16[2,256,1024]{2,1,0:T(8,128)(2,1)}, u32[]{:S(2)}) copy-start(bf16[2,256,1024]{2,1,0:T(8,128)(2,1)} %keys_ref.3) | copy-start | bytes 3145732
  0.0 1.6 %copy-start.4 = (bf16[2,256,1024]{2,1,0:T(8,128)(2,1)S(1)}, bf16[2,256,1024]{2,1,0:T(8,128)(2,1)}, u32[]{:S(2)}) copy-start(bf16[2,256,1024]{2,1,0:T(8,128)(2,1)} %values_ref.3) | copy-start | bytes 3145732
  0.0 20.0 %copy-start = (bf16[4096,2048]{1,0:T(8,128)(2,1)S(1)}, bf16[4096,2048]{1,0:T(8,128)(2,1)}, u32[]{:S(2)}) copy-start(bf16[4096,2048]{1,0:T(8,128)(2,1)} %query_ref.3) | copy-start | bytes 50331652
  0.0 20.0 %copy-start.1 = (bf16[4096,256]{1,0:T(8,128)(2,1)S(1)}, bf16[4096,256]{1,0:T(8,128)(2,1)}, u32[]{:S(2)}) copy-start(bf16[4096,256]{1,0:T(8,128)(2,1)} %key_ref.3) | copy-start | bytes 6291460
  0.0 20.0 %copy-start.2 = (bf16[4096,256]{1,0:T(8,128)(2,1)S(1)}, bf16[4096,256]{1,0:T(8,128)(2,1)}, u32[]{:S(2)}) copy-start(bf16[4096,256]{1,0:T(8,128)(2,1)} %value_ref.3) | copy-start | bytes 6291460
  0.0 1.0 %copy-start.8 = (bf16[2,16384]{1,0:T(2,128)(2,1)S(1)}, bf16[2,16384]{1,0:T(2,128)(2,1)}, u32[]{:S(2)}) copy-start(bf16[2,16384]{1,0:T(2,128)(2,1)} %tokens_ref.1) | copy-start | bytes 196612
  1.8 16.0 %collective-permute-start.1 = (bf16[800,256]{1,0:T(8,128)(2,1)S(1)}, bf16[800,256]{1,0:T(8,128)(2,1)S(1)}, u32[]{:S(2)}, u32[]{:S(2)}) collective-permute-start(bf16[800,256]{1,0:T(8,128)(2,1)S(1)} %get-tuple-element.31), channel_id=1, source_target_pairs={{0,2},{1,3},{2,0},{3,1},{4,6},{5,7},{6,4},{7,5},{8,10},{9,11},{10,... | collective-permute-start | bytes 1228808 | tf_op jit(solution)/shard_map/ppermute | solution.py:263
  17.8 4.1 %collective-permute-start.2 = (bf16[1040,256]{1,0:T(8,128)(2,1)S(1)}, bf16[1040,256]{1,0:T(8,128)(2,1)S(1)}, u32[]{:S(2)}, u32[]{:S(2)}) collective-permute-start(bf16[1040,256]{1,0:T(8,128)(2,1)S(1)} %get-tuple-element.32), channel_id=1, source_target_pairs={{0,1},{1,0},{2,3},{3,2},{4,5},{5,4},{6,7},{7,6},{8,9},{9,8},{10,11... | collective-permute-start | bytes 1597448 | tf_op jit(solution)/shard_map/ppermute | solution.py:263
  17.8 17.1 %collective-permute-start.7 = (bf16[1040,256]{1,0:T(8,128)(2,1)S(1)}, bf16[1040,256]{1,0:T(8,128)(2,1)S(1)}, u32[]{:S(2)}, u32[]{:S(2)}) collective-permute-start(bf16[1040,256]{1,0:T(8,128)(2,1)S(1)} %get-tuple-element.38), channel_id=1, source_target_pairs={{0,3},{1,2},{2,1},{3,0},{4,7},{5,6},{6,5},{7,4},{8,11},{9,10},{10,... | collective-permute-start | bytes 1597448 | tf_op jit(solution)/shard_map/ppermute | solution.py:263
  17.9 4.0 %collective-permute-start = (bf16[16,2,2048]{2,1,0:T(2,128)(2,1)S(1)}, bf16[16,2,2048]{2,1,0:T(2,128)(2,1)S(1)}, u32[]{:S(2)}, u32[]{:S(2)}) collective-permute-start(bf16[16,2,2048]{2,1,0:T(2,128)(2,1)S(1)} %all_to_all.5.refs_3_.rows_ref._), channel_id=1, source_target_pairs={{0,1},{1,0},{2,3},{3,2},{4,5},{5,4},{6,7},{7,6},{8,9},{9,8},{10,11... | collective-permute-start | bytes 393224 | tf_op jit(solution)/shard_map/ppermute | solution.py:259
  18.3 16.6 %collective-permute-start.6 = (bf16[240,256]{1,0:T(8,128)(2,1)S(1)}, bf16[240,256]{1,0:T(8,128)(2,1)S(1)}, u32[]{:S(2)}, u32[]{:S(2)}) collective-permute-start(bf16[240,256]{1,0:T(8,128)(2,1)S(1)} %get-tuple-element.37), channel_id=1, source_target_pairs={{0,2},{1,3},{2,0},{3,1},{4,6},{5,7},{6,4},{7,5},{8,10},{9,11},{10,... | collective-permute-start | bytes 368648 | tf_op jit(solution)/shard_map/ppermute | solution.py:263
  21.9 11.9 %copy-start.7 = (f32[1,128]{1,0:T(1,128)S(1)}, f32[1,128]{1,0:T(1,128)}, u32[]{:S(2)}) copy-start(f32[1,128]{1,0:T(1,128)} %constant.2.clone.frequency_ref) | copy-start | bytes 1540
  24.0 7.3 %collective-permute-start.3 = (f32[4,2,2560]{2,1,0:T(2,128)S(1)}, f32[4,2,2560]{2,1,0:T(2,128)S(1)}, u32[]{:S(2)}, u32[]{:S(2)}) collective-permute-start(f32[4,2,2560]{2,1,0:T(2,128)S(1)} %get-tuple-element.33), channel_id=1, source_target_pairs={{0,12},{4,8},{8,4},{12,0},{1,13},{5,9},{9,5},{13,1},{2,14},{6,10},... | collective-permute-start | bytes 245768 | tf_op jit(solution)/shard_map/ppermute | solution.py:259
  25.8 8.1 %collective-permute-start.4 = (f32[4,2,2560]{2,1,0:T(2,128)S(1)}, f32[4,2,2560]{2,1,0:T(2,128)S(1)}, u32[]{:S(2)}, u32[]{:S(2)}) collective-permute-start(f32[4,2,2560]{2,1,0:T(2,128)S(1)} %get-tuple-element.34), channel_id=1, source_target_pairs={{0,8},{4,12},{8,0},{12,4},{1,9},{5,13},{9,1},{13,5},{2,10},{6,14},... | collective-permute-start | bytes 245768 | tf_op jit(solution)/shard_map/ppermute | solution.py:259
  25.8 8.1 %collective-permute-start.5 = (f32[4,2,2560]{2,1,0:T(2,128)S(1)}, f32[4,2,2560]{2,1,0:T(2,128)S(1)}, u32[]{:S(2)}, u32[]{:S(2)}) collective-permute-start(f32[4,2,2560]{2,1,0:T(2,128)S(1)} %get-tuple-element.35), channel_id=1, source_target_pairs={{0,4},{4,0},{8,12},{12,8},{1,5},{5,1},{9,13},{13,9},{2,6},{6,2},{1... | collective-permute-start | bytes 245768 | tf_op jit(solution)/shard_map/ppermute | solution.py:259
  33.9 8.6 %slice-start = ((s8[16777216]{0:T(1024)(128)(4,1)}), s8[4194304]{0:T(1024)(128)(4,1)S(1)}, s32[]{:S(2)}) async-start(s8[16777216]{0:T(1024)(128)(4,1)} %bitcast.2), calls=%async_computation.1 | async-start | bytes 8388608
  34.7 7.8 %slice-start.1 = ((s8[16777216]{0:T(1024)(128)(4,1)}), s8[4194304]{0:T(1024)(128)(4,1)S(1)}, s32[]{:S(2)}) async-start(s8[16777216]{0:T(1024)(128)(4,1)} %bitcast.2), calls=%async_computation.2 | async-start | bytes 8388608
  34.7 7.7 %slice-start.2 = ((s8[16777216]{0:T(1024)(128)(4,1)}), s8[4194304]{0:T(1024)(128)(4,1)S(1)}, s32[]{:S(2)}) async-start(s8[16777216]{0:T(1024)(128)(4,1)} %bitcast.2), calls=%async_computation.3 | async-start | bytes 8388608
  34.7 7.7 %slice-start.3 = ((s8[16777216]{0:T(1024)(128)(4,1)}), s8[4194304]{0:T(1024)(128)(4,1)S(1)}, s32[]{:S(2)}) async-start(s8[16777216]{0:T(1024)(128)(4,1)} %bitcast.2), calls=%async_computation.4 | async-start | bytes 8388608
  35.8 5.4 %collective-permute-start.10 = (bf16[4,2,2048]{2,1,0:T(2,128)(2,1)S(1)}, bf16[4,2,2048]{2,1,0:T(2,128)(2,1)S(1)}, u32[]{:S(2)}, u32[]{:S(2)}) collective-permute-start(bf16[4,2,2048]{2,1,0:T(2,128)(2,1)S(1)} %shard_map.109.refs_0_), channel_id=1, source_target_pairs={{0,8},{4,12},{8,0},{12,4},{1,9},{5,13},{9,1},{13,5},{2,10},{6,14},... | collective-permute-start | bytes 98312 | tf_op jit(solution)/shard_map/ppermute | solution.py:259
  36.6 5.8 %collective-permute-start.8 = (bf16[4,2,2048]{2,1,0:T(2,128)(2,1)S(1)}, bf16[4,2,2048]{2,1,0:T(2,128)(2,1)S(1)}, u32[]{:S(2)}, u32[]{:S(2)}) collective-permute-start(bf16[4,2,2048]{2,1,0:T(2,128)(2,1)S(1)} %shard_map.109.refs_0_), channel_id=1, source_target_pairs={{0,12},{4,8},{8,4},{12,0},{1,13},{5,9},{9,5},{13,1},{2,14},{6,10},... | collective-permute-start | bytes 98312 | tf_op jit(solution)/shard_map/ppermute | solution.py:259
  38.2 4.3 %collective-permute-start.9 = (bf16[4,2,2048]{2,1,0:T(2,128)(2,1)S(1)}, bf16[4,2,2048]{2,1,0:T(2,128)(2,1)S(1)}, u32[]{:S(2)}, u32[]{:S(2)}) collective-permute-start(bf16[4,2,2048]{2,1,0:T(2,128)(2,1)S(1)} %shard_map.109.refs_0_), channel_id=1, source_target_pairs={{0,4},{4,0},{8,12},{12,8},{1,5},{5,1},{9,13},{13,9},{2,6},{6,2},{1... | collective-permute-start | bytes 98312 | tf_op jit(solution)/shard_map/ppermute | solution.py:259
  44.0 2.2 %collective-permute-start.13 = (f32[8,2,2048]{2,1,0:T(2,128)S(1)}, f32[8,2,2048]{2,1,0:T(2,128)S(1)}, u32[]{:S(2)}, u32[]{:S(2)}) collective-permute-start(f32[8,2,2048]{2,1,0:T(2,128)S(1)} %get-tuple-element.44), channel_id=1, source_target_pairs={{0,1},{1,0},{2,3},{3,2},{4,5},{5,4},{6,7},{7,6},{8,9},{9,8},{10,11... | collective-permute-start | bytes 393224 | tf_op jit(solution)/shard_map/ppermute | solution.py:263
  45.7 2.0 %collective-permute-start.11 = (f32[8,2,2048]{2,1,0:T(2,128)S(1)}, f32[8,2,2048]{2,1,0:T(2,128)S(1)}, u32[]{:S(2)}, u32[]{:S(2)}) collective-permute-start(f32[8,2,2048]{2,1,0:T(2,128)S(1)} %get-tuple-element.40), channel_id=1, source_target_pairs={{0,1},{1,0},{2,3},{3,2},{4,5},{5,4},{6,7},{7,6},{8,9},{9,8},{10,11... | collective-permute-start | bytes 393224 | tf_op jit(solution)/shard_map/ppermute | solution.py:263
  46.2 4.7 %collective-permute-start.14 = (f32[4,2,2048]{2,1,0:T(2,128)S(1)}, f32[4,2,2048]{2,1,0:T(2,128)S(1)}, u32[]{:S(2)}, u32[]{:S(2)}) collective-permute-start(f32[4,2,2048]{2,1,0:T(2,128)S(1)} %get-tuple-element.46), channel_id=1, source_target_pairs={{0,2},{1,3},{2,0},{3,1},{4,6},{5,7},{6,4},{7,5},{8,10},{9,11},{10,... | collective-permute-start | bytes 196616 | tf_op jit(solution)/shard_map/ppermute | solution.py:263
  47.7 4.3 %collective-permute-start.12 = (f32[4,2,2048]{2,1,0:T(2,128)S(1)}, f32[4,2,2048]{2,1,0:T(2,128)S(1)}, u32[]{:S(2)}, u32[]{:S(2)}) collective-permute-start(f32[4,2,2048]{2,1,0:T(2,128)S(1)} %get-tuple-element.42), channel_id=1, source_target_pairs={{0,2},{1,3},{2,0},{3,1},{4,6},{5,7},{6,4},{7,5},{8,10},{9,11},{10,... | collective-permute-start | bytes 196616 | tf_op jit(solution)/shard_map/ppermute | solution.py:263
  52.1 4.7 %collective-permute-start.15 = (bf16[2,4096]{1,0:T(2,128)(2,1)S(1)}, bf16[2,4096]{1,0:T(2,128)(2,1)S(1)}, u32[]{:S(2)}, u32[]{:S(2)}) collective-permute-start(bf16[2,4096]{1,0:T(2,128)(2,1)S(1)} %get-tuple-element.47), channel_id=1, source_target_pairs={{0,8},{4,12},{8,0},{12,4},{1,9},{5,13},{9,1},{13,5},{2,10},{6,14},... | collective-permute-start | bytes 49160 | tf_op jit(solution)/shard_map/ppermute | solution.py:259
  53.4 5.5 %collective-permute-start.16 = (bf16[2,4096]{1,0:T(2,128)(2,1)S(1)}, bf16[2,4096]{1,0:T(2,128)(2,1)S(1)}, u32[]{:S(2)}, u32[]{:S(2)}) collective-permute-start(bf16[2,4096]{1,0:T(2,128)(2,1)S(1)} %get-tuple-element.48), channel_id=1, source_target_pairs={{0,12},{4,8},{8,4},{12,0},{1,13},{5,9},{9,5},{13,1},{2,14},{6,10},... | collective-permute-start | bytes 49160 | tf_op jit(solution)/shard_map/ppermute | solution.py:259
  55.3 3.8 %collective-permute-start.17 = (bf16[2,4096]{1,0:T(2,128)(2,1)S(1)}, bf16[2,4096]{1,0:T(2,128)(2,1)S(1)}, u32[]{:S(2)}, u32[]{:S(2)}) collective-permute-start(bf16[2,4096]{1,0:T(2,128)(2,1)S(1)} %get-tuple-element.49), channel_id=1, source_target_pairs={{0,4},{4,0},{8,12},{12,8},{1,5},{5,1},{9,13},{13,9},{2,6},{6,2},{1... | collective-permute-start | bytes 49160 | tf_op jit(solution)/shard_map/ppermute | solution.py:259

commit v25 on v24

--- a/solution.py
+++ b/solution.py
@@ -242,7 +242,7 @@
 
 def finish_kernel(*refs):
     result_ref = refs[-1]
-    order = [*sequence(len(refs) - 1), 0]
+    order = range(len(refs) - 2, -1, -1)
     blocks = [refs[order.index(k)] for k in range(len(order))]
     own = lax.axis_index("gx")
     cols = blocks[0].shape[-1]
@@ -442,7 +442,7 @@
         in_specs=[IN_VMEM] * wide,
         out_specs=IN_VMEM,
         compiler_params=params(8),
-    )(*[blocks[k] for k in [*sequence(wide), 0]])
+    )(*blocks[::-1])
 
 
 def solution(mesh):

time: 59.9 us -> 59.6 us (level)
  waiting for transfers between devices: 15.5 us -> 14.3 us
  starting transfers between devices: 19.8 us -> 20.7 us
    ppermute x10, waiting for transfers between devices: 11.9 us -> 10.7 us  [swap_pairs(): lax.ppermute(value, axis, [(i, i ^ step) for i in range(lax.axis_size(axi...]
    ppermute x10, starting transfers between devices: 12 us -> 12.9 us  [swap_pairs(): lax.ppermute(value, axis, [(i, i ^ step) for i in range(lax.axis_size(axi...]
  transfers between devices with their start and end apart: 18 -> 18, of which waited for: 10 -> 9; matrix products, arithmetic and copies ran while one was open for 0% -> 0% of each run, Pallas kernels for 11% -> 11%
where the time goes in v25:
time: 59.6 us; the launch traced here: 59.4 us
  starting transfers between devices  20.7 us (35%)
  waiting for transfers between devices  14.3 us (24%)
  blocking collectives  13 us (22%)
  Pallas kernels  9.97 us (17%)
  local copies, waits for them, and re-layouts  1.27 us (2%)
    all_to_all x1, blocking collectives, swap_blocks(): return lax.all_to_all(blocks, axes, split_axis=0, concat_axis=0, tiled=True)  13 us
    ppermute x10, starting transfers between devices, swap_pairs(): lax.ppermute(value, axis, [(i, i ^ step) for i in range(lax.axis_size(axi...  12.9 us
    ppermute x10, waiting for transfers between devices, swap_pairs(): lax.ppermute(value, axis, [(i, i ^ step) for i in range(lax.axis_size(axi...  10.7 us
    ppermute x8, starting transfers between devices, swap_plane(): lax.ppermute(value, PLANE, [(i, i ^ step) for i in range(lax.axis_size(PL...  7.79 us
    ppermute x8, waiting for transfers between devices, swap_plane(): lax.ppermute(value, PLANE, [(i, i ^ step) for i in range(lax.axis_size(PL...  3.56 us
    pallas_call x2, Pallas kernels, shards(): pl.pallas_call(functools.partial(output_kernel, p * part_cols, part_cols,...  3.09 us
    pallas_call x1, Pallas kernels, shards(): pl.pallas_call(functools.partial(project_kernel, False, wide, plane), out...  1.98 us
    pallas_call x1, Pallas kernels, shards(): pl.pallas_call(functools.partial(project_kernel, True, wide, plane), out_...  1.9 us
  transfers between devices with their start and end apart: 18, of which 9 were waited for; matrix products, arithmetic and copies ran while one was open for 0% of the time, Pallas kernels for 11%

profile of v25, /device:TPU:0, one launch (start us, length us, event | category | flops | bytes accessed | tf_op | source)
XLA Modules:
  0.0 59.4 jit_solution(4599131478061797804)
XLA Ops:
  0.0 0.0 copy-start.1
  0.0 0.0 copy-start.2
  0.0 0.0 copy-start.8
  0.0 1.0 %copy-done.8 = bf16[2,16384]{1,0:T(2,128)(2,1)S(1)} copy-done((bf16[2,16384]{1,0:T(2,128)(2,1)S(1)}, bf16[2,16384]{1,0:T(2,128)(2,1)}, u32[]{:S(2)}) %copy-start.8) | copy-done | bytes 65560
  1.0 0.2 shard_map.100.scaled_ref
  1.3 0.0 copy-done.5
  1.3 0.1 shard_map.101._
  1.4 0.0 copy-done.6
  1.4 0.0 copy-done.3
  1.4 0.2 copy-done.4
  1.6 0.2 shard_map.102
  1.8 3.0 %collective-permute-start.1 = (bf16[800,256]{1,0:T(8,128)(2,1)S(1)}, bf16[800,256]{1,0:T(8,128)(2,1)S(1)}, u32[]{:S(2)}, u32[]{:S(2)}) collective-permute-start(bf16[800,256]{1,0:T(8,128)(2,1)S(1)} %get-tuple-element.31), channel_id=1, source_target_pairs={{0,2},{1,3},{2,0},{3,1},{4,6},{5,7},{6,4},{7,5},{8,10},{9,11},{10,... | collective-permute-start | bytes 1228808 | tf_op jit(solution)/shard_map/ppermute | solution.py:263
  4.9 13.0 %all_to_all.5.refs_3_.rows_ref._ = bf16[16,2,2048]{2,1,0:T(2,128)(2,1)S(1)} all-to-all(bf16[16,2,2048]{2,1,0:T(2,128)(2,1)S(1)} %shard_map.101._), channel_id=1, replica_groups=mesh['groups'=2,'gx'=4,'gy'=2,'gz'=2] {'gx','gy','gz'}, dimensions={0} | all-to-all | bytes 262144 | tf_op jit(solution)/shard_map/all_to_all | solution.py:255
  17.8 0.0 collective-permute-done.1.refs_4_
  17.8 0.0 collective-permute-start.2
  17.8 0.1 collective-permute-start.7
  17.9 0.4 collective-permute-start
  18.3 1.7 %collective-permute-start.6 = (bf16[240,256]{1,0:T(8,128)(2,1)S(1)}, bf16[240,256]{1,0:T(8,128)(2,1)S(1)}, u32[]{:S(2)}, u32[]{:S(2)}) collective-permute-start(bf16[240,256]{1,0:T(8,128)(2,1)S(1)} %get-tuple-element.37), channel_id=1, source_target_pairs={{0,2},{1,3},{2,0},{3,1},{4,6},{5,7},{6,4},{7,5},{8,10},{9,11},{10,... | collective-permute-start | bytes 368648 | tf_op jit(solution)/shard_map/ppermute | solution.py:263
  20.0 0.0 copy-done
  20.0 0.0 copy-done.2
  20.0 1.9 %shard_map.104.refs_1_ = f32[32,2560]{1,0:T(8,128)S(1)} custom-call(bf16[16,2,2048]{2,1,0:T(2,128)(2,1)S(1)} %all_to_all.5.refs_3_.rows_ref._, bf16[4096,2048]{1,0:T(8,128)(2,1)S(1)} %copy-done, bf16[4096,256]{1,0:T(8,128)(2,1)S(1)} %copy-done.1, bf16[4096,256]{1,0:T(8,128)(2,1)S(1)} %copy-done.2), custom_call_target="tpu_custom_call" | custom-call | flops 335544320 | bytes 10485760 | tf_op jit(solution)/shard_map/pallas_call | solution.py:358
  21.9 0.0 collective-permute-done.rows_ref
  22.0 0.0 collective-permute-done.2.refs_0_.refs_5_.refs_7_
  22.0 2.0 %shard_map.105 = (f32[4,2,2560]{2,1,0:T(2,128)S(1)}, f32[4,2,2560]{2,1,0:T(2,128)S(1)}, f32[4,2,2560]{2,1,0:T(2,128)S(1)}, f32[4,2,2560]{2,1,0:T(2,128)S(1)}) custom-call(bf16[16,2,2048]{2,1,0:T(2,128)(2,1)S(1)} %collective-permute-done.rows_ref, bf16[4096,2048]{1,0:T(8,128)(2,1)S(1)} %copy-done, bf16[4096,256]{1,0:T(8,128)(2,1)S(1)} %copy-done.1, ...), custom_call_target="tpu_custom_call" | custom-call | flops 335544320 | bytes 10485760 | tf_op jit(solution)/shard_map/pallas_call | solution.py:366
  24.0 1.8 %collective-permute-start.3 = (f32[4,2,2560]{2,1,0:T(2,128)S(1)}, f32[4,2,2560]{2,1,0:T(2,128)S(1)}, u32[]{:S(2)}, u32[]{:S(2)}) collective-permute-start(f32[4,2,2560]{2,1,0:T(2,128)S(1)} %get-tuple-element.33), channel_id=1, source_target_pairs={{0,12},{4,8},{8,4},{12,0},{1,13},{5,9},{9,5},{13,1},{2,14},{6,10},... | collective-permute-start | bytes 245768 | tf_op jit(solution)/shard_map/ppermute | solution.py:259
  25.8 0.0 collective-permute-start.4
  25.8 2.6 %collective-permute-start.5 = (f32[4,2,2560]{2,1,0:T(2,128)S(1)}, f32[4,2,2560]{2,1,0:T(2,128)S(1)}, u32[]{:S(2)}, u32[]{:S(2)}) collective-permute-start(f32[4,2,2560]{2,1,0:T(2,128)S(1)} %get-tuple-element.35), channel_id=1, source_target_pairs={{0,4},{4,0},{8,12},{12,8},{1,5},{5,1},{9,13},{13,9},{2,6},{6,2},{1... | collective-permute-start | bytes 245768 | tf_op jit(solution)/shard_map/ppermute | solution.py:259
  28.4 0.1 shard_map.106.refs_4_.refs_6_
  28.5 2.7 %collective-permute-done.3.refs_0_ = f32[4,2,2560]{2,1,0:T(2,128)S(1)} collective-permute-done((f32[4,2,2560]{2,1,0:T(2,128)S(1)}, f32[4,2,2560]{2,1,0:T(2,128)S(1)}, u32[]{:S(2)}, u32[]{:S(2)}) %collective-permute-start.3) | collective-permute-done | bytes 81952 | tf_op jit(solution)/shard_map/ppermute | solution.py:259
  31.2 2.6 %collective-permute-done.4.refs_1_ = f32[4,2,2560]{2,1,0:T(2,128)S(1)} collective-permute-done((f32[4,2,2560]{2,1,0:T(2,128)S(1)}, f32[4,2,2560]{2,1,0:T(2,128)S(1)}, u32[]{:S(2)}, u32[]{:S(2)}) %collective-permute-start.4) | collective-permute-done | bytes 81952 | tf_op jit(solution)/shard_map/ppermute | solution.py:259
  33.8 0.0 collective-permute-done.5.refs_2_
  33.9 0.8 %shard_map.107.refs_0_ = bf16[2,2,2048]{2,1,0:T(2,128)(2,1)S(1)} custom-call(f32[1,128]{1,0:T(1,128)S(1)} %copy-done.7, f32[4,2,2560]{2,1,0:T(2,128)S(1)} %collective-permute-done.3.refs_0_, f32[4,2,2560]{2,1,0:T(2,128)S(1)} %collective-permute-done.4.refs_1_, f32[4,2,2560]{2,1,0:T(2,128)S(1)} %collective-permute-done.5.refs_2_, ...), custom_call_target="tpu_custom_call" | custom-call | flops 1 | bytes 1 | tf_op jit(solution)/shard_map/pallas_call | solution.py:384
  34.7 0.0 slice-start.1
  34.7 0.0 slice-start.2
  34.7 0.0 slice-start.3
  34.7 0.2 collective-permute-done.6.refs_5_
  34.9 0.0 collective-permute-done.7.refs_8_
  34.9 0.8 %shard_map.108.refs_1_ = bf16[2,2,2048]{2,1,0:T(2,128)(2,1)S(1)} custom-call(f32[1,128]{1,0:T(1,128)S(1)} %copy-done.7, f32[4,2,2560]{2,1,0:T(2,128)S(1)} %collective-permute-done.3.refs_0_, f32[4,2,2560]{2,1,0:T(2,128)S(1)} %collective-permute-done.4.refs_1_, f32[4,2,2560]{2,1,0:T(2,128)S(1)} %collective-permute-done.5.refs_2_, ...), custom_call_target="tpu_custom_call" | custom-call | flops 10000000000 | bytes 4194304 | tf_op jit(solution)/shard_map/pallas_call | solution.py:384
  35.8 0.8 %collective-permute-start.10 = (bf16[4,2,2048]{2,1,0:T(2,128)(2,1)S(1)}, bf16[4,2,2048]{2,1,0:T(2,128)(2,1)S(1)}, u32[]{:S(2)}, u32[]{:S(2)}) collective-permute-start(bf16[4,2,2048]{2,1,0:T(2,128)(2,1)S(1)} %shard_map.109.refs_0_), channel_id=1, source_target_pairs={{0,8},{4,12},{8,0},{12,4},{1,9},{5,13},{9,1},{13,5},{2,10},{6,14},... | collective-permute-start | bytes 98312 | tf_op jit(solution)/shard_map/ppermute | solution.py:259
  36.6 1.6 %collective-permute-start.8 = (bf16[4,2,2048]{2,1,0:T(2,128)(2,1)S(1)}, bf16[4,2,2048]{2,1,0:T(2,128)(2,1)S(1)}, u32[]{:S(2)}, u32[]{:S(2)}) collective-permute-start(bf16[4,2,2048]{2,1,0:T(2,128)(2,1)S(1)} %shard_map.109.refs_0_), channel_id=1, source_target_pairs={{0,12},{4,8},{8,4},{12,0},{1,13},{5,9},{9,5},{13,1},{2,14},{6,10},... | collective-permute-start | bytes 98312 | tf_op jit(solution)/shard_map/ppermute | solution.py:259
  38.2 1.2 %collective-permute-start.9 = (bf16[4,2,2048]{2,1,0:T(2,128)(2,1)S(1)}, bf16[4,2,2048]{2,1,0:T(2,128)(2,1)S(1)}, u32[]{:S(2)}, u32[]{:S(2)}) collective-permute-start(bf16[4,2,2048]{2,1,0:T(2,128)(2,1)S(1)} %shard_map.109.refs_0_), channel_id=1, source_target_pairs={{0,4},{4,0},{8,12},{12,8},{1,5},{5,1},{9,13},{13,9},{2,6},{6,2},{1... | collective-permute-start | bytes 98312 | tf_op jit(solution)/shard_map/ppermute | solution.py:259
  39.3 1.8 %collective-permute-done.10.refs_3_ = bf16[4,2,2048]{2,1,0:T(2,128)(2,1)S(1)} collective-permute-done((bf16[4,2,2048]{2,1,0:T(2,128)(2,1)S(1)}, bf16[4,2,2048]{2,1,0:T(2,128)(2,1)S(1)}, u32[]{:S(2)}, u32[]{:S(2)}) %collective-permute-start.10) | collective-permute-done | bytes 32800 | tf_op jit(solution)/shard_map/ppermute | solution.py:259
  41.1 1.3 %collective-permute-done.8.refs_1_ = bf16[4,2,2048]{2,1,0:T(2,128)(2,1)S(1)} collective-permute-done((bf16[4,2,2048]{2,1,0:T(2,128)(2,1)S(1)}, bf16[4,2,2048]{2,1,0:T(2,128)(2,1)S(1)}, u32[]{:S(2)}, u32[]{:S(2)}) %collective-permute-start.8) | collective-permute-done | bytes 32800 | tf_op jit(solution)/shard_map/ppermute | solution.py:259
  42.4 0.0 collective-permute-done.9.refs_2_
  42.4 0.0 slice-done
  42.4 0.0 slice-done.2
  42.5 1.5 %shard_map.112 = (f32[8,2,2048]{2,1,0:T(2,128)S(1)}, f32[8,2,2048]{2,1,0:T(2,128)S(1)}) custom-call(bf16[2048,4096]{1,0:T(8,128)(2,1)S(1)} %bitcast.3, bf16[4,2,2048]{2,1,0:T(2,128)(2,1)S(1)} %shard_map.109.refs_0_, bf16[4,2,2048]{2,1,0:T(2,128)(2,1)S(1)} %collective-permute-done.8.refs_1_, bf16[4,2,2048]{2,1,0:T(2,128)(2,1)S(1)} %collective-permute-done.9.refs_2_, ...), custom_call_target="tpu_custom_call" | custom-call | flops 268435456 | bytes 8388608 | tf_op jit(solution)/shard_map/pallas_call | solution.py:408
  44.0 0.1 collective-permute-start.13
  44.1 1.5 %shard_map.110 = (f32[8,2,2048]{2,1,0:T(2,128)S(1)}, f32[8,2,2048]{2,1,0:T(2,128)S(1)}) custom-call(bf16[2048,4096]{1,0:T(8,128)(2,1)S(1)} %bitcast.3, bf16[4,2,2048]{2,1,0:T(2,128)(2,1)S(1)} %shard_map.109.refs_0_, bf16[4,2,2048]{2,1,0:T(2,128)(2,1)S(1)} %collective-permute-done.8.refs_1_, bf16[4,2,2048]{2,1,0:T(2,128)(2,1)S(1)} %collective-permute-done.9.refs_2_, ...), custom_call_target="tpu_custom_call" | custom-call | flops 268435456 | bytes 8388608 | tf_op jit(solution)/shard_map/pallas_call | solution.py:408
  45.7 0.6 collective-permute-start.11
  46.2 0.0 collective-permute-done.13.b_ref
  46.2 1.4 %collective-permute-start.14 = (f32[4,2,2048]{2,1,0:T(2,128)S(1)}, f32[4,2,2048]{2,1,0:T(2,128)S(1)}, u32[]{:S(2)}, u32[]{:S(2)}) collective-permute-start(f32[4,2,2048]{2,1,0:T(2,128)S(1)} %get-tuple-element.46), channel_id=1, source_target_pairs={{0,2},{1,3},{2,0},{3,1},{4,6},{5,7},{6,4},{7,5},{8,10},{9,11},{10,... | collective-permute-start | bytes 196616 | tf_op jit(solution)/shard_map/ppermute | solution.py:263
  47.7 0.0 collective-permute-done.11.b_ref
  47.7 1.0 %collective-permute-start.12 = (f32[4,2,2048]{2,1,0:T(2,128)S(1)}, f32[4,2,2048]{2,1,0:T(2,128)S(1)}, u32[]{:S(2)}, u32[]{:S(2)}) collective-permute-start(f32[4,2,2048]{2,1,0:T(2,128)S(1)} %get-tuple-element.42), channel_id=1, source_target_pairs={{0,2},{1,3},{2,0},{3,1},{4,6},{5,7},{6,4},{7,5},{8,10},{9,11},{10,... | collective-permute-start | bytes 196616 | tf_op jit(solution)/shard_map/ppermute | solution.py:263
  48.7 2.3 %collective-permute-done.14.refs_3_ = f32[4,2,2048]{2,1,0:T(2,128)S(1)} collective-permute-done((f32[4,2,2048]{2,1,0:T(2,128)S(1)}, f32[4,2,2048]{2,1,0:T(2,128)S(1)}, u32[]{:S(2)}, u32[]{:S(2)}) %collective-permute-start.14) | collective-permute-done | bytes 65568 | tf_op jit(solution)/shard_map/ppermute | solution.py:263
  51.0 1.0 %collective-permute-done.12.refs_1_ = f32[4,2,2048]{2,1,0:T(2,128)S(1)} collective-permute-done((f32[4,2,2048]{2,1,0:T(2,128)S(1)}, f32[4,2,2048]{2,1,0:T(2,128)S(1)}, u32[]{:S(2)}, u32[]{:S(2)}) %collective-permute-start.12) | collective-permute-done | bytes 65568 | tf_op jit(solution)/shard_map/ppermute | solution.py:263
  52.0 0.1 shard_map.114
  52.1 2.1 %collective-permute-start.15 = (bf16[2,4096]{1,0:T(2,128)(2,1)S(1)}, bf16[2,4096]{1,0:T(2,128)(2,1)S(1)}, u32[]{:S(2)}, u32[]{:S(2)}) collective-permute-start(bf16[2,4096]{1,0:T(2,128)(2,1)S(1)} %get-tuple-element.47), channel_id=1, source_target_pairs={{0,12},{4,8},{8,4},{12,0},{1,13},{5,9},{9,5},{13,1},{2,14},{6,10},... | collective-permute-start | bytes 49160 | tf_op jit(solution)/shard_map/ppermute | solution.py:259
  54.2 0.2 collective-permute-start.16
  54.4 2.2 %collective-permute-start.17 = (bf16[2,4096]{1,0:T(2,128)(2,1)S(1)}, bf16[2,4096]{1,0:T(2,128)(2,1)S(1)}, u32[]{:S(2)}, u32[]{:S(2)}) collective-permute-start(bf16[2,4096]{1,0:T(2,128)(2,1)S(1)} %get-tuple-element.49), channel_id=1, source_target_pairs={{0,4},{4,0},{8,12},{12,8},{1,5},{5,1},{9,13},{13,9},{2,6},{6,2},{1... | collective-permute-start | bytes 49160 | tf_op jit(solution)/shard_map/ppermute | solution.py:259
  56.5 1.3 %collective-permute-done.15.refs_0_ = bf16[2,4096]{1,0:T(2,128)(2,1)S(1)} collective-permute-done((bf16[2,4096]{1,0:T(2,128)(2,1)S(1)}, bf16[2,4096]{1,0:T(2,128)(2,1)S(1)}, u32[]{:S(2)}, u32[]{:S(2)}) %collective-permute-start.15) | collective-permute-done | bytes 16416 | tf_op jit(solution)/shard_map/ppermute | solution.py:259
  57.8 0.9 %collective-permute-done.16.refs_1_ = bf16[2,4096]{1,0:T(2,128)(2,1)S(1)} collective-permute-done((bf16[2,4096]{1,0:T(2,128)(2,1)S(1)}, bf16[2,4096]{1,0:T(2,128)(2,1)S(1)}, u32[]{:S(2)}, u32[]{:S(2)}) %collective-permute-start.16) | collective-permute-done | bytes 16416 | tf_op jit(solution)/shard_map/ppermute | solution.py:259
  58.8 0.0 collective-permute-done.17.refs_2_
  58.8 0.6 %shard_map.115 = bf16[2,16384]{1,0:T(2,128)(2,1)} custom-call(bf16[2,4096]{1,0:T(2,128)(2,1)S(1)} %collective-permute-done.15.refs_0_, bf16[2,4096]{1,0:T(2,128)(2,1)S(1)} %collective-permute-done.16.refs_1_, bf16[2,4096]{1,0:T(2,128)(2,1)S(1)} %collective-permute-done.17.refs_2_, bf16[2,4096]{1,0:T(2,128)(2,1)S(1)} %get-tuple-element.50.refs_3_), custom_call_target="tpu_custom_call" | custom-call | tf_op jit(solution)/shard_map/pallas_call | solution.py:439
  (16 shorter events, 0.1 us)
Async XLA Ops:
  0.0 1.3 %copy-start.5 = (f32[16384]{0:T(1024)S(1)}, f32[16384]{0:T(1024)}, u32[]{:S(2)}) copy-start(f32[16384]{0:T(1024)} %param.11) | copy-start | bytes 196612
  0.0 1.4 %copy-start.6 = (s32[2]{0:T(128)S(1)}, s32[2]{0:T(128)}, u32[]{:S(2)}) copy-start(s32[2]{0:T(128)} %param.18) | copy-start | bytes 28
  0.0 1.4 %copy-start.3 = (bf16[2,256,1024]{2,1,0:T(8,128)(2,1)S(1)}, bf16[2,256,1024]{2,1,0:T(8,128)(2,1)}, u32[]{:S(2)}) copy-start(bf16[2,256,1024]{2,1,0:T(8,128)(2,1)} %keys_ref.3) | copy-start | bytes 3145732
  0.0 1.6 %copy-start.4 = (bf16[2,256,1024]{2,1,0:T(8,128)(2,1)S(1)}, bf16[2,256,1024]{2,1,0:T(8,128)(2,1)}, u32[]{:S(2)}) copy-start(bf16[2,256,1024]{2,1,0:T(8,128)(2,1)} %values_ref.3) | copy-start | bytes 3145732
  0.0 20.0 %copy-start = (bf16[4096,2048]{1,0:T(8,128)(2,1)S(1)}, bf16[4096,2048]{1,0:T(8,128)(2,1)}, u32[]{:S(2)}) copy-start(bf16[4096,2048]{1,0:T(8,128)(2,1)} %query_ref.3) | copy-start | bytes 50331652
  0.0 20.0 %copy-start.1 = (bf16[4096,256]{1,0:T(8,128)(2,1)S(1)}, bf16[4096,256]{1,0:T(8,128)(2,1)}, u32[]{:S(2)}) copy-start(bf16[4096,256]{1,0:T(8,128)(2,1)} %key_ref.3) | copy-start | bytes 6291460
  0.0 20.0 %copy-start.2 = (bf16[4096,256]{1,0:T(8,128)(2,1)S(1)}, bf16[4096,256]{1,0:T(8,128)(2,1)}, u32[]{:S(2)}) copy-start(bf16[4096,256]{1,0:T(8,128)(2,1)} %value_ref.3) | copy-start | bytes 6291460
  0.0 1.0 %copy-start.8 = (bf16[2,16384]{1,0:T(2,128)(2,1)S(1)}, bf16[2,16384]{1,0:T(2,128)(2,1)}, u32[]{:S(2)}) copy-start(bf16[2,16384]{1,0:T(2,128)(2,1)} %tokens_ref.1) | copy-start | bytes 196612
  1.8 16.0 %collective-permute-start.1 = (bf16[800,256]{1,0:T(8,128)(2,1)S(1)}, bf16[800,256]{1,0:T(8,128)(2,1)S(1)}, u32[]{:S(2)}, u32[]{:S(2)}) collective-permute-start(bf16[800,256]{1,0:T(8,128)(2,1)S(1)} %get-tuple-element.31), channel_id=1, source_target_pairs={{0,2},{1,3},{2,0},{3,1},{4,6},{5,7},{6,4},{7,5},{8,10},{9,11},{10,... | collective-permute-start | bytes 1228808 | tf_op jit(solution)/shard_map/ppermute | solution.py:263
  17.8 4.1 %collective-permute-start.2 = (bf16[1040,256]{1,0:T(8,128)(2,1)S(1)}, bf16[1040,256]{1,0:T(8,128)(2,1)S(1)}, u32[]{:S(2)}, u32[]{:S(2)}) collective-permute-start(bf16[1040,256]{1,0:T(8,128)(2,1)S(1)} %get-tuple-element.32), channel_id=1, source_target_pairs={{0,1},{1,0},{2,3},{3,2},{4,5},{5,4},{6,7},{7,6},{8,9},{9,8},{10,11... | collective-permute-start | bytes 1597448 | tf_op jit(solution)/shard_map/ppermute | solution.py:263
  17.8 17.1 %collective-permute-start.7 = (bf16[1040,256]{1,0:T(8,128)(2,1)S(1)}, bf16[1040,256]{1,0:T(8,128)(2,1)S(1)}, u32[]{:S(2)}, u32[]{:S(2)}) collective-permute-start(bf16[1040,256]{1,0:T(8,128)(2,1)S(1)} %get-tuple-element.38), channel_id=1, source_target_pairs={{0,3},{1,2},{2,1},{3,0},{4,7},{5,6},{6,5},{7,4},{8,11},{9,10},{10,... | collective-permute-start | bytes 1597448 | tf_op jit(solution)/shard_map/ppermute | solution.py:263
  17.9 4.0 %collective-permute-start = (bf16[16,2,2048]{2,1,0:T(2,128)(2,1)S(1)}, bf16[16,2,2048]{2,1,0:T(2,128)(2,1)S(1)}, u32[]{:S(2)}, u32[]{:S(2)}) collective-permute-start(bf16[16,2,2048]{2,1,0:T(2,128)(2,1)S(1)} %all_to_all.5.refs_3_.rows_ref._), channel_id=1, source_target_pairs={{0,1},{1,0},{2,3},{3,2},{4,5},{5,4},{6,7},{7,6},{8,9},{9,8},{10,11... | collective-permute-start | bytes 393224 | tf_op jit(solution)/shard_map/ppermute | solution.py:259
  18.3 16.6 %collective-permute-start.6 = (bf16[240,256]{1,0:T(8,128)(2,1)S(1)}, bf16[240,256]{1,0:T(8,128)(2,1)S(1)}, u32[]{:S(2)}, u32[]{:S(2)}) collective-permute-start(bf16[240,256]{1,0:T(8,128)(2,1)S(1)} %get-tuple-element.37), channel_id=1, source_target_pairs={{0,2},{1,3},{2,0},{3,1},{4,6},{5,7},{6,4},{7,5},{8,10},{9,11},{10,... | collective-permute-start | bytes 368648 | tf_op jit(solution)/shard_map/ppermute | solution.py:263
  21.9 11.9 %copy-start.7 = (f32[1,128]{1,0:T(1,128)S(1)}, f32[1,128]{1,0:T(1,128)}, u32[]{:S(2)}) copy-start(f32[1,128]{1,0:T(1,128)} %constant.2.clone.frequency_ref) | copy-start | bytes 1540
  24.0 7.3 %collective-permute-start.3 = (f32[4,2,2560]{2,1,0:T(2,128)S(1)}, f32[4,2,2560]{2,1,0:T(2,128)S(1)}, u32[]{:S(2)}, u32[]{:S(2)}) collective-permute-start(f32[4,2,2560]{2,1,0:T(2,128)S(1)} %get-tuple-element.33), channel_id=1, source_target_pairs={{0,12},{4,8},{8,4},{12,0},{1,13},{5,9},{9,5},{13,1},{2,14},{6,10},... | collective-permute-start | bytes 245768 | tf_op jit(solution)/shard_map/ppermute | solution.py:259
  25.8 8.1 %collective-permute-start.4 = (f32[4,2,2560]{2,1,0:T(2,128)S(1)}, f32[4,2,2560]{2,1,0:T(2,128)S(1)}, u32[]{:S(2)}, u32[]{:S(2)}) collective-permute-start(f32[4,2,2560]{2,1,0:T(2,128)S(1)} %get-tuple-element.34), channel_id=1, source_target_pairs={{0,8},{4,12},{8,0},{12,4},{1,9},{5,13},{9,1},{13,5},{2,10},{6,14},... | collective-permute-start | bytes 245768 | tf_op jit(solution)/shard_map/ppermute | solution.py:259
  25.8 8.1 %collective-permute-start.5 = (f32[4,2,2560]{2,1,0:T(2,128)S(1)}, f32[4,2,2560]{2,1,0:T(2,128)S(1)}, u32[]{:S(2)}, u32[]{:S(2)}) collective-permute-start(f32[4,2,2560]{2,1,0:T(2,128)S(1)} %get-tuple-element.35), channel_id=1, source_target_pairs={{0,4},{4,0},{8,12},{12,8},{1,5},{5,1},{9,13},{13,9},{2,6},{6,2},{1... | collective-permute-start | bytes 245768 | tf_op jit(solution)/shard_map/ppermute | solution.py:259
  33.9 8.6 %slice-start = ((s8[16777216]{0:T(1024)(128)(4,1)}), s8[4194304]{0:T(1024)(128)(4,1)S(1)}, s32[]{:S(2)}) async-start(s8[16777216]{0:T(1024)(128)(4,1)} %bitcast.2), calls=%async_computation.1 | async-start | bytes 8388608
  34.7 7.8 %slice-start.1 = ((s8[16777216]{0:T(1024)(128)(4,1)}), s8[4194304]{0:T(1024)(128)(4,1)S(1)}, s32[]{:S(2)}) async-start(s8[16777216]{0:T(1024)(128)(4,1)} %bitcast.2), calls=%async_computation.2 | async-start | bytes 8388608
  34.7 7.7 %slice-start.2 = ((s8[16777216]{0:T(1024)(128)(4,1)}), s8[4194304]{0:T(1024)(128)(4,1)S(1)}, s32[]{:S(2)}) async-start(s8[16777216]{0:T(1024)(128)(4,1)} %bitcast.2), calls=%async_computation.3 | async-start | bytes 8388608
  34.7 7.7 %slice-start.3 = ((s8[16777216]{0:T(1024)(128)(4,1)}), s8[4194304]{0:T(1024)(128)(4,1)S(1)}, s32[]{:S(2)}) async-start(s8[16777216]{0:T(1024)(128)(4,1)} %bitcast.2), calls=%async_computation.4 | async-start | bytes 8388608
  35.8 5.4 %collective-permute-start.10 = (bf16[4,2,2048]{2,1,0:T(2,128)(2,1)S(1)}, bf16[4,2,2048]{2,1,0:T(2,128)(2,1)S(1)}, u32[]{:S(2)}, u32[]{:S(2)}) collective-permute-start(bf16[4,2,2048]{2,1,0:T(2,128)(2,1)S(1)} %shard_map.109.refs_0_), channel_id=1, source_target_pairs={{0,8},{4,12},{8,0},{12,4},{1,9},{5,13},{9,1},{13,5},{2,10},{6,14},... | collective-permute-start | bytes 98312 | tf_op jit(solution)/shard_map/ppermute | solution.py:259
  36.6 5.8 %collective-permute-start.8 = (bf16[4,2,2048]{2,1,0:T(2,128)(2,1)S(1)}, bf16[4,2,2048]{2,1,0:T(2,128)(2,1)S(1)}, u32[]{:S(2)}, u32[]{:S(2)}) collective-permute-start(bf16[4,2,2048]{2,1,0:T(2,128)(2,1)S(1)} %shard_map.109.refs_0_), channel_id=1, source_target_pairs={{0,12},{4,8},{8,4},{12,0},{1,13},{5,9},{9,5},{13,1},{2,14},{6,10},... | collective-permute-start | bytes 98312 | tf_op jit(solution)/shard_map/ppermute | solution.py:259
  38.2 4.3 %collective-permute-start.9 = (bf16[4,2,2048]{2,1,0:T(2,128)(2,1)S(1)}, bf16[4,2,2048]{2,1,0:T(2,128)(2,1)S(1)}, u32[]{:S(2)}, u32[]{:S(2)}) collective-permute-start(bf16[4,2,2048]{2,1,0:T(2,128)(2,1)S(1)} %shard_map.109.refs_0_), channel_id=1, source_target_pairs={{0,4},{4,0},{8,12},{12,8},{1,5},{5,1},{9,13},{13,9},{2,6},{6,2},{1... | collective-permute-start | bytes 98312 | tf_op jit(solution)/shard_map/ppermute | solution.py:259
  44.0 2.2 %collective-permute-start.13 = (f32[8,2,2048]{2,1,0:T(2,128)S(1)}, f32[8,2,2048]{2,1,0:T(2,128)S(1)}, u32[]{:S(2)}, u32[]{:S(2)}) collective-permute-start(f32[8,2,2048]{2,1,0:T(2,128)S(1)} %get-tuple-element.44), channel_id=1, source_target_pairs={{0,1},{1,0},{2,3},{3,2},{4,5},{5,4},{6,7},{7,6},{8,9},{9,8},{10,11... | collective-permute-start | bytes 393224 | tf_op jit(solution)/shard_map/ppermute | solution.py:263
  45.7 2.0 %collective-permute-start.11 = (f32[8,2,2048]{2,1,0:T(2,128)S(1)}, f32[8,2,2048]{2,1,0:T(2,128)S(1)}, u32[]{:S(2)}, u32[]{:S(2)}) collective-permute-start(f32[8,2,2048]{2,1,0:T(2,128)S(1)} %get-tuple-element.40), channel_id=1, source_target_pairs={{0,1},{1,0},{2,3},{3,2},{4,5},{5,4},{6,7},{7,6},{8,9},{9,8},{10,11... | collective-permute-start | bytes 393224 | tf_op jit(solution)/shard_map/ppermute | solution.py:263
  46.2 4.7 %collective-permute-start.14 = (f32[4,2,2048]{2,1,0:T(2,128)S(1)}, f32[4,2,2048]{2,1,0:T(2,128)S(1)}, u32[]{:S(2)}, u32[]{:S(2)}) collective-permute-start(f32[4,2,2048]{2,1,0:T(2,128)S(1)} %get-tuple-element.46), channel_id=1, source_target_pairs={{0,2},{1,3},{2,0},{3,1},{4,6},{5,7},{6,4},{7,5},{8,10},{9,11},{10,... | collective-permute-start | bytes 196616 | tf_op jit(solution)/shard_map/ppermute | solution.py:263
  47.7 4.3 %collective-permute-start.12 = (f32[4,2,2048]{2,1,0:T(2,128)S(1)}, f32[4,2,2048]{2,1,0:T(2,128)S(1)}, u32[]{:S(2)}, u32[]{:S(2)}) collective-permute-start(f32[4,2,2048]{2,1,0:T(2,128)S(1)} %get-tuple-element.42), channel_id=1, source_target_pairs={{0,2},{1,3},{2,0},{3,1},{4,6},{5,7},{6,4},{7,5},{8,10},{9,11},{10,... | collective-permute-start | bytes 196616 | tf_op jit(solution)/shard_map/ppermute | solution.py:263
  52.1 5.8 %collective-permute-start.15 = (bf16[2,4096]{1,0:T(2,128)(2,1)S(1)}, bf16[2,4096]{1,0:T(2,128)(2,1)S(1)}, u32[]{:S(2)}, u32[]{:S(2)}) collective-permute-start(bf16[2,4096]{1,0:T(2,128)(2,1)S(1)} %get-tuple-element.47), channel_id=1, source_target_pairs={{0,12},{4,8},{8,4},{12,0},{1,13},{5,9},{9,5},{13,1},{2,14},{6,10},... | collective-permute-start | bytes 49160 | tf_op jit(solution)/shard_map/ppermute | solution.py:259
  54.2 4.6 %collective-permute-start.16 = (bf16[2,4096]{1,0:T(2,128)(2,1)S(1)}, bf16[2,4096]{1,0:T(2,128)(2,1)S(1)}, u32[]{:S(2)}, u32[]{:S(2)}) collective-permute-start(bf16[2,4096]{1,0:T(2,128)(2,1)S(1)} %get-tuple-element.48), channel_id=1, source_target_pairs={{0,8},{4,12},{8,0},{12,4},{1,9},{5,13},{9,1},{13,5},{2,10},{6,14},... | collective-permute-start | bytes 49160 | tf_op jit(solution)/shard_map/ppermute | solution.py:259
  54.4 4.4 %collective-permute-start.17 = (bf16[2,4096]{1,0:T(2,128)(2,1)S(1)}, bf16[2,4096]{1,0:T(2,128)(2,1)S(1)}, u32[]{:S(2)}, u32[]{:S(2)}) collective-permute-start(bf16[2,4096]{1,0:T(2,128)(2,1)S(1)} %get-tuple-element.49), channel_id=1, source_target_pairs={{0,4},{4,0},{8,12},{12,8},{1,5},{5,1},{9,13},{13,9},{2,6},{6,2},{1... | collective-permute-start | bytes 49160 | tf_op jit(solution)/shard_map/ppermute | solution.py:259

commit v26 on v25

--- a/solution.py
+++ b/solution.py
@@ -17,7 +17,7 @@
 
 
 def sequence(wide):
-    return sorted(range(1, wide), key=lambda k: (k != wide // 2, -k))
+    return list(range(wide - 1, 0, -1))
 
 
 def scale_kernel(tokens_ref, scaled_ref):

time: 59.6 us -> 59.8 us (level)
  starting transfers between devices: 20.7 us -> 21.7 us
  waiting for transfers between devices: 14.3 us -> 13.5 us
    ppermute x10, starting transfers between devices: 12.9 us -> 13.8 us  [swap_pairs(): lax.ppermute(value, axis, [(i, i ^ step) for i in range(lax.axis_size(axi...]
    ppermute x10, waiting for transfers between devices: 10.7 us -> 9.98 us  [swap_pairs(): lax.ppermute(value, axis, [(i, i ^ step) for i in range(lax.axis_size(axi...]
  transfers between devices with their start and end apart: 18 -> 18, of which waited for: 9 -> 10; matrix products, arithmetic and copies ran while one was open for 0% -> 0% of each run, Pallas kernels for 11% -> 11%
where the time goes in v26:
time: 59.8 us; the launch traced here: 59.6 us
  starting transfers between devices  21.7 us (36%)
  waiting for transfers between devices  13.5 us (23%)
  blocking collectives  13 us (22%)
  Pallas kernels  9.96 us (17%)
  local copies, waits for them, and re-layouts  1.27 us (2%)
    ppermute x10, starting transfers between devices, swap_pairs(): lax.ppermute(value, axis, [(i, i ^ step) for i in range(lax.axis_size(axi...  13.8 us
    all_to_all x1, blocking collectives, swap_blocks(): return lax.all_to_all(blocks, axes, split_axis=0, concat_axis=0, tiled=True)  13 us
    ppermute x10, waiting for transfers between devices, swap_pairs(): lax.ppermute(value, axis, [(i, i ^ step) for i in range(lax.axis_size(axi...  9.98 us
    ppermute x8, starting transfers between devices, swap_plane(): lax.ppermute(value, PLANE, [(i, i ^ step) for i in range(lax.axis_size(PL...  7.86 us
    ppermute x8, waiting for transfers between devices, swap_plane(): lax.ppermute(value, PLANE, [(i, i ^ step) for i in range(lax.axis_size(PL...  3.56 us
    pallas_call x2, Pallas kernels, shards(): pl.pallas_call(functools.partial(output_kernel, p * part_cols, part_cols,...  3.09 us
    pallas_call x1, Pallas kernels, shards(): pl.pallas_call(functools.partial(project_kernel, False, wide, plane), out...  1.98 us
    pallas_call x1, Pallas kernels, shards(): pl.pallas_call(functools.partial(project_kernel, True, wide, plane), out_...  1.9 us
  transfers between devices with their start and end apart: 18, of which 10 were waited for; matrix products, arithmetic and copies ran while one was open for 0% of the time, Pallas kernels for 11%

profile of v26, /device:TPU:0, one launch (start us, length us, event | category | flops | bytes accessed | tf_op | source)
XLA Modules:
  0.0 59.6 jit_solution(11808347993817378844)
XLA Ops:
  0.0 0.0 copy-start.1
  0.0 0.0 copy-start.2
  0.0 0.0 copy-start.8
  0.0 1.0 %copy-done.8 = bf16[2,16384]{1,0:T(2,128)(2,1)S(1)} copy-done((bf16[2,16384]{1,0:T(2,128)(2,1)S(1)}, bf16[2,16384]{1,0:T(2,128)(2,1)}, u32[]{:S(2)}) %copy-start.8) | copy-done | bytes 65560
  1.0 0.2 shard_map.100.scaled_ref
  1.3 0.0 copy-done.5
  1.3 0.1 shard_map.101._
  1.4 0.0 copy-done.6
  1.4 0.0 copy-done.3
  1.4 0.2 copy-done.4
  1.6 0.2 shard_map.102
  1.8 3.0 %collective-permute-start.1 = (bf16[800,256]{1,0:T(8,128)(2,1)S(1)}, bf16[800,256]{1,0:T(8,128)(2,1)S(1)}, u32[]{:S(2)}, u32[]{:S(2)}) collective-permute-start(bf16[800,256]{1,0:T(8,128)(2,1)S(1)} %get-tuple-element.31), channel_id=1, source_target_pairs={{0,2},{1,3},{2,0},{3,1},{4,6},{5,7},{6,4},{7,5},{8,10},{9,11},{10,... | collective-permute-start | bytes 1228808 | tf_op jit(solution)/shard_map/ppermute | solution.py:263
  4.9 13.0 %all_to_all.5.refs_3_.rows_ref._ = bf16[16,2,2048]{2,1,0:T(2,128)(2,1)S(1)} all-to-all(bf16[16,2,2048]{2,1,0:T(2,128)(2,1)S(1)} %shard_map.101._), channel_id=1, replica_groups=mesh['groups'=2,'gx'=4,'gy'=2,'gz'=2] {'gx','gy','gz'}, dimensions={0} | all-to-all | bytes 262144 | tf_op jit(solution)/shard_map/all_to_all | solution.py:255
  17.8 0.0 collective-permute-done.1.refs_4_
  17.8 0.0 collective-permute-start.2
  17.8 0.1 collective-permute-start.7
  17.9 0.4 collective-permute-start
  18.3 1.7 %collective-permute-start.6 = (bf16[240,256]{1,0:T(8,128)(2,1)S(1)}, bf16[240,256]{1,0:T(8,128)(2,1)S(1)}, u32[]{:S(2)}, u32[]{:S(2)}) collective-permute-start(bf16[240,256]{1,0:T(8,128)(2,1)S(1)} %get-tuple-element.37), channel_id=1, source_target_pairs={{0,2},{1,3},{2,0},{3,1},{4,6},{5,7},{6,4},{7,5},{8,10},{9,11},{10,... | collective-permute-start | bytes 368648 | tf_op jit(solution)/shard_map/ppermute | solution.py:263
  20.0 0.0 copy-done
  20.0 0.0 copy-done.1
  20.0 0.0 copy-done.2
  20.0 1.9 %shard_map.104.refs_1_ = f32[32,2560]{1,0:T(8,128)S(1)} custom-call(bf16[16,2,2048]{2,1,0:T(2,128)(2,1)S(1)} %all_to_all.5.refs_3_.rows_ref._, bf16[4096,2048]{1,0:T(8,128)(2,1)S(1)} %copy-done, bf16[4096,256]{1,0:T(8,128)(2,1)S(1)} %copy-done.1, bf16[4096,256]{1,0:T(8,128)(2,1)S(1)} %copy-done.2), custom_call_target="tpu_custom_call" | custom-call | flops 335544320 | bytes 10485760 | tf_op jit(solution)/shard_map/pallas_call | solution.py:358
  21.9 0.0 collective-permute-done.rows_ref
  22.0 0.0 collective-permute-done.2.refs_0_.refs_5_.refs_7_
  22.0 2.0 %shard_map.105 = (f32[4,2,2560]{2,1,0:T(2,128)S(1)}, f32[4,2,2560]{2,1,0:T(2,128)S(1)}, f32[4,2,2560]{2,1,0:T(2,128)S(1)}, f32[4,2,2560]{2,1,0:T(2,128)S(1)}) custom-call(bf16[16,2,2048]{2,1,0:T(2,128)(2,1)S(1)} %collective-permute-done.rows_ref, bf16[4096,2048]{1,0:T(8,128)(2,1)S(1)} %copy-done, bf16[4096,256]{1,0:T(8,128)(2,1)S(1)} %copy-done.1, ...), custom_call_target="tpu_custom_call" | custom-call | flops 335544320 | bytes 10485760 | tf_op jit(solution)/shard_map/pallas_call | solution.py:366
  24.0 1.8 %collective-permute-start.3 = (f32[4,2,2560]{2,1,0:T(2,128)S(1)}, f32[4,2,2560]{2,1,0:T(2,128)S(1)}, u32[]{:S(2)}, u32[]{:S(2)}) collective-permute-start(f32[4,2,2560]{2,1,0:T(2,128)S(1)} %get-tuple-element.33), channel_id=1, source_target_pairs={{0,12},{4,8},{8,4},{12,0},{1,13},{5,9},{9,5},{13,1},{2,14},{6,10},... | collective-permute-start | bytes 245768 | tf_op jit(solution)/shard_map/ppermute | solution.py:259
  25.8 0.0 collective-permute-start.4
  25.8 2.6 %collective-permute-start.5 = (f32[4,2,2560]{2,1,0:T(2,128)S(1)}, f32[4,2,2560]{2,1,0:T(2,128)S(1)}, u32[]{:S(2)}, u32[]{:S(2)}) collective-permute-start(f32[4,2,2560]{2,1,0:T(2,128)S(1)} %get-tuple-element.35), channel_id=1, source_target_pairs={{0,4},{4,0},{8,12},{12,8},{1,5},{5,1},{9,13},{13,9},{2,6},{6,2},{1... | collective-permute-start | bytes 245768 | tf_op jit(solution)/shard_map/ppermute | solution.py:259
  28.4 0.1 shard_map.106.refs_4_.refs_6_
  28.5 2.7 %collective-permute-done.3.refs_0_ = f32[4,2,2560]{2,1,0:T(2,128)S(1)} collective-permute-done((f32[4,2,2560]{2,1,0:T(2,128)S(1)}, f32[4,2,2560]{2,1,0:T(2,128)S(1)}, u32[]{:S(2)}, u32[]{:S(2)}) %collective-permute-start.3) | collective-permute-done | bytes 81952 | tf_op jit(solution)/shard_map/ppermute | solution.py:259
  31.2 2.6 %collective-permute-done.4.refs_1_ = f32[4,2,2560]{2,1,0:T(2,128)S(1)} collective-permute-done((f32[4,2,2560]{2,1,0:T(2,128)S(1)}, f32[4,2,2560]{2,1,0:T(2,128)S(1)}, u32[]{:S(2)}, u32[]{:S(2)}) %collective-permute-start.4) | collective-permute-done | bytes 81952 | tf_op jit(solution)/shard_map/ppermute | solution.py:259
  33.8 0.0 collective-permute-done.5.refs_2_
  33.9 0.0 copy-done.7
  33.9 0.8 %shard_map.107.refs_0_ = bf16[2,2,2048]{2,1,0:T(2,128)(2,1)S(1)} custom-call(f32[1,128]{1,0:T(1,128)S(1)} %copy-done.7, f32[4,2,2560]{2,1,0:T(2,128)S(1)} %collective-permute-done.3.refs_0_, f32[4,2,2560]{2,1,0:T(2,128)S(1)} %collective-permute-done.4.refs_1_, f32[4,2,2560]{2,1,0:T(2,128)S(1)} %collective-permute-done.5.refs_2_, ...), custom_call_target="tpu_custom_call" | custom-call | flops 1 | bytes 1 | tf_op jit(solution)/shard_map/pallas_call | solution.py:384
  34.7 0.0 slice-start.1
  34.7 0.0 slice-start.2
  34.7 0.0 slice-start.3
  34.7 0.2 collective-permute-done.6.refs_5_
  34.9 0.0 collective-permute-done.7.refs_8_
  34.9 0.8 %shard_map.108.refs_1_ = bf16[2,2,2048]{2,1,0:T(2,128)(2,1)S(1)} custom-call(f32[1,128]{1,0:T(1,128)S(1)} %copy-done.7, f32[4,2,2560]{2,1,0:T(2,128)S(1)} %collective-permute-done.3.refs_0_, f32[4,2,2560]{2,1,0:T(2,128)S(1)} %collective-permute-done.4.refs_1_, f32[4,2,2560]{2,1,0:T(2,128)S(1)} %collective-permute-done.5.refs_2_, ...), custom_call_target="tpu_custom_call" | custom-call | flops 10000000000 | bytes 4194304 | tf_op jit(solution)/shard_map/pallas_call | solution.py:384
  35.8 1.8 %collective-permute-start.10 = (bf16[4,2,2048]{2,1,0:T(2,128)(2,1)S(1)}, bf16[4,2,2048]{2,1,0:T(2,128)(2,1)S(1)}, u32[]{:S(2)}, u32[]{:S(2)}) collective-permute-start(bf16[4,2,2048]{2,1,0:T(2,128)(2,1)S(1)} %shard_map.109.refs_0_), channel_id=1, source_target_pairs={{0,12},{4,8},{8,4},{12,0},{1,13},{5,9},{9,5},{13,1},{2,14},{6,10},... | collective-permute-start | bytes 98312 | tf_op jit(solution)/shard_map/ppermute | solution.py:259
  37.6 0.0 collective-permute-start.8
  37.6 2.6 %collective-permute-start.9 = (bf16[4,2,2048]{2,1,0:T(2,128)(2,1)S(1)}, bf16[4,2,2048]{2,1,0:T(2,128)(2,1)S(1)}, u32[]{:S(2)}, u32[]{:S(2)}) collective-permute-start(bf16[4,2,2048]{2,1,0:T(2,128)(2,1)S(1)} %shard_map.109.refs_0_), channel_id=1, source_target_pairs={{0,4},{4,0},{8,12},{12,8},{1,5},{5,1},{9,13},{13,9},{2,6},{6,2},{1... | collective-permute-start | bytes 98312 | tf_op jit(solution)/shard_map/ppermute | solution.py:259
  40.2 1.3 %collective-permute-done.10.refs_3_ = bf16[4,2,2048]{2,1,0:T(2,128)(2,1)S(1)} collective-permute-done((bf16[4,2,2048]{2,1,0:T(2,128)(2,1)S(1)}, bf16[4,2,2048]{2,1,0:T(2,128)(2,1)S(1)}, u32[]{:S(2)}, u32[]{:S(2)}) %collective-permute-start.10) | collective-permute-done | bytes 32800 | tf_op jit(solution)/shard_map/ppermute | solution.py:259
  41.6 0.9 %collective-permute-done.8.refs_1_ = bf16[4,2,2048]{2,1,0:T(2,128)(2,1)S(1)} collective-permute-done((bf16[4,2,2048]{2,1,0:T(2,128)(2,1)S(1)}, bf16[4,2,2048]{2,1,0:T(2,128)(2,1)S(1)}, u32[]{:S(2)}, u32[]{:S(2)}) %collective-permute-start.8) | collective-permute-done | bytes 32800 | tf_op jit(solution)/shard_map/ppermute | solution.py:259
  42.5 0.0 collective-permute-done.9.refs_2_
  42.5 1.5 %shard_map.112 = (f32[8,2,2048]{2,1,0:T(2,128)S(1)}, f32[8,2,2048]{2,1,0:T(2,128)S(1)}) custom-call(bf16[2048,4096]{1,0:T(8,128)(2,1)S(1)} %bitcast.3, bf16[4,2,2048]{2,1,0:T(2,128)(2,1)S(1)} %shard_map.109.refs_0_, bf16[4,2,2048]{2,1,0:T(2,128)(2,1)S(1)} %collective-permute-done.8.refs_1_, bf16[4,2,2048]{2,1,0:T(2,128)(2,1)S(1)} %collective-permute-done.9.refs_2_, ...), custom_call_target="tpu_custom_call" | custom-call | flops 268435456 | bytes 8388608 | tf_op jit(solution)/shard_map/pallas_call | solution.py:408
  44.1 0.1 collective-permute-start.13
  44.1 1.5 %shard_map.110 = (f32[8,2,2048]{2,1,0:T(2,128)S(1)}, f32[8,2,2048]{2,1,0:T(2,128)S(1)}) custom-call(bf16[2048,4096]{1,0:T(8,128)(2,1)S(1)} %bitcast.3, bf16[4,2,2048]{2,1,0:T(2,128)(2,1)S(1)} %shard_map.109.refs_0_, bf16[4,2,2048]{2,1,0:T(2,128)(2,1)S(1)} %collective-permute-done.8.refs_1_, bf16[4,2,2048]{2,1,0:T(2,128)(2,1)S(1)} %collective-permute-done.9.refs_2_, ...), custom_call_target="tpu_custom_call" | custom-call | flops 268435456 | bytes 8388608 | tf_op jit(solution)/shard_map/pallas_call | solution.py:408
  45.7 0.6 collective-permute-start.11
  46.3 0.0 collective-permute-done.13.b_ref
  46.3 1.5 %collective-permute-start.14 = (f32[4,2,2048]{2,1,0:T(2,128)S(1)}, f32[4,2,2048]{2,1,0:T(2,128)S(1)}, u32[]{:S(2)}, u32[]{:S(2)}) collective-permute-start(f32[4,2,2048]{2,1,0:T(2,128)S(1)} %get-tuple-element.46), channel_id=1, source_target_pairs={{0,2},{1,3},{2,0},{3,1},{4,6},{5,7},{6,4},{7,5},{8,10},{9,11},{10,... | collective-permute-start | bytes 196616 | tf_op jit(solution)/shard_map/ppermute | solution.py:263
  47.8 0.0 collective-permute-done.11.b_ref
  47.8 1.0 %collective-permute-start.12 = (f32[4,2,2048]{2,1,0:T(2,128)S(1)}, f32[4,2,2048]{2,1,0:T(2,128)S(1)}, u32[]{:S(2)}, u32[]{:S(2)}) collective-permute-start(f32[4,2,2048]{2,1,0:T(2,128)S(1)} %get-tuple-element.42), channel_id=1, source_target_pairs={{0,2},{1,3},{2,0},{3,1},{4,6},{5,7},{6,4},{7,5},{8,10},{9,11},{10,... | collective-permute-start | bytes 196616 | tf_op jit(solution)/shard_map/ppermute | solution.py:263
  48.8 2.3 %collective-permute-done.14.refs_3_ = f32[4,2,2048]{2,1,0:T(2,128)S(1)} collective-permute-done((f32[4,2,2048]{2,1,0:T(2,128)S(1)}, f32[4,2,2048]{2,1,0:T(2,128)S(1)}, u32[]{:S(2)}, u32[]{:S(2)}) %collective-permute-start.14) | collective-permute-done | bytes 65568 | tf_op jit(solution)/shard_map/ppermute | solution.py:263
  51.0 1.1 %collective-permute-done.12.refs_1_ = f32[4,2,2048]{2,1,0:T(2,128)S(1)} collective-permute-done((f32[4,2,2048]{2,1,0:T(2,128)S(1)}, f32[4,2,2048]{2,1,0:T(2,128)S(1)}, u32[]{:S(2)}, u32[]{:S(2)}) %collective-permute-start.12) | collective-permute-done | bytes 65568 | tf_op jit(solution)/shard_map/ppermute | solution.py:263
  52.1 0.1 shard_map.114
  52.2 2.0 %collective-permute-start.15 = (bf16[2,4096]{1,0:T(2,128)(2,1)S(1)}, bf16[2,4096]{1,0:T(2,128)(2,1)S(1)}, u32[]{:S(2)}, u32[]{:S(2)}) collective-permute-start(bf16[2,4096]{1,0:T(2,128)(2,1)S(1)} %get-tuple-element.47), channel_id=1, source_target_pairs={{0,12},{4,8},{8,4},{12,0},{1,13},{5,9},{9,5},{13,1},{2,14},{6,10},... | collective-permute-start | bytes 49160 | tf_op jit(solution)/shard_map/ppermute | solution.py:259
  54.2 1.1 %collective-permute-start.16 = (bf16[2,4096]{1,0:T(2,128)(2,1)S(1)}, bf16[2,4096]{1,0:T(2,128)(2,1)S(1)}, u32[]{:S(2)}, u32[]{:S(2)}) collective-permute-start(bf16[2,4096]{1,0:T(2,128)(2,1)S(1)} %get-tuple-element.48), channel_id=1, source_target_pairs={{0,8},{4,12},{8,0},{12,4},{1,9},{5,13},{9,1},{13,5},{2,10},{6,14},... | collective-permute-start | bytes 49160 | tf_op jit(solution)/shard_map/ppermute | solution.py:259
  55.3 1.4 %collective-permute-start.17 = (bf16[2,4096]{1,0:T(2,128)(2,1)S(1)}, bf16[2,4096]{1,0:T(2,128)(2,1)S(1)}, u32[]{:S(2)}, u32[]{:S(2)}) collective-permute-start(bf16[2,4096]{1,0:T(2,128)(2,1)S(1)} %get-tuple-element.49), channel_id=1, source_target_pairs={{0,4},{4,0},{8,12},{12,8},{1,5},{5,1},{9,13},{13,9},{2,6},{6,2},{1... | collective-permute-start | bytes 49160 | tf_op jit(solution)/shard_map/ppermute | solution.py:259
  56.6 1.1 %collective-permute-done.15.refs_0_ = bf16[2,4096]{1,0:T(2,128)(2,1)S(1)} collective-permute-done((bf16[2,4096]{1,0:T(2,128)(2,1)S(1)}, bf16[2,4096]{1,0:T(2,128)(2,1)S(1)}, u32[]{:S(2)}, u32[]{:S(2)}) %collective-permute-start.15) | collective-permute-done | bytes 16416 | tf_op jit(solution)/shard_map/ppermute | solution.py:259
  57.8 1.0 %collective-permute-done.16.refs_1_ = bf16[2,4096]{1,0:T(2,128)(2,1)S(1)} collective-permute-done((bf16[2,4096]{1,0:T(2,128)(2,1)S(1)}, bf16[2,4096]{1,0:T(2,128)(2,1)S(1)}, u32[]{:S(2)}, u32[]{:S(2)}) %collective-permute-start.16) | collective-permute-done | bytes 16416 | tf_op jit(solution)/shard_map/ppermute | solution.py:259
  58.8 0.2 collective-permute-done.17.refs_2_
  59.0 0.6 %shard_map.115 = bf16[2,16384]{1,0:T(2,128)(2,1)} custom-call(bf16[2,4096]{1,0:T(2,128)(2,1)S(1)} %collective-permute-done.15.refs_0_, bf16[2,4096]{1,0:T(2,128)(2,1)S(1)} %collective-permute-done.16.refs_1_, bf16[2,4096]{1,0:T(2,128)(2,1)S(1)} %collective-permute-done.17.refs_2_, bf16[2,4096]{1,0:T(2,128)(2,1)S(1)} %get-tuple-element.50.refs_3_), custom_call_target="tpu_custom_call" | custom-call | tf_op jit(solution)/shard_map/pallas_call | solution.py:439
  (16 shorter events, 0.1 us)
Async XLA Ops:
  0.0 1.3 %copy-start.5 = (f32[16384]{0:T(1024)S(1)}, f32[16384]{0:T(1024)}, u32[]{:S(2)}) copy-start(f32[16384]{0:T(1024)} %param.11) | copy-start | bytes 196612
  0.0 1.4 %copy-start.6 = (s32[2]{0:T(128)S(1)}, s32[2]{0:T(128)}, u32[]{:S(2)}) copy-start(s32[2]{0:T(128)} %param.18) | copy-start | bytes 28
  0.0 1.4 %copy-start.3 = (bf16[2,256,1024]{2,1,0:T(8,128)(2,1)S(1)}, bf16[2,256,1024]{2,1,0:T(8,128)(2,1)}, u32[]{:S(2)}) copy-start(bf16[2,256,1024]{2,1,0:T(8,128)(2,1)} %keys_ref.3) | copy-start | bytes 3145732
  0.0 1.6 %copy-start.4 = (bf16[2,256,1024]{2,1,0:T(8,128)(2,1)S(1)}, bf16[2,256,1024]{2,1,0:T(8,128)(2,1)}, u32[]{:S(2)}) copy-start(bf16[2,256,1024]{2,1,0:T(8,128)(2,1)} %values_ref.3) | copy-start | bytes 3145732
  0.0 20.0 %copy-start = (bf16[4096,2048]{1,0:T(8,128)(2,1)S(1)}, bf16[4096,2048]{1,0:T(8,128)(2,1)}, u32[]{:S(2)}) copy-start(bf16[4096,2048]{1,0:T(8,128)(2,1)} %query_ref.3) | copy-start | bytes 50331652
  0.0 20.0 %copy-start.1 = (bf16[4096,256]{1,0:T(8,128)(2,1)S(1)}, bf16[4096,256]{1,0:T(8,128)(2,1)}, u32[]{:S(2)}) copy-start(bf16[4096,256]{1,0:T(8,128)(2,1)} %key_ref.3) | copy-start | bytes 6291460
  0.0 20.0 %copy-start.2 = (bf16[4096,256]{1,0:T(8,128)(2,1)S(1)}, bf16[4096,256]{1,0:T(8,128)(2,1)}, u32[]{:S(2)}) copy-start(bf16[4096,256]{1,0:T(8,128)(2,1)} %value_ref.3) | copy-start | bytes 6291460
  0.0 1.0 %copy-start.8 = (bf16[2,16384]{1,0:T(2,128)(2,1)S(1)}, bf16[2,16384]{1,0:T(2,128)(2,1)}, u32[]{:S(2)}) copy-start(bf16[2,16384]{1,0:T(2,128)(2,1)} %tokens_ref.1) | copy-start | bytes 196612
  1.8 16.0 %collective-permute-start.1 = (bf16[800,256]{1,0:T(8,128)(2,1)S(1)}, bf16[800,256]{1,0:T(8,128)(2,1)S(1)}, u32[]{:S(2)}, u32[]{:S(2)}) collective-permute-start(bf16[800,256]{1,0:T(8,128)(2,1)S(1)} %get-tuple-element.31), channel_id=1, source_target_pairs={{0,2},{1,3},{2,0},{3,1},{4,6},{5,7},{6,4},{7,5},{8,10},{9,11},{10,... | collective-permute-start | bytes 1228808 | tf_op jit(solution)/shard_map/ppermute | solution.py:263
  17.8 4.1 %collective-permute-start.2 = (bf16[1040,256]{1,0:T(8,128)(2,1)S(1)}, bf16[1040,256]{1,0:T(8,128)(2,1)S(1)}, u32[]{:S(2)}, u32[]{:S(2)}) collective-permute-start(bf16[1040,256]{1,0:T(8,128)(2,1)S(1)} %get-tuple-element.32), channel_id=1, source_target_pairs={{0,1},{1,0},{2,3},{3,2},{4,5},{5,4},{6,7},{7,6},{8,9},{9,8},{10,11... | collective-permute-start | bytes 1597448 | tf_op jit(solution)/shard_map/ppermute | solution.py:263
  17.8 17.1 %collective-permute-start.7 = (bf16[1040,256]{1,0:T(8,128)(2,1)S(1)}, bf16[1040,256]{1,0:T(8,128)(2,1)S(1)}, u32[]{:S(2)}, u32[]{:S(2)}) collective-permute-start(bf16[1040,256]{1,0:T(8,128)(2,1)S(1)} %get-tuple-element.38), channel_id=1, source_target_pairs={{0,3},{1,2},{2,1},{3,0},{4,7},{5,6},{6,5},{7,4},{8,11},{9,10},{10,... | collective-permute-start | bytes 1597448 | tf_op jit(solution)/shard_map/ppermute | solution.py:263
  17.9 4.0 %collective-permute-start = (bf16[16,2,2048]{2,1,0:T(2,128)(2,1)S(1)}, bf16[16,2,2048]{2,1,0:T(2,128)(2,1)S(1)}, u32[]{:S(2)}, u32[]{:S(2)}) collective-permute-start(bf16[16,2,2048]{2,1,0:T(2,128)(2,1)S(1)} %all_to_all.5.refs_3_.rows_ref._), channel_id=1, source_target_pairs={{0,1},{1,0},{2,3},{3,2},{4,5},{5,4},{6,7},{7,6},{8,9},{9,8},{10,11... | collective-permute-start | bytes 393224 | tf_op jit(solution)/shard_map/ppermute | solution.py:259
  18.3 16.6 %collective-permute-start.6 = (bf16[240,256]{1,0:T(8,128)(2,1)S(1)}, bf16[240,256]{1,0:T(8,128)(2,1)S(1)}, u32[]{:S(2)}, u32[]{:S(2)}) collective-permute-start(bf16[240,256]{1,0:T(8,128)(2,1)S(1)} %get-tuple-element.37), channel_id=1, source_target_pairs={{0,2},{1,3},{2,0},{3,1},{4,6},{5,7},{6,4},{7,5},{8,10},{9,11},{10,... | collective-permute-start | bytes 368648 | tf_op jit(solution)/shard_map/ppermute | solution.py:263
  21.9 11.9 %copy-start.7 = (f32[1,128]{1,0:T(1,128)S(1)}, f32[1,128]{1,0:T(1,128)}, u32[]{:S(2)}) copy-start(f32[1,128]{1,0:T(1,128)} %constant.2.clone.frequency_ref) | copy-start | bytes 1540
  24.0 7.3 %collective-permute-start.3 = (f32[4,2,2560]{2,1,0:T(2,128)S(1)}, f32[4,2,2560]{2,1,0:T(2,128)S(1)}, u32[]{:S(2)}, u32[]{:S(2)}) collective-permute-start(f32[4,2,2560]{2,1,0:T(2,128)S(1)} %get-tuple-element.33), channel_id=1, source_target_pairs={{0,12},{4,8},{8,4},{12,0},{1,13},{5,9},{9,5},{13,1},{2,14},{6,10},... | collective-permute-start | bytes 245768 | tf_op jit(solution)/shard_map/ppermute | solution.py:259
  25.8 8.1 %collective-permute-start.4 = (f32[4,2,2560]{2,1,0:T(2,128)S(1)}, f32[4,2,2560]{2,1,0:T(2,128)S(1)}, u32[]{:S(2)}, u32[]{:S(2)}) collective-permute-start(f32[4,2,2560]{2,1,0:T(2,128)S(1)} %get-tuple-element.34), channel_id=1, source_target_pairs={{0,8},{4,12},{8,0},{12,4},{1,9},{5,13},{9,1},{13,5},{2,10},{6,14},... | collective-permute-start | bytes 245768 | tf_op jit(solution)/shard_map/ppermute | solution.py:259
  25.8 8.1 %collective-permute-start.5 = (f32[4,2,2560]{2,1,0:T(2,128)S(1)}, f32[4,2,2560]{2,1,0:T(2,128)S(1)}, u32[]{:S(2)}, u32[]{:S(2)}) collective-permute-start(f32[4,2,2560]{2,1,0:T(2,128)S(1)} %get-tuple-element.35), channel_id=1, source_target_pairs={{0,4},{4,0},{8,12},{12,8},{1,5},{5,1},{9,13},{13,9},{2,6},{6,2},{1... | collective-permute-start | bytes 245768 | tf_op jit(solution)/shard_map/ppermute | solution.py:259
  33.9 8.6 %slice-start = ((s8[16777216]{0:T(1024)(128)(4,1)}), s8[4194304]{0:T(1024)(128)(4,1)S(1)}, s32[]{:S(2)}) async-start(s8[16777216]{0:T(1024)(128)(4,1)} %bitcast.2), calls=%async_computation.1 | async-start | bytes 8388608
  34.7 7.8 %slice-start.1 = ((s8[16777216]{0:T(1024)(128)(4,1)}), s8[4194304]{0:T(1024)(128)(4,1)S(1)}, s32[]{:S(2)}) async-start(s8[16777216]{0:T(1024)(128)(4,1)} %bitcast.2), calls=%async_computation.2 | async-start | bytes 8388608
  34.7 7.8 %slice-start.2 = ((s8[16777216]{0:T(1024)(128)(4,1)}), s8[4194304]{0:T(1024)(128)(4,1)S(1)}, s32[]{:S(2)}) async-start(s8[16777216]{0:T(1024)(128)(4,1)} %bitcast.2), calls=%async_computation.3 | async-start | bytes 8388608
  34.7 7.8 %slice-start.3 = ((s8[16777216]{0:T(1024)(128)(4,1)}), s8[4194304]{0:T(1024)(128)(4,1)S(1)}, s32[]{:S(2)}) async-start(s8[16777216]{0:T(1024)(128)(4,1)} %bitcast.2), calls=%async_computation.4 | async-start | bytes 8388608
  35.8 5.8 %collective-permute-start.10 = (bf16[4,2,2048]{2,1,0:T(2,128)(2,1)S(1)}, bf16[4,2,2048]{2,1,0:T(2,128)(2,1)S(1)}, u32[]{:S(2)}, u32[]{:S(2)}) collective-permute-start(bf16[4,2,2048]{2,1,0:T(2,128)(2,1)S(1)} %shard_map.109.refs_0_), channel_id=1, source_target_pairs={{0,12},{4,8},{8,4},{12,0},{1,13},{5,9},{9,5},{13,1},{2,14},{6,10},... | collective-permute-start | bytes 98312 | tf_op jit(solution)/shard_map/ppermute | solution.py:259
  37.6 4.9 %collective-permute-start.8 = (bf16[4,2,2048]{2,1,0:T(2,128)(2,1)S(1)}, bf16[4,2,2048]{2,1,0:T(2,128)(2,1)S(1)}, u32[]{:S(2)}, u32[]{:S(2)}) collective-permute-start(bf16[4,2,2048]{2,1,0:T(2,128)(2,1)S(1)} %shard_map.109.refs_0_), channel_id=1, source_target_pairs={{0,8},{4,12},{8,0},{12,4},{1,9},{5,13},{9,1},{13,5},{2,10},{6,14},... | collective-permute-start | bytes 98312 | tf_op jit(solution)/shard_map/ppermute | solution.py:259
  37.6 4.9 %collective-permute-start.9 = (bf16[4,2,2048]{2,1,0:T(2,128)(2,1)S(1)}, bf16[4,2,2048]{2,1,0:T(2,128)(2,1)S(1)}, u32[]{:S(2)}, u32[]{:S(2)}) collective-permute-start(bf16[4,2,2048]{2,1,0:T(2,128)(2,1)S(1)} %shard_map.109.refs_0_), channel_id=1, source_target_pairs={{0,4},{4,0},{8,12},{12,8},{1,5},{5,1},{9,13},{13,9},{2,6},{6,2},{1... | collective-permute-start | bytes 98312 | tf_op jit(solution)/shard_map/ppermute | solution.py:259
  44.1 2.2 %collective-permute-start.13 = (f32[8,2,2048]{2,1,0:T(2,128)S(1)}, f32[8,2,2048]{2,1,0:T(2,128)S(1)}, u32[]{:S(2)}, u32[]{:S(2)}) collective-permute-start(f32[8,2,2048]{2,1,0:T(2,128)S(1)} %get-tuple-element.44), channel_id=1, source_target_pairs={{0,1},{1,0},{2,3},{3,2},{4,5},{5,4},{6,7},{7,6},{8,9},{9,8},{10,11... | collective-permute-start | bytes 393224 | tf_op jit(solution)/shard_map/ppermute | solution.py:263
  45.7 2.1 %collective-permute-start.11 = (f32[8,2,2048]{2,1,0:T(2,128)S(1)}, f32[8,2,2048]{2,1,0:T(2,128)S(1)}, u32[]{:S(2)}, u32[]{:S(2)}) collective-permute-start(f32[8,2,2048]{2,1,0:T(2,128)S(1)} %get-tuple-element.40), channel_id=1, source_target_pairs={{0,1},{1,0},{2,3},{3,2},{4,5},{5,4},{6,7},{7,6},{8,9},{9,8},{10,11... | collective-permute-start | bytes 393224 | tf_op jit(solution)/shard_map/ppermute | solution.py:263
  46.3 4.7 %collective-permute-start.14 = (f32[4,2,2048]{2,1,0:T(2,128)S(1)}, f32[4,2,2048]{2,1,0:T(2,128)S(1)}, u32[]{:S(2)}, u32[]{:S(2)}) collective-permute-start(f32[4,2,2048]{2,1,0:T(2,128)S(1)} %get-tuple-element.46), channel_id=1, source_target_pairs={{0,2},{1,3},{2,0},{3,1},{4,6},{5,7},{6,4},{7,5},{8,10},{9,11},{10,... | collective-permute-start | bytes 196616 | tf_op jit(solution)/shard_map/ppermute | solution.py:263
  47.8 4.3 %collective-permute-start.12 = (f32[4,2,2048]{2,1,0:T(2,128)S(1)}, f32[4,2,2048]{2,1,0:T(2,128)S(1)}, u32[]{:S(2)}, u32[]{:S(2)}) collective-permute-start(f32[4,2,2048]{2,1,0:T(2,128)S(1)} %get-tuple-element.42), channel_id=1, source_target_pairs={{0,2},{1,3},{2,0},{3,1},{4,6},{5,7},{6,4},{7,5},{8,10},{9,11},{10,... | collective-permute-start | bytes 196616 | tf_op jit(solution)/shard_map/ppermute | solution.py:263
  52.2 5.6 %collective-permute-start.15 = (bf16[2,4096]{1,0:T(2,128)(2,1)S(1)}, bf16[2,4096]{1,0:T(2,128)(2,1)S(1)}, u32[]{:S(2)}, u32[]{:S(2)}) collective-permute-start(bf16[2,4096]{1,0:T(2,128)(2,1)S(1)} %get-tuple-element.47), channel_id=1, source_target_pairs={{0,12},{4,8},{8,4},{12,0},{1,13},{5,9},{9,5},{13,1},{2,14},{6,10},... | collective-permute-start | bytes 49160 | tf_op jit(solution)/shard_map/ppermute | solution.py:259
  54.2 4.6 %collective-permute-start.16 = (bf16[2,4096]{1,0:T(2,128)(2,1)S(1)}, bf16[2,4096]{1,0:T(2,128)(2,1)S(1)}, u32[]{:S(2)}, u32[]{:S(2)}) collective-permute-start(bf16[2,4096]{1,0:T(2,128)(2,1)S(1)} %get-tuple-element.48), channel_id=1, source_target_pairs={{0,8},{4,12},{8,0},{12,4},{1,9},{5,13},{9,1},{13,5},{2,10},{6,14},... | collective-permute-start | bytes 49160 | tf_op jit(solution)/shard_map/ppermute | solution.py:259
  55.3 3.7 %collective-permute-start.17 = (bf16[2,4096]{1,0:T(2,128)(2,1)S(1)}, bf16[2,4096]{1,0:T(2,128)(2,1)S(1)}, u32[]{:S(2)}, u32[]{:S(2)}) collective-permute-start(bf16[2,4096]{1,0:T(2,128)(2,1)S(1)} %get-tuple-element.49), channel_id=1, source_target_pairs={{0,4},{4,0},{8,12},{12,8},{1,5},{5,1},{9,13},{13,9},{2,6},{6,2},{1... | collective-permute-start | bytes 49160 | tf_op jit(solution)/shard_map/ppermute | solution.py:259
